TPU v7x, 32 devices: a whole 2x2x4 slice. The times are simulated.
32 devices in a mesh: occ: 4 (over z), vir: 8 (over y, x, core).
Axes of the slice: x: 2, y: 2, z: 4, core: 2. Of those that a mesh axis runs over, the one named last changes fastest.
Arguments:
- amplitudes: float32 [4096, 3072], P(('occ', 'vir')), may hold values from -6 to 6
- amp_mask: int32 [128, 24], P(('occ', 'vir')), may hold values 0 or 1
- integrals: float32 [3072, 3072], P('vir', 'occ'), may hold values from -0.1875 to 0.1875
- int_mask: int32 [24, 24], P('vir', 'occ'), may hold values from 0 to 1, as said below
Outputs:
- residual: float32 [4096, 3072], P(('occ', 'vir'))
Inputs may be any that keep to these rules, and one draw needn't show every extreme that they name: `int_mask`: 0/1 entries. `amp_mask`: 0/1 entries.
All inputs are finite; a program needn't handle non-finite values. No bound on the sum of `amp_mask` on one device may be relied on, other than what follows from the above.
Results may differ from a plain program's by a relative error of at most 0.000071.
Values sent between devices are 32-bit elements; how exact they have to be, the bound alone decides.
No kernel may reach another device: no remote copies, remote signals or barrier semaphores. Data moves between devices by JAX's collectives and lax.ppermute only.
A program may use at most 192 MiB of HBM per device.

v0:
```python
import jax
import jax.numpy as jnp
from jax import lax
from jax.sharding import PartitionSpec as P

TILE_O = 32
TILE_V = 128


def per_device(amplitudes, amp_mask, integrals, int_mask):
    row_count = amplitudes.shape[0]
    col_count = amplitudes.shape[1]
    amp_scale = amp_mask.astype(jnp.float32)[:, None, :, None]
    kept = (
        amplitudes.reshape(amp_mask.shape[0], TILE_O, amp_mask.shape[1], TILE_V) * amp_scale
    ).reshape(row_count, col_count)
    int_scale = int_mask.astype(jnp.float32)[:, None, :, None]
    weighted = (
        integrals.reshape(int_mask.shape[0], TILE_V, int_mask.shape[1], TILE_V) * int_scale
    ).reshape(integrals.shape)
    relayed = lax.all_to_all(kept, "vir", split_axis=1, concat_axis=0, tiled=True)
    partial_sums = jnp.dot(
        relayed,
        lax.all_gather(weighted, "occ", axis=1, tiled=True),
        precision=lax.Precision.HIGHEST,
        preferred_element_type=jnp.float32,
    )
    return lax.psum_scatter(partial_sums, "vir", scatter_dimension=0, tiled=True)


def solution(mesh):
    in_specs = (P(("occ", "vir"), None), P(("occ", "vir"), None), P("vir", "occ"), P("vir", "occ"))
    out_specs = P(("occ", "vir"), None)
    return jax.shard_map(
        per_device, mesh=mesh, in_specs=in_specs, out_specs=out_specs, check_vma=False
    )
```

profile of v0, /device:TPU:0, one launch (start us, length us, event | category | flops | bytes accessed | tf_op | source)
XLA Modules:
  0.0 223.1 jit_solution(17999281017317525701)
XLA Ops:
  6.5 0.0 copy-start.1
  6.5 0.0 all-gather.2.cloned.1.call-start
  6.5 0.8 convert_element_type.7
  7.3 0.2 mul.25
  7.5 0.3 copy-done.1
  7.8 0.0 copy-start.2
  7.8 1.4 bitcast_multiply_fusion.1
  9.2 0.0 copy-start
  9.2 0.0 all-gather.2.cloned.1.call-update
  9.2 0.0 reduce-scatter.2.cloned.1.call-start
  9.3 0.0 copy-done.2
  9.3 0.2 mul.22
  9.4 1.1 copy-done
  10.6 0.4 bitcast_multiply_fusion
  10.9 0.5 copy.8
  11.4 25.9 %all_to_all.19 = f32[128,8,384]{0,2,1:T(8,128)S(1)} all-to-all(f32[128,8,384]{0,2,1:T(8,128)S(1)} %bitcast.14), channel_id=1, replica_groups=mesh['occ'=4,'vir'=8] {'vir'}, dimensions={1} | all-to-all | bytes 3145728 | tf_op jit(solution)/shard_map/all_to_all | solution.py:21
  37.4 0.5 copy.9
  37.8 63.6 %all-gather.2.cloned.1.call-done = f32[384,3072]{1,0:T(8,128)} async-done(((f32[384,768]{1,0:T(8,128)}), f32[384,3072]{1,0:T(8,128)}) %all-gather.2.cloned.1.call-update) | async-done | bytes 4718608 | tf_op jit(solution)/shard_map/all_gather | solution.py:24
  101.5 23.8 %fusion = f32[1024,3072]{1,0:T(8,128)} fusion(f32[1024,384]{1,0:T(8,128)S(1)} %bitcast.13, f32[384,3072]{1,0:T(8,128)} %all-gather.2.cloned.1.call-done), kind=kOutput, calls=%fused_computation.2 | convolution fusion | flops 14495514624 | bytes 18874368 | tf_op jit(solution)/shard_map/dot_general | solution.py:22
  125.3 0.0 reduce-scatter.2.cloned.1.call-update
  125.3 91.0 %reduce-scatter.2.cloned.1.call-done = f32[128,3072]{1,0:T(8,128)} async-done(((f32[1024,3072]{1,0:T(8,128)}), f32[128,3072]{1,0:T(8,128)}) %reduce-scatter.2.cloned.1.call-update) | async-done | bytes 1572880 | tf_op jit(solution)/shard_map/reduce_scatter | solution.py:28
  (1 shorter events, 0.0 us)
Async XLA Ops:
  6.5 1.3 copy-start.1
  6.5 94.9 %all-gather.2.cloned.1.call-start = ((), (), s32[]{:S(2)}) async-start(), calls=%async_computation.2 | async-start | bytes 5898240 | tf_op jit(solution)/shard_map/all_gather | solution.py:24
  7.8 1.4 copy-start.2
  9.2 1.4 copy-start
  9.2 207.0 %reduce-scatter.2.cloned.1.call-start = ((), (), s32[]{:S(2)}) async-start(), calls=%async_computation.3 | async-start | bytes 14155776 | tf_op jit(solution)/shard_map/reduce_scatter | solution.py:28
Sparse Core Ops, SparseCore 0:
  9.3 92.0 all-gather.1
  125.4 90.7 reduce-scatter.1
where the time goes:
time: 223 us
  waiting for transfers between devices  155 us (70%)
  blocking collectives  25.9 us (12%)
  matrix products  23.8 us (11%)
  between operations  13.4 us (6%)
  local copies, waits for them, and re-layouts  2.73 us (1%)
  other arithmetic  2.49 us (1%)
    reduce_scatter x1, waiting for transfers between devices, per_device(): lax.psum_scatter(partial_sums, 'vir', scatter_dimension=0, tiled=True)  91 us
    all_gather x1, waiting for transfers between devices, per_device(): lax.all_gather(weighted, 'occ', axis=1, tiled=True)  63.6 us
    all_to_all x1, blocking collectives, per_device(): lax.all_to_all(kept, 'vir', split_axis=1, concat_axis=0, tiled=True)  25.9 us
    dot_general x1, matrix products, per_device(): jnp.dot(relayed, lax.all_gather(weighted, 'occ', axis=1, tiled=True), pre...  23.8 us
  transfers between devices with their start and end apart: 2, of which 2 were waited for; matrix products, arithmetic and copies ran while one was open for 1% of the time, Pallas kernels for 0%

commit v1 on v0

v1 whole, which is shorter than its diff:
```python
import jax
import jax.numpy as jnp
from jax import lax
from jax.sharding import PartitionSpec as P

TILE_O = 32
TILE_V = 128
HIGH = lax.Precision.HIGH


def masked(values, mask, tile_rows):
    tile_r, tile_c = mask.shape
    scale = mask.astype(jnp.float32)[:, None, :, None]
    return (values.reshape(tile_r, tile_rows, tile_c, TILE_V) * scale).reshape(values.shape)


def line_blocks(own, nodes):
    here = lax.axis_index("occ")
    blocks = [own]
    origins = [list(range(nodes))]
    size = 1
    while size < nodes:
        fresh, fresh_origins = [], []
        place = here % (2 * size)
        dist = jnp.where(place < size, size - 1 - place, place - size)
        middles = [g * 2 * size + size for g in range(nodes // (2 * size))]
        for block, origin in zip(blocks, origins):
            pairs = [(m - 1, m) for m in middles] + [(m, m - 1) for m in middles]
            moving = lax.ppermute(block, "occ", pairs)
            got = moving
            for hop in range(1, size):
                pairs = [(m - hop, m - hop - 1) for m in middles] + [(m + hop - 1, m + hop) for m in middles]
                moving = lax.ppermute(moving, "occ", pairs)
                got = jnp.where(dist == hop, moving, got)
            fresh.append(got)
            table = [0] * nodes
            for m in middles:
                for k in range(size):
                    table[m - 1 - k] = origin[m]
                    table[m + k] = origin[m - 1]
            fresh_origins.append(table)
        blocks += fresh
        origins += fresh_origins
        size *= 2
    return blocks, origins


def per_device(sizes, amplitudes, amp_mask, integrals, int_mask):
    n_occ, n_vir = sizes
    rows = amplitudes.shape[0]
    half = rows // 2
    groups = n_vir // 2
    width = integrals.shape[1]
    depth = 2 * integrals.shape[0]

    def swap(x, bits):
        return lax.ppermute(x, "vir", [(i, i ^ bits) for i in range(n_vir)])

    me = lax.axis_index("vir")
    kept = masked(amplitudes, amp_mask, TILE_O)
    weighted = masked(integrals, int_mask, TILE_V)
    blocks, origins = line_blocks(weighted, n_occ)

    rel = []
    for r in range(groups):
        start = ((me // 2) ^ r) * depth
        part = lax.dynamic_slice_in_dim(kept, start, depth, axis=1)
        rel.append(part if r == 0 else swap(part, 2 * r))

    bits = []
    while (1 << len(bits)) < groups:
        bits.append(1 << len(bits))
    orders = [bits, bits[::-1]]
    cut = [slice(0, half), slice(half, rows)]
    away = [[r for r in range(groups) if r & o[0]] for o in orders]
    near = [[r for r in range(groups) if not r & o[0]] for o in orders]
    lhs_away = jnp.concatenate([rel[r][cut[h]] for h in range(2) for r in away[h]], axis=0)
    lhs_near = jnp.concatenate([rel[r][cut[h]] for h in range(2) for r in near[h]], axis=0)

    low = me % 2
    out = jnp.zeros((rows, n_occ * width), jnp.float32)
    for block, origin in zip(blocks, origins):
        other = swap(block, 1)
        first = jnp.where(low == 0, block, other)
        second = jnp.where(low == 0, other, block)
        rhs = jnp.concatenate([first, second], axis=0)
        sent = jnp.dot(lhs_away, rhs, precision=HIGH, preferred_element_type=jnp.float32)
        stay = jnp.dot(lhs_near, rhs, precision=HIGH, preferred_element_type=jnp.float32)
        count = groups // 2
        done = []
        for h in range(2):
            s = sent[h * count * half : (h + 1) * count * half]
            k = stay[h * count * half : (h + 1) * count * half]
            k = k + swap(s, 2 * orders[h][0])
            held = {r: k[i * half : (i + 1) * half] for i, r in enumerate(near[h])}
            for bit in orders[h][1:]:
                going = [r for r in held if r & bit]
                s = jnp.concatenate([held[r] for r in going], axis=0)
                got = swap(s, 2 * bit)
                for i, r in enumerate(going):
                    held[r ^ bit] = held[r ^ bit] + got[i * half : (i + 1) * half]
                    del held[r]
            done.append(held[0])
        col = jnp.array(origin, jnp.int32)[lax.axis_index("occ")] * width
        out = lax.dynamic_update_slice(out, jnp.concatenate(done, axis=0), (0, col))
    return out


def solution(mesh):
    sizes = (mesh.shape["occ"], mesh.shape["vir"])

    def run(*args):
        return per_device(sizes, *args)

    in_specs = (P(("occ", "vir"), None), P(("occ", "vir"), None), P("vir", "occ"), P("vir", "occ"))
    out_specs = P(("occ", "vir"), None)
    return jax.shard_map(run, mesh=mesh, in_specs=in_specs, out_specs=out_specs, check_vma=False)
```

time: 223 us -> 136 us (0.61)
  waiting for transfers between devices: 155 us -> 71.6 us
  starting transfers between devices: 0.04 us -> 33.5 us
  blocking collectives: 25.9 us -> 0 us
  matrix products: 23.8 us -> 10.8 us
  between operations: 13.4 us -> 2.38 us
  other arithmetic: 2.49 us -> 10.6 us
  local copies, waits for them, and re-layouts: 2.73 us -> 6.98 us
    reduce_scatter x1 -> x0, waiting for transfers between devices: 91 us -> none  [per_device(): lax.psum_scatter(partial_sums, 'vir', scatter_dimension=0, tiled=True)]
    ppermute x0 -> x28, waiting for transfers between devices: none -> 71.6 us  [the longest x23 46.3 us: swap(): return lax.ppermute(x, 'vir', [(i, i ^ bits) for i in range(n_vir)])]
    all_gather x1 -> x0, waiting for transfers between devices: 63.6 us -> none  [per_device(): lax.all_gather(weighted, 'occ', axis=1, tiled=True)]
    ppermute x0 -> x28, starting transfers between devices: none -> 33.5 us  [the longest x23 23.7 us: swap(): return lax.ppermute(x, 'vir', [(i, i ^ bits) for i in range(n_vir)])]
    all_to_all x1 -> x0, blocking collectives: 25.9 us -> none  [per_device(): lax.all_to_all(kept, 'vir', split_axis=1, concat_axis=0, tiled=True)]
    dot_general x1 -> x8, matrix products: 23.8 us -> 10.8 us  [the longest x4 5.38 us: per_device(): jnp.dot(lhs_away, rhs, precision=HIGH, preferred_element_type=jnp.float32)]
    select_n x0 -> x6, other arithmetic: none -> 5.45 us  [the longest x4 3.88 us: per_device(): first = jnp.where(low == 0, block, other)]
    slice x0 -> x16, local copies, waits for them, and re-layouts: none -> 2.35 us  [the longest x4 1.13 us: per_device(): rel[r][cut[h]]]
  transfers between devices with their start and end apart: 2 -> 28, of which waited for: 2 -> 17; matrix products, arithmetic and copies ran while one was open for 1% -> 17% of each run, Pallas kernels for 0% -> 0%
where the time goes in v1:
time: 136 us
  waiting for transfers between devices  71.6 us (53%)
  starting transfers between devices  33.5 us (25%)
  matrix products  10.8 us (8%)
  other arithmetic  10.6 us (8%)
  local copies, waits for them, and re-layouts  6.98 us (5%)
  between operations  2.38 us (2%)
    ppermute x23, waiting for transfers between devices, swap(): return lax.ppermute(x, 'vir', [(i, i ^ bits) for i in range(n_vir)])  46.3 us
    ppermute x23, starting transfers between devices, swap(): return lax.ppermute(x, 'vir', [(i, i ^ bits) for i in range(n_vir)])  23.7 us
    ppermute x2, waiting for transfers between devices, line_blocks(): moving = lax.ppermute(moving, 'occ', pairs)  23.4 us
    ppermute x3, starting transfers between devices, line_blocks(): moving = lax.ppermute(block, 'occ', pairs)  7.03 us
    dot_general x4, matrix products, per_device(): jnp.dot(lhs_away, rhs, precision=HIGH, preferred_element_type=jnp.float32)  5.38 us
    dot_general x4, matrix products, per_device(): jnp.dot(lhs_near, rhs, precision=HIGH, preferred_element_type=jnp.float32)  5.37 us
    select_n x4, other arithmetic, per_device(): first = jnp.where(low == 0, block, other)  3.88 us
    ppermute x2, starting transfers between devices, line_blocks(): moving = lax.ppermute(moving, 'occ', pairs)  2.76 us
  transfers between devices with their start and end apart: 28, of which 17 were waited for; matrix products, arithmetic and copies ran while one was open for 17% of the time, Pallas kernels for 0%

profile of v1, /device:TPU:0, one launch (start us, length us, event | category | flops | bytes accessed | tf_op | source)
XLA Modules:
  0.0 135.8 jit_solution(13627989064839227552)
XLA Ops:
  0.0 0.8 convert_element_type.7
  1.0 0.3 copy-done.7
  1.3 1.4 %bitcast_multiply_fusion.1 = f32[384,768]{1,0:T(8,128)} fusion(f32[384,768]{1,0:T(8,128)S(1)} %copy-done.7, f32[48,8,6,128]{3,2,1,0:T(8,128)S(1)} %bitcast.11), kind=kLoop, calls=%fused_computation.13 | loop fusion | flops 294912 | bytes 3538944 | tf_op jit(solution)/shard_map/mul | solution.py:14
  2.7 1.8 %collective-permute-start.14 = (f32[384,768]{1,0:T(8,128)}, f32[384,768]{1,0:T(8,128)}, u32[]{:S(2)}, u32[]{:S(2)}) collective-permute-start(f32[384,768]{1,0:T(8,128)} %bitcast_multiply_fusion.1), channel_id=1, source_target_pairs={{8,16},{16,8},{9,17},{17,9},{10,18},{18,10},{11,19},{19,11},{12,20... | collective-permute-start | bytes 3538952 | tf_op jit(solution)/shard_map/ppermute | solution.py:29
  4.5 0.5 collective-permute-start.2
  5.2 0.4 bitcast_multiply_fusion
  5.6 1.0 copy-done
  6.7 2.5 %collective-permute-start = (f32[128,768]{1,0:T(8,128)S(1)}, f32[128,768]{1,0:T(8,128)S(1)}, u32[]{:S(2)}, u32[]{:S(2)}) collective-permute-start(f32[128,768]{1,0:T(8,128)S(1)} %get-tuple-element.17), channel_id=1, source_target_pairs={{0,4},{1,5},{2,6},{3,7},{4,0},{5,1},{6,2},{7,3},{8,12},{9,13},{10,... | collective-permute-start | bytes 1179656 | tf_op jit(solution)/shard_map/ppermute | solution.py:57
  9.2 1.5 %collective-permute-start.1 = (f32[128,768]{1,0:T(8,128)S(1)}, f32[128,768]{1,0:T(8,128)S(1)}, u32[]{:S(2)}, u32[]{:S(2)}) collective-permute-start(f32[128,768]{1,0:T(8,128)S(1)} %get-tuple-element.15), channel_id=1, source_target_pairs={{0,2},{1,3},{2,0},{3,1},{4,6},{5,7},{6,4},{7,5},{8,10},{9,11},{10,... | collective-permute-start | bytes 1179656 | tf_op jit(solution)/shard_map/ppermute | solution.py:57
  10.7 3.5 %collective-permute-start.8 = (f32[384,768]{1,0:T(8,128)}, f32[384,768]{1,0:T(8,128)}, u32[]{:S(2)}, u32[]{:S(2)}) collective-permute-start(f32[384,768]{1,0:T(8,128)} %bitcast_multiply_fusion.1), channel_id=1, source_target_pairs={{0,8},{16,24},{8,0},{24,16},{1,9},{17,25},{9,1},{25,17},{2,10},{18... | collective-permute-start | bytes 3538952 | tf_op jit(solution)/shard_map/ppermute | solution.py:29
  14.2 4.8 %collective-permute-done = f32[128,768]{1,0:T(8,128)S(1)} collective-permute-done((f32[128,768]{1,0:T(8,128)S(1)}, f32[128,768]{1,0:T(8,128)S(1)}, u32[]{:S(2)}, u32[]{:S(2)}) %collective-permute-start) | collective-permute-done | bytes 393248 | tf_op jit(solution)/shard_map/ppermute | solution.py:57
  19.0 2.7 %collective-permute-start.3 = (f32[128,768]{1,0:T(8,128)S(1)}, f32[128,768]{1,0:T(8,128)S(1)}, u32[]{:S(2)}, u32[]{:S(2)}) collective-permute-start(f32[128,768]{1,0:T(8,128)S(1)} %get-tuple-element.16), channel_id=1, source_target_pairs={{0,6},{1,7},{2,4},{3,5},{4,2},{5,3},{6,0},{7,1},{8,14},{9,15},{10,... | collective-permute-start | bytes 1179656 | tf_op jit(solution)/shard_map/ppermute | solution.py:57
  21.7 9.2 %collective-permute-done.3 = f32[128,768]{1,0:T(8,128)S(1)} collective-permute-done((f32[128,768]{1,0:T(8,128)S(1)}, f32[128,768]{1,0:T(8,128)S(1)}, u32[]{:S(2)}, u32[]{:S(2)}) %collective-permute-start.3) | collective-permute-done | bytes 393248 | tf_op jit(solution)/shard_map/ppermute | solution.py:57
  31.0 1.3 collective-permute-start.15
  32.3 1.8 %broadcast_select_fusion.9 = (f32[384,768]{1,0:T(8,128)S(1)}, f32[384,768]{1,0:T(8,128)S(1)}) fusion(f32[384,768]{1,0:T(8,128)} %bitcast_multiply_fusion.1, f32[384,768]{1,0:T(8,128)} %collective-permute-done.2, pred[]{:T(512)S(6)} %eq.7), kind=kLoop, calls=%fused_computation.25 | loop fusion | flops 589824 | bytes 4718593 | tf_op jit(solution)/shard_map/jit(_where)/select_n | solution.py:84
  34.1 1.3 fusion.6
  35.3 0.9 fusion.19
  36.3 1.5 %collective-permute-start.4 = (f32[128,768]{1,0:T(8,128)}, f32[128,768]{1,0:T(8,128)}, u32[]{:S(2)}, u32[]{:S(2)}) collective-permute-start(f32[128,768]{1,0:T(8,128)} %get-tuple-element.32), channel_id=1, source_target_pairs={{0,2},{1,3},{2,0},{3,1},{4,6},{5,7},{6,4},{7,5},{8,10},{9,11},{10,... | collective-permute-start | bytes 1179656 | tf_op jit(solution)/shard_map/ppermute | solution.py:57
  37.8 1.5 %collective-permute-start.6 = (f32[128,768]{1,0:T(8,128)}, f32[128,768]{1,0:T(8,128)}, u32[]{:S(2)}, u32[]{:S(2)}) collective-permute-start(f32[128,768]{1,0:T(8,128)} %get-tuple-element.33), channel_id=1, source_target_pairs={{0,4},{1,5},{2,6},{3,7},{4,0},{5,1},{6,2},{7,3},{8,12},{9,13},{10,... | collective-permute-start | bytes 1179656 | tf_op jit(solution)/shard_map/ppermute | solution.py:57
  39.3 2.0 %collective-permute-done.8 = f32[384,768]{1,0:T(8,128)} collective-permute-done((f32[384,768]{1,0:T(8,128)}, f32[384,768]{1,0:T(8,128)}, u32[]{:S(2)}, u32[]{:S(2)}) %collective-permute-start.8) | collective-permute-done | bytes 1179680 | tf_op jit(solution)/shard_map/ppermute | solution.py:29
  41.3 1.7 %collective-permute-start.21 = (f32[384,768]{1,0:T(8,128)}, f32[384,768]{1,0:T(8,128)}, u32[]{:S(2)}, u32[]{:S(2)}) collective-permute-start(f32[384,768]{1,0:T(8,128)} %collective-permute-done.8), channel_id=1, source_target_pairs={{8,16},{16,8},{9,17},{17,9},{10,18},{18,10},{11,19},{19,11},{12,20... | collective-permute-start | bytes 3538952 | tf_op jit(solution)/shard_map/ppermute | solution.py:29
  43.0 1.0 constant_dynamic-slice_fusion
  44.1 1.3 fusion.7
  45.4 1.4 %collective-permute-done.4 = f32[128,768]{1,0:T(8,128)} collective-permute-done((f32[128,768]{1,0:T(8,128)}, f32[128,768]{1,0:T(8,128)}, u32[]{:S(2)}, u32[]{:S(2)}) %collective-permute-start.4) | collective-permute-done | bytes 393248 | tf_op jit(solution)/shard_map/ppermute | solution.py:57
  46.8 1.0 collective-permute-done.6
  47.8 1.2 slice_add_fusion.7
  49.0 1.6 %collective-permute-start.5 = (f32[64,768]{1,0:T(8,128)S(1)}, f32[64,768]{1,0:T(8,128)S(1)}, u32[]{:S(2)}, u32[]{:S(2)}) collective-permute-start(f32[64,768]{1,0:T(8,128)S(1)} %slice.169), channel_id=1, source_target_pairs={{0,4},{1,5},{2,6},{3,7},{4,0},{5,1},{6,2},{7,3},{8,12},{9,13},{10,... | collective-permute-start | bytes 589832 | tf_op jit(solution)/shard_map/ppermute | solution.py:57
  50.6 0.6 dynamic_slice.29
  51.8 0.7 dynamic_slice.30
  53.1 0.6 dynamic_slice.31
  54.4 0.6 collective-permute-start.7
  55.0 10.8 %collective-permute-done.15 = f32[384,768]{1,0:T(8,128)} collective-permute-done((f32[384,768]{1,0:T(8,128)}, f32[384,768]{1,0:T(8,128)}, u32[]{:S(2)}, u32[]{:S(2)}) %collective-permute-start.15) | collective-permute-done | bytes 1179680 | tf_op jit(solution)/shard_map/ppermute | solution.py:33
  65.8 1.4 %broadcast_select_fusion.1 = f32[384,768]{1,0:T(8,128)S(1)} fusion(f32[384,768]{1,0:T(8,128)} %collective-permute-done.15, f32[384,768]{1,0:T(8,128)} %collective-permute-done.14, pred[]{:T(512)S(6)} %eq.8), kind=kLoop, calls=%fused_computation.17 | loop fusion | flops 294912 | bytes 3538945 | tf_op jit(solution)/shard_map/jit(_where)/select_n | solution.py:34
  67.3 1.5 %collective-permute-start.22 = (f32[384,768]{1,0:T(8,128)}, f32[384,768]{1,0:T(8,128)S(1)}, u32[]{:S(2)}, u32[]{:S(2)}) collective-permute-start(f32[384,768]{1,0:T(8,128)} %collective-permute-done.21), channel_id=1, source_target_pairs={{8,0},{16,24},{9,1},{17,25},{10,2},{18,26},{11,3},{19,27},{12,4},{... | collective-permute-start | bytes 3538952 | tf_op jit(solution)/shard_map/ppermute | solution.py:33
  68.8 1.8 %broadcast_select_fusion.7 = (f32[384,768]{1,0:T(8,128)S(1)}, f32[384,768]{1,0:T(8,128)S(1)}) fusion(f32[384,768]{1,0:T(8,128)} %collective-permute-done.8, f32[384,768]{1,0:T(8,128)} %collective-permute-done.9, pred[]{:T(512)S(6)} %eq.7), kind=kLoop, calls=%fused_computation.23 | loop fusion | flops 589824 | bytes 4718593 | tf_op jit(solution)/shard_map/jit(_where)/select_n | solution.py:84
  70.6 1.4 %fusion.4 = f32[256,768]{1,0:T(8,128)S(1)} fusion(f32[384,768]{1,0:T(8,128)S(1)} %get-tuple-element.10, f32[384,768]{1,0:T(8,128)S(1)} %get-tuple-element.9, f32[64,768]{1,0:T(8,128)S(1)} %get-tuple-element.39, f32[64,768]{1,0:T(8,128)S(1)} %get-tuple-element.35, f32[64,768]{1,0:T(8,128)S(1)} %get-tuple-element.38, f32[64,768]{1,0:T(8,128)S(1)} %get-tuple-element.37), kind=kOutput, calls=%fused_computation.8 | convolution fusion | flops 907149312 | bytes 3932160 | tf_op jit(solution)/shard_map/dot_general | solution.py:87
  72.0 0.6 collective-permute-start.10
  72.6 0.5 collective-permute-start.12
  73.4 0.7 copy-done.2
  74.2 1.4 %fusion.5 = f32[256,768]{1,0:T(8,128)S(1)} fusion(f32[384,768]{1,0:T(8,128)S(1)} %get-tuple-element.10, f32[384,768]{1,0:T(8,128)S(1)} %get-tuple-element.9, f32[64,768]{1,0:T(8,128)S(1)} %get-tuple-element.36, f32[64,768]{1,0:T(8,128)S(1)} %copy-done.4, f32[64,768]{1,0:T(8,128)S(1)} %get-tuple-element.34, f32[64,768]{1,0:T(8,128)S(1)} %copy-done.2), kind=kOutput, calls=%fused_computation.9 | convolution fusion | flops 907149312 | bytes 3932160 | tf_op jit(solution)/shard_map/dot_general | solution.py:88
  75.5 8.0 %collective-permute-done.10 = f32[128,768]{1,0:T(8,128)S(1)} collective-permute-done((f32[128,768]{1,0:T(8,128)S(1)}, f32[128,768]{1,0:T(8,128)S(1)}, u32[]{:S(2)}, u32[]{:S(2)}) %collective-permute-start.10) | collective-permute-done | bytes 393248 | tf_op jit(solution)/shard_map/ppermute | solution.py:57
  83.9 0.6 collective-permute-start.11
  84.5 1.6 %collective-permute-start.13 = (f32[64,768]{1,0:T(8,128)S(1)}, f32[64,768]{1,0:T(8,128)S(1)}, u32[]{:S(2)}, u32[]{:S(2)}) collective-permute-start(f32[64,768]{1,0:T(8,128)S(1)} %slice.181), channel_id=1, source_target_pairs={{0,2},{1,3},{2,0},{3,1},{4,6},{5,7},{6,4},{7,5},{8,10},{9,11},{10,... | collective-permute-start | bytes 589832 | tf_op jit(solution)/shard_map/ppermute | solution.py:57
  86.1 12.6 %collective-permute-done.22 = f32[384,768]{1,0:T(8,128)S(1)} collective-permute-done((f32[384,768]{1,0:T(8,128)}, f32[384,768]{1,0:T(8,128)S(1)}, u32[]{:S(2)}, u32[]{:S(2)}) %collective-permute-start.22) | collective-permute-done | bytes 1179680 | tf_op jit(solution)/shard_map/ppermute | solution.py:33
  99.1 1.4 %fusion.2 = f32[256,768]{1,0:T(8,128)S(1)} fusion(f32[384,768]{1,0:T(8,128)S(1)} %get-tuple-element.8, f32[384,768]{1,0:T(8,128)S(1)} %get-tuple-element.7, f32[64,768]{1,0:T(8,128)S(1)} %get-tuple-element.39, f32[64,768]{1,0:T(8,128)S(1)} %get-tuple-element.35, f32[64,768]{1,0:T(8,128)S(1)} %get-tuple-element.38, f32[64,768]{1,0:T(8,128)S(1)} %get-tuple-element.37), kind=kOutput, calls=%fused_computation.6 | convolution fusion | flops 907149312 | bytes 3932160 | tf_op jit(solution)/shard_map/dot_general | solution.py:87
  100.5 0.6 collective-permute-start.17
  101.1 0.5 collective-permute-start.19
  101.7 1.4 %fusion.3 = f32[256,768]{1,0:T(8,128)S(1)} fusion(f32[384,768]{1,0:T(8,128)S(1)} %get-tuple-element.8, f32[384,768]{1,0:T(8,128)S(1)} %get-tuple-element.7, f32[64,768]{1,0:T(8,128)S(1)} %get-tuple-element.36, f32[64,768]{1,0:T(8,128)S(1)} %copy-done.4, f32[64,768]{1,0:T(8,128)S(1)} %get-tuple-element.34, f32[64,768]{1,0:T(8,128)S(1)} %copy-done.2), kind=kOutput, calls=%fused_computation.7 | convolution fusion | flops 907149312 | bytes 3932160 | tf_op jit(solution)/shard_map/dot_general | solution.py:88
  103.1 9.0 %collective-permute-done.17 = f32[128,768]{1,0:T(8,128)S(1)} collective-permute-done((f32[128,768]{1,0:T(8,128)S(1)}, f32[128,768]{1,0:T(8,128)S(1)}, u32[]{:S(2)}, u32[]{:S(2)}) %collective-permute-start.17) | collective-permute-done | bytes 393248 | tf_op jit(solution)/shard_map/ppermute | solution.py:57
  112.5 0.6 collective-permute-start.18
  113.2 1.4 %fusion = f32[256,768]{1,0:T(8,128)S(1)} fusion(f32[384,768]{1,0:T(8,128)S(1)} %get-tuple-element.6, f32[384,768]{1,0:T(8,128)S(1)} %get-tuple-element.5, f32[64,768]{1,0:T(8,128)S(1)} %get-tuple-element.39, f32[64,768]{1,0:T(8,128)S(1)} %get-tuple-element.35, f32[64,768]{1,0:T(8,128)S(1)} %get-tuple-element.38, f32[64,768]{1,0:T(8,128)S(1)} %get-tuple-element.37), kind=kOutput, calls=%fused_computation.4 | convolution fusion | flops 907149312 | bytes 3932160 | tf_op jit(solution)/shard_map/dot_general | solution.py:87
  114.6 1.6 %collective-permute-start.24 = (f32[128,768]{1,0:T(8,128)S(1)}, f32[128,768]{1,0:T(8,128)S(1)}, u32[]{:S(2)}, u32[]{:S(2)}) collective-permute-start(f32[128,768]{1,0:T(8,128)S(1)} %get-tuple-element.20), channel_id=1, source_target_pairs={{0,2},{1,3},{2,0},{3,1},{4,6},{5,7},{6,4},{7,5},{8,10},{9,11},{10,... | collective-permute-start | bytes 1179656 | tf_op jit(solution)/shard_map/ppermute | solution.py:57
  116.2 1.5 %collective-permute-start.26 = (f32[128,768]{1,0:T(8,128)S(1)}, f32[128,768]{1,0:T(8,128)S(1)}, u32[]{:S(2)}, u32[]{:S(2)}) collective-permute-start(f32[128,768]{1,0:T(8,128)S(1)} %get-tuple-element.21), channel_id=1, source_target_pairs={{0,4},{1,5},{2,6},{3,7},{4,0},{5,1},{6,2},{7,3},{8,12},{9,13},{10,... | collective-permute-start | bytes 1179656 | tf_op jit(solution)/shard_map/ppermute | solution.py:57
  117.8 0.6 collective-permute-start.20
  118.4 1.5 %collective-permute-done.18 = f32[64,768]{1,0:T(8,128)S(1)} collective-permute-done((f32[64,768]{1,0:T(8,128)S(1)}, f32[64,768]{1,0:T(8,128)S(1)}, u32[]{:S(2)}, u32[]{:S(2)}) %collective-permute-start.18) | collective-permute-done | bytes 196640 | tf_op jit(solution)/shard_map/ppermute | solution.py:57
  119.9 1.4 %fusion.1 = f32[256,768]{1,0:T(8,128)S(1)} fusion(f32[384,768]{1,0:T(8,128)S(1)} %get-tuple-element.6, f32[384,768]{1,0:T(8,128)S(1)} %get-tuple-element.5, f32[64,768]{1,0:T(8,128)S(1)} %get-tuple-element.36, f32[64,768]{1,0:T(8,128)S(1)} %copy-done.4, f32[64,768]{1,0:T(8,128)S(1)} %get-tuple-element.34, f32[64,768]{1,0:T(8,128)S(1)} %copy-done.2), kind=kOutput, calls=%fused_computation.5 | convolution fusion | flops 907149312 | bytes 3932160 | tf_op jit(solution)/shard_map/dot_general | solution.py:88
  121.3 5.4 %collective-permute-done.24 = f32[128,768]{1,0:T(8,128)S(1)} collective-permute-done((f32[128,768]{1,0:T(8,128)S(1)}, f32[128,768]{1,0:T(8,128)S(1)}, u32[]{:S(2)}, u32[]{:S(2)}) %collective-permute-start.24) | collective-permute-done | bytes 393248 | tf_op jit(solution)/shard_map/ppermute | solution.py:57
  126.8 0.5 collective-permute-done.26
  127.3 1.1 collective-permute-start.25
  128.5 0.6 collective-permute-done.20
  129.2 1.5 %collective-permute-start.27 = (f32[64,768]{1,0:T(8,128)S(1)}, f32[64,768]{1,0:T(8,128)S(1)}, u32[]{:S(2)}, u32[]{:S(2)}) collective-permute-start(f32[64,768]{1,0:T(8,128)S(1)} %slice.197), channel_id=1, source_target_pairs={{0,2},{1,3},{2,0},{3,1},{4,6},{5,7},{6,4},{7,5},{8,10},{9,11},{10,... | collective-permute-start | bytes 589832 | tf_op jit(solution)/shard_map/ppermute | solution.py:57
  130.7 2.5 %collective-permute-done.25 = f32[64,768]{1,0:T(8,128)S(1)} collective-permute-done((f32[64,768]{1,0:T(8,128)S(1)}, f32[64,768]{1,0:T(8,128)S(1)}, u32[]{:S(2)}, u32[]{:S(2)}) %collective-permute-start.25) | collective-permute-done | bytes 196640 | tf_op jit(solution)/shard_map/ppermute | solution.py:57
  133.2 1.7 %collective-permute-done.27 = f32[64,768]{1,0:T(8,128)S(1)} collective-permute-done((f32[64,768]{1,0:T(8,128)S(1)}, f32[64,768]{1,0:T(8,128)S(1)}, u32[]{:S(2)}, u32[]{:S(2)}) %collective-permute-start.27) | collective-permute-done | bytes 196640 | tf_op jit(solution)/shard_map/ppermute | solution.py:57
  135.0 0.8 maximum_dynamic-update-slice_fusion.3
  (73 shorter events, 2.8 us)
Async XLA Ops:
  0.0 1.3 copy-start.7
  1.3 3.7 %copy-start.8 = (s32[4,24]{1,0:T(4,128)S(1)}, s32[4,24]{1,0:T(4,128)}, u32[]{:S(2)}) copy-start(s32[4,24]{1,0:T(4,128)} %param.9) | copy-start | bytes 1156
  2.7 2.5 %copy-start.6 = (f32[128,3072]{1,0:T(8,128)S(1)}, f32[128,3072]{1,0:T(8,128)}, u32[]{:S(2)}) copy-start(f32[128,3072]{1,0:T(8,128)} %param.8) | copy-start | bytes 4718596
  2.7 28.3 %collective-permute-start.14 = (f32[384,768]{1,0:T(8,128)}, f32[384,768]{1,0:T(8,128)}, u32[]{:S(2)}, u32[]{:S(2)}) collective-permute-start(f32[384,768]{1,0:T(8,128)} %bitcast_multiply_fusion.1), channel_id=1, source_target_pairs={{8,16},{16,8},{9,17},{17,9},{10,18},{18,10},{11,19},{19,11},{12,20... | collective-permute-start | bytes 3538952 | tf_op jit(solution)/shard_map/ppermute | solution.py:29
  4.5 27.8 %collective-permute-start.2 = (f32[384,768]{1,0:T(8,128)}, f32[384,768]{1,0:T(8,128)}, u32[]{:S(2)}, u32[]{:S(2)}) collective-permute-start(f32[384,768]{1,0:T(8,128)} %bitcast_multiply_fusion.1), channel_id=1, source_target_pairs={{0,1},{1,0},{2,3},{3,2},{4,5},{5,4},{6,7},{7,6},{8,9},{9,8},{10,11... | collective-permute-start | bytes 3538952 | tf_op jit(solution)/shard_map/ppermute | solution.py:57
  5.5 1.1 copy-start
  6.7 12.3 %collective-permute-start = (f32[128,768]{1,0:T(8,128)S(1)}, f32[128,768]{1,0:T(8,128)S(1)}, u32[]{:S(2)}, u32[]{:S(2)}) collective-permute-start(f32[128,768]{1,0:T(8,128)S(1)} %get-tuple-element.17), channel_id=1, source_target_pairs={{0,4},{1,5},{2,6},{3,7},{4,0},{5,1},{6,2},{7,3},{8,12},{9,13},{10,... | collective-permute-start | bytes 1179656 | tf_op jit(solution)/shard_map/ppermute | solution.py:57
  9.2 12.5 %collective-permute-start.1 = (f32[128,768]{1,0:T(8,128)S(1)}, f32[128,768]{1,0:T(8,128)S(1)}, u32[]{:S(2)}, u32[]{:S(2)}) collective-permute-start(f32[128,768]{1,0:T(8,128)S(1)} %get-tuple-element.15), channel_id=1, source_target_pairs={{0,2},{1,3},{2,0},{3,1},{4,6},{5,7},{6,4},{7,5},{8,10},{9,11},{10,... | collective-permute-start | bytes 1179656 | tf_op jit(solution)/shard_map/ppermute | solution.py:57
  10.7 30.6 %collective-permute-start.8 = (f32[384,768]{1,0:T(8,128)}, f32[384,768]{1,0:T(8,128)}, u32[]{:S(2)}, u32[]{:S(2)}) collective-permute-start(f32[384,768]{1,0:T(8,128)} %bitcast_multiply_fusion.1), channel_id=1, source_target_pairs={{0,8},{16,24},{8,0},{24,16},{1,9},{17,25},{9,1},{25,17},{2,10},{18... | collective-permute-start | bytes 3538952 | tf_op jit(solution)/shard_map/ppermute | solution.py:29
  19.0 12.0 %collective-permute-start.3 = (f32[128,768]{1,0:T(8,128)S(1)}, f32[128,768]{1,0:T(8,128)S(1)}, u32[]{:S(2)}, u32[]{:S(2)}) collective-permute-start(f32[128,768]{1,0:T(8,128)S(1)} %get-tuple-element.16), channel_id=1, source_target_pairs={{0,6},{1,7},{2,4},{3,5},{4,2},{5,3},{6,0},{7,1},{8,14},{9,15},{10,... | collective-permute-start | bytes 1179656 | tf_op jit(solution)/shard_map/ppermute | solution.py:57
  31.0 34.8 %collective-permute-start.15 = (f32[384,768]{1,0:T(8,128)}, f32[384,768]{1,0:T(8,128)}, u32[]{:S(2)}, u32[]{:S(2)}) collective-permute-start(f32[384,768]{1,0:T(8,128)} %collective-permute-done.14), channel_id=1, source_target_pairs={{8,0},{16,24},{9,1},{17,25},{10,2},{18,26},{11,3},{19,27},{12,4},{... | collective-permute-start | bytes 3538952 | tf_op jit(solution)/shard_map/ppermute | solution.py:33
  36.3 10.5 %collective-permute-start.4 = (f32[128,768]{1,0:T(8,128)}, f32[128,768]{1,0:T(8,128)}, u32[]{:S(2)}, u32[]{:S(2)}) collective-permute-start(f32[128,768]{1,0:T(8,128)} %get-tuple-element.32), channel_id=1, source_target_pairs={{0,2},{1,3},{2,0},{3,1},{4,6},{5,7},{6,4},{7,5},{8,10},{9,11},{10,... | collective-permute-start | bytes 1179656 | tf_op jit(solution)/shard_map/ppermute | solution.py:57
  37.8 10.0 %collective-permute-start.6 = (f32[128,768]{1,0:T(8,128)}, f32[128,768]{1,0:T(8,128)}, u32[]{:S(2)}, u32[]{:S(2)}) collective-permute-start(f32[128,768]{1,0:T(8,128)} %get-tuple-element.33), channel_id=1, source_target_pairs={{0,4},{1,5},{2,6},{3,7},{4,0},{5,1},{6,2},{7,3},{8,12},{9,13},{10,... | collective-permute-start | bytes 1179656 | tf_op jit(solution)/shard_map/ppermute | solution.py:57
  41.3 26.0 %collective-permute-start.21 = (f32[384,768]{1,0:T(8,128)}, f32[384,768]{1,0:T(8,128)}, u32[]{:S(2)}, u32[]{:S(2)}) collective-permute-start(f32[384,768]{1,0:T(8,128)} %collective-permute-done.8), channel_id=1, source_target_pairs={{8,16},{16,8},{9,17},{17,9},{10,18},{18,10},{11,19},{19,11},{12,20... | collective-permute-start | bytes 3538952 | tf_op jit(solution)/shard_map/ppermute | solution.py:29
  43.0 25.8 %collective-permute-start.9 = (f32[384,768]{1,0:T(8,128)}, f32[384,768]{1,0:T(8,128)}, u32[]{:S(2)}, u32[]{:S(2)}) collective-permute-start(f32[384,768]{1,0:T(8,128)} %collective-permute-done.8), channel_id=1, source_target_pairs={{0,1},{1,0},{2,3},{3,2},{4,5},{5,4},{6,7},{7,6},{8,9},{9,8},{10,11... | collective-permute-start | bytes 3538952 | tf_op jit(solution)/shard_map/ppermute | solution.py:57
  44.0 1.3 copy-start.1
  44.1 1.3 copy-start.3
  45.4 5.3 %copy-start.11 = (s32[4]{0:T(128)S(1)}, s32[4]{0:T(128)}, u32[]{:S(2)}) copy-start(s32[4]{0:T(128)} %constant.72.clone) | copy-start | bytes 52
  45.4 6.4 %copy-start.10 = (s32[4]{0:T(128)S(1)}, s32[4]{0:T(128)}, u32[]{:S(2)}) copy-start(s32[4]{0:T(128)} %constant.73.clone) | copy-start | bytes 52
  45.4 7.7 %copy-start.9 = (s32[4]{0:T(128)S(1)}, s32[4]{0:T(128)}, u32[]{:S(2)}) copy-start(s32[4]{0:T(128)} %constant.74.clone) | copy-start | bytes 52
  49.0 5.9 %collective-permute-start.5 = (f32[64,768]{1,0:T(8,128)S(1)}, f32[64,768]{1,0:T(8,128)S(1)}, u32[]{:S(2)}, u32[]{:S(2)}) collective-permute-start(f32[64,768]{1,0:T(8,128)S(1)} %slice.169), channel_id=1, source_target_pairs={{0,4},{1,5},{2,6},{3,7},{4,0},{5,1},{6,2},{7,3},{8,12},{9,13},{10,... | collective-permute-start | bytes 589832 | tf_op jit(solution)/shard_map/ppermute | solution.py:57
  54.4 18.7 %collective-permute-start.7 = (f32[64,768]{1,0:T(8,128)S(1)}, f32[64,768]{1,0:T(8,128)S(1)}, u32[]{:S(2)}, u32[]{:S(2)}) collective-permute-start(f32[64,768]{1,0:T(8,128)S(1)} %slice.173), channel_id=1, source_target_pairs={{0,2},{1,3},{2,0},{3,1},{4,6},{5,7},{6,4},{7,5},{8,10},{9,11},{10,... | collective-permute-start | bytes 589832 | tf_op jit(solution)/shard_map/ppermute | solution.py:57
  67.2 31.7 %collective-permute-start.16 = (f32[384,768]{1,0:T(8,128)S(1)}, f32[384,768]{1,0:T(8,128)S(1)}, u32[]{:S(2)}, u32[]{:S(2)}) collective-permute-start(f32[384,768]{1,0:T(8,128)S(1)} %broadcast_select_fusion.1), channel_id=1, source_target_pairs={{0,1},{1,0},{2,3},{3,2},{4,5},{5,4},{6,7},{7,6},{8,9},{9,8},{10,11... | collective-permute-start | bytes 3538952 | tf_op jit(solution)/shard_map/ppermute | solution.py:57
  67.3 31.4 %collective-permute-start.22 = (f32[384,768]{1,0:T(8,128)}, f32[384,768]{1,0:T(8,128)S(1)}, u32[]{:S(2)}, u32[]{:S(2)}) collective-permute-start(f32[384,768]{1,0:T(8,128)} %collective-permute-done.21), channel_id=1, source_target_pairs={{8,0},{16,24},{9,1},{17,25},{10,2},{18,26},{11,3},{19,27},{12,4},{... | collective-permute-start | bytes 3538952 | tf_op jit(solution)/shard_map/ppermute | solution.py:33
  72.0 11.6 %collective-permute-start.10 = (f32[128,768]{1,0:T(8,128)S(1)}, f32[128,768]{1,0:T(8,128)S(1)}, u32[]{:S(2)}, u32[]{:S(2)}) collective-permute-start(f32[128,768]{1,0:T(8,128)S(1)} %get-tuple-element.28), channel_id=1, source_target_pairs={{0,2},{1,3},{2,0},{3,1},{4,6},{5,7},{6,4},{7,5},{8,10},{9,11},{10,... | collective-permute-start | bytes 1179656 | tf_op jit(solution)/shard_map/ppermute | solution.py:57
  72.6 11.2 %collective-permute-start.12 = (f32[128,768]{1,0:T(8,128)S(1)}, f32[128,768]{1,0:T(8,128)S(1)}, u32[]{:S(2)}, u32[]{:S(2)}) collective-permute-start(f32[128,768]{1,0:T(8,128)S(1)} %get-tuple-element.29), channel_id=1, source_target_pairs={{0,4},{1,5},{2,6},{3,7},{4,0},{5,1},{6,2},{7,3},{8,12},{9,13},{10,... | collective-permute-start | bytes 1179656 | tf_op jit(solution)/shard_map/ppermute | solution.py:57
  73.1 0.9 copy-start.2
  73.2 1.0 copy-start.4
  83.9 17.7 %collective-permute-start.11 = (f32[64,768]{1,0:T(8,128)S(1)}, f32[64,768]{1,0:T(8,128)S(1)}, u32[]{:S(2)}, u32[]{:S(2)}) collective-permute-start(f32[64,768]{1,0:T(8,128)S(1)} %slice.177), channel_id=1, source_target_pairs={{0,4},{1,5},{2,6},{3,7},{4,0},{5,1},{6,2},{7,3},{8,12},{9,13},{10,... | collective-permute-start | bytes 589832 | tf_op jit(solution)/shard_map/ppermute | solution.py:57
  84.5 17.1 %collective-permute-start.13 = (f32[64,768]{1,0:T(8,128)S(1)}, f32[64,768]{1,0:T(8,128)S(1)}, u32[]{:S(2)}, u32[]{:S(2)}) collective-permute-start(f32[64,768]{1,0:T(8,128)S(1)} %slice.181), channel_id=1, source_target_pairs={{0,2},{1,3},{2,0},{3,1},{4,6},{5,7},{6,4},{7,5},{8,10},{9,11},{10,... | collective-permute-start | bytes 589832 | tf_op jit(solution)/shard_map/ppermute | solution.py:57
  98.8 14.2 %collective-permute-start.23 = (f32[384,768]{1,0:T(8,128)S(1)}, f32[384,768]{1,0:T(8,128)S(1)}, u32[]{:S(2)}, u32[]{:S(2)}) collective-permute-start(f32[384,768]{1,0:T(8,128)S(1)} %broadcast_select_fusion), channel_id=1, source_target_pairs={{0,1},{1,0},{2,3},{3,2},{4,5},{5,4},{6,7},{7,6},{8,9},{9,8},{10,11... | collective-permute-start | bytes 3538952 | tf_op jit(solution)/shard_map/ppermute | solution.py:57
  100.5 11.6 %collective-permute-start.17 = (f32[128,768]{1,0:T(8,128)S(1)}, f32[128,768]{1,0:T(8,128)S(1)}, u32[]{:S(2)}, u32[]{:S(2)}) collective-permute-start(f32[128,768]{1,0:T(8,128)S(1)} %get-tuple-element.24), channel_id=1, source_target_pairs={{0,2},{1,3},{2,0},{3,1},{4,6},{5,7},{6,4},{7,5},{8,10},{9,11},{10,... | collective-permute-start | bytes 1179656 | tf_op jit(solution)/shard_map/ppermute | solution.py:57
  101.1 11.2 %collective-permute-start.19 = (f32[128,768]{1,0:T(8,128)S(1)}, f32[128,768]{1,0:T(8,128)S(1)}, u32[]{:S(2)}, u32[]{:S(2)}) collective-permute-start(f32[128,768]{1,0:T(8,128)S(1)} %get-tuple-element.25), channel_id=1, source_target_pairs={{0,4},{1,5},{2,6},{3,7},{4,0},{5,1},{6,2},{7,3},{8,12},{9,13},{10,... | collective-permute-start | bytes 1179656 | tf_op jit(solution)/shard_map/ppermute | solution.py:57
  112.5 7.4 %collective-permute-start.18 = (f32[64,768]{1,0:T(8,128)S(1)}, f32[64,768]{1,0:T(8,128)S(1)}, u32[]{:S(2)}, u32[]{:S(2)}) collective-permute-start(f32[64,768]{1,0:T(8,128)S(1)} %slice.185), channel_id=1, source_target_pairs={{0,4},{1,5},{2,6},{3,7},{4,0},{5,1},{6,2},{7,3},{8,12},{9,13},{10,... | collective-permute-start | bytes 589832 | tf_op jit(solution)/shard_map/ppermute | solution.py:57
  114.6 12.1 %collective-permute-start.24 = (f32[128,768]{1,0:T(8,128)S(1)}, f32[128,768]{1,0:T(8,128)S(1)}, u32[]{:S(2)}, u32[]{:S(2)}) collective-permute-start(f32[128,768]{1,0:T(8,128)S(1)} %get-tuple-element.20), channel_id=1, source_target_pairs={{0,2},{1,3},{2,0},{3,1},{4,6},{5,7},{6,4},{7,5},{8,10},{9,11},{10,... | collective-permute-start | bytes 1179656 | tf_op jit(solution)/shard_map/ppermute | solution.py:57
  116.2 11.0 %collective-permute-start.26 = (f32[128,768]{1,0:T(8,128)S(1)}, f32[128,768]{1,0:T(8,128)S(1)}, u32[]{:S(2)}, u32[]{:S(2)}) collective-permute-start(f32[128,768]{1,0:T(8,128)S(1)} %get-tuple-element.21), channel_id=1, source_target_pairs={{0,4},{1,5},{2,6},{3,7},{4,0},{5,1},{6,2},{7,3},{8,12},{9,13},{10,... | collective-permute-start | bytes 1179656 | tf_op jit(solution)/shard_map/ppermute | solution.py:57
  117.8 11.3 %collective-permute-start.20 = (f32[64,768]{1,0:T(8,128)S(1)}, f32[64,768]{1,0:T(8,128)S(1)}, u32[]{:S(2)}, u32[]{:S(2)}) collective-permute-start(f32[64,768]{1,0:T(8,128)S(1)} %slice.189), channel_id=1, source_target_pairs={{0,2},{1,3},{2,0},{3,1},{4,6},{5,7},{6,4},{7,5},{8,10},{9,11},{10,... | collective-permute-start | bytes 589832 | tf_op jit(solution)/shard_map/ppermute | solution.py:57
  127.3 5.9 %collective-permute-start.25 = (f32[64,768]{1,0:T(8,128)S(1)}, f32[64,768]{1,0:T(8,128)S(1)}, u32[]{:S(2)}, u32[]{:S(2)}) collective-permute-start(f32[64,768]{1,0:T(8,128)S(1)} %slice.193), channel_id=1, source_target_pairs={{0,4},{1,5},{2,6},{3,7},{4,0},{5,1},{6,2},{7,3},{8,12},{9,13},{10,... | collective-permute-start | bytes 589832 | tf_op jit(solution)/shard_map/ppermute | solution.py:57
  129.2 5.8 %copy-start.5 = (f32[128,3072]{1,0:T(8,128)}, f32[128,3072]{1,0:T(8,128)S(1)}, u32[]{:S(2)}) copy-start(f32[128,3072]{1,0:T(8,128)S(1)} %maximum_dynamic-update-slice_fusion.2) | copy-start | bytes 4718596
  129.2 5.7 %collective-permute-start.27 = (f32[64,768]{1,0:T(8,128)S(1)}, f32[64,768]{1,0:T(8,128)S(1)}, u32[]{:S(2)}, u32[]{:S(2)}) collective-permute-start(f32[64,768]{1,0:T(8,128)S(1)} %slice.197), channel_id=1, source_target_pairs={{0,2},{1,3},{2,0},{3,1},{4,6},{5,7},{6,4},{7,5},{8,10},{9,11},{10,... | collective-permute-start | bytes 589832 | tf_op jit(solution)/shard_map/ppermute | solution.py:57

commit v2 on v1

--- a/solution.py
+++ b/solution.py
@@ -14,7 +14,11 @@
     return (values.reshape(tile_r, tile_rows, tile_c, TILE_V) * scale).reshape(values.shape)
 
 
-def line_blocks(own, nodes):
+def after(value, *earlier):
+    return lax.optimization_barrier((value,) + earlier)[0]
+
+
+def line_blocks(own, nodes, split_last):
     here = lax.axis_index("occ")
     blocks = [own]
     origins = [list(range(nodes))]
@@ -24,15 +28,22 @@
         place = here % (2 * size)
         dist = jnp.where(place < size, size - 1 - place, place - size)
         middles = [g * 2 * size + size for g in range(nodes // (2 * size))]
-        for block, origin in zip(blocks, origins):
+        for n, (block, origin) in enumerate(zip(blocks, origins)):
             pairs = [(m - 1, m) for m in middles] + [(m, m - 1) for m in middles]
-            moving = lax.ppermute(block, "occ", pairs)
-            got = moving
-            for hop in range(1, size):
-                pairs = [(m - hop, m - hop - 1) for m in middles] + [(m + hop - 1, m + hop) for m in middles]
-                moving = lax.ppermute(moving, "occ", pairs)
-                got = jnp.where(dist == hop, moving, got)
-            fresh.append(got)
+            got = lax.ppermute(block, "occ", pairs)
+            parts = [got]
+            if split_last and size * 2 == nodes and n == size - 1:
+                mid = got.shape[1] // 2
+                parts = [got[:, :mid], got[:, mid:]]
+            whole = []
+            for moving in parts:
+                got = moving
+                for hop in range(1, size):
+                    pairs = [(m - hop, m - hop - 1) for m in middles] + [(m + hop - 1, m + hop) for m in middles]
+                    moving = lax.ppermute(moving, "occ", pairs)
+                    got = jnp.where(dist == hop, moving, got)
+                whole.append(got)
+            fresh.append(whole if len(whole) > 1 else whole[0])
             table = [0] * nodes
             for m in middles:
                 for k in range(size):
@@ -51,20 +62,25 @@
     half = rows // 2
     groups = n_vir // 2
     width = integrals.shape[1]
-    depth = 2 * integrals.shape[0]
+    own_depth = integrals.shape[0]
 
     def swap(x, bits):
         return lax.ppermute(x, "vir", [(i, i ^ bits) for i in range(n_vir)])
 
     me = lax.axis_index("vir")
+    low = me % 2
+    blocks, origins = line_blocks(integrals, n_occ, True)
+
+    mask_own = lax.all_gather(int_mask, "occ", axis=0)
+    mask_pair = jnp.concatenate([mask_own, swap(mask_own, 1)], axis=1)
+
     kept = masked(amplitudes, amp_mask, TILE_O)
-    weighted = masked(integrals, int_mask, TILE_V)
-    blocks, origins = line_blocks(weighted, n_occ)
-
     rel = []
     for r in range(groups):
-        start = ((me // 2) ^ r) * depth
-        part = lax.dynamic_slice_in_dim(kept, start, depth, axis=1)
+        start = ((me // 2) ^ r) * (2 * own_depth)
+        mine = lax.dynamic_slice_in_dim(kept, start + low * own_depth, own_depth, axis=1)
+        others = lax.dynamic_slice_in_dim(kept, start + (1 - low) * own_depth, own_depth, axis=1)
+        part = jnp.concatenate([mine, others], axis=1)
         rel.append(part if r == 0 else swap(part, 2 * r))
 
     bits = []
@@ -77,15 +93,27 @@
     lhs_away = jnp.concatenate([rel[r][cut[h]] for h in range(2) for r in away[h]], axis=0)
     lhs_near = jnp.concatenate([rel[r][cut[h]] for h in range(2) for r in near[h]], axis=0)
 
-    low = me % 2
+    pieces = []
+    for block, origin in zip(blocks, origins):
+        place = jnp.array(origin, jnp.int32)[lax.axis_index("occ")]
+        mask = lax.dynamic_index_in_dim(mask_pair, place, 0, keepdims=False)
+        parts = block if isinstance(block, list) else [block]
+        offset = 0
+        for part in parts:
+            tiles = part.shape[1] // TILE_V
+            pieces.append((part, mask[:, offset // TILE_V : offset // TILE_V + tiles], place * width + offset))
+            offset += part.shape[1]
+
     out = jnp.zeros((rows, n_occ * width), jnp.float32)
-    for block, origin in zip(blocks, origins):
+    previous = None
+    for block, mask, col in pieces:
+        if previous is not None:
+            block = after(block, previous)
         other = swap(block, 1)
-        first = jnp.where(low == 0, block, other)
-        second = jnp.where(low == 0, other, block)
-        rhs = jnp.concatenate([first, second], axis=0)
+        rhs = masked(jnp.concatenate([block, other], axis=0), mask, TILE_V)
         sent = jnp.dot(lhs_away, rhs, precision=HIGH, preferred_element_type=jnp.float32)
         stay = jnp.dot(lhs_near, rhs, precision=HIGH, preferred_element_type=jnp.float32)
+        previous = sent
         count = groups // 2
         done = []
         for h in range(2):
@@ -101,7 +129,6 @@
                     held[r ^ bit] = held[r ^ bit] + got[i * half : (i + 1) * half]
                     del held[r]
             done.append(held[0])
-        col = jnp.array(origin, jnp.int32)[lax.axis_index("occ")] * width
         out = lax.dynamic_update_slice(out, jnp.concatenate(done, axis=0), (0, col))
     return out
 

time: 136 us -> 187 us (1.38)
  blocking collectives: 0 us -> 34.1 us
  matrix products: 10.8 us -> 19.8 us
  between operations: 2.38 us -> 8.3 us
  local copies, waits for them, and re-layouts: 6.98 us -> 12.6 us
  waiting for transfers between devices: 71.6 us -> 66.1 us
  starting transfers between devices: 33.5 us -> 38.1 us
  other arithmetic: 10.6 us -> 6.93 us
    all_gather x0 -> x1, blocking collectives: none -> 34.1 us  [per_device(): mask_own = lax.all_gather(int_mask, 'occ', axis=0)]
    ppermute x23 -> x29, waiting for transfers between devices: 46.3 us -> 30.9 us  [swap(): return lax.ppermute(x, 'vir', [(i, i ^ bits) for i in range(n_vir)])]
    ppermute x2 -> x3, waiting for transfers between devices: 23.4 us -> 35.2 us  [line_blocks(): moving = lax.ppermute(moving, 'occ', pairs)]
    ppermute x23 -> x29, starting transfers between devices: 23.7 us -> 30 us  [swap(): return lax.ppermute(x, 'vir', [(i, i ^ bits) for i in range(n_vir)])]
    dot_general x4 -> x5, matrix products: 5.37 us -> 10.1 us  [per_device(): jnp.dot(lhs_near, rhs, precision=HIGH, preferred_element_type=jnp.float32)]
    dot_general x4 -> x5, matrix products: 5.38 us -> 9.72 us  [per_device(): jnp.dot(lhs_away, rhs, precision=HIGH, preferred_element_type=jnp.float32)]
    select_n x4 -> x0, other arithmetic: 3.88 us -> none  [per_device(): first = jnp.where(low == 0, block, other)]
    ppermute x3, starting transfers between devices: 7.03 us -> 4 us  [line_blocks(): got = lax.ppermute(block, 'occ', pairs)]
  transfers between devices with their start and end apart: 28 -> 35, of which waited for: 17 -> 18; matrix products, arithmetic and copies ran while one was open for 17% -> 20% of each run, Pallas kernels for 0% -> 0%
where the time goes in v2:
time: 187 us; the launch traced here: 186 us
  waiting for transfers between devices  66.1 us (35%)
  starting transfers between devices  38.1 us (20%)
  blocking collectives  34.1 us (18%)
  matrix products  19.8 us (11%)
  local copies, waits for them, and re-layouts  12.6 us (7%)
  between operations  8.3 us (4%)
  other arithmetic  6.93 us (4%)
    ppermute x3, waiting for transfers between devices, line_blocks(): moving = lax.ppermute(moving, 'occ', pairs)  35.2 us
    all_gather x1, blocking collectives, per_device(): mask_own = lax.all_gather(int_mask, 'occ', axis=0)  34.1 us
    ppermute x29, waiting for transfers between devices, swap(): return lax.ppermute(x, 'vir', [(i, i ^ bits) for i in range(n_vir)])  30.9 us
    ppermute x29, starting transfers between devices, swap(): return lax.ppermute(x, 'vir', [(i, i ^ bits) for i in range(n_vir)])  30 us
    dot_general x5, matrix products, per_device(): jnp.dot(lhs_near, rhs, precision=HIGH, preferred_element_type=jnp.float32)  10.1 us
    dot_general x5, matrix products, per_device(): jnp.dot(lhs_away, rhs, precision=HIGH, preferred_element_type=jnp.float32)  9.72 us
    ppermute x3, starting transfers between devices, line_blocks(): moving = lax.ppermute(moving, 'occ', pairs)  4.06 us
    ppermute x3, starting transfers between devices, line_blocks(): got = lax.ppermute(block, 'occ', pairs)  4 us
  transfers between devices with their start and end apart: 35, of which 18 were waited for; matrix products, arithmetic and copies ran while one was open for 20% of the time, Pallas kernels for 0%

profile of v2, /device:TPU:0, one launch (start us, length us, event | category | flops | bytes accessed | tf_op | source)
XLA Modules:
  0.0 186.0 jit_solution(8422984621011575388)
XLA Ops:
  0.5 0.7 convert_element_type.39
  1.8 1.0 constant_dynamic-slice_fusion.7
  2.9 4.0 %collective-permute-start.4 = (f32[128,768]{1,0:T(8,128)S(1)}, f32[128,768]{1,0:T(8,128)S(1)}, u32[]{:S(2)}, u32[]{:S(2)}) collective-permute-start(f32[128,768]{1,0:T(8,128)S(1)} %pad_maximum_fusion.3), channel_id=1, source_target_pairs={{0,6},{1,7},{2,4},{3,5},{4,2},{5,3},{6,0},{7,1},{8,14},{9,15},{10,... | collective-permute-start | bytes 1179656 | tf_op jit(solution)/shard_map/ppermute | solution.py:68
  6.8 1.6 collective-permute-start.9
  8.4 34.1 %all-gather.1 = s32[4,3,6]{2,1,0:T(4,128)S(1)} all-gather(s32[1,3,6]{2,1,0:T(4,128)S(1)} %bitcast.59), channel_id=2, replica_groups=mesh['occ'=4,'vir'=8] {'occ'}, dimensions={0}, use_global_device_ids=true | all-gather | bytes 360 | tf_op jit(solution)/shard_map/all_gather | solution.py:74
  45.0 0.7 dynamic_slice.59
  50.6 1.7 collective-permute-start.15
  53.0 1.1 collective-permute-done
  54.1 0.7 fusion.45
  54.8 8.9 %collective-permute-done.1 = f32[128,768]{1,0:T(8,128)S(1)} collective-permute-done((f32[128,768]{1,0:T(8,128)S(1)}, f32[128,768]{1,0:T(8,128)S(1)}, u32[]{:S(2)}, u32[]{:S(2)}) %collective-permute-start.1) | collective-permute-done | bytes 393248 | tf_op jit(solution)/shard_map/ppermute | solution.py:68
  63.7 0.7 fusion.46
  65.1 3.2 %fusion.8 = f32[256,768]{1,0:T(8,128)S(1)} fusion(f32[96,8,6,128]{3,2,1,0:T(8,128)S(1)} %bitcast.48, f32[384,768]{1,0:T(8,128)} %collective-permute-done.2, f32[384,768]{1,0:T(8,128)} %param.10, f32[64,768]{1,0:T(8,128)S(1)} %get-tuple-element.48, f32[64,768]{1,0:T(8,128)S(1)} %get-tuple-element.44, f32[64,768]{1,0:T(8,128)S(1)} %get-tuple-element.47, ...), kind=kOutput, calls=%fused_computation.53 | convolution fusion | flops 907739136 | bytes 6291456 | tf_op jit(solution)/shard_map/dot_general | solution.py:114
  68.3 0.9 fusion.42
  69.8 1.5 collective-permute-start.7
  71.3 0.7 fusion.7
  74.0 1.3 collective-permute-start.16
  75.3 3.6 %fusion.9 = f32[256,768]{1,0:T(8,128)S(1)} fusion(f32[96,8,6,128]{3,2,1,0:T(8,128)S(1)} %bitcast.49, f32[384,768]{1,0:T(8,128)} %collective-permute-done.2, f32[384,768]{1,0:T(8,128)} %param.10, f32[128,384]{1,0:T(8,128)} %get-tuple-element.20, f32[128,384]{1,0:T(8,128)} %get-tuple-element.13, f32[64,768]{1,0:T(8,128)} %get-tuple-element.45, ...), kind=kOutput, calls=%fused_computation.54 | convolution fusion | flops 908918784 | bytes 6488064 | tf_op jit(solution)/shard_map/dot_general | solution.py:115
  78.9 1.1 collective-permute-done.5
  80.3 1.2 slice_add_fusion.5
  81.5 0.7 slice.223
  82.2 1.5 collective-permute-start.8
  84.9 1.3 copy.35
  86.2 1.6 copy.16
  87.8 0.7 collective-permute-start.22
  88.6 1.6 collective-permute-start.6
  90.2 0.9 slice_add_fusion.14
  91.1 3.2 %collective-permute-done.6 = f32[64,768]{1,0:T(8,128)S(1)} collective-permute-done((f32[64,768]{1,0:T(8,128)S(1)}, f32[64,768]{1,0:T(8,128)S(1)}, u32[]{:S(2)}, u32[]{:S(2)}) %collective-permute-start.6) | collective-permute-done | bytes 196640 | tf_op jit(solution)/shard_map/ppermute | solution.py:68
  94.9 0.6 copy-done.1
  95.6 3.2 %fusion.10 = f32[256,768]{1,0:T(8,128)S(1)} fusion(f32[96,8,6,128]{3,2,1,0:T(8,128)S(1)} %bitcast.50, f32[384,768]{1,0:T(8,128)} %collective-permute-done.10, f32[384,768]{1,0:T(8,128)} %collective-permute-done.9, f32[64,768]{1,0:T(8,128)S(1)} %get-tuple-element.48, f32[64,768]{1,0:T(8,128)S(1)} %copy-done.1, f32[64,768]{1,0:T(8,128)S(1)} %get-tuple-element.47, ...), kind=kOutput, calls=%fused_computation.55 | convolution fusion | flops 907739136 | bytes 6291456 | tf_op jit(solution)/shard_map/dot_general | solution.py:114
  99.5 1.5 collective-permute-start.13
  101.0 8.1 %collective-permute-done.16 = f32[384,768]{1,0:T(8,128)} collective-permute-done((f32[384,768]{1,0:T(8,128)}, f32[384,768]{1,0:T(8,128)}, u32[]{:S(2)}, u32[]{:S(2)}) %collective-permute-start.16) | collective-permute-done | bytes 1179680 | tf_op jit(solution)/shard_map/ppermute | solution.py:43
  109.2 1.4 broadcast_select_fusion
  110.7 1.5 collective-permute-start.29
  112.2 3.2 %fusion.11 = f32[256,768]{1,0:T(8,128)S(1)} fusion(f32[96,8,6,128]{3,2,1,0:T(8,128)S(1)} %bitcast.51, f32[384,768]{1,0:T(8,128)} %collective-permute-done.10, f32[384,768]{1,0:T(8,128)} %collective-permute-done.9, f32[128,384]{1,0:T(8,128)S(1)} %copy-done.9, f32[128,384]{1,0:T(8,128)S(1)} %copy-done.7, f32[64,768]{1,0:T(8,128)S(1)} %copy-done.11, ...), kind=kOutput, calls=%fused_computation.56 | convolution fusion | flops 908918784 | bytes 6488064 | tf_op jit(solution)/shard_map/dot_general | solution.py:115
  116.2 1.6 collective-permute-start.12
  117.8 18.9 %collective-permute-done.29 = f32[384,384]{1,0:T(8,128)S(1)} collective-permute-done((f32[384,384]{1,0:T(8,128)S(1)}, f32[384,384]{1,0:T(8,128)S(1)}, u32[]{:S(2)}, u32[]{:S(2)}) %collective-permute-start.29) | collective-permute-done | bytes 589856 | tf_op jit(solution)/shard_map/ppermute | solution.py:43
  136.8 1.3 collective-permute-start.23
  138.5 1.6 fusion.12
  140.2 1.6 collective-permute-start.18
  141.8 1.5 collective-permute-start.20
  143.3 8.2 %collective-permute-done.23 = f32[384,384]{1,0:T(8,128)S(1)} collective-permute-done((f32[384,384]{1,0:T(8,128)S(1)}, f32[384,384]{1,0:T(8,128)S(1)}, u32[]{:S(2)}, u32[]{:S(2)}) %collective-permute-start.23) | collective-permute-done | bytes 589856 | tf_op jit(solution)/shard_map/ppermute | solution.py:43
  151.7 1.6 fusion.13
  153.4 1.5 collective-permute-start.21
  155.0 1.6 collective-permute-start.19
  156.6 0.8 fusion.5
  158.6 0.8 fusion.6
  159.4 1.7 collective-permute-done.21
  161.2 1.6 collective-permute-done.19
  162.8 2.2 %collective-permute-done.25 = f32[128,384]{1,0:T(8,128)S(1)} collective-permute-done((f32[128,384]{1,0:T(8,128)S(1)}, f32[128,384]{1,0:T(8,128)S(1)}, u32[]{:S(2)}, u32[]{:S(2)}) %collective-permute-start.25) | collective-permute-done | bytes 196640 | tf_op jit(solution)/shard_map/ppermute | solution.py:68
  165.0 1.3 collective-permute-done.27
  166.4 0.6 collective-permute-start.28
  167.0 1.6 collective-permute-start.26
  168.6 2.4 %collective-permute-done.28 = f32[64,384]{1,0:T(8,128)S(1)} collective-permute-done((f32[64,384]{1,0:T(8,128)S(1)}, f32[64,384]{1,0:T(8,128)S(1)}, u32[]{:S(2)}, u32[]{:S(2)}) %collective-permute-start.28) | collective-permute-done | bytes 98336 | tf_op jit(solution)/shard_map/ppermute | solution.py:68
  171.0 0.7 collective-permute-done.26
  171.7 0.8 fusion.3
  172.6 1.5 collective-permute-start.31
  174.2 1.5 collective-permute-start.33
  175.7 0.8 fusion.4
  176.5 1.8 collective-permute-done.31
  178.4 1.5 collective-permute-done.33
  180.6 1.6 collective-permute-start.32
  182.1 2.4 %collective-permute-done.34 = f32[64,384]{1,0:T(8,128)S(1)} collective-permute-done((f32[64,384]{1,0:T(8,128)S(1)}, f32[64,384]{1,0:T(8,128)S(1)}, u32[]{:S(2)}, u32[]{:S(2)}) %collective-permute-start.34) | collective-permute-done | bytes 98336 | tf_op jit(solution)/shard_map/ppermute | solution.py:68
  184.6 0.6 collective-permute-done.32
  185.3 0.7 maximum_dynamic-update-slice_fusion.4
  (118 shorter events, 11.2 us)
Async XLA Ops:
  0.0 1.4 copy-start.5
  0.0 64.4 %collective-permute-start.2 = (f32[384,768]{1,0:T(8,128)}, f32[384,768]{1,0:T(8,128)}, u32[]{:S(2)}, u32[]{:S(2)}) collective-permute-start(f32[384,768]{1,0:T(8,128)} %param.10), channel_id=1, source_target_pairs={{0,1},{1,0},{2,3},{3,2},{4,5},{5,4},{6,7},{7,6},{8,9},{9,8},{10,11... | collective-permute-start | bytes 3538952 | tf_op jit(solution)/shard_map/ppermute | solution.py:68
  1.8 6.6 %copy-start.13 = (s32[3,6]{1,0:T(4,128)S(1)}, s32[3,6]{1,0:T(4,128)}, u32[]{:S(2)}) copy-start(s32[3,6]{1,0:T(4,128)} %param.11) | copy-start | bytes 220
  2.8 40.3 %copy-start.16 = (s32[4]{0:T(128)S(1)}, s32[4]{0:T(128)}, u32[]{:S(2)}) copy-start(s32[4]{0:T(128)} %constant.83.clone) | copy-start | bytes 52
  2.8 42.2 %copy-start.15 = (s32[4]{0:T(128)S(1)}, s32[4]{0:T(128)}, u32[]{:S(2)}) copy-start(s32[4]{0:T(128)} %constant.81.clone) | copy-start | bytes 52
  2.8 44.2 %copy-start.14 = (s32[4]{0:T(128)S(1)}, s32[4]{0:T(128)}, u32[]{:S(2)}) copy-start(s32[4]{0:T(128)} %constant.82.clone) | copy-start | bytes 52
  2.9 49.5 %collective-permute-start.4 = (f32[128,768]{1,0:T(8,128)S(1)}, f32[128,768]{1,0:T(8,128)S(1)}, u32[]{:S(2)}, u32[]{:S(2)}) collective-permute-start(f32[128,768]{1,0:T(8,128)S(1)} %pad_maximum_fusion.3), channel_id=1, source_target_pairs={{0,6},{1,7},{2,4},{3,5},{4,2},{5,3},{6,0},{7,1},{8,14},{9,15},{10,... | collective-permute-start | bytes 1179656 | tf_op jit(solution)/shard_map/ppermute | solution.py:68
  6.8 67.1 %collective-permute-start.9 = (f32[384,768]{1,0:T(8,128)}, f32[384,768]{1,0:T(8,128)}, u32[]{:S(2)}, u32[]{:S(2)}) collective-permute-start(f32[384,768]{1,0:T(8,128)} %param.10), channel_id=1, source_target_pairs={{0,8},{16,24},{8,0},{24,16},{1,9},{17,25},{9,1},{25,17},{2,10},{18... | collective-permute-start | bytes 3538952 | tf_op jit(solution)/shard_map/ppermute | solution.py:33
  42.5 8.2 %collective-permute-start.3 = (s32[4,3,6]{2,1,0:T(4,128)S(1)}, s32[4,3,6]{2,1,0:T(4,128)S(1)}, u32[]{:S(2)}, u32[]{:S(2)}) collective-permute-start(s32[4,3,6]{2,1,0:T(4,128)S(1)} %all-gather.1), channel_id=1, source_target_pairs={{0,1},{1,0},{2,3},{3,2},{4,5},{5,4},{6,7},{7,6},{8,9},{9,8},{10,11... | collective-permute-start | bytes 872 | tf_op jit(solution)/shard_map/ppermute | solution.py:68
  42.5 11.6 %collective-permute-start = (f32[128,768]{1,0:T(8,128)S(1)}, f32[128,768]{1,0:T(8,128)S(1)}, u32[]{:S(2)}, u32[]{:S(2)}) collective-permute-start(f32[128,768]{1,0:T(8,128)S(1)} %pad_maximum_fusion.1), channel_id=1, source_target_pairs={{0,4},{1,5},{2,6},{3,7},{4,0},{5,1},{6,2},{7,3},{8,12},{9,13},{10,... | collective-permute-start | bytes 1179656 | tf_op jit(solution)/shard_map/ppermute | solution.py:68
  50.6 23.4 %collective-permute-start.15 = (f32[384,768]{1,0:T(8,128)}, f32[384,768]{1,0:T(8,128)}, u32[]{:S(2)}, u32[]{:S(2)}) collective-permute-start(f32[384,768]{1,0:T(8,128)} %param.10), channel_id=1, source_target_pairs={{8,16},{16,8},{9,17},{17,9},{10,18},{18,10},{11,19},{19,11},{12,20... | collective-permute-start | bytes 3538952 | tf_op jit(solution)/shard_map/ppermute | solution.py:33
  52.4 11.3 %collective-permute-start.1 = (f32[128,768]{1,0:T(8,128)S(1)}, f32[128,768]{1,0:T(8,128)S(1)}, u32[]{:S(2)}, u32[]{:S(2)}) collective-permute-start(f32[128,768]{1,0:T(8,128)S(1)} %pad_maximum_fusion.2), channel_id=1, source_target_pairs={{0,2},{1,3},{2,0},{3,1},{4,6},{5,7},{6,4},{7,5},{8,10},{9,11},{10,... | collective-permute-start | bytes 1179656 | tf_op jit(solution)/shard_map/ppermute | solution.py:68
  54.8 9.9 %copy-start = (f32[64,768]{1,0:T(8,128)}, f32[64,768]{1,0:T(8,128)S(1)}, u32[]{:S(2)}) copy-start(f32[64,768]{1,0:T(8,128)S(1)} %get-tuple-element.44) | copy-start | bytes 589828
  64.4 0.7 copy-start.2
  68.3 3.0 %copy-start.6 = (f32[128,384]{1,0:T(8,128)S(1)}, f32[128,384]{1,0:T(8,128)}, u32[]{:S(2)}) copy-start(f32[128,384]{1,0:T(8,128)} %get-tuple-element.13) | copy-start | bytes 589828
  68.3 3.0 %copy-start.8 = (f32[128,384]{1,0:T(8,128)S(1)}, f32[128,384]{1,0:T(8,128)}, u32[]{:S(2)}) copy-start(f32[128,384]{1,0:T(8,128)} %get-tuple-element.20) | copy-start | bytes 589828
  69.3 10.7 %collective-permute-start.5 = (f32[128,768]{1,0:T(8,128)}, f32[128,768]{1,0:T(8,128)}, u32[]{:S(2)}, u32[]{:S(2)}) collective-permute-start(f32[128,768]{1,0:T(8,128)} %get-tuple-element.33), channel_id=1, source_target_pairs={{0,2},{1,3},{2,0},{3,1},{4,6},{5,7},{6,4},{7,5},{8,10},{9,11},{10,... | collective-permute-start | bytes 1179656 | tf_op jit(solution)/shard_map/ppermute | solution.py:68
  69.8 10.5 %collective-permute-start.7 = (f32[128,768]{1,0:T(8,128)}, f32[128,768]{1,0:T(8,128)}, u32[]{:S(2)}, u32[]{:S(2)}) collective-permute-start(f32[128,768]{1,0:T(8,128)} %get-tuple-element.34), channel_id=1, source_target_pairs={{0,4},{1,5},{2,6},{3,7},{4,0},{5,1},{6,2},{7,3},{8,12},{9,13},{10,... | collective-permute-start | bytes 1179656 | tf_op jit(solution)/shard_map/ppermute | solution.py:68
  73.9 20.7 %collective-permute-start.10 = (f32[384,768]{1,0:T(8,128)}, f32[384,768]{1,0:T(8,128)}, u32[]{:S(2)}, u32[]{:S(2)}) collective-permute-start(f32[384,768]{1,0:T(8,128)} %collective-permute-done.9), channel_id=1, source_target_pairs={{0,1},{1,0},{2,3},{3,2},{4,5},{5,4},{6,7},{7,6},{8,9},{9,8},{10,11... | collective-permute-start | bytes 3538952 | tf_op jit(solution)/shard_map/ppermute | solution.py:68
  74.0 35.1 %collective-permute-start.16 = (f32[384,768]{1,0:T(8,128)}, f32[384,768]{1,0:T(8,128)}, u32[]{:S(2)}, u32[]{:S(2)}) collective-permute-start(f32[384,768]{1,0:T(8,128)} %collective-permute-done.15), channel_id=1, source_target_pairs={{8,0},{16,24},{9,1},{17,25},{10,2},{18,26},{11,3},{19,27},{12,4},{... | collective-permute-start | bytes 3538952 | tf_op jit(solution)/shard_map/ppermute | solution.py:43
  82.2 8.0 %collective-permute-start.8 = (f32[64,768]{1,0:T(8,128)}, f32[64,768]{1,0:T(8,128)}, u32[]{:S(2)}, u32[]{:S(2)}) collective-permute-start(f32[64,768]{1,0:T(8,128)} %slice.223), channel_id=1, source_target_pairs={{0,2},{1,3},{2,0},{3,1},{4,6},{5,7},{6,4},{7,5},{8,10},{9,11},{10,... | collective-permute-start | bytes 589832 | tf_op jit(solution)/shard_map/ppermute | solution.py:68
  87.8 22.8 %collective-permute-start.22 = (f32[384,768]{1,0:T(8,128)}, f32[384,768]{1,0:T(8,128)S(1)}, u32[]{:S(2)}, u32[]{:S(2)}) collective-permute-start(f32[384,768]{1,0:T(8,128)} %collective-permute-done.9), channel_id=1, source_target_pairs={{8,16},{16,8},{9,17},{17,9},{10,18},{18,10},{11,19},{19,11},{12,20... | collective-permute-start | bytes 3538952 | tf_op jit(solution)/shard_map/ppermute | solution.py:33
  88.6 5.8 %collective-permute-start.6 = (f32[64,768]{1,0:T(8,128)S(1)}, f32[64,768]{1,0:T(8,128)S(1)}, u32[]{:S(2)}, u32[]{:S(2)}) collective-permute-start(f32[64,768]{1,0:T(8,128)S(1)} %slice.219), channel_id=1, source_target_pairs={{0,4},{1,5},{2,6},{3,7},{4,0},{5,1},{6,2},{7,3},{8,12},{9,13},{10,... | collective-permute-start | bytes 589832 | tf_op jit(solution)/shard_map/ppermute | solution.py:68
  94.6 0.9 copy-start.1
  94.6 1.0 copy-start.3
  98.9 16.6 %collective-permute-start.11 = (f32[128,768]{1,0:T(8,128)S(1)}, f32[128,768]{1,0:T(8,128)S(1)}, u32[]{:S(2)}, u32[]{:S(2)}) collective-permute-start(f32[128,768]{1,0:T(8,128)S(1)} %get-tuple-element.29), channel_id=1, source_target_pairs={{0,2},{1,3},{2,0},{3,1},{4,6},{5,7},{6,4},{7,5},{8,10},{9,11},{10,... | collective-permute-start | bytes 1179656 | tf_op jit(solution)/shard_map/ppermute | solution.py:68
  99.5 12.7 %copy-start.7 = (f32[128,384]{1,0:T(8,128)S(1)}, f32[128,384]{1,0:T(8,128)}, u32[]{:S(2)}) copy-start(f32[128,384]{1,0:T(8,128)} %get-tuple-element.13) | copy-start | bytes 589828
  99.5 12.7 %copy-start.9 = (f32[128,384]{1,0:T(8,128)S(1)}, f32[128,384]{1,0:T(8,128)}, u32[]{:S(2)}) copy-start(f32[128,384]{1,0:T(8,128)} %get-tuple-element.20) | copy-start | bytes 589828
  99.5 12.7 %copy-start.10 = (f32[64,768]{1,0:T(8,128)S(1)}, f32[64,768]{1,0:T(8,128)}, u32[]{:S(2)}) copy-start(f32[64,768]{1,0:T(8,128)} %get-tuple-element.43) | copy-start | bytes 589828
  99.5 12.7 %copy-start.11 = (f32[64,768]{1,0:T(8,128)S(1)}, f32[64,768]{1,0:T(8,128)}, u32[]{:S(2)}) copy-start(f32[64,768]{1,0:T(8,128)} %get-tuple-element.45) | copy-start | bytes 589828
  99.5 12.7 %copy-start.12 = (f32[64,768]{1,0:T(8,128)S(1)}, f32[64,768]{1,0:T(8,128)}, u32[]{:S(2)}) copy-start(f32[64,768]{1,0:T(8,128)} %fusion.7) | copy-start | bytes 589828
  99.5 16.0 %collective-permute-start.13 = (f32[128,768]{1,0:T(8,128)S(1)}, f32[128,768]{1,0:T(8,128)S(1)}, u32[]{:S(2)}, u32[]{:S(2)}) collective-permute-start(f32[128,768]{1,0:T(8,128)S(1)} %get-tuple-element.30), channel_id=1, source_target_pairs={{0,4},{1,5},{2,6},{3,7},{4,0},{5,1},{6,2},{7,3},{8,12},{9,13},{10,... | collective-permute-start | bytes 1179656 | tf_op jit(solution)/shard_map/ppermute | solution.py:68
  110.6 27.7 %collective-permute-start.17 = (f32[384,768]{1,0:T(8,128)S(1)}, f32[384,768]{1,0:T(8,128)S(1)}, u32[]{:S(2)}, u32[]{:S(2)}) collective-permute-start(f32[384,768]{1,0:T(8,128)S(1)} %broadcast_select_fusion), channel_id=1, source_target_pairs={{0,1},{1,0},{2,3},{3,2},{4,5},{5,4},{6,7},{7,6},{8,9},{9,8},{10,11... | collective-permute-start | bytes 3538952 | tf_op jit(solution)/shard_map/ppermute | solution.py:68
  110.7 26.0 %collective-permute-start.29 = (f32[384,384]{1,0:T(8,128)S(1)}, f32[384,384]{1,0:T(8,128)S(1)}, u32[]{:S(2)}, u32[]{:S(2)}) collective-permute-start(f32[384,384]{1,0:T(8,128)S(1)} %slice.249), channel_id=1, source_target_pairs={{8,0},{16,24},{9,1},{17,25},{10,2},{18,26},{11,3},{19,27},{12,4},{... | collective-permute-start | bytes 1769480 | tf_op jit(solution)/shard_map/ppermute | solution.py:43
  115.6 22.5 %collective-permute-start.14 = (f32[64,768]{1,0:T(8,128)S(1)}, f32[64,768]{1,0:T(8,128)S(1)}, u32[]{:S(2)}, u32[]{:S(2)}) collective-permute-start(f32[64,768]{1,0:T(8,128)S(1)} %slice.231), channel_id=1, source_target_pairs={{0,2},{1,3},{2,0},{3,1},{4,6},{5,7},{6,4},{7,5},{8,10},{9,11},{10,... | collective-permute-start | bytes 589832 | tf_op jit(solution)/shard_map/ppermute | solution.py:68
  116.2 22.0 %collective-permute-start.12 = (f32[64,768]{1,0:T(8,128)S(1)}, f32[64,768]{1,0:T(8,128)S(1)}, u32[]{:S(2)}, u32[]{:S(2)}) collective-permute-start(f32[64,768]{1,0:T(8,128)S(1)} %slice.227), channel_id=1, source_target_pairs={{0,4},{1,5},{2,6},{3,7},{4,0},{5,1},{6,2},{7,3},{8,12},{9,13},{10,... | collective-permute-start | bytes 589832 | tf_op jit(solution)/shard_map/ppermute | solution.py:68
  136.8 14.7 %collective-permute-start.23 = (f32[384,384]{1,0:T(8,128)S(1)}, f32[384,384]{1,0:T(8,128)S(1)}, u32[]{:S(2)}, u32[]{:S(2)}) collective-permute-start(f32[384,384]{1,0:T(8,128)S(1)} %get-tuple-element.22), channel_id=1, source_target_pairs={{8,0},{16,24},{9,1},{17,25},{10,2},{18,26},{11,3},{19,27},{12,4},{... | collective-permute-start | bytes 1769480 | tf_op jit(solution)/shard_map/ppermute | solution.py:43
  140.2 13.1 %collective-permute-start.18 = (f32[128,768]{1,0:T(8,128)S(1)}, f32[128,768]{1,0:T(8,128)S(1)}, u32[]{:S(2)}, u32[]{:S(2)}) collective-permute-start(f32[128,768]{1,0:T(8,128)S(1)} %get-tuple-element.25), channel_id=1, source_target_pairs={{0,2},{1,3},{2,0},{3,1},{4,6},{5,7},{6,4},{7,5},{8,10},{9,11},{10,... | collective-permute-start | bytes 1179656 | tf_op jit(solution)/shard_map/ppermute | solution.py:68
  141.8 11.5 %collective-permute-start.20 = (f32[128,768]{1,0:T(8,128)S(1)}, f32[128,768]{1,0:T(8,128)S(1)}, u32[]{:S(2)}, u32[]{:S(2)}) collective-permute-start(f32[128,768]{1,0:T(8,128)S(1)} %get-tuple-element.26), channel_id=1, source_target_pairs={{0,4},{1,5},{2,6},{3,7},{4,0},{5,1},{6,2},{7,3},{8,12},{9,13},{10,... | collective-permute-start | bytes 1179656 | tf_op jit(solution)/shard_map/ppermute | solution.py:68
  151.6 5.0 %collective-permute-start.24 = (f32[384,384]{1,0:T(8,128)S(1)}, f32[384,384]{1,0:T(8,128)S(1)}, u32[]{:S(2)}, u32[]{:S(2)}) collective-permute-start(f32[384,384]{1,0:T(8,128)S(1)} %broadcast_select_fusion.2), channel_id=1, source_target_pairs={{0,1},{1,0},{2,3},{3,2},{4,5},{5,4},{6,7},{7,6},{8,9},{9,8},{10,11... | collective-permute-start | bytes 1769480 | tf_op jit(solution)/shard_map/ppermute | solution.py:68
  153.4 7.8 %collective-permute-start.21 = (f32[64,768]{1,0:T(8,128)S(1)}, f32[64,768]{1,0:T(8,128)S(1)}, u32[]{:S(2)}, u32[]{:S(2)}) collective-permute-start(f32[64,768]{1,0:T(8,128)S(1)} %slice.239), channel_id=1, source_target_pairs={{0,2},{1,3},{2,0},{3,1},{4,6},{5,7},{6,4},{7,5},{8,10},{9,11},{10,... | collective-permute-start | bytes 589832 | tf_op jit(solution)/shard_map/ppermute | solution.py:68
  155.0 7.8 %collective-permute-start.19 = (f32[64,768]{1,0:T(8,128)S(1)}, f32[64,768]{1,0:T(8,128)S(1)}, u32[]{:S(2)}, u32[]{:S(2)}) collective-permute-start(f32[64,768]{1,0:T(8,128)S(1)} %slice.235), channel_id=1, source_target_pairs={{0,4},{1,5},{2,6},{3,7},{4,0},{5,1},{6,2},{7,3},{8,12},{9,13},{10,... | collective-permute-start | bytes 589832 | tf_op jit(solution)/shard_map/ppermute | solution.py:68
  157.5 7.5 %collective-permute-start.25 = (f32[128,384]{1,0:T(8,128)S(1)}, f32[128,384]{1,0:T(8,128)S(1)}, u32[]{:S(2)}, u32[]{:S(2)}) collective-permute-start(f32[128,384]{1,0:T(8,128)S(1)} %get-tuple-element.41), channel_id=1, source_target_pairs={{0,2},{1,3},{2,0},{3,1},{4,6},{5,7},{6,4},{7,5},{8,10},{9,11},{10,... | collective-permute-start | bytes 589832 | tf_op jit(solution)/shard_map/ppermute | solution.py:68
  158.1 8.2 %collective-permute-start.27 = (f32[128,384]{1,0:T(8,128)S(1)}, f32[128,384]{1,0:T(8,128)S(1)}, u32[]{:S(2)}, u32[]{:S(2)}) collective-permute-start(f32[128,384]{1,0:T(8,128)S(1)} %get-tuple-element.42), channel_id=1, source_target_pairs={{0,4},{1,5},{2,6},{3,7},{4,0},{5,1},{6,2},{7,3},{8,12},{9,13},{10,... | collective-permute-start | bytes 589832 | tf_op jit(solution)/shard_map/ppermute | solution.py:68
  158.6 13.1 %collective-permute-start.30 = (f32[384,384]{1,0:T(8,128)S(1)}, f32[384,384]{1,0:T(8,128)S(1)}, u32[]{:S(2)}, u32[]{:S(2)}) collective-permute-start(f32[384,384]{1,0:T(8,128)S(1)} %get-tuple-element.12), channel_id=1, source_target_pairs={{0,1},{1,0},{2,3},{3,2},{4,5},{5,4},{6,7},{7,6},{8,9},{9,8},{10,11... | collective-permute-start | bytes 1769480 | tf_op jit(solution)/shard_map/ppermute | solution.py:68
  166.4 4.7 %collective-permute-start.28 = (f32[64,384]{1,0:T(8,128)S(1)}, f32[64,384]{1,0:T(8,128)S(1)}, u32[]{:S(2)}, u32[]{:S(2)}) collective-permute-start(f32[64,384]{1,0:T(8,128)S(1)} %slice.248), channel_id=1, source_target_pairs={{0,2},{1,3},{2,0},{3,1},{4,6},{5,7},{6,4},{7,5},{8,10},{9,11},{10,... | collective-permute-start | bytes 294920 | tf_op jit(solution)/shard_map/ppermute | solution.py:68
  167.0 4.7 %collective-permute-start.26 = (f32[64,384]{1,0:T(8,128)S(1)}, f32[64,384]{1,0:T(8,128)S(1)}, u32[]{:S(2)}, u32[]{:S(2)}) collective-permute-start(f32[64,384]{1,0:T(8,128)S(1)} %slice.244), channel_id=1, source_target_pairs={{0,4},{1,5},{2,6},{3,7},{4,0},{5,1},{6,2},{7,3},{8,12},{9,13},{10,... | collective-permute-start | bytes 294920 | tf_op jit(solution)/shard_map/ppermute | solution.py:68
  172.6 5.7 %collective-permute-start.31 = (f32[128,384]{1,0:T(8,128)S(1)}, f32[128,384]{1,0:T(8,128)S(1)}, u32[]{:S(2)}, u32[]{:S(2)}) collective-permute-start(f32[128,384]{1,0:T(8,128)S(1)} %get-tuple-element.37), channel_id=1, source_target_pairs={{0,2},{1,3},{2,0},{3,1},{4,6},{5,7},{6,4},{7,5},{8,10},{9,11},{10,... | collective-permute-start | bytes 589832 | tf_op jit(solution)/shard_map/ppermute | solution.py:68
  174.2 5.7 %collective-permute-start.33 = (f32[128,384]{1,0:T(8,128)S(1)}, f32[128,384]{1,0:T(8,128)S(1)}, u32[]{:S(2)}, u32[]{:S(2)}) collective-permute-start(f32[128,384]{1,0:T(8,128)S(1)} %get-tuple-element.38), channel_id=1, source_target_pairs={{0,4},{1,5},{2,6},{3,7},{4,0},{5,1},{6,2},{7,3},{8,12},{9,13},{10,... | collective-permute-start | bytes 589832 | tf_op jit(solution)/shard_map/ppermute | solution.py:68
  179.9 4.7 %collective-permute-start.34 = (f32[64,384]{1,0:T(8,128)S(1)}, f32[64,384]{1,0:T(8,128)S(1)}, u32[]{:S(2)}, u32[]{:S(2)}) collective-permute-start(f32[64,384]{1,0:T(8,128)S(1)} %slice.257), channel_id=1, source_target_pairs={{0,2},{1,3},{2,0},{3,1},{4,6},{5,7},{6,4},{7,5},{8,10},{9,11},{10,... | collective-permute-start | bytes 294920 | tf_op jit(solution)/shard_map/ppermute | solution.py:68
  180.5 4.7 %copy-start.4 = (f32[128,3072]{1,0:T(8,128)}, f32[128,3072]{1,0:T(8,128)S(1)}, u32[]{:S(2)}) copy-start(f32[128,3072]{1,0:T(8,128)S(1)} %maximum_dynamic-update-slice_fusion.3) | copy-start | bytes 4718596
  180.6 4.7 %collective-permute-start.32 = (f32[64,384]{1,0:T(8,128)S(1)}, f32[64,384]{1,0:T(8,128)S(1)}, u32[]{:S(2)}, u32[]{:S(2)}) collective-permute-start(f32[64,384]{1,0:T(8,128)S(1)} %slice.253), channel_id=1, source_target_pairs={{0,4},{1,5},{2,6},{3,7},{4,0},{5,1},{6,2},{7,3},{8,12},{9,13},{10,... | collective-permute-start | bytes 294920 | tf_op jit(solution)/shard_map/ppermute | solution.py:68

commit v3 on v2

v3 whole, which is shorter than its diff:
```python
import jax
import jax.numpy as jnp
from jax import lax
from jax.sharding import PartitionSpec as P

TILE_O = 32
TILE_V = 128
HIGH = lax.Precision.HIGH


def masked(values, mask, tile_rows):
    tile_r, tile_c = mask.shape
    scale = mask.astype(jnp.float32)[:, None, :, None]
    return (values.reshape(tile_r, tile_rows, tile_c, TILE_V) * scale).reshape(values.shape)


def after(value, *earlier):
    return lax.optimization_barrier((value,) + earlier)[0]


def line_blocks(own, own_later, nodes, split_last):
    here = lax.axis_index("occ")
    blocks = [own]
    origins = [list(range(nodes))]
    size = 1
    while size < nodes:
        fresh, fresh_origins = [], []
        place = here % (2 * size)
        dist = jnp.where(place < size, size - 1 - place, place - size)
        middles = [g * 2 * size + size for g in range(nodes // (2 * size))]
        for n, (block, origin) in enumerate(zip(blocks, origins)):
            pairs = [(m - 1, m) for m in middles] + [(m, m - 1) for m in middles]
            got = lax.ppermute(own_later if size > 1 and n == 0 else block, "occ", pairs)
            parts = [got]
            if split_last and size * 2 == nodes and n == size - 1:
                mid = got.shape[1] // 2
                parts = [got[:, :mid], got[:, mid:]]
            whole = []
            for moving in parts:
                got = moving
                for hop in range(1, size):
                    pairs = [(m - hop, m - hop - 1) for m in middles] + [(m + hop - 1, m + hop) for m in middles]
                    moving = lax.ppermute(moving, "occ", pairs)
                    got = jnp.where(dist == hop, moving, got)
                whole.append(got)
            fresh.append(whole if len(whole) > 1 else whole[0])
            table = [0] * nodes
            for m in middles:
                for k in range(size):
                    table[m - 1 - k] = origin[m]
                    table[m + k] = origin[m - 1]
            fresh_origins.append(table)
        blocks += fresh
        origins += fresh_origins
        size *= 2
    return blocks, origins


def per_device(sizes, amplitudes, amp_mask, integrals, int_mask):
    n_occ, n_vir = sizes
    rows = amplitudes.shape[0]
    half = rows // 2
    groups = n_vir // 2
    width = integrals.shape[1]
    own_depth = integrals.shape[0]

    def swap(x, bits):
        return lax.ppermute(x, "vir", [(i, i ^ bits) for i in range(n_vir)])

    me = lax.axis_index("vir")
    low = me % 2
    weighted = masked(integrals, int_mask, TILE_V)
    kept = masked(amplitudes, after(amp_mask, weighted), TILE_O)

    parts = []
    for r in range(groups):
        start = ((me // 2) ^ r) * (2 * own_depth)
        mine = lax.dynamic_slice_in_dim(kept, start + low * own_depth, own_depth, axis=1)
        others = lax.dynamic_slice_in_dim(kept, start + (1 - low) * own_depth, own_depth, axis=1)
        parts.append(jnp.concatenate([mine, others], axis=1))
    rel = [parts[0]] + [None] * (groups - 1)
    for r in range(groups - 1, 0, -1):
        rel[r] = swap(parts[r], 2 * r)

    blocks, origins = line_blocks(weighted, after(weighted, *parts), n_occ, True)

    bits = []
    while (1 << len(bits)) < groups:
        bits.append(1 << len(bits))
    orders = [bits, bits[::-1]]
    cut = [slice(0, half), slice(half, rows)]
    away = [[r for r in range(groups) if r & o[0]] for o in orders]
    near = [[r for r in range(groups) if not r & o[0]] for o in orders]
    lhs_away = [jnp.concatenate([rel[r][cut[h]] for r in away[h]], axis=0) for h in range(2)]
    lhs_near = [jnp.concatenate([rel[r][cut[h]] for r in near[h]], axis=0) for h in range(2)]
    away_own = jnp.concatenate([x[:, :own_depth] for x in lhs_away], axis=0)
    near_own = jnp.concatenate([x[:, :own_depth] for x in lhs_near], axis=0)
    away_other = [x[:, own_depth:] for x in lhs_away]
    near_other = jnp.concatenate([x[:, own_depth:] for x in lhs_near], axis=0)
    count = groups // 2 * half

    pieces = []
    for n, (block, origin) in enumerate(zip(blocks, origins)):
        place = jnp.array(origin, jnp.int32)[lax.axis_index("occ")]
        offset = 0
        for part in block if isinstance(block, list) else [block]:
            pieces.append((after(part, *parts) if n == 0 else part, place * width + offset))
            offset += part.shape[1]

    out = jnp.zeros((rows, n_occ * width), jnp.float32)
    token = None
    waiting = None
    for block, col in pieces:
        other = swap(block, 1)
        if token is not None:
            block = after(block, *token)
        sent_own = dot(away_own, block)
        stay_own = dot(near_own, block)
        other = after(other, sent_own)
        sent = [dot(away_other[h], other) + sent_own[h * count : (h + 1) * count] for h in range(2)]
        first = [swap(sent[h], 2 * orders[h][0]) for h in range(2)]
        stay = dot(near_other, other) + stay_own
        if waiting is not None:
            out = finish(out, waiting, stay)
        held = []
        for h in range(2):
            held.append({
                r: stay[h * count + i * half : h * count + (i + 1) * half] + first[h][i * half : (i + 1) * half]
                for i, r in enumerate(near[h])
            })
        for level in range(1, len(bits)):
            going = [[r for r in held[h] if r & orders[h][level]] for h in range(2)]
            moved = [jnp.concatenate([held[h][r] for r in going[h]], axis=0) for h in range(2)]
            got = [swap(moved[h], 2 * orders[h][level]) for h in range(2)]
            if level == len(bits) - 1:
                token = moved
                waiting = ([held[h][0] for h in range(2)], got, col)
                break
            for h in range(2):
                for i, r in enumerate(going[h]):
                    held[h][r ^ orders[h][level]] += got[h][i * half : (i + 1) * half]
                    del held[h][r]
    return finish(out, waiting, None)


def dot(a, b):
    return jnp.dot(a, b, precision=HIGH, preferred_element_type=jnp.float32)


def finish(out, waiting, dep):
    held, got, col = waiting
    if dep is not None:
        got = lax.optimization_barrier((*got, dep))[:2]
    done = jnp.concatenate([held[h] + got[h] for h in range(2)], axis=0)
    return lax.dynamic_update_slice(out, done, (0, col))


def solution(mesh):
    sizes = (mesh.shape["occ"], mesh.shape["vir"])

    def run(*args):
        return per_device(sizes, *args)

    in_specs = (P(("occ", "vir"), None), P(("occ", "vir"), None), P("vir", "occ"), P("vir", "occ"))
    out_specs = P(("occ", "vir"), None)
    return jax.shard_map(run, mesh=mesh, in_specs=in_specs, out_specs=out_specs, check_vma=False)
```

time: 187 us -> 154 us (0.82)
  blocking collectives: 34.1 us -> 0 us
  waiting for transfers between devices: 66.1 us -> 83.9 us
  between operations: 8.3 us -> 2.52 us
  matrix products: 19.8 us -> 15.2 us
  local copies, waits for them, and re-layouts: 12.6 us -> 8.38 us
    all_gather x1 -> x0, blocking collectives: 34.1 us -> none  [per_device(): mask_own = lax.all_gather(int_mask, 'occ', axis=0)]
    ppermute x29 -> x28, waiting for transfers between devices: 30.9 us -> 39.8 us  [swap(): return lax.ppermute(x, 'vir', [(i, i ^ bits) for i in range(n_vir)])]
    ppermute x3, waiting for transfers between devices: 35.2 us -> 42.8 us  [line_blocks(): moving = lax.ppermute(moving, 'occ', pairs)]
    dot_general x10 -> x25, matrix products: 19.8 us -> 15.2 us  [dot(): return jnp.dot(a, b, precision=HIGH, preferred_element_type=jnp.float32)]
    mul x8 -> x2, local copies, waits for them, and re-layouts: 3.31 us -> 0.34 us  [masked(): values.reshape(tile_r, tile_rows, tile_c, TILE_V) * scale]
    concatenate x4 -> x8, other arithmetic: 0.77 us -> 3.52 us  [the longest x4 3.41 us: per_device(): parts.append(jnp.concatenate([mine, others], axis=1))]
    add x15 -> x11, other arithmetic: 2.62 us -> 0.48 us  [the longest x6 0.3 us: finish(): done = jnp.concatenate([held[h] + got[h] for h in range(2)], axis=0)]
    slice x15 -> x0, local copies, waits for them, and re-layouts: 1.91 us -> none  [the longest x5 1.11 us: per_device(): s = sent[h * count * half:(h + 1) * count * half]]
  transfers between devices with their start and end apart: 35 -> 34, of which waited for: 18 -> 19; matrix products, arithmetic and copies ran while one was open for 20% -> 16% of each run, Pallas kernels for 0% -> 0%
where the time goes in v3:
time: 154 us
  waiting for transfers between devices  83.9 us (54%)
  starting transfers between devices  36.8 us (24%)
  matrix products  15.2 us (10%)
  local copies, waits for them, and re-layouts  8.38 us (5%)
  other arithmetic  6.61 us (4%)
  between operations  2.52 us (2%)
    ppermute x3, waiting for transfers between devices, line_blocks(): moving = lax.ppermute(moving, 'occ', pairs)  42.8 us
    ppermute x28, waiting for transfers between devices, swap(): return lax.ppermute(x, 'vir', [(i, i ^ bits) for i in range(n_vir)])  39.8 us
    ppermute x28, starting transfers between devices, swap(): return lax.ppermute(x, 'vir', [(i, i ^ bits) for i in range(n_vir)])  29.7 us
    dot_general x25, matrix products, dot(): return jnp.dot(a, b, precision=HIGH, preferred_element_type=jnp.float32)  15.2 us
    ppermute x3, starting transfers between devices, line_blocks(): moving = lax.ppermute(moving, 'occ', pairs)  4.06 us
    concatenate x4, other arithmetic, per_device(): parts.append(jnp.concatenate([mine, others], axis=1))  3.41 us
    slice x3, local copies, waits for them, and re-layouts, per_device(): rel[r][cut[h]]  3.15 us
  transfers between devices with their start and end apart: 34, of which 19 were waited for; matrix products, arithmetic and copies ran while one was open for 16% of the time, Pallas kernels for 0%

profile of v3, /device:TPU:0, one launch (start us, length us, event | category | flops | bytes accessed | tf_op | source)
XLA Modules:
  0.0 153.5 jit_solution(12714801683386298578)
XLA Ops:
  0.0 0.8 convert_element_type.6
  2.2 1.2 copy-done.1
  3.8 0.9 constant_dynamic-slice_fusion.6
  4.7 0.8 pad_maximum_fusion.6
  5.5 3.9 %collective-permute-start.3 = (f32[128,768]{1,0:T(8,128)}, f32[128,768]{1,0:T(8,128)}, u32[]{:S(2)}, u32[]{:S(2)}) collective-permute-start(f32[128,768]{1,0:T(8,128)} %pad_maximum_fusion.6), channel_id=1, source_target_pairs={{0,6},{1,7},{2,4},{3,5},{4,2},{5,3},{6,0},{7,1},{8,14},{9,15},{10,... | collective-permute-start | bytes 1179656 | tf_op jit(solution)/shard_map/ppermute | solution.py:68
  9.4 1.6 %collective-permute-start.8 = (f32[384,768]{1,0:T(8,128)S(1)}, f32[384,768]{1,0:T(8,128)S(1)}, u32[]{:S(2)}, u32[]{:S(2)}) collective-permute-start(f32[384,768]{1,0:T(8,128)S(1)} %bitcast_multiply_fusion.1), channel_id=1, source_target_pairs={{0,8},{16,24},{8,0},{24,16},{1,9},{17,25},{9,1},{25,17},{2,10},{18... | collective-permute-start | bytes 3538952 | tf_op jit(solution)/shard_map/ppermute | solution.py:33
  11.0 0.8 pad_maximum_fusion.3
  12.3 0.8 pad_maximum_fusion.4
  13.6 0.6 dynamic_slice.45
  14.8 0.7 dynamic_slice.46
  16.1 0.6 dynamic_slice.47
  17.4 1.1 fusion.5
  18.4 1.3 collective-permute-done.3
  19.7 0.7 collective-permute-start.14
  20.4 1.1 fusion.35
  21.5 5.7 %collective-permute-done = f32[128,768]{1,0:T(8,128)} collective-permute-done((f32[128,768]{1,0:T(8,128)}, f32[128,768]{1,0:T(8,128)}, u32[]{:S(2)}, u32[]{:S(2)}) %collective-permute-start) | collective-permute-done | bytes 393248 | tf_op jit(solution)/shard_map/ppermute | solution.py:68
  27.2 1.0 fusion.33
  28.3 1.1 fusion.34
  29.5 0.8 fusion.17
  30.3 0.8 fusion.36
  31.6 1.8 %collective-permute-start.6 = (f32[128,768]{1,0:T(8,128)S(1)}, f32[128,768]{1,0:T(8,128)S(1)}, u32[]{:S(2)}, u32[]{:S(2)}) collective-permute-start(f32[128,768]{1,0:T(8,128)S(1)} %convolution_add_fusion.7), channel_id=1, source_target_pairs={{0,4},{1,5},{2,6},{3,7},{4,0},{5,1},{6,2},{7,3},{8,12},{9,13},{10,... | collective-permute-start | bytes 1179656 | tf_op jit(solution)/shard_map/ppermute | solution.py:68
  33.9 1.6 %collective-permute-start.4 = (f32[128,768]{1,0:T(8,128)S(1)}, f32[128,768]{1,0:T(8,128)S(1)}, u32[]{:S(2)}, u32[]{:S(2)}) collective-permute-start(f32[128,768]{1,0:T(8,128)S(1)} %convolution_add_fusion.8), channel_id=1, source_target_pairs={{0,2},{1,3},{2,0},{3,1},{4,6},{5,7},{6,4},{7,5},{8,10},{9,11},{10,... | collective-permute-start | bytes 1179656 | tf_op jit(solution)/shard_map/ppermute | solution.py:68
  35.5 1.3 collective-permute-done.8
  36.8 0.7 collective-permute-start.21
  37.6 1.3 collective-permute-start.15
  38.9 0.8 convolution_add_fusion.2
  39.7 3.0 %collective-permute-done.6 = f32[128,768]{1,0:T(8,128)S(1)} collective-permute-done((f32[128,768]{1,0:T(8,128)S(1)}, f32[128,768]{1,0:T(8,128)S(1)}, u32[]{:S(2)}, u32[]{:S(2)}) %collective-permute-start.6) | collective-permute-done | bytes 393248 | tf_op jit(solution)/shard_map/ppermute | solution.py:68
  42.7 2.0 %collective-permute-done.4 = f32[128,768]{1,0:T(8,128)S(1)} collective-permute-done((f32[128,768]{1,0:T(8,128)S(1)}, f32[128,768]{1,0:T(8,128)S(1)}, u32[]{:S(2)}, u32[]{:S(2)}) %collective-permute-start.4) | collective-permute-done | bytes 393248 | tf_op jit(solution)/shard_map/ppermute | solution.py:68
  45.2 1.7 %collective-permute-start.7 = (f32[64,768]{1,0:T(8,128)S(1)}, f32[64,768]{1,0:T(8,128)S(1)}, u32[]{:S(2)}, u32[]{:S(2)}) collective-permute-start(f32[64,768]{1,0:T(8,128)S(1)} %get-tuple-element.63), channel_id=1, source_target_pairs={{0,2},{1,3},{2,0},{3,1},{4,6},{5,7},{6,4},{7,5},{8,10},{9,11},{10,... | collective-permute-start | bytes 589832 | tf_op jit(solution)/shard_map/ppermute | solution.py:68
  46.9 0.8 fusion.37
  47.7 0.8 fusion.16
  49.1 1.6 %collective-permute-start.12 = (f32[128,768]{1,0:T(8,128)S(1)}, f32[128,768]{1,0:T(8,128)S(1)}, u32[]{:S(2)}, u32[]{:S(2)}) collective-permute-start(f32[128,768]{1,0:T(8,128)S(1)} %convolution_add_fusion.5), channel_id=1, source_target_pairs={{0,4},{1,5},{2,6},{3,7},{4,0},{5,1},{6,2},{7,3},{8,12},{9,13},{10,... | collective-permute-start | bytes 1179656 | tf_op jit(solution)/shard_map/ppermute | solution.py:68
  51.2 24.0 %collective-permute-done.15 = f32[384,768]{1,0:T(8,128)S(1)} collective-permute-done((f32[384,768]{1,0:T(8,128)S(1)}, f32[384,768]{1,0:T(8,128)S(1)}, u32[]{:S(2)}, u32[]{:S(2)}) %collective-permute-start.15) | collective-permute-done | bytes 1179680 | tf_op jit(solution)/shard_map/ppermute | solution.py:43
  75.2 1.5 collective-permute-start.10
  76.8 0.8 convolution_add_fusion.1
  77.8 1.5 collective-permute-start.28
  79.6 3.4 %collective-permute-done.10 = f32[128,768]{1,0:T(8,128)S(1)} collective-permute-done((f32[128,768]{1,0:T(8,128)S(1)}, f32[128,768]{1,0:T(8,128)S(1)}, u32[]{:S(2)}, u32[]{:S(2)}) %collective-permute-start.10) | collective-permute-done | bytes 393248 | tf_op jit(solution)/shard_map/ppermute | solution.py:68
  83.0 1.6 %collective-permute-start.11 = (f32[64,768]{1,0:T(8,128)S(1)}, f32[64,768]{1,0:T(8,128)S(1)}, u32[]{:S(2)}, u32[]{:S(2)}) collective-permute-start(f32[64,768]{1,0:T(8,128)S(1)} %get-tuple-element.60), channel_id=1, source_target_pairs={{0,4},{1,5},{2,6},{3,7},{4,0},{5,1},{6,2},{7,3},{8,12},{9,13},{10,... | collective-permute-start | bytes 589832 | tf_op jit(solution)/shard_map/ppermute | solution.py:68
  84.6 2.3 %collective-permute-start.13 = (f32[64,768]{1,0:T(8,128)S(1)}, f32[64,768]{1,0:T(8,128)S(1)}, u32[]{:S(2)}, u32[]{:S(2)}) collective-permute-start(f32[64,768]{1,0:T(8,128)S(1)} %get-tuple-element.59), channel_id=1, source_target_pairs={{0,2},{1,3},{2,0},{3,1},{4,6},{5,7},{6,4},{7,5},{8,10},{9,11},{10,... | collective-permute-start | bytes 589832 | tf_op jit(solution)/shard_map/ppermute | solution.py:68
  86.9 0.8 fusion.15
  87.8 7.7 %collective-permute-done.28 = f32[384,384]{1,0:T(8,128)S(1)} collective-permute-done((f32[384,384]{1,0:T(8,128)S(1)}, f32[384,384]{1,0:T(8,128)S(1)}, u32[]{:S(2)}, u32[]{:S(2)}) %collective-permute-start.28) | collective-permute-done | bytes 589856 | tf_op jit(solution)/shard_map/ppermute | solution.py:43
  95.5 1.3 collective-permute-start.22
  97.5 0.8 fusion.18
  98.3 1.6 %collective-permute-start.19 = (f32[128,768]{1,0:T(8,128)S(1)}, f32[128,768]{1,0:T(8,128)S(1)}, u32[]{:S(2)}, u32[]{:S(2)}) collective-permute-start(f32[128,768]{1,0:T(8,128)S(1)} %convolution_add_fusion.3), channel_id=1, source_target_pairs={{0,4},{1,5},{2,6},{3,7},{4,0},{5,1},{6,2},{7,3},{8,12},{9,13},{10,... | collective-permute-start | bytes 1179656 | tf_op jit(solution)/shard_map/ppermute | solution.py:68
  100.4 0.8 convolution_add_fusion
  101.2 11.2 %collective-permute-done.22 = f32[384,384]{1,0:T(8,128)S(1)} collective-permute-done((f32[384,384]{1,0:T(8,128)S(1)}, f32[384,384]{1,0:T(8,128)S(1)}, u32[]{:S(2)}, u32[]{:S(2)}) %collective-permute-start.22) | collective-permute-done | bytes 589856 | tf_op jit(solution)/shard_map/ppermute | solution.py:43
  113.2 9.0 %collective-permute-done.17 = f32[128,768]{1,0:T(8,128)S(1)} collective-permute-done((f32[128,768]{1,0:T(8,128)S(1)}, f32[128,768]{1,0:T(8,128)S(1)}, u32[]{:S(2)}, u32[]{:S(2)}) %collective-permute-start.17) | collective-permute-done | bytes 393248 | tf_op jit(solution)/shard_map/ppermute | solution.py:68
  122.3 1.6 %collective-permute-start.18 = (f32[64,768]{1,0:T(8,128)S(1)}, f32[64,768]{1,0:T(8,128)S(1)}, u32[]{:S(2)}, u32[]{:S(2)}) collective-permute-start(f32[64,768]{1,0:T(8,128)S(1)} %get-tuple-element.56), channel_id=1, source_target_pairs={{0,4},{1,5},{2,6},{3,7},{4,0},{5,1},{6,2},{7,3},{8,12},{9,13},{10,... | collective-permute-start | bytes 589832 | tf_op jit(solution)/shard_map/ppermute | solution.py:68
  126.2 0.6 collective-permute-start.26
  126.8 1.5 collective-permute-start.24
  128.9 0.9 collective-permute-done.18
  129.8 0.9 collective-permute-done.20
  130.8 1.4 collective-permute-done.26
  132.8 1.5 collective-permute-start.25
  134.3 1.3 collective-permute-start.27
  137.6 0.8 collective-permute-start.30
  138.8 0.6 collective-permute-start.32
  140.0 3.4 %collective-permute-done.30 = f32[128,384]{1,0:T(8,128)S(1)} collective-permute-done((f32[128,384]{1,0:T(8,128)S(1)}, f32[128,384]{1,0:T(8,128)S(1)}, u32[]{:S(2)}, u32[]{:S(2)}) %collective-permute-start.30) | collective-permute-done | bytes 196640 | tf_op jit(solution)/shard_map/ppermute | solution.py:68
  143.4 0.8 collective-permute-start.31
  144.3 1.3 collective-permute-done.32
  145.6 2.5 %collective-permute-done.31 = f32[64,384]{1,0:T(8,128)S(1)} collective-permute-done((f32[64,384]{1,0:T(8,128)S(1)}, f32[64,384]{1,0:T(8,128)S(1)}, u32[]{:S(2)}, u32[]{:S(2)}) %collective-permute-start.31) | collective-permute-done | bytes 98336 | tf_op jit(solution)/shard_map/ppermute | solution.py:68
  148.1 0.8 collective-permute-start.33
  149.0 3.8 %collective-permute-done.33 = f32[64,384]{1,0:T(8,128)S(1)} collective-permute-done((f32[64,384]{1,0:T(8,128)S(1)}, f32[64,384]{1,0:T(8,128)S(1)}, u32[]{:S(2)}, u32[]{:S(2)}) %collective-permute-start.33) | collective-permute-done | bytes 98336 | tf_op jit(solution)/shard_map/ppermute | solution.py:68
  152.8 0.7 maximum_dynamic-update-slice_fusion.4
  (85 shorter events, 14.6 us)
Async XLA Ops:
  0.0 1.3 copy-start.2
  1.3 0.7 copy-start.3
  2.0 1.4 copy-start.1
  4.7 8.9 %copy-start.6 = (s32[4]{0:T(128)S(1)}, s32[4]{0:T(128)}, u32[]{:S(2)}) copy-start(s32[4]{0:T(128)} %constant.76.clone) | copy-start | bytes 52
  4.7 10.0 %copy-start.5 = (s32[4]{0:T(128)S(1)}, s32[4]{0:T(128)}, u32[]{:S(2)}) copy-start(s32[4]{0:T(128)} %constant.77.clone) | copy-start | bytes 52
  4.7 11.3 %copy-start.4 = (s32[4]{0:T(128)S(1)}, s32[4]{0:T(128)}, u32[]{:S(2)}) copy-start(s32[4]{0:T(128)} %constant.78.clone) | copy-start | bytes 52
  5.5 14.2 %collective-permute-start.3 = (f32[128,768]{1,0:T(8,128)}, f32[128,768]{1,0:T(8,128)}, u32[]{:S(2)}, u32[]{:S(2)}) collective-permute-start(f32[128,768]{1,0:T(8,128)} %pad_maximum_fusion.6), channel_id=1, source_target_pairs={{0,6},{1,7},{2,4},{3,5},{4,2},{5,3},{6,0},{7,1},{8,14},{9,15},{10,... | collective-permute-start | bytes 1179656 | tf_op jit(solution)/shard_map/ppermute | solution.py:68
  9.4 27.4 %collective-permute-start.8 = (f32[384,768]{1,0:T(8,128)S(1)}, f32[384,768]{1,0:T(8,128)S(1)}, u32[]{:S(2)}, u32[]{:S(2)}) collective-permute-start(f32[384,768]{1,0:T(8,128)S(1)} %bitcast_multiply_fusion.1), channel_id=1, source_target_pairs={{0,8},{16,24},{8,0},{24,16},{1,9},{17,25},{9,1},{25,17},{2,10},{18... | collective-permute-start | bytes 3538952 | tf_op jit(solution)/shard_map/ppermute | solution.py:33
  11.8 15.5 %collective-permute-start = (f32[128,768]{1,0:T(8,128)}, f32[128,768]{1,0:T(8,128)}, u32[]{:S(2)}, u32[]{:S(2)}) collective-permute-start(f32[128,768]{1,0:T(8,128)} %pad_maximum_fusion.3), channel_id=1, source_target_pairs={{0,4},{1,5},{2,6},{3,7},{4,0},{5,1},{6,2},{7,3},{8,12},{9,13},{10,... | collective-permute-start | bytes 1179656 | tf_op jit(solution)/shard_map/ppermute | solution.py:68
  13.1 15.3 %collective-permute-start.1 = (f32[128,768]{1,0:T(8,128)}, f32[128,768]{1,0:T(8,128)}, u32[]{:S(2)}, u32[]{:S(2)}) collective-permute-start(f32[128,768]{1,0:T(8,128)} %pad_maximum_fusion.4), channel_id=1, source_target_pairs={{0,2},{1,3},{2,0},{3,1},{4,6},{5,7},{6,4},{7,5},{8,10},{9,11},{10,... | collective-permute-start | bytes 1179656 | tf_op jit(solution)/shard_map/ppermute | solution.py:68
  13.6 17.5 %collective-permute-start.2 = (f32[384,768]{1,0:T(8,128)S(1)}, f32[384,768]{1,0:T(8,128)S(1)}, u32[]{:S(2)}, u32[]{:S(2)}) collective-permute-start(f32[384,768]{1,0:T(8,128)S(1)} %bitcast_multiply_fusion.1), channel_id=1, source_target_pairs={{0,1},{1,0},{2,3},{3,2},{4,5},{5,4},{6,7},{7,6},{8,9},{9,8},{10,11... | collective-permute-start | bytes 3538952 | tf_op jit(solution)/shard_map/ppermute | solution.py:68
  19.7 17.9 %collective-permute-start.14 = (f32[384,768]{1,0:T(8,128)S(1)}, f32[384,768]{1,0:T(8,128)S(1)}, u32[]{:S(2)}, u32[]{:S(2)}) collective-permute-start(f32[384,768]{1,0:T(8,128)S(1)} %bitcast_multiply_fusion.1), channel_id=1, source_target_pairs={{8,16},{16,8},{9,17},{17,9},{10,18},{18,10},{11,19},{19,11},{12,20... | collective-permute-start | bytes 3538952 | tf_op jit(solution)/shard_map/ppermute | solution.py:33
  31.6 11.1 %collective-permute-start.6 = (f32[128,768]{1,0:T(8,128)S(1)}, f32[128,768]{1,0:T(8,128)S(1)}, u32[]{:S(2)}, u32[]{:S(2)}) collective-permute-start(f32[128,768]{1,0:T(8,128)S(1)} %convolution_add_fusion.7), channel_id=1, source_target_pairs={{0,4},{1,5},{2,6},{3,7},{4,0},{5,1},{6,2},{7,3},{8,12},{9,13},{10,... | collective-permute-start | bytes 1179656 | tf_op jit(solution)/shard_map/ppermute | solution.py:68
  33.9 10.8 %collective-permute-start.4 = (f32[128,768]{1,0:T(8,128)S(1)}, f32[128,768]{1,0:T(8,128)S(1)}, u32[]{:S(2)}, u32[]{:S(2)}) collective-permute-start(f32[128,768]{1,0:T(8,128)S(1)} %convolution_add_fusion.8), channel_id=1, source_target_pairs={{0,2},{1,3},{2,0},{3,1},{4,6},{5,7},{6,4},{7,5},{8,10},{9,11},{10,... | collective-permute-start | bytes 1179656 | tf_op jit(solution)/shard_map/ppermute | solution.py:68
  36.8 11.7 %collective-permute-start.9 = (f32[384,768]{1,0:T(8,128)S(1)}, f32[384,768]{1,0:T(8,128)S(1)}, u32[]{:S(2)}, u32[]{:S(2)}) collective-permute-start(f32[384,768]{1,0:T(8,128)S(1)} %collective-permute-done.8), channel_id=1, source_target_pairs={{0,1},{1,0},{2,3},{3,2},{4,5},{5,4},{6,7},{7,6},{8,9},{9,8},{10,11... | collective-permute-start | bytes 3538952 | tf_op jit(solution)/shard_map/ppermute | solution.py:68
  36.8 40.9 %collective-permute-start.21 = (f32[384,768]{1,0:T(8,128)S(1)}, f32[384,768]{1,0:T(8,128)S(1)}, u32[]{:S(2)}, u32[]{:S(2)}) collective-permute-start(f32[384,768]{1,0:T(8,128)S(1)} %collective-permute-done.8), channel_id=1, source_target_pairs={{8,16},{16,8},{9,17},{17,9},{10,18},{18,10},{11,19},{19,11},{12,20... | collective-permute-start | bytes 3538952 | tf_op jit(solution)/shard_map/ppermute | solution.py:33
  37.6 37.6 %collective-permute-start.15 = (f32[384,768]{1,0:T(8,128)S(1)}, f32[384,768]{1,0:T(8,128)S(1)}, u32[]{:S(2)}, u32[]{:S(2)}) collective-permute-start(f32[384,768]{1,0:T(8,128)S(1)} %collective-permute-done.14), channel_id=1, source_target_pairs={{8,0},{16,24},{9,1},{17,25},{10,2},{18,26},{11,3},{19,27},{12,4},{... | collective-permute-start | bytes 3538952 | tf_op jit(solution)/shard_map/ppermute | solution.py:43
  44.8 32.9 %collective-permute-start.5 = (f32[64,768]{1,0:T(8,128)S(1)}, f32[64,768]{1,0:T(8,128)S(1)}, u32[]{:S(2)}, u32[]{:S(2)}) collective-permute-start(f32[64,768]{1,0:T(8,128)S(1)} %get-tuple-element.64), channel_id=1, source_target_pairs={{0,4},{1,5},{2,6},{3,7},{4,0},{5,1},{6,2},{7,3},{8,12},{9,13},{10,... | collective-permute-start | bytes 589832 | tf_op jit(solution)/shard_map/ppermute | solution.py:68
  45.2 32.5 %collective-permute-start.7 = (f32[64,768]{1,0:T(8,128)S(1)}, f32[64,768]{1,0:T(8,128)S(1)}, u32[]{:S(2)}, u32[]{:S(2)}) collective-permute-start(f32[64,768]{1,0:T(8,128)S(1)} %get-tuple-element.63), channel_id=1, source_target_pairs={{0,2},{1,3},{2,0},{3,1},{4,6},{5,7},{6,4},{7,5},{8,10},{9,11},{10,... | collective-permute-start | bytes 589832 | tf_op jit(solution)/shard_map/ppermute | solution.py:68
  49.1 30.5 %collective-permute-start.12 = (f32[128,768]{1,0:T(8,128)S(1)}, f32[128,768]{1,0:T(8,128)S(1)}, u32[]{:S(2)}, u32[]{:S(2)}) collective-permute-start(f32[128,768]{1,0:T(8,128)S(1)} %convolution_add_fusion.5), channel_id=1, source_target_pairs={{0,4},{1,5},{2,6},{3,7},{4,0},{5,1},{6,2},{7,3},{8,12},{9,13},{10,... | collective-permute-start | bytes 1179656 | tf_op jit(solution)/shard_map/ppermute | solution.py:68
  75.2 7.8 %collective-permute-start.10 = (f32[128,768]{1,0:T(8,128)S(1)}, f32[128,768]{1,0:T(8,128)S(1)}, u32[]{:S(2)}, u32[]{:S(2)}) collective-permute-start(f32[128,768]{1,0:T(8,128)S(1)} %convolution_add_fusion.6), channel_id=1, source_target_pairs={{0,2},{1,3},{2,0},{3,1},{4,6},{5,7},{6,4},{7,5},{8,10},{9,11},{10,... | collective-permute-start | bytes 1179656 | tf_op jit(solution)/shard_map/ppermute | solution.py:68
  77.7 19.2 %collective-permute-start.16 = (f32[384,768]{1,0:T(8,128)S(1)}, f32[384,768]{1,0:T(8,128)S(1)}, u32[]{:S(2)}, u32[]{:S(2)}) collective-permute-start(f32[384,768]{1,0:T(8,128)S(1)} %broadcast_select_fusion), channel_id=1, source_target_pairs={{0,1},{1,0},{2,3},{3,2},{4,5},{5,4},{6,7},{7,6},{8,9},{9,8},{10,11... | collective-permute-start | bytes 3538952 | tf_op jit(solution)/shard_map/ppermute | solution.py:68
  77.8 17.6 %collective-permute-start.28 = (f32[384,384]{1,0:T(8,128)S(1)}, f32[384,384]{1,0:T(8,128)S(1)}, u32[]{:S(2)}, u32[]{:S(2)}) collective-permute-start(f32[384,384]{1,0:T(8,128)S(1)} %slice.329), channel_id=1, source_target_pairs={{8,0},{16,24},{9,1},{17,25},{10,2},{18,26},{11,3},{19,27},{12,4},{... | collective-permute-start | bytes 1769480 | tf_op jit(solution)/shard_map/ppermute | solution.py:43
  83.0 30.0 %collective-permute-start.11 = (f32[64,768]{1,0:T(8,128)S(1)}, f32[64,768]{1,0:T(8,128)S(1)}, u32[]{:S(2)}, u32[]{:S(2)}) collective-permute-start(f32[64,768]{1,0:T(8,128)S(1)} %get-tuple-element.60), channel_id=1, source_target_pairs={{0,4},{1,5},{2,6},{3,7},{4,0},{5,1},{6,2},{7,3},{8,12},{9,13},{10,... | collective-permute-start | bytes 589832 | tf_op jit(solution)/shard_map/ppermute | solution.py:68
  84.6 28.4 %collective-permute-start.13 = (f32[64,768]{1,0:T(8,128)S(1)}, f32[64,768]{1,0:T(8,128)S(1)}, u32[]{:S(2)}, u32[]{:S(2)}) collective-permute-start(f32[64,768]{1,0:T(8,128)S(1)} %get-tuple-element.59), channel_id=1, source_target_pairs={{0,2},{1,3},{2,0},{3,1},{4,6},{5,7},{6,4},{7,5},{8,10},{9,11},{10,... | collective-permute-start | bytes 589832 | tf_op jit(solution)/shard_map/ppermute | solution.py:68
  95.5 16.8 %collective-permute-start.22 = (f32[384,384]{1,0:T(8,128)S(1)}, f32[384,384]{1,0:T(8,128)S(1)}, u32[]{:S(2)}, u32[]{:S(2)}) collective-permute-start(f32[384,384]{1,0:T(8,128)S(1)} %get-tuple-element.52), channel_id=1, source_target_pairs={{8,0},{16,24},{9,1},{17,25},{10,2},{18,26},{11,3},{19,27},{12,4},{... | collective-permute-start | bytes 1769480 | tf_op jit(solution)/shard_map/ppermute | solution.py:43
  96.8 39.9 %collective-permute-start.29 = (f32[384,384]{1,0:T(8,128)S(1)}, f32[384,384]{1,0:T(8,128)S(1)}, u32[]{:S(2)}, u32[]{:S(2)}) collective-permute-start(f32[384,384]{1,0:T(8,128)S(1)} %get-tuple-element.39), channel_id=1, source_target_pairs={{0,1},{1,0},{2,3},{3,2},{4,5},{5,4},{6,7},{7,6},{8,9},{9,8},{10,11... | collective-permute-start | bytes 1769480 | tf_op jit(solution)/shard_map/ppermute | solution.py:68
  98.3 14.9 %collective-permute-start.19 = (f32[128,768]{1,0:T(8,128)S(1)}, f32[128,768]{1,0:T(8,128)S(1)}, u32[]{:S(2)}, u32[]{:S(2)}) collective-permute-start(f32[128,768]{1,0:T(8,128)S(1)} %convolution_add_fusion.3), channel_id=1, source_target_pairs={{0,4},{1,5},{2,6},{3,7},{4,0},{5,1},{6,2},{7,3},{8,12},{9,13},{10,... | collective-permute-start | bytes 1179656 | tf_op jit(solution)/shard_map/ppermute | solution.py:68
  112.4 9.8 %collective-permute-start.17 = (f32[128,768]{1,0:T(8,128)S(1)}, f32[128,768]{1,0:T(8,128)S(1)}, u32[]{:S(2)}, u32[]{:S(2)}) collective-permute-start(f32[128,768]{1,0:T(8,128)S(1)} %convolution_add_fusion.4), channel_id=1, source_target_pairs={{0,2},{1,3},{2,0},{3,1},{4,6},{5,7},{6,4},{7,5},{8,10},{9,11},{10,... | collective-permute-start | bytes 1179656 | tf_op jit(solution)/shard_map/ppermute | solution.py:68
  113.0 12.5 %collective-permute-start.23 = (f32[384,384]{1,0:T(8,128)S(1)}, f32[384,384]{1,0:T(8,128)S(1)}, u32[]{:S(2)}, u32[]{:S(2)}) collective-permute-start(f32[384,384]{1,0:T(8,128)S(1)} %broadcast_select_fusion.2), channel_id=1, source_target_pairs={{0,1},{1,0},{2,3},{3,2},{4,5},{5,4},{6,7},{7,6},{8,9},{9,8},{10,11... | collective-permute-start | bytes 1769480 | tf_op jit(solution)/shard_map/ppermute | solution.py:68
  122.3 7.5 %collective-permute-start.18 = (f32[64,768]{1,0:T(8,128)S(1)}, f32[64,768]{1,0:T(8,128)S(1)}, u32[]{:S(2)}, u32[]{:S(2)}) collective-permute-start(f32[64,768]{1,0:T(8,128)S(1)} %get-tuple-element.56), channel_id=1, source_target_pairs={{0,4},{1,5},{2,6},{3,7},{4,0},{5,1},{6,2},{7,3},{8,12},{9,13},{10,... | collective-permute-start | bytes 589832 | tf_op jit(solution)/shard_map/ppermute | solution.py:68
  123.9 6.8 %collective-permute-start.20 = (f32[64,768]{1,0:T(8,128)S(1)}, f32[64,768]{1,0:T(8,128)S(1)}, u32[]{:S(2)}, u32[]{:S(2)}) collective-permute-start(f32[64,768]{1,0:T(8,128)S(1)} %get-tuple-element.55), channel_id=1, source_target_pairs={{0,2},{1,3},{2,0},{3,1},{4,6},{5,7},{6,4},{7,5},{8,10},{9,11},{10,... | collective-permute-start | bytes 589832 | tf_op jit(solution)/shard_map/ppermute | solution.py:68
  126.2 6.0 %collective-permute-start.26 = (f32[128,384]{1,0:T(8,128)S(1)}, f32[128,384]{1,0:T(8,128)S(1)}, u32[]{:S(2)}, u32[]{:S(2)}) collective-permute-start(f32[128,384]{1,0:T(8,128)S(1)} %convolution_add_fusion.13), channel_id=1, source_target_pairs={{0,4},{1,5},{2,6},{3,7},{4,0},{5,1},{6,2},{7,3},{8,12},{9,13},{10,... | collective-permute-start | bytes 589832 | tf_op jit(solution)/shard_map/ppermute | solution.py:68
  126.8 6.0 %collective-permute-start.24 = (f32[128,384]{1,0:T(8,128)S(1)}, f32[128,384]{1,0:T(8,128)S(1)}, u32[]{:S(2)}, u32[]{:S(2)}) collective-permute-start(f32[128,384]{1,0:T(8,128)S(1)} %convolution_add_fusion.14), channel_id=1, source_target_pairs={{0,2},{1,3},{2,0},{3,1},{4,6},{5,7},{6,4},{7,5},{8,10},{9,11},{10,... | collective-permute-start | bytes 589832 | tf_op jit(solution)/shard_map/ppermute | solution.py:68
  132.8 6.6 %collective-permute-start.25 = (f32[64,384]{1,0:T(8,128)S(1)}, f32[64,384]{1,0:T(8,128)S(1)}, u32[]{:S(2)}, u32[]{:S(2)}) collective-permute-start(f32[64,384]{1,0:T(8,128)S(1)} %get-tuple-element.70), channel_id=1, source_target_pairs={{0,4},{1,5},{2,6},{3,7},{4,0},{5,1},{6,2},{7,3},{8,12},{9,13},{10,... | collective-permute-start | bytes 294920 | tf_op jit(solution)/shard_map/ppermute | solution.py:68
  134.3 5.6 %collective-permute-start.27 = (f32[64,384]{1,0:T(8,128)S(1)}, f32[64,384]{1,0:T(8,128)S(1)}, u32[]{:S(2)}, u32[]{:S(2)}) collective-permute-start(f32[64,384]{1,0:T(8,128)S(1)} %get-tuple-element.69), channel_id=1, source_target_pairs={{0,2},{1,3},{2,0},{3,1},{4,6},{5,7},{6,4},{7,5},{8,10},{9,11},{10,... | collective-permute-start | bytes 294920 | tf_op jit(solution)/shard_map/ppermute | solution.py:68
  137.6 5.7 %collective-permute-start.30 = (f32[128,384]{1,0:T(8,128)S(1)}, f32[128,384]{1,0:T(8,128)S(1)}, u32[]{:S(2)}, u32[]{:S(2)}) collective-permute-start(f32[128,384]{1,0:T(8,128)S(1)} %convolution_add_fusion.12), channel_id=1, source_target_pairs={{0,2},{1,3},{2,0},{3,1},{4,6},{5,7},{6,4},{7,5},{8,10},{9,11},{10,... | collective-permute-start | bytes 589832 | tf_op jit(solution)/shard_map/ppermute | solution.py:68
  138.8 6.8 %collective-permute-start.32 = (f32[128,384]{1,0:T(8,128)S(1)}, f32[128,384]{1,0:T(8,128)S(1)}, u32[]{:S(2)}, u32[]{:S(2)}) collective-permute-start(f32[128,384]{1,0:T(8,128)S(1)} %convolution_add_fusion.11), channel_id=1, source_target_pairs={{0,4},{1,5},{2,6},{3,7},{4,0},{5,1},{6,2},{7,3},{8,12},{9,13},{10,... | collective-permute-start | bytes 589832 | tf_op jit(solution)/shard_map/ppermute | solution.py:68
  143.4 4.7 %collective-permute-start.31 = (f32[64,384]{1,0:T(8,128)S(1)}, f32[64,384]{1,0:T(8,128)S(1)}, u32[]{:S(2)}, u32[]{:S(2)}) collective-permute-start(f32[64,384]{1,0:T(8,128)S(1)} %slice_add_fusion.14), channel_id=1, source_target_pairs={{0,4},{1,5},{2,6},{3,7},{4,0},{5,1},{6,2},{7,3},{8,12},{9,13},{10,... | collective-permute-start | bytes 294920 | tf_op jit(solution)/shard_map/ppermute | solution.py:68
  148.1 4.7 %collective-permute-start.33 = (f32[64,384]{1,0:T(8,128)S(1)}, f32[64,384]{1,0:T(8,128)S(1)}, u32[]{:S(2)}, u32[]{:S(2)}) collective-permute-start(f32[64,384]{1,0:T(8,128)S(1)} %get-tuple-element.66), channel_id=1, source_target_pairs={{0,2},{1,3},{2,0},{3,1},{4,6},{5,7},{6,4},{7,5},{8,10},{9,11},{10,... | collective-permute-start | bytes 294920 | tf_op jit(solution)/shard_map/ppermute | solution.py:68
  148.9 3.9 %copy-start = (f32[128,3072]{1,0:T(8,128)}, f32[128,3072]{1,0:T(8,128)S(1)}, u32[]{:S(2)}) copy-start(f32[128,3072]{1,0:T(8,128)S(1)} %maximum_dynamic-update-slice_fusion.3) | copy-start | bytes 4718596

commit v4 on v1

v4 whole, which is shorter than its diff:
```python
import functools

import jax
import jax.numpy as jnp
from jax import lax
from jax.experimental import pallas as pl
from jax.experimental.pallas import tpu as pltpu
from jax.sharding import PartitionSpec as P

TILE_O = 32
TILE_V = 128
VMEM_LIMIT = 40 * 1024 * 1024


def masked(values, mask, tile_rows):
    tile_r, tile_c = mask.shape
    scale = mask.astype(jnp.float32)[:, None, :, None]
    return (values.reshape(tile_r, tile_rows, tile_c, TILE_V) * scale).reshape(values.shape)


def after(value, *earlier):
    return lax.optimization_barrier((value,) + earlier)[0]


def in_vmem(count):
    return [pl.BlockSpec(memory_space=pltpu.VMEM)] * count


def cut_kernel(groups, own_tiles, place_ref, mask_ref, amp_ref, *out_refs):
    group, low = place_ref[0], place_ref[1]
    for r in range(groups):
        start = (group ^ r) * (2 * own_tiles)
        for t in range(2 * own_tiles):
            half = low if t < own_tiles else 1 - low
            q = start + half * own_tiles + t % own_tiles
            columns = pl.ds(pl.multiple_of(q * TILE_V, TILE_V), TILE_V)
            for o in range(amp_ref.shape[0] // TILE_O):
                rows = pl.ds(o * TILE_O, TILE_O)
                scale = mask_ref[o, q].astype(jnp.float32)
                out_refs[r][rows, pl.ds(t * TILE_V, TILE_V)] = amp_ref[rows, columns] * scale


def cut_amplitudes(place, mask, amplitudes, groups, own_tiles):
    rows = amplitudes.shape[0]
    depth = 2 * own_tiles * TILE_V
    smem = pl.BlockSpec(memory_space=pltpu.SMEM)
    return pl.pallas_call(
        functools.partial(cut_kernel, groups, own_tiles),
        out_shape=[jax.ShapeDtypeStruct((rows, depth), jnp.float32)] * groups,
        in_specs=[smem, smem] + in_vmem(1),
        out_specs=in_vmem(groups),
        compiler_params=pltpu.CompilerParams(vmem_limit_bytes=VMEM_LIMIT),
        cost_estimate=pl.CostEstimate(flops=1, bytes_accessed=1, transcendentals=0),
        name="cut",
    )(place, mask, amplitudes)


def split(x):
    high = x.astype(jnp.bfloat16)
    return high, (x - high.astype(jnp.float32)).astype(jnp.bfloat16)


def dot_kernel(lists, names, *refs):
    n = len(names)
    rel = dict(zip(names, refs[:n]))
    own_ref, other_ref = refs[n : n + 2]
    outs = refs[n + 2 :]
    depth = own_ref.shape[0]
    rows = refs[0].shape[0]
    parts = {r: split(rel[r][...]) for r in names}
    width = own_ref.shape[1] // 2
    for h in range(2):
        columns = pl.ds(h * width, width)
        right = [split(ref[:, columns]) for ref in (own_ref, other_ref)]
        for i, r in enumerate(lists[h]):
            total = None
            for k in range(2):
                b_high, b_low = right[k]
                a_high, a_low = (x[:, k * depth : (k + 1) * depth] for x in parts[r])
                for a, b in ((a_high, b_low), (a_low, b_high), (a_high, b_high)):
                    term = jnp.dot(a, b, preferred_element_type=jnp.float32)
                    total = term if total is None else total + term
            outs[h][i * rows : (i + 1) * rows, :] = total


def products(lists, rel, own, other):
    names = sorted(set(lists[0]) | set(lists[1]))
    rows, depth = rel[0].shape
    width = own.shape[1] // 2
    count = len(lists[0])
    return pl.pallas_call(
        functools.partial(dot_kernel, lists, names),
        out_shape=[jax.ShapeDtypeStruct((rows * count, width), jnp.float32)] * 2,
        in_specs=in_vmem(len(names) + 2),
        out_specs=in_vmem(2),
        compiler_params=pltpu.CompilerParams(vmem_limit_bytes=VMEM_LIMIT),
        cost_estimate=pl.CostEstimate(flops=1, bytes_accessed=1, transcendentals=0),
        name="products",
    )(*[rel[r] for r in names], own, other)


def pick(values, here):
    result = jnp.int32(values[0])
    for i in range(1, len(values)):
        result = jnp.where(here == i, jnp.int32(values[i]), result)
    return result


def line_blocks(own, nodes):
    here = lax.axis_index("occ")
    blocks = [own]
    places = [here]
    origins = [list(range(nodes))]
    size = 1
    while size < nodes:
        fresh, fresh_origins = [], []
        place = here % (2 * size)
        dist = jnp.where(place < size, size - 1 - place, place - size)
        middles = [g * 2 * size + size for g in range(nodes // (2 * size))]
        for block, origin in zip(blocks, origins):
            pairs = [(m - 1, m) for m in middles] + [(m, m - 1) for m in middles]
            moving = lax.ppermute(block, "occ", pairs)
            got = moving
            for hop in range(1, size):
                pairs = [(m - hop, m - hop - 1) for m in middles] + [(m + hop - 1, m + hop) for m in middles]
                moving = lax.ppermute(moving, "occ", pairs)
                got = jnp.where(dist == hop, moving, got)
            fresh.append(got)
            table = [0] * nodes
            for m in middles:
                for k in range(size):
                    table[m - 1 - k] = origin[m]
                    table[m + k] = origin[m - 1]
            fresh_origins.append(table)
        blocks += fresh
        origins += fresh_origins
        size *= 2
    return blocks, [pick(origin, here) for origin in origins]


def per_device(sizes, amplitudes, amp_mask, integrals, int_mask):
    n_occ, n_vir = sizes
    rows = amplitudes.shape[0]
    groups = n_vir // 2
    own_depth, width = integrals.shape
    half = width // 2

    def swap(x, bits):
        return lax.ppermute(x, "vir", [(i, i ^ bits) for i in range(n_vir)])

    me = lax.axis_index("vir")
    weighted = masked(integrals, int_mask, TILE_V)
    blocks, places = line_blocks(weighted, n_occ)

    position = jnp.stack([me // 2, me % 2]).astype(jnp.int32)
    parts = cut_amplitudes(after(position, weighted), amp_mask, amplitudes, groups, own_depth // TILE_V)
    rel = [parts[0]] + [None] * (groups - 1)
    for r in range(groups - 1, 0, -1):
        rel[r] = swap(parts[r], 2 * r)

    bits = []
    while (1 << len(bits)) < groups:
        bits.append(1 << len(bits))
    orders = [bits, bits[::-1]]
    away = [[r for r in range(groups) if r & o[0]] for o in orders]
    near = [[r for r in range(groups) if not r & o[0]] for o in orders]

    out = jnp.zeros((rows, n_occ * width), jnp.float32)
    token = parts
    for block, place in zip(blocks, places):
        block = after(block, *token)
        other = swap(block, 1)
        sent = products(away, rel, block, other)
        moving = [swap(sent[h], 2 * orders[h][0]) for h in range(2)]
        stay = products(near, rel, block, after(other, *sent))
        held = [{r: stay[h][i * rows : (i + 1) * rows] for i, r in enumerate(near[h])} for h in range(2)]
        for level in range(len(bits)):
            for h in range(2):
                for i, r in enumerate(sorted(held[h])):
                    held[h][r] = held[h][r] + moving[h][i * rows : (i + 1) * rows]
            if level + 1 == len(bits):
                break
            for h in range(2):
                bit = orders[h][level + 1]
                going = [r for r in sorted(held[h]) if r & bit]
                moving[h] = swap(jnp.concatenate([held[h][r] for r in going], axis=0), 2 * bit)
                for r in going:
                    del held[h][r]
        done = jnp.concatenate([held[h][0] for h in range(2)], axis=1)
        out = lax.dynamic_update_slice(out, done, (0, place * width))
        token = moving
    return out


def solution(mesh):
    sizes = (mesh.shape["occ"], mesh.shape["vir"])

    def run(*args):
        return per_device(sizes, *args)

    in_specs = (P(("occ", "vir"), None), P(("occ", "vir"), None), P("vir", "occ"), P("vir", "occ"))
    out_specs = P(("occ", "vir"), None)
    return jax.shard_map(run, mesh=mesh, in_specs=in_specs, out_specs=out_specs, check_vma=False)
```

time: 136 us -> 148 us (1.088)
  Pallas kernels: 0 us -> 18.5 us
  matrix products: 10.8 us -> 0 us
  waiting for transfers between devices: 71.6 us -> 80.6 us
  starting transfers between devices: 33.5 us -> 30.7 us
  local copies, waits for them, and re-layouts: 6.98 us -> 4.48 us
  other arithmetic: 10.6 us -> 12.8 us
  between operations: 2.38 us -> 0.42 us
    pallas_call x0 -> x9, Pallas kernels: none -> 18.5 us  [the longest x8 17.8 us: products(): pl.pallas_call(functools.partial(dot_kernel, lists, names), out_shape=[ja...]
    dot_general x8 -> x0, matrix products: 10.8 us -> none  [the longest x4 5.38 us: per_device(): jnp.dot(lhs_away, rhs, precision=HIGH, preferred_element_type=jnp.float32)]
    add x12 -> x16, other arithmetic: 1.69 us -> 7.92 us  [per_device(): held[h][r] = held[h][r] + moving[h][i * rows:(i + 1) * rows]]
    ppermute x23, waiting for transfers between devices: 46.3 us -> 51.8 us  [swap(): return lax.ppermute(x, 'vir', [(i, i ^ bits) for i in range(n_vir)])]
    ppermute x2, waiting for transfers between devices: 23.4 us -> 28.8 us  [line_blocks(): moving = lax.ppermute(moving, 'occ', pairs)]
    select_n x4 -> x0, other arithmetic: 3.88 us -> none  [per_device(): first = jnp.where(low == 0, block, other)]
    slice x16 -> x0, local copies, waits for them, and re-layouts: 2.35 us -> none  [the longest x4 1.13 us: per_device(): rel[r][cut[h]]]
    ppermute x3, waiting for transfers between devices: 1.98 us -> 0.01 us  [line_blocks(): moving = lax.ppermute(block, 'occ', pairs)]
  transfers between devices with their start and end apart: 28 -> 28, of which waited for: 17 -> 15; matrix products, arithmetic and copies ran while one was open for 17% -> 7% of each run, Pallas kernels for 0% -> 11%
where the time goes in v4:
time: 148 us
  waiting for transfers between devices  80.6 us (54%)
  starting transfers between devices  30.7 us (21%)
  Pallas kernels  18.5 us (12%)
  other arithmetic  12.8 us (9%)
  local copies, waits for them, and re-layouts  4.48 us (3%)
    ppermute x23, waiting for transfers between devices, swap(): return lax.ppermute(x, 'vir', [(i, i ^ bits) for i in range(n_vir)])  51.8 us
    ppermute x2, waiting for transfers between devices, line_blocks(): moving = lax.ppermute(moving, 'occ', pairs)  28.8 us
    ppermute x23, starting transfers between devices, swap(): return lax.ppermute(x, 'vir', [(i, i ^ bits) for i in range(n_vir)])  22.5 us
    pallas_call x8, Pallas kernels, products(): pl.pallas_call(functools.partial(dot_kernel, lists, names), out_shape=[ja...  17.8 us
    add x16, other arithmetic, per_device(): held[h][r] = held[h][r] + moving[h][i * rows:(i + 1) * rows]  7.92 us
    ppermute x3, starting transfers between devices, line_blocks(): moving = lax.ppermute(block, 'occ', pairs)  5.44 us
    unnamed x40, local copies, waits for them, and re-layouts  4.17 us
  transfers between devices with their start and end apart: 28, of which 15 were waited for; matrix products, arithmetic and copies ran while one was open for 7% of the time, Pallas kernels for 11%

profile of v4, /device:TPU:0, one launch (start us, length us, event | category | flops | bytes accessed | tf_op | source)
XLA Modules:
  0.0 147.6 jit_solution(1142226223948732408)
XLA Ops:
  0.0 0.8 convert_element_type.3
  1.3 0.3 bitcast_multiply_fusion.refs_3_
  1.6 1.1 copy-done.2
  2.7 0.8 cut.1
  3.5 0.5 collective-permute-start.2
  4.0 2.6 %collective-permute-start = (f32[128,768]{1,0:T(8,128)S(1)}, f32[128,768]{1,0:T(8,128)S(1)}, u32[]{:S(2)}, u32[]{:S(2)}) collective-permute-start(f32[128,768]{1,0:T(8,128)S(1)} %get-tuple-element.36), channel_id=1, source_target_pairs={{0,2},{1,3},{2,0},{3,1},{4,6},{5,7},{6,4},{7,5},{8,10},{9,11},{10,... | collective-permute-start | bytes 1179656 | tf_op jit(solution)/shard_map/ppermute | solution.py:149
  6.6 1.5 %collective-permute-start.1 = (f32[128,768]{1,0:T(8,128)S(1)}, f32[128,768]{1,0:T(8,128)S(1)}, u32[]{:S(2)}, u32[]{:S(2)}) collective-permute-start(f32[128,768]{1,0:T(8,128)S(1)} %get-tuple-element.37), channel_id=1, source_target_pairs={{0,4},{1,5},{2,6},{3,7},{4,0},{5,1},{6,2},{7,3},{8,12},{9,13},{10,... | collective-permute-start | bytes 1179656 | tf_op jit(solution)/shard_map/ppermute | solution.py:149
  8.1 2.0 %collective-permute-start.8 = (f32[384,768]{1,0:T(8,128)S(1)}, f32[384,768]{1,0:T(8,128)}, u32[]{:S(2)}, u32[]{:S(2)}) collective-permute-start(f32[384,768]{1,0:T(8,128)S(1)} %bitcast_multiply_fusion.refs_3_), channel_id=1, source_target_pairs={{0,8},{16,24},{8,0},{24,16},{1,9},{17,25},{9,1},{25,17},{2,10},{18... | collective-permute-start | bytes 3538952 | tf_op jit(solution)/shard_map/ppermute | solution.py:122
  10.1 6.4 %collective-permute-done.refs_0_.refs_1_ = f32[128,768]{1,0:T(8,128)S(1)} collective-permute-done((f32[128,768]{1,0:T(8,128)S(1)}, f32[128,768]{1,0:T(8,128)S(1)}, u32[]{:S(2)}, u32[]{:S(2)}) %collective-permute-start) | collective-permute-done | bytes 393248 | tf_op jit(solution)/shard_map/ppermute | solution.py:149
  16.5 9.6 %collective-permute-done.1.refs_1_.refs_2_ = f32[128,768]{1,0:T(8,128)S(1)} collective-permute-done((f32[128,768]{1,0:T(8,128)S(1)}, f32[128,768]{1,0:T(8,128)S(1)}, u32[]{:S(2)}, u32[]{:S(2)}) %collective-permute-start.1) | collective-permute-done | bytes 393248 | tf_op jit(solution)/shard_map/ppermute | solution.py:149
  26.2 1.7 %products.8 = (f32[256,384]{1,0:T(8,128)S(1)}, f32[256,384]{1,0:T(8,128)S(1)}) custom-call(f32[128,768]{1,0:T(8,128)S(1)} %collective-permute-done.refs_0_.refs_1_, f32[128,768]{1,0:T(8,128)S(1)} %collective-permute-done.1.refs_1_.refs_2_, f32[128,768]{1,0:T(8,128)S(1)} %collective-permute-done.3.refs_2_, f32[384,768]{1,0:T(8,128)S(1)} %bitcast_multiply_fusion.refs_3_, ...), custom_call_target="tpu_custom_call" | custom-call | flops 1 | bytes 1 | tf_op jit(solution)/shard_map/products/pallas_call | solution.py:91
  27.9 1.6 %collective-permute-start.6 = (f32[256,384]{1,0:T(8,128)S(1)}, f32[256,384]{1,0:T(8,128)S(1)}, u32[]{:S(2)}, u32[]{:S(2)}) collective-permute-start(f32[256,384]{1,0:T(8,128)S(1)} %get-tuple-element.41), channel_id=1, source_target_pairs={{0,4},{1,5},{2,6},{3,7},{4,0},{5,1},{6,2},{7,3},{8,12},{9,13},{10,... | collective-permute-start | bytes 1179656 | tf_op jit(solution)/shard_map/ppermute | solution.py:149
  29.5 0.5 collective-permute-start.4
  30.0 1.7 %collective-permute-start.14 = (f32[384,768]{1,0:T(8,128)S(1)}, f32[384,768]{1,0:T(8,128)}, u32[]{:S(2)}, u32[]{:S(2)}) collective-permute-start(f32[384,768]{1,0:T(8,128)S(1)} %bitcast_multiply_fusion.refs_3_), channel_id=1, source_target_pairs={{8,16},{16,8},{9,17},{17,9},{10,18},{18,10},{11,19},{19,11},{12,20... | collective-permute-start | bytes 3538952 | tf_op jit(solution)/shard_map/ppermute | solution.py:122
  31.7 1.7 %products.9 = (f32[256,384]{1,0:T(8,128)S(1)}, f32[256,384]{1,0:T(8,128)S(1)}) custom-call(f32[128,768]{1,0:T(8,128)S(1)} %get-tuple-element.35.refs_0_, f32[128,768]{1,0:T(8,128)S(1)} %collective-permute-done.refs_0_.refs_1_, f32[128,768]{1,0:T(8,128)S(1)} %collective-permute-done.1.refs_1_.refs_2_, f32[384,768]{1,0:T(8,128)S(1)} %bitcast_multiply_fusion.refs_3_, ...), custom_call_target="tpu_custom_call" | custom-call | flops 1 | bytes 1 | tf_op jit(solution)/shard_map/products/pallas_call | solution.py:91
  33.4 5.0 %collective-permute-done.6 = f32[256,384]{1,0:T(8,128)S(1)} collective-permute-done((f32[256,384]{1,0:T(8,128)S(1)}, f32[256,384]{1,0:T(8,128)S(1)}, u32[]{:S(2)}, u32[]{:S(2)}) %collective-permute-start.6) | collective-permute-done | bytes 393248 | tf_op jit(solution)/shard_map/ppermute | solution.py:149
  38.5 1.5 %collective-permute-start.7 = (f32[128,384]{1,0:T(8,128)S(1)}, f32[128,384]{1,0:T(8,128)S(1)}, u32[]{:S(2)}, u32[]{:S(2)}) collective-permute-start(f32[128,384]{1,0:T(8,128)S(1)} %slice_add_fusion.12), channel_id=1, source_target_pairs={{0,2},{1,3},{2,0},{3,1},{4,6},{5,7},{6,4},{7,5},{8,10},{9,11},{10,... | collective-permute-start | bytes 589832 | tf_op jit(solution)/shard_map/ppermute | solution.py:149
  40.0 0.6 collective-permute-start.5
  40.6 3.6 %collective-permute-done.7 = f32[128,384]{1,0:T(8,128)S(1)} collective-permute-done((f32[128,384]{1,0:T(8,128)S(1)}, f32[128,384]{1,0:T(8,128)S(1)}, u32[]{:S(2)}, u32[]{:S(2)}) %collective-permute-start.7) | collective-permute-done | bytes 196640 | tf_op jit(solution)/shard_map/ppermute | solution.py:149
  44.2 1.5 %collective-permute-done.5 = f32[128,384]{1,0:T(8,128)S(1)} collective-permute-done((f32[128,384]{1,0:T(8,128)S(1)}, f32[128,384]{1,0:T(8,128)S(1)}, u32[]{:S(2)}, u32[]{:S(2)}) %collective-permute-start.5) | collective-permute-done | bytes 196640 | tf_op jit(solution)/shard_map/ppermute | solution.py:149
  45.8 1.3 collective-permute-start.15
  47.1 1.7 %collective-permute-done.9.refs_4_ = f32[384,768]{1,0:T(8,128)S(1)} collective-permute-done((f32[384,768]{1,0:T(8,128)}, f32[384,768]{1,0:T(8,128)S(1)}, u32[]{:S(2)}, u32[]{:S(2)}) %collective-permute-start.9) | collective-permute-done | bytes 1179680 | tf_op jit(solution)/shard_map/ppermute | solution.py:149
  48.8 3.8 %products.10 = (f32[256,384]{1,0:T(8,128)}, f32[256,384]{1,0:T(8,128)}) custom-call(f32[128,768]{1,0:T(8,128)S(1)} %collective-permute-done.refs_0_.refs_1_, f32[128,768]{1,0:T(8,128)S(1)} %collective-permute-done.1.refs_1_.refs_2_, f32[128,768]{1,0:T(8,128)S(1)} %collective-permute-done.3.refs_2_, f32[384,768]{1,0:T(8,128)} %collective-permute-done.8.refs_3_, ...), custom_call_target="tpu_custom_call" | custom-call | flops 1 | bytes 1 | tf_op jit(solution)/shard_map/products/pallas_call | solution.py:91
  52.6 0.6 collective-permute-start.12
  53.2 1.5 %collective-permute-start.10 = (f32[256,384]{1,0:T(8,128)}, f32[256,384]{1,0:T(8,128)}, u32[]{:S(2)}, u32[]{:S(2)}) collective-permute-start(f32[256,384]{1,0:T(8,128)} %get-tuple-element.46), channel_id=1, source_target_pairs={{0,2},{1,3},{2,0},{3,1},{4,6},{5,7},{6,4},{7,5},{8,10},{9,11},{10,... | collective-permute-start | bytes 1179656 | tf_op jit(solution)/shard_map/ppermute | solution.py:149
  54.7 1.7 %collective-permute-start.21 = (f32[384,768]{1,0:T(8,128)}, f32[384,768]{1,0:T(8,128)}, u32[]{:S(2)}, u32[]{:S(2)}) collective-permute-start(f32[384,768]{1,0:T(8,128)} %collective-permute-done.8.refs_3_), channel_id=1, source_target_pairs={{8,16},{16,8},{9,17},{17,9},{10,18},{18,10},{11,19},{19,11},{12,20... | collective-permute-start | bytes 3538952 | tf_op jit(solution)/shard_map/ppermute | solution.py:122
  56.4 3.0 %products.11 = (f32[256,384]{1,0:T(8,128)S(1)}, f32[256,384]{1,0:T(8,128)S(1)}) custom-call(f32[128,768]{1,0:T(8,128)S(1)} %get-tuple-element.35.refs_0_, f32[128,768]{1,0:T(8,128)S(1)} %collective-permute-done.refs_0_.refs_1_, f32[128,768]{1,0:T(8,128)S(1)} %collective-permute-done.1.refs_1_.refs_2_, f32[384,768]{1,0:T(8,128)} %collective-permute-done.8.refs_3_, ...), custom_call_target="tpu_custom_call" | custom-call | flops 1 | bytes 1 | tf_op jit(solution)/shard_map/products/pallas_call | solution.py:91
  59.4 4.7 %collective-permute-done.12 = f32[256,384]{1,0:T(8,128)} collective-permute-done((f32[256,384]{1,0:T(8,128)}, f32[256,384]{1,0:T(8,128)}, u32[]{:S(2)}, u32[]{:S(2)}) %collective-permute-start.12) | collective-permute-done | bytes 393248 | tf_op jit(solution)/shard_map/ppermute | solution.py:149
  64.1 0.9 slice_add_fusion.8
  65.1 0.6 collective-permute-start.13
  65.7 0.9 slice_add_fusion.10
  66.7 1.6 %collective-permute-start.11 = (f32[128,384]{1,0:T(8,128)S(1)}, f32[128,384]{1,0:T(8,128)}, u32[]{:S(2)}, u32[]{:S(2)}) collective-permute-start(f32[128,384]{1,0:T(8,128)S(1)} %slice_add_fusion.10), channel_id=1, source_target_pairs={{0,4},{1,5},{2,6},{3,7},{4,0},{5,1},{6,2},{7,3},{8,12},{9,13},{10,... | collective-permute-start | bytes 589832 | tf_op jit(solution)/shard_map/ppermute | solution.py:149
  68.2 17.7 %collective-permute-done.15 = f32[384,768]{1,0:T(8,128)} collective-permute-done((f32[384,768]{1,0:T(8,128)}, f32[384,768]{1,0:T(8,128)}, u32[]{:S(2)}, u32[]{:S(2)}) %collective-permute-start.15) | collective-permute-done | bytes 1179680 | tf_op jit(solution)/shard_map/ppermute | solution.py:126
  85.9 1.4 broadcast_select_fusion.1.refs_3_
  87.4 0.7 copy-done.18
  88.1 1.5 collective-permute-start.22
  89.6 1.4 collective-permute-done.16.refs_4_
  90.9 2.5 %products.12 = (f32[256,384]{1,0:T(8,128)}, f32[256,384]{1,0:T(8,128)}) custom-call(f32[128,768]{1,0:T(8,128)S(1)} %collective-permute-done.refs_0_.refs_1_, f32[128,768]{1,0:T(8,128)S(1)} %collective-permute-done.1.refs_1_.refs_2_, f32[128,768]{1,0:T(8,128)S(1)} %collective-permute-done.3.refs_2_, f32[384,768]{1,0:T(8,128)S(1)} %broadcast_select_fusion.1.refs_3_, ...), custom_call_target="tpu_custom_call" | custom-call | flops 1 | bytes 1 | tf_op jit(solution)/shard_map/products/pallas_call | solution.py:91
  93.4 1.7 %collective-permute-start.19 = (f32[256,384]{1,0:T(8,128)}, f32[256,384]{1,0:T(8,128)}, u32[]{:S(2)}, u32[]{:S(2)}) collective-permute-start(f32[256,384]{1,0:T(8,128)} %get-tuple-element.53), channel_id=1, source_target_pairs={{0,4},{1,5},{2,6},{3,7},{4,0},{5,1},{6,2},{7,3},{8,12},{9,13},{10,... | collective-permute-start | bytes 1179656 | tf_op jit(solution)/shard_map/ppermute | solution.py:149
  95.2 0.4 collective-permute-start.17
  95.5 1.3 copy-done.1
  96.8 1.7 %products.13 = (f32[256,384]{1,0:T(8,128)S(1)}, f32[256,384]{1,0:T(8,128)S(1)}) custom-call(f32[128,768]{1,0:T(8,128)S(1)} %get-tuple-element.35.refs_0_, f32[128,768]{1,0:T(8,128)S(1)} %collective-permute-done.refs_0_.refs_1_, f32[128,768]{1,0:T(8,128)S(1)} %collective-permute-done.1.refs_1_.refs_2_, f32[384,768]{1,0:T(8,128)S(1)} %broadcast_select_fusion.1.refs_3_, ...), custom_call_target="tpu_custom_call" | custom-call | flops 1 | bytes 1 | tf_op jit(solution)/shard_map/products/pallas_call | solution.py:91
  98.5 6.4 %collective-permute-done.19 = f32[256,384]{1,0:T(8,128)} collective-permute-done((f32[256,384]{1,0:T(8,128)}, f32[256,384]{1,0:T(8,128)}, u32[]{:S(2)}, u32[]{:S(2)}) %collective-permute-start.19) | collective-permute-done | bytes 393248 | tf_op jit(solution)/shard_map/ppermute | solution.py:149
  104.9 0.9 slice_add_fusion.4
  105.8 1.7 %collective-permute-start.20 = (f32[128,384]{1,0:T(8,128)S(1)}, f32[128,384]{1,0:T(8,128)S(1)}, u32[]{:S(2)}, u32[]{:S(2)}) collective-permute-start(f32[128,384]{1,0:T(8,128)S(1)} %slice_add_fusion.4), channel_id=1, source_target_pairs={{0,2},{1,3},{2,0},{3,1},{4,6},{5,7},{6,4},{7,5},{8,10},{9,11},{10,... | collective-permute-start | bytes 589832 | tf_op jit(solution)/shard_map/ppermute | solution.py:149
  107.5 0.9 slice_add_fusion.6
  108.5 0.6 collective-permute-start.18
  109.1 11.1 %collective-permute-done.22 = f32[384,768]{1,0:T(8,128)} collective-permute-done((f32[384,768]{1,0:T(8,128)}, f32[384,768]{1,0:T(8,128)}, u32[]{:S(2)}, u32[]{:S(2)}) %collective-permute-start.22) | collective-permute-done | bytes 1179680 | tf_op jit(solution)/shard_map/ppermute | solution.py:126
  120.2 1.4 broadcast_select_fusion.refs_3_
  122.1 0.8 copy-done.6
  122.9 1.0 fusion.4
  123.9 1.1 fusion.5
  125.0 1.7 %products.14 = (f32[256,384]{1,0:T(8,128)S(1)}, f32[256,384]{1,0:T(8,128)S(1)}) custom-call(f32[128,768]{1,0:T(8,128)S(1)} %collective-permute-done.refs_0_.refs_1_, f32[128,768]{1,0:T(8,128)S(1)} %collective-permute-done.1.refs_1_.refs_2_, f32[128,768]{1,0:T(8,128)S(1)} %collective-permute-done.3.refs_2_, f32[384,768]{1,0:T(8,128)S(1)} %broadcast_select_fusion.refs_3_, ...), custom_call_target="tpu_custom_call" | custom-call | flops 1 | bytes 1 | tf_op jit(solution)/shard_map/products/pallas_call | solution.py:91
  126.7 1.6 %collective-permute-start.26 = (f32[256,384]{1,0:T(8,128)S(1)}, f32[256,384]{1,0:T(8,128)S(1)}, u32[]{:S(2)}, u32[]{:S(2)}) collective-permute-start(f32[256,384]{1,0:T(8,128)S(1)} %get-tuple-element.59), channel_id=1, source_target_pairs={{0,4},{1,5},{2,6},{3,7},{4,0},{5,1},{6,2},{7,3},{8,12},{9,13},{10,... | collective-permute-start | bytes 1179656 | tf_op jit(solution)/shard_map/ppermute | solution.py:149
  128.2 1.0 fusion.2
  129.2 0.6 collective-permute-start.24
  129.8 1.0 fusion.3
  130.8 1.7 %products.15 = (f32[256,384]{1,0:T(8,128)S(1)}, f32[256,384]{1,0:T(8,128)S(1)}) custom-call(f32[128,768]{1,0:T(8,128)S(1)} %get-tuple-element.35.refs_0_, f32[128,768]{1,0:T(8,128)S(1)} %collective-permute-done.refs_0_.refs_1_, f32[128,768]{1,0:T(8,128)S(1)} %collective-permute-done.1.refs_1_.refs_2_, f32[384,768]{1,0:T(8,128)S(1)} %broadcast_select_fusion.refs_3_, ...), custom_call_target="tpu_custom_call" | custom-call | flops 1 | bytes 1 | tf_op jit(solution)/shard_map/products/pallas_call | solution.py:91
  132.6 5.7 %collective-permute-done.26 = f32[256,384]{1,0:T(8,128)S(1)} collective-permute-done((f32[256,384]{1,0:T(8,128)S(1)}, f32[256,384]{1,0:T(8,128)S(1)}, u32[]{:S(2)}, u32[]{:S(2)}) %collective-permute-start.26) | collective-permute-done | bytes 393248 | tf_op jit(solution)/shard_map/ppermute | solution.py:149
  138.3 1.9 %collective-permute-start.27 = (f32[128,384]{1,0:T(8,128)S(1)}, f32[128,384]{1,0:T(8,128)S(1)}, u32[]{:S(2)}, u32[]{:S(2)}) collective-permute-start(f32[128,384]{1,0:T(8,128)S(1)} %slice_add_fusion), channel_id=1, source_target_pairs={{0,2},{1,3},{2,0},{3,1},{4,6},{5,7},{6,4},{7,5},{8,10},{9,11},{10,... | collective-permute-start | bytes 589832 | tf_op jit(solution)/shard_map/ppermute | solution.py:149
  140.5 0.7 collective-permute-start.25
  141.2 3.7 %collective-permute-done.27 = f32[128,384]{1,0:T(8,128)S(1)} collective-permute-done((f32[128,384]{1,0:T(8,128)S(1)}, f32[128,384]{1,0:T(8,128)S(1)}, u32[]{:S(2)}, u32[]{:S(2)}) %collective-permute-start.27) | collective-permute-done | bytes 196640 | tf_op jit(solution)/shard_map/ppermute | solution.py:149
  145.0 1.8 %collective-permute-done.25 = f32[128,384]{1,0:T(8,128)S(1)} collective-permute-done((f32[128,384]{1,0:T(8,128)S(1)}, f32[128,384]{1,0:T(8,128)S(1)}, u32[]{:S(2)}, u32[]{:S(2)}) %collective-permute-start.25) | collective-permute-done | bytes 196640 | tf_op jit(solution)/shard_map/ppermute | solution.py:149
  146.8 0.8 maximum_dynamic-update-slice_fusion.3
  (68 shorter events, 1.5 us)
Async XLA Ops:
  0.0 1.3 copy-start.9
  1.3 1.4 copy-start.2
  1.3 1.4 copy-start.7
  3.5 22.7 %collective-permute-start.2 = (f32[384,768]{1,0:T(8,128)S(1)}, f32[384,768]{1,0:T(8,128)S(1)}, u32[]{:S(2)}, u32[]{:S(2)}) collective-permute-start(f32[384,768]{1,0:T(8,128)S(1)} %bitcast_multiply_fusion.refs_3_), channel_id=1, source_target_pairs={{0,1},{1,0},{2,3},{3,2},{4,5},{5,4},{6,7},{7,6},{8,9},{9,8},{10,11... | collective-permute-start | bytes 3538952 | tf_op jit(solution)/shard_map/ppermute | solution.py:149
  4.0 12.5 %collective-permute-start = (f32[128,768]{1,0:T(8,128)S(1)}, f32[128,768]{1,0:T(8,128)S(1)}, u32[]{:S(2)}, u32[]{:S(2)}) collective-permute-start(f32[128,768]{1,0:T(8,128)S(1)} %get-tuple-element.36), channel_id=1, source_target_pairs={{0,2},{1,3},{2,0},{3,1},{4,6},{5,7},{6,4},{7,5},{8,10},{9,11},{10,... | collective-permute-start | bytes 1179656 | tf_op jit(solution)/shard_map/ppermute | solution.py:149
  6.6 19.6 %collective-permute-start.1 = (f32[128,768]{1,0:T(8,128)S(1)}, f32[128,768]{1,0:T(8,128)S(1)}, u32[]{:S(2)}, u32[]{:S(2)}) collective-permute-start(f32[128,768]{1,0:T(8,128)S(1)} %get-tuple-element.37), channel_id=1, source_target_pairs={{0,4},{1,5},{2,6},{3,7},{4,0},{5,1},{6,2},{7,3},{8,12},{9,13},{10,... | collective-permute-start | bytes 1179656 | tf_op jit(solution)/shard_map/ppermute | solution.py:149
  8.1 18.1 %collective-permute-start.3 = (f32[128,768]{1,0:T(8,128)S(1)}, f32[128,768]{1,0:T(8,128)S(1)}, u32[]{:S(2)}, u32[]{:S(2)}) collective-permute-start(f32[128,768]{1,0:T(8,128)S(1)} %get-tuple-element.38), channel_id=1, source_target_pairs={{0,6},{1,7},{2,4},{3,5},{4,2},{5,3},{6,0},{7,1},{8,14},{9,15},{10,... | collective-permute-start | bytes 1179656 | tf_op jit(solution)/shard_map/ppermute | solution.py:149
  8.1 32.5 %collective-permute-start.8 = (f32[384,768]{1,0:T(8,128)S(1)}, f32[384,768]{1,0:T(8,128)}, u32[]{:S(2)}, u32[]{:S(2)}) collective-permute-start(f32[384,768]{1,0:T(8,128)S(1)} %bitcast_multiply_fusion.refs_3_), channel_id=1, source_target_pairs={{0,8},{16,24},{8,0},{24,16},{1,9},{17,25},{9,1},{25,17},{2,10},{18... | collective-permute-start | bytes 3538952 | tf_op jit(solution)/shard_map/ppermute | solution.py:122
  27.9 10.5 %collective-permute-start.6 = (f32[256,384]{1,0:T(8,128)S(1)}, f32[256,384]{1,0:T(8,128)S(1)}, u32[]{:S(2)}, u32[]{:S(2)}) collective-permute-start(f32[256,384]{1,0:T(8,128)S(1)} %get-tuple-element.41), channel_id=1, source_target_pairs={{0,4},{1,5},{2,6},{3,7},{4,0},{5,1},{6,2},{7,3},{8,12},{9,13},{10,... | collective-permute-start | bytes 1179656 | tf_op jit(solution)/shard_map/ppermute | solution.py:149
  29.5 10.5 %collective-permute-start.4 = (f32[256,384]{1,0:T(8,128)S(1)}, f32[256,384]{1,0:T(8,128)S(1)}, u32[]{:S(2)}, u32[]{:S(2)}) collective-permute-start(f32[256,384]{1,0:T(8,128)S(1)} %get-tuple-element.40), channel_id=1, source_target_pairs={{0,2},{1,3},{2,0},{3,1},{4,6},{5,7},{6,4},{7,5},{8,10},{9,11},{10,... | collective-permute-start | bytes 1179656 | tf_op jit(solution)/shard_map/ppermute | solution.py:149
  30.0 15.7 %collective-permute-start.14 = (f32[384,768]{1,0:T(8,128)S(1)}, f32[384,768]{1,0:T(8,128)}, u32[]{:S(2)}, u32[]{:S(2)}) collective-permute-start(f32[384,768]{1,0:T(8,128)S(1)} %bitcast_multiply_fusion.refs_3_), channel_id=1, source_target_pairs={{8,16},{16,8},{9,17},{17,9},{10,18},{18,10},{11,19},{19,11},{12,20... | collective-permute-start | bytes 3538952 | tf_op jit(solution)/shard_map/ppermute | solution.py:122
  38.4 14.1 %copy-start.10 = (f32[256,384]{1,0:T(8,128)}, f32[256,384]{1,0:T(8,128)S(1)}, u32[]{:S(2)}) copy-start(f32[256,384]{1,0:T(8,128)S(1)} %collective-permute-done.6) | copy-start | bytes 1179652
  38.5 5.7 %collective-permute-start.7 = (f32[128,384]{1,0:T(8,128)S(1)}, f32[128,384]{1,0:T(8,128)S(1)}, u32[]{:S(2)}, u32[]{:S(2)}) collective-permute-start(f32[128,384]{1,0:T(8,128)S(1)} %slice_add_fusion.12), channel_id=1, source_target_pairs={{0,2},{1,3},{2,0},{3,1},{4,6},{5,7},{6,4},{7,5},{8,10},{9,11},{10,... | collective-permute-start | bytes 589832 | tf_op jit(solution)/shard_map/ppermute | solution.py:149
  40.0 5.8 %copy-start.12 = (f32[256,384]{1,0:T(8,128)}, f32[256,384]{1,0:T(8,128)S(1)}, u32[]{:S(2)}) copy-start(f32[256,384]{1,0:T(8,128)S(1)} %collective-permute-done.4) | copy-start | bytes 1179652
  40.0 5.7 %collective-permute-start.5 = (f32[128,384]{1,0:T(8,128)S(1)}, f32[128,384]{1,0:T(8,128)S(1)}, u32[]{:S(2)}, u32[]{:S(2)}) collective-permute-start(f32[128,384]{1,0:T(8,128)S(1)} %slice_add_fusion.14), channel_id=1, source_target_pairs={{0,4},{1,5},{2,6},{3,7},{4,0},{5,1},{6,2},{7,3},{8,12},{9,13},{10,... | collective-permute-start | bytes 589832 | tf_op jit(solution)/shard_map/ppermute | solution.py:149
  44.2 8.4 %copy-start.14 = (f32[128,384]{1,0:T(8,128)}, f32[128,384]{1,0:T(8,128)S(1)}, u32[]{:S(2)}) copy-start(f32[128,384]{1,0:T(8,128)S(1)} %collective-permute-done.7) | copy-start | bytes 589828
  45.7 6.8 %copy-start.16 = (f32[128,384]{1,0:T(8,128)}, f32[128,384]{1,0:T(8,128)S(1)}, u32[]{:S(2)}) copy-start(f32[128,384]{1,0:T(8,128)S(1)} %collective-permute-done.5) | copy-start | bytes 589828
  45.7 3.1 %collective-permute-start.9 = (f32[384,768]{1,0:T(8,128)}, f32[384,768]{1,0:T(8,128)S(1)}, u32[]{:S(2)}, u32[]{:S(2)}) collective-permute-start(f32[384,768]{1,0:T(8,128)} %collective-permute-done.8.refs_3_), channel_id=1, source_target_pairs={{0,1},{1,0},{2,3},{3,2},{4,5},{5,4},{6,7},{7,6},{8,9},{9,8},{10,11... | collective-permute-start | bytes 3538952 | tf_op jit(solution)/shard_map/ppermute | solution.py:149
  45.8 40.2 %collective-permute-start.15 = (f32[384,768]{1,0:T(8,128)}, f32[384,768]{1,0:T(8,128)}, u32[]{:S(2)}, u32[]{:S(2)}) collective-permute-start(f32[384,768]{1,0:T(8,128)} %collective-permute-done.14), channel_id=1, source_target_pairs={{8,0},{16,24},{9,1},{17,25},{10,2},{18,26},{11,3},{19,27},{12,4},{... | collective-permute-start | bytes 3538952 | tf_op jit(solution)/shard_map/ppermute | solution.py:126
  52.6 11.5 %collective-permute-start.12 = (f32[256,384]{1,0:T(8,128)}, f32[256,384]{1,0:T(8,128)}, u32[]{:S(2)}, u32[]{:S(2)}) collective-permute-start(f32[256,384]{1,0:T(8,128)} %get-tuple-element.47), channel_id=1, source_target_pairs={{0,4},{1,5},{2,6},{3,7},{4,0},{5,1},{6,2},{7,3},{8,12},{9,13},{10,... | collective-permute-start | bytes 1179656 | tf_op jit(solution)/shard_map/ppermute | solution.py:149
  53.2 12.5 %collective-permute-start.10 = (f32[256,384]{1,0:T(8,128)}, f32[256,384]{1,0:T(8,128)}, u32[]{:S(2)}, u32[]{:S(2)}) collective-permute-start(f32[256,384]{1,0:T(8,128)} %get-tuple-element.46), channel_id=1, source_target_pairs={{0,2},{1,3},{2,0},{3,1},{4,6},{5,7},{6,4},{7,5},{8,10},{9,11},{10,... | collective-permute-start | bytes 1179656 | tf_op jit(solution)/shard_map/ppermute | solution.py:149
  54.7 33.3 %collective-permute-start.21 = (f32[384,768]{1,0:T(8,128)}, f32[384,768]{1,0:T(8,128)}, u32[]{:S(2)}, u32[]{:S(2)}) collective-permute-start(f32[384,768]{1,0:T(8,128)} %collective-permute-done.8.refs_3_), channel_id=1, source_target_pairs={{8,16},{16,8},{9,17},{17,9},{10,18},{18,10},{11,19},{19,11},{12,20... | collective-permute-start | bytes 3538952 | tf_op jit(solution)/shard_map/ppermute | solution.py:122
  59.4 27.9 %copy-start.3 = (f32[256,384]{1,0:T(8,128)}, f32[256,384]{1,0:T(8,128)S(1)}, u32[]{:S(2)}) copy-start(f32[256,384]{1,0:T(8,128)S(1)} %get-tuple-element.49) | copy-start | bytes 1179652
  59.4 27.9 %copy-start.5 = (f32[256,384]{1,0:T(8,128)}, f32[256,384]{1,0:T(8,128)S(1)}, u32[]{:S(2)}) copy-start(f32[256,384]{1,0:T(8,128)S(1)} %get-tuple-element.50) | copy-start | bytes 1179652
  65.1 22.3 %collective-permute-start.13 = (f32[128,384]{1,0:T(8,128)S(1)}, f32[128,384]{1,0:T(8,128)S(1)}, u32[]{:S(2)}, u32[]{:S(2)}) collective-permute-start(f32[128,384]{1,0:T(8,128)S(1)} %slice_add_fusion.8), channel_id=1, source_target_pairs={{0,2},{1,3},{2,0},{3,1},{4,6},{5,7},{6,4},{7,5},{8,10},{9,11},{10,... | collective-permute-start | bytes 589832 | tf_op jit(solution)/shard_map/ppermute | solution.py:149
  66.7 21.4 %collective-permute-start.11 = (f32[128,384]{1,0:T(8,128)S(1)}, f32[128,384]{1,0:T(8,128)}, u32[]{:S(2)}, u32[]{:S(2)}) collective-permute-start(f32[128,384]{1,0:T(8,128)S(1)} %slice_add_fusion.10), channel_id=1, source_target_pairs={{0,4},{1,5},{2,6},{3,7},{4,0},{5,1},{6,2},{7,3},{8,12},{9,13},{10,... | collective-permute-start | bytes 589832 | tf_op jit(solution)/shard_map/ppermute | solution.py:149
  87.4 0.7 copy-start.18
  88.1 2.8 %collective-permute-start.16 = (f32[384,768]{1,0:T(8,128)S(1)}, f32[384,768]{1,0:T(8,128)S(1)}, u32[]{:S(2)}, u32[]{:S(2)}) collective-permute-start(f32[384,768]{1,0:T(8,128)S(1)} %broadcast_select_fusion.1.refs_3_), channel_id=1, source_target_pairs={{0,1},{1,0},{2,3},{3,2},{4,5},{5,4},{6,7},{7,6},{8,9},{9,8},{10,11... | collective-permute-start | bytes 3538952 | tf_op jit(solution)/shard_map/ppermute | solution.py:149
  88.1 32.1 %collective-permute-start.22 = (f32[384,768]{1,0:T(8,128)}, f32[384,768]{1,0:T(8,128)}, u32[]{:S(2)}, u32[]{:S(2)}) collective-permute-start(f32[384,768]{1,0:T(8,128)} %collective-permute-done.21), channel_id=1, source_target_pairs={{8,0},{16,24},{9,1},{17,25},{10,2},{18,26},{11,3},{19,27},{12,4},{... | collective-permute-start | bytes 3538952 | tf_op jit(solution)/shard_map/ppermute | solution.py:126
  90.9 2.5 %copy-start = (f32[384,768]{1,0:T(8,128)}, f32[384,768]{1,0:T(8,128)S(1)}, u32[]{:S(2)}) copy-start(f32[384,768]{1,0:T(8,128)S(1)} %collective-permute-done.16.refs_4_) | copy-start | bytes 3538948
  93.4 11.5 %collective-permute-start.19 = (f32[256,384]{1,0:T(8,128)}, f32[256,384]{1,0:T(8,128)}, u32[]{:S(2)}, u32[]{:S(2)}) collective-permute-start(f32[256,384]{1,0:T(8,128)} %get-tuple-element.53), channel_id=1, source_target_pairs={{0,4},{1,5},{2,6},{3,7},{4,0},{5,1},{6,2},{7,3},{8,12},{9,13},{10,... | collective-permute-start | bytes 1179656 | tf_op jit(solution)/shard_map/ppermute | solution.py:149
  95.2 12.3 %collective-permute-start.17 = (f32[256,384]{1,0:T(8,128)}, f32[256,384]{1,0:T(8,128)}, u32[]{:S(2)}, u32[]{:S(2)}) collective-permute-start(f32[256,384]{1,0:T(8,128)} %get-tuple-element.52), channel_id=1, source_target_pairs={{0,2},{1,3},{2,0},{3,1},{4,6},{5,7},{6,4},{7,5},{8,10},{9,11},{10,... | collective-permute-start | bytes 1179656 | tf_op jit(solution)/shard_map/ppermute | solution.py:149
  95.5 1.3 copy-start.1
  105.8 15.8 %collective-permute-start.20 = (f32[128,384]{1,0:T(8,128)S(1)}, f32[128,384]{1,0:T(8,128)S(1)}, u32[]{:S(2)}, u32[]{:S(2)}) collective-permute-start(f32[128,384]{1,0:T(8,128)S(1)} %slice_add_fusion.4), channel_id=1, source_target_pairs={{0,2},{1,3},{2,0},{3,1},{4,6},{5,7},{6,4},{7,5},{8,10},{9,11},{10,... | collective-permute-start | bytes 589832 | tf_op jit(solution)/shard_map/ppermute | solution.py:149
  108.4 13.3 %copy-start.11 = (f32[256,384]{1,0:T(8,128)S(1)}, f32[256,384]{1,0:T(8,128)}, u32[]{:S(2)}) copy-start(f32[256,384]{1,0:T(8,128)} %copy-done.10) | copy-start | bytes 1179652
  108.5 13.3 %copy-start.15 = (f32[128,384]{1,0:T(8,128)S(1)}, f32[128,384]{1,0:T(8,128)}, u32[]{:S(2)}) copy-start(f32[128,384]{1,0:T(8,128)} %copy-done.14) | copy-start | bytes 589828
  108.5 13.3 %copy-start.13 = (f32[256,384]{1,0:T(8,128)S(1)}, f32[256,384]{1,0:T(8,128)}, u32[]{:S(2)}) copy-start(f32[256,384]{1,0:T(8,128)} %copy-done.12) | copy-start | bytes 1179652
  108.5 13.3 %copy-start.17 = (f32[128,384]{1,0:T(8,128)S(1)}, f32[128,384]{1,0:T(8,128)}, u32[]{:S(2)}) copy-start(f32[128,384]{1,0:T(8,128)} %copy-done.16) | copy-start | bytes 589828
  108.5 13.1 %collective-permute-start.18 = (f32[128,384]{1,0:T(8,128)S(1)}, f32[128,384]{1,0:T(8,128)S(1)}, u32[]{:S(2)}, u32[]{:S(2)}) collective-permute-start(f32[128,384]{1,0:T(8,128)S(1)} %slice_add_fusion.6), channel_id=1, source_target_pairs={{0,4},{1,5},{2,6},{3,7},{4,0},{5,1},{6,2},{7,3},{8,12},{9,13},{10,... | collective-permute-start | bytes 589832 | tf_op jit(solution)/shard_map/ppermute | solution.py:149
  121.6 3.3 %collective-permute-start.23 = (f32[384,768]{1,0:T(8,128)S(1)}, f32[384,768]{1,0:T(8,128)S(1)}, u32[]{:S(2)}, u32[]{:S(2)}) collective-permute-start(f32[384,768]{1,0:T(8,128)S(1)} %broadcast_select_fusion.refs_3_), channel_id=1, source_target_pairs={{0,1},{1,0},{2,3},{3,2},{4,5},{5,4},{6,7},{7,6},{8,9},{9,8},{10,11... | collective-permute-start | bytes 3538952 | tf_op jit(solution)/shard_map/ppermute | solution.py:149
  121.8 1.0 copy-start.6
  121.8 1.0 copy-start.19
  122.0 1.8 %copy-start.4 = (f32[256,384]{1,0:T(8,128)S(1)}, f32[256,384]{1,0:T(8,128)}, u32[]{:S(2)}) copy-start(f32[256,384]{1,0:T(8,128)} %copy-done.3) | copy-start | bytes 1179652
  126.7 11.6 %collective-permute-start.26 = (f32[256,384]{1,0:T(8,128)S(1)}, f32[256,384]{1,0:T(8,128)S(1)}, u32[]{:S(2)}, u32[]{:S(2)}) collective-permute-start(f32[256,384]{1,0:T(8,128)S(1)} %get-tuple-element.59), channel_id=1, source_target_pairs={{0,4},{1,5},{2,6},{3,7},{4,0},{5,1},{6,2},{7,3},{8,12},{9,13},{10,... | collective-permute-start | bytes 1179656 | tf_op jit(solution)/shard_map/ppermute | solution.py:149
  129.2 11.3 %collective-permute-start.24 = (f32[256,384]{1,0:T(8,128)S(1)}, f32[256,384]{1,0:T(8,128)S(1)}, u32[]{:S(2)}, u32[]{:S(2)}) collective-permute-start(f32[256,384]{1,0:T(8,128)S(1)} %get-tuple-element.58), channel_id=1, source_target_pairs={{0,2},{1,3},{2,0},{3,1},{4,6},{5,7},{6,4},{7,5},{8,10},{9,11},{10,... | collective-permute-start | bytes 1179656 | tf_op jit(solution)/shard_map/ppermute | solution.py:149
  130.8 1.7 %copy-start.8 = (f32[128,3072]{1,0:T(8,128)}, f32[128,3072]{1,0:T(8,128)S(1)}, u32[]{:S(2)}) copy-start(f32[128,3072]{1,0:T(8,128)S(1)} %maximum_dynamic-update-slice_fusion.2) | copy-start | bytes 4718596
  138.3 6.7 %collective-permute-start.27 = (f32[128,384]{1,0:T(8,128)S(1)}, f32[128,384]{1,0:T(8,128)S(1)}, u32[]{:S(2)}, u32[]{:S(2)}) collective-permute-start(f32[128,384]{1,0:T(8,128)S(1)} %slice_add_fusion), channel_id=1, source_target_pairs={{0,2},{1,3},{2,0},{3,1},{4,6},{5,7},{6,4},{7,5},{8,10},{9,11},{10,... | collective-permute-start | bytes 589832 | tf_op jit(solution)/shard_map/ppermute | solution.py:149
  140.5 6.2 %collective-permute-start.25 = (f32[128,384]{1,0:T(8,128)S(1)}, f32[128,384]{1,0:T(8,128)S(1)}, u32[]{:S(2)}, u32[]{:S(2)}) collective-permute-start(f32[128,384]{1,0:T(8,128)S(1)} %slice_add_fusion.2), channel_id=1, source_target_pairs={{0,4},{1,5},{2,6},{3,7},{4,0},{5,1},{6,2},{7,3},{8,12},{9,13},{10,... | collective-permute-start | bytes 589832 | tf_op jit(solution)/shard_map/ppermute | solution.py:149

commit v5 on v4

--- a/solution.py
+++ b/solution.py
@@ -9,7 +9,7 @@
 
 TILE_O = 32
 TILE_V = 128
-VMEM_LIMIT = 40 * 1024 * 1024
+VMEM_LIMIT = 12 * 1024 * 1024
 
 
 def masked(values, mask, tile_rows):
@@ -60,43 +60,51 @@
     return high, (x - high.astype(jnp.float32)).astype(jnp.bfloat16)
 
 
-def dot_kernel(lists, names, *refs):
+def dot_kernel(lists, names, choices, *refs):
     n = len(names)
+    which_ref, refs = refs[0], refs[1:]
     rel = dict(zip(names, refs[:n]))
-    own_ref, other_ref = refs[n : n + 2]
-    outs = refs[n + 2 :]
-    depth = own_ref.shape[0]
-    rows = refs[0].shape[0]
-    parts = {r: split(rel[r][...]) for r in names}
-    width = own_ref.shape[1] // 2
-    for h in range(2):
-        columns = pl.ds(h * width, width)
-        right = [split(ref[:, columns]) for ref in (own_ref, other_ref)]
-        for i, r in enumerate(lists[h]):
-            total = None
-            for k in range(2):
-                b_high, b_low = right[k]
-                a_high, a_low = (x[:, k * depth : (k + 1) * depth] for x in parts[r])
-                for a, b in ((a_high, b_low), (a_low, b_high), (a_high, b_high)):
-                    term = jnp.dot(a, b, preferred_element_type=jnp.float32)
-                    total = term if total is None else total + term
-            outs[h][i * rows : (i + 1) * rows, :] = total
-
-
-def products(lists, rel, own, other):
+    outs = refs[n + 2 * choices :]
+
+    def body(own_ref, other_ref):
+        depth = own_ref.shape[0]
+        rows = refs[0].shape[0]
+        parts = {r: split(rel[r][...]) for r in names}
+        width = own_ref.shape[1] // 2
+        for h in range(2):
+            columns = pl.ds(h * width, width)
+            right = [split(ref[:, columns]) for ref in (own_ref, other_ref)]
+            for i, r in enumerate(lists[h]):
+                total = None
+                for k in range(2):
+                    b_high, b_low = right[k]
+                    a_high, a_low = (x[:, k * depth : (k + 1) * depth] for x in parts[r])
+                    for a, b in ((a_high, b_low), (a_low, b_high), (a_high, b_high)):
+                        term = jnp.dot(a, b, preferred_element_type=jnp.float32)
+                        total = term if total is None else total + term
+                outs[h][i * rows : (i + 1) * rows, :] = total
+
+    for c in range(choices):
+        if choices == 1:
+            body(refs[n], refs[n + 1])
+        else:
+            pl.when(which_ref[0] == c)(functools.partial(body, refs[n + 2 * c], refs[n + 2 * c + 1]))
+
+
+def products(lists, rel, which, rights):
     names = sorted(set(lists[0]) | set(lists[1]))
-    rows, depth = rel[0].shape
-    width = own.shape[1] // 2
+    rows = rel[0].shape[0]
+    width = rights[0][0].shape[1] // 2
     count = len(lists[0])
     return pl.pallas_call(
-        functools.partial(dot_kernel, lists, names),
+        functools.partial(dot_kernel, lists, names, len(rights)),
         out_shape=[jax.ShapeDtypeStruct((rows * count, width), jnp.float32)] * 2,
-        in_specs=in_vmem(len(names) + 2),
+        in_specs=[pl.BlockSpec(memory_space=pltpu.SMEM)] + in_vmem(len(names) + 2 * len(rights)),
         out_specs=in_vmem(2),
         compiler_params=pltpu.CompilerParams(vmem_limit_bytes=VMEM_LIMIT),
         cost_estimate=pl.CostEstimate(flops=1, bytes_accessed=1, transcendentals=0),
         name="products",
-    )(*[rel[r] for r in names], own, other)
+    )(which, *[rel[r] for r in names], *[x for pair in rights for x in pair])
 
 
 def pick(values, here):
@@ -107,24 +115,24 @@
 
 
 def line_blocks(own, nodes):
+    blocks = [[own]]
+    origins = [list(range(nodes))]
+    dists = [[0] * nodes]
     here = lax.axis_index("occ")
-    blocks = [own]
-    places = [here]
-    origins = [list(range(nodes))]
     size = 1
     while size < nodes:
         fresh, fresh_origins = [], []
-        place = here % (2 * size)
-        dist = jnp.where(place < size, size - 1 - place, place - size)
+        dist = [size - 1 - p if p < size else p - size for p in [i % (2 * size) for i in range(nodes)]]
         middles = [g * 2 * size + size for g in range(nodes // (2 * size))]
-        for block, origin in zip(blocks, origins):
+        for block, origin, far in zip(blocks, origins, dists):
+            whole = block[0]
+            for k in range(1, len(block)):
+                whole = jnp.where(pick(far, here) == k, block[k], whole)
             pairs = [(m - 1, m) for m in middles] + [(m, m - 1) for m in middles]
-            moving = lax.ppermute(block, "occ", pairs)
-            got = moving
+            got = [lax.ppermute(whole, "occ", pairs)]
             for hop in range(1, size):
                 pairs = [(m - hop, m - hop - 1) for m in middles] + [(m + hop - 1, m + hop) for m in middles]
-                moving = lax.ppermute(moving, "occ", pairs)
-                got = jnp.where(dist == hop, moving, got)
+                got.append(lax.ppermute(got[-1], "occ", pairs))
             fresh.append(got)
             table = [0] * nodes
             for m in middles:
@@ -132,10 +140,11 @@
                     table[m - 1 - k] = origin[m]
                     table[m + k] = origin[m - 1]
             fresh_origins.append(table)
+        dists += [dist] * len(fresh)
         blocks += fresh
         origins += fresh_origins
         size *= 2
-    return blocks, [pick(origin, here) for origin in origins]
+    return blocks, dists, origins
 
 
 def per_device(sizes, amplitudes, amp_mask, integrals, int_mask):
@@ -148,12 +157,19 @@
     def swap(x, bits):
         return lax.ppermute(x, "vir", [(i, i ^ bits) for i in range(n_vir)])
 
+    def swap_cores(x, planes):
+        pairs = [(o * n_vir + i, o * n_vir + (i ^ 1)) for o in planes for i in range(n_vir)]
+        return lax.ppermute(x, ("occ", "vir"), pairs)
+
     me = lax.axis_index("vir")
+    here = lax.axis_index("occ")
     weighted = masked(integrals, int_mask, TILE_V)
-    blocks, places = line_blocks(weighted, n_occ)
+    blocks, dists, origins = line_blocks(weighted, n_occ)
 
     position = jnp.stack([me // 2, me % 2]).astype(jnp.int32)
     parts = cut_amplitudes(after(position, weighted), amp_mask, amplitudes, groups, own_depth // TILE_V)
+    other = swap(weighted, 1)
+    parts = lax.optimization_barrier((*parts, other))[:groups]
     rel = [parts[0]] + [None] * (groups - 1)
     for r in range(groups - 1, 0, -1):
         rel[r] = swap(parts[r], 2 * r)
@@ -166,15 +182,33 @@
     near = [[r for r in range(groups) if not r & o[0]] for o in orders]
 
     out = jnp.zeros((rows, n_occ * width), jnp.float32)
-    token = parts
-    for block, place in zip(blocks, places):
-        block = after(block, *token)
-        other = swap(block, 1)
-        sent = products(away, rel, block, other)
+    last = len(blocks) - 1
+    token = None
+    for n, (block, far, origin) in enumerate(zip(blocks, dists, origins)):
+        which = pick(far, here)
+        if n > 1:
+            block = list(lax.optimization_barrier((*block, *sent)))[: len(block)]
+        if n == 0:
+            rights = [(after(weighted, *[b[0] for b in blocks[1:3]]), other)]
+        elif n == last:
+            rights = [(b, swap_cores(b, [o for o in range(n_occ) if far[o] == k])) for k, b in enumerate(block)]
+        else:
+            whole = block[0]
+            for k in range(1, len(block)):
+                whole = jnp.where(which == k, block[k], whole)
+            rights = [(whole, swap(whole, 1))]
+        if token is not None:
+            flat = lax.optimization_barrier((*[x for pair in rights for x in pair], *token))
+            rights = [(flat[2 * k], flat[2 * k + 1]) for k in range(len(rights))]
+        which = which.reshape(1)
+        sent = products(away, rel, which, rights)
         moving = [swap(sent[h], 2 * orders[h][0]) for h in range(2)]
-        stay = products(near, rel, block, after(other, *sent))
+        stay = products(near, rel, after(which, *sent), rights)
         held = [{r: stay[h][i * rows : (i + 1) * rows] for i, r in enumerate(near[h])} for h in range(2)]
+        moved = [None, None]
         for level in range(len(bits)):
+            if n == 1 and level == 0 and last > 2:
+                moving = list(lax.optimization_barrier((*moving, blocks[2][-1], blocks[3][0]))[:2])
             for h in range(2):
                 for i, r in enumerate(sorted(held[h])):
                     held[h][r] = held[h][r] + moving[h][i * rows : (i + 1) * rows]
@@ -183,12 +217,13 @@
             for h in range(2):
                 bit = orders[h][level + 1]
                 going = [r for r in sorted(held[h]) if r & bit]
-                moving[h] = swap(jnp.concatenate([held[h][r] for r in going], axis=0), 2 * bit)
+                moved[h] = jnp.concatenate([held[h][r] for r in going], axis=0)
+                moving[h] = swap(moved[h], 2 * bit)
                 for r in going:
                     del held[h][r]
         done = jnp.concatenate([held[h][0] for h in range(2)], axis=1)
-        out = lax.dynamic_update_slice(out, done, (0, place * width))
-        token = moving
+        out = lax.dynamic_update_slice(out, done, (0, pick(origin, here) * width))
+        token = moving if n == 0 else moved
     return out
 
 

time: 148 us -> 144 us (0.973)
  waiting for transfers between devices: 80.6 us -> 71.3 us
  other arithmetic: 12.8 us -> 5.96 us
  Pallas kernels: 18.5 us -> 24.1 us
  starting transfers between devices: 30.7 us -> 34.1 us
  local copies, waits for them, and re-layouts: 4.48 us -> 7.28 us
    ppermute x23 -> x22, waiting for transfers between devices: 51.8 us -> 35.2 us  [swap(): return lax.ppermute(x, 'vir', [(i, i ^ bits) for i in range(n_vir)])]
    ppermute x5 -> x7, waiting for transfers between devices: 28.8 us -> 36.1 us  [the longest x3 18.2 us: line_blocks(): got = [lax.ppermute(whole, 'occ', pairs)]]
    pallas_call x8, Pallas kernels: 17.8 us -> 23.3 us  [products(): pl.pallas_call(functools.partial(dot_kernel, lists, names, len(rights)),...]
    add x16, other arithmetic: 7.92 us -> 2.46 us  [per_device(): held[h][r] = held[h][r] + moving[h][i * rows:(i + 1) * rows]]
    ppermute x5 -> x7, starting transfers between devices: 8.2 us -> 11.4 us  [the longest x3 6.02 us: line_blocks(): got = [lax.ppermute(whole, 'occ', pairs)]]
    unnamed x40 -> x26, local copies, waits for them, and re-layouts: 4.17 us -> 6.96 us
    ppermute x23 -> x22, starting transfers between devices: 22.5 us -> 22.7 us  [swap(): return lax.ppermute(x, 'vir', [(i, i ^ bits) for i in range(n_vir)])]
  transfers between devices with their start and end apart: 28 -> 29, of which waited for: 15 -> 16; matrix products, arithmetic and copies ran while one was open for 7% -> 3% of each run, Pallas kernels for 11% -> 17%
where the time goes in v5:
time: 144 us; the launch traced here: 143 us
  waiting for transfers between devices  71.3 us (50%)
  starting transfers between devices  34.1 us (24%)
  Pallas kernels  24.1 us (17%)
  local copies, waits for them, and re-layouts  7.28 us (5%)
  other arithmetic  5.96 us (4%)
    ppermute x22, waiting for transfers between devices, swap(): return lax.ppermute(x, 'vir', [(i, i ^ bits) for i in range(n_vir)])  35.2 us
    pallas_call x8, Pallas kernels, products(): pl.pallas_call(functools.partial(dot_kernel, lists, names, len(rights)),...  23.3 us
    ppermute x22, starting transfers between devices, swap(): return lax.ppermute(x, 'vir', [(i, i ^ bits) for i in range(n_vir)])  22.7 us
    ppermute x3, waiting for transfers between devices, line_blocks(): got = [lax.ppermute(whole, 'occ', pairs)]  18.2 us
    ppermute x2, waiting for transfers between devices, line_blocks(): got.append(lax.ppermute(got[-1], 'occ', pairs))  17.9 us
    unnamed x26, local copies, waits for them, and re-layouts  6.96 us
    ppermute x3, starting transfers between devices, line_blocks(): got = [lax.ppermute(whole, 'occ', pairs)]  6.02 us
  transfers between devices with their start and end apart: 29, of which 16 were waited for; matrix products, arithmetic and copies ran while one was open for 3% of the time, Pallas kernels for 17%

profile of v5, /device:TPU:0, one launch (start us, length us, event | category | flops | bytes accessed | tf_op | source)
XLA Modules:
  0.0 143.1 jit_solution(4519453861104566597)
XLA Ops:
  0.0 0.8 convert_element_type.3
  0.8 0.2 mul.23
  1.0 0.3 copy-done.8
  1.3 0.3 bitcast_multiply_fusion.refs_4_
  1.6 0.5 collective-permute-start
  2.2 2.6 %collective-permute-start.4 = (f32[384,768]{1,0:T(8,128)S(1)}, f32[384,768]{1,0:T(8,128)}, u32[]{:S(2)}, u32[]{:S(2)}) collective-permute-start(f32[384,768]{1,0:T(8,128)S(1)} %bitcast_multiply_fusion.refs_4_), channel_id=1, source_target_pairs={{0,8},{16,24},{8,0},{24,16},{1,9},{17,25},{9,1},{25,17},{2,10},{18... | collective-permute-start | bytes 3538952 | tf_op jit(solution)/shard_map/ppermute | solution.py:132
  4.8 1.7 %collective-permute-start.5 = (f32[384,768]{1,0:T(8,128)S(1)}, f32[384,768]{1,0:T(8,128)}, u32[]{:S(2)}, u32[]{:S(2)}) collective-permute-start(f32[384,768]{1,0:T(8,128)S(1)} %bitcast_multiply_fusion.refs_4_), channel_id=1, source_target_pairs={{8,16},{16,8},{9,17},{17,9},{10,18},{18,10},{11,19},{19,11},{12,20... | collective-permute-start | bytes 3538952 | tf_op jit(solution)/shard_map/ppermute | solution.py:132
  6.6 1.4 copy-done.3
  8.0 0.8 cut.1
  8.8 1.0 copy-done
  9.8 1.5 %collective-permute-start.1 = (f32[128,768]{1,0:T(8,128)S(1)}, f32[128,768]{1,0:T(8,128)S(1)}, u32[]{:S(2)}, u32[]{:S(2)}) collective-permute-start(f32[128,768]{1,0:T(8,128)S(1)} %get-tuple-element.54), channel_id=1, source_target_pairs={{0,2},{1,3},{2,0},{3,1},{4,6},{5,7},{6,4},{7,5},{8,10},{9,11},{10,... | collective-permute-start | bytes 1179656 | tf_op jit(solution)/shard_map/ppermute | solution.py:158
  11.3 1.5 %collective-permute-start.2 = (f32[128,768]{1,0:T(8,128)S(1)}, f32[128,768]{1,0:T(8,128)S(1)}, u32[]{:S(2)}, u32[]{:S(2)}) collective-permute-start(f32[128,768]{1,0:T(8,128)S(1)} %get-tuple-element.55), channel_id=1, source_target_pairs={{0,4},{1,5},{2,6},{3,7},{4,0},{5,1},{6,2},{7,3},{8,12},{9,13},{10,... | collective-permute-start | bytes 1179656 | tf_op jit(solution)/shard_map/ppermute | solution.py:158
  12.8 0.5 collective-permute-start.3
  13.3 18.2 %collective-permute-done.4.refs_4_ = f32[384,768]{1,0:T(8,128)} collective-permute-done((f32[384,768]{1,0:T(8,128)S(1)}, f32[384,768]{1,0:T(8,128)}, u32[]{:S(2)}, u32[]{:S(2)}) %collective-permute-start.4) | collective-permute-done | bytes 1179680 | tf_op jit(solution)/shard_map/ppermute | solution.py:132
  31.5 1.3 collective-permute-start.13
  32.8 1.3 copy-done.1
  34.1 1.7 %products.8 = (f32[256,384]{1,0:T(8,128)S(1)}, f32[256,384]{1,0:T(8,128)S(1)}) custom-call(s32[1]{0:T(128)} %constant.34.clone.1.refs_0_, f32[128,768]{1,0:T(8,128)S(1)} %collective-permute-done.1.refs_1_.refs_2_, f32[128,768]{1,0:T(8,128)S(1)} %collective-permute-done.2.refs_2_.refs_3_, f32[128,768]{1,0:T(8,128)S(1)} %collective-permute-done.3.refs_3_, ...), custom_call_target="tpu_custom_call" | custom-call | flops 1 | bytes 1 | tf_op jit(solution)/shard_map/products/pallas_call | solution.py:99
  35.8 1.8 %collective-permute-start.8 = (f32[256,384]{1,0:T(8,128)S(1)}, f32[256,384]{1,0:T(8,128)S(1)}, u32[]{:S(2)}, u32[]{:S(2)}) collective-permute-start(f32[256,384]{1,0:T(8,128)S(1)} %get-tuple-element.59), channel_id=1, source_target_pairs={{0,4},{1,5},{2,6},{3,7},{4,0},{5,1},{6,2},{7,3},{8,12},{9,13},{10,... | collective-permute-start | bytes 1179656 | tf_op jit(solution)/shard_map/ppermute | solution.py:158
  37.6 1.7 %collective-permute-start.14 = (f32[384,768]{1,0:T(8,128)}, f32[384,768]{1,0:T(8,128)}, u32[]{:S(2)}, u32[]{:S(2)}) collective-permute-start(f32[384,768]{1,0:T(8,128)} %collective-permute-done.4.refs_4_), channel_id=1, source_target_pairs={{8,16},{16,8},{9,17},{17,9},{10,18},{18,10},{11,19},{19,11},{12,20... | collective-permute-start | bytes 3538952 | tf_op jit(solution)/shard_map/ppermute | solution.py:132
  39.3 1.5 %collective-permute-start.6 = (f32[256,384]{1,0:T(8,128)S(1)}, f32[256,384]{1,0:T(8,128)S(1)}, u32[]{:S(2)}, u32[]{:S(2)}) collective-permute-start(f32[256,384]{1,0:T(8,128)S(1)} %get-tuple-element.58), channel_id=1, source_target_pairs={{0,2},{1,3},{2,0},{3,1},{4,6},{5,7},{6,4},{7,5},{8,10},{9,11},{10,... | collective-permute-start | bytes 1179656 | tf_op jit(solution)/shard_map/ppermute | solution.py:158
  40.7 1.7 %products.9 = (f32[256,384]{1,0:T(8,128)S(1)}, f32[256,384]{1,0:T(8,128)S(1)}) custom-call(s32[1]{0:T(128)} %constant.34.clone.1.refs_0_, f32[128,768]{1,0:T(8,128)S(1)} %get-tuple-element.61.refs_1_, f32[128,768]{1,0:T(8,128)S(1)} %collective-permute-done.1.refs_1_.refs_2_, f32[128,768]{1,0:T(8,128)S(1)} %collective-permute-done.2.refs_2_.refs_3_, ...), custom_call_target="tpu_custom_call" | custom-call | flops 1 | bytes 1 | tf_op jit(solution)/shard_map/products/pallas_call | solution.py:99
  42.5 4.9 %collective-permute-done.8 = f32[256,384]{1,0:T(8,128)S(1)} collective-permute-done((f32[256,384]{1,0:T(8,128)S(1)}, f32[256,384]{1,0:T(8,128)S(1)}, u32[]{:S(2)}, u32[]{:S(2)}) %collective-permute-start.8) | collective-permute-done | bytes 393248 | tf_op jit(solution)/shard_map/ppermute | solution.py:158
  47.4 1.7 %collective-permute-start.9 = (f32[128,384]{1,0:T(8,128)S(1)}, f32[128,384]{1,0:T(8,128)S(1)}, u32[]{:S(2)}, u32[]{:S(2)}) collective-permute-start(f32[128,384]{1,0:T(8,128)S(1)} %slice_add_fusion.8), channel_id=1, source_target_pairs={{0,2},{1,3},{2,0},{3,1},{4,6},{5,7},{6,4},{7,5},{8,10},{9,11},{10,... | collective-permute-start | bytes 589832 | tf_op jit(solution)/shard_map/ppermute | solution.py:158
  49.1 1.9 %collective-permute-done.6 = f32[256,384]{1,0:T(8,128)S(1)} collective-permute-done((f32[256,384]{1,0:T(8,128)S(1)}, f32[256,384]{1,0:T(8,128)S(1)}, u32[]{:S(2)}, u32[]{:S(2)}) %collective-permute-start.6) | collective-permute-done | bytes 393248 | tf_op jit(solution)/shard_map/ppermute | solution.py:158
  51.0 0.8 copy-done.10
  51.9 2.8 %collective-permute-done.9 = f32[128,384]{1,0:T(8,128)S(1)} collective-permute-done((f32[128,384]{1,0:T(8,128)S(1)}, f32[128,384]{1,0:T(8,128)S(1)}, u32[]{:S(2)}, u32[]{:S(2)}) %collective-permute-start.9) | collective-permute-done | bytes 196640 | tf_op jit(solution)/shard_map/ppermute | solution.py:158
  54.7 3.0 %collective-permute-done.7 = f32[128,384]{1,0:T(8,128)S(1)} collective-permute-done((f32[128,384]{1,0:T(8,128)S(1)}, f32[128,384]{1,0:T(8,128)S(1)}, u32[]{:S(2)}, u32[]{:S(2)}) %collective-permute-start.7) | collective-permute-done | bytes 196640 | tf_op jit(solution)/shard_map/ppermute | solution.py:158
  57.7 0.7 copy-done.12
  58.4 3.3 %products.10 = (f32[256,384]{1,0:T(8,128)S(1)}, f32[256,384]{1,0:T(8,128)S(1)}) custom-call(s32[1]{0:T(128)} %constant.34.clone.1.refs_0_, f32[128,768]{1,0:T(8,128)S(1)} %collective-permute-done.1.refs_1_.refs_2_, f32[128,768]{1,0:T(8,128)S(1)} %collective-permute-done.2.refs_2_.refs_3_, f32[128,768]{1,0:T(8,128)S(1)} %collective-permute-done.3.refs_3_, ...), custom_call_target="tpu_custom_call" | custom-call | flops 1 | bytes 1 | tf_op jit(solution)/shard_map/products/pallas_call | solution.py:99
  61.7 0.7 copy-done.5
  62.5 0.7 copy-done.6
  63.2 0.4 collective-permute-done.13
  63.6 1.4 broadcast_select_fusion.refs_4_
  65.1 1.3 collective-permute-start.22
  66.5 1.6 %collective-permute-start.11 = (f32[256,384]{1,0:T(8,128)}, f32[256,384]{1,0:T(8,128)S(1)}, u32[]{:S(2)}, u32[]{:S(2)}) collective-permute-start(f32[256,384]{1,0:T(8,128)} %copy-done.6), channel_id=1, source_target_pairs={{0,2},{1,3},{2,0},{3,1},{4,6},{5,7},{6,4},{7,5},{8,10},{9,11},{10,... | collective-permute-start | bytes 1179656 | tf_op jit(solution)/shard_map/ppermute | solution.py:158
  68.0 1.5 %collective-permute-start.12 = (f32[256,384]{1,0:T(8,128)}, f32[256,384]{1,0:T(8,128)S(1)}, u32[]{:S(2)}, u32[]{:S(2)}) collective-permute-start(f32[256,384]{1,0:T(8,128)} %copy-done.5), channel_id=1, source_target_pairs={{0,4},{1,5},{2,6},{3,7},{4,0},{5,1},{6,2},{7,3},{8,12},{9,13},{10,... | collective-permute-start | bytes 1179656 | tf_op jit(solution)/shard_map/ppermute | solution.py:158
  69.5 1.1 fusion.4
  70.6 1.1 fusion.5
  71.6 3.3 %products.11 = (f32[256,384]{1,0:T(8,128)S(1)}, f32[256,384]{1,0:T(8,128)S(1)}) custom-call(s32[1]{0:T(128)} %constant.34.clone.1.refs_0_, f32[128,768]{1,0:T(8,128)S(1)} %get-tuple-element.61.refs_1_, f32[128,768]{1,0:T(8,128)S(1)} %collective-permute-done.1.refs_1_.refs_2_, f32[128,768]{1,0:T(8,128)S(1)} %collective-permute-done.2.refs_2_.refs_3_, ...), custom_call_target="tpu_custom_call" | custom-call | flops 1 | bytes 1 | tf_op jit(solution)/shard_map/products/pallas_call | solution.py:99
  75.0 3.2 %collective-permute-done.11 = f32[256,384]{1,0:T(8,128)S(1)} collective-permute-done((f32[256,384]{1,0:T(8,128)}, f32[256,384]{1,0:T(8,128)S(1)}, u32[]{:S(2)}, u32[]{:S(2)}) %collective-permute-start.11) | collective-permute-done | bytes 393248 | tf_op jit(solution)/shard_map/ppermute | solution.py:158
  78.2 1.2 collective-permute-done.12
  79.5 0.6 collective-permute-start.16
  80.1 3.0 %products.12 = (f32[256,384]{1,0:T(8,128)S(1)}, f32[256,384]{1,0:T(8,128)S(1)}) custom-call(s32[1]{0:T(128)} %bitcast.2.refs_0_, f32[128,768]{1,0:T(8,128)S(1)} %collective-permute-done.1.refs_1_.refs_2_, f32[128,768]{1,0:T(8,128)S(1)} %collective-permute-done.2.refs_2_.refs_3_, f32[128,768]{1,0:T(8,128)S(1)} %collective-permute-done.3.refs_3_, ...), custom_call_target="tpu_custom_call" | custom-call | flops 1 | bytes 1 | tf_op jit(solution)/shard_map/products/pallas_call | solution.py:99
  83.1 17.4 %collective-permute-done.22.refs_6_ = f32[384,768]{1,0:T(8,128)} collective-permute-done((f32[384,768]{1,0:T(8,128)}, f32[384,768]{1,0:T(8,128)}, u32[]{:S(2)}, u32[]{:S(2)}) %collective-permute-start.22) | collective-permute-done | bytes 1179680 | tf_op jit(solution)/shard_map/ppermute | solution.py:135
  100.5 0.7 collective-permute-start.23
  101.3 2.1 %collective-permute-start.24 = (f32[384,768]{1,0:T(8,128)}, f32[384,768]{1,0:T(8,128)S(1)}, u32[]{:S(2)}, u32[]{:S(2)}) collective-permute-start(f32[384,768]{1,0:T(8,128)} %collective-permute-done.22.refs_6_), channel_id=1, source_target_pairs={{0,1},{1,0},{2,3},{3,2},{4,5},{5,4},{6,7},{7,6},{24,25},{25,24},{2... | collective-permute-start | bytes 3538952 | tf_op jit(solution)/shard_map/ppermute | solution.py:162
  103.7 1.9 %collective-permute-start.20 = (f32[256,384]{1,0:T(8,128)S(1)}, f32[256,384]{1,0:T(8,128)S(1)}, u32[]{:S(2)}, u32[]{:S(2)}) collective-permute-start(f32[256,384]{1,0:T(8,128)S(1)} %get-tuple-element.78), channel_id=1, source_target_pairs={{0,4},{1,5},{2,6},{3,7},{4,0},{5,1},{6,2},{7,3},{8,12},{9,13},{10,... | collective-permute-start | bytes 1179656 | tf_op jit(solution)/shard_map/ppermute | solution.py:158
  105.7 1.6 %collective-permute-start.18 = (f32[256,384]{1,0:T(8,128)S(1)}, f32[256,384]{1,0:T(8,128)S(1)}, u32[]{:S(2)}, u32[]{:S(2)}) collective-permute-start(f32[256,384]{1,0:T(8,128)S(1)} %get-tuple-element.77), channel_id=1, source_target_pairs={{0,2},{1,3},{2,0},{3,1},{4,6},{5,7},{6,4},{7,5},{8,10},{9,11},{10,... | collective-permute-start | bytes 1179656 | tf_op jit(solution)/shard_map/ppermute | solution.py:158
  107.3 4.1 %collective-permute-done.15 = f32[128,384]{1,0:T(8,128)S(1)} collective-permute-done((f32[128,384]{1,0:T(8,128)S(1)}, f32[128,384]{1,0:T(8,128)S(1)}, u32[]{:S(2)}, u32[]{:S(2)}) %collective-permute-start.15) | collective-permute-done | bytes 196640 | tf_op jit(solution)/shard_map/ppermute | solution.py:158
  111.4 3.0 %products.13 = (f32[256,384]{1,0:T(8,128)S(1)}, f32[256,384]{1,0:T(8,128)S(1)}) custom-call(s32[1]{0:T(128)} %bitcast.2.refs_0_, f32[128,768]{1,0:T(8,128)S(1)} %get-tuple-element.61.refs_1_, f32[128,768]{1,0:T(8,128)S(1)} %collective-permute-done.1.refs_1_.refs_2_, f32[128,768]{1,0:T(8,128)S(1)} %collective-permute-done.2.refs_2_.refs_3_, ...), custom_call_target="tpu_custom_call" | custom-call | flops 1 | bytes 1 | tf_op jit(solution)/shard_map/products/pallas_call | solution.py:99
  114.4 5.0 %collective-permute-done.20 = f32[256,384]{1,0:T(8,128)S(1)} collective-permute-done((f32[256,384]{1,0:T(8,128)S(1)}, f32[256,384]{1,0:T(8,128)S(1)}, u32[]{:S(2)}, u32[]{:S(2)}) %collective-permute-start.20) | collective-permute-done | bytes 393248 | tf_op jit(solution)/shard_map/ppermute | solution.py:158
  119.4 1.6 %collective-permute-start.21 = (f32[128,384]{1,0:T(8,128)S(1)}, f32[128,384]{1,0:T(8,128)S(1)}, u32[]{:S(2)}, u32[]{:S(2)}) collective-permute-start(f32[128,384]{1,0:T(8,128)S(1)} %slice_add_fusion.4), channel_id=1, source_target_pairs={{0,2},{1,3},{2,0},{3,1},{4,6},{5,7},{6,4},{7,5},{8,10},{9,11},{10,... | collective-permute-start | bytes 589832 | tf_op jit(solution)/shard_map/ppermute | solution.py:158
  121.0 0.4 collective-permute-start.19
  121.3 3.4 %products.14 = (f32[256,384]{1,0:T(8,128)S(1)}, f32[256,384]{1,0:T(8,128)S(1)}) custom-call(s32[1]{0:T(128)} %bitcast.2.refs_0_, f32[128,768]{1,0:T(8,128)S(1)} %collective-permute-done.1.refs_1_.refs_2_, f32[128,768]{1,0:T(8,128)S(1)} %collective-permute-done.2.refs_2_.refs_3_, f32[128,768]{1,0:T(8,128)S(1)} %collective-permute-done.3.refs_3_, ...), custom_call_target="tpu_custom_call" | custom-call | flops 1 | bytes 1 | tf_op jit(solution)/shard_map/products/pallas_call | solution.py:99
  124.7 1.8 %collective-permute-start.27 = (f32[256,384]{1,0:T(8,128)S(1)}, f32[256,384]{1,0:T(8,128)S(1)}, u32[]{:S(2)}, u32[]{:S(2)}) collective-permute-start(f32[256,384]{1,0:T(8,128)S(1)} %get-tuple-element.89), channel_id=1, source_target_pairs={{0,4},{1,5},{2,6},{3,7},{4,0},{5,1},{6,2},{7,3},{8,12},{9,13},{10,... | collective-permute-start | bytes 1179656 | tf_op jit(solution)/shard_map/ppermute | solution.py:158
  126.5 1.0 collective-permute-start.25
  127.6 0.3 collective-permute-done.19
  128.0 3.9 %products.15 = (f32[256,384]{1,0:T(8,128)S(1)}, f32[256,384]{1,0:T(8,128)S(1)}) custom-call(s32[1]{0:T(128)} %bitcast.2.refs_0_, f32[128,768]{1,0:T(8,128)S(1)} %get-tuple-element.61.refs_1_, f32[128,768]{1,0:T(8,128)S(1)} %collective-permute-done.1.refs_1_.refs_2_, f32[128,768]{1,0:T(8,128)S(1)} %collective-permute-done.2.refs_2_.refs_3_, ...), custom_call_target="tpu_custom_call" | custom-call | flops 1 | bytes 1 | tf_op jit(solution)/shard_map/products/pallas_call | solution.py:99
  131.9 3.8 %collective-permute-done.27 = f32[256,384]{1,0:T(8,128)S(1)} collective-permute-done((f32[256,384]{1,0:T(8,128)S(1)}, f32[256,384]{1,0:T(8,128)S(1)}, u32[]{:S(2)}, u32[]{:S(2)}) %collective-permute-start.27) | collective-permute-done | bytes 393248 | tf_op jit(solution)/shard_map/ppermute | solution.py:158
  135.7 0.6 collective-permute-start.28
  136.5 0.9 collective-permute-start.26
  137.4 4.2 %collective-permute-done.28 = f32[128,384]{1,0:T(8,128)S(1)} collective-permute-done((f32[128,384]{1,0:T(8,128)S(1)}, f32[128,384]{1,0:T(8,128)S(1)}, u32[]{:S(2)}, u32[]{:S(2)}) %collective-permute-start.28) | collective-permute-done | bytes 196640 | tf_op jit(solution)/shard_map/ppermute | solution.py:158
  141.7 0.6 collective-permute-done.26
  142.3 0.8 maximum_dynamic-update-slice_fusion.3
  (55 shorter events, 1.2 us)
Async XLA Ops:
  0.0 1.3 copy-start.8
  1.3 5.3 %copy-start.4 = (s32[4,24]{1,0:T(4,128)S(1)}, s32[4,24]{1,0:T(4,128)}, u32[]{:S(2)}) copy-start(s32[4,24]{1,0:T(4,128)} %mask_ref.1) | copy-start | bytes 1156
  1.6 7.1 %collective-permute-start = (f32[384,768]{1,0:T(8,128)S(1)}, f32[384,768]{1,0:T(8,128)S(1)}, u32[]{:S(2)}, u32[]{:S(2)}) collective-permute-start(f32[384,768]{1,0:T(8,128)S(1)} %bitcast_multiply_fusion.refs_4_), channel_id=1, source_target_pairs={{0,1},{1,0},{2,3},{3,2},{4,5},{5,4},{6,7},{7,6},{8,9},{9,8},{10,11... | collective-permute-start | bytes 3538952 | tf_op jit(solution)/shard_map/ppermute | solution.py:158
  2.2 29.3 %collective-permute-start.4 = (f32[384,768]{1,0:T(8,128)S(1)}, f32[384,768]{1,0:T(8,128)}, u32[]{:S(2)}, u32[]{:S(2)}) collective-permute-start(f32[384,768]{1,0:T(8,128)S(1)} %bitcast_multiply_fusion.refs_4_), channel_id=1, source_target_pairs={{0,8},{16,24},{8,0},{24,16},{1,9},{17,25},{9,1},{25,17},{2,10},{18... | collective-permute-start | bytes 3538952 | tf_op jit(solution)/shard_map/ppermute | solution.py:132
  4.8 26.7 %collective-permute-start.5 = (f32[384,768]{1,0:T(8,128)S(1)}, f32[384,768]{1,0:T(8,128)}, u32[]{:S(2)}, u32[]{:S(2)}) collective-permute-start(f32[384,768]{1,0:T(8,128)S(1)} %bitcast_multiply_fusion.refs_4_), channel_id=1, source_target_pairs={{8,16},{16,8},{9,17},{17,9},{10,18},{18,10},{11,19},{19,11},{12,20... | collective-permute-start | bytes 3538952 | tf_op jit(solution)/shard_map/ppermute | solution.py:132
  6.6 1.4 copy-start.3
  8.8 1.0 copy-start
  9.8 23.0 %collective-permute-start.1 = (f32[128,768]{1,0:T(8,128)S(1)}, f32[128,768]{1,0:T(8,128)S(1)}, u32[]{:S(2)}, u32[]{:S(2)}) collective-permute-start(f32[128,768]{1,0:T(8,128)S(1)} %get-tuple-element.54), channel_id=1, source_target_pairs={{0,2},{1,3},{2,0},{3,1},{4,6},{5,7},{6,4},{7,5},{8,10},{9,11},{10,... | collective-permute-start | bytes 1179656 | tf_op jit(solution)/shard_map/ppermute | solution.py:158
  11.3 21.5 %collective-permute-start.2 = (f32[128,768]{1,0:T(8,128)S(1)}, f32[128,768]{1,0:T(8,128)S(1)}, u32[]{:S(2)}, u32[]{:S(2)}) collective-permute-start(f32[128,768]{1,0:T(8,128)S(1)} %get-tuple-element.55), channel_id=1, source_target_pairs={{0,4},{1,5},{2,6},{3,7},{4,0},{5,1},{6,2},{7,3},{8,12},{9,13},{10,... | collective-permute-start | bytes 1179656 | tf_op jit(solution)/shard_map/ppermute | solution.py:158
  12.8 20.0 %collective-permute-start.3 = (f32[128,768]{1,0:T(8,128)S(1)}, f32[128,768]{1,0:T(8,128)S(1)}, u32[]{:S(2)}, u32[]{:S(2)}) collective-permute-start(f32[128,768]{1,0:T(8,128)S(1)} %get-tuple-element.56), channel_id=1, source_target_pairs={{0,6},{1,7},{2,4},{3,5},{4,2},{5,3},{6,0},{7,1},{8,14},{9,15},{10,... | collective-permute-start | bytes 1179656 | tf_op jit(solution)/shard_map/ppermute | solution.py:158
  31.5 26.9 %collective-permute-start.10 = (f32[384,768]{1,0:T(8,128)}, f32[384,768]{1,0:T(8,128)}, u32[]{:S(2)}, u32[]{:S(2)}) collective-permute-start(f32[384,768]{1,0:T(8,128)} %collective-permute-done.4.refs_4_), channel_id=1, source_target_pairs={{0,1},{1,0},{2,3},{3,2},{4,5},{5,4},{6,7},{7,6},{8,9},{9,8},{10,11... | collective-permute-start | bytes 3538952 | tf_op jit(solution)/shard_map/ppermute | solution.py:158
  31.5 32.1 %collective-permute-start.13 = (f32[384,768]{1,0:T(8,128)}, f32[384,768]{1,0:T(8,128)}, u32[]{:S(2)}, u32[]{:S(2)}) collective-permute-start(f32[384,768]{1,0:T(8,128)} %collective-permute-done.5), channel_id=1, source_target_pairs={{8,0},{16,24},{9,1},{17,25},{10,2},{18,26},{11,3},{19,27},{12,4},{... | collective-permute-start | bytes 3538952 | tf_op jit(solution)/shard_map/ppermute | solution.py:135
  32.8 1.3 copy-start.1
  34.1 6.7 %copy-start.2 = (f32[384,768]{1,0:T(8,128)S(1)}, f32[384,768]{1,0:T(8,128)}, u32[]{:S(2)}) copy-start(f32[384,768]{1,0:T(8,128)} %copy-done) | copy-start | bytes 3538948
  35.8 11.6 %collective-permute-start.8 = (f32[256,384]{1,0:T(8,128)S(1)}, f32[256,384]{1,0:T(8,128)S(1)}, u32[]{:S(2)}, u32[]{:S(2)}) collective-permute-start(f32[256,384]{1,0:T(8,128)S(1)} %get-tuple-element.59), channel_id=1, source_target_pairs={{0,4},{1,5},{2,6},{3,7},{4,0},{5,1},{6,2},{7,3},{8,12},{9,13},{10,... | collective-permute-start | bytes 1179656 | tf_op jit(solution)/shard_map/ppermute | solution.py:158
  37.6 27.6 %collective-permute-start.14 = (f32[384,768]{1,0:T(8,128)}, f32[384,768]{1,0:T(8,128)}, u32[]{:S(2)}, u32[]{:S(2)}) collective-permute-start(f32[384,768]{1,0:T(8,128)} %collective-permute-done.4.refs_4_), channel_id=1, source_target_pairs={{8,16},{16,8},{9,17},{17,9},{10,18},{18,10},{11,19},{19,11},{12,20... | collective-permute-start | bytes 3538952 | tf_op jit(solution)/shard_map/ppermute | solution.py:132
  39.3 11.8 %collective-permute-start.6 = (f32[256,384]{1,0:T(8,128)S(1)}, f32[256,384]{1,0:T(8,128)S(1)}, u32[]{:S(2)}, u32[]{:S(2)}) collective-permute-start(f32[256,384]{1,0:T(8,128)S(1)} %get-tuple-element.58), channel_id=1, source_target_pairs={{0,2},{1,3},{2,0},{3,1},{4,6},{5,7},{6,4},{7,5},{8,10},{9,11},{10,... | collective-permute-start | bytes 1179656 | tf_op jit(solution)/shard_map/ppermute | solution.py:158
  47.4 3.7 %copy-start.9 = (f32[256,384]{1,0:T(8,128)}, f32[256,384]{1,0:T(8,128)S(1)}, u32[]{:S(2)}) copy-start(f32[256,384]{1,0:T(8,128)S(1)} %collective-permute-done.8) | copy-start | bytes 1179652
  47.4 7.3 %collective-permute-start.9 = (f32[128,384]{1,0:T(8,128)S(1)}, f32[128,384]{1,0:T(8,128)S(1)}, u32[]{:S(2)}, u32[]{:S(2)}) collective-permute-start(f32[128,384]{1,0:T(8,128)S(1)} %slice_add_fusion.8), channel_id=1, source_target_pairs={{0,2},{1,3},{2,0},{3,1},{4,6},{5,7},{6,4},{7,5},{8,10},{9,11},{10,... | collective-permute-start | bytes 589832 | tf_op jit(solution)/shard_map/ppermute | solution.py:158
  51.0 0.8 copy-start.10
  51.8 5.8 %collective-permute-start.7 = (f32[128,384]{1,0:T(8,128)S(1)}, f32[128,384]{1,0:T(8,128)S(1)}, u32[]{:S(2)}, u32[]{:S(2)}) collective-permute-start(f32[128,384]{1,0:T(8,128)S(1)} %slice_add_fusion.10), channel_id=1, source_target_pairs={{0,4},{1,5},{2,6},{3,7},{4,0},{5,1},{6,2},{7,3},{8,12},{9,13},{10,... | collective-permute-start | bytes 589832 | tf_op jit(solution)/shard_map/ppermute | solution.py:158
  54.7 3.0 %copy-start.11 = (f32[128,384]{1,0:T(8,128)}, f32[128,384]{1,0:T(8,128)S(1)}, u32[]{:S(2)}) copy-start(f32[128,384]{1,0:T(8,128)S(1)} %collective-permute-done.9) | copy-start | bytes 589828
  57.7 0.7 copy-start.12
  61.7 0.8 copy-start.5
  62.5 0.7 copy-start.6
  65.0 15.1 %collective-permute-start.17 = (f32[384,768]{1,0:T(8,128)S(1)}, f32[384,768]{1,0:T(8,128)}, u32[]{:S(2)}, u32[]{:S(2)}) collective-permute-start(f32[384,768]{1,0:T(8,128)S(1)} %broadcast_select_fusion.refs_4_), channel_id=1, source_target_pairs={{0,1},{1,0},{2,3},{3,2},{4,5},{5,4},{6,7},{7,6},{8,9},{9,8},{10,11... | collective-permute-start | bytes 3538952 | tf_op jit(solution)/shard_map/ppermute | solution.py:158
  65.1 35.4 %collective-permute-start.22 = (f32[384,768]{1,0:T(8,128)}, f32[384,768]{1,0:T(8,128)}, u32[]{:S(2)}, u32[]{:S(2)}) collective-permute-start(f32[384,768]{1,0:T(8,128)} %collective-permute-done.14.refs_4_), channel_id=1, source_target_pairs={{8,0},{16,24},{9,1},{17,25},{10,2},{18,26},{11,3},{19,27},{12,4},{... | collective-permute-start | bytes 3538952 | tf_op jit(solution)/shard_map/ppermute | solution.py:135
  66.5 11.8 %collective-permute-start.11 = (f32[256,384]{1,0:T(8,128)}, f32[256,384]{1,0:T(8,128)S(1)}, u32[]{:S(2)}, u32[]{:S(2)}) collective-permute-start(f32[256,384]{1,0:T(8,128)} %copy-done.6), channel_id=1, source_target_pairs={{0,2},{1,3},{2,0},{3,1},{4,6},{5,7},{6,4},{7,5},{8,10},{9,11},{10,... | collective-permute-start | bytes 1179656 | tf_op jit(solution)/shard_map/ppermute | solution.py:158
  68.0 11.4 %collective-permute-start.12 = (f32[256,384]{1,0:T(8,128)}, f32[256,384]{1,0:T(8,128)S(1)}, u32[]{:S(2)}, u32[]{:S(2)}) collective-permute-start(f32[256,384]{1,0:T(8,128)} %copy-done.5), channel_id=1, source_target_pairs={{0,4},{1,5},{2,6},{3,7},{4,0},{5,1},{6,2},{7,3},{8,12},{9,13},{10,... | collective-permute-start | bytes 1179656 | tf_op jit(solution)/shard_map/ppermute | solution.py:158
  79.5 26.2 %collective-permute-start.16 = (f32[128,384]{1,0:T(8,128)S(1)}, f32[128,384]{1,0:T(8,128)S(1)}, u32[]{:S(2)}, u32[]{:S(2)}) collective-permute-start(f32[128,384]{1,0:T(8,128)S(1)} %slice_add_fusion.12), channel_id=1, source_target_pairs={{0,2},{1,3},{2,0},{3,1},{4,6},{5,7},{6,4},{7,5},{8,10},{9,11},{10,... | collective-permute-start | bytes 589832 | tf_op jit(solution)/shard_map/ppermute | solution.py:158
  100.5 20.8 %collective-permute-start.23 = (f32[384,768]{1,0:T(8,128)}, f32[384,768]{1,0:T(8,128)S(1)}, u32[]{:S(2)}, u32[]{:S(2)}) collective-permute-start(f32[384,768]{1,0:T(8,128)} %collective-permute-done.14.refs_4_), channel_id=1, source_target_pairs={{8,9},{9,8},{10,11},{11,10},{12,13},{13,12},{14,15},{15,14},{16,17... | collective-permute-start | bytes 3538952 | tf_op jit(solution)/shard_map/ppermute | solution.py:162
  101.3 20.1 %collective-permute-start.24 = (f32[384,768]{1,0:T(8,128)}, f32[384,768]{1,0:T(8,128)S(1)}, u32[]{:S(2)}, u32[]{:S(2)}) collective-permute-start(f32[384,768]{1,0:T(8,128)} %collective-permute-done.22.refs_6_), channel_id=1, source_target_pairs={{0,1},{1,0},{2,3},{3,2},{4,5},{5,4},{6,7},{7,6},{24,25},{25,24},{2... | collective-permute-start | bytes 3538952 | tf_op jit(solution)/shard_map/ppermute | solution.py:162
  103.6 7.8 %collective-permute-start.15 = (f32[128,384]{1,0:T(8,128)S(1)}, f32[128,384]{1,0:T(8,128)S(1)}, u32[]{:S(2)}, u32[]{:S(2)}) collective-permute-start(f32[128,384]{1,0:T(8,128)S(1)} %slice_add_fusion.13), channel_id=1, source_target_pairs={{0,4},{1,5},{2,6},{3,7},{4,0},{5,1},{6,2},{7,3},{8,12},{9,13},{10,... | collective-permute-start | bytes 589832 | tf_op jit(solution)/shard_map/ppermute | solution.py:158
  103.7 15.6 %collective-permute-start.20 = (f32[256,384]{1,0:T(8,128)S(1)}, f32[256,384]{1,0:T(8,128)S(1)}, u32[]{:S(2)}, u32[]{:S(2)}) collective-permute-start(f32[256,384]{1,0:T(8,128)S(1)} %get-tuple-element.78), channel_id=1, source_target_pairs={{0,4},{1,5},{2,6},{3,7},{4,0},{5,1},{6,2},{7,3},{8,12},{9,13},{10,... | collective-permute-start | bytes 1179656 | tf_op jit(solution)/shard_map/ppermute | solution.py:158
  105.7 15.3 %collective-permute-start.18 = (f32[256,384]{1,0:T(8,128)S(1)}, f32[256,384]{1,0:T(8,128)S(1)}, u32[]{:S(2)}, u32[]{:S(2)}) collective-permute-start(f32[256,384]{1,0:T(8,128)S(1)} %get-tuple-element.77), channel_id=1, source_target_pairs={{0,2},{1,3},{2,0},{3,1},{4,6},{5,7},{6,4},{7,5},{8,10},{9,11},{10,... | collective-permute-start | bytes 1179656 | tf_op jit(solution)/shard_map/ppermute | solution.py:158
  119.4 7.1 %collective-permute-start.21 = (f32[128,384]{1,0:T(8,128)S(1)}, f32[128,384]{1,0:T(8,128)S(1)}, u32[]{:S(2)}, u32[]{:S(2)}) collective-permute-start(f32[128,384]{1,0:T(8,128)S(1)} %slice_add_fusion.4), channel_id=1, source_target_pairs={{0,2},{1,3},{2,0},{3,1},{4,6},{5,7},{6,4},{7,5},{8,10},{9,11},{10,... | collective-permute-start | bytes 589832 | tf_op jit(solution)/shard_map/ppermute | solution.py:158
  121.0 6.9 %collective-permute-start.19 = (f32[128,384]{1,0:T(8,128)S(1)}, f32[128,384]{1,0:T(8,128)S(1)}, u32[]{:S(2)}, u32[]{:S(2)}) collective-permute-start(f32[128,384]{1,0:T(8,128)S(1)} %slice_add_fusion.6), channel_id=1, source_target_pairs={{0,4},{1,5},{2,6},{3,7},{4,0},{5,1},{6,2},{7,3},{8,12},{9,13},{10,... | collective-permute-start | bytes 589832 | tf_op jit(solution)/shard_map/ppermute | solution.py:158
  124.7 11.0 %collective-permute-start.27 = (f32[256,384]{1,0:T(8,128)S(1)}, f32[256,384]{1,0:T(8,128)S(1)}, u32[]{:S(2)}, u32[]{:S(2)}) collective-permute-start(f32[256,384]{1,0:T(8,128)S(1)} %get-tuple-element.89), channel_id=1, source_target_pairs={{0,4},{1,5},{2,6},{3,7},{4,0},{5,1},{6,2},{7,3},{8,12},{9,13},{10,... | collective-permute-start | bytes 1179656 | tf_op jit(solution)/shard_map/ppermute | solution.py:158
  126.5 10.0 %collective-permute-start.25 = (f32[256,384]{1,0:T(8,128)S(1)}, f32[256,384]{1,0:T(8,128)S(1)}, u32[]{:S(2)}, u32[]{:S(2)}) collective-permute-start(f32[256,384]{1,0:T(8,128)S(1)} %get-tuple-element.88), channel_id=1, source_target_pairs={{0,2},{1,3},{2,0},{3,1},{4,6},{5,7},{6,4},{7,5},{8,10},{9,11},{10,... | collective-permute-start | bytes 1179656 | tf_op jit(solution)/shard_map/ppermute | solution.py:158
  128.0 3.9 %copy-start.7 = (f32[128,3072]{1,0:T(8,128)}, f32[128,3072]{1,0:T(8,128)S(1)}, u32[]{:S(2)}) copy-start(f32[128,3072]{1,0:T(8,128)S(1)} %maximum_dynamic-update-slice_fusion.2) | copy-start | bytes 4718596
  135.7 5.9 %collective-permute-start.28 = (f32[128,384]{1,0:T(8,128)S(1)}, f32[128,384]{1,0:T(8,128)S(1)}, u32[]{:S(2)}, u32[]{:S(2)}) collective-permute-start(f32[128,384]{1,0:T(8,128)S(1)} %slice_add_fusion), channel_id=1, source_target_pairs={{0,2},{1,3},{2,0},{3,1},{4,6},{5,7},{6,4},{7,5},{8,10},{9,11},{10,... | collective-permute-start | bytes 589832 | tf_op jit(solution)/shard_map/ppermute | solution.py:158
  136.5 5.7 %collective-permute-start.26 = (f32[128,384]{1,0:T(8,128)S(1)}, f32[128,384]{1,0:T(8,128)S(1)}, u32[]{:S(2)}, u32[]{:S(2)}) collective-permute-start(f32[128,384]{1,0:T(8,128)S(1)} %slice_add_fusion.2), channel_id=1, source_target_pairs={{0,4},{1,5},{2,6},{3,7},{4,0},{5,1},{6,2},{7,3},{8,12},{9,13},{10,... | collective-permute-start | bytes 589832 | tf_op jit(solution)/shard_map/ppermute | solution.py:158

commit v6 on v4

--- a/solution.py
+++ b/solution.py
@@ -9,7 +9,7 @@
 
 TILE_O = 32
 TILE_V = 128
-VMEM_LIMIT = 40 * 1024 * 1024
+VMEM_LIMIT = 12 * 1024 * 1024
 
 
 def masked(values, mask, tile_rows):
@@ -85,7 +85,7 @@
 
 def products(lists, rel, own, other):
     names = sorted(set(lists[0]) | set(lists[1]))
-    rows, depth = rel[0].shape
+    rows = rel[0].shape[0]
     width = own.shape[1] // 2
     count = len(lists[0])
     return pl.pallas_call(
@@ -99,43 +99,20 @@
     )(*[rel[r] for r in names], own, other)
 
 
-def pick(values, here):
-    result = jnp.int32(values[0])
-    for i in range(1, len(values)):
-        result = jnp.where(here == i, jnp.int32(values[i]), result)
-    return result
-
-
 def line_blocks(own, nodes):
     here = lax.axis_index("occ")
-    blocks = [own]
-    places = [here]
-    origins = [list(range(nodes))]
-    size = 1
-    while size < nodes:
-        fresh, fresh_origins = [], []
-        place = here % (2 * size)
-        dist = jnp.where(place < size, size - 1 - place, place - size)
-        middles = [g * 2 * size + size for g in range(nodes // (2 * size))]
-        for block, origin in zip(blocks, origins):
-            pairs = [(m - 1, m) for m in middles] + [(m, m - 1) for m in middles]
-            moving = lax.ppermute(block, "occ", pairs)
-            got = moving
-            for hop in range(1, size):
-                pairs = [(m - hop, m - hop - 1) for m in middles] + [(m + hop - 1, m + hop) for m in middles]
-                moving = lax.ppermute(moving, "occ", pairs)
-                got = jnp.where(dist == hop, moving, got)
-            fresh.append(got)
-            table = [0] * nodes
-            for m in middles:
-                for k in range(size):
-                    table[m - 1 - k] = origin[m]
-                    table[m + k] = origin[m - 1]
-            fresh_origins.append(table)
-        blocks += fresh
-        origins += fresh_origins
-        size *= 2
-    return blocks, [pick(origin, here) for origin in origins]
+
+    def direct(x, d):
+        return lax.ppermute(x, "occ", [(i, i ^ d) for i in range(nodes)])
+
+    if nodes != 4:
+        return [(d, own if d == 0 else direct(own, d)) for d in range(nodes)]
+    near = direct(own, 1)
+    centre = lax.ppermute(own, "occ", [(1, 2), (2, 1)])
+    far = lax.ppermute(own, "occ", [(0, 3), (3, 0)])
+    middle = (here == 1) | (here == 2)
+    last = lax.ppermute(jnp.where(middle, centre, own), "occ", [(1, 0), (2, 3), (0, 2), (3, 1)])
+    return [(0, own), (1, near), (3, (middle, centre, far)), (2, last)]
 
 
 def per_device(sizes, amplitudes, amp_mask, integrals, int_mask):
@@ -143,14 +120,13 @@
     rows = amplitudes.shape[0]
     groups = n_vir // 2
     own_depth, width = integrals.shape
-    half = width // 2
 
     def swap(x, bits):
         return lax.ppermute(x, "vir", [(i, i ^ bits) for i in range(n_vir)])
 
     me = lax.axis_index("vir")
     weighted = masked(integrals, int_mask, TILE_V)
-    blocks, places = line_blocks(weighted, n_occ)
+    blocks = line_blocks(weighted, n_occ)
 
     position = jnp.stack([me // 2, me % 2]).astype(jnp.int32)
     parts = cut_amplitudes(after(position, weighted), amp_mask, amplitudes, groups, own_depth // TILE_V)
@@ -166,15 +142,30 @@
     near = [[r for r in range(groups) if not r & o[0]] for o in orders]
 
     out = jnp.zeros((rows, n_occ * width), jnp.float32)
-    token = parts
-    for block, place in zip(blocks, places):
-        block = after(block, *token)
-        other = swap(block, 1)
+    token = [rel[1]]
+    for n, (d, block) in enumerate(blocks):
+        if isinstance(block, tuple):
+            middle, centre, far = block
+            centre, far = lax.optimization_barrier((centre, far, *sent))[:2]
+            block = jnp.where(middle, centre, far)
+        elif n > 1:
+            block = after(block, *sent)
+        if n == 0:
+            first_blocks = [blocks[1][1]] + ([blocks[2][1][1]] if isinstance(blocks[2][1], tuple) else [])
+            other = swap(after(block, rel[1]), 1)
+            block = after(block, *first_blocks)
+        else:
+            other = swap(block, 1)
+            block, other = lax.optimization_barrier((block, other, *token))[:2]
         sent = products(away, rel, block, other)
         moving = [swap(sent[h], 2 * orders[h][0]) for h in range(2)]
-        stay = products(near, rel, block, after(other, *sent))
+        stay = products(near, rel, after(block, *sent), other)
         held = [{r: stay[h][i * rows : (i + 1) * rows] for i, r in enumerate(near[h])} for h in range(2)]
+        moved = [None, None]
         for level in range(len(bits)):
+            if n in (1, 2) and level == 0:
+                soon = blocks[n + 1][1]
+                moving = list(lax.optimization_barrier((*moving, soon[2] if isinstance(soon, tuple) else soon))[:2])
             for h in range(2):
                 for i, r in enumerate(sorted(held[h])):
                     held[h][r] = held[h][r] + moving[h][i * rows : (i + 1) * rows]
@@ -183,12 +174,14 @@
             for h in range(2):
                 bit = orders[h][level + 1]
                 going = [r for r in sorted(held[h]) if r & bit]
-                moving[h] = swap(jnp.concatenate([held[h][r] for r in going], axis=0), 2 * bit)
+                moved[h] = jnp.concatenate([held[h][r] for r in going], axis=0)
+                moving[h] = swap(moved[h], 2 * bit)
                 for r in going:
                     del held[h][r]
         done = jnp.concatenate([held[h][0] for h in range(2)], axis=1)
+        place = lax.axis_index("occ") ^ d
         out = lax.dynamic_update_slice(out, done, (0, place * width))
-        token = moving
+        token = moved if n > 1 else moving
     return out
 
 

time: 148 us -> 134 us (0.905)
  waiting for transfers between devices: 80.6 us -> 65 us
  Pallas kernels: 18.5 us -> 21.1 us
  starting transfers between devices: 30.7 us -> 33 us
  local copies, waits for them, and re-layouts: 4.48 us -> 2.44 us
    ppermute x5 -> x4, waiting for transfers between devices: 28.8 us -> 19.7 us  [the longest x1 15.2 us: direct(): return lax.ppermute(x, 'occ', [(i, i ^ d) for i in range(nodes)])]
    ppermute x23, waiting for transfers between devices: 51.8 us -> 45.3 us  [swap(): return lax.ppermute(x, 'vir', [(i, i ^ bits) for i in range(n_vir)])]
    ppermute x23, starting transfers between devices: 22.5 us -> 25.2 us  [swap(): return lax.ppermute(x, 'vir', [(i, i ^ bits) for i in range(n_vir)])]
    pallas_call x8, Pallas kernels: 17.8 us -> 20.4 us  [products(): pl.pallas_call(functools.partial(dot_kernel, lists, names), out_shape=[ja...]
    unnamed x40 -> x34, local copies, waits for them, and re-layouts: 4.17 us -> 2.13 us
    ppermute x5 -> x4, starting transfers between devices: 8.2 us -> 7.81 us  [the longest x1 5.51 us: line_blocks(): far = lax.ppermute(own, 'occ', [(0, 3), (3, 0)])]
  transfers between devices with their start and end apart: 28 -> 27, of which waited for: 15 -> 18; matrix products, arithmetic and copies ran while one was open for 7% -> 6% of each run, Pallas kernels for 11% -> 15%
where the time goes in v6:
time: 134 us; the launch traced here: 133 us
  waiting for transfers between devices  65 us (49%)
  starting transfers between devices  33 us (25%)
  Pallas kernels  21.1 us (16%)
  other arithmetic  11.4 us (9%)
  local copies, waits for them, and re-layouts  2.44 us (2%)
    ppermute x23, waiting for transfers between devices, swap(): return lax.ppermute(x, 'vir', [(i, i ^ bits) for i in range(n_vir)])  45.3 us
    ppermute x23, starting transfers between devices, swap(): return lax.ppermute(x, 'vir', [(i, i ^ bits) for i in range(n_vir)])  25.2 us
    pallas_call x8, Pallas kernels, products(): pl.pallas_call(functools.partial(dot_kernel, lists, names), out_shape=[ja...  20.4 us
    ppermute x1, waiting for transfers between devices, direct(): return lax.ppermute(x, 'occ', [(i, i ^ d) for i in range(nodes)])  15.2 us
    add x16, other arithmetic, per_device(): held[h][r] = held[h][r] + moving[h][i * rows:(i + 1) * rows]  6.7 us
    ppermute x1, starting transfers between devices, line_blocks(): far = lax.ppermute(own, 'occ', [(0, 3), (3, 0)])  5.51 us
    ppermute x1, waiting for transfers between devices, line_blocks(): lax.ppermute(jnp.where(middle, centre, own), 'occ', [(1, 0), (2, 3), (0,...  4.03 us
  transfers between devices with their start and end apart: 27, of which 18 were waited for; matrix products, arithmetic and copies ran while one was open for 6% of the time, Pallas kernels for 15%

profile of v6, /device:TPU:0, one launch (start us, length us, event | category | flops | bytes accessed | tf_op | source)
XLA Modules:
  0.0 133.3 jit_solution(7629761259690340458)
XLA Ops:
  0.0 0.8 convert_element_type.3
  1.0 0.3 copy-done.10
  1.3 0.3 bitcast_multiply_fusion.refs_3_
  1.6 1.1 copy-done.2
  2.7 0.8 cut.1
  3.5 3.0 %collective-permute-start = (f32[128,768]{1,0:T(8,128)S(1)}, f32[128,768]{1,0:T(8,128)S(1)}, u32[]{:S(2)}, u32[]{:S(2)}) collective-permute-start(f32[128,768]{1,0:T(8,128)S(1)} %get-tuple-element.47), channel_id=1, source_target_pairs={{0,2},{1,3},{2,0},{3,1},{4,6},{5,7},{6,4},{7,5},{8,10},{9,11},{10,... | collective-permute-start | bytes 1179656 | tf_op jit(solution)/shard_map/ppermute | solution.py:125
  6.5 1.6 %collective-permute-start.2 = (f32[384,768]{1,0:T(8,128)S(1)}, f32[384,768]{1,0:T(8,128)}, u32[]{:S(2)}, u32[]{:S(2)}) collective-permute-start(f32[384,768]{1,0:T(8,128)S(1)} %bitcast_multiply_fusion.refs_3_), channel_id=1, source_target_pairs={{0,8},{8,0},{16,24},{24,16},{1,9},{9,1},{17,25},{25,17},{2,10},{10... | collective-permute-start | bytes 3538952 | tf_op jit(solution)/shard_map/ppermute | solution.py:106
  8.1 0.7 collective-permute-start.3
  8.8 6.8 %collective-permute-done.refs_0_.refs_1_ = f32[128,768]{1,0:T(8,128)S(1)} collective-permute-done((f32[128,768]{1,0:T(8,128)S(1)}, f32[128,768]{1,0:T(8,128)S(1)}, u32[]{:S(2)}, u32[]{:S(2)}) %collective-permute-start) | collective-permute-done | bytes 393248 | tf_op jit(solution)/shard_map/ppermute | solution.py:125
  15.6 1.8 %collective-permute-start.1 = (f32[128,768]{1,0:T(8,128)S(1)}, f32[128,768]{1,0:T(8,128)S(1)}, u32[]{:S(2)}, u32[]{:S(2)}) collective-permute-start(f32[128,768]{1,0:T(8,128)S(1)} %get-tuple-element.48), channel_id=1, source_target_pairs={{0,4},{1,5},{2,6},{3,7},{4,0},{5,1},{6,2},{7,3},{8,12},{9,13},{10,... | collective-permute-start | bytes 1179656 | tf_op jit(solution)/shard_map/ppermute | solution.py:125
  17.4 1.4 %collective-permute-start.4 = (f32[128,768]{1,0:T(8,128)S(1)}, f32[128,768]{1,0:T(8,128)S(1)}, u32[]{:S(2)}, u32[]{:S(2)}) collective-permute-start(f32[128,768]{1,0:T(8,128)S(1)} %get-tuple-element.50), channel_id=1, source_target_pairs={{0,6},{1,7},{2,4},{3,5},{4,2},{5,3},{6,0},{7,1},{8,14},{9,15},{10,... | collective-permute-start | bytes 1179656 | tf_op jit(solution)/shard_map/ppermute | solution.py:125
  18.8 15.2 %collective-permute-done.2.refs_3_ = f32[384,768]{1,0:T(8,128)} collective-permute-done((f32[384,768]{1,0:T(8,128)S(1)}, f32[384,768]{1,0:T(8,128)}, u32[]{:S(2)}, u32[]{:S(2)}) %collective-permute-start.2) | collective-permute-done | bytes 1179680 | tf_op jit(solution)/shard_map/ppermute | solution.py:106
  34.0 5.5 %collective-permute-start.13 = (f32[384,768]{1,0:T(8,128)S(1)}, f32[384,768]{1,0:T(8,128)}, u32[]{:S(2)}, u32[]{:S(2)}) collective-permute-start(f32[384,768]{1,0:T(8,128)S(1)} %bitcast_multiply_fusion.refs_3_), channel_id=1, source_target_pairs={{0,24},{24,0},{1,25},{25,1},{2,26},{26,2},{3,27},{27,3},{4,28},{28... | collective-permute-start | bytes 3538952 | tf_op jit(solution)/shard_map/ppermute | solution.py:112
  39.6 1.7 %products.8 = (f32[256,384]{1,0:T(8,128)S(1)}, f32[256,384]{1,0:T(8,128)S(1)}) custom-call(f32[128,768]{1,0:T(8,128)S(1)} %collective-permute-done.refs_0_.refs_1_, f32[128,768]{1,0:T(8,128)S(1)} %collective-permute-done.1.refs_1_.refs_2_, f32[128,768]{1,0:T(8,128)S(1)} %collective-permute-done.4.refs_2_, f32[384,768]{1,0:T(8,128)S(1)} %bitcast_multiply_fusion.refs_3_, ...), custom_call_target="tpu_custom_call" | custom-call | flops 1 | bytes 1 | tf_op jit(solution)/shard_map/products/pallas_call | solution.py:91
  41.3 1.6 %collective-permute-start.8 = (f32[256,384]{1,0:T(8,128)S(1)}, f32[256,384]{1,0:T(8,128)S(1)}, u32[]{:S(2)}, u32[]{:S(2)}) collective-permute-start(f32[256,384]{1,0:T(8,128)S(1)} %get-tuple-element.53), channel_id=1, source_target_pairs={{0,4},{1,5},{2,6},{3,7},{4,0},{5,1},{6,2},{7,3},{8,12},{9,13},{10,... | collective-permute-start | bytes 1179656 | tf_op jit(solution)/shard_map/ppermute | solution.py:125
  42.9 0.5 collective-permute-start.6
  43.4 1.7 %products.9 = (f32[256,384]{1,0:T(8,128)S(1)}, f32[256,384]{1,0:T(8,128)S(1)}) custom-call(f32[128,768]{1,0:T(8,128)S(1)} %get-tuple-element.46.refs_0_, f32[128,768]{1,0:T(8,128)S(1)} %collective-permute-done.refs_0_.refs_1_, f32[128,768]{1,0:T(8,128)S(1)} %collective-permute-done.1.refs_1_.refs_2_, f32[384,768]{1,0:T(8,128)S(1)} %bitcast_multiply_fusion.refs_3_, ...), custom_call_target="tpu_custom_call" | custom-call | flops 1 | bytes 1 | tf_op jit(solution)/shard_map/products/pallas_call | solution.py:91
  45.2 7.4 %collective-permute-done.8 = f32[256,384]{1,0:T(8,128)S(1)} collective-permute-done((f32[256,384]{1,0:T(8,128)S(1)}, f32[256,384]{1,0:T(8,128)S(1)}, u32[]{:S(2)}, u32[]{:S(2)}) %collective-permute-start.8) | collective-permute-done | bytes 393248 | tf_op jit(solution)/shard_map/ppermute | solution.py:125
  52.6 0.8 slice_add_fusion.4
  53.4 0.5 collective-permute-start.9
  53.9 0.8 copy-done.11
  54.7 0.7 slice_add_fusion.6
  55.4 1.5 %collective-permute-start.7 = (f32[128,384]{1,0:T(8,128)}, f32[128,384]{1,0:T(8,128)S(1)}, u32[]{:S(2)}, u32[]{:S(2)}) collective-permute-start(f32[128,384]{1,0:T(8,128)} %slice_add_fusion.6), channel_id=1, source_target_pairs={{0,4},{1,5},{2,6},{3,7},{4,0},{5,1},{6,2},{7,3},{8,12},{9,13},{10,... | collective-permute-start | bytes 589832 | tf_op jit(solution)/shard_map/ppermute | solution.py:125
  56.9 3.0 %collective-permute-done.9 = f32[128,384]{1,0:T(8,128)S(1)} collective-permute-done((f32[128,384]{1,0:T(8,128)}, f32[128,384]{1,0:T(8,128)S(1)}, u32[]{:S(2)}, u32[]{:S(2)}) %collective-permute-start.9) | collective-permute-done | bytes 196640 | tf_op jit(solution)/shard_map/ppermute | solution.py:125
  59.9 1.7 %collective-permute-done.7 = f32[128,384]{1,0:T(8,128)S(1)} collective-permute-done((f32[128,384]{1,0:T(8,128)}, f32[128,384]{1,0:T(8,128)S(1)}, u32[]{:S(2)}, u32[]{:S(2)}) %collective-permute-start.7) | collective-permute-done | bytes 196640 | tf_op jit(solution)/shard_map/ppermute | solution.py:125
  61.6 4.1 %products.10 = (f32[256,384]{1,0:T(8,128)}, f32[256,384]{1,0:T(8,128)}) custom-call(f32[128,768]{1,0:T(8,128)S(1)} %collective-permute-done.refs_0_.refs_1_, f32[128,768]{1,0:T(8,128)S(1)} %collective-permute-done.1.refs_1_.refs_2_, f32[128,768]{1,0:T(8,128)S(1)} %collective-permute-done.4.refs_2_, f32[384,768]{1,0:T(8,128)} %collective-permute-done.2.refs_3_, ...), custom_call_target="tpu_custom_call" | custom-call | flops 1 | bytes 1 | tf_op jit(solution)/shard_map/products/pallas_call | solution.py:91
  65.8 0.5 collective-permute-done.13
  66.3 1.4 %broadcast_select_fusion.1.refs_3_ = f32[384,768]{1,0:T(8,128)S(1)} fusion(f32[384,768]{1,0:T(8,128)S(1)} %copy-done.8, f32[384,768]{1,0:T(8,128)} %collective-permute-done.13, pred[]{:T(512)S(6)} %or.3), kind=kLoop, calls=%fused_computation.2 | loop fusion | flops 294912 | bytes 3538945 | tf_op jit(solution)/shard_map/jit(_where)/select_n | solution.py:150
  67.8 1.2 broadcast_select_fusion
  69.0 1.0 collective-permute-start.11
  70.0 1.5 %collective-permute-start.12 = (f32[256,384]{1,0:T(8,128)}, f32[256,384]{1,0:T(8,128)}, u32[]{:S(2)}, u32[]{:S(2)}) collective-permute-start(f32[256,384]{1,0:T(8,128)} %get-tuple-element.60), channel_id=1, source_target_pairs={{0,4},{1,5},{2,6},{3,7},{4,0},{5,1},{6,2},{7,3},{8,12},{9,13},{10,... | collective-permute-start | bytes 1179656 | tf_op jit(solution)/shard_map/ppermute | solution.py:125
  71.5 1.1 fusion.2
  72.7 3.4 %products.11 = (f32[256,384]{1,0:T(8,128)S(1)}, f32[256,384]{1,0:T(8,128)S(1)}) custom-call(f32[128,768]{1,0:T(8,128)S(1)} %get-tuple-element.46.refs_0_, f32[128,768]{1,0:T(8,128)S(1)} %collective-permute-done.refs_0_.refs_1_, f32[128,768]{1,0:T(8,128)S(1)} %collective-permute-done.1.refs_1_.refs_2_, f32[384,768]{1,0:T(8,128)} %collective-permute-done.2.refs_3_, ...), custom_call_target="tpu_custom_call" | custom-call | flops 1 | bytes 1 | tf_op jit(solution)/shard_map/products/pallas_call | solution.py:91
  76.1 4.7 %collective-permute-done.11 = f32[256,384]{1,0:T(8,128)} collective-permute-done((f32[256,384]{1,0:T(8,128)}, f32[256,384]{1,0:T(8,128)}, u32[]{:S(2)}, u32[]{:S(2)}) %collective-permute-start.11) | collective-permute-done | bytes 393248 | tf_op jit(solution)/shard_map/ppermute | solution.py:125
  80.8 0.8 collective-permute-done.12
  81.5 1.0 slice_add_fusion.10
  82.5 1.1 collective-permute-start.15
  83.6 1.0 slice_add_fusion.11
  84.5 1.6 %collective-permute-start.14 = (f32[128,384]{1,0:T(8,128)S(1)}, f32[128,384]{1,0:T(8,128)S(1)}, u32[]{:S(2)}, u32[]{:S(2)}) collective-permute-start(f32[128,384]{1,0:T(8,128)S(1)} %slice_add_fusion.11), channel_id=1, source_target_pairs={{0,4},{1,5},{2,6},{3,7},{4,0},{5,1},{6,2},{7,3},{8,12},{9,13},{10,... | collective-permute-start | bytes 589832 | tf_op jit(solution)/shard_map/ppermute | solution.py:125
  86.1 2.6 %collective-permute-done.15 = f32[128,384]{1,0:T(8,128)S(1)} collective-permute-done((f32[128,384]{1,0:T(8,128)S(1)}, f32[128,384]{1,0:T(8,128)S(1)}, u32[]{:S(2)}, u32[]{:S(2)}) %collective-permute-start.15) | collective-permute-done | bytes 196640 | tf_op jit(solution)/shard_map/ppermute | solution.py:125
  88.8 1.7 %collective-permute-done.14 = f32[128,384]{1,0:T(8,128)S(1)} collective-permute-done((f32[128,384]{1,0:T(8,128)S(1)}, f32[128,384]{1,0:T(8,128)S(1)}, u32[]{:S(2)}, u32[]{:S(2)}) %collective-permute-start.14) | collective-permute-done | bytes 196640 | tf_op jit(solution)/shard_map/ppermute | solution.py:125
  90.5 3.0 %products.12 = (f32[256,384]{1,0:T(8,128)S(1)}, f32[256,384]{1,0:T(8,128)S(1)}) custom-call(f32[128,768]{1,0:T(8,128)S(1)} %collective-permute-done.refs_0_.refs_1_, f32[128,768]{1,0:T(8,128)S(1)} %collective-permute-done.1.refs_1_.refs_2_, f32[128,768]{1,0:T(8,128)S(1)} %copy-done.1, f32[384,768]{1,0:T(8,128)S(1)} %broadcast_select_fusion.1.refs_3_, ...), custom_call_target="tpu_custom_call" | custom-call | flops 1 | bytes 1 | tf_op jit(solution)/shard_map/products/pallas_call | solution.py:91
  93.5 4.0 %collective-permute-done.19.refs_3_ = f32[384,768]{1,0:T(8,128)S(1)} collective-permute-done((f32[384,768]{1,0:T(8,128)}, f32[384,768]{1,0:T(8,128)S(1)}, u32[]{:S(2)}, u32[]{:S(2)}) %collective-permute-start.19) | collective-permute-done | bytes 1179680 | tf_op jit(solution)/shard_map/ppermute | solution.py:114
  97.7 1.1 collective-permute-start.17
  98.8 1.5 %collective-permute-start.18 = (f32[256,384]{1,0:T(8,128)S(1)}, f32[256,384]{1,0:T(8,128)S(1)}, u32[]{:S(2)}, u32[]{:S(2)}) collective-permute-start(f32[256,384]{1,0:T(8,128)S(1)} %get-tuple-element.71), channel_id=1, source_target_pairs={{0,4},{1,5},{2,6},{3,7},{4,0},{5,1},{6,2},{7,3},{8,12},{9,13},{10,... | collective-permute-start | bytes 1179656 | tf_op jit(solution)/shard_map/ppermute | solution.py:125
  100.3 1.0 add_add_fusion.2
  101.3 1.0 add_add_fusion.3
  102.3 3.0 %products.13 = (f32[256,384]{1,0:T(8,128)S(1)}, f32[256,384]{1,0:T(8,128)S(1)}) custom-call(f32[128,768]{1,0:T(8,128)S(1)} %get-tuple-element.46.refs_0_, f32[128,768]{1,0:T(8,128)S(1)} %collective-permute-done.refs_0_.refs_1_, f32[128,768]{1,0:T(8,128)S(1)} %collective-permute-done.1.refs_1_.refs_2_, f32[384,768]{1,0:T(8,128)S(1)} %broadcast_select_fusion.1.refs_3_, ...), custom_call_target="tpu_custom_call" | custom-call | flops 1 | bytes 1 | tf_op jit(solution)/shard_map/products/pallas_call | solution.py:91
  105.3 4.0 %collective-permute-done.17 = f32[256,384]{1,0:T(8,128)S(1)} collective-permute-done((f32[256,384]{1,0:T(8,128)S(1)}, f32[256,384]{1,0:T(8,128)S(1)}, u32[]{:S(2)}, u32[]{:S(2)}) %collective-permute-start.17) | collective-permute-done | bytes 393248 | tf_op jit(solution)/shard_map/ppermute | solution.py:125
  109.3 0.8 collective-permute-done.18
  110.1 1.1 collective-permute-start.21
  111.2 1.6 %collective-permute-start.20 = (f32[128,384]{1,0:T(8,128)S(1)}, f32[128,384]{1,0:T(8,128)S(1)}, u32[]{:S(2)}, u32[]{:S(2)}) collective-permute-start(f32[128,384]{1,0:T(8,128)S(1)} %slice_add_fusion.9), channel_id=1, source_target_pairs={{0,4},{1,5},{2,6},{3,7},{4,0},{5,1},{6,2},{7,3},{8,12},{9,13},{10,... | collective-permute-start | bytes 589832 | tf_op jit(solution)/shard_map/ppermute | solution.py:125
  112.8 1.7 %products.14 = (f32[256,384]{1,0:T(8,128)S(1)}, f32[256,384]{1,0:T(8,128)S(1)}) custom-call(f32[128,768]{1,0:T(8,128)S(1)} %collective-permute-done.refs_0_.refs_1_, f32[128,768]{1,0:T(8,128)S(1)} %collective-permute-done.1.refs_1_.refs_2_, f32[128,768]{1,0:T(8,128)S(1)} %copy-done.1, f32[384,768]{1,0:T(8,128)S(1)} %collective-permute-done.19.refs_3_, ...), custom_call_target="tpu_custom_call" | custom-call | flops 1 | bytes 1 | tf_op jit(solution)/shard_map/products/pallas_call | solution.py:91
  114.5 0.6 collective-permute-start.25
  115.1 1.3 collective-permute-done.21
  116.4 1.1 collective-permute-start.23
  117.5 0.9 collective-permute-done.20
  118.4 1.7 %products.15 = (f32[256,384]{1,0:T(8,128)S(1)}, f32[256,384]{1,0:T(8,128)S(1)}) custom-call(f32[128,768]{1,0:T(8,128)S(1)} %get-tuple-element.46.refs_0_, f32[128,768]{1,0:T(8,128)S(1)} %collective-permute-done.refs_0_.refs_1_, f32[128,768]{1,0:T(8,128)S(1)} %collective-permute-done.1.refs_1_.refs_2_, f32[384,768]{1,0:T(8,128)S(1)} %collective-permute-done.19.refs_3_, ...), custom_call_target="tpu_custom_call" | custom-call | flops 1 | bytes 1 | tf_op jit(solution)/shard_map/products/pallas_call | solution.py:91
  120.2 5.4 %collective-permute-done.25 = f32[256,384]{1,0:T(8,128)S(1)} collective-permute-done((f32[256,384]{1,0:T(8,128)S(1)}, f32[256,384]{1,0:T(8,128)S(1)}, u32[]{:S(2)}, u32[]{:S(2)}) %collective-permute-start.25) | collective-permute-done | bytes 393248 | tf_op jit(solution)/shard_map/ppermute | solution.py:125
  125.6 1.1 collective-permute-start.26
  126.8 1.6 %collective-permute-start.24 = (f32[128,384]{1,0:T(8,128)S(1)}, f32[128,384]{1,0:T(8,128)S(1)}, u32[]{:S(2)}, u32[]{:S(2)}) collective-permute-start(f32[128,384]{1,0:T(8,128)S(1)} %slice_add_fusion.2), channel_id=1, source_target_pairs={{0,4},{1,5},{2,6},{3,7},{4,0},{5,1},{6,2},{7,3},{8,12},{9,13},{10,... | collective-permute-start | bytes 589832 | tf_op jit(solution)/shard_map/ppermute | solution.py:125
  128.3 3.1 %collective-permute-done.26 = f32[128,384]{1,0:T(8,128)S(1)} collective-permute-done((f32[128,384]{1,0:T(8,128)S(1)}, f32[128,384]{1,0:T(8,128)S(1)}, u32[]{:S(2)}, u32[]{:S(2)}) %collective-permute-start.26) | collective-permute-done | bytes 196640 | tf_op jit(solution)/shard_map/ppermute | solution.py:125
  131.5 1.0 collective-permute-done.24
  132.5 0.8 maximum_dynamic-update-slice_fusion.3
  (60 shorter events, 0.9 us)
Async XLA Ops:
  0.0 1.3 copy-start.10
  1.3 1.4 %copy-start.2 = (f32[128,3072]{1,0:T(8,128)S(1)}, f32[128,3072]{1,0:T(8,128)}, u32[]{:S(2)}) copy-start(f32[128,3072]{1,0:T(8,128)} %amp_ref.1) | copy-start | bytes 4718596
  1.3 1.4 %copy-start.6 = (s32[4,24]{1,0:T(4,128)S(1)}, s32[4,24]{1,0:T(4,128)}, u32[]{:S(2)}) copy-start(s32[4,24]{1,0:T(4,128)} %mask_ref.1) | copy-start | bytes 1156
  3.5 12.1 %collective-permute-start = (f32[128,768]{1,0:T(8,128)S(1)}, f32[128,768]{1,0:T(8,128)S(1)}, u32[]{:S(2)}, u32[]{:S(2)}) collective-permute-start(f32[128,768]{1,0:T(8,128)S(1)} %get-tuple-element.47), channel_id=1, source_target_pairs={{0,2},{1,3},{2,0},{3,1},{4,6},{5,7},{6,4},{7,5},{8,10},{9,11},{10,... | collective-permute-start | bytes 1179656 | tf_op jit(solution)/shard_map/ppermute | solution.py:125
  6.5 27.5 %collective-permute-start.2 = (f32[384,768]{1,0:T(8,128)S(1)}, f32[384,768]{1,0:T(8,128)}, u32[]{:S(2)}, u32[]{:S(2)}) collective-permute-start(f32[384,768]{1,0:T(8,128)S(1)} %bitcast_multiply_fusion.refs_3_), channel_id=1, source_target_pairs={{0,8},{8,0},{16,24},{24,16},{1,9},{9,1},{17,25},{25,17},{2,10},{10... | collective-permute-start | bytes 3538952 | tf_op jit(solution)/shard_map/ppermute | solution.py:106
  8.1 26.0 %collective-permute-start.3 = (f32[384,768]{1,0:T(8,128)S(1)}, f32[384,768]{1,0:T(8,128)S(1)}, u32[]{:S(2)}, u32[]{:S(2)}) collective-permute-start(f32[384,768]{1,0:T(8,128)S(1)} %bitcast_multiply_fusion.refs_3_), channel_id=1, source_target_pairs={{8,16},{16,8},{9,17},{17,9},{10,18},{18,10},{11,19},{19,11},{12,20... | collective-permute-start | bytes 3538952 | tf_op jit(solution)/shard_map/ppermute | solution.py:111
  15.6 24.0 %collective-permute-start.5 = (f32[384,768]{1,0:T(8,128)S(1)}, f32[384,768]{1,0:T(8,128)S(1)}, u32[]{:S(2)}, u32[]{:S(2)}) collective-permute-start(f32[384,768]{1,0:T(8,128)S(1)} %bitcast_multiply_fusion.refs_3_), channel_id=1, source_target_pairs={{0,1},{1,0},{2,3},{3,2},{4,5},{5,4},{6,7},{7,6},{8,9},{9,8},{10,11... | collective-permute-start | bytes 3538952 | tf_op jit(solution)/shard_map/ppermute | solution.py:125
  15.6 23.9 %collective-permute-start.1 = (f32[128,768]{1,0:T(8,128)S(1)}, f32[128,768]{1,0:T(8,128)S(1)}, u32[]{:S(2)}, u32[]{:S(2)}) collective-permute-start(f32[128,768]{1,0:T(8,128)S(1)} %get-tuple-element.48), channel_id=1, source_target_pairs={{0,4},{1,5},{2,6},{3,7},{4,0},{5,1},{6,2},{7,3},{8,12},{9,13},{10,... | collective-permute-start | bytes 1179656 | tf_op jit(solution)/shard_map/ppermute | solution.py:125
  17.4 22.2 %collective-permute-start.4 = (f32[128,768]{1,0:T(8,128)S(1)}, f32[128,768]{1,0:T(8,128)S(1)}, u32[]{:S(2)}, u32[]{:S(2)}) collective-permute-start(f32[128,768]{1,0:T(8,128)S(1)} %get-tuple-element.50), channel_id=1, source_target_pairs={{0,6},{1,7},{2,4},{3,5},{4,2},{5,3},{6,0},{7,1},{8,14},{9,15},{10,... | collective-permute-start | bytes 1179656 | tf_op jit(solution)/shard_map/ppermute | solution.py:125
  34.0 27.6 %collective-permute-start.10 = (f32[384,768]{1,0:T(8,128)}, f32[384,768]{1,0:T(8,128)}, u32[]{:S(2)}, u32[]{:S(2)}) collective-permute-start(f32[384,768]{1,0:T(8,128)} %collective-permute-done.2.refs_3_), channel_id=1, source_target_pairs={{0,1},{1,0},{2,3},{3,2},{4,5},{5,4},{6,7},{7,6},{8,9},{9,8},{10,11... | collective-permute-start | bytes 3538952 | tf_op jit(solution)/shard_map/ppermute | solution.py:125
  34.0 5.5 %copy-start.7 = (f32[384,768]{1,0:T(8,128)}, f32[384,768]{1,0:T(8,128)S(1)}, u32[]{:S(2)}) copy-start(f32[384,768]{1,0:T(8,128)S(1)} %collective-permute-done.3) | copy-start | bytes 3538948
  34.0 32.2 %collective-permute-start.13 = (f32[384,768]{1,0:T(8,128)S(1)}, f32[384,768]{1,0:T(8,128)}, u32[]{:S(2)}, u32[]{:S(2)}) collective-permute-start(f32[384,768]{1,0:T(8,128)S(1)} %bitcast_multiply_fusion.refs_3_), channel_id=1, source_target_pairs={{0,24},{24,0},{1,25},{25,1},{2,26},{26,2},{3,27},{27,3},{4,28},{28... | collective-permute-start | bytes 3538952 | tf_op jit(solution)/shard_map/ppermute | solution.py:112
  39.6 22.0 %copy-start = (f32[128,768]{1,0:T(8,128)}, f32[128,768]{1,0:T(8,128)S(1)}, u32[]{:S(2)}) copy-start(f32[128,768]{1,0:T(8,128)S(1)} %collective-permute-done.4.refs_2_) | copy-start | bytes 1179652
  41.3 11.3 %collective-permute-start.8 = (f32[256,384]{1,0:T(8,128)S(1)}, f32[256,384]{1,0:T(8,128)S(1)}, u32[]{:S(2)}, u32[]{:S(2)}) collective-permute-start(f32[256,384]{1,0:T(8,128)S(1)} %get-tuple-element.53), channel_id=1, source_target_pairs={{0,4},{1,5},{2,6},{3,7},{4,0},{5,1},{6,2},{7,3},{8,12},{9,13},{10,... | collective-permute-start | bytes 1179656 | tf_op jit(solution)/shard_map/ppermute | solution.py:125
  42.9 11.0 %collective-permute-start.6 = (f32[256,384]{1,0:T(8,128)S(1)}, f32[256,384]{1,0:T(8,128)S(1)}, u32[]{:S(2)}, u32[]{:S(2)}) collective-permute-start(f32[256,384]{1,0:T(8,128)S(1)} %get-tuple-element.52), channel_id=1, source_target_pairs={{0,2},{1,3},{2,0},{3,1},{4,6},{5,7},{6,4},{7,5},{8,10},{9,11},{10,... | collective-permute-start | bytes 1179656 | tf_op jit(solution)/shard_map/ppermute | solution.py:125
  45.2 7.5 %copy-start.5 = (f32[256,384]{1,0:T(8,128)}, f32[256,384]{1,0:T(8,128)S(1)}, u32[]{:S(2)}) copy-start(f32[256,384]{1,0:T(8,128)S(1)} %get-tuple-element.56) | copy-start | bytes 1179652
  45.2 20.6 %copy-start.3 = (f32[256,384]{1,0:T(8,128)}, f32[256,384]{1,0:T(8,128)S(1)}, u32[]{:S(2)}) copy-start(f32[256,384]{1,0:T(8,128)S(1)} %get-tuple-element.55) | copy-start | bytes 1179652
  52.6 2.8 %copy-start.13 = (f32[256,384]{1,0:T(8,128)}, f32[256,384]{1,0:T(8,128)S(1)}, u32[]{:S(2)}) copy-start(f32[256,384]{1,0:T(8,128)S(1)} %collective-permute-done.8) | copy-start | bytes 1179652
  53.4 6.5 %collective-permute-start.9 = (f32[128,384]{1,0:T(8,128)}, f32[128,384]{1,0:T(8,128)S(1)}, u32[]{:S(2)}, u32[]{:S(2)}) collective-permute-start(f32[128,384]{1,0:T(8,128)} %slice_add_fusion.4), channel_id=1, source_target_pairs={{0,2},{1,3},{2,0},{3,1},{4,6},{5,7},{6,4},{7,5},{8,10},{9,11},{10,... | collective-permute-start | bytes 589832 | tf_op jit(solution)/shard_map/ppermute | solution.py:125
  53.9 0.8 copy-start.11
  55.4 6.2 %collective-permute-start.7 = (f32[128,384]{1,0:T(8,128)}, f32[128,384]{1,0:T(8,128)S(1)}, u32[]{:S(2)}, u32[]{:S(2)}) collective-permute-start(f32[128,384]{1,0:T(8,128)} %slice_add_fusion.6), channel_id=1, source_target_pairs={{0,4},{1,5},{2,6},{3,7},{4,0},{5,1},{6,2},{7,3},{8,12},{9,13},{10,... | collective-permute-start | bytes 589832 | tf_op jit(solution)/shard_map/ppermute | solution.py:125
  56.9 9.4 %copy-start.8 = (f32[384,768]{1,0:T(8,128)S(1)}, f32[384,768]{1,0:T(8,128)}, u32[]{:S(2)}) copy-start(f32[384,768]{1,0:T(8,128)} %copy-done.7) | copy-start | bytes 3538948
  59.9 5.9 %copy-start.16 = (f32[128,384]{1,0:T(8,128)}, f32[128,384]{1,0:T(8,128)S(1)}, u32[]{:S(2)}) copy-start(f32[128,384]{1,0:T(8,128)S(1)} %collective-permute-done.9) | copy-start | bytes 589828
  61.6 4.2 %copy-start.14 = (f32[128,384]{1,0:T(8,128)}, f32[128,384]{1,0:T(8,128)S(1)}, u32[]{:S(2)}) copy-start(f32[128,384]{1,0:T(8,128)S(1)} %collective-permute-done.7) | copy-start | bytes 589828
  67.7 22.8 %collective-permute-start.16 = (f32[384,768]{1,0:T(8,128)S(1)}, f32[384,768]{1,0:T(8,128)}, u32[]{:S(2)}, u32[]{:S(2)}) collective-permute-start(f32[384,768]{1,0:T(8,128)S(1)} %broadcast_select_fusion.1.refs_3_), channel_id=1, source_target_pairs={{0,1},{1,0},{2,3},{3,2},{4,5},{5,4},{6,7},{7,6},{8,9},{9,8},{10,11... | collective-permute-start | bytes 3538952 | tf_op jit(solution)/shard_map/ppermute | solution.py:125
  69.0 28.6 %collective-permute-start.19 = (f32[384,768]{1,0:T(8,128)}, f32[384,768]{1,0:T(8,128)S(1)}, u32[]{:S(2)}, u32[]{:S(2)}) collective-permute-start(f32[384,768]{1,0:T(8,128)} %broadcast_select_fusion), channel_id=1, source_target_pairs={{8,0},{16,24},{0,16},{24,8},{9,1},{17,25},{1,17},{25,9},{10,2},{18... | collective-permute-start | bytes 3538952 | tf_op jit(solution)/shard_map/ppermute | solution.py:114
  69.0 11.8 %collective-permute-start.11 = (f32[256,384]{1,0:T(8,128)}, f32[256,384]{1,0:T(8,128)}, u32[]{:S(2)}, u32[]{:S(2)}) collective-permute-start(f32[256,384]{1,0:T(8,128)} %get-tuple-element.59), channel_id=1, source_target_pairs={{0,2},{1,3},{2,0},{3,1},{4,6},{5,7},{6,4},{7,5},{8,10},{9,11},{10,... | collective-permute-start | bytes 1179656 | tf_op jit(solution)/shard_map/ppermute | solution.py:125
  70.0 11.5 %collective-permute-start.12 = (f32[256,384]{1,0:T(8,128)}, f32[256,384]{1,0:T(8,128)}, u32[]{:S(2)}, u32[]{:S(2)}) collective-permute-start(f32[256,384]{1,0:T(8,128)} %get-tuple-element.60), channel_id=1, source_target_pairs={{0,4},{1,5},{2,6},{3,7},{4,0},{5,1},{6,2},{7,3},{8,12},{9,13},{10,... | collective-permute-start | bytes 1179656 | tf_op jit(solution)/shard_map/ppermute | solution.py:125
  72.7 13.4 %copy-start.15 = (f32[128,384]{1,0:T(8,128)S(1)}, f32[128,384]{1,0:T(8,128)}, u32[]{:S(2)}) copy-start(f32[128,384]{1,0:T(8,128)} %copy-done.14) | copy-start | bytes 589828
  76.0 10.1 %copy-start.4 = (f32[256,384]{1,0:T(8,128)S(1)}, f32[256,384]{1,0:T(8,128)}, u32[]{:S(2)}) copy-start(f32[256,384]{1,0:T(8,128)} %copy-done.3) | copy-start | bytes 1179652
  76.1 10.0 %copy-start.12 = (f32[256,384]{1,0:T(8,128)S(1)}, f32[256,384]{1,0:T(8,128)}, u32[]{:S(2)}) copy-start(f32[256,384]{1,0:T(8,128)} %copy-done.11) | copy-start | bytes 1179652
  76.1 14.4 %copy-start.1 = (f32[128,768]{1,0:T(8,128)S(1)}, f32[128,768]{1,0:T(8,128)}, u32[]{:S(2)}) copy-start(f32[128,768]{1,0:T(8,128)} %copy-done) | copy-start | bytes 1179652
  82.5 6.3 %collective-permute-start.15 = (f32[128,384]{1,0:T(8,128)S(1)}, f32[128,384]{1,0:T(8,128)S(1)}, u32[]{:S(2)}, u32[]{:S(2)}) collective-permute-start(f32[128,384]{1,0:T(8,128)S(1)} %slice_add_fusion.10), channel_id=1, source_target_pairs={{0,2},{1,3},{2,0},{3,1},{4,6},{5,7},{6,4},{7,5},{8,10},{9,11},{10,... | collective-permute-start | bytes 589832 | tf_op jit(solution)/shard_map/ppermute | solution.py:125
  84.5 6.0 %collective-permute-start.14 = (f32[128,384]{1,0:T(8,128)S(1)}, f32[128,384]{1,0:T(8,128)S(1)}, u32[]{:S(2)}, u32[]{:S(2)}) collective-permute-start(f32[128,384]{1,0:T(8,128)S(1)} %slice_add_fusion.11), channel_id=1, source_target_pairs={{0,4},{1,5},{2,6},{3,7},{4,0},{5,1},{6,2},{7,3},{8,12},{9,13},{10,... | collective-permute-start | bytes 589832 | tf_op jit(solution)/shard_map/ppermute | solution.py:125
  97.5 15.2 %collective-permute-start.22 = (f32[384,768]{1,0:T(8,128)S(1)}, f32[384,768]{1,0:T(8,128)S(1)}, u32[]{:S(2)}, u32[]{:S(2)}) collective-permute-start(f32[384,768]{1,0:T(8,128)S(1)} %collective-permute-done.19.refs_3_), channel_id=1, source_target_pairs={{0,1},{1,0},{2,3},{3,2},{4,5},{5,4},{6,7},{7,6},{8,9},{9,8},{10,11... | collective-permute-start | bytes 3538952 | tf_op jit(solution)/shard_map/ppermute | solution.py:125
  97.7 11.6 %collective-permute-start.17 = (f32[256,384]{1,0:T(8,128)S(1)}, f32[256,384]{1,0:T(8,128)S(1)}, u32[]{:S(2)}, u32[]{:S(2)}) collective-permute-start(f32[256,384]{1,0:T(8,128)S(1)} %get-tuple-element.70), channel_id=1, source_target_pairs={{0,2},{1,3},{2,0},{3,1},{4,6},{5,7},{6,4},{7,5},{8,10},{9,11},{10,... | collective-permute-start | bytes 1179656 | tf_op jit(solution)/shard_map/ppermute | solution.py:125
  98.8 11.2 %collective-permute-start.18 = (f32[256,384]{1,0:T(8,128)S(1)}, f32[256,384]{1,0:T(8,128)S(1)}, u32[]{:S(2)}, u32[]{:S(2)}) collective-permute-start(f32[256,384]{1,0:T(8,128)S(1)} %get-tuple-element.71), channel_id=1, source_target_pairs={{0,4},{1,5},{2,6},{3,7},{4,0},{5,1},{6,2},{7,3},{8,12},{9,13},{10,... | collective-permute-start | bytes 1179656 | tf_op jit(solution)/shard_map/ppermute | solution.py:125
  110.1 6.3 %collective-permute-start.21 = (f32[128,384]{1,0:T(8,128)S(1)}, f32[128,384]{1,0:T(8,128)S(1)}, u32[]{:S(2)}, u32[]{:S(2)}) collective-permute-start(f32[128,384]{1,0:T(8,128)S(1)} %slice_add_fusion.8), channel_id=1, source_target_pairs={{0,2},{1,3},{2,0},{3,1},{4,6},{5,7},{6,4},{7,5},{8,10},{9,11},{10,... | collective-permute-start | bytes 589832 | tf_op jit(solution)/shard_map/ppermute | solution.py:125
  111.2 7.1 %collective-permute-start.20 = (f32[128,384]{1,0:T(8,128)S(1)}, f32[128,384]{1,0:T(8,128)S(1)}, u32[]{:S(2)}, u32[]{:S(2)}) collective-permute-start(f32[128,384]{1,0:T(8,128)S(1)} %slice_add_fusion.9), channel_id=1, source_target_pairs={{0,4},{1,5},{2,6},{3,7},{4,0},{5,1},{6,2},{7,3},{8,12},{9,13},{10,... | collective-permute-start | bytes 589832 | tf_op jit(solution)/shard_map/ppermute | solution.py:125
  114.5 11.1 %collective-permute-start.25 = (f32[256,384]{1,0:T(8,128)S(1)}, f32[256,384]{1,0:T(8,128)S(1)}, u32[]{:S(2)}, u32[]{:S(2)}) collective-permute-start(f32[256,384]{1,0:T(8,128)S(1)} %get-tuple-element.81), channel_id=1, source_target_pairs={{0,4},{1,5},{2,6},{3,7},{4,0},{5,1},{6,2},{7,3},{8,12},{9,13},{10,... | collective-permute-start | bytes 1179656 | tf_op jit(solution)/shard_map/ppermute | solution.py:125
  116.4 10.3 %collective-permute-start.23 = (f32[256,384]{1,0:T(8,128)S(1)}, f32[256,384]{1,0:T(8,128)S(1)}, u32[]{:S(2)}, u32[]{:S(2)}) collective-permute-start(f32[256,384]{1,0:T(8,128)S(1)} %get-tuple-element.80), channel_id=1, source_target_pairs={{0,2},{1,3},{2,0},{3,1},{4,6},{5,7},{6,4},{7,5},{8,10},{9,11},{10,... | collective-permute-start | bytes 1179656 | tf_op jit(solution)/shard_map/ppermute | solution.py:125
  118.4 1.8 %copy-start.9 = (f32[128,3072]{1,0:T(8,128)}, f32[128,3072]{1,0:T(8,128)S(1)}, u32[]{:S(2)}) copy-start(f32[128,3072]{1,0:T(8,128)S(1)} %maximum_dynamic-update-slice_fusion.2) | copy-start | bytes 4718596
  125.6 5.8 %collective-permute-start.26 = (f32[128,384]{1,0:T(8,128)S(1)}, f32[128,384]{1,0:T(8,128)S(1)}, u32[]{:S(2)}, u32[]{:S(2)}) collective-permute-start(f32[128,384]{1,0:T(8,128)S(1)} %slice_add_fusion), channel_id=1, source_target_pairs={{0,2},{1,3},{2,0},{3,1},{4,6},{5,7},{6,4},{7,5},{8,10},{9,11},{10,... | collective-permute-start | bytes 589832 | tf_op jit(solution)/shard_map/ppermute | solution.py:125
  126.8 5.7 %collective-permute-start.24 = (f32[128,384]{1,0:T(8,128)S(1)}, f32[128,384]{1,0:T(8,128)S(1)}, u32[]{:S(2)}, u32[]{:S(2)}) collective-permute-start(f32[128,384]{1,0:T(8,128)S(1)} %slice_add_fusion.2), channel_id=1, source_target_pairs={{0,4},{1,5},{2,6},{3,7},{4,0},{5,1},{6,2},{7,3},{8,12},{9,13},{10,... | collective-permute-start | bytes 589832 | tf_op jit(solution)/shard_map/ppermute | solution.py:125

commit v7 on v6

v7 whole, which is shorter than its diff:
```python
import functools

import jax
import jax.numpy as jnp
from jax import lax
from jax.experimental import pallas as pl
from jax.experimental.pallas import tpu as pltpu
from jax.sharding import PartitionSpec as P

TILE_O = 32
TILE_V = 128
VMEM_LIMIT = 12 * 1024 * 1024


def masked(values, mask, tile_rows):
    tile_r, tile_c = mask.shape
    scale = mask.astype(jnp.float32)[:, None, :, None]
    return (values.reshape(tile_r, tile_rows, tile_c, TILE_V) * scale).reshape(values.shape)


def after(value, *earlier):
    return lax.optimization_barrier((value,) + earlier)[0]


def in_vmem(count):
    return [pl.BlockSpec(memory_space=pltpu.VMEM)] * count


def kernel_call(body, outs, operands, smem, name):
    smem_spec = pl.BlockSpec(memory_space=pltpu.SMEM)
    return pl.pallas_call(
        body,
        out_shape=[jax.ShapeDtypeStruct(shape, jnp.float32) for shape in outs],
        in_specs=[smem_spec] * smem + in_vmem(len(operands) - smem),
        out_specs=in_vmem(len(outs)),
        compiler_params=pltpu.CompilerParams(vmem_limit_bytes=VMEM_LIMIT),
        cost_estimate=pl.CostEstimate(flops=1, bytes_accessed=1, transcendentals=0),
        name=name,
    )(*operands)


def tiles(start, count):
    return pl.ds(pl.multiple_of(start * TILE_V, TILE_V), count * TILE_V)


def cut_kernel(groups, depth_tiles, place_ref, mask_ref, amp_ref, *out_refs):
    for r in range(groups):
        start = (place_ref[0] ^ r) * depth_tiles
        for t in range(depth_tiles):
            for o in range(amp_ref.shape[0] // TILE_O):
                rows = pl.ds(o * TILE_O, TILE_O)
                scale = mask_ref[o, start + t].astype(jnp.float32)
                out_refs[r][rows, tiles(t, 1)] = amp_ref[rows, tiles(start + t, 1)] * scale


def halves_kernel(place_ref, mask_ref, int_ref, mine_ref, theirs_ref):
    low = place_ref[1]
    count = mine_ref.shape[1] // TILE_V
    for half, out_ref in ((low, mine_ref), (1 - low, theirs_ref)):
        for t in range(count):
            q = half * count + t
            for k in range(int_ref.shape[0] // TILE_V):
                scale = mask_ref[k, q].astype(jnp.float32)
                out_ref[tiles(k, 1), tiles(t, 1)] = int_ref[tiles(k, 1), tiles(q, 1)] * scale


def join_kernel(place_ref, mine_ref, other_ref, out_ref):
    low = place_ref[1]
    depth = mine_ref.shape[0]
    out_ref[pl.ds(pl.multiple_of(low * depth, depth), depth), :] = mine_ref[...]
    out_ref[pl.ds(pl.multiple_of((1 - low) * depth, depth), depth), :] = other_ref[...]


def split(x):
    high = x.astype(jnp.bfloat16)
    return high, (x - high.astype(jnp.float32)).astype(jnp.bfloat16)


def dot_kernel(count, *refs):
    left, block_ref, outs = refs[: 2 * count], refs[2 * count], refs[2 * count + 1 :]
    rows = left[0].shape[0]
    b_high, b_low = split(block_ref[...])
    for h in range(2):
        for i in range(count):
            a_high, a_low = split(left[h * count + i][...])
            total = None
            for a, b in ((a_high, b_low), (a_low, b_high), (a_high, b_high)):
                term = jnp.dot(a, b, preferred_element_type=jnp.float32)
                total = term if total is None else total + term
            outs[h][i * rows : (i + 1) * rows, :] = total


def products(left, block):
    count = len(left[0])
    shape = (count * left[0][0].shape[0], block.shape[1])
    return kernel_call(functools.partial(dot_kernel, count), [shape] * 2, [*left[0], *left[1], block], 0, "products")


def line_blocks(own, nodes):
    here = lax.axis_index("occ")

    def direct(x, d):
        return lax.ppermute(x, "occ", [(i, i ^ d) for i in range(nodes)])

    if nodes != 4:
        return [(d, own if d == 0 else direct(own, d)) for d in range(nodes)]
    near = direct(own, 1)
    centre = lax.ppermute(own, "occ", [(1, 2), (2, 1)])
    far = lax.ppermute(own, "occ", [(0, 3), (3, 0)])
    middle = (here == 1) | (here == 2)
    last = lax.ppermute(jnp.where(middle, centre, own), "occ", [(1, 0), (2, 3), (0, 2), (3, 1)])
    return [(0, own), (1, near), (3, (middle, centre, far)), (2, last)]


def per_device(sizes, amplitudes, amp_mask, integrals, int_mask):
    n_occ, n_vir = sizes
    rows = amplitudes.shape[0]
    groups = n_vir // 2
    own_depth, width = integrals.shape
    depth, half = 2 * own_depth, width // 2

    def swap(x, bits):
        return lax.ppermute(x, "vir", [(i, i ^ bits) for i in range(n_vir)])

    me, here = lax.axis_index("vir"), lax.axis_index("occ")
    position = jnp.stack([me // 2, me % 2]).astype(jnp.int32)
    mine, theirs = kernel_call(halves_kernel, [(own_depth, half)] * 2, [position, int_mask, integrals], 2, "halves")
    other = swap(theirs, 1)
    parts = kernel_call(
        functools.partial(cut_kernel, groups, depth // TILE_V), [(rows, depth)] * groups, [after(position, mine), amp_mask, amplitudes], 2, "cut"
    )
    (whole,) = kernel_call(join_kernel, [(depth, half)], [position, mine, after(other, *parts)], 1, "join")
    blocks = line_blocks(whole, n_occ)

    rel = [[parts[0]] + [None] * (groups - 1), [None] * groups]
    for r in range(groups - 1, 0, -1):
        rel[0][r] = swap(parts[r], 2 * r)
    for r in range(groups - 1, -1, -1):
        rel[1][r] = swap(rel[0][r] if r else after(parts[0], rel[0][groups - 1]), 1)

    bits = []
    while (1 << len(bits)) < groups:
        bits.append(1 << len(bits))
    orders = [bits, bits[::-1]]
    away = [[r for r in range(groups) if r & o[0]] for o in orders]
    near = [[r for r in range(groups) if not r & o[0]] for o in orders]

    out = jnp.zeros((rows, n_occ * width), jnp.float32)
    token = None
    for n, (d, block) in enumerate(blocks):
        if isinstance(block, tuple):
            middle, centre, far = block
            centre, far = lax.optimization_barrier((centre, far, *sent))[:2]
            block = jnp.where(middle, centre, far)
        if n == 0:
            block = after(block, blocks[1][1], *(blocks[2][1][1:2] if isinstance(blocks[2][1], tuple) else ()))
        else:
            block = after(block, *token)
        sent = products([[rel[h][r] for r in away[h]] for h in range(2)], block)
        moving = [swap(sent[h], 2 * orders[h][0]) for h in range(2)]
        stay = products([[rel[h][r] for r in near[h]] for h in range(2)], after(block, *sent))
        held = [{r: stay[h][i * rows : (i + 1) * rows] for i, r in enumerate(near[h])} for h in range(2)]
        moved = [None, None]
        for level in range(len(bits)):
            if n in (1, 2) and level == 0:
                soon = blocks[n + 1][1]
                moving = list(lax.optimization_barrier((*moving, soon[2] if isinstance(soon, tuple) else soon))[:2])
            for h in range(2):
                for i, r in enumerate(sorted(held[h])):
                    held[h][r] = held[h][r] + moving[h][i * rows : (i + 1) * rows]
            if level + 1 == len(bits):
                break
            for h in range(2):
                bit = orders[h][level + 1]
                going = [r for r in sorted(held[h]) if r & bit]
                moved[h] = jnp.concatenate([held[h][r] for r in going], axis=0)
                moving[h] = swap(moved[h], 2 * bit)
                for r in going:
                    del held[h][r]
        column = (here ^ d) * width
        out = lax.dynamic_update_slice(out, held[0][0], (0, column + (me % 2) * half))
        out = lax.dynamic_update_slice(out, swap(held[1][0], 1), (0, column + (1 - me % 2) * half))
        token = moved if n > 1 else moving
    return out


def solution(mesh):
    sizes = (mesh.shape["occ"], mesh.shape["vir"])

    def run(*args):
        return per_device(sizes, *args)

    in_specs = (P(("occ", "vir"), None), P(("occ", "vir"), None), P("vir", "occ"), P("vir", "occ"))
    out_specs = P(("occ", "vir"), None)
    return jax.shard_map(run, mesh=mesh, in_specs=in_specs, out_specs=out_specs, check_vma=False)
```

time: 134 us -> 125 us (0.933)
  waiting for transfers between devices: 65 us -> 57 us
  other arithmetic: 11.4 us -> 5.78 us
  local copies, waits for them, and re-layouts: 2.44 us -> 7.09 us
  Pallas kernels: 21.1 us -> 18.2 us
  starting transfers between devices: 33 us -> 35.6 us
    ppermute x23 -> x28, waiting for transfers between devices: 45.3 us -> 34.8 us  [swap(): return lax.ppermute(x, 'vir', [(i, i ^ bits) for i in range(n_vir)])]
    ppermute x1, waiting for transfers between devices: 15.2 us -> 4.93 us  [direct(): return lax.ppermute(x, 'occ', [(i, i ^ d) for i in range(nodes)])]
    ppermute x1, waiting for transfers between devices: 0.48 us -> 7.06 us  [line_blocks(): far = lax.ppermute(own, 'occ', [(0, 3), (3, 0)])]
    ppermute x1, waiting for transfers between devices: 4.03 us -> 10.2 us  [line_blocks(): lax.ppermute(jnp.where(middle, centre, own), 'occ', [(1, 0), (2, 3), (0,...]
    unnamed x34 -> x22, local copies, waits for them, and re-layouts: 2.13 us -> 6.2 us
    ppermute x1, starting transfers between devices: 0.01 us -> 3.86 us  [line_blocks(): lax.ppermute(jnp.where(middle, centre, own), 'occ', [(1, 0), (2, 3), (0,...]
    add x16 -> x12, other arithmetic: 6.7 us -> 3.11 us  [per_device(): held[h][r] = held[h][r] + moving[h][i * rows:(i + 1) * rows]]
    pallas_call x9 -> x11, Pallas kernels: 21.1 us -> 18.2 us  [kernel_call(): pl.pallas_call(body, out_shape=[jax.ShapeDtypeStruct(shape, jnp.float32)...]
  transfers between devices with their start and end apart: 27 -> 32, of which waited for: 18 -> 13; matrix products, arithmetic and copies ran while one was open for 6% -> 5% of each run, Pallas kernels for 15% -> 14%
where the time goes in v7:
time: 125 us; the launch traced here: 124 us
  waiting for transfers between devices  57 us (46%)
  starting transfers between devices  35.6 us (28%)
  Pallas kernels  18.2 us (15%)
  local copies, waits for them, and re-layouts  7.09 us (6%)
  other arithmetic  5.78 us (5%)
    ppermute x28, waiting for transfers between devices, swap(): return lax.ppermute(x, 'vir', [(i, i ^ bits) for i in range(n_vir)])  34.8 us
    ppermute x28, starting transfers between devices, swap(): return lax.ppermute(x, 'vir', [(i, i ^ bits) for i in range(n_vir)])  22.9 us
    pallas_call x11, Pallas kernels, kernel_call(): pl.pallas_call(body, out_shape=[jax.ShapeDtypeStruct(shape, jnp.float32)...  18.2 us
    ppermute x1, waiting for transfers between devices, line_blocks(): lax.ppermute(jnp.where(middle, centre, own), 'occ', [(1, 0), (2, 3), (0,...  10.2 us
    ppermute x1, waiting for transfers between devices, line_blocks(): far = lax.ppermute(own, 'occ', [(0, 3), (3, 0)])  7.06 us
    unnamed x22, local copies, waits for them, and re-layouts  6.2 us
    ppermute x1, starting transfers between devices, line_blocks(): far = lax.ppermute(own, 'occ', [(0, 3), (3, 0)])  5.5 us
    ppermute x1, waiting for transfers between devices, direct(): return lax.ppermute(x, 'occ', [(i, i ^ d) for i in range(nodes)])  4.93 us
  transfers between devices with their start and end apart: 32, of which 13 were waited for; matrix products, arithmetic and copies ran while one was open for 5% of the time, Pallas kernels for 14%

profile of v7, /device:TPU:0, one launch (start us, length us, event | category | flops | bytes accessed | tf_op | source)
XLA Modules:
  0.0 124.1 jit_solution(14219577816238674241)
XLA Ops:
  0.0 0.1 pad_add_fusion.place_ref
  0.1 1.3 %copy-done.5 = f32[384,768]{1,0:T(8,128)S(1)} copy-done((f32[384,768]{1,0:T(8,128)S(1)}, f32[384,768]{1,0:T(8,128)}, u32[]{:S(2)}) %copy-start.5) | copy-done | bytes 1179672
  1.3 0.7 copy-done.6
  2.0 0.7 halves.1
  2.7 0.5 collective-permute-start.5
  3.2 1.4 %copy-done.4 = f32[128,3072]{1,0:T(8,128)S(1)} copy-done((f32[128,3072]{1,0:T(8,128)S(1)}, f32[128,3072]{1,0:T(8,128)}, u32[]{:S(2)}) %copy-start.4) | copy-done | bytes 1572888
  4.6 0.7 copy-done.7
  5.3 0.8 cut.1
  6.1 0.6 join.1.refs_4_
  6.7 2.7 %collective-permute-start.6 = (f32[768,384]{1,0:T(8,128)S(1)}, f32[768,384]{1,0:T(8,128)S(1)}, u32[]{:S(2)}, u32[]{:S(2)}) collective-permute-start(f32[768,384]{1,0:T(8,128)S(1)} %join.1.refs_4_), channel_id=1, source_target_pairs={{0,8},{8,0},{16,24},{24,16},{1,9},{9,1},{17,25},{25,17},{2,10},{10... | collective-permute-start | bytes 3538952 | tf_op jit(solution)/shard_map/ppermute | solution.py:103
  9.4 0.7 collective-permute-start.7
  10.1 1.6 %collective-permute-start = (f32[128,768]{1,0:T(8,128)S(1)}, f32[128,768]{1,0:T(8,128)S(1)}, u32[]{:S(2)}, u32[]{:S(2)}) collective-permute-start(f32[128,768]{1,0:T(8,128)S(1)} %get-tuple-element.47), channel_id=1, source_target_pairs={{0,4},{1,5},{2,6},{3,7},{4,0},{5,1},{6,2},{7,3},{8,12},{9,13},{10,... | collective-permute-start | bytes 1179656 | tf_op jit(solution)/shard_map/ppermute | solution.py:123
  11.7 1.4 %collective-permute-start.1 = (f32[128,768]{1,0:T(8,128)S(1)}, f32[128,768]{1,0:T(8,128)S(1)}, u32[]{:S(2)}, u32[]{:S(2)}) collective-permute-start(f32[128,768]{1,0:T(8,128)S(1)} %get-tuple-element.48), channel_id=1, source_target_pairs={{0,6},{1,7},{2,4},{3,5},{4,2},{5,3},{6,0},{7,1},{8,14},{9,15},{10,... | collective-permute-start | bytes 1179656 | tf_op jit(solution)/shard_map/ppermute | solution.py:123
  13.1 0.5 collective-permute-start.3
  13.7 16.2 %collective-permute-done.refs_1_ = f32[128,768]{1,0:T(8,128)S(1)} collective-permute-done((f32[128,768]{1,0:T(8,128)S(1)}, f32[128,768]{1,0:T(8,128)S(1)}, u32[]{:S(2)}, u32[]{:S(2)}) %collective-permute-start) | collective-permute-done | bytes 393248 | tf_op jit(solution)/shard_map/ppermute | solution.py:123
  29.8 0.5 collective-permute-start.9
  30.4 0.7 collective-permute-done.3.refs_0_
  31.1 4.9 %collective-permute-done.6.refs_4_ = f32[768,384]{1,0:T(8,128)S(1)} collective-permute-done((f32[768,384]{1,0:T(8,128)S(1)}, f32[768,384]{1,0:T(8,128)S(1)}, u32[]{:S(2)}, u32[]{:S(2)}) %collective-permute-start.6) | collective-permute-done | bytes 1179680 | tf_op jit(solution)/shard_map/ppermute | solution.py:103
  36.0 1.0 copy-done.2
  37.1 2.1 %products.8 = (f32[256,384]{1,0:T(8,128)}, f32[256,384]{1,0:T(8,128)}) custom-call(f32[128,768]{1,0:T(8,128)S(1)} %collective-permute-done.3.refs_0_, f32[128,768]{1,0:T(8,128)S(1)} %collective-permute-done.1.refs_1_, f32[128,768]{1,0:T(8,128)S(1)} %collective-permute-done.8.refs_2_, f32[128,768]{1,0:T(8,128)S(1)} %collective-permute-done.9.refs_3_, ...), custom_call_target="tpu_custom_call" | custom-call | flops 1 | bytes 1 | tf_op jit(solution)/shard_map/products/pallas_call | solution.py:31
  39.2 1.7 %collective-permute-start.10 = (f32[256,384]{1,0:T(8,128)}, f32[256,384]{1,0:T(8,128)}, u32[]{:S(2)}, u32[]{:S(2)}) collective-permute-start(f32[256,384]{1,0:T(8,128)} %get-tuple-element.54), channel_id=1, source_target_pairs={{0,2},{1,3},{2,0},{3,1},{4,6},{5,7},{6,4},{7,5},{8,10},{9,11},{10,... | collective-permute-start | bytes 1179656 | tf_op jit(solution)/shard_map/ppermute | solution.py:123
  40.9 1.5 %collective-permute-start.12 = (f32[256,384]{1,0:T(8,128)}, f32[256,384]{1,0:T(8,128)}, u32[]{:S(2)}, u32[]{:S(2)}) collective-permute-start(f32[256,384]{1,0:T(8,128)} %get-tuple-element.55), channel_id=1, source_target_pairs={{0,4},{1,5},{2,6},{3,7},{4,0},{5,1},{6,2},{7,3},{8,12},{9,13},{10,... | collective-permute-start | bytes 1179656 | tf_op jit(solution)/shard_map/ppermute | solution.py:123
  42.4 5.5 %collective-permute-start.17 = (f32[768,384]{1,0:T(8,128)S(1)}, f32[768,384]{1,0:T(8,128)}, u32[]{:S(2)}, u32[]{:S(2)}) collective-permute-start(f32[768,384]{1,0:T(8,128)S(1)} %join.1.refs_4_), channel_id=1, source_target_pairs={{0,24},{24,0},{1,25},{25,1},{2,26},{26,2},{3,27},{27,3},{4,28},{28... | collective-permute-start | bytes 3538952 | tf_op jit(solution)/shard_map/ppermute | solution.py:109
  48.0 2.5 %products.9 = (f32[256,384]{1,0:T(8,128)S(1)}, f32[256,384]{1,0:T(8,128)S(1)}) custom-call(f32[128,768]{1,0:T(8,128)S(1)} %get-tuple-element.49.refs_0_, f32[128,768]{1,0:T(8,128)S(1)} %collective-permute-done.refs_1_, f32[128,768]{1,0:T(8,128)S(1)} %collective-permute-done.2.refs_2_, f32[128,768]{1,0:T(8,128)} %collective-permute-done.4.refs_3_, ...), custom_call_target="tpu_custom_call" | custom-call | flops 1 | bytes 1 | tf_op jit(solution)/shard_map/products/pallas_call | solution.py:31
  50.5 0.6 collective-permute-done.10
  51.1 0.9 slice_add_fusion.6
  52.0 1.7 %collective-permute-start.11 = (f32[128,384]{1,0:T(8,128)S(1)}, f32[128,384]{1,0:T(8,128)S(1)}, u32[]{:S(2)}, u32[]{:S(2)}) collective-permute-start(f32[128,384]{1,0:T(8,128)S(1)} %slice_add_fusion.6), channel_id=1, source_target_pairs={{0,4},{1,5},{2,6},{3,7},{4,0},{5,1},{6,2},{7,3},{8,12},{9,13},{10,... | collective-permute-start | bytes 589832 | tf_op jit(solution)/shard_map/ppermute | solution.py:123
  53.8 1.0 slice_add_fusion.4
  54.7 1.6 %collective-permute-start.13 = (f32[128,384]{1,0:T(8,128)S(1)}, f32[128,384]{1,0:T(8,128)S(1)}, u32[]{:S(2)}, u32[]{:S(2)}) collective-permute-start(f32[128,384]{1,0:T(8,128)S(1)} %slice_add_fusion.4), channel_id=1, source_target_pairs={{0,2},{1,3},{2,0},{3,1},{4,6},{5,7},{6,4},{7,5},{8,10},{9,11},{10,... | collective-permute-start | bytes 589832 | tf_op jit(solution)/shard_map/ppermute | solution.py:123
  56.3 0.1 broadcast_select_fusion
  56.4 3.9 %collective-permute-start.23 = (f32[768,384]{1,0:T(8,128)S(1)}, f32[768,384]{1,0:T(8,128)S(1)}, u32[]{:S(2)}, u32[]{:S(2)}) collective-permute-start(f32[768,384]{1,0:T(8,128)S(1)} %broadcast_select_fusion), channel_id=1, source_target_pairs={{8,0},{16,24},{0,16},{24,8},{9,1},{17,25},{1,17},{25,9},{10,2},{18... | collective-permute-start | bytes 3538952 | tf_op jit(solution)/shard_map/ppermute | solution.py:111
  60.3 0.8 collective-permute-done.13
  61.0 1.4 %products.10 = (f32[256,384]{1,0:T(8,128)S(1)}, f32[256,384]{1,0:T(8,128)S(1)}) custom-call(f32[128,768]{1,0:T(8,128)S(1)} %collective-permute-done.3.refs_0_, f32[128,768]{1,0:T(8,128)S(1)} %collective-permute-done.1.refs_1_, f32[128,768]{1,0:T(8,128)S(1)} %collective-permute-done.8.refs_2_, f32[128,768]{1,0:T(8,128)S(1)} %copy-done.1, f32[768,384]{1,0:T(8,128)S(1)} %copy-done.3), custom_call_target="tpu_custom_call" | custom-call | flops 1 | bytes 1 | tf_op jit(solution)/shard_map/products/pallas_call | solution.py:31
  62.5 1.6 %collective-permute-start.15 = (f32[256,384]{1,0:T(8,128)S(1)}, f32[256,384]{1,0:T(8,128)S(1)}, u32[]{:S(2)}, u32[]{:S(2)}) collective-permute-start(f32[256,384]{1,0:T(8,128)S(1)} %get-tuple-element.60), channel_id=1, source_target_pairs={{0,2},{1,3},{2,0},{3,1},{4,6},{5,7},{6,4},{7,5},{8,10},{9,11},{10,... | collective-permute-start | bytes 1179656 | tf_op jit(solution)/shard_map/ppermute | solution.py:123
  64.0 0.5 collective-permute-start.16
  64.5 1.0 fusion.3
  65.6 2.4 %products.11 = (f32[256,384]{1,0:T(8,128)S(1)}, f32[256,384]{1,0:T(8,128)S(1)}) custom-call(f32[128,768]{1,0:T(8,128)S(1)} %get-tuple-element.49.refs_0_, f32[128,768]{1,0:T(8,128)S(1)} %collective-permute-done.refs_1_, f32[128,768]{1,0:T(8,128)S(1)} %collective-permute-done.2.refs_2_, f32[128,768]{1,0:T(8,128)} %collective-permute-done.4.refs_3_, ...), custom_call_target="tpu_custom_call" | custom-call | flops 1 | bytes 1 | tf_op jit(solution)/shard_map/products/pallas_call | solution.py:31
  68.0 7.1 %collective-permute-done.17 = f32[768,384]{1,0:T(8,128)} collective-permute-done((f32[768,384]{1,0:T(8,128)S(1)}, f32[768,384]{1,0:T(8,128)}, u32[]{:S(2)}, u32[]{:S(2)}) %collective-permute-start.17) | collective-permute-done | bytes 1179680 | tf_op jit(solution)/shard_map/ppermute | solution.py:109
  75.1 1.4 %broadcast_select_fusion.1.refs_4_ = f32[768,384]{1,0:T(8,128)S(1)} fusion(f32[768,384]{1,0:T(8,128)S(1)} %copy-done.9, f32[768,384]{1,0:T(8,128)} %collective-permute-done.17, pred[]{:T(512)S(6)} %or.3), kind=kLoop, calls=%fused_computation.1 | loop fusion | flops 294912 | bytes 3538945 | tf_op jit(solution)/shard_map/jit(_where)/select_n | solution.py:154
  76.5 0.6 collective-permute-start.18
  77.1 0.4 collective-permute-start.19
  77.5 0.1 broadcast_in_dim.3
  77.7 1.0 fusion.5
  78.7 3.6 %collective-permute-done.18 = f32[128,384]{1,0:T(8,128)S(1)} collective-permute-done((f32[128,384]{1,0:T(8,128)S(1)}, f32[128,384]{1,0:T(8,128)S(1)}, u32[]{:S(2)}, u32[]{:S(2)}) %collective-permute-start.18) | collective-permute-done | bytes 196640 | tf_op jit(solution)/shard_map/ppermute | solution.py:123
  82.2 0.6 collective-permute-done.19
  82.8 1.4 %products.12 = (f32[256,384]{1,0:T(8,128)S(1)}, f32[256,384]{1,0:T(8,128)S(1)}) custom-call(f32[128,768]{1,0:T(8,128)S(1)} %collective-permute-done.3.refs_0_, f32[128,768]{1,0:T(8,128)S(1)} %collective-permute-done.1.refs_1_, f32[128,768]{1,0:T(8,128)S(1)} %collective-permute-done.8.refs_2_, f32[128,768]{1,0:T(8,128)S(1)} %copy-done.1, ...), custom_call_target="tpu_custom_call" | custom-call | flops 1 | bytes 1 | tf_op jit(solution)/shard_map/products/pallas_call | solution.py:31
  84.3 0.4 collective-permute-start.21
  84.7 1.7 %collective-permute-start.22 = (f32[256,384]{1,0:T(8,128)S(1)}, f32[256,384]{1,0:T(8,128)S(1)}, u32[]{:S(2)}, u32[]{:S(2)}) collective-permute-start(f32[256,384]{1,0:T(8,128)S(1)} %get-tuple-element.71), channel_id=1, source_target_pairs={{0,4},{1,5},{2,6},{3,7},{4,0},{5,1},{6,2},{7,3},{8,12},{9,13},{10,... | collective-permute-start | bytes 1179656 | tf_op jit(solution)/shard_map/ppermute | solution.py:123
  86.5 2.4 %products.13 = (f32[256,384]{1,0:T(8,128)S(1)}, f32[256,384]{1,0:T(8,128)S(1)}) custom-call(f32[128,768]{1,0:T(8,128)S(1)} %get-tuple-element.49.refs_0_, f32[128,768]{1,0:T(8,128)S(1)} %collective-permute-done.refs_1_, f32[128,768]{1,0:T(8,128)S(1)} %collective-permute-done.2.refs_2_, f32[128,768]{1,0:T(8,128)} %collective-permute-done.4.refs_3_, ...), custom_call_target="tpu_custom_call" | custom-call | flops 1 | bytes 1 | tf_op jit(solution)/shard_map/products/pallas_call | solution.py:31
  89.0 10.2 %collective-permute-done.23.refs_4_ = f32[768,384]{1,0:T(8,128)S(1)} collective-permute-done((f32[768,384]{1,0:T(8,128)S(1)}, f32[768,384]{1,0:T(8,128)S(1)}, u32[]{:S(2)}, u32[]{:S(2)}) %collective-permute-start.23) | collective-permute-done | bytes 1179680 | tf_op jit(solution)/shard_map/ppermute | solution.py:111
  99.3 0.6 collective-permute-start.25
  99.9 0.6 collective-permute-start.24
  100.5 1.4 %products.14 = (f32[256,384]{1,0:T(8,128)S(1)}, f32[256,384]{1,0:T(8,128)S(1)}) custom-call(f32[128,768]{1,0:T(8,128)S(1)} %collective-permute-done.3.refs_0_, f32[128,768]{1,0:T(8,128)S(1)} %collective-permute-done.1.refs_1_, f32[128,768]{1,0:T(8,128)S(1)} %collective-permute-done.8.refs_2_, f32[128,768]{1,0:T(8,128)S(1)} %copy-done.1, ...), custom_call_target="tpu_custom_call" | custom-call | flops 1 | bytes 1 | tf_op jit(solution)/shard_map/products/pallas_call | solution.py:31
  101.9 1.6 %collective-permute-start.27 = (f32[256,384]{1,0:T(8,128)S(1)}, f32[256,384]{1,0:T(8,128)S(1)}, u32[]{:S(2)}, u32[]{:S(2)}) collective-permute-start(f32[256,384]{1,0:T(8,128)S(1)} %get-tuple-element.78), channel_id=1, source_target_pairs={{0,2},{1,3},{2,0},{3,1},{4,6},{5,7},{6,4},{7,5},{8,10},{9,11},{10,... | collective-permute-start | bytes 1179656 | tf_op jit(solution)/shard_map/ppermute | solution.py:123
  103.4 1.5 %collective-permute-start.29 = (f32[256,384]{1,0:T(8,128)S(1)}, f32[256,384]{1,0:T(8,128)S(1)}, u32[]{:S(2)}, u32[]{:S(2)}) collective-permute-start(f32[256,384]{1,0:T(8,128)S(1)} %get-tuple-element.79), channel_id=1, source_target_pairs={{0,4},{1,5},{2,6},{3,7},{4,0},{5,1},{6,2},{7,3},{8,12},{9,13},{10,... | collective-permute-start | bytes 1179656 | tf_op jit(solution)/shard_map/ppermute | solution.py:123
  105.0 2.4 %products.15 = (f32[256,384]{1,0:T(8,128)S(1)}, f32[256,384]{1,0:T(8,128)S(1)}) custom-call(f32[128,768]{1,0:T(8,128)S(1)} %get-tuple-element.49.refs_0_, f32[128,768]{1,0:T(8,128)S(1)} %collective-permute-done.refs_1_, f32[128,768]{1,0:T(8,128)S(1)} %collective-permute-done.2.refs_2_, f32[128,768]{1,0:T(8,128)} %collective-permute-done.4.refs_3_, ...), custom_call_target="tpu_custom_call" | custom-call | flops 1 | bytes 1 | tf_op jit(solution)/shard_map/products/pallas_call | solution.py:31
  107.5 0.3 collective-permute-done.24
  107.8 7.1 %collective-permute-done.29 = f32[256,384]{1,0:T(8,128)S(1)} collective-permute-done((f32[256,384]{1,0:T(8,128)S(1)}, f32[256,384]{1,0:T(8,128)S(1)}, u32[]{:S(2)}, u32[]{:S(2)}) %collective-permute-start.29) | collective-permute-done | bytes 393248 | tf_op jit(solution)/shard_map/ppermute | solution.py:123
  115.0 1.6 %collective-permute-start.30 = (f32[128,384]{1,0:T(8,128)S(1)}, f32[128,384]{1,0:T(8,128)S(1)}, u32[]{:S(2)}, u32[]{:S(2)}) collective-permute-start(f32[128,384]{1,0:T(8,128)S(1)} %slice_add_fusion), channel_id=1, source_target_pairs={{0,2},{1,3},{2,0},{3,1},{4,6},{5,7},{6,4},{7,5},{8,10},{9,11},{10,... | collective-permute-start | bytes 589832 | tf_op jit(solution)/shard_map/ppermute | solution.py:123
  116.5 0.6 collective-permute-start.28
  117.1 3.6 %collective-permute-done.30 = f32[128,384]{1,0:T(8,128)S(1)} collective-permute-done((f32[128,384]{1,0:T(8,128)S(1)}, f32[128,384]{1,0:T(8,128)S(1)}, u32[]{:S(2)}, u32[]{:S(2)}) %collective-permute-start.30) | collective-permute-done | bytes 196640 | tf_op jit(solution)/shard_map/ppermute | solution.py:123
  120.8 1.5 %collective-permute-done.28 = f32[128,384]{1,0:T(8,128)S(1)} collective-permute-done((f32[128,384]{1,0:T(8,128)S(1)}, f32[128,384]{1,0:T(8,128)S(1)}, u32[]{:S(2)}, u32[]{:S(2)}) %collective-permute-start.28) | collective-permute-done | bytes 196640 | tf_op jit(solution)/shard_map/ppermute | solution.py:123
  122.3 1.1 copy-done.10
  123.5 0.7 constant_dynamic-update-slice_fusion
  (57 shorter events, 0.8 us)
Async XLA Ops:
  0.1 1.3 %copy-start.5 = (f32[384,768]{1,0:T(8,128)S(1)}, f32[384,768]{1,0:T(8,128)}, u32[]{:S(2)}) copy-start(f32[384,768]{1,0:T(8,128)} %int_ref.1) | copy-start | bytes 3538948
  1.3 0.7 copy-start.6
  2.7 3.4 %collective-permute-start.5 = (f32[384,384]{1,0:T(8,128)S(1)}, f32[384,384]{1,0:T(8,128)S(1)}, u32[]{:S(2)}, u32[]{:S(2)}) collective-permute-start(f32[384,384]{1,0:T(8,128)S(1)} %get-tuple-element.51), channel_id=1, source_target_pairs={{0,1},{1,0},{2,3},{3,2},{4,5},{5,4},{6,7},{7,6},{8,9},{9,8},{10,11... | collective-permute-start | bytes 1769480 | tf_op jit(solution)/shard_map/ppermute | solution.py:123
  3.2 1.4 %copy-start.4 = (f32[128,3072]{1,0:T(8,128)S(1)}, f32[128,3072]{1,0:T(8,128)}, u32[]{:S(2)}) copy-start(f32[128,3072]{1,0:T(8,128)} %amp_ref.1) | copy-start | bytes 4718596
  4.6 0.7 copy-start.7
  6.7 29.3 %collective-permute-start.6 = (f32[768,384]{1,0:T(8,128)S(1)}, f32[768,384]{1,0:T(8,128)S(1)}, u32[]{:S(2)}, u32[]{:S(2)}) collective-permute-start(f32[768,384]{1,0:T(8,128)S(1)} %join.1.refs_4_), channel_id=1, source_target_pairs={{0,8},{8,0},{16,24},{24,16},{1,9},{9,1},{17,25},{25,17},{2,10},{10... | collective-permute-start | bytes 3538952 | tf_op jit(solution)/shard_map/ppermute | solution.py:103
  9.4 27.6 %collective-permute-start.7 = (f32[768,384]{1,0:T(8,128)S(1)}, f32[768,384]{1,0:T(8,128)S(1)}, u32[]{:S(2)}, u32[]{:S(2)}) collective-permute-start(f32[768,384]{1,0:T(8,128)S(1)} %join.1.refs_4_), channel_id=1, source_target_pairs={{8,16},{16,8},{9,17},{17,9},{10,18},{18,10},{11,19},{19,11},{12,20... | collective-permute-start | bytes 3538952 | tf_op jit(solution)/shard_map/ppermute | solution.py:108
  10.1 19.7 %collective-permute-start = (f32[128,768]{1,0:T(8,128)S(1)}, f32[128,768]{1,0:T(8,128)S(1)}, u32[]{:S(2)}, u32[]{:S(2)}) collective-permute-start(f32[128,768]{1,0:T(8,128)S(1)} %get-tuple-element.47), channel_id=1, source_target_pairs={{0,4},{1,5},{2,6},{3,7},{4,0},{5,1},{6,2},{7,3},{8,12},{9,13},{10,... | collective-permute-start | bytes 1179656 | tf_op jit(solution)/shard_map/ppermute | solution.py:123
  11.7 18.1 %collective-permute-start.1 = (f32[128,768]{1,0:T(8,128)S(1)}, f32[128,768]{1,0:T(8,128)S(1)}, u32[]{:S(2)}, u32[]{:S(2)}) collective-permute-start(f32[128,768]{1,0:T(8,128)S(1)} %get-tuple-element.48), channel_id=1, source_target_pairs={{0,6},{1,7},{2,4},{3,5},{4,2},{5,3},{6,0},{7,1},{8,14},{9,15},{10,... | collective-permute-start | bytes 1179656 | tf_op jit(solution)/shard_map/ppermute | solution.py:123
  13.1 17.9 %collective-permute-start.3 = (f32[128,768]{1,0:T(8,128)S(1)}, f32[128,768]{1,0:T(8,128)S(1)}, u32[]{:S(2)}, u32[]{:S(2)}) collective-permute-start(f32[128,768]{1,0:T(8,128)S(1)} %get-tuple-element.50), channel_id=1, source_target_pairs={{0,2},{1,3},{2,0},{3,1},{4,6},{5,7},{6,4},{7,5},{8,10},{9,11},{10,... | collective-permute-start | bytes 1179656 | tf_op jit(solution)/shard_map/ppermute | solution.py:123
  29.8 7.2 %collective-permute-start.8 = (f32[128,768]{1,0:T(8,128)S(1)}, f32[128,768]{1,0:T(8,128)S(1)}, u32[]{:S(2)}, u32[]{:S(2)}) collective-permute-start(f32[128,768]{1,0:T(8,128)S(1)} %collective-permute-done.refs_1_), channel_id=1, source_target_pairs={{0,1},{1,0},{2,3},{3,2},{4,5},{5,4},{6,7},{7,6},{8,9},{9,8},{10,11... | collective-permute-start | bytes 1179656 | tf_op jit(solution)/shard_map/ppermute | solution.py:123
  29.8 7.2 %collective-permute-start.9 = (f32[128,768]{1,0:T(8,128)S(1)}, f32[128,768]{1,0:T(8,128)S(1)}, u32[]{:S(2)}, u32[]{:S(2)}) collective-permute-start(f32[128,768]{1,0:T(8,128)S(1)} %collective-permute-done.1.refs_1_), channel_id=1, source_target_pairs={{0,1},{1,0},{2,3},{3,2},{4,5},{5,4},{6,7},{7,6},{8,9},{9,8},{10,11... | collective-permute-start | bytes 1179656 | tf_op jit(solution)/shard_map/ppermute | solution.py:123
  31.1 16.9 %collective-permute-start.2 = (f32[128,768]{1,0:T(8,128)S(1)}, f32[128,768]{1,0:T(8,128)S(1)}, u32[]{:S(2)}, u32[]{:S(2)}) collective-permute-start(f32[128,768]{1,0:T(8,128)S(1)} %get-tuple-element.49.refs_0_), channel_id=1, source_target_pairs={{0,1},{1,0},{2,3},{3,2},{4,5},{5,4},{6,7},{7,6},{8,9},{9,8},{10,11... | collective-permute-start | bytes 1179656 | tf_op jit(solution)/shard_map/ppermute | solution.py:123
  36.0 1.0 copy-start.2
  37.0 11.0 %collective-permute-start.4 = (f32[128,768]{1,0:T(8,128)S(1)}, f32[128,768]{1,0:T(8,128)}, u32[]{:S(2)}, u32[]{:S(2)}) collective-permute-start(f32[128,768]{1,0:T(8,128)S(1)} %collective-permute-done.3.refs_0_), channel_id=1, source_target_pairs={{0,1},{1,0},{2,3},{3,2},{4,5},{5,4},{6,7},{7,6},{8,9},{9,8},{10,11... | collective-permute-start | bytes 1179656 | tf_op jit(solution)/shard_map/ppermute | solution.py:123
  37.0 5.4 %copy-start.8 = (f32[768,384]{1,0:T(8,128)}, f32[768,384]{1,0:T(8,128)S(1)}, u32[]{:S(2)}) copy-start(f32[768,384]{1,0:T(8,128)S(1)} %collective-permute-done.7) | copy-start | bytes 3538948
  37.1 3.8 %copy-start = (f32[128,768]{1,0:T(8,128)}, f32[128,768]{1,0:T(8,128)S(1)}, u32[]{:S(2)}) copy-start(f32[128,768]{1,0:T(8,128)S(1)} %collective-permute-done.9.refs_3_) | copy-start | bytes 1179652
  39.2 11.8 %collective-permute-start.10 = (f32[256,384]{1,0:T(8,128)}, f32[256,384]{1,0:T(8,128)}, u32[]{:S(2)}, u32[]{:S(2)}) collective-permute-start(f32[256,384]{1,0:T(8,128)} %get-tuple-element.54), channel_id=1, source_target_pairs={{0,2},{1,3},{2,0},{3,1},{4,6},{5,7},{6,4},{7,5},{8,10},{9,11},{10,... | collective-permute-start | bytes 1179656 | tf_op jit(solution)/shard_map/ppermute | solution.py:123
  40.9 12.9 %collective-permute-start.12 = (f32[256,384]{1,0:T(8,128)}, f32[256,384]{1,0:T(8,128)}, u32[]{:S(2)}, u32[]{:S(2)}) collective-permute-start(f32[256,384]{1,0:T(8,128)} %get-tuple-element.55), channel_id=1, source_target_pairs={{0,4},{1,5},{2,6},{3,7},{4,0},{5,1},{6,2},{7,3},{8,12},{9,13},{10,... | collective-permute-start | bytes 1179656 | tf_op jit(solution)/shard_map/ppermute | solution.py:123
  42.4 32.7 %collective-permute-start.17 = (f32[768,384]{1,0:T(8,128)S(1)}, f32[768,384]{1,0:T(8,128)}, u32[]{:S(2)}, u32[]{:S(2)}) collective-permute-start(f32[768,384]{1,0:T(8,128)S(1)} %join.1.refs_4_), channel_id=1, source_target_pairs={{0,24},{24,0},{1,25},{25,1},{2,26},{26,2},{3,27},{27,3},{4,28},{28... | collective-permute-start | bytes 3538952 | tf_op jit(solution)/shard_map/ppermute | solution.py:109
  48.0 8.3 %copy-start.9 = (f32[768,384]{1,0:T(8,128)S(1)}, f32[768,384]{1,0:T(8,128)}, u32[]{:S(2)}) copy-start(f32[768,384]{1,0:T(8,128)} %copy-done.8) | copy-start | bytes 3538948
  52.0 8.3 %collective-permute-start.11 = (f32[128,384]{1,0:T(8,128)S(1)}, f32[128,384]{1,0:T(8,128)S(1)}, u32[]{:S(2)}, u32[]{:S(2)}) collective-permute-start(f32[128,384]{1,0:T(8,128)S(1)} %slice_add_fusion.6), channel_id=1, source_target_pairs={{0,4},{1,5},{2,6},{3,7},{4,0},{5,1},{6,2},{7,3},{8,12},{9,13},{10,... | collective-permute-start | bytes 589832 | tf_op jit(solution)/shard_map/ppermute | solution.py:123
  54.7 6.3 %copy-start.1 = (f32[128,768]{1,0:T(8,128)S(1)}, f32[128,768]{1,0:T(8,128)}, u32[]{:S(2)}) copy-start(f32[128,768]{1,0:T(8,128)} %copy-done) | copy-start | bytes 1179652
  54.7 6.3 %copy-start.3 = (f32[768,384]{1,0:T(8,128)S(1)}, f32[768,384]{1,0:T(8,128)}, u32[]{:S(2)}) copy-start(f32[768,384]{1,0:T(8,128)} %copy-done.2) | copy-start | bytes 3538948
  54.7 6.3 %collective-permute-start.13 = (f32[128,384]{1,0:T(8,128)S(1)}, f32[128,384]{1,0:T(8,128)S(1)}, u32[]{:S(2)}, u32[]{:S(2)}) collective-permute-start(f32[128,384]{1,0:T(8,128)S(1)} %slice_add_fusion.4), channel_id=1, source_target_pairs={{0,2},{1,3},{2,0},{3,1},{4,6},{5,7},{6,4},{7,5},{8,10},{9,11},{10,... | collective-permute-start | bytes 589832 | tf_op jit(solution)/shard_map/ppermute | solution.py:123
  56.4 42.8 %collective-permute-start.23 = (f32[768,384]{1,0:T(8,128)S(1)}, f32[768,384]{1,0:T(8,128)S(1)}, u32[]{:S(2)}, u32[]{:S(2)}) collective-permute-start(f32[768,384]{1,0:T(8,128)S(1)} %broadcast_select_fusion), channel_id=1, source_target_pairs={{8,0},{16,24},{0,16},{24,8},{9,1},{17,25},{1,17},{25,9},{10,2},{18... | collective-permute-start | bytes 3538952 | tf_op jit(solution)/shard_map/ppermute | solution.py:111
  62.5 14.0 %collective-permute-start.15 = (f32[256,384]{1,0:T(8,128)S(1)}, f32[256,384]{1,0:T(8,128)S(1)}, u32[]{:S(2)}, u32[]{:S(2)}) collective-permute-start(f32[256,384]{1,0:T(8,128)S(1)} %get-tuple-element.60), channel_id=1, source_target_pairs={{0,2},{1,3},{2,0},{3,1},{4,6},{5,7},{6,4},{7,5},{8,10},{9,11},{10,... | collective-permute-start | bytes 1179656 | tf_op jit(solution)/shard_map/ppermute | solution.py:123
  64.0 12.5 %collective-permute-start.16 = (f32[256,384]{1,0:T(8,128)S(1)}, f32[256,384]{1,0:T(8,128)S(1)}, u32[]{:S(2)}, u32[]{:S(2)}) collective-permute-start(f32[256,384]{1,0:T(8,128)S(1)} %get-tuple-element.61), channel_id=1, source_target_pairs={{0,4},{1,5},{2,6},{3,7},{4,0},{5,1},{6,2},{7,3},{8,12},{9,13},{10,... | collective-permute-start | bytes 1179656 | tf_op jit(solution)/shard_map/ppermute | solution.py:123
  65.5 13.1 %collective-permute-start.14 = (f32[128,384]{1,0:T(8,128)S(1)}, f32[128,384]{1,0:T(8,128)S(1)}, u32[]{:S(2)}, u32[]{:S(2)}) collective-permute-start(f32[128,384]{1,0:T(8,128)S(1)} %fusion.3), channel_id=1, source_target_pairs={{0,1},{1,0},{2,3},{3,2},{4,5},{5,4},{6,7},{7,6},{8,9},{9,8},{10,11... | collective-permute-start | bytes 589832 | tf_op jit(solution)/shard_map/ppermute | solution.py:123
  76.5 5.7 %collective-permute-start.18 = (f32[128,384]{1,0:T(8,128)S(1)}, f32[128,384]{1,0:T(8,128)S(1)}, u32[]{:S(2)}, u32[]{:S(2)}) collective-permute-start(f32[128,384]{1,0:T(8,128)S(1)} %slice_add_fusion.11), channel_id=1, source_target_pairs={{0,4},{1,5},{2,6},{3,7},{4,0},{5,1},{6,2},{7,3},{8,12},{9,13},{10,... | collective-permute-start | bytes 589832 | tf_op jit(solution)/shard_map/ppermute | solution.py:123
  77.1 5.7 %collective-permute-start.19 = (f32[128,384]{1,0:T(8,128)S(1)}, f32[128,384]{1,0:T(8,128)S(1)}, u32[]{:S(2)}, u32[]{:S(2)}) collective-permute-start(f32[128,384]{1,0:T(8,128)S(1)} %slice_add_fusion.10), channel_id=1, source_target_pairs={{0,2},{1,3},{2,0},{3,1},{4,6},{5,7},{6,4},{7,5},{8,10},{9,11},{10,... | collective-permute-start | bytes 589832 | tf_op jit(solution)/shard_map/ppermute | solution.py:123
  84.3 15.0 %collective-permute-start.21 = (f32[256,384]{1,0:T(8,128)S(1)}, f32[256,384]{1,0:T(8,128)S(1)}, u32[]{:S(2)}, u32[]{:S(2)}) collective-permute-start(f32[256,384]{1,0:T(8,128)S(1)} %get-tuple-element.70), channel_id=1, source_target_pairs={{0,2},{1,3},{2,0},{3,1},{4,6},{5,7},{6,4},{7,5},{8,10},{9,11},{10,... | collective-permute-start | bytes 1179656 | tf_op jit(solution)/shard_map/ppermute | solution.py:123
  84.7 14.6 %collective-permute-start.22 = (f32[256,384]{1,0:T(8,128)S(1)}, f32[256,384]{1,0:T(8,128)S(1)}, u32[]{:S(2)}, u32[]{:S(2)}) collective-permute-start(f32[256,384]{1,0:T(8,128)S(1)} %get-tuple-element.71), channel_id=1, source_target_pairs={{0,4},{1,5},{2,6},{3,7},{4,0},{5,1},{6,2},{7,3},{8,12},{9,13},{10,... | collective-permute-start | bytes 1179656 | tf_op jit(solution)/shard_map/ppermute | solution.py:123
  86.4 2.5 %collective-permute-start.20 = (f32[128,384]{1,0:T(8,128)S(1)}, f32[128,384]{1,0:T(8,128)S(1)}, u32[]{:S(2)}, u32[]{:S(2)}) collective-permute-start(f32[128,384]{1,0:T(8,128)S(1)} %add_add_fusion.1), channel_id=1, source_target_pairs={{0,1},{1,0},{2,3},{3,2},{4,5},{5,4},{6,7},{7,6},{8,9},{9,8},{10,11... | collective-permute-start | bytes 589832 | tf_op jit(solution)/shard_map/ppermute | solution.py:123
  99.3 8.1 %collective-permute-start.25 = (f32[128,384]{1,0:T(8,128)S(1)}, f32[128,384]{1,0:T(8,128)S(1)}, u32[]{:S(2)}, u32[]{:S(2)}) collective-permute-start(f32[128,384]{1,0:T(8,128)S(1)} %slice_add_fusion.8), channel_id=1, source_target_pairs={{0,2},{1,3},{2,0},{3,1},{4,6},{5,7},{6,4},{7,5},{8,10},{9,11},{10,... | collective-permute-start | bytes 589832 | tf_op jit(solution)/shard_map/ppermute | solution.py:123
  99.9 7.9 %collective-permute-start.24 = (f32[128,384]{1,0:T(8,128)S(1)}, f32[128,384]{1,0:T(8,128)S(1)}, u32[]{:S(2)}, u32[]{:S(2)}) collective-permute-start(f32[128,384]{1,0:T(8,128)S(1)} %slice_add_fusion.9), channel_id=1, source_target_pairs={{0,4},{1,5},{2,6},{3,7},{4,0},{5,1},{6,2},{7,3},{8,12},{9,13},{10,... | collective-permute-start | bytes 589832 | tf_op jit(solution)/shard_map/ppermute | solution.py:123
  101.9 14.6 %collective-permute-start.27 = (f32[256,384]{1,0:T(8,128)S(1)}, f32[256,384]{1,0:T(8,128)S(1)}, u32[]{:S(2)}, u32[]{:S(2)}) collective-permute-start(f32[256,384]{1,0:T(8,128)S(1)} %get-tuple-element.78), channel_id=1, source_target_pairs={{0,2},{1,3},{2,0},{3,1},{4,6},{5,7},{6,4},{7,5},{8,10},{9,11},{10,... | collective-permute-start | bytes 1179656 | tf_op jit(solution)/shard_map/ppermute | solution.py:123
  103.4 11.5 %collective-permute-start.29 = (f32[256,384]{1,0:T(8,128)S(1)}, f32[256,384]{1,0:T(8,128)S(1)}, u32[]{:S(2)}, u32[]{:S(2)}) collective-permute-start(f32[256,384]{1,0:T(8,128)S(1)} %get-tuple-element.79), channel_id=1, source_target_pairs={{0,4},{1,5},{2,6},{3,7},{4,0},{5,1},{6,2},{7,3},{8,12},{9,13},{10,... | collective-permute-start | bytes 1179656 | tf_op jit(solution)/shard_map/ppermute | solution.py:123
  107.4 9.7 %collective-permute-start.26 = (f32[128,384]{1,0:T(8,128)S(1)}, f32[128,384]{1,0:T(8,128)S(1)}, u32[]{:S(2)}, u32[]{:S(2)}) collective-permute-start(f32[128,384]{1,0:T(8,128)S(1)} %add_add_fusion), channel_id=1, source_target_pairs={{0,1},{1,0},{2,3},{3,2},{4,5},{5,4},{6,7},{7,6},{8,9},{9,8},{10,11... | collective-permute-start | bytes 589832 | tf_op jit(solution)/shard_map/ppermute | solution.py:123
  115.0 5.7 %collective-permute-start.30 = (f32[128,384]{1,0:T(8,128)S(1)}, f32[128,384]{1,0:T(8,128)S(1)}, u32[]{:S(2)}, u32[]{:S(2)}) collective-permute-start(f32[128,384]{1,0:T(8,128)S(1)} %slice_add_fusion), channel_id=1, source_target_pairs={{0,2},{1,3},{2,0},{3,1},{4,6},{5,7},{6,4},{7,5},{8,10},{9,11},{10,... | collective-permute-start | bytes 589832 | tf_op jit(solution)/shard_map/ppermute | solution.py:123
  116.5 5.7 %collective-permute-start.28 = (f32[128,384]{1,0:T(8,128)S(1)}, f32[128,384]{1,0:T(8,128)S(1)}, u32[]{:S(2)}, u32[]{:S(2)}) collective-permute-start(f32[128,384]{1,0:T(8,128)S(1)} %slice_add_fusion.2), channel_id=1, source_target_pairs={{0,4},{1,5},{2,6},{3,7},{4,0},{5,1},{6,2},{7,3},{8,12},{9,13},{10,... | collective-permute-start | bytes 589832 | tf_op jit(solution)/shard_map/ppermute | solution.py:123
  120.7 1.6 %collective-permute-start.31 = (f32[128,384]{1,0:T(8,128)S(1)}, f32[128,384]{1,0:T(8,128)S(1)}, u32[]{:S(2)}, u32[]{:S(2)}) collective-permute-start(f32[128,384]{1,0:T(8,128)S(1)} %fusion), channel_id=1, source_target_pairs={{0,1},{1,0},{2,3},{3,2},{4,5},{5,4},{6,7},{7,6},{8,9},{9,8},{10,11... | collective-permute-start | bytes 589832 | tf_op jit(solution)/shard_map/ppermute | solution.py:123
  122.3 1.1 copy-start.10

commit v8 on v7

v8 whole, which is shorter than its diff:
```python
import functools

import jax
import jax.numpy as jnp
from jax import lax
from jax.experimental import pallas as pl
from jax.experimental.pallas import tpu as pltpu
from jax.sharding import PartitionSpec as P

TILE_O = 32
TILE_V = 128
VMEM_LIMIT = 12 * 1024 * 1024


def after(value, *earlier):
    return lax.optimization_barrier((value,) + earlier)[0]


def in_vmem(count):
    return [pl.BlockSpec(memory_space=pltpu.VMEM)] * count


def in_hbm(count):
    return [pl.BlockSpec(memory_space=pltpu.HBM)] * count


def kernel_call(body, outs, operands, name, from_hbm=False, scratch=()):
    if from_hbm:
        operands = [pltpu.with_memory_space_constraint(x, pltpu.HBM) for x in operands]
    return pl.pallas_call(
        body,
        out_shape=[pltpu.VMEM(shape, jnp.float32) for shape in outs],
        in_specs=in_hbm(len(operands)) if from_hbm else in_vmem(len(operands)),
        out_specs=in_vmem(len(outs)),
        scratch_shapes=list(scratch),
        compiler_params=pltpu.CompilerParams(vmem_limit_bytes=VMEM_LIMIT),
        cost_estimate=pl.CostEstimate(flops=1, bytes_accessed=1, transcendentals=0),
        name=name,
    )(*operands)


def tiles(start, count):
    return pl.ds(pl.multiple_of(start * TILE_V, TILE_V), count * TILE_V)


def cut_kernel(groups, depth_tiles, mask_hbm, amp_hbm, *refs):
    out_refs, (mask_ref, amp_ref, mask_sem, amp_sems) = refs[:groups], refs[groups:]
    group = lax.axis_index("vir") // 2
    mask_copy = pltpu.make_async_copy(mask_hbm, mask_ref, mask_sem)
    mask_copy.start()
    starts = [(group ^ r) * depth_tiles for r in range(groups)]
    order = range(groups - 1, -1, -1)
    copies = {
        r: pltpu.make_async_copy(amp_hbm.at[:, tiles(starts[r], depth_tiles)], amp_ref.at[r], amp_sems.at[r]) for r in order
    }
    for r in order:
        copies[r].start()
    mask_copy.wait()
    for r in order:
        copies[r].wait()
        for t in range(depth_tiles):
            for o in range(amp_hbm.shape[0] // TILE_O):
                rows = pl.ds(o * TILE_O, TILE_O)
                scale = mask_ref[o, starts[r] + t].astype(jnp.float32)
                out_refs[r][rows, tiles(t, 1)] = amp_ref[r, rows, tiles(t, 1)] * scale


def cut(mask, amplitudes, groups, depth):
    rows = amplitudes.shape[0]
    scratch = [
        pltpu.SMEM(mask.shape, jnp.int32),
        pltpu.VMEM((groups, rows, depth), jnp.float32),
        pltpu.SemaphoreType.DMA,
        pltpu.SemaphoreType.DMA((groups,)),
    ]
    body = functools.partial(cut_kernel, groups, depth // TILE_V)
    return kernel_call(body, [(rows, depth)] * groups, [mask, amplitudes], "cut", True, scratch)


def halves_kernel(mask_hbm, int_hbm, mine_ref, theirs_ref, mask_ref, int_ref, mask_sem, int_sems):
    low = lax.axis_index("vir") % 2
    count = mine_ref.shape[1] // TILE_V
    mask_copy = pltpu.make_async_copy(mask_hbm, mask_ref, mask_sem)
    mask_copy.start()
    work = ((1 - low, theirs_ref), (low, mine_ref))
    copies = [
        pltpu.make_async_copy(int_hbm.at[:, tiles(half * count, count)], int_ref.at[i], int_sems.at[i])
        for i, (half, _) in enumerate(work)
    ]
    for copy in copies:
        copy.start()
    mask_copy.wait()
    for i, (half, out_ref) in enumerate(work):
        copies[i].wait()
        for t in range(count):
            for k in range(int_hbm.shape[0] // TILE_V):
                scale = mask_ref[k, half * count + t].astype(jnp.float32)
                out_ref[tiles(k, 1), tiles(t, 1)] = int_ref[i, tiles(k, 1), tiles(t, 1)] * scale


def halves(mask, integrals):
    depth, width = integrals.shape
    scratch = [
        pltpu.SMEM(mask.shape, jnp.int32),
        pltpu.VMEM((2, depth, width // 2), jnp.float32),
        pltpu.SemaphoreType.DMA,
        pltpu.SemaphoreType.DMA((2,)),
    ]
    return kernel_call(halves_kernel, [(depth, width // 2)] * 2, [mask, integrals], "halves", True, scratch)


def join_kernel(mine_ref, other_ref, out_ref):
    low = lax.axis_index("vir") % 2
    depth = mine_ref.shape[0]
    out_ref[pl.ds(pl.multiple_of(low * depth, depth), depth), :] = mine_ref[...]
    out_ref[pl.ds(pl.multiple_of((1 - low) * depth, depth), depth), :] = other_ref[...]


def fold_kernel(rows, stays, goes, held_ref, got_ref, *out_refs):
    for out_ref, places in zip(out_refs, (stays, goes)):
        for i, k in enumerate(places):
            take = pl.ds(k * rows, rows)
            out_ref[i * rows : (i + 1) * rows, :] = held_ref[take, :] + got_ref[take, :]


def fold(rows, stays, goes, held, got):
    outs = [(len(places) * rows, held.shape[1]) for places in (stays, goes) if places]
    return kernel_call(functools.partial(fold_kernel, rows, stays, goes), outs, [held, got], "fold")


def write_kernel(d, half, offset, held_ref, got_ref, other_ref, *refs):
    out_ref, piece_ref, sems = refs[-3:]
    low = lax.axis_index("vir") % 2
    place = lax.axis_index("occ") ^ d
    width = held_ref.shape[1] // TILE_V
    starts = [(2 * place + h) * (half // TILE_V) + offset // TILE_V for h in (low, 1 - low)]
    piece_ref[...] = held_ref[...] + got_ref[...]
    copies = [
        pltpu.make_async_copy(source, out_ref.at[:, tiles(start, width)], sems.at[i])
        for i, (source, start) in enumerate(zip((piece_ref, other_ref), starts))
    ]
    for copy in copies:
        copy.start()
    for copy in copies:
        copy.wait()


def write(out, shape, d, half, offset, held, got, other):
    given = [] if out is None else [out]
    return pl.pallas_call(
        functools.partial(write_kernel, d, half, offset),
        out_shape=jax.ShapeDtypeStruct(shape, jnp.float32),
        in_specs=in_vmem(3) + in_hbm(len(given)),
        out_specs=pl.BlockSpec(memory_space=pltpu.HBM),
        scratch_shapes=[pltpu.VMEM(held.shape, jnp.float32), pltpu.SemaphoreType.DMA((2,))],
        input_output_aliases={3: 0} if given else {},
        compiler_params=pltpu.CompilerParams(vmem_limit_bytes=VMEM_LIMIT),
        cost_estimate=pl.CostEstimate(flops=1, bytes_accessed=1, transcendentals=0),
        name="write",
    )(held, got, other, *given)


def split(x):
    high = x.astype(jnp.bfloat16)
    return high, (x - high.astype(jnp.float32)).astype(jnp.bfloat16)


def dot_kernel(count, *refs):
    left, block_ref, outs = refs[: 2 * count], refs[2 * count], refs[2 * count + 1 :]
    rows = left[0].shape[0]
    b_high, b_low = split(block_ref[...])
    for h in range(2):
        for i in range(count):
            a_high, a_low = split(left[h * count + i][...])
            total = None
            for a, b in ((a_high, b_low), (a_low, b_high), (a_high, b_high)):
                term = jnp.dot(a, b, preferred_element_type=jnp.float32)
                total = term if total is None else total + term
            outs[h][i * rows : (i + 1) * rows, :] = total


def products(left, block):
    count = len(left[0])
    shape = (count * left[0][0].shape[0], block.shape[1])
    return kernel_call(functools.partial(dot_kernel, count), [shape] * 2, [*left[0], *left[1], block], "products")


def line_blocks(own, nodes):
    here = lax.axis_index("occ")

    def direct(x, d):
        return lax.ppermute(x, "occ", [(i, i ^ d) for i in range(nodes)])

    if nodes != 4:
        return [(d, own if d == 0 else direct(own, d), 0) for d in range(nodes)]
    near = direct(own, 1)
    centre = lax.ppermute(own, "occ", [(1, 2), (2, 1)])
    far = lax.ppermute(own, "occ", [(0, 3), (3, 0)])
    middle = (here == 1) | (here == 2)
    count = own.shape[1] // TILE_V
    cuts = [0, (2 * count + 2) // 3 * TILE_V, own.shape[1]]
    last = []
    for lo, hi in zip(cuts, cuts[1:]):
        moving = jnp.where(middle, centre[:, lo:hi], own[:, lo:hi])
        last.append((2, lax.ppermute(moving, "occ", [(1, 0), (2, 3), (0, 2), (3, 1)]), lo))
    return [(0, own, 0), (1, near, 0), (3, (middle, centre, far), 0), *last]


def per_device(sizes, amplitudes, amp_mask, integrals, int_mask):
    n_occ, n_vir = sizes
    rows = amplitudes.shape[0]
    groups = n_vir // 2
    own_depth, width = integrals.shape
    depth, half = 2 * own_depth, width // 2

    def swap(x, bits):
        return lax.ppermute(x, "vir", [(i, i ^ bits) for i in range(n_vir)])

    mine, theirs = halves(int_mask, integrals)
    other = swap(theirs, 1)
    parts = cut(after(amp_mask, mine), amplitudes, groups, depth)
    (whole,) = kernel_call(join_kernel, [(depth, half)], [mine, after(other, *parts)], "join")
    blocks = line_blocks(whole, n_occ)
    arrived = [block[2] if isinstance(block, tuple) else block for _, block, _ in blocks]

    rel = [[parts[0]] + [None] * (groups - 1), [None] * groups]
    for r in range(groups - 1, 0, -1):
        rel[0][r] = swap(parts[r], 2 * r)
    for r in range(groups - 1, -1, -1):
        rel[1][r] = swap(rel[0][r] if r else after(parts[0], rel[0][groups - 1]), 1)

    bits = []
    while (1 << len(bits)) < groups:
        bits.append(1 << len(bits))
    orders = [bits, bits[::-1]]
    away = [[r for r in range(groups) if r & o[0]] for o in orders]
    near = [[r for r in range(groups) if not r & o[0]] for o in orders]

    out = None
    token = None
    for n, (d, block, offset) in enumerate(blocks):
        if isinstance(block, tuple):
            middle, centre, far = block
            centre, far = lax.optimization_barrier((centre, far, *sent))[:2]
            block = jnp.where(middle, centre, far)
        if n == 0:
            block = after(block, blocks[1][1], *(blocks[2][1][1:2] if isinstance(blocks[2][1], tuple) else ()))
        else:
            block = after(block, *token)
        sent = products([[rel[h][r] for r in away[h]] for h in range(2)], block)
        moving = [swap(sent[h], 2 * orders[h][0]) for h in range(2)]
        soon = arrived[n + 1 : n + 2] if n > 0 else []
        held = list(products([[rel[h][r] for r in near[h]] for h in range(2)], after(block, *sent, *soon)))
        names = [near[0], near[1]]
        for level in range(1, len(bits)):
            for h in (1, 0):
                bit = orders[h][level]
                stays = [i for i, r in enumerate(names[h]) if not r & bit]
                goes = [i for i, r in enumerate(names[h]) if r & bit]
                held[h], moved = fold(rows, stays, goes, held[h], moving[h])
                moving[h] = swap(moved, 2 * bit)
                names[h] = [names[h][i] for i in stays]
        token = held if out is None else [*held, out]
        (theirs,) = fold(rows, [0], [], held[1], moving[1])
        out = write(out, (rows, n_occ * width), d, half, offset, held[0], moving[0], swap(theirs, 1))
    return out


def solution(mesh):
    sizes = (mesh.shape["occ"], mesh.shape["vir"])

    def run(*args):
        return per_device(sizes, *args)

    in_specs = (P(("occ", "vir"), None), P(("occ", "vir"), None), P("vir", "occ"), P("vir", "occ"))
    out_specs = P(("occ", "vir"), None)
    return jax.shard_map(run, mesh=mesh, in_specs=in_specs, out_specs=out_specs, check_vma=False)
```

time: 125 us -> 138 us (1.10)
  starting transfers between devices: 35.6 us -> 69.2 us
  waiting for transfers between devices: 57 us -> 42.1 us
  local copies, waits for them, and re-layouts: 7.09 us -> 3.11 us
  other arithmetic: 5.78 us -> 2.65 us
  Pallas kernels: 18.2 us -> 20.5 us
    ppermute x1 -> x2, starting transfers between devices: 3.86 us -> 33.7 us  [line_blocks(): lax.ppermute(moving, 'occ', [(1, 0), (2, 3), (0, 2), (3, 1)])]
    ppermute x1 -> x2, waiting for transfers between devices: 10.2 us -> 2.71 us  [line_blocks(): lax.ppermute(moving, 'occ', [(1, 0), (2, 3), (0, 2), (3, 1)])]
    ppermute x1, waiting for transfers between devices: 7.06 us -> 0.01 us  [line_blocks(): far = lax.ppermute(own, 'occ', [(0, 3), (3, 0)])]
    ppermute x28 -> x33, starting transfers between devices: 22.9 us -> 27.4 us  [swap(): return lax.ppermute(x, 'vir', [(i, i ^ bits) for i in range(n_vir)])]
    ppermute x1, waiting for transfers between devices: 4.93 us -> 0.56 us  [direct(): return lax.ppermute(x, 'occ', [(i, i ^ d) for i in range(nodes)])]
    ppermute x28 -> x33, waiting for transfers between devices: 34.8 us -> 38.8 us  [swap(): return lax.ppermute(x, 'vir', [(i, i ^ bits) for i in range(n_vir)])]
    add x12 -> x0, other arithmetic: 3.11 us -> none  [per_device(): held[h][r] = held[h][r] + moving[h][i * rows:(i + 1) * rows]]
    unnamed x22 -> x32, local copies, waits for them, and re-layouts: 6.2 us -> 3.11 us
  transfers between devices with their start and end apart: 32 -> 38, of which waited for: 13 -> 15; matrix products, arithmetic and copies ran while one was open for 5% -> 2% of each run, Pallas kernels for 14% -> 13%
where the time goes in v8:
time: 138 us
  starting transfers between devices  69.2 us (50%)
  waiting for transfers between devices  42.1 us (31%)
  Pallas kernels  20.5 us (15%)
  local copies, waits for them, and re-layouts  3.11 us (2%)
  other arithmetic  2.65 us (2%)
    ppermute x33, waiting for transfers between devices, swap(): return lax.ppermute(x, 'vir', [(i, i ^ bits) for i in range(n_vir)])  38.8 us
    ppermute x2, starting transfers between devices, line_blocks(): lax.ppermute(moving, 'occ', [(1, 0), (2, 3), (0, 2), (3, 1)])  33.7 us
    ppermute x33, starting transfers between devices, swap(): return lax.ppermute(x, 'vir', [(i, i ^ bits) for i in range(n_vir)])  27.4 us
    pallas_call x28, Pallas kernels, kernel_call(): pl.pallas_call(body, out_shape=[pltpu.VMEM(shape, jnp.float32) for shape...  16.7 us
    ppermute x1, starting transfers between devices, line_blocks(): far = lax.ppermute(own, 'occ', [(0, 3), (3, 0)])  4.37 us
    pallas_call x5, Pallas kernels, write(): pl.pallas_call(functools.partial(write_kernel, d, half, offset), out_shap...  3.76 us
    unnamed x32, local copies, waits for them, and re-layouts  3.11 us
    ppermute x1, starting transfers between devices, direct(): return lax.ppermute(x, 'occ', [(i, i ^ d) for i in range(nodes)])  3.01 us
  transfers between devices with their start and end apart: 38, of which 15 were waited for; matrix products, arithmetic and copies ran while one was open for 2% of the time, Pallas kernels for 13%

profile of v8, /device:TPU:0, one launch (start us, length us, event | category | flops | bytes accessed | tf_op | source)
XLA Modules:
  0.0 138.1 jit_solution(15321623528373946529)
XLA Ops:
  0.0 1.3 halves.1
  1.3 0.5 collective-permute-start.5
  1.8 1.4 %cut.1 = (f32[128,768]{1,0:T(8,128)S(1)}, f32[128,768]{1,0:T(8,128)S(1)}, f32[128,768]{1,0:T(8,128)S(1)}, f32[128,768]{1,0:T(8,128)S(1)}) custom-call(s32[4,24]{1,0:T(4,128)} %mask_hbm.2, f32[128,3072]{1,0:T(8,128)} %amp_hbm.1), custom_call_target="tpu_custom_call" | custom-call | flops 1 | bytes 1 | tf_op jit(solution)/shard_map/cut/pallas_call | solution.py:30
  3.6 3.0 %collective-permute-start.12 = (f32[768,384]{1,0:T(8,128)S(1)}, f32[768,384]{1,0:T(8,128)S(1)}, u32[]{:S(2)}, u32[]{:S(2)}) collective-permute-start(f32[768,384]{1,0:T(8,128)S(1)} %join.1.refs_4_), channel_id=1, source_target_pairs={{0,8},{8,0},{16,24},{24,16},{1,9},{9,1},{17,25},{25,17},{2,10},{10... | collective-permute-start | bytes 3538952 | tf_op jit(solution)/shard_map/ppermute | solution.py:192
  6.6 0.7 collective-permute-start.6
  7.3 1.6 %collective-permute-start = (f32[128,768]{1,0:T(8,128)S(1)}, f32[128,768]{1,0:T(8,128)S(1)}, u32[]{:S(2)}, u32[]{:S(2)}) collective-permute-start(f32[128,768]{1,0:T(8,128)S(1)} %get-tuple-element.69), channel_id=1, source_target_pairs={{0,4},{1,5},{2,6},{3,7},{4,0},{5,1},{6,2},{7,3},{8,12},{9,13},{10,... | collective-permute-start | bytes 1179656 | tf_op jit(solution)/shard_map/ppermute | solution.py:217
  8.9 1.4 %collective-permute-start.1 = (f32[128,768]{1,0:T(8,128)S(1)}, f32[128,768]{1,0:T(8,128)S(1)}, u32[]{:S(2)}, u32[]{:S(2)}) collective-permute-start(f32[128,768]{1,0:T(8,128)S(1)} %get-tuple-element.70), channel_id=1, source_target_pairs={{0,6},{1,7},{2,4},{3,5},{4,2},{5,3},{6,0},{7,1},{8,14},{9,15},{10,... | collective-permute-start | bytes 1179656 | tf_op jit(solution)/shard_map/ppermute | solution.py:217
  10.3 0.5 collective-permute-start.3
  10.9 15.8 %collective-permute-done.refs_1_ = f32[128,768]{1,0:T(8,128)S(1)} collective-permute-done((f32[128,768]{1,0:T(8,128)S(1)}, f32[128,768]{1,0:T(8,128)S(1)}, u32[]{:S(2)}, u32[]{:S(2)}) %collective-permute-start) | collective-permute-done | bytes 393248 | tf_op jit(solution)/shard_map/ppermute | solution.py:217
  27.2 0.7 collective-permute-done.3.refs_0_
  27.9 4.4 %collective-permute-start.9 = (f32[768,384]{1,0:T(8,128)S(1)}, f32[768,384]{1,0:T(8,128)}, u32[]{:S(2)}, u32[]{:S(2)}) collective-permute-start(f32[768,384]{1,0:T(8,128)S(1)} %join.1.refs_4_), channel_id=1, source_target_pairs={{0,24},{24,0},{1,25},{25,1},{2,26},{26,2},{3,27},{27,3},{4,28},{28... | collective-permute-start | bytes 3538952 | tf_op jit(solution)/shard_map/ppermute | solution.py:198
  32.3 0.6 collective-permute-done.12.refs_4_
  33.4 0.5 copy-done.14
  33.9 1.4 %products.10 = (f32[256,384]{1,0:T(8,128)S(1)}, f32[256,384]{1,0:T(8,128)S(1)}) custom-call(f32[128,768]{1,0:T(8,128)S(1)} %collective-permute-done.3.refs_0_, f32[128,768]{1,0:T(8,128)S(1)} %collective-permute-done.1.refs_1_, f32[128,768]{1,0:T(8,128)S(1)} %collective-permute-done.10.refs_2_, f32[128,768]{1,0:T(8,128)S(1)} %collective-permute-done.11.refs_3_, ...), custom_call_target="tpu_custom_call" | custom-call | flops 1 | bytes 1 | tf_op jit(solution)/shard_map/products/pallas_call | solution.py:30
  35.3 1.7 %collective-permute-start.13 = (f32[256,384]{1,0:T(8,128)S(1)}, f32[256,384]{1,0:T(8,128)S(1)}, u32[]{:S(2)}, u32[]{:S(2)}) collective-permute-start(f32[256,384]{1,0:T(8,128)S(1)} %get-tuple-element.76), channel_id=1, source_target_pairs={{0,2},{1,3},{2,0},{3,1},{4,6},{5,7},{6,4},{7,5},{8,10},{9,11},{10,... | collective-permute-start | bytes 1179656 | tf_op jit(solution)/shard_map/ppermute | solution.py:217
  37.0 1.5 %collective-permute-start.14 = (f32[256,384]{1,0:T(8,128)S(1)}, f32[256,384]{1,0:T(8,128)S(1)}, u32[]{:S(2)}, u32[]{:S(2)}) collective-permute-start(f32[256,384]{1,0:T(8,128)S(1)} %get-tuple-element.77), channel_id=1, source_target_pairs={{0,4},{1,5},{2,6},{3,7},{4,0},{5,1},{6,2},{7,3},{8,12},{9,13},{10,... | collective-permute-start | bytes 1179656 | tf_op jit(solution)/shard_map/ppermute | solution.py:217
  38.6 1.4 %products.11 = (f32[256,384]{1,0:T(8,128)S(1)}, f32[256,384]{1,0:T(8,128)S(1)}) custom-call(f32[128,768]{1,0:T(8,128)S(1)} %get-tuple-element.71.refs_0_, f32[128,768]{1,0:T(8,128)S(1)} %collective-permute-done.refs_1_, f32[128,768]{1,0:T(8,128)S(1)} %collective-permute-done.2.refs_2_, f32[128,768]{1,0:T(8,128)S(1)} %collective-permute-done.4.refs_3_, ...), custom_call_target="tpu_custom_call" | custom-call | flops 1 | bytes 1 | tf_op jit(solution)/shard_map/products/pallas_call | solution.py:30
  40.0 6.9 %collective-permute-done.13.got_ref = f32[256,384]{1,0:T(8,128)S(1)} collective-permute-done((f32[256,384]{1,0:T(8,128)S(1)}, f32[256,384]{1,0:T(8,128)S(1)}, u32[]{:S(2)}, u32[]{:S(2)}) %collective-permute-start.13) | collective-permute-done | bytes 393248 | tf_op jit(solution)/shard_map/ppermute | solution.py:217
  46.9 0.7 copy-done.6
  47.6 0.6 collective-permute-done.14.got_ref
  48.3 0.7 copy-done.13
  49.0 2.2 %products.12 = (f32[256,384]{1,0:T(8,128)S(1)}, f32[256,384]{1,0:T(8,128)}) custom-call(f32[128,768]{1,0:T(8,128)S(1)} %collective-permute-done.3.refs_0_, f32[128,768]{1,0:T(8,128)S(1)} %collective-permute-done.1.refs_1_, f32[128,768]{1,0:T(8,128)S(1)} %collective-permute-done.10.refs_2_, f32[128,768]{1,0:T(8,128)S(1)} %collective-permute-done.11.refs_3_, ...), custom_call_target="tpu_custom_call" | custom-call | flops 1 | bytes 1 | tf_op jit(solution)/shard_map/products/pallas_call | solution.py:30
  51.1 0.8 copy-done.10
  51.9 1.5 %collective-permute-start.16 = (f32[256,384]{1,0:T(8,128)}, f32[256,384]{1,0:T(8,128)}, u32[]{:S(2)}, u32[]{:S(2)}) collective-permute-start(f32[256,384]{1,0:T(8,128)} %get-tuple-element.85), channel_id=1, source_target_pairs={{0,4},{1,5},{2,6},{3,7},{4,0},{5,1},{6,2},{7,3},{8,12},{9,13},{10,... | collective-permute-start | bytes 1179656 | tf_op jit(solution)/shard_map/ppermute | solution.py:217
  53.4 1.0 collective-permute-start.18
  54.5 1.0 collective-permute-start.15
  55.4 1.2 slice_select_fusion
  56.7 30.1 %collective-permute-start.8 = (f32[768,256]{1,0:T(8,128)S(1)}, f32[768,256]{1,0:T(8,128)S(1)}, u32[]{:S(2)}, u32[]{:S(2)}) collective-permute-start(f32[768,256]{1,0:T(8,128)S(1)} %slice_select_fusion), channel_id=1, source_target_pairs={{8,0},{16,24},{0,16},{24,8},{9,1},{17,25},{1,17},{25,9},{10,2},{18... | collective-permute-start | bytes 2359304 | tf_op jit(solution)/shard_map/ppermute | solution.py:205
  86.8 0.6 collective-permute-start.17
  87.3 1.4 %products.13 = (f32[256,384]{1,0:T(8,128)S(1)}, f32[256,384]{1,0:T(8,128)S(1)}) custom-call(f32[128,768]{1,0:T(8,128)S(1)} %get-tuple-element.71.refs_0_, f32[128,768]{1,0:T(8,128)S(1)} %collective-permute-done.refs_1_, f32[128,768]{1,0:T(8,128)S(1)} %collective-permute-done.2.refs_2_, f32[128,768]{1,0:T(8,128)S(1)} %collective-permute-done.4.refs_3_, ...), custom_call_target="tpu_custom_call" | custom-call | flops 1 | bytes 1 | tf_op jit(solution)/shard_map/products/pallas_call | solution.py:30
  88.9 1.1 fold.18
  90.0 1.1 collective-permute-start.23
  91.1 1.4 %broadcast_select_fusion.refs_4_ = f32[768,384]{1,0:T(8,128)S(1)} fusion(f32[768,384]{1,0:T(8,128)S(1)} %copy-done.15, f32[768,384]{1,0:T(8,128)} %collective-permute-done.9, pred[]{:T(512)S(6)} %or.3), kind=kLoop, calls=%fused_computation.1 | loop fusion | flops 294912 | bytes 3538945 | tf_op jit(solution)/shard_map/jit(_where)/select_n | solution.py:245
  92.6 0.8 write.5.refs_0_
  93.8 1.4 %products.14 = (f32[256,384]{1,0:T(8,128)S(1)}, f32[256,384]{1,0:T(8,128)S(1)}) custom-call(f32[128,768]{1,0:T(8,128)S(1)} %collective-permute-done.3.refs_0_, f32[128,768]{1,0:T(8,128)S(1)} %collective-permute-done.1.refs_1_, f32[128,768]{1,0:T(8,128)S(1)} %copy-done.1, f32[128,768]{1,0:T(8,128)S(1)} %copy-done.3, f32[768,384]{1,0:T(8,128)S(1)} %broadcast_select_fusion.refs_4_), custom_call_target="tpu_custom_call" | custom-call | flops 1 | bytes 1 | tf_op jit(solution)/shard_map/products/pallas_call | solution.py:30
  95.3 1.6 %collective-permute-start.21 = (f32[256,384]{1,0:T(8,128)S(1)}, f32[256,384]{1,0:T(8,128)S(1)}, u32[]{:S(2)}, u32[]{:S(2)}) collective-permute-start(f32[256,384]{1,0:T(8,128)S(1)} %get-tuple-element.97), channel_id=1, source_target_pairs={{0,4},{1,5},{2,6},{3,7},{4,0},{5,1},{6,2},{7,3},{8,12},{9,13},{10,... | collective-permute-start | bytes 1179656 | tf_op jit(solution)/shard_map/ppermute | solution.py:217
  96.9 1.0 collective-permute-start.20
  97.9 0.5 collective-permute-start.22
  98.5 2.7 %collective-permute-done.8.refs_4_ = f32[768,256]{1,0:T(8,128)S(1)} collective-permute-done((f32[768,256]{1,0:T(8,128)S(1)}, f32[768,256]{1,0:T(8,128)S(1)}, u32[]{:S(2)}, u32[]{:S(2)}) %collective-permute-start.8) | collective-permute-done | bytes 786464 | tf_op jit(solution)/shard_map/ppermute | solution.py:205
  101.2 3.6 %collective-permute-start.7 = (f32[768,128]{1,0:T(8,128)S(1)}, f32[768,128]{1,0:T(8,128)S(1)}, u32[]{:S(2)}, u32[]{:S(2)}) collective-permute-start(f32[768,128]{1,0:T(8,128)S(1)} %slice_select_fusion.1), channel_id=1, source_target_pairs={{8,0},{16,24},{0,16},{24,8},{9,1},{17,25},{1,17},{25,9},{10,2},{18... | collective-permute-start | bytes 1179656 | tf_op jit(solution)/shard_map/ppermute | solution.py:205
  104.8 1.4 %products.15 = (f32[256,384]{1,0:T(8,128)S(1)}, f32[256,384]{1,0:T(8,128)S(1)}) custom-call(f32[128,768]{1,0:T(8,128)S(1)} %get-tuple-element.71.refs_0_, f32[128,768]{1,0:T(8,128)S(1)} %collective-permute-done.refs_1_, f32[128,768]{1,0:T(8,128)S(1)} %collective-permute-done.2.refs_2_, f32[128,768]{1,0:T(8,128)S(1)} %collective-permute-done.4.refs_3_, ...), custom_call_target="tpu_custom_call" | custom-call | flops 1 | bytes 1 | tf_op jit(solution)/shard_map/products/pallas_call | solution.py:30
  106.2 1.1 collective-permute-done.21.got_ref
  107.3 1.1 collective-permute-start.28
  108.5 2.3 %collective-permute-done.22.got_ref = f32[128,384]{1,0:T(8,128)S(1)} collective-permute-done((f32[128,384]{1,0:T(8,128)S(1)}, f32[128,384]{1,0:T(8,128)S(1)}, u32[]{:S(2)}, u32[]{:S(2)}) %collective-permute-start.22) | collective-permute-done | bytes 196640 | tf_op jit(solution)/shard_map/ppermute | solution.py:217
  110.7 0.8 write.6.refs_0_
  111.5 0.8 products.16
  112.3 1.6 %collective-permute-start.26 = (f32[256,256]{1,0:T(8,128)S(1)}, f32[256,256]{1,0:T(8,128)S(1)}, u32[]{:S(2)}, u32[]{:S(2)}) collective-permute-start(f32[256,256]{1,0:T(8,128)S(1)} %get-tuple-element.107), channel_id=1, source_target_pairs={{0,4},{1,5},{2,6},{3,7},{4,0},{5,1},{6,2},{7,3},{8,12},{9,13},{10,... | collective-permute-start | bytes 786440 | tf_op jit(solution)/shard_map/ppermute | solution.py:217
  113.9 1.0 collective-permute-start.25
  115.6 0.8 products.17
  116.4 5.3 %collective-permute-done.26.got_ref = f32[256,256]{1,0:T(8,128)S(1)} collective-permute-done((f32[256,256]{1,0:T(8,128)S(1)}, f32[256,256]{1,0:T(8,128)S(1)}, u32[]{:S(2)}, u32[]{:S(2)}) %collective-permute-start.26) | collective-permute-done | bytes 262176 | tf_op jit(solution)/shard_map/ppermute | solution.py:217
  121.7 1.1 collective-permute-start.36
  122.8 1.4 collective-permute-done.27.got_ref
  124.2 0.8 write.7.refs_0_
  125.0 0.8 products.18
  125.7 1.6 %collective-permute-start.32 = (f32[256,128]{1,0:T(8,128)S(1)}, f32[256,128]{1,0:T(8,128)S(1)}, u32[]{:S(2)}, u32[]{:S(2)}) collective-permute-start(f32[256,128]{1,0:T(8,128)S(1)} %get-tuple-element.117), channel_id=1, source_target_pairs={{0,4},{1,5},{2,6},{3,7},{4,0},{5,1},{6,2},{7,3},{8,12},{9,13},{10,... | collective-permute-start | bytes 393224 | tf_op jit(solution)/shard_map/ppermute | solution.py:217
  127.3 1.0 collective-permute-start.30
  128.3 0.5 collective-permute-start.35
  129.0 0.8 products.19
  129.7 1.8 %collective-permute-done.32.got_ref = f32[256,128]{1,0:T(8,128)S(1)} collective-permute-done((f32[256,128]{1,0:T(8,128)S(1)}, f32[256,128]{1,0:T(8,128)S(1)}, u32[]{:S(2)}, u32[]{:S(2)}) %collective-permute-start.32) | collective-permute-done | bytes 131104 | tf_op jit(solution)/shard_map/ppermute | solution.py:217
  131.6 1.1 collective-permute-start.33
  132.7 1.0 collective-permute-start.31
  133.7 2.2 %collective-permute-done.33.got_ref = f32[128,128]{1,0:T(8,128)S(1)} collective-permute-done((f32[128,128]{1,0:T(8,128)S(1)}, f32[128,128]{1,0:T(8,128)S(1)}, u32[]{:S(2)}, u32[]{:S(2)}) %collective-permute-start.33) | collective-permute-done | bytes 65568 | tf_op jit(solution)/shard_map/ppermute | solution.py:217
  136.0 0.7 write.8.refs_0_
  137.3 0.7 write.9
  (80 shorter events, 3.6 us)
Async XLA Ops:
  1.3 2.1 %collective-permute-start.5 = (f32[384,384]{1,0:T(8,128)S(1)}, f32[384,384]{1,0:T(8,128)S(1)}, u32[]{:S(2)}, u32[]{:S(2)}) collective-permute-start(f32[384,384]{1,0:T(8,128)S(1)} %get-tuple-element.73), channel_id=1, source_target_pairs={{0,1},{1,0},{2,3},{3,2},{4,5},{5,4},{6,7},{7,6},{8,9},{9,8},{10,11... | collective-permute-start | bytes 1769480 | tf_op jit(solution)/shard_map/ppermute | solution.py:217
  3.6 29.3 %collective-permute-start.12 = (f32[768,384]{1,0:T(8,128)S(1)}, f32[768,384]{1,0:T(8,128)S(1)}, u32[]{:S(2)}, u32[]{:S(2)}) collective-permute-start(f32[768,384]{1,0:T(8,128)S(1)} %join.1.refs_4_), channel_id=1, source_target_pairs={{0,8},{8,0},{16,24},{24,16},{1,9},{9,1},{17,25},{25,17},{2,10},{10... | collective-permute-start | bytes 3538952 | tf_op jit(solution)/shard_map/ppermute | solution.py:192
  6.6 26.3 %collective-permute-start.6 = (f32[768,384]{1,0:T(8,128)S(1)}, f32[768,384]{1,0:T(8,128)S(1)}, u32[]{:S(2)}, u32[]{:S(2)}) collective-permute-start(f32[768,384]{1,0:T(8,128)S(1)} %join.1.refs_4_), channel_id=1, source_target_pairs={{8,16},{16,8},{9,17},{17,9},{10,18},{18,10},{11,19},{19,11},{12,20... | collective-permute-start | bytes 3538952 | tf_op jit(solution)/shard_map/ppermute | solution.py:197
  7.3 19.4 %collective-permute-start = (f32[128,768]{1,0:T(8,128)S(1)}, f32[128,768]{1,0:T(8,128)S(1)}, u32[]{:S(2)}, u32[]{:S(2)}) collective-permute-start(f32[128,768]{1,0:T(8,128)S(1)} %get-tuple-element.69), channel_id=1, source_target_pairs={{0,4},{1,5},{2,6},{3,7},{4,0},{5,1},{6,2},{7,3},{8,12},{9,13},{10,... | collective-permute-start | bytes 1179656 | tf_op jit(solution)/shard_map/ppermute | solution.py:217
  8.9 17.8 %collective-permute-start.1 = (f32[128,768]{1,0:T(8,128)S(1)}, f32[128,768]{1,0:T(8,128)S(1)}, u32[]{:S(2)}, u32[]{:S(2)}) collective-permute-start(f32[128,768]{1,0:T(8,128)S(1)} %get-tuple-element.70), channel_id=1, source_target_pairs={{0,6},{1,7},{2,4},{3,5},{4,2},{5,3},{6,0},{7,1},{8,14},{9,15},{10,... | collective-permute-start | bytes 1179656 | tf_op jit(solution)/shard_map/ppermute | solution.py:217
  10.3 17.6 %collective-permute-start.3 = (f32[128,768]{1,0:T(8,128)S(1)}, f32[128,768]{1,0:T(8,128)S(1)}, u32[]{:S(2)}, u32[]{:S(2)}) collective-permute-start(f32[128,768]{1,0:T(8,128)S(1)} %get-tuple-element.72), channel_id=1, source_target_pairs={{0,2},{1,3},{2,0},{3,1},{4,6},{5,7},{6,4},{7,5},{8,10},{9,11},{10,... | collective-permute-start | bytes 1179656 | tf_op jit(solution)/shard_map/ppermute | solution.py:217
  26.7 6.7 %collective-permute-start.10 = (f32[128,768]{1,0:T(8,128)S(1)}, f32[128,768]{1,0:T(8,128)S(1)}, u32[]{:S(2)}, u32[]{:S(2)}) collective-permute-start(f32[128,768]{1,0:T(8,128)S(1)} %collective-permute-done.refs_1_), channel_id=1, source_target_pairs={{0,1},{1,0},{2,3},{3,2},{4,5},{5,4},{6,7},{7,6},{8,9},{9,8},{10,11... | collective-permute-start | bytes 1179656 | tf_op jit(solution)/shard_map/ppermute | solution.py:217
  26.7 7.2 %collective-permute-start.11 = (f32[128,768]{1,0:T(8,128)S(1)}, f32[128,768]{1,0:T(8,128)S(1)}, u32[]{:S(2)}, u32[]{:S(2)}) collective-permute-start(f32[128,768]{1,0:T(8,128)S(1)} %collective-permute-done.1.refs_1_), channel_id=1, source_target_pairs={{0,1},{1,0},{2,3},{3,2},{4,5},{5,4},{6,7},{7,6},{8,9},{9,8},{10,11... | collective-permute-start | bytes 1179656 | tf_op jit(solution)/shard_map/ppermute | solution.py:217
  27.9 58.9 %collective-permute-start.9 = (f32[768,384]{1,0:T(8,128)S(1)}, f32[768,384]{1,0:T(8,128)}, u32[]{:S(2)}, u32[]{:S(2)}) collective-permute-start(f32[768,384]{1,0:T(8,128)S(1)} %join.1.refs_4_), channel_id=1, source_target_pairs={{0,24},{24,0},{1,25},{25,1},{2,26},{26,2},{3,27},{27,3},{4,28},{28... | collective-permute-start | bytes 3538952 | tf_op jit(solution)/shard_map/ppermute | solution.py:198
  32.8 16.1 %copy-start.4 = (f32[768,384]{1,0:T(8,128)}, f32[768,384]{1,0:T(8,128)S(1)}, u32[]{:S(2)}) copy-start(f32[768,384]{1,0:T(8,128)S(1)} %collective-permute-done.12.refs_4_) | copy-start | bytes 3538948
  32.8 5.7 %collective-permute-start.2 = (f32[128,768]{1,0:T(8,128)S(1)}, f32[128,768]{1,0:T(8,128)S(1)}, u32[]{:S(2)}, u32[]{:S(2)}) collective-permute-start(f32[128,768]{1,0:T(8,128)S(1)} %get-tuple-element.71.refs_0_), channel_id=1, source_target_pairs={{0,1},{1,0},{2,3},{3,2},{4,5},{5,4},{6,7},{7,6},{8,9},{9,8},{10,11... | collective-permute-start | bytes 1179656 | tf_op jit(solution)/shard_map/ppermute | solution.py:217
  32.9 1.1 copy-start.14
  32.9 5.7 %collective-permute-start.4 = (f32[128,768]{1,0:T(8,128)S(1)}, f32[128,768]{1,0:T(8,128)S(1)}, u32[]{:S(2)}, u32[]{:S(2)}) collective-permute-start(f32[128,768]{1,0:T(8,128)S(1)} %collective-permute-done.3.refs_0_), channel_id=1, source_target_pairs={{0,1},{1,0},{2,3},{3,2},{4,5},{5,4},{6,7},{7,6},{8,9},{9,8},{10,11... | collective-permute-start | bytes 1179656 | tf_op jit(solution)/shard_map/ppermute | solution.py:217
  33.9 15.1 %copy-start = (f32[128,768]{1,0:T(8,128)}, f32[128,768]{1,0:T(8,128)S(1)}, u32[]{:S(2)}) copy-start(f32[128,768]{1,0:T(8,128)S(1)} %collective-permute-done.10.refs_2_) | copy-start | bytes 1179652
  33.9 15.1 %copy-start.2 = (f32[128,768]{1,0:T(8,128)}, f32[128,768]{1,0:T(8,128)S(1)}, u32[]{:S(2)}) copy-start(f32[128,768]{1,0:T(8,128)S(1)} %collective-permute-done.11.refs_3_) | copy-start | bytes 1179652
  35.3 11.6 %collective-permute-start.13 = (f32[256,384]{1,0:T(8,128)S(1)}, f32[256,384]{1,0:T(8,128)S(1)}, u32[]{:S(2)}, u32[]{:S(2)}) collective-permute-start(f32[256,384]{1,0:T(8,128)S(1)} %get-tuple-element.76), channel_id=1, source_target_pairs={{0,2},{1,3},{2,0},{3,1},{4,6},{5,7},{6,4},{7,5},{8,10},{9,11},{10,... | collective-permute-start | bytes 1179656 | tf_op jit(solution)/shard_map/ppermute | solution.py:217
  37.0 11.2 %collective-permute-start.14 = (f32[256,384]{1,0:T(8,128)S(1)}, f32[256,384]{1,0:T(8,128)S(1)}, u32[]{:S(2)}, u32[]{:S(2)}) collective-permute-start(f32[256,384]{1,0:T(8,128)S(1)} %get-tuple-element.77), channel_id=1, source_target_pairs={{0,4},{1,5},{2,6},{3,7},{4,0},{5,1},{6,2},{7,3},{8,12},{9,13},{10,... | collective-permute-start | bytes 1179656 | tf_op jit(solution)/shard_map/ppermute | solution.py:217
  46.9 0.7 copy-start.6
  47.6 3.5 %copy-start.11 = (f32[128,384]{1,0:T(8,128)}, f32[128,384]{1,0:T(8,128)S(1)}, u32[]{:S(2)}) copy-start(f32[128,384]{1,0:T(8,128)S(1)} %get-tuple-element.93) | copy-start | bytes 589828
  48.3 0.7 copy-start.13
  49.0 2.2 %copy-start.8 = (f32[128,384]{1,0:T(8,128)}, f32[128,384]{1,0:T(8,128)S(1)}, u32[]{:S(2)}) copy-start(f32[128,384]{1,0:T(8,128)S(1)} %get-tuple-element.82.held_ref) | copy-start | bytes 589828
  51.1 0.8 copy-start.10
  51.9 37.0 %collective-permute-start.16 = (f32[256,384]{1,0:T(8,128)}, f32[256,384]{1,0:T(8,128)}, u32[]{:S(2)}, u32[]{:S(2)}) collective-permute-start(f32[256,384]{1,0:T(8,128)} %get-tuple-element.85), channel_id=1, source_target_pairs={{0,4},{1,5},{2,6},{3,7},{4,0},{5,1},{6,2},{7,3},{8,12},{9,13},{10,... | collective-permute-start | bytes 1179656 | tf_op jit(solution)/shard_map/ppermute | solution.py:217
  53.4 35.4 %collective-permute-start.18 = (f32[128,384]{1,0:T(8,128)}, f32[128,384]{1,0:T(8,128)S(1)}, u32[]{:S(2)}, u32[]{:S(2)}) collective-permute-start(f32[128,384]{1,0:T(8,128)} %copy-done.13), channel_id=1, source_target_pairs={{0,2},{1,3},{2,0},{3,1},{4,6},{5,7},{6,4},{7,5},{8,10},{9,11},{10,... | collective-permute-start | bytes 589832 | tf_op jit(solution)/shard_map/ppermute | solution.py:217
  54.4 32.3 %copy-start.12 = (f32[128,384]{1,0:T(8,128)S(1)}, f32[128,384]{1,0:T(8,128)}, u32[]{:S(2)}) copy-start(f32[128,384]{1,0:T(8,128)} %copy-done.11) | copy-start | bytes 589828
  54.5 32.9 %copy-start.5 = (f32[768,384]{1,0:T(8,128)S(1)}, f32[768,384]{1,0:T(8,128)}, u32[]{:S(2)}) copy-start(f32[768,384]{1,0:T(8,128)} %copy-done.4) | copy-start | bytes 3538948
  54.5 38.1 %collective-permute-start.15 = (f32[256,384]{1,0:T(8,128)}, f32[256,384]{1,0:T(8,128)S(1)}, u32[]{:S(2)}, u32[]{:S(2)}) collective-permute-start(f32[256,384]{1,0:T(8,128)} %copy-done.10), channel_id=1, source_target_pairs={{0,2},{1,3},{2,0},{3,1},{4,6},{5,7},{6,4},{7,5},{8,10},{9,11},{10,... | collective-permute-start | bytes 1179656 | tf_op jit(solution)/shard_map/ppermute | solution.py:217
  56.7 44.6 %collective-permute-start.8 = (f32[768,256]{1,0:T(8,128)S(1)}, f32[768,256]{1,0:T(8,128)S(1)}, u32[]{:S(2)}, u32[]{:S(2)}) collective-permute-start(f32[768,256]{1,0:T(8,128)S(1)} %slice_select_fusion), channel_id=1, source_target_pairs={{8,0},{16,24},{0,16},{24,8},{9,1},{17,25},{1,17},{25,9},{10,2},{18... | collective-permute-start | bytes 2359304 | tf_op jit(solution)/shard_map/ppermute | solution.py:205
  86.8 2.0 %copy-start.9 = (f32[128,384]{1,0:T(8,128)S(1)}, f32[128,384]{1,0:T(8,128)}, u32[]{:S(2)}) copy-start(f32[128,384]{1,0:T(8,128)} %copy-done.8) | copy-start | bytes 589828
  86.8 5.8 %collective-permute-start.17 = (f32[128,384]{1,0:T(8,128)S(1)}, f32[128,384]{1,0:T(8,128)S(1)}, u32[]{:S(2)}, u32[]{:S(2)}) collective-permute-start(f32[128,384]{1,0:T(8,128)S(1)} %copy-done.12), channel_id=1, source_target_pairs={{0,4},{1,5},{2,6},{3,7},{4,0},{5,1},{6,2},{7,3},{8,12},{9,13},{10,... | collective-permute-start | bytes 589832 | tf_op jit(solution)/shard_map/ppermute | solution.py:217
  88.8 2.4 %copy-start.15 = (f32[768,384]{1,0:T(8,128)S(1)}, f32[768,384]{1,0:T(8,128)}, u32[]{:S(2)}) copy-start(f32[768,384]{1,0:T(8,128)} %copy-done.14) | copy-start | bytes 3538948
  88.8 3.8 %collective-permute-start.19 = (f32[128,384]{1,0:T(8,128)S(1)}, f32[128,384]{1,0:T(8,128)S(1)}, u32[]{:S(2)}, u32[]{:S(2)}) collective-permute-start(f32[128,384]{1,0:T(8,128)S(1)} %fold.19), channel_id=1, source_target_pairs={{0,1},{1,0},{2,3},{3,2},{4,5},{5,4},{6,7},{7,6},{8,9},{9,8},{10,11... | collective-permute-start | bytes 589832 | tf_op jit(solution)/shard_map/ppermute | solution.py:217
  90.0 2.6 %copy-start.7 = (f32[128,384]{1,0:T(8,128)S(1)}, f32[128,384]{1,0:T(8,128)}, u32[]{:S(2)}) copy-start(f32[128,384]{1,0:T(8,128)} %copy-done.6) | copy-start | bytes 589828
  90.0 8.3 %collective-permute-start.23 = (f32[128,384]{1,0:T(8,128)S(1)}, f32[128,384]{1,0:T(8,128)S(1)}, u32[]{:S(2)}, u32[]{:S(2)}) collective-permute-start(f32[128,384]{1,0:T(8,128)S(1)} %get-tuple-element.104), channel_id=1, source_target_pairs={{0,2},{1,3},{2,0},{3,1},{4,6},{5,7},{6,4},{7,5},{8,10},{9,11},{10,... | collective-permute-start | bytes 589832 | tf_op jit(solution)/shard_map/ppermute | solution.py:217
  92.6 1.1 copy-start.1
  92.6 1.2 copy-start.3
  95.3 12.0 %collective-permute-start.21 = (f32[256,384]{1,0:T(8,128)S(1)}, f32[256,384]{1,0:T(8,128)S(1)}, u32[]{:S(2)}, u32[]{:S(2)}) collective-permute-start(f32[256,384]{1,0:T(8,128)S(1)} %get-tuple-element.97), channel_id=1, source_target_pairs={{0,4},{1,5},{2,6},{3,7},{4,0},{5,1},{6,2},{7,3},{8,12},{9,13},{10,... | collective-permute-start | bytes 1179656 | tf_op jit(solution)/shard_map/ppermute | solution.py:217
  96.9 11.6 %collective-permute-start.20 = (f32[256,384]{1,0:T(8,128)S(1)}, f32[256,384]{1,0:T(8,128)S(1)}, u32[]{:S(2)}, u32[]{:S(2)}) collective-permute-start(f32[256,384]{1,0:T(8,128)S(1)} %get-tuple-element.96), channel_id=1, source_target_pairs={{0,2},{1,3},{2,0},{3,1},{4,6},{5,7},{6,4},{7,5},{8,10},{9,11},{10,... | collective-permute-start | bytes 1179656 | tf_op jit(solution)/shard_map/ppermute | solution.py:217
  97.9 12.9 %collective-permute-start.22 = (f32[128,384]{1,0:T(8,128)S(1)}, f32[128,384]{1,0:T(8,128)S(1)}, u32[]{:S(2)}, u32[]{:S(2)}) collective-permute-start(f32[128,384]{1,0:T(8,128)S(1)} %get-tuple-element.103), channel_id=1, source_target_pairs={{0,4},{1,5},{2,6},{3,7},{4,0},{5,1},{6,2},{7,3},{8,12},{9,13},{10,... | collective-permute-start | bytes 589832 | tf_op jit(solution)/shard_map/ppermute | solution.py:217
  98.4 12.3 %collective-permute-start.24 = (f32[128,384]{1,0:T(8,128)S(1)}, f32[128,384]{1,0:T(8,128)S(1)}, u32[]{:S(2)}, u32[]{:S(2)}) collective-permute-start(f32[128,384]{1,0:T(8,128)S(1)} %fold.22), channel_id=1, source_target_pairs={{0,1},{1,0},{2,3},{3,2},{4,5},{5,4},{6,7},{7,6},{8,9},{9,8},{10,11... | collective-permute-start | bytes 589832 | tf_op jit(solution)/shard_map/ppermute | solution.py:217
  101.2 14.3 %collective-permute-start.7 = (f32[768,128]{1,0:T(8,128)S(1)}, f32[768,128]{1,0:T(8,128)S(1)}, u32[]{:S(2)}, u32[]{:S(2)}) collective-permute-start(f32[768,128]{1,0:T(8,128)S(1)} %slice_select_fusion.1), channel_id=1, source_target_pairs={{8,0},{16,24},{0,16},{24,8},{9,1},{17,25},{1,17},{25,9},{10,2},{18... | collective-permute-start | bytes 1179656 | tf_op jit(solution)/shard_map/ppermute | solution.py:205
  107.3 8.1 %collective-permute-start.28 = (f32[128,384]{1,0:T(8,128)S(1)}, f32[128,384]{1,0:T(8,128)S(1)}, u32[]{:S(2)}, u32[]{:S(2)}) collective-permute-start(f32[128,384]{1,0:T(8,128)S(1)} %get-tuple-element.114), channel_id=1, source_target_pairs={{0,2},{1,3},{2,0},{3,1},{4,6},{5,7},{6,4},{7,5},{8,10},{9,11},{10,... | collective-permute-start | bytes 589832 | tf_op jit(solution)/shard_map/ppermute | solution.py:217
  112.3 9.3 %collective-permute-start.26 = (f32[256,256]{1,0:T(8,128)S(1)}, f32[256,256]{1,0:T(8,128)S(1)}, u32[]{:S(2)}, u32[]{:S(2)}) collective-permute-start(f32[256,256]{1,0:T(8,128)S(1)} %get-tuple-element.107), channel_id=1, source_target_pairs={{0,4},{1,5},{2,6},{3,7},{4,0},{5,1},{6,2},{7,3},{8,12},{9,13},{10,... | collective-permute-start | bytes 786440 | tf_op jit(solution)/shard_map/ppermute | solution.py:217
  113.9 8.8 %collective-permute-start.25 = (f32[256,256]{1,0:T(8,128)S(1)}, f32[256,256]{1,0:T(8,128)S(1)}, u32[]{:S(2)}, u32[]{:S(2)}) collective-permute-start(f32[256,256]{1,0:T(8,128)S(1)} %get-tuple-element.106), channel_id=1, source_target_pairs={{0,2},{1,3},{2,0},{3,1},{4,6},{5,7},{6,4},{7,5},{8,10},{9,11},{10,... | collective-permute-start | bytes 786440 | tf_op jit(solution)/shard_map/ppermute | solution.py:217
  114.9 9.2 %collective-permute-start.27 = (f32[128,384]{1,0:T(8,128)S(1)}, f32[128,384]{1,0:T(8,128)S(1)}, u32[]{:S(2)}, u32[]{:S(2)}) collective-permute-start(f32[128,384]{1,0:T(8,128)S(1)} %get-tuple-element.113), channel_id=1, source_target_pairs={{0,4},{1,5},{2,6},{3,7},{4,0},{5,1},{6,2},{7,3},{8,12},{9,13},{10,... | collective-permute-start | bytes 589832 | tf_op jit(solution)/shard_map/ppermute | solution.py:217
  115.5 8.7 %collective-permute-start.29 = (f32[128,384]{1,0:T(8,128)S(1)}, f32[128,384]{1,0:T(8,128)S(1)}, u32[]{:S(2)}, u32[]{:S(2)}) collective-permute-start(f32[128,384]{1,0:T(8,128)S(1)} %fold.25), channel_id=1, source_target_pairs={{0,1},{1,0},{2,3},{3,2},{4,5},{5,4},{6,7},{7,6},{8,9},{9,8},{10,11... | collective-permute-start | bytes 589832 | tf_op jit(solution)/shard_map/ppermute | solution.py:217
  121.7 7.2 %collective-permute-start.36 = (f32[128,256]{1,0:T(8,128)S(1)}, f32[128,256]{1,0:T(8,128)S(1)}, u32[]{:S(2)}, u32[]{:S(2)}) collective-permute-start(f32[128,256]{1,0:T(8,128)S(1)} %get-tuple-element.126), channel_id=1, source_target_pairs={{0,2},{1,3},{2,0},{3,1},{4,6},{5,7},{6,4},{7,5},{8,10},{9,11},{10,... | collective-permute-start | bytes 393224 | tf_op jit(solution)/shard_map/ppermute | solution.py:217
  125.7 5.8 %collective-permute-start.32 = (f32[256,128]{1,0:T(8,128)S(1)}, f32[256,128]{1,0:T(8,128)S(1)}, u32[]{:S(2)}, u32[]{:S(2)}) collective-permute-start(f32[256,128]{1,0:T(8,128)S(1)} %get-tuple-element.117), channel_id=1, source_target_pairs={{0,4},{1,5},{2,6},{3,7},{4,0},{5,1},{6,2},{7,3},{8,12},{9,13},{10,... | collective-permute-start | bytes 393224 | tf_op jit(solution)/shard_map/ppermute | solution.py:217
  127.3 5.4 %collective-permute-start.30 = (f32[256,128]{1,0:T(8,128)S(1)}, f32[256,128]{1,0:T(8,128)S(1)}, u32[]{:S(2)}, u32[]{:S(2)}) collective-permute-start(f32[256,128]{1,0:T(8,128)S(1)} %get-tuple-element.116), channel_id=1, source_target_pairs={{0,2},{1,3},{2,0},{3,1},{4,6},{5,7},{6,4},{7,5},{8,10},{9,11},{10,... | collective-permute-start | bytes 393224 | tf_op jit(solution)/shard_map/ppermute | solution.py:217
  128.3 7.7 %collective-permute-start.35 = (f32[128,256]{1,0:T(8,128)S(1)}, f32[128,256]{1,0:T(8,128)S(1)}, u32[]{:S(2)}, u32[]{:S(2)}) collective-permute-start(f32[128,256]{1,0:T(8,128)S(1)} %get-tuple-element.125), channel_id=1, source_target_pairs={{0,4},{1,5},{2,6},{3,7},{4,0},{5,1},{6,2},{7,3},{8,12},{9,13},{10,... | collective-permute-start | bytes 393224 | tf_op jit(solution)/shard_map/ppermute | solution.py:217
  128.9 7.1 %collective-permute-start.37 = (f32[128,256]{1,0:T(8,128)S(1)}, f32[128,256]{1,0:T(8,128)S(1)}, u32[]{:S(2)}, u32[]{:S(2)}) collective-permute-start(f32[128,256]{1,0:T(8,128)S(1)} %fold.29), channel_id=1, source_target_pairs={{0,1},{1,0},{2,3},{3,2},{4,5},{5,4},{6,7},{7,6},{8,9},{9,8},{10,11... | collective-permute-start | bytes 393224 | tf_op jit(solution)/shard_map/ppermute | solution.py:217
  131.6 4.3 %collective-permute-start.33 = (f32[128,128]{1,0:T(8,128)S(1)}, f32[128,128]{1,0:T(8,128)S(1)}, u32[]{:S(2)}, u32[]{:S(2)}) collective-permute-start(f32[128,128]{1,0:T(8,128)S(1)} %get-tuple-element.124), channel_id=1, source_target_pairs={{0,2},{1,3},{2,0},{3,1},{4,6},{5,7},{6,4},{7,5},{8,10},{9,11},{10,... | collective-permute-start | bytes 196616 | tf_op jit(solution)/shard_map/ppermute | solution.py:217
  132.7 4.3 %collective-permute-start.31 = (f32[128,128]{1,0:T(8,128)S(1)}, f32[128,128]{1,0:T(8,128)S(1)}, u32[]{:S(2)}, u32[]{:S(2)}) collective-permute-start(f32[128,128]{1,0:T(8,128)S(1)} %get-tuple-element.121), channel_id=1, source_target_pairs={{0,4},{1,5},{2,6},{3,7},{4,0},{5,1},{6,2},{7,3},{8,12},{9,13},{10,... | collective-permute-start | bytes 196616 | tf_op jit(solution)/shard_map/ppermute | solution.py:217
  135.9 1.3 collective-permute-start.34

commit v9 on v8

--- a/solution.py
+++ b/solution.py
@@ -25,8 +25,8 @@
 
 
 def kernel_call(body, outs, operands, name, from_hbm=False, scratch=()):
-    if from_hbm:
-        operands = [pltpu.with_memory_space_constraint(x, pltpu.HBM) for x in operands]
+    space = pltpu.HBM if from_hbm else pltpu.VMEM
+    operands = [pltpu.with_memory_space_constraint(x, space) for x in operands]
     return pl.pallas_call(
         body,
         out_shape=[pltpu.VMEM(shape, jnp.float32) for shape in outs],
@@ -193,17 +193,12 @@
 
     if nodes != 4:
         return [(d, own if d == 0 else direct(own, d), 0) for d in range(nodes)]
+    centre = lax.ppermute(own, "occ", [(1, 2), (2, 1)])
     near = direct(own, 1)
-    centre = lax.ppermute(own, "occ", [(1, 2), (2, 1)])
-    far = lax.ppermute(own, "occ", [(0, 3), (3, 0)])
+    far = lax.ppermute(after(own, centre, near), "occ", [(0, 3), (3, 0)])
     middle = (here == 1) | (here == 2)
-    count = own.shape[1] // TILE_V
-    cuts = [0, (2 * count + 2) // 3 * TILE_V, own.shape[1]]
-    last = []
-    for lo, hi in zip(cuts, cuts[1:]):
-        moving = jnp.where(middle, centre[:, lo:hi], own[:, lo:hi])
-        last.append((2, lax.ppermute(moving, "occ", [(1, 0), (2, 3), (0, 2), (3, 1)]), lo))
-    return [(0, own, 0), (1, near, 0), (3, (middle, centre, far), 0), *last]
+    last = lax.ppermute(jnp.where(middle, centre, own), "occ", [(1, 0), (2, 3), (0, 2), (3, 1)])
+    return [(0, own, 0), (1, near, 0), (3, (middle, centre, far), 0), (2, last, 0)]
 
 
 def per_device(sizes, amplitudes, amp_mask, integrals, int_mask):
@@ -249,7 +244,9 @@
             block = after(block, *token)
         sent = products([[rel[h][r] for r in away[h]] for h in range(2)], block)
         moving = [swap(sent[h], 2 * orders[h][0]) for h in range(2)]
-        soon = arrived[n + 1 : n + 2] if n > 0 else []
+        soon = arrived[2:3] if n == 1 else []
+        if n == 2:
+            moving = list(lax.optimization_barrier((*moving, *arrived[3:4]))[:2])
         held = list(products([[rel[h][r] for r in near[h]] for h in range(2)], after(block, *sent, *soon)))
         names = [near[0], near[1]]
         for level in range(1, len(bits)):

time: 138 us -> 122 us (0.88)
  starting transfers between devices: 69.2 us -> 34.4 us
  waiting for transfers between devices: 42.1 us -> 59.9 us
  Pallas kernels: 20.5 us -> 24.6 us
  local copies, waits for them, and re-layouts: 3.11 us -> 1.06 us
    ppermute x3 -> x2, starting transfers between devices: 38 us -> 3.59 us  [the longest x1 3.25 us: line_blocks(): far = lax.ppermute(after(own, centre, near), 'occ', [(0, 3), (3, 0)])]
    ppermute x33 -> x28, waiting for transfers between devices: 38.8 us -> 50.4 us  [swap(): return lax.ppermute(x, 'vir', [(i, i ^ bits) for i in range(n_vir)])]
    ppermute x1, waiting for transfers between devices: 0.56 us -> 6.45 us  [direct(): return lax.ppermute(x, 'occ', [(i, i ^ d) for i in range(nodes)])]
    pallas_call x28 -> x23, Pallas kernels: 16.7 us -> 21.4 us  [kernel_call(): pl.pallas_call(body, out_shape=[pltpu.VMEM(shape, jnp.float32) for shape...]
    ppermute x33 -> x28, starting transfers between devices: 27.4 us -> 24.3 us  [swap(): return lax.ppermute(x, 'vir', [(i, i ^ bits) for i in range(n_vir)])]
    ppermute x1, starting transfers between devices: 3.01 us -> 5.76 us  [direct(): return lax.ppermute(x, 'occ', [(i, i ^ d) for i in range(nodes)])]
    unnamed x32 -> x12, local copies, waits for them, and re-layouts: 3.11 us -> 1.06 us
    pallas_call x5 -> x4, Pallas kernels: 3.76 us -> 3.13 us  [write(): pl.pallas_call(functools.partial(write_kernel, d, half, offset), out_shap...]
  transfers between devices with their start and end apart: 38 -> 32, of which waited for: 15 -> 14; matrix products, arithmetic and copies ran while one was open for 2% -> 1% of each run, Pallas kernels for 13% -> 17%
where the time goes in v9:
time: 122 us
  waiting for transfers between devices  59.9 us (49%)
  starting transfers between devices  34.4 us (28%)
  Pallas kernels  24.6 us (20%)
  other arithmetic  1.53 us (1%)
    ppermute x28, waiting for transfers between devices, swap(): return lax.ppermute(x, 'vir', [(i, i ^ bits) for i in range(n_vir)])  50.4 us
    ppermute x28, starting transfers between devices, swap(): return lax.ppermute(x, 'vir', [(i, i ^ bits) for i in range(n_vir)])  24.3 us
    pallas_call x23, Pallas kernels, kernel_call(): pl.pallas_call(body, out_shape=[pltpu.VMEM(shape, jnp.float32) for shape...  21.4 us
    ppermute x1, waiting for transfers between devices, direct(): return lax.ppermute(x, 'occ', [(i, i ^ d) for i in range(nodes)])  6.45 us
    ppermute x1, starting transfers between devices, direct(): return lax.ppermute(x, 'occ', [(i, i ^ d) for i in range(nodes)])  5.76 us
    ppermute x1, starting transfers between devices, line_blocks(): far = lax.ppermute(after(own, centre, near), 'occ', [(0, 3), (3, 0)])  3.25 us
    pallas_call x4, Pallas kernels, write(): pl.pallas_call(functools.partial(write_kernel, d, half, offset), out_shap...  3.13 us
  transfers between devices with their start and end apart: 32, of which 14 were waited for; matrix products, arithmetic and copies ran while one was open for 1% of the time, Pallas kernels for 17%

profile of v9, /device:TPU:0, one launch (start us, length us, event | category | flops | bytes accessed | tf_op | source)
XLA Modules:
  0.0 121.9 jit_solution(13818664441694780876)
XLA Ops:
  0.0 1.3 %halves.1 = (f32[384,384]{1,0:T(8,128)S(1)}, f32[384,384]{1,0:T(8,128)S(1)}) custom-call(s32[3,6]{1,0:T(4,128)} %mask_hbm.1, f32[384,768]{1,0:T(8,128)} %int_hbm.1), custom_call_target="tpu_custom_call" | custom-call | flops 1 | bytes 1 | tf_op jit(solution)/shard_map/halves/pallas_call | solution.py:30
  1.3 0.5 collective-permute-start.5
  1.8 1.4 %cut.1 = (f32[128,768]{1,0:T(8,128)S(1)}, f32[128,768]{1,0:T(8,128)S(1)}, f32[128,768]{1,0:T(8,128)S(1)}, f32[128,768]{1,0:T(8,128)S(1)}) custom-call(s32[4,24]{1,0:T(4,128)} %mask_hbm.2, f32[128,3072]{1,0:T(8,128)} %amp_hbm.1), custom_call_target="tpu_custom_call" | custom-call | flops 1 | bytes 1 | tf_op jit(solution)/shard_map/cut/pallas_call | solution.py:30
  3.3 0.2 collective-permute-done.5.other_ref
  3.5 0.1 join.1.refs_4_
  3.6 0.7 collective-permute-start.6
  4.3 5.8 %collective-permute-start.8 = (f32[768,384]{1,0:T(8,128)S(1)}, f32[768,384]{1,0:T(8,128)S(1)}, u32[]{:S(2)}, u32[]{:S(2)}) collective-permute-start(f32[768,384]{1,0:T(8,128)S(1)} %join.1.refs_4_), channel_id=1, source_target_pairs={{0,8},{8,0},{16,24},{24,16},{1,9},{9,1},{17,25},{25,17},{2,10},{10... | collective-permute-start | bytes 3538952 | tf_op jit(solution)/shard_map/ppermute | solution.py:192
  10.1 1.5 %collective-permute-start = (f32[128,768]{1,0:T(8,128)S(1)}, f32[128,768]{1,0:T(8,128)S(1)}, u32[]{:S(2)}, u32[]{:S(2)}) collective-permute-start(f32[128,768]{1,0:T(8,128)S(1)} %get-tuple-element.62), channel_id=1, source_target_pairs={{0,4},{1,5},{2,6},{3,7},{4,0},{5,1},{6,2},{7,3},{8,12},{9,13},{10,... | collective-permute-start | bytes 1179656 | tf_op jit(solution)/shard_map/ppermute | solution.py:212
  11.6 1.4 %collective-permute-start.1 = (f32[128,768]{1,0:T(8,128)S(1)}, f32[128,768]{1,0:T(8,128)S(1)}, u32[]{:S(2)}, u32[]{:S(2)}) collective-permute-start(f32[128,768]{1,0:T(8,128)S(1)} %get-tuple-element.63), channel_id=1, source_target_pairs={{0,6},{1,7},{2,4},{3,5},{4,2},{5,3},{6,0},{7,1},{8,14},{9,15},{10,... | collective-permute-start | bytes 1179656 | tf_op jit(solution)/shard_map/ppermute | solution.py:212
  13.0 0.5 collective-permute-start.3
  13.6 15.5 %collective-permute-done.refs_1_ = f32[128,768]{1,0:T(8,128)S(1)} collective-permute-done((f32[128,768]{1,0:T(8,128)S(1)}, f32[128,768]{1,0:T(8,128)S(1)}, u32[]{:S(2)}, u32[]{:S(2)}) %collective-permute-start) | collective-permute-done | bytes 393248 | tf_op jit(solution)/shard_map/ppermute | solution.py:212
  29.1 0.5 collective-permute-start.11
  29.6 6.4 %collective-permute-done.8.refs_4_ = f32[768,384]{1,0:T(8,128)S(1)} collective-permute-done((f32[768,384]{1,0:T(8,128)S(1)}, f32[768,384]{1,0:T(8,128)S(1)}, u32[]{:S(2)}, u32[]{:S(2)}) %collective-permute-start.8) | collective-permute-done | bytes 1179680 | tf_op jit(solution)/shard_map/ppermute | solution.py:192
  36.1 1.0 copy-done.2
  37.1 3.2 %collective-permute-start.9 = (f32[768,384]{1,0:T(8,128)S(1)}, f32[768,384]{1,0:T(8,128)}, u32[]{:S(2)}, u32[]{:S(2)}) collective-permute-start(f32[768,384]{1,0:T(8,128)S(1)} %join.1.refs_4_), channel_id=1, source_target_pairs={{0,24},{24,0},{1,25},{25,1},{2,26},{26,2},{3,27},{27,3},{4,28},{28... | collective-permute-start | bytes 3538952 | tf_op jit(solution)/shard_map/ppermute | solution.py:198
  40.4 0.1 collective-permute-start.2
  40.4 0.5 collective-permute-start.4
  41.0 2.1 %products.8 = (f32[256,384]{1,0:T(8,128)}, f32[256,384]{1,0:T(8,128)}) custom-call(f32[128,768]{1,0:T(8,128)S(1)} %collective-permute-done.3.refs_0_, f32[128,768]{1,0:T(8,128)S(1)} %collective-permute-done.1.refs_1_, f32[128,768]{1,0:T(8,128)S(1)} %collective-permute-done.10.refs_2_, f32[128,768]{1,0:T(8,128)S(1)} %collective-permute-done.11.refs_3_, ...), custom_call_target="tpu_custom_call" | custom-call | flops 1 | bytes 1 | tf_op jit(solution)/shard_map/products/pallas_call | solution.py:30
  43.1 1.5 %collective-permute-start.13 = (f32[256,384]{1,0:T(8,128)}, f32[256,384]{1,0:T(8,128)}, u32[]{:S(2)}, u32[]{:S(2)}) collective-permute-start(f32[256,384]{1,0:T(8,128)} %get-tuple-element.71), channel_id=1, source_target_pairs={{0,4},{1,5},{2,6},{3,7},{4,0},{5,1},{6,2},{7,3},{8,12},{9,13},{10,... | collective-permute-start | bytes 1179656 | tf_op jit(solution)/shard_map/ppermute | solution.py:212
  44.6 1.5 %collective-permute-start.12 = (f32[256,384]{1,0:T(8,128)}, f32[256,384]{1,0:T(8,128)}, u32[]{:S(2)}, u32[]{:S(2)}) collective-permute-start(f32[256,384]{1,0:T(8,128)} %get-tuple-element.70), channel_id=1, source_target_pairs={{0,2},{1,3},{2,0},{3,1},{4,6},{5,7},{6,4},{7,5},{8,10},{9,11},{10,... | collective-permute-start | bytes 1179656 | tf_op jit(solution)/shard_map/ppermute | solution.py:212
  46.1 2.5 %products.9 = (f32[256,384]{1,0:T(8,128)S(1)}, f32[256,384]{1,0:T(8,128)S(1)}) custom-call(f32[128,768]{1,0:T(8,128)S(1)} %get-tuple-element.64.refs_0_, f32[128,768]{1,0:T(8,128)S(1)} %collective-permute-done.refs_1_, f32[128,768]{1,0:T(8,128)S(1)} %collective-permute-done.2.refs_2_, f32[128,768]{1,0:T(8,128)} %collective-permute-done.4.refs_3_, ...), custom_call_target="tpu_custom_call" | custom-call | flops 1 | bytes 1 | tf_op jit(solution)/shard_map/products/pallas_call | solution.py:30
  48.6 5.9 %collective-permute-done.13.got_ref = f32[256,384]{1,0:T(8,128)} collective-permute-done((f32[256,384]{1,0:T(8,128)}, f32[256,384]{1,0:T(8,128)}, u32[]{:S(2)}, u32[]{:S(2)}) %collective-permute-start.13) | collective-permute-done | bytes 393248 | tf_op jit(solution)/shard_map/ppermute | solution.py:212
  54.5 1.0 fold.13
  55.6 1.6 %collective-permute-start.17 = (f32[128,384]{1,0:T(8,128)S(1)}, f32[128,384]{1,0:T(8,128)S(1)}, u32[]{:S(2)}, u32[]{:S(2)}) collective-permute-start(f32[128,384]{1,0:T(8,128)S(1)} %get-tuple-element.88), channel_id=1, source_target_pairs={{0,2},{1,3},{2,0},{3,1},{4,6},{5,7},{6,4},{7,5},{8,10},{9,11},{10,... | collective-permute-start | bytes 589832 | tf_op jit(solution)/shard_map/ppermute | solution.py:212
  57.1 0.1 broadcast_select_fusion.1
  57.3 0.3 collective-permute-start.7
  57.6 1.1 fold.12
  58.7 1.6 %collective-permute-start.16 = (f32[128,384]{1,0:T(8,128)S(1)}, f32[128,384]{1,0:T(8,128)S(1)}, u32[]{:S(2)}, u32[]{:S(2)}) collective-permute-start(f32[128,384]{1,0:T(8,128)S(1)} %get-tuple-element.87), channel_id=1, source_target_pairs={{0,4},{1,5},{2,6},{3,7},{4,0},{5,1},{6,2},{7,3},{8,12},{9,13},{10,... | collective-permute-start | bytes 589832 | tf_op jit(solution)/shard_map/ppermute | solution.py:212
  60.3 1.4 %products.10 = (f32[256,384]{1,0:T(8,128)S(1)}, f32[256,384]{1,0:T(8,128)S(1)}) custom-call(f32[128,768]{1,0:T(8,128)S(1)} %collective-permute-done.3.refs_0_, f32[128,768]{1,0:T(8,128)S(1)} %collective-permute-done.1.refs_1_, f32[128,768]{1,0:T(8,128)S(1)} %collective-permute-done.10.refs_2_, f32[128,768]{1,0:T(8,128)S(1)} %copy-done.1, ...), custom_call_target="tpu_custom_call" | custom-call | flops 1 | bytes 1 | tf_op jit(solution)/shard_map/products/pallas_call | solution.py:30
  61.7 0.6 collective-permute-start.14
  62.3 0.9 collective-permute-start.15
  63.2 2.4 %collective-permute-done.16.got_ref = f32[128,384]{1,0:T(8,128)S(1)} collective-permute-done((f32[128,384]{1,0:T(8,128)S(1)}, f32[128,384]{1,0:T(8,128)S(1)}, u32[]{:S(2)}, u32[]{:S(2)}) %collective-permute-start.16) | collective-permute-done | bytes 196640 | tf_op jit(solution)/shard_map/ppermute | solution.py:212
  65.7 1.4 %collective-permute-done.18.other_ref = f32[128,384]{1,0:T(8,128)S(1)} collective-permute-done((f32[128,384]{1,0:T(8,128)S(1)}, f32[128,384]{1,0:T(8,128)S(1)}, u32[]{:S(2)}, u32[]{:S(2)}) %collective-permute-start.18) | collective-permute-done | bytes 196640 | tf_op jit(solution)/shard_map/ppermute | solution.py:212
  67.1 0.8 write.4.refs_0_
  67.9 2.0 %collective-permute-done.9 = f32[768,384]{1,0:T(8,128)} collective-permute-done((f32[768,384]{1,0:T(8,128)S(1)}, f32[768,384]{1,0:T(8,128)}, u32[]{:S(2)}, u32[]{:S(2)}) %collective-permute-start.9) | collective-permute-done | bytes 1179680 | tf_op jit(solution)/shard_map/ppermute | solution.py:198
  69.8 2.4 %products.11 = (f32[256,384]{1,0:T(8,128)S(1)}, f32[256,384]{1,0:T(8,128)S(1)}) custom-call(f32[128,768]{1,0:T(8,128)S(1)} %get-tuple-element.64.refs_0_, f32[128,768]{1,0:T(8,128)S(1)} %collective-permute-done.refs_1_, f32[128,768]{1,0:T(8,128)S(1)} %collective-permute-done.2.refs_2_, f32[128,768]{1,0:T(8,128)} %collective-permute-done.4.refs_3_, ...), custom_call_target="tpu_custom_call" | custom-call | flops 1 | bytes 1 | tf_op jit(solution)/shard_map/products/pallas_call | solution.py:30
  72.3 0.5 collective-permute-done.15.got_ref
  72.9 1.4 %broadcast_select_fusion.refs_4_ = f32[768,384]{1,0:T(8,128)S(1)} fusion(f32[768,384]{1,0:T(8,128)S(1)} %copy-done.5, f32[768,384]{1,0:T(8,128)} %collective-permute-done.9, pred[]{:T(512)S(6)} %or.3), kind=kLoop, calls=%fused_computation | loop fusion | flops 294912 | bytes 3538945 | tf_op jit(solution)/shard_map/jit(_where)/select_n | solution.py:240
  74.3 1.4 %products.12 = (f32[256,384]{1,0:T(8,128)S(1)}, f32[256,384]{1,0:T(8,128)S(1)}) custom-call(f32[128,768]{1,0:T(8,128)S(1)} %collective-permute-done.3.refs_0_, f32[128,768]{1,0:T(8,128)S(1)} %collective-permute-done.1.refs_1_, f32[128,768]{1,0:T(8,128)S(1)} %collective-permute-done.10.refs_2_, f32[128,768]{1,0:T(8,128)S(1)} %copy-done.1, ...), custom_call_target="tpu_custom_call" | custom-call | flops 1 | bytes 1 | tf_op jit(solution)/shard_map/products/pallas_call | solution.py:30
  75.7 1.0 collective-permute-start.19
  76.8 1.5 %collective-permute-start.20 = (f32[256,384]{1,0:T(8,128)S(1)}, f32[256,384]{1,0:T(8,128)S(1)}, u32[]{:S(2)}, u32[]{:S(2)}) collective-permute-start(f32[256,384]{1,0:T(8,128)S(1)} %get-tuple-element.91), channel_id=1, source_target_pairs={{0,4},{1,5},{2,6},{3,7},{4,0},{5,1},{6,2},{7,3},{8,12},{9,13},{10,... | collective-permute-start | bytes 1179656 | tf_op jit(solution)/shard_map/ppermute | solution.py:212
  78.3 1.1 collective-permute-start.22
  79.3 0.5 collective-permute-start.21
  79.8 9.8 %collective-permute-done.22.got_ref = f32[128,384]{1,0:T(8,128)S(1)} collective-permute-done((f32[128,384]{1,0:T(8,128)S(1)}, f32[128,384]{1,0:T(8,128)S(1)}, u32[]{:S(2)}, u32[]{:S(2)}) %collective-permute-start.22) | collective-permute-done | bytes 196640 | tf_op jit(solution)/shard_map/ppermute | solution.py:212
  89.7 0.1 collective-permute-start.23
  89.7 2.4 %products.13 = (f32[256,384]{1,0:T(8,128)S(1)}, f32[256,384]{1,0:T(8,128)S(1)}) custom-call(f32[128,768]{1,0:T(8,128)S(1)} %get-tuple-element.64.refs_0_, f32[128,768]{1,0:T(8,128)S(1)} %collective-permute-done.refs_1_, f32[128,768]{1,0:T(8,128)S(1)} %collective-permute-done.2.refs_2_, f32[128,768]{1,0:T(8,128)} %collective-permute-done.4.refs_3_, ...), custom_call_target="tpu_custom_call" | custom-call | flops 1 | bytes 1 | tf_op jit(solution)/shard_map/products/pallas_call | solution.py:30
  92.2 1.1 collective-permute-done.7.refs_4_
  93.4 0.8 write.5.refs_0_
  94.2 1.4 %products.14 = (f32[256,384]{1,0:T(8,128)S(1)}, f32[256,384]{1,0:T(8,128)S(1)}) custom-call(f32[128,768]{1,0:T(8,128)S(1)} %collective-permute-done.3.refs_0_, f32[128,768]{1,0:T(8,128)S(1)} %collective-permute-done.1.refs_1_, f32[128,768]{1,0:T(8,128)S(1)} %collective-permute-done.10.refs_2_, f32[128,768]{1,0:T(8,128)S(1)} %copy-done.1, ...), custom_call_target="tpu_custom_call" | custom-call | flops 1 | bytes 1 | tf_op jit(solution)/shard_map/products/pallas_call | solution.py:30
  95.6 1.6 %collective-permute-start.26 = (f32[256,384]{1,0:T(8,128)S(1)}, f32[256,384]{1,0:T(8,128)S(1)}, u32[]{:S(2)}, u32[]{:S(2)}) collective-permute-start(f32[256,384]{1,0:T(8,128)S(1)} %get-tuple-element.103), channel_id=1, source_target_pairs={{0,4},{1,5},{2,6},{3,7},{4,0},{5,1},{6,2},{7,3},{8,12},{9,13},{10,... | collective-permute-start | bytes 1179656 | tf_op jit(solution)/shard_map/ppermute | solution.py:212
  97.2 1.5 %collective-permute-start.24 = (f32[256,384]{1,0:T(8,128)S(1)}, f32[256,384]{1,0:T(8,128)S(1)}, u32[]{:S(2)}, u32[]{:S(2)}) collective-permute-start(f32[256,384]{1,0:T(8,128)S(1)} %get-tuple-element.102), channel_id=1, source_target_pairs={{0,2},{1,3},{2,0},{3,1},{4,6},{5,7},{6,4},{7,5},{8,10},{9,11},{10,... | collective-permute-start | bytes 1179656 | tf_op jit(solution)/shard_map/ppermute | solution.py:212
  98.7 0.5 collective-permute-start.30
  99.2 2.4 %products.15 = (f32[256,384]{1,0:T(8,128)S(1)}, f32[256,384]{1,0:T(8,128)S(1)}) custom-call(f32[128,768]{1,0:T(8,128)S(1)} %get-tuple-element.64.refs_0_, f32[128,768]{1,0:T(8,128)S(1)} %collective-permute-done.refs_1_, f32[128,768]{1,0:T(8,128)S(1)} %collective-permute-done.2.refs_2_, f32[128,768]{1,0:T(8,128)} %collective-permute-done.4.refs_3_, ...), custom_call_target="tpu_custom_call" | custom-call | flops 1 | bytes 1 | tf_op jit(solution)/shard_map/products/pallas_call | solution.py:30
  101.6 5.1 %collective-permute-done.26.got_ref = f32[256,384]{1,0:T(8,128)S(1)} collective-permute-done((f32[256,384]{1,0:T(8,128)S(1)}, f32[256,384]{1,0:T(8,128)S(1)}, u32[]{:S(2)}, u32[]{:S(2)}) %collective-permute-start.26) | collective-permute-done | bytes 393248 | tf_op jit(solution)/shard_map/ppermute | solution.py:212
  106.7 1.6 %collective-permute-start.27 = (f32[128,384]{1,0:T(8,128)S(1)}, f32[128,384]{1,0:T(8,128)S(1)}, u32[]{:S(2)}, u32[]{:S(2)}) collective-permute-start(f32[128,384]{1,0:T(8,128)S(1)} %get-tuple-element.110), channel_id=1, source_target_pairs={{0,2},{1,3},{2,0},{3,1},{4,6},{5,7},{6,4},{7,5},{8,10},{9,11},{10,... | collective-permute-start | bytes 589832 | tf_op jit(solution)/shard_map/ppermute | solution.py:212
  108.3 1.5 %collective-permute-start.29 = (f32[128,384]{1,0:T(8,128)S(1)}, f32[128,384]{1,0:T(8,128)S(1)}, u32[]{:S(2)}, u32[]{:S(2)}) collective-permute-start(f32[128,384]{1,0:T(8,128)S(1)} %get-tuple-element.111), channel_id=1, source_target_pairs={{0,4},{1,5},{2,6},{3,7},{4,0},{5,1},{6,2},{7,3},{8,12},{9,13},{10,... | collective-permute-start | bytes 589832 | tf_op jit(solution)/shard_map/ppermute | solution.py:212
  109.8 3.6 %collective-permute-done.30.got_ref = f32[128,384]{1,0:T(8,128)S(1)} collective-permute-done((f32[128,384]{1,0:T(8,128)S(1)}, f32[128,384]{1,0:T(8,128)S(1)}, u32[]{:S(2)}, u32[]{:S(2)}) %collective-permute-start.30) | collective-permute-done | bytes 196640 | tf_op jit(solution)/shard_map/ppermute | solution.py:212
  113.4 0.1 collective-permute-start.31
  113.6 0.6 collective-permute-start.25
  114.1 2.2 %collective-permute-done.27.got_ref = f32[128,384]{1,0:T(8,128)S(1)} collective-permute-done((f32[128,384]{1,0:T(8,128)S(1)}, f32[128,384]{1,0:T(8,128)S(1)}, u32[]{:S(2)}, u32[]{:S(2)}) %collective-permute-start.27) | collective-permute-done | bytes 196640 | tf_op jit(solution)/shard_map/ppermute | solution.py:212
  116.4 0.1 collective-permute-start.28
  116.5 0.8 write.6.refs_0_
  117.3 3.7 %collective-permute-done.25.got_ref = f32[128,384]{1,0:T(8,128)S(1)} collective-permute-done((f32[128,384]{1,0:T(8,128)S(1)}, f32[128,384]{1,0:T(8,128)S(1)}, u32[]{:S(2)}, u32[]{:S(2)}) %collective-permute-start.25) | collective-permute-done | bytes 196640 | tf_op jit(solution)/shard_map/ppermute | solution.py:212
  120.9 0.8 write.7
  (41 shorter events, 0.4 us)
Async XLA Ops:
  1.3 2.1 %collective-permute-start.5 = (f32[384,384]{1,0:T(8,128)S(1)}, f32[384,384]{1,0:T(8,128)S(1)}, u32[]{:S(2)}, u32[]{:S(2)}) collective-permute-start(f32[384,384]{1,0:T(8,128)S(1)} %get-tuple-element.66), channel_id=1, source_target_pairs={{0,1},{1,0},{2,3},{3,2},{4,5},{5,4},{6,7},{7,6},{8,9},{9,8},{10,11... | collective-permute-start | bytes 1769480 | tf_op jit(solution)/shard_map/ppermute | solution.py:212
  3.6 26.0 %collective-permute-start.6 = (f32[768,384]{1,0:T(8,128)S(1)}, f32[768,384]{1,0:T(8,128)S(1)}, u32[]{:S(2)}, u32[]{:S(2)}) collective-permute-start(f32[768,384]{1,0:T(8,128)S(1)} %join.1.refs_4_), channel_id=1, source_target_pairs={{8,16},{16,8},{9,17},{17,9},{10,18},{18,10},{11,19},{19,11},{12,20... | collective-permute-start | bytes 3538952 | tf_op jit(solution)/shard_map/ppermute | solution.py:196
  4.3 31.7 %collective-permute-start.8 = (f32[768,384]{1,0:T(8,128)S(1)}, f32[768,384]{1,0:T(8,128)S(1)}, u32[]{:S(2)}, u32[]{:S(2)}) collective-permute-start(f32[768,384]{1,0:T(8,128)S(1)} %join.1.refs_4_), channel_id=1, source_target_pairs={{0,8},{8,0},{16,24},{24,16},{1,9},{9,1},{17,25},{25,17},{2,10},{10... | collective-permute-start | bytes 3538952 | tf_op jit(solution)/shard_map/ppermute | solution.py:192
  10.1 19.0 %collective-permute-start = (f32[128,768]{1,0:T(8,128)S(1)}, f32[128,768]{1,0:T(8,128)S(1)}, u32[]{:S(2)}, u32[]{:S(2)}) collective-permute-start(f32[128,768]{1,0:T(8,128)S(1)} %get-tuple-element.62), channel_id=1, source_target_pairs={{0,4},{1,5},{2,6},{3,7},{4,0},{5,1},{6,2},{7,3},{8,12},{9,13},{10,... | collective-permute-start | bytes 1179656 | tf_op jit(solution)/shard_map/ppermute | solution.py:212
  11.6 17.5 %collective-permute-start.1 = (f32[128,768]{1,0:T(8,128)S(1)}, f32[128,768]{1,0:T(8,128)S(1)}, u32[]{:S(2)}, u32[]{:S(2)}) collective-permute-start(f32[128,768]{1,0:T(8,128)S(1)} %get-tuple-element.63), channel_id=1, source_target_pairs={{0,6},{1,7},{2,4},{3,5},{4,2},{5,3},{6,0},{7,1},{8,14},{9,15},{10,... | collective-permute-start | bytes 1179656 | tf_op jit(solution)/shard_map/ppermute | solution.py:212
  13.0 27.4 %collective-permute-start.3 = (f32[128,768]{1,0:T(8,128)S(1)}, f32[128,768]{1,0:T(8,128)S(1)}, u32[]{:S(2)}, u32[]{:S(2)}) collective-permute-start(f32[128,768]{1,0:T(8,128)S(1)} %get-tuple-element.65), channel_id=1, source_target_pairs={{0,2},{1,3},{2,0},{3,1},{4,6},{5,7},{6,4},{7,5},{8,10},{9,11},{10,... | collective-permute-start | bytes 1179656 | tf_op jit(solution)/shard_map/ppermute | solution.py:212
  29.1 11.8 %collective-permute-start.10 = (f32[128,768]{1,0:T(8,128)S(1)}, f32[128,768]{1,0:T(8,128)S(1)}, u32[]{:S(2)}, u32[]{:S(2)}) collective-permute-start(f32[128,768]{1,0:T(8,128)S(1)} %collective-permute-done.refs_1_), channel_id=1, source_target_pairs={{0,1},{1,0},{2,3},{3,2},{4,5},{5,4},{6,7},{7,6},{8,9},{9,8},{10,11... | collective-permute-start | bytes 1179656 | tf_op jit(solution)/shard_map/ppermute | solution.py:212
  29.1 11.8 %collective-permute-start.11 = (f32[128,768]{1,0:T(8,128)S(1)}, f32[128,768]{1,0:T(8,128)S(1)}, u32[]{:S(2)}, u32[]{:S(2)}) collective-permute-start(f32[128,768]{1,0:T(8,128)S(1)} %collective-permute-done.1.refs_1_), channel_id=1, source_target_pairs={{0,1},{1,0},{2,3},{3,2},{4,5},{5,4},{6,7},{7,6},{8,9},{9,8},{10,11... | collective-permute-start | bytes 1179656 | tf_op jit(solution)/shard_map/ppermute | solution.py:212
  29.6 11.3 %copy-start.4 = (f32[768,384]{1,0:T(8,128)}, f32[768,384]{1,0:T(8,128)S(1)}, u32[]{:S(2)}) copy-start(f32[768,384]{1,0:T(8,128)S(1)} %collective-permute-done.6) | copy-start | bytes 3538948
  36.1 1.0 copy-start.2
  37.1 32.7 %collective-permute-start.9 = (f32[768,384]{1,0:T(8,128)S(1)}, f32[768,384]{1,0:T(8,128)}, u32[]{:S(2)}, u32[]{:S(2)}) collective-permute-start(f32[768,384]{1,0:T(8,128)S(1)} %join.1.refs_4_), channel_id=1, source_target_pairs={{0,24},{24,0},{1,25},{25,1},{2,26},{26,2},{3,27},{27,3},{4,28},{28... | collective-permute-start | bytes 3538952 | tf_op jit(solution)/shard_map/ppermute | solution.py:198
  40.4 5.8 %collective-permute-start.2 = (f32[128,768]{1,0:T(8,128)S(1)}, f32[128,768]{1,0:T(8,128)S(1)}, u32[]{:S(2)}, u32[]{:S(2)}) collective-permute-start(f32[128,768]{1,0:T(8,128)S(1)} %get-tuple-element.64.refs_0_), channel_id=1, source_target_pairs={{0,1},{1,0},{2,3},{3,2},{4,5},{5,4},{6,7},{7,6},{8,9},{9,8},{10,11... | collective-permute-start | bytes 1179656 | tf_op jit(solution)/shard_map/ppermute | solution.py:212
  40.4 5.7 %collective-permute-start.4 = (f32[128,768]{1,0:T(8,128)S(1)}, f32[128,768]{1,0:T(8,128)}, u32[]{:S(2)}, u32[]{:S(2)}) collective-permute-start(f32[128,768]{1,0:T(8,128)S(1)} %collective-permute-done.3.refs_0_), channel_id=1, source_target_pairs={{0,1},{1,0},{2,3},{3,2},{4,5},{5,4},{6,7},{7,6},{8,9},{9,8},{10,11... | collective-permute-start | bytes 1179656 | tf_op jit(solution)/shard_map/ppermute | solution.py:212
  40.9 2.2 %copy-start = (f32[128,768]{1,0:T(8,128)}, f32[128,768]{1,0:T(8,128)S(1)}, u32[]{:S(2)}) copy-start(f32[128,768]{1,0:T(8,128)S(1)} %collective-permute-done.11.refs_3_) | copy-start | bytes 1179652
  43.1 11.4 %collective-permute-start.13 = (f32[256,384]{1,0:T(8,128)}, f32[256,384]{1,0:T(8,128)}, u32[]{:S(2)}, u32[]{:S(2)}) collective-permute-start(f32[256,384]{1,0:T(8,128)} %get-tuple-element.71), channel_id=1, source_target_pairs={{0,4},{1,5},{2,6},{3,7},{4,0},{5,1},{6,2},{7,3},{8,12},{9,13},{10,... | collective-permute-start | bytes 1179656 | tf_op jit(solution)/shard_map/ppermute | solution.py:212
  44.6 13.0 %collective-permute-start.12 = (f32[256,384]{1,0:T(8,128)}, f32[256,384]{1,0:T(8,128)}, u32[]{:S(2)}, u32[]{:S(2)}) collective-permute-start(f32[256,384]{1,0:T(8,128)} %get-tuple-element.70), channel_id=1, source_target_pairs={{0,2},{1,3},{2,0},{3,1},{4,6},{5,7},{6,4},{7,5},{8,10},{9,11},{10,... | collective-permute-start | bytes 1179656 | tf_op jit(solution)/shard_map/ppermute | solution.py:212
  46.1 11.0 %copy-start.5 = (f32[768,384]{1,0:T(8,128)S(1)}, f32[768,384]{1,0:T(8,128)}, u32[]{:S(2)}) copy-start(f32[768,384]{1,0:T(8,128)} %copy-done.4) | copy-start | bytes 3538948
  55.6 4.7 %copy-start.1 = (f32[128,768]{1,0:T(8,128)S(1)}, f32[128,768]{1,0:T(8,128)}, u32[]{:S(2)}) copy-start(f32[128,768]{1,0:T(8,128)} %copy-done) | copy-start | bytes 1179652
  55.6 6.7 %collective-permute-start.17 = (f32[128,384]{1,0:T(8,128)S(1)}, f32[128,384]{1,0:T(8,128)S(1)}, u32[]{:S(2)}, u32[]{:S(2)}) collective-permute-start(f32[128,384]{1,0:T(8,128)S(1)} %get-tuple-element.88), channel_id=1, source_target_pairs={{0,2},{1,3},{2,0},{3,1},{4,6},{5,7},{6,4},{7,5},{8,10},{9,11},{10,... | collective-permute-start | bytes 589832 | tf_op jit(solution)/shard_map/ppermute | solution.py:212
  57.1 3.1 %copy-start.3 = (f32[768,384]{1,0:T(8,128)S(1)}, f32[768,384]{1,0:T(8,128)}, u32[]{:S(2)}) copy-start(f32[768,384]{1,0:T(8,128)} %copy-done.2) | copy-start | bytes 3538948
  57.3 36.0 %collective-permute-start.7 = (f32[768,384]{1,0:T(8,128)S(1)}, f32[768,384]{1,0:T(8,128)S(1)}, u32[]{:S(2)}, u32[]{:S(2)}) collective-permute-start(f32[768,384]{1,0:T(8,128)S(1)} %broadcast_select_fusion.1), channel_id=1, source_target_pairs={{8,0},{16,24},{0,16},{24,8},{9,1},{17,25},{1,17},{25,9},{10,2},{18... | collective-permute-start | bytes 3538952 | tf_op jit(solution)/shard_map/ppermute | solution.py:200
  58.7 7.0 %collective-permute-start.16 = (f32[128,384]{1,0:T(8,128)S(1)}, f32[128,384]{1,0:T(8,128)S(1)}, u32[]{:S(2)}, u32[]{:S(2)}) collective-permute-start(f32[128,384]{1,0:T(8,128)S(1)} %get-tuple-element.87), channel_id=1, source_target_pairs={{0,4},{1,5},{2,6},{3,7},{4,0},{5,1},{6,2},{7,3},{8,12},{9,13},{10,... | collective-permute-start | bytes 589832 | tf_op jit(solution)/shard_map/ppermute | solution.py:212
  61.7 10.6 %collective-permute-start.14 = (f32[256,384]{1,0:T(8,128)S(1)}, f32[256,384]{1,0:T(8,128)S(1)}, u32[]{:S(2)}, u32[]{:S(2)}) collective-permute-start(f32[256,384]{1,0:T(8,128)S(1)} %get-tuple-element.78), channel_id=1, source_target_pairs={{0,2},{1,3},{2,0},{3,1},{4,6},{5,7},{6,4},{7,5},{8,10},{9,11},{10,... | collective-permute-start | bytes 1179656 | tf_op jit(solution)/shard_map/ppermute | solution.py:212
  62.3 10.6 %collective-permute-start.15 = (f32[256,384]{1,0:T(8,128)S(1)}, f32[256,384]{1,0:T(8,128)S(1)}, u32[]{:S(2)}, u32[]{:S(2)}) collective-permute-start(f32[256,384]{1,0:T(8,128)S(1)} %get-tuple-element.79), channel_id=1, source_target_pairs={{0,4},{1,5},{2,6},{3,7},{4,0},{5,1},{6,2},{7,3},{8,12},{9,13},{10,... | collective-permute-start | bytes 1179656 | tf_op jit(solution)/shard_map/ppermute | solution.py:212
  65.6 1.4 %collective-permute-start.18 = (f32[128,384]{1,0:T(8,128)S(1)}, f32[128,384]{1,0:T(8,128)S(1)}, u32[]{:S(2)}, u32[]{:S(2)}) collective-permute-start(f32[128,384]{1,0:T(8,128)S(1)} %fold.16), channel_id=1, source_target_pairs={{0,1},{1,0},{2,3},{3,2},{4,5},{5,4},{6,7},{7,6},{8,9},{9,8},{10,11... | collective-permute-start | bytes 589832 | tf_op jit(solution)/shard_map/ppermute | solution.py:212
  75.7 17.5 %collective-permute-start.19 = (f32[256,384]{1,0:T(8,128)S(1)}, f32[256,384]{1,0:T(8,128)S(1)}, u32[]{:S(2)}, u32[]{:S(2)}) collective-permute-start(f32[256,384]{1,0:T(8,128)S(1)} %get-tuple-element.90), channel_id=1, source_target_pairs={{0,2},{1,3},{2,0},{3,1},{4,6},{5,7},{6,4},{7,5},{8,10},{9,11},{10,... | collective-permute-start | bytes 1179656 | tf_op jit(solution)/shard_map/ppermute | solution.py:212
  76.8 16.5 %collective-permute-start.20 = (f32[256,384]{1,0:T(8,128)S(1)}, f32[256,384]{1,0:T(8,128)S(1)}, u32[]{:S(2)}, u32[]{:S(2)}) collective-permute-start(f32[256,384]{1,0:T(8,128)S(1)} %get-tuple-element.91), channel_id=1, source_target_pairs={{0,4},{1,5},{2,6},{3,7},{4,0},{5,1},{6,2},{7,3},{8,12},{9,13},{10,... | collective-permute-start | bytes 1179656 | tf_op jit(solution)/shard_map/ppermute | solution.py:212
  78.3 11.3 %collective-permute-start.22 = (f32[128,384]{1,0:T(8,128)S(1)}, f32[128,384]{1,0:T(8,128)S(1)}, u32[]{:S(2)}, u32[]{:S(2)}) collective-permute-start(f32[128,384]{1,0:T(8,128)S(1)} %get-tuple-element.100), channel_id=1, source_target_pairs={{0,2},{1,3},{2,0},{3,1},{4,6},{5,7},{6,4},{7,5},{8,10},{9,11},{10,... | collective-permute-start | bytes 589832 | tf_op jit(solution)/shard_map/ppermute | solution.py:212
  79.3 14.0 %collective-permute-start.21 = (f32[128,384]{1,0:T(8,128)S(1)}, f32[128,384]{1,0:T(8,128)S(1)}, u32[]{:S(2)}, u32[]{:S(2)}) collective-permute-start(f32[128,384]{1,0:T(8,128)S(1)} %get-tuple-element.99), channel_id=1, source_target_pairs={{0,4},{1,5},{2,6},{3,7},{4,0},{5,1},{6,2},{7,3},{8,12},{9,13},{10,... | collective-permute-start | bytes 589832 | tf_op jit(solution)/shard_map/ppermute | solution.py:212
  89.7 3.7 %collective-permute-start.23 = (f32[128,384]{1,0:T(8,128)S(1)}, f32[128,384]{1,0:T(8,128)S(1)}, u32[]{:S(2)}, u32[]{:S(2)}) collective-permute-start(f32[128,384]{1,0:T(8,128)S(1)} %fold.19), channel_id=1, source_target_pairs={{0,1},{1,0},{2,3},{3,2},{4,5},{5,4},{6,7},{7,6},{8,9},{9,8},{10,11... | collective-permute-start | bytes 589832 | tf_op jit(solution)/shard_map/ppermute | solution.py:212
  95.6 11.1 %collective-permute-start.26 = (f32[256,384]{1,0:T(8,128)S(1)}, f32[256,384]{1,0:T(8,128)S(1)}, u32[]{:S(2)}, u32[]{:S(2)}) collective-permute-start(f32[256,384]{1,0:T(8,128)S(1)} %get-tuple-element.103), channel_id=1, source_target_pairs={{0,4},{1,5},{2,6},{3,7},{4,0},{5,1},{6,2},{7,3},{8,12},{9,13},{10,... | collective-permute-start | bytes 1179656 | tf_op jit(solution)/shard_map/ppermute | solution.py:212
  97.2 16.3 %collective-permute-start.24 = (f32[256,384]{1,0:T(8,128)S(1)}, f32[256,384]{1,0:T(8,128)S(1)}, u32[]{:S(2)}, u32[]{:S(2)}) collective-permute-start(f32[256,384]{1,0:T(8,128)S(1)} %get-tuple-element.102), channel_id=1, source_target_pairs={{0,2},{1,3},{2,0},{3,1},{4,6},{5,7},{6,4},{7,5},{8,10},{9,11},{10,... | collective-permute-start | bytes 1179656 | tf_op jit(solution)/shard_map/ppermute | solution.py:212
  98.7 14.7 %collective-permute-start.30 = (f32[128,384]{1,0:T(8,128)S(1)}, f32[128,384]{1,0:T(8,128)S(1)}, u32[]{:S(2)}, u32[]{:S(2)}) collective-permute-start(f32[128,384]{1,0:T(8,128)S(1)} %get-tuple-element.112), channel_id=1, source_target_pairs={{0,2},{1,3},{2,0},{3,1},{4,6},{5,7},{6,4},{7,5},{8,10},{9,11},{10,... | collective-permute-start | bytes 589832 | tf_op jit(solution)/shard_map/ppermute | solution.py:212
  106.7 9.6 %collective-permute-start.27 = (f32[128,384]{1,0:T(8,128)S(1)}, f32[128,384]{1,0:T(8,128)S(1)}, u32[]{:S(2)}, u32[]{:S(2)}) collective-permute-start(f32[128,384]{1,0:T(8,128)S(1)} %get-tuple-element.110), channel_id=1, source_target_pairs={{0,2},{1,3},{2,0},{3,1},{4,6},{5,7},{6,4},{7,5},{8,10},{9,11},{10,... | collective-permute-start | bytes 589832 | tf_op jit(solution)/shard_map/ppermute | solution.py:212
  108.3 8.2 %collective-permute-start.29 = (f32[128,384]{1,0:T(8,128)S(1)}, f32[128,384]{1,0:T(8,128)S(1)}, u32[]{:S(2)}, u32[]{:S(2)}) collective-permute-start(f32[128,384]{1,0:T(8,128)S(1)} %get-tuple-element.111), channel_id=1, source_target_pairs={{0,4},{1,5},{2,6},{3,7},{4,0},{5,1},{6,2},{7,3},{8,12},{9,13},{10,... | collective-permute-start | bytes 589832 | tf_op jit(solution)/shard_map/ppermute | solution.py:212
  113.4 3.0 %collective-permute-start.31 = (f32[128,384]{1,0:T(8,128)S(1)}, f32[128,384]{1,0:T(8,128)S(1)}, u32[]{:S(2)}, u32[]{:S(2)}) collective-permute-start(f32[128,384]{1,0:T(8,128)S(1)} %fold.23), channel_id=1, source_target_pairs={{0,1},{1,0},{2,3},{3,2},{4,5},{5,4},{6,7},{7,6},{8,9},{9,8},{10,11... | collective-permute-start | bytes 589832 | tf_op jit(solution)/shard_map/ppermute | solution.py:212
  113.6 7.4 %collective-permute-start.25 = (f32[128,384]{1,0:T(8,128)S(1)}, f32[128,384]{1,0:T(8,128)S(1)}, u32[]{:S(2)}, u32[]{:S(2)}) collective-permute-start(f32[128,384]{1,0:T(8,128)S(1)} %get-tuple-element.107), channel_id=1, source_target_pairs={{0,4},{1,5},{2,6},{3,7},{4,0},{5,1},{6,2},{7,3},{8,12},{9,13},{10,... | collective-permute-start | bytes 589832 | tf_op jit(solution)/shard_map/ppermute | solution.py:212
  116.4 4.5 %collective-permute-start.28 = (f32[128,384]{1,0:T(8,128)S(1)}, f32[128,384]{1,0:T(8,128)S(1)}, u32[]{:S(2)}, u32[]{:S(2)}) collective-permute-start(f32[128,384]{1,0:T(8,128)S(1)} %fold.22), channel_id=1, source_target_pairs={{0,1},{1,0},{2,3},{3,2},{4,5},{5,4},{6,7},{7,6},{8,9},{9,8},{10,11... | collective-permute-start | bytes 589832 | tf_op jit(solution)/shard_map/ppermute | solution.py:212

commit v10 on v9

--- a/solution.py
+++ b/solution.py
@@ -216,7 +216,6 @@
     parts = cut(after(amp_mask, mine), amplitudes, groups, depth)
     (whole,) = kernel_call(join_kernel, [(depth, half)], [mine, after(other, *parts)], "join")
     blocks = line_blocks(whole, n_occ)
-    arrived = [block[2] if isinstance(block, tuple) else block for _, block, _ in blocks]
 
     rel = [[parts[0]] + [None] * (groups - 1), [None] * groups]
     for r in range(groups - 1, 0, -1):
@@ -233,21 +232,17 @@
 
     out = None
     token = None
+    settled = []
     for n, (d, block, offset) in enumerate(blocks):
         if isinstance(block, tuple):
             middle, centre, far = block
             centre, far = lax.optimization_barrier((centre, far, *sent))[:2]
             block = jnp.where(middle, centre, far)
-        if n == 0:
-            block = after(block, blocks[1][1], *(blocks[2][1][1:2] if isinstance(blocks[2][1], tuple) else ()))
-        else:
+        if n > 0:
             block = after(block, *token)
         sent = products([[rel[h][r] for r in away[h]] for h in range(2)], block)
         moving = [swap(sent[h], 2 * orders[h][0]) for h in range(2)]
-        soon = arrived[2:3] if n == 1 else []
-        if n == 2:
-            moving = list(lax.optimization_barrier((*moving, *arrived[3:4]))[:2])
-        held = list(products([[rel[h][r] for r in near[h]] for h in range(2)], after(block, *sent, *soon)))
+        held = list(products([[rel[h][r] for r in near[h]] for h in range(2)], after(block, *sent, *settled)))
         names = [near[0], near[1]]
         for level in range(1, len(bits)):
             for h in (1, 0):
@@ -258,6 +253,7 @@
                 moving[h] = swap(moved, 2 * bit)
                 names[h] = [names[h][i] for i in stays]
         token = held if out is None else [*held, out]
+        settled = moving
         (theirs,) = fold(rows, [0], [], held[1], moving[1])
         out = write(out, (rows, n_occ * width), d, half, offset, held[0], moving[0], swap(theirs, 1))
     return out

time: 122 us -> 119 us (0.975)
  Pallas kernels: 24.6 us -> 20.5 us
    ppermute x28, waiting for transfers between devices: 50.4 us -> 54.8 us  [swap(): return lax.ppermute(x, 'vir', [(i, i ^ bits) for i in range(n_vir)])]
    pallas_call x23, Pallas kernels: 21.4 us -> 17.3 us  [kernel_call(): pl.pallas_call(body, out_shape=[pltpu.VMEM(shape, jnp.float32) for shape...]
    ppermute x1, starting transfers between devices: 5.76 us -> 3.01 us  [direct(): return lax.ppermute(x, 'occ', [(i, i ^ d) for i in range(nodes)])]
    ppermute x1, starting transfers between devices: 3.25 us -> 5.66 us  [line_blocks(): far = lax.ppermute(after(own, centre, near), 'occ', [(0, 3), (3, 0)])]
    ppermute x1, waiting for transfers between devices: 1.95 us -> 0.01 us  [line_blocks(): far = lax.ppermute(after(own, centre, near), 'occ', [(0, 3), (3, 0)])]
  transfers between devices with their start and end apart: 32 -> 32, of which waited for: 14 -> 12; matrix products, arithmetic and copies ran while one was open for 1% -> 1% of each run, Pallas kernels for 17% -> 14%
where the time goes in v10:
time: 119 us; the launch traced here: 118 us
  waiting for transfers between devices  60.5 us (51%)
  starting transfers between devices  34.5 us (29%)
  Pallas kernels  20.5 us (17%)
  other arithmetic  1.53 us (1%)
    ppermute x28, waiting for transfers between devices, swap(): return lax.ppermute(x, 'vir', [(i, i ^ bits) for i in range(n_vir)])  54.8 us
    ppermute x28, starting transfers between devices, swap(): return lax.ppermute(x, 'vir', [(i, i ^ bits) for i in range(n_vir)])  24 us
    pallas_call x23, Pallas kernels, kernel_call(): pl.pallas_call(body, out_shape=[pltpu.VMEM(shape, jnp.float32) for shape...  17.3 us
    ppermute x1, starting transfers between devices, line_blocks(): far = lax.ppermute(after(own, centre, near), 'occ', [(0, 3), (3, 0)])  5.66 us
    ppermute x1, waiting for transfers between devices, direct(): return lax.ppermute(x, 'occ', [(i, i ^ d) for i in range(nodes)])  5.65 us
    pallas_call x4, Pallas kernels, write(): pl.pallas_call(functools.partial(write_kernel, d, half, offset), out_shap...  3.13 us
    ppermute x1, starting transfers between devices, direct(): return lax.ppermute(x, 'occ', [(i, i ^ d) for i in range(nodes)])  3.01 us
  transfers between devices with their start and end apart: 32, of which 12 were waited for; matrix products, arithmetic and copies ran while one was open for 1% of the time, Pallas kernels for 14%

profile of v10, /device:TPU:0, one launch (start us, length us, event | category | flops | bytes accessed | tf_op | source)
XLA Modules:
  0.0 118.5 jit_solution(1356730646185831799)
XLA Ops:
  0.0 1.3 %halves.1 = (f32[384,384]{1,0:T(8,128)S(1)}, f32[384,384]{1,0:T(8,128)S(1)}) custom-call(s32[3,6]{1,0:T(4,128)} %mask_hbm.1, f32[384,768]{1,0:T(8,128)} %int_hbm.1), custom_call_target="tpu_custom_call" | custom-call | flops 1 | bytes 1 | tf_op jit(solution)/shard_map/halves/pallas_call | solution.py:30
  1.3 0.5 collective-permute-start.5
  1.8 1.4 %cut.1 = (f32[128,768]{1,0:T(8,128)S(1)}, f32[128,768]{1,0:T(8,128)S(1)}, f32[128,768]{1,0:T(8,128)S(1)}, f32[128,768]{1,0:T(8,128)S(1)}) custom-call(s32[4,24]{1,0:T(4,128)} %mask_hbm.2, f32[128,3072]{1,0:T(8,128)} %amp_hbm.1), custom_call_target="tpu_custom_call" | custom-call | flops 1 | bytes 1 | tf_op jit(solution)/shard_map/cut/pallas_call | solution.py:30
  3.3 0.2 collective-permute-done.5.other_ref
  3.5 0.1 join.1.refs_4_
  3.6 3.0 %collective-permute-start.8 = (f32[768,384]{1,0:T(8,128)S(1)}, f32[768,384]{1,0:T(8,128)S(1)}, u32[]{:S(2)}, u32[]{:S(2)}) collective-permute-start(f32[768,384]{1,0:T(8,128)S(1)} %join.1.refs_4_), channel_id=1, source_target_pairs={{0,8},{8,0},{16,24},{24,16},{1,9},{9,1},{17,25},{25,17},{2,10},{10... | collective-permute-start | bytes 3538952 | tf_op jit(solution)/shard_map/ppermute | solution.py:192
  6.6 0.7 collective-permute-start.6
  7.3 1.6 %collective-permute-start = (f32[128,768]{1,0:T(8,128)S(1)}, f32[128,768]{1,0:T(8,128)S(1)}, u32[]{:S(2)}, u32[]{:S(2)}) collective-permute-start(f32[128,768]{1,0:T(8,128)S(1)} %get-tuple-element.59), channel_id=1, source_target_pairs={{0,4},{1,5},{2,6},{3,7},{4,0},{5,1},{6,2},{7,3},{8,12},{9,13},{10,... | collective-permute-start | bytes 1179656 | tf_op jit(solution)/shard_map/ppermute | solution.py:212
  8.9 1.4 %collective-permute-start.1 = (f32[128,768]{1,0:T(8,128)S(1)}, f32[128,768]{1,0:T(8,128)S(1)}, u32[]{:S(2)}, u32[]{:S(2)}) collective-permute-start(f32[128,768]{1,0:T(8,128)S(1)} %get-tuple-element.60), channel_id=1, source_target_pairs={{0,6},{1,7},{2,4},{3,5},{4,2},{5,3},{6,0},{7,1},{8,14},{9,15},{10,... | collective-permute-start | bytes 1179656 | tf_op jit(solution)/shard_map/ppermute | solution.py:212
  10.3 0.5 collective-permute-start.3
  10.9 15.8 %collective-permute-done.refs_1_ = f32[128,768]{1,0:T(8,128)S(1)} collective-permute-done((f32[128,768]{1,0:T(8,128)S(1)}, f32[128,768]{1,0:T(8,128)S(1)}, u32[]{:S(2)}, u32[]{:S(2)}) %collective-permute-start) | collective-permute-done | bytes 393248 | tf_op jit(solution)/shard_map/ppermute | solution.py:212
  26.7 0.0 collective-permute-start.10
  26.7 0.5 collective-permute-start.11
  27.2 5.7 %collective-permute-done.8.refs_4_ = f32[768,384]{1,0:T(8,128)S(1)} collective-permute-done((f32[768,384]{1,0:T(8,128)S(1)}, f32[768,384]{1,0:T(8,128)S(1)}, u32[]{:S(2)}, u32[]{:S(2)}) %collective-permute-start.8) | collective-permute-done | bytes 1179680 | tf_op jit(solution)/shard_map/ppermute | solution.py:192
  32.8 1.0 copy-done.4
  33.9 5.7 %collective-permute-start.9 = (f32[768,384]{1,0:T(8,128)S(1)}, f32[768,384]{1,0:T(8,128)}, u32[]{:S(2)}, u32[]{:S(2)}) collective-permute-start(f32[768,384]{1,0:T(8,128)S(1)} %join.1.refs_4_), channel_id=1, source_target_pairs={{0,24},{24,0},{1,25},{25,1},{2,26},{26,2},{3,27},{27,3},{4,28},{28... | collective-permute-start | bytes 3538952 | tf_op jit(solution)/shard_map/ppermute | solution.py:198
  39.5 0.1 collective-permute-start.2
  39.6 0.0 collective-permute-done.3.refs_0_
  39.6 0.5 collective-permute-start.4
  40.1 2.2 %products.8 = (f32[256,384]{1,0:T(8,128)}, f32[256,384]{1,0:T(8,128)}) custom-call(f32[128,768]{1,0:T(8,128)S(1)} %collective-permute-done.3.refs_0_, f32[128,768]{1,0:T(8,128)S(1)} %collective-permute-done.1.refs_1_, f32[128,768]{1,0:T(8,128)S(1)} %collective-permute-done.10.refs_2_, f32[128,768]{1,0:T(8,128)S(1)} %collective-permute-done.11.refs_3_, ...), custom_call_target="tpu_custom_call" | custom-call | flops 1 | bytes 1 | tf_op jit(solution)/shard_map/products/pallas_call | solution.py:30
  42.3 1.6 %collective-permute-start.13 = (f32[256,384]{1,0:T(8,128)}, f32[256,384]{1,0:T(8,128)}, u32[]{:S(2)}, u32[]{:S(2)}) collective-permute-start(f32[256,384]{1,0:T(8,128)} %get-tuple-element.67), channel_id=1, source_target_pairs={{0,4},{1,5},{2,6},{3,7},{4,0},{5,1},{6,2},{7,3},{8,12},{9,13},{10,... | collective-permute-start | bytes 1179656 | tf_op jit(solution)/shard_map/ppermute | solution.py:212
  43.9 1.5 %collective-permute-start.12 = (f32[256,384]{1,0:T(8,128)}, f32[256,384]{1,0:T(8,128)}, u32[]{:S(2)}, u32[]{:S(2)}) collective-permute-start(f32[256,384]{1,0:T(8,128)} %get-tuple-element.66), channel_id=1, source_target_pairs={{0,2},{1,3},{2,0},{3,1},{4,6},{5,7},{6,4},{7,5},{8,10},{9,11},{10,... | collective-permute-start | bytes 1179656 | tf_op jit(solution)/shard_map/ppermute | solution.py:212
  45.4 1.4 %products.9 = (f32[256,384]{1,0:T(8,128)S(1)}, f32[256,384]{1,0:T(8,128)S(1)}) custom-call(f32[128,768]{1,0:T(8,128)S(1)} %get-tuple-element.61.refs_0_, f32[128,768]{1,0:T(8,128)S(1)} %collective-permute-done.refs_1_, f32[128,768]{1,0:T(8,128)S(1)} %collective-permute-done.2.refs_2_, f32[128,768]{1,0:T(8,128)S(1)} %collective-permute-done.4.refs_3_, ...), custom_call_target="tpu_custom_call" | custom-call | flops 1 | bytes 1 | tf_op jit(solution)/shard_map/products/pallas_call | solution.py:30
  46.8 7.0 %collective-permute-done.13.got_ref = f32[256,384]{1,0:T(8,128)} collective-permute-done((f32[256,384]{1,0:T(8,128)}, f32[256,384]{1,0:T(8,128)}, u32[]{:S(2)}, u32[]{:S(2)}) %collective-permute-start.13) | collective-permute-done | bytes 393248 | tf_op jit(solution)/shard_map/ppermute | solution.py:212
  53.8 1.0 fold.13
  54.9 1.6 %collective-permute-start.15 = (f32[128,384]{1,0:T(8,128)S(1)}, f32[128,384]{1,0:T(8,128)S(1)}, u32[]{:S(2)}, u32[]{:S(2)}) collective-permute-start(f32[128,384]{1,0:T(8,128)S(1)} %get-tuple-element.79), channel_id=1, source_target_pairs={{0,2},{1,3},{2,0},{3,1},{4,6},{5,7},{6,4},{7,5},{8,10},{9,11},{10,... | collective-permute-start | bytes 589832 | tf_op jit(solution)/shard_map/ppermute | solution.py:212
  56.4 0.1 broadcast_select_fusion.1
  56.6 1.1 collective-permute-start.7
  57.6 1.1 fold.12
  58.7 1.6 %collective-permute-start.14 = (f32[128,384]{1,0:T(8,128)S(1)}, f32[128,384]{1,0:T(8,128)S(1)}, u32[]{:S(2)}, u32[]{:S(2)}) collective-permute-start(f32[128,384]{1,0:T(8,128)S(1)} %get-tuple-element.78), channel_id=1, source_target_pairs={{0,4},{1,5},{2,6},{3,7},{4,0},{5,1},{6,2},{7,3},{8,12},{9,13},{10,... | collective-permute-start | bytes 589832 | tf_op jit(solution)/shard_map/ppermute | solution.py:212
  60.3 1.4 %products.10 = (f32[256,384]{1,0:T(8,128)S(1)}, f32[256,384]{1,0:T(8,128)S(1)}) custom-call(f32[128,768]{1,0:T(8,128)S(1)} %collective-permute-done.3.refs_0_, f32[128,768]{1,0:T(8,128)S(1)} %collective-permute-done.1.refs_1_, f32[128,768]{1,0:T(8,128)S(1)} %copy-done.1, f32[128,768]{1,0:T(8,128)S(1)} %copy-done.3, f32[768,384]{1,0:T(8,128)S(1)} %copy-done.5), custom_call_target="tpu_custom_call" | custom-call | flops 1 | bytes 1 | tf_op jit(solution)/shard_map/products/pallas_call | solution.py:30
  61.7 0.6 collective-permute-start.17
  62.3 0.5 collective-permute-start.16
  62.8 3.4 %collective-permute-done.14.got_ref = f32[128,384]{1,0:T(8,128)S(1)} collective-permute-done((f32[128,384]{1,0:T(8,128)S(1)}, f32[128,384]{1,0:T(8,128)S(1)}, u32[]{:S(2)}, u32[]{:S(2)}) %collective-permute-start.14) | collective-permute-done | bytes 196640 | tf_op jit(solution)/shard_map/ppermute | solution.py:212
  66.2 1.4 %collective-permute-done.18.other_ref = f32[128,384]{1,0:T(8,128)S(1)} collective-permute-done((f32[128,384]{1,0:T(8,128)S(1)}, f32[128,384]{1,0:T(8,128)S(1)}, u32[]{:S(2)}, u32[]{:S(2)}) %collective-permute-start.18) | collective-permute-done | bytes 196640 | tf_op jit(solution)/shard_map/ppermute | solution.py:212
  67.7 0.8 write.4.refs_0_
  68.4 1.4 %products.11 = (f32[256,384]{1,0:T(8,128)S(1)}, f32[256,384]{1,0:T(8,128)S(1)}) custom-call(f32[128,768]{1,0:T(8,128)S(1)} %get-tuple-element.61.refs_0_, f32[128,768]{1,0:T(8,128)S(1)} %collective-permute-done.refs_1_, f32[128,768]{1,0:T(8,128)S(1)} %collective-permute-done.2.refs_2_, f32[128,768]{1,0:T(8,128)S(1)} %collective-permute-done.4.refs_3_, ...), custom_call_target="tpu_custom_call" | custom-call | flops 1 | bytes 1 | tf_op jit(solution)/shard_map/products/pallas_call | solution.py:30
  69.9 3.0 %collective-permute-done.17.got_ref = f32[256,384]{1,0:T(8,128)S(1)} collective-permute-done((f32[256,384]{1,0:T(8,128)S(1)}, f32[256,384]{1,0:T(8,128)S(1)}, u32[]{:S(2)}, u32[]{:S(2)}) %collective-permute-start.17) | collective-permute-done | bytes 393248 | tf_op jit(solution)/shard_map/ppermute | solution.py:212
  72.9 0.6 collective-permute-start.20
  73.5 1.4 %broadcast_select_fusion.refs_4_ = f32[768,384]{1,0:T(8,128)S(1)} fusion(f32[768,384]{1,0:T(8,128)S(1)} %copy-done.7, f32[768,384]{1,0:T(8,128)} %collective-permute-done.9, pred[]{:T(512)S(6)} %or.3), kind=kLoop, calls=%fused_computation | loop fusion | flops 294912 | bytes 3538945 | tf_op jit(solution)/shard_map/jit(_where)/select_n | solution.py:240
  74.9 1.4 %products.12 = (f32[256,384]{1,0:T(8,128)S(1)}, f32[256,384]{1,0:T(8,128)S(1)}) custom-call(f32[128,768]{1,0:T(8,128)S(1)} %collective-permute-done.3.refs_0_, f32[128,768]{1,0:T(8,128)S(1)} %collective-permute-done.1.refs_1_, f32[128,768]{1,0:T(8,128)S(1)} %copy-done.1, f32[128,768]{1,0:T(8,128)S(1)} %copy-done.3, f32[768,384]{1,0:T(8,128)S(1)} %broadcast_select_fusion.refs_4_), custom_call_target="tpu_custom_call" | custom-call | flops 1 | bytes 1 | tf_op jit(solution)/shard_map/products/pallas_call | solution.py:30
  76.4 1.6 %collective-permute-start.21 = (f32[256,384]{1,0:T(8,128)S(1)}, f32[256,384]{1,0:T(8,128)S(1)}, u32[]{:S(2)}, u32[]{:S(2)}) collective-permute-start(f32[256,384]{1,0:T(8,128)S(1)} %get-tuple-element.86), channel_id=1, source_target_pairs={{0,2},{1,3},{2,0},{3,1},{4,6},{5,7},{6,4},{7,5},{8,10},{9,11},{10,... | collective-permute-start | bytes 1179656 | tf_op jit(solution)/shard_map/ppermute | solution.py:212
  77.9 1.3 %collective-permute-start.22 = (f32[256,384]{1,0:T(8,128)S(1)}, f32[256,384]{1,0:T(8,128)S(1)}, u32[]{:S(2)}, u32[]{:S(2)}) collective-permute-start(f32[256,384]{1,0:T(8,128)S(1)} %get-tuple-element.87), channel_id=1, source_target_pairs={{0,4},{1,5},{2,6},{3,7},{4,0},{5,1},{6,2},{7,3},{8,12},{9,13},{10,... | collective-permute-start | bytes 1179656 | tf_op jit(solution)/shard_map/ppermute | solution.py:212
  79.2 0.8 collective-permute-start.19
  80.0 0.3 collective-permute-done.20.got_ref
  80.3 0.1 collective-permute-start.23
  80.3 10.6 %collective-permute-done.19.got_ref = f32[128,384]{1,0:T(8,128)S(1)} collective-permute-done((f32[128,384]{1,0:T(8,128)S(1)}, f32[128,384]{1,0:T(8,128)S(1)}, u32[]{:S(2)}, u32[]{:S(2)}) %collective-permute-start.19) | collective-permute-done | bytes 196640 | tf_op jit(solution)/shard_map/ppermute | solution.py:212
  90.9 1.4 %products.13 = (f32[256,384]{1,0:T(8,128)S(1)}, f32[256,384]{1,0:T(8,128)S(1)}) custom-call(f32[128,768]{1,0:T(8,128)S(1)} %get-tuple-element.61.refs_0_, f32[128,768]{1,0:T(8,128)S(1)} %collective-permute-done.refs_1_, f32[128,768]{1,0:T(8,128)S(1)} %collective-permute-done.2.refs_2_, f32[128,768]{1,0:T(8,128)S(1)} %collective-permute-done.4.refs_3_, ...), custom_call_target="tpu_custom_call" | custom-call | flops 1 | bytes 1 | tf_op jit(solution)/shard_map/products/pallas_call | solution.py:30
  92.3 0.8 write.5.refs_0_
  93.3 1.4 %products.14 = (f32[256,384]{1,0:T(8,128)S(1)}, f32[256,384]{1,0:T(8,128)S(1)}) custom-call(f32[128,768]{1,0:T(8,128)S(1)} %collective-permute-done.3.refs_0_, f32[128,768]{1,0:T(8,128)S(1)} %collective-permute-done.1.refs_1_, f32[128,768]{1,0:T(8,128)S(1)} %copy-done.1, f32[128,768]{1,0:T(8,128)S(1)} %copy-done.3, f32[768,384]{1,0:T(8,128)S(1)} %collective-permute-done.7.refs_4_), custom_call_target="tpu_custom_call" | custom-call | flops 1 | bytes 1 | tf_op jit(solution)/shard_map/products/pallas_call | solution.py:30
  94.7 0.8 collective-permute-start.28
  95.5 1.3 %collective-permute-start.24 = (f32[128,384]{1,0:T(8,128)S(1)}, f32[128,384]{1,0:T(8,128)S(1)}, u32[]{:S(2)}, u32[]{:S(2)}) collective-permute-start(f32[128,384]{1,0:T(8,128)S(1)} %get-tuple-element.98), channel_id=1, source_target_pairs={{0,4},{1,5},{2,6},{3,7},{4,0},{5,1},{6,2},{7,3},{8,12},{9,13},{10,... | collective-permute-start | bytes 589832 | tf_op jit(solution)/shard_map/ppermute | solution.py:212
  96.8 0.5 collective-permute-start.25
  97.3 1.5 %collective-permute-start.26 = (f32[256,384]{1,0:T(8,128)S(1)}, f32[256,384]{1,0:T(8,128)S(1)}, u32[]{:S(2)}, u32[]{:S(2)}) collective-permute-start(f32[256,384]{1,0:T(8,128)S(1)} %get-tuple-element.96), channel_id=1, source_target_pairs={{0,2},{1,3},{2,0},{3,1},{4,6},{5,7},{6,4},{7,5},{8,10},{9,11},{10,... | collective-permute-start | bytes 1179656 | tf_op jit(solution)/shard_map/ppermute | solution.py:212
  98.8 8.3 %collective-permute-done.24.got_ref = f32[128,384]{1,0:T(8,128)S(1)} collective-permute-done((f32[128,384]{1,0:T(8,128)S(1)}, f32[128,384]{1,0:T(8,128)S(1)}, u32[]{:S(2)}, u32[]{:S(2)}) %collective-permute-start.24) | collective-permute-done | bytes 196640 | tf_op jit(solution)/shard_map/ppermute | solution.py:212
  107.1 1.4 %products.15 = (f32[256,384]{1,0:T(8,128)S(1)}, f32[256,384]{1,0:T(8,128)S(1)}) custom-call(f32[128,768]{1,0:T(8,128)S(1)} %get-tuple-element.61.refs_0_, f32[128,768]{1,0:T(8,128)S(1)} %collective-permute-done.refs_1_, f32[128,768]{1,0:T(8,128)S(1)} %collective-permute-done.2.refs_2_, f32[128,768]{1,0:T(8,128)S(1)} %collective-permute-done.4.refs_3_, ...), custom_call_target="tpu_custom_call" | custom-call | flops 1 | bytes 1 | tf_op jit(solution)/shard_map/products/pallas_call | solution.py:30
  108.6 1.5 %collective-permute-start.29 = (f32[128,384]{1,0:T(8,128)S(1)}, f32[128,384]{1,0:T(8,128)S(1)}, u32[]{:S(2)}, u32[]{:S(2)}) collective-permute-start(f32[128,384]{1,0:T(8,128)S(1)} %get-tuple-element.106), channel_id=1, source_target_pairs={{0,2},{1,3},{2,0},{3,1},{4,6},{5,7},{6,4},{7,5},{8,10},{9,11},{10,... | collective-permute-start | bytes 589832 | tf_op jit(solution)/shard_map/ppermute | solution.py:212
  110.1 0.1 collective-permute-start.31
  110.2 1.6 %collective-permute-start.27 = (f32[128,384]{1,0:T(8,128)S(1)}, f32[128,384]{1,0:T(8,128)S(1)}, u32[]{:S(2)}, u32[]{:S(2)}) collective-permute-start(f32[128,384]{1,0:T(8,128)S(1)} %get-tuple-element.103), channel_id=1, source_target_pairs={{0,4},{1,5},{2,6},{3,7},{4,0},{5,1},{6,2},{7,3},{8,12},{9,13},{10,... | collective-permute-start | bytes 589832 | tf_op jit(solution)/shard_map/ppermute | solution.py:212
  111.8 2.5 %collective-permute-done.29.got_ref = f32[128,384]{1,0:T(8,128)S(1)} collective-permute-done((f32[128,384]{1,0:T(8,128)S(1)}, f32[128,384]{1,0:T(8,128)S(1)}, u32[]{:S(2)}, u32[]{:S(2)}) %collective-permute-start.29) | collective-permute-done | bytes 196640 | tf_op jit(solution)/shard_map/ppermute | solution.py:212
  114.3 0.1 collective-permute-start.30
  114.4 0.8 write.6.refs_0_
  115.2 2.4 %collective-permute-done.27.got_ref = f32[128,384]{1,0:T(8,128)S(1)} collective-permute-done((f32[128,384]{1,0:T(8,128)S(1)}, f32[128,384]{1,0:T(8,128)S(1)}, u32[]{:S(2)}, u32[]{:S(2)}) %collective-permute-start.27) | collective-permute-done | bytes 196640 | tf_op jit(solution)/shard_map/ppermute | solution.py:212
  117.6 0.8 write.7
  (45 shorter events, 0.4 us)
Async XLA Ops:
  1.3 2.1 %collective-permute-start.5 = (f32[384,384]{1,0:T(8,128)S(1)}, f32[384,384]{1,0:T(8,128)S(1)}, u32[]{:S(2)}, u32[]{:S(2)}) collective-permute-start(f32[384,384]{1,0:T(8,128)S(1)} %get-tuple-element.63), channel_id=1, source_target_pairs={{0,1},{1,0},{2,3},{3,2},{4,5},{5,4},{6,7},{7,6},{8,9},{9,8},{10,11... | collective-permute-start | bytes 1769480 | tf_op jit(solution)/shard_map/ppermute | solution.py:212
  3.6 29.3 %collective-permute-start.8 = (f32[768,384]{1,0:T(8,128)S(1)}, f32[768,384]{1,0:T(8,128)S(1)}, u32[]{:S(2)}, u32[]{:S(2)}) collective-permute-start(f32[768,384]{1,0:T(8,128)S(1)} %join.1.refs_4_), channel_id=1, source_target_pairs={{0,8},{8,0},{16,24},{24,16},{1,9},{9,1},{17,25},{25,17},{2,10},{10... | collective-permute-start | bytes 3538952 | tf_op jit(solution)/shard_map/ppermute | solution.py:192
  6.6 27.3 %collective-permute-start.6 = (f32[768,384]{1,0:T(8,128)S(1)}, f32[768,384]{1,0:T(8,128)S(1)}, u32[]{:S(2)}, u32[]{:S(2)}) collective-permute-start(f32[768,384]{1,0:T(8,128)S(1)} %join.1.refs_4_), channel_id=1, source_target_pairs={{8,16},{16,8},{9,17},{17,9},{10,18},{18,10},{11,19},{19,11},{12,20... | collective-permute-start | bytes 3538952 | tf_op jit(solution)/shard_map/ppermute | solution.py:196
  7.3 19.4 %collective-permute-start = (f32[128,768]{1,0:T(8,128)S(1)}, f32[128,768]{1,0:T(8,128)S(1)}, u32[]{:S(2)}, u32[]{:S(2)}) collective-permute-start(f32[128,768]{1,0:T(8,128)S(1)} %get-tuple-element.59), channel_id=1, source_target_pairs={{0,4},{1,5},{2,6},{3,7},{4,0},{5,1},{6,2},{7,3},{8,12},{9,13},{10,... | collective-permute-start | bytes 1179656 | tf_op jit(solution)/shard_map/ppermute | solution.py:212
  8.9 17.8 %collective-permute-start.1 = (f32[128,768]{1,0:T(8,128)S(1)}, f32[128,768]{1,0:T(8,128)S(1)}, u32[]{:S(2)}, u32[]{:S(2)}) collective-permute-start(f32[128,768]{1,0:T(8,128)S(1)} %get-tuple-element.60), channel_id=1, source_target_pairs={{0,6},{1,7},{2,4},{3,5},{4,2},{5,3},{6,0},{7,1},{8,14},{9,15},{10,... | collective-permute-start | bytes 1179656 | tf_op jit(solution)/shard_map/ppermute | solution.py:212
  10.3 29.3 %collective-permute-start.3 = (f32[128,768]{1,0:T(8,128)S(1)}, f32[128,768]{1,0:T(8,128)S(1)}, u32[]{:S(2)}, u32[]{:S(2)}) collective-permute-start(f32[128,768]{1,0:T(8,128)S(1)} %get-tuple-element.62), channel_id=1, source_target_pairs={{0,2},{1,3},{2,0},{3,1},{4,6},{5,7},{6,4},{7,5},{8,10},{9,11},{10,... | collective-permute-start | bytes 1179656 | tf_op jit(solution)/shard_map/ppermute | solution.py:212
  26.7 13.5 %collective-permute-start.10 = (f32[128,768]{1,0:T(8,128)S(1)}, f32[128,768]{1,0:T(8,128)S(1)}, u32[]{:S(2)}, u32[]{:S(2)}) collective-permute-start(f32[128,768]{1,0:T(8,128)S(1)} %collective-permute-done.refs_1_), channel_id=1, source_target_pairs={{0,1},{1,0},{2,3},{3,2},{4,5},{5,4},{6,7},{7,6},{8,9},{9,8},{10,11... | collective-permute-start | bytes 1179656 | tf_op jit(solution)/shard_map/ppermute | solution.py:212
  26.7 13.5 %collective-permute-start.11 = (f32[128,768]{1,0:T(8,128)S(1)}, f32[128,768]{1,0:T(8,128)S(1)}, u32[]{:S(2)}, u32[]{:S(2)}) collective-permute-start(f32[128,768]{1,0:T(8,128)S(1)} %collective-permute-done.1.refs_1_), channel_id=1, source_target_pairs={{0,1},{1,0},{2,3},{3,2},{4,5},{5,4},{6,7},{7,6},{8,9},{9,8},{10,11... | collective-permute-start | bytes 1179656 | tf_op jit(solution)/shard_map/ppermute | solution.py:212
  32.8 1.0 copy-start.4
  33.9 8.4 %copy-start.6 = (f32[768,384]{1,0:T(8,128)}, f32[768,384]{1,0:T(8,128)S(1)}, u32[]{:S(2)}) copy-start(f32[768,384]{1,0:T(8,128)S(1)} %collective-permute-done.6) | copy-start | bytes 3538948
  33.9 39.7 %collective-permute-start.9 = (f32[768,384]{1,0:T(8,128)S(1)}, f32[768,384]{1,0:T(8,128)}, u32[]{:S(2)}, u32[]{:S(2)}) collective-permute-start(f32[768,384]{1,0:T(8,128)S(1)} %join.1.refs_4_), channel_id=1, source_target_pairs={{0,24},{24,0},{1,25},{25,1},{2,26},{26,2},{3,27},{27,3},{4,28},{28... | collective-permute-start | bytes 3538952 | tf_op jit(solution)/shard_map/ppermute | solution.py:198
  39.5 5.9 %collective-permute-start.2 = (f32[128,768]{1,0:T(8,128)S(1)}, f32[128,768]{1,0:T(8,128)S(1)}, u32[]{:S(2)}, u32[]{:S(2)}) collective-permute-start(f32[128,768]{1,0:T(8,128)S(1)} %get-tuple-element.61.refs_0_), channel_id=1, source_target_pairs={{0,1},{1,0},{2,3},{3,2},{4,5},{5,4},{6,7},{7,6},{8,9},{9,8},{10,11... | collective-permute-start | bytes 1179656 | tf_op jit(solution)/shard_map/ppermute | solution.py:212
  39.6 5.8 %collective-permute-start.4 = (f32[128,768]{1,0:T(8,128)S(1)}, f32[128,768]{1,0:T(8,128)S(1)}, u32[]{:S(2)}, u32[]{:S(2)}) collective-permute-start(f32[128,768]{1,0:T(8,128)S(1)} %collective-permute-done.3.refs_0_), channel_id=1, source_target_pairs={{0,1},{1,0},{2,3},{3,2},{4,5},{5,4},{6,7},{7,6},{8,9},{9,8},{10,11... | collective-permute-start | bytes 1179656 | tf_op jit(solution)/shard_map/ppermute | solution.py:212
  40.1 2.2 %copy-start = (f32[128,768]{1,0:T(8,128)}, f32[128,768]{1,0:T(8,128)S(1)}, u32[]{:S(2)}) copy-start(f32[128,768]{1,0:T(8,128)S(1)} %collective-permute-done.10.refs_2_) | copy-start | bytes 1179652
  40.1 2.2 %copy-start.2 = (f32[128,768]{1,0:T(8,128)}, f32[128,768]{1,0:T(8,128)S(1)}, u32[]{:S(2)}) copy-start(f32[128,768]{1,0:T(8,128)S(1)} %collective-permute-done.11.refs_3_) | copy-start | bytes 1179652
  42.3 11.5 %collective-permute-start.13 = (f32[256,384]{1,0:T(8,128)}, f32[256,384]{1,0:T(8,128)}, u32[]{:S(2)}, u32[]{:S(2)}) collective-permute-start(f32[256,384]{1,0:T(8,128)} %get-tuple-element.67), channel_id=1, source_target_pairs={{0,4},{1,5},{2,6},{3,7},{4,0},{5,1},{6,2},{7,3},{8,12},{9,13},{10,... | collective-permute-start | bytes 1179656 | tf_op jit(solution)/shard_map/ppermute | solution.py:212
  43.9 13.7 %collective-permute-start.12 = (f32[256,384]{1,0:T(8,128)}, f32[256,384]{1,0:T(8,128)}, u32[]{:S(2)}, u32[]{:S(2)}) collective-permute-start(f32[256,384]{1,0:T(8,128)} %get-tuple-element.66), channel_id=1, source_target_pairs={{0,2},{1,3},{2,0},{3,1},{4,6},{5,7},{6,4},{7,5},{8,10},{9,11},{10,... | collective-permute-start | bytes 1179656 | tf_op jit(solution)/shard_map/ppermute | solution.py:212
  45.4 11.0 %copy-start.7 = (f32[768,384]{1,0:T(8,128)S(1)}, f32[768,384]{1,0:T(8,128)}, u32[]{:S(2)}) copy-start(f32[768,384]{1,0:T(8,128)} %copy-done.6) | copy-start | bytes 3538948
  54.8 5.4 %copy-start.1 = (f32[128,768]{1,0:T(8,128)S(1)}, f32[128,768]{1,0:T(8,128)}, u32[]{:S(2)}) copy-start(f32[128,768]{1,0:T(8,128)} %copy-done) | copy-start | bytes 1179652
  54.9 5.4 %copy-start.3 = (f32[128,768]{1,0:T(8,128)S(1)}, f32[128,768]{1,0:T(8,128)}, u32[]{:S(2)}) copy-start(f32[128,768]{1,0:T(8,128)} %copy-done.2) | copy-start | bytes 1179652
  54.9 7.4 %collective-permute-start.15 = (f32[128,384]{1,0:T(8,128)S(1)}, f32[128,384]{1,0:T(8,128)S(1)}, u32[]{:S(2)}, u32[]{:S(2)}) collective-permute-start(f32[128,384]{1,0:T(8,128)S(1)} %get-tuple-element.79), channel_id=1, source_target_pairs={{0,2},{1,3},{2,0},{3,1},{4,6},{5,7},{6,4},{7,5},{8,10},{9,11},{10,... | collective-permute-start | bytes 589832 | tf_op jit(solution)/shard_map/ppermute | solution.py:212
  56.4 3.8 %copy-start.5 = (f32[768,384]{1,0:T(8,128)S(1)}, f32[768,384]{1,0:T(8,128)}, u32[]{:S(2)}) copy-start(f32[768,384]{1,0:T(8,128)} %copy-done.4) | copy-start | bytes 3538948
  56.6 36.7 %collective-permute-start.7 = (f32[768,384]{1,0:T(8,128)S(1)}, f32[768,384]{1,0:T(8,128)S(1)}, u32[]{:S(2)}, u32[]{:S(2)}) collective-permute-start(f32[768,384]{1,0:T(8,128)S(1)} %broadcast_select_fusion.1), channel_id=1, source_target_pairs={{8,0},{16,24},{0,16},{24,8},{9,1},{17,25},{1,17},{25,9},{10,2},{18... | collective-permute-start | bytes 3538952 | tf_op jit(solution)/shard_map/ppermute | solution.py:200
  58.7 7.5 %collective-permute-start.14 = (f32[128,384]{1,0:T(8,128)S(1)}, f32[128,384]{1,0:T(8,128)S(1)}, u32[]{:S(2)}, u32[]{:S(2)}) collective-permute-start(f32[128,384]{1,0:T(8,128)S(1)} %get-tuple-element.78), channel_id=1, source_target_pairs={{0,4},{1,5},{2,6},{3,7},{4,0},{5,1},{6,2},{7,3},{8,12},{9,13},{10,... | collective-permute-start | bytes 589832 | tf_op jit(solution)/shard_map/ppermute | solution.py:212
  61.7 11.1 %collective-permute-start.17 = (f32[256,384]{1,0:T(8,128)S(1)}, f32[256,384]{1,0:T(8,128)S(1)}, u32[]{:S(2)}, u32[]{:S(2)}) collective-permute-start(f32[256,384]{1,0:T(8,128)S(1)} %get-tuple-element.75), channel_id=1, source_target_pairs={{0,4},{1,5},{2,6},{3,7},{4,0},{5,1},{6,2},{7,3},{8,12},{9,13},{10,... | collective-permute-start | bytes 1179656 | tf_op jit(solution)/shard_map/ppermute | solution.py:212
  62.3 11.2 %collective-permute-start.16 = (f32[256,384]{1,0:T(8,128)S(1)}, f32[256,384]{1,0:T(8,128)S(1)}, u32[]{:S(2)}, u32[]{:S(2)}) collective-permute-start(f32[256,384]{1,0:T(8,128)S(1)} %get-tuple-element.74), channel_id=1, source_target_pairs={{0,2},{1,3},{2,0},{3,1},{4,6},{5,7},{6,4},{7,5},{8,10},{9,11},{10,... | collective-permute-start | bytes 1179656 | tf_op jit(solution)/shard_map/ppermute | solution.py:212
  66.2 1.4 %collective-permute-start.18 = (f32[128,384]{1,0:T(8,128)S(1)}, f32[128,384]{1,0:T(8,128)S(1)}, u32[]{:S(2)}, u32[]{:S(2)}) collective-permute-start(f32[128,384]{1,0:T(8,128)S(1)} %fold.16), channel_id=1, source_target_pairs={{0,1},{1,0},{2,3},{3,2},{4,5},{5,4},{6,7},{7,6},{8,9},{9,8},{10,11... | collective-permute-start | bytes 589832 | tf_op jit(solution)/shard_map/ppermute | solution.py:212
  72.9 7.4 %collective-permute-start.20 = (f32[128,384]{1,0:T(8,128)S(1)}, f32[128,384]{1,0:T(8,128)S(1)}, u32[]{:S(2)}, u32[]{:S(2)}) collective-permute-start(f32[128,384]{1,0:T(8,128)S(1)} %get-tuple-element.89), channel_id=1, source_target_pairs={{0,2},{1,3},{2,0},{3,1},{4,6},{5,7},{6,4},{7,5},{8,10},{9,11},{10,... | collective-permute-start | bytes 589832 | tf_op jit(solution)/shard_map/ppermute | solution.py:212
  76.4 16.8 %collective-permute-start.21 = (f32[256,384]{1,0:T(8,128)S(1)}, f32[256,384]{1,0:T(8,128)S(1)}, u32[]{:S(2)}, u32[]{:S(2)}) collective-permute-start(f32[256,384]{1,0:T(8,128)S(1)} %get-tuple-element.86), channel_id=1, source_target_pairs={{0,2},{1,3},{2,0},{3,1},{4,6},{5,7},{6,4},{7,5},{8,10},{9,11},{10,... | collective-permute-start | bytes 1179656 | tf_op jit(solution)/shard_map/ppermute | solution.py:212
  77.9 15.3 %collective-permute-start.22 = (f32[256,384]{1,0:T(8,128)S(1)}, f32[256,384]{1,0:T(8,128)S(1)}, u32[]{:S(2)}, u32[]{:S(2)}) collective-permute-start(f32[256,384]{1,0:T(8,128)S(1)} %get-tuple-element.87), channel_id=1, source_target_pairs={{0,4},{1,5},{2,6},{3,7},{4,0},{5,1},{6,2},{7,3},{8,12},{9,13},{10,... | collective-permute-start | bytes 1179656 | tf_op jit(solution)/shard_map/ppermute | solution.py:212
  79.2 11.7 %collective-permute-start.19 = (f32[128,384]{1,0:T(8,128)S(1)}, f32[128,384]{1,0:T(8,128)S(1)}, u32[]{:S(2)}, u32[]{:S(2)}) collective-permute-start(f32[128,384]{1,0:T(8,128)S(1)} %get-tuple-element.88), channel_id=1, source_target_pairs={{0,4},{1,5},{2,6},{3,7},{4,0},{5,1},{6,2},{7,3},{8,12},{9,13},{10,... | collective-permute-start | bytes 589832 | tf_op jit(solution)/shard_map/ppermute | solution.py:212
  80.3 12.1 %collective-permute-start.23 = (f32[128,384]{1,0:T(8,128)S(1)}, f32[128,384]{1,0:T(8,128)S(1)}, u32[]{:S(2)}, u32[]{:S(2)}) collective-permute-start(f32[128,384]{1,0:T(8,128)S(1)} %fold.19), channel_id=1, source_target_pairs={{0,1},{1,0},{2,3},{3,2},{4,5},{5,4},{6,7},{7,6},{8,9},{9,8},{10,11... | collective-permute-start | bytes 589832 | tf_op jit(solution)/shard_map/ppermute | solution.py:212
  94.7 13.8 %collective-permute-start.28 = (f32[256,384]{1,0:T(8,128)S(1)}, f32[256,384]{1,0:T(8,128)S(1)}, u32[]{:S(2)}, u32[]{:S(2)}) collective-permute-start(f32[256,384]{1,0:T(8,128)S(1)} %get-tuple-element.97), channel_id=1, source_target_pairs={{0,4},{1,5},{2,6},{3,7},{4,0},{5,1},{6,2},{7,3},{8,12},{9,13},{10,... | collective-permute-start | bytes 1179656 | tf_op jit(solution)/shard_map/ppermute | solution.py:212
  95.5 11.6 %collective-permute-start.24 = (f32[128,384]{1,0:T(8,128)S(1)}, f32[128,384]{1,0:T(8,128)S(1)}, u32[]{:S(2)}, u32[]{:S(2)}) collective-permute-start(f32[128,384]{1,0:T(8,128)S(1)} %get-tuple-element.98), channel_id=1, source_target_pairs={{0,4},{1,5},{2,6},{3,7},{4,0},{5,1},{6,2},{7,3},{8,12},{9,13},{10,... | collective-permute-start | bytes 589832 | tf_op jit(solution)/shard_map/ppermute | solution.py:212
  96.8 10.3 %collective-permute-start.25 = (f32[128,384]{1,0:T(8,128)S(1)}, f32[128,384]{1,0:T(8,128)S(1)}, u32[]{:S(2)}, u32[]{:S(2)}) collective-permute-start(f32[128,384]{1,0:T(8,128)S(1)} %get-tuple-element.99), channel_id=1, source_target_pairs={{0,2},{1,3},{2,0},{3,1},{4,6},{5,7},{6,4},{7,5},{8,10},{9,11},{10,... | collective-permute-start | bytes 589832 | tf_op jit(solution)/shard_map/ppermute | solution.py:212
  97.3 12.8 %collective-permute-start.26 = (f32[256,384]{1,0:T(8,128)S(1)}, f32[256,384]{1,0:T(8,128)S(1)}, u32[]{:S(2)}, u32[]{:S(2)}) collective-permute-start(f32[256,384]{1,0:T(8,128)S(1)} %get-tuple-element.96), channel_id=1, source_target_pairs={{0,2},{1,3},{2,0},{3,1},{4,6},{5,7},{6,4},{7,5},{8,10},{9,11},{10,... | collective-permute-start | bytes 1179656 | tf_op jit(solution)/shard_map/ppermute | solution.py:212
  108.6 5.7 %collective-permute-start.29 = (f32[128,384]{1,0:T(8,128)S(1)}, f32[128,384]{1,0:T(8,128)S(1)}, u32[]{:S(2)}, u32[]{:S(2)}) collective-permute-start(f32[128,384]{1,0:T(8,128)S(1)} %get-tuple-element.106), channel_id=1, source_target_pairs={{0,2},{1,3},{2,0},{3,1},{4,6},{5,7},{6,4},{7,5},{8,10},{9,11},{10,... | collective-permute-start | bytes 589832 | tf_op jit(solution)/shard_map/ppermute | solution.py:212
  110.1 4.3 %collective-permute-start.31 = (f32[128,384]{1,0:T(8,128)S(1)}, f32[128,384]{1,0:T(8,128)S(1)}, u32[]{:S(2)}, u32[]{:S(2)}) collective-permute-start(f32[128,384]{1,0:T(8,128)S(1)} %fold.23), channel_id=1, source_target_pairs={{0,1},{1,0},{2,3},{3,2},{4,5},{5,4},{6,7},{7,6},{8,9},{9,8},{10,11... | collective-permute-start | bytes 589832 | tf_op jit(solution)/shard_map/ppermute | solution.py:212
  110.2 7.4 %collective-permute-start.27 = (f32[128,384]{1,0:T(8,128)S(1)}, f32[128,384]{1,0:T(8,128)S(1)}, u32[]{:S(2)}, u32[]{:S(2)}) collective-permute-start(f32[128,384]{1,0:T(8,128)S(1)} %get-tuple-element.103), channel_id=1, source_target_pairs={{0,4},{1,5},{2,6},{3,7},{4,0},{5,1},{6,2},{7,3},{8,12},{9,13},{10,... | collective-permute-start | bytes 589832 | tf_op jit(solution)/shard_map/ppermute | solution.py:212
  114.3 3.2 %collective-permute-start.30 = (f32[128,384]{1,0:T(8,128)S(1)}, f32[128,384]{1,0:T(8,128)S(1)}, u32[]{:S(2)}, u32[]{:S(2)}) collective-permute-start(f32[128,384]{1,0:T(8,128)S(1)} %fold.22), channel_id=1, source_target_pairs={{0,1},{1,0},{2,3},{3,2},{4,5},{5,4},{6,7},{7,6},{8,9},{9,8},{10,11... | collective-permute-start | bytes 589832 | tf_op jit(solution)/shard_map/ppermute | solution.py:212

commit v11 on v10

--- a/solution.py
+++ b/solution.py
@@ -9,7 +9,7 @@
 
 TILE_O = 32
 TILE_V = 128
-VMEM_LIMIT = 12 * 1024 * 1024
+VMEM_LIMIT = 6 * 1024 * 1024
 
 
 def after(value, *earlier):
@@ -186,19 +186,22 @@
 
 
 def line_blocks(own, nodes):
-    here = lax.axis_index("occ")
-
     def direct(x, d):
         return lax.ppermute(x, "occ", [(i, i ^ d) for i in range(nodes)])
 
     if nodes != 4:
-        return [(d, own if d == 0 else direct(own, d), 0) for d in range(nodes)]
+        return [(d, own if d == 0 else direct(own, d)) for d in range(nodes)]
     centre = lax.ppermute(own, "occ", [(1, 2), (2, 1)])
     near = direct(own, 1)
+    return [(0, own), (1, near), (3, centre), (2, None)]
+
+
+def far_blocks(own, near, centre):
     far = lax.ppermute(after(own, centre, near), "occ", [(0, 3), (3, 0)])
+    here = lax.axis_index("occ")
     middle = (here == 1) | (here == 2)
     last = lax.ppermute(jnp.where(middle, centre, own), "occ", [(1, 0), (2, 3), (0, 2), (3, 1)])
-    return [(0, own, 0), (1, near, 0), (3, (middle, centre, far), 0), (2, last, 0)]
+    return (middle, centre, far), last
 
 
 def per_device(sizes, amplitudes, amp_mask, integrals, int_mask):
@@ -231,17 +234,21 @@
     near = [[r for r in range(groups) if not r & o[0]] for o in orders]
 
     out = None
-    token = None
-    settled = []
-    for n, (d, block, offset) in enumerate(blocks):
+    token = settled = []
+    for n in range(n_occ):
+        d, block = blocks[n]
         if isinstance(block, tuple):
             middle, centre, far = block
-            centre, far = lax.optimization_barrier((centre, far, *sent))[:2]
+            centre, far = lax.optimization_barrier((centre, far, *token))[:2]
             block = jnp.where(middle, centre, far)
-        if n > 0:
+        elif n > 0:
             block = after(block, *token)
         sent = products([[rel[h][r] for r in away[h]] for h in range(2)], block)
         moving = [swap(sent[h], 2 * orders[h][0]) for h in range(2)]
+        if n == 0 and blocks[-1][1] is None:
+            first, second = lax.optimization_barrier((blocks[1][1], blocks[2][1], *sent))[:2]
+            passed = far_blocks(block, first, second)
+            blocks[1:] = [(1, first), (3, passed[0]), (2, passed[1])]
         held = list(products([[rel[h][r] for r in near[h]] for h in range(2)], after(block, *sent, *settled)))
         names = [near[0], near[1]]
         for level in range(1, len(bits)):
@@ -252,10 +259,10 @@
                 held[h], moved = fold(rows, stays, goes, held[h], moving[h])
                 moving[h] = swap(moved, 2 * bit)
                 names[h] = [names[h][i] for i in stays]
-        token = held if out is None else [*held, out]
-        settled = moving
+        token = held if n == 0 else [*moving, out]
+        settled = moving if n == 0 else []
         (theirs,) = fold(rows, [0], [], held[1], moving[1])
-        out = write(out, (rows, n_occ * width), d, half, offset, held[0], moving[0], swap(theirs, 1))
+        out = write(out, (rows, n_occ * width), d, half, 0, held[0], moving[0], swap(theirs, 1))
     return out
 
 

time: 119 us -> 123 us (1.034)
  waiting for transfers between devices: 60.5 us -> 66.3 us
  starting transfers between devices: 34.5 us -> 32.4 us
    ppermute x28, waiting for transfers between devices: 54.8 us -> 63.1 us  [swap(): return lax.ppermute(x, 'vir', [(i, i ^ bits) for i in range(n_vir)])]
    ppermute x2, starting transfers between devices: 6.72 us -> 3.76 us  [the longest x1 3.25 us: far_blocks(): far = lax.ppermute(after(own, centre, near), 'occ', [(0, 3), (3, 0)])]
    ppermute x1, starting transfers between devices: 3.01 us -> 5.76 us  [direct(): return lax.ppermute(x, 'occ', [(i, i ^ d) for i in range(nodes)])]
    ppermute x1, waiting for transfers between devices: 5.65 us -> 3.26 us  [direct(): return lax.ppermute(x, 'occ', [(i, i ^ d) for i in range(nodes)])]
    ppermute x28, starting transfers between devices: 24 us -> 22.1 us  [swap(): return lax.ppermute(x, 'vir', [(i, i ^ bits) for i in range(n_vir)])]
  transfers between devices with their start and end apart: 32 -> 32, of which waited for: 12 -> 19; matrix products, arithmetic and copies ran while one was open for 1% -> 1% of each run, Pallas kernels for 14% -> 14%
where the time goes in v11:
time: 123 us
  waiting for transfers between devices  66.3 us (54%)
  starting transfers between devices  32.4 us (26%)
  Pallas kernels  20.4 us (17%)
  other arithmetic  1.52 us (1%)
  local copies, waits for them, and re-layouts  1.39 us (1%)
    ppermute x28, waiting for transfers between devices, swap(): return lax.ppermute(x, 'vir', [(i, i ^ bits) for i in range(n_vir)])  63.1 us
    ppermute x28, starting transfers between devices, swap(): return lax.ppermute(x, 'vir', [(i, i ^ bits) for i in range(n_vir)])  22.1 us
    pallas_call x23, Pallas kernels, kernel_call(): pl.pallas_call(body, out_shape=[pltpu.VMEM(shape, jnp.float32) for shape...  17.3 us
    ppermute x1, starting transfers between devices, direct(): return lax.ppermute(x, 'occ', [(i, i ^ d) for i in range(nodes)])  5.76 us
    ppermute x1, waiting for transfers between devices, direct(): return lax.ppermute(x, 'occ', [(i, i ^ d) for i in range(nodes)])  3.26 us
    ppermute x1, starting transfers between devices, far_blocks(): far = lax.ppermute(after(own, centre, near), 'occ', [(0, 3), (3, 0)])  3.25 us
    pallas_call x4, Pallas kernels, write(): pl.pallas_call(functools.partial(write_kernel, d, half, offset), out_shap...  3.12 us
  transfers between devices with their start and end apart: 32, of which 19 were waited for; matrix products, arithmetic and copies ran while one was open for 1% of the time, Pallas kernels for 14%

profile of v11, /device:TPU:0, one launch (start us, length us, event | category | flops | bytes accessed | tf_op | source)
XLA Modules:
  0.0 122.5 jit_solution(6004635373880218156)
XLA Ops:
  0.0 1.3 %halves.1 = (f32[384,384]{1,0:T(8,128)S(1)}, f32[384,384]{1,0:T(8,128)S(1)}) custom-call(s32[3,6]{1,0:T(4,128)} %mask_hbm.1, f32[384,768]{1,0:T(8,128)} %int_hbm.1), custom_call_target="tpu_custom_call" | custom-call | flops 1 | bytes 1 | tf_op jit(solution)/shard_map/halves/pallas_call | solution.py:30
  1.3 0.5 collective-permute-start.5
  1.8 1.4 %cut.1 = (f32[128,768]{1,0:T(8,128)S(1)}, f32[128,768]{1,0:T(8,128)S(1)}, f32[128,768]{1,0:T(8,128)S(1)}, f32[128,768]{1,0:T(8,128)S(1)}) custom-call(s32[4,24]{1,0:T(4,128)} %mask_hbm.2, f32[128,3072]{1,0:T(8,128)} %amp_hbm.1), custom_call_target="tpu_custom_call" | custom-call | flops 1 | bytes 1 | tf_op jit(solution)/shard_map/cut/pallas_call | solution.py:30
  3.3 0.2 collective-permute-done.5.other_ref
  3.6 0.7 collective-permute-start.7
  4.3 5.8 %collective-permute-start.6 = (f32[768,384]{1,0:T(8,128)S(1)}, f32[768,384]{1,0:T(8,128)S(1)}, u32[]{:S(2)}, u32[]{:S(2)}) collective-permute-start(f32[768,384]{1,0:T(8,128)S(1)} %join.1.refs_4_), channel_id=1, source_target_pairs={{0,8},{8,0},{16,24},{24,16},{1,9},{9,1},{17,25},{25,17},{2,10},{10... | collective-permute-start | bytes 3538952 | tf_op jit(solution)/shard_map/ppermute | solution.py:190
  10.1 1.5 %collective-permute-start = (f32[128,768]{1,0:T(8,128)S(1)}, f32[128,768]{1,0:T(8,128)S(1)}, u32[]{:S(2)}, u32[]{:S(2)}) collective-permute-start(f32[128,768]{1,0:T(8,128)S(1)} %get-tuple-element.60), channel_id=1, source_target_pairs={{0,4},{1,5},{2,6},{3,7},{4,0},{5,1},{6,2},{7,3},{8,12},{9,13},{10,... | collective-permute-start | bytes 1179656 | tf_op jit(solution)/shard_map/ppermute | solution.py:215
  11.6 1.4 %collective-permute-start.1 = (f32[128,768]{1,0:T(8,128)S(1)}, f32[128,768]{1,0:T(8,128)S(1)}, u32[]{:S(2)}, u32[]{:S(2)}) collective-permute-start(f32[128,768]{1,0:T(8,128)S(1)} %get-tuple-element.61), channel_id=1, source_target_pairs={{0,6},{1,7},{2,4},{3,5},{4,2},{5,3},{6,0},{7,1},{8,14},{9,15},{10,... | collective-permute-start | bytes 1179656 | tf_op jit(solution)/shard_map/ppermute | solution.py:215
  13.0 0.5 collective-permute-start.3
  13.6 15.5 %collective-permute-done.refs_1_ = f32[128,768]{1,0:T(8,128)S(1)} collective-permute-done((f32[128,768]{1,0:T(8,128)S(1)}, f32[128,768]{1,0:T(8,128)S(1)}, u32[]{:S(2)}, u32[]{:S(2)}) %collective-permute-start) | collective-permute-done | bytes 393248 | tf_op jit(solution)/shard_map/ppermute | solution.py:215
  29.1 0.5 collective-permute-start.9
  29.6 0.7 collective-permute-done.3.refs_0_
  30.3 0.5 collective-permute-done.8.refs_2_
  30.8 0.6 collective-permute-done.9.refs_3_
  31.4 1.4 %products.8 = (f32[256,384]{1,0:T(8,128)S(1)}, f32[256,384]{1,0:T(8,128)S(1)}) custom-call(f32[128,768]{1,0:T(8,128)S(1)} %collective-permute-done.3.refs_0_, f32[128,768]{1,0:T(8,128)S(1)} %collective-permute-done.1.refs_1_, f32[128,768]{1,0:T(8,128)S(1)} %collective-permute-done.8.refs_2_, f32[128,768]{1,0:T(8,128)S(1)} %collective-permute-done.9.refs_3_, ...), custom_call_target="tpu_custom_call" | custom-call | flops 1 | bytes 1 | tf_op jit(solution)/shard_map/products/pallas_call | solution.py:30
  32.8 3.3 %collective-permute-done.6.refs_4_ = f32[768,384]{1,0:T(8,128)S(1)} collective-permute-done((f32[768,384]{1,0:T(8,128)S(1)}, f32[768,384]{1,0:T(8,128)S(1)}, u32[]{:S(2)}, u32[]{:S(2)}) %collective-permute-start.6) | collective-permute-done | bytes 1179680 | tf_op jit(solution)/shard_map/ppermute | solution.py:190
  36.1 3.2 %collective-permute-start.11 = (f32[768,384]{1,0:T(8,128)S(1)}, f32[768,384]{1,0:T(8,128)}, u32[]{:S(2)}, u32[]{:S(2)}) collective-permute-start(f32[768,384]{1,0:T(8,128)S(1)} %join.1.refs_4_), channel_id=1, source_target_pairs={{0,24},{24,0},{1,25},{25,1},{2,26},{26,2},{3,27},{27,3},{4,28},{28... | collective-permute-start | bytes 3538952 | tf_op jit(solution)/shard_map/ppermute | solution.py:200
  39.4 0.5 collective-permute-start.4
  39.9 1.5 %collective-permute-start.12 = (f32[256,384]{1,0:T(8,128)S(1)}, f32[256,384]{1,0:T(8,128)S(1)}, u32[]{:S(2)}, u32[]{:S(2)}) collective-permute-start(f32[256,384]{1,0:T(8,128)S(1)} %get-tuple-element.66), channel_id=1, source_target_pairs={{0,2},{1,3},{2,0},{3,1},{4,6},{5,7},{6,4},{7,5},{8,10},{9,11},{10,... | collective-permute-start | bytes 1179656 | tf_op jit(solution)/shard_map/ppermute | solution.py:215
  41.4 1.5 %collective-permute-start.13 = (f32[256,384]{1,0:T(8,128)S(1)}, f32[256,384]{1,0:T(8,128)S(1)}, u32[]{:S(2)}, u32[]{:S(2)}) collective-permute-start(f32[256,384]{1,0:T(8,128)S(1)} %get-tuple-element.67), channel_id=1, source_target_pairs={{0,4},{1,5},{2,6},{3,7},{4,0},{5,1},{6,2},{7,3},{8,12},{9,13},{10,... | collective-permute-start | bytes 1179656 | tf_op jit(solution)/shard_map/ppermute | solution.py:215
  42.9 1.4 %products.9 = (f32[256,384]{1,0:T(8,128)S(1)}, f32[256,384]{1,0:T(8,128)S(1)}) custom-call(f32[128,768]{1,0:T(8,128)S(1)} %get-tuple-element.62.refs_0_, f32[128,768]{1,0:T(8,128)S(1)} %collective-permute-done.refs_1_, f32[128,768]{1,0:T(8,128)S(1)} %collective-permute-done.2.refs_2_, f32[128,768]{1,0:T(8,128)S(1)} %collective-permute-done.4.refs_3_, ...), custom_call_target="tpu_custom_call" | custom-call | flops 1 | bytes 1 | tf_op jit(solution)/shard_map/products/pallas_call | solution.py:30
  44.3 6.6 %collective-permute-done.12.got_ref = f32[256,384]{1,0:T(8,128)S(1)} collective-permute-done((f32[256,384]{1,0:T(8,128)S(1)}, f32[256,384]{1,0:T(8,128)S(1)}, u32[]{:S(2)}, u32[]{:S(2)}) %collective-permute-start.12) | collective-permute-done | bytes 393248 | tf_op jit(solution)/shard_map/ppermute | solution.py:215
  51.0 0.7 copy-done.10
  51.7 0.5 collective-permute-done.13.got_ref
  52.3 0.7 copy-done.11
  52.9 2.1 %products.10 = (f32[256,384]{1,0:T(8,128)}, f32[256,384]{1,0:T(8,128)}) custom-call(f32[128,768]{1,0:T(8,128)S(1)} %collective-permute-done.3.refs_0_, f32[128,768]{1,0:T(8,128)S(1)} %collective-permute-done.1.refs_1_, f32[128,768]{1,0:T(8,128)S(1)} %collective-permute-done.8.refs_2_, f32[128,768]{1,0:T(8,128)S(1)} %collective-permute-done.9.refs_3_, ...), custom_call_target="tpu_custom_call" | custom-call | flops 1 | bytes 1 | tf_op jit(solution)/shard_map/products/pallas_call | solution.py:30
  55.1 1.0 collective-permute-start.16
  56.1 1.5 %collective-permute-start.18 = (f32[256,384]{1,0:T(8,128)}, f32[256,384]{1,0:T(8,128)}, u32[]{:S(2)}, u32[]{:S(2)}) collective-permute-start(f32[256,384]{1,0:T(8,128)} %get-tuple-element.78), channel_id=1, source_target_pairs={{0,4},{1,5},{2,6},{3,7},{4,0},{5,1},{6,2},{7,3},{8,12},{9,13},{10,... | collective-permute-start | bytes 1179656 | tf_op jit(solution)/shard_map/ppermute | solution.py:215
  57.7 1.0 collective-permute-start.15
  58.6 0.5 collective-permute-start.14
  59.2 0.1 broadcast_select_fusion.1
  59.3 10.3 %collective-permute-done.15.got_ref = f32[128,384]{1,0:T(8,128)S(1)} collective-permute-done((f32[128,384]{1,0:T(8,128)}, f32[128,384]{1,0:T(8,128)S(1)}, u32[]{:S(2)}, u32[]{:S(2)}) %collective-permute-start.15) | collective-permute-done | bytes 196640 | tf_op jit(solution)/shard_map/ppermute | solution.py:215
  69.6 0.5 collective-permute-start.10
  70.1 0.5 collective-permute-done.14.got_ref
  70.7 1.4 %products.11 = (f32[256,384]{1,0:T(8,128)S(1)}, f32[256,384]{1,0:T(8,128)S(1)}) custom-call(f32[128,768]{1,0:T(8,128)S(1)} %get-tuple-element.62.refs_0_, f32[128,768]{1,0:T(8,128)S(1)} %collective-permute-done.refs_1_, f32[128,768]{1,0:T(8,128)S(1)} %copy-done.1, f32[128,768]{1,0:T(8,128)S(1)} %copy-done.3, f32[768,384]{1,0:T(8,128)S(1)} %copy-done.5), custom_call_target="tpu_custom_call" | custom-call | flops 1 | bytes 1 | tf_op jit(solution)/shard_map/products/pallas_call | solution.py:30
  72.1 1.1 fold.14
  73.2 1.6 %collective-permute-start.17 = (f32[128,384]{1,0:T(8,128)S(1)}, f32[128,384]{1,0:T(8,128)S(1)}, u32[]{:S(2)}, u32[]{:S(2)}) collective-permute-start(f32[128,384]{1,0:T(8,128)S(1)} %get-tuple-element.83), channel_id=1, source_target_pairs={{0,4},{1,5},{2,6},{3,7},{4,0},{5,1},{6,2},{7,3},{8,12},{9,13},{10,... | collective-permute-start | bytes 589832 | tf_op jit(solution)/shard_map/ppermute | solution.py:215
  74.8 1.0 fold.15
  75.8 1.0 collective-permute-start.19
  76.8 0.8 write.4.refs_0_
  77.6 2.9 %collective-permute-done.17.got_ref = f32[128,384]{1,0:T(8,128)S(1)} collective-permute-done((f32[128,384]{1,0:T(8,128)S(1)}, f32[128,384]{1,0:T(8,128)S(1)}, u32[]{:S(2)}, u32[]{:S(2)}) %collective-permute-start.17) | collective-permute-done | bytes 196640 | tf_op jit(solution)/shard_map/ppermute | solution.py:215
  80.6 2.4 %collective-permute-done.19.got_ref = f32[128,384]{1,0:T(8,128)S(1)} collective-permute-done((f32[128,384]{1,0:T(8,128)S(1)}, f32[128,384]{1,0:T(8,128)S(1)}, u32[]{:S(2)}, u32[]{:S(2)}) %collective-permute-start.19) | collective-permute-done | bytes 196640 | tf_op jit(solution)/shard_map/ppermute | solution.py:215
  82.9 1.4 %broadcast_select_fusion.refs_4_ = f32[768,384]{1,0:T(8,128)S(1)} fusion(f32[768,384]{1,0:T(8,128)S(1)} %copy-done.13, f32[768,384]{1,0:T(8,128)} %collective-permute-done.11, pred[]{:T(512)S(6)} %or.3), kind=kLoop, calls=%fused_computation | loop fusion | flops 294912 | bytes 3538945 | tf_op jit(solution)/shard_map/jit(_where)/select_n | solution.py:243
  84.3 1.4 %products.12 = (f32[256,384]{1,0:T(8,128)S(1)}, f32[256,384]{1,0:T(8,128)S(1)}) custom-call(f32[128,768]{1,0:T(8,128)S(1)} %collective-permute-done.3.refs_0_, f32[128,768]{1,0:T(8,128)S(1)} %collective-permute-done.1.refs_1_, f32[128,768]{1,0:T(8,128)S(1)} %collective-permute-done.8.refs_2_, f32[128,768]{1,0:T(8,128)S(1)} %collective-permute-done.9.refs_3_, ...), custom_call_target="tpu_custom_call" | custom-call | flops 1 | bytes 1 | tf_op jit(solution)/shard_map/products/pallas_call | solution.py:30
  85.7 1.0 collective-permute-start.21
  86.7 0.5 collective-permute-start.23
  87.3 1.4 %products.13 = (f32[256,384]{1,0:T(8,128)S(1)}, f32[256,384]{1,0:T(8,128)S(1)}) custom-call(f32[128,768]{1,0:T(8,128)S(1)} %get-tuple-element.62.refs_0_, f32[128,768]{1,0:T(8,128)S(1)} %collective-permute-done.refs_1_, f32[128,768]{1,0:T(8,128)S(1)} %copy-done.1, f32[128,768]{1,0:T(8,128)S(1)} %copy-done.3, f32[768,384]{1,0:T(8,128)S(1)} %broadcast_select_fusion.refs_4_), custom_call_target="tpu_custom_call" | custom-call | flops 1 | bytes 1 | tf_op jit(solution)/shard_map/products/pallas_call | solution.py:30
  88.7 7.5 %collective-permute-done.21.got_ref = f32[256,384]{1,0:T(8,128)S(1)} collective-permute-done((f32[256,384]{1,0:T(8,128)S(1)}, f32[256,384]{1,0:T(8,128)S(1)}, u32[]{:S(2)}, u32[]{:S(2)}) %collective-permute-start.21) | collective-permute-done | bytes 393248 | tf_op jit(solution)/shard_map/ppermute | solution.py:215
  96.3 0.6 collective-permute-start.22
  96.9 1.2 collective-permute-start.24
  98.1 0.8 write.5.refs_0_
  98.9 3.1 %collective-permute-done.22.got_ref = f32[128,384]{1,0:T(8,128)S(1)} collective-permute-done((f32[128,384]{1,0:T(8,128)S(1)}, f32[128,384]{1,0:T(8,128)S(1)}, u32[]{:S(2)}, u32[]{:S(2)}) %collective-permute-start.22) | collective-permute-done | bytes 196640 | tf_op jit(solution)/shard_map/ppermute | solution.py:215
  102.0 0.6 collective-permute-done.24.got_ref
  102.6 1.4 %products.14 = (f32[256,384]{1,0:T(8,128)S(1)}, f32[256,384]{1,0:T(8,128)S(1)}) custom-call(f32[128,768]{1,0:T(8,128)S(1)} %collective-permute-done.3.refs_0_, f32[128,768]{1,0:T(8,128)S(1)} %collective-permute-done.1.refs_1_, f32[128,768]{1,0:T(8,128)S(1)} %collective-permute-done.8.refs_2_, f32[128,768]{1,0:T(8,128)S(1)} %collective-permute-done.9.refs_3_, ...), custom_call_target="tpu_custom_call" | custom-call | flops 1 | bytes 1 | tf_op jit(solution)/shard_map/products/pallas_call | solution.py:30
  104.0 1.6 %collective-permute-start.28 = (f32[256,384]{1,0:T(8,128)S(1)}, f32[256,384]{1,0:T(8,128)S(1)}, u32[]{:S(2)}, u32[]{:S(2)}) collective-permute-start(f32[256,384]{1,0:T(8,128)S(1)} %get-tuple-element.99), channel_id=1, source_target_pairs={{0,4},{1,5},{2,6},{3,7},{4,0},{5,1},{6,2},{7,3},{8,12},{9,13},{10,... | collective-permute-start | bytes 1179656 | tf_op jit(solution)/shard_map/ppermute | solution.py:215
  105.6 0.9 collective-permute-start.26
  106.5 1.4 %products.15 = (f32[256,384]{1,0:T(8,128)S(1)}, f32[256,384]{1,0:T(8,128)S(1)}) custom-call(f32[128,768]{1,0:T(8,128)S(1)} %get-tuple-element.62.refs_0_, f32[128,768]{1,0:T(8,128)S(1)} %collective-permute-done.refs_1_, f32[128,768]{1,0:T(8,128)S(1)} %copy-done.1, f32[128,768]{1,0:T(8,128)S(1)} %copy-done.3, f32[768,384]{1,0:T(8,128)S(1)} %collective-permute-done.10.refs_4_), custom_call_target="tpu_custom_call" | custom-call | flops 1 | bytes 1 | tf_op jit(solution)/shard_map/products/pallas_call | solution.py:30
  107.9 4.3 %collective-permute-done.28.got_ref = f32[256,384]{1,0:T(8,128)S(1)} collective-permute-done((f32[256,384]{1,0:T(8,128)S(1)}, f32[256,384]{1,0:T(8,128)S(1)}, u32[]{:S(2)}, u32[]{:S(2)}) %collective-permute-start.28) | collective-permute-done | bytes 393248 | tf_op jit(solution)/shard_map/ppermute | solution.py:215
  112.3 1.4 %collective-permute-start.29 = (f32[128,384]{1,0:T(8,128)S(1)}, f32[128,384]{1,0:T(8,128)S(1)}, u32[]{:S(2)}, u32[]{:S(2)}) collective-permute-start(f32[128,384]{1,0:T(8,128)S(1)} %get-tuple-element.106), channel_id=1, source_target_pairs={{0,2},{1,3},{2,0},{3,1},{4,6},{5,7},{6,4},{7,5},{8,10},{9,11},{10,... | collective-permute-start | bytes 589832 | tf_op jit(solution)/shard_map/ppermute | solution.py:215
  113.8 2.0 %collective-permute-done.26.got_ref = f32[256,384]{1,0:T(8,128)S(1)} collective-permute-done((f32[256,384]{1,0:T(8,128)S(1)}, f32[256,384]{1,0:T(8,128)S(1)}, u32[]{:S(2)}, u32[]{:S(2)}) %collective-permute-start.26) | collective-permute-done | bytes 393248 | tf_op jit(solution)/shard_map/ppermute | solution.py:215
  115.9 2.1 %collective-permute-done.29.got_ref = f32[128,384]{1,0:T(8,128)S(1)} collective-permute-done((f32[128,384]{1,0:T(8,128)S(1)}, f32[128,384]{1,0:T(8,128)S(1)}, u32[]{:S(2)}, u32[]{:S(2)}) %collective-permute-start.29) | collective-permute-done | bytes 196640 | tf_op jit(solution)/shard_map/ppermute | solution.py:215
  118.1 0.8 write.6.refs_0_
  118.9 2.7 %collective-permute-done.27.got_ref = f32[128,384]{1,0:T(8,128)S(1)} collective-permute-done((f32[128,384]{1,0:T(8,128)S(1)}, f32[128,384]{1,0:T(8,128)S(1)}, u32[]{:S(2)}, u32[]{:S(2)}) %collective-permute-start.27) | collective-permute-done | bytes 196640 | tf_op jit(solution)/shard_map/ppermute | solution.py:215
  121.6 0.8 write.7
  (57 shorter events, 0.9 us)
Async XLA Ops:
  1.3 2.1 %collective-permute-start.5 = (f32[384,384]{1,0:T(8,128)S(1)}, f32[384,384]{1,0:T(8,128)S(1)}, u32[]{:S(2)}, u32[]{:S(2)}) collective-permute-start(f32[384,384]{1,0:T(8,128)S(1)} %get-tuple-element.64), channel_id=1, source_target_pairs={{0,1},{1,0},{2,3},{3,2},{4,5},{5,4},{6,7},{7,6},{8,9},{9,8},{10,11... | collective-permute-start | bytes 1769480 | tf_op jit(solution)/shard_map/ppermute | solution.py:215
  3.6 29.2 %collective-permute-start.7 = (f32[768,384]{1,0:T(8,128)S(1)}, f32[768,384]{1,0:T(8,128)S(1)}, u32[]{:S(2)}, u32[]{:S(2)}) collective-permute-start(f32[768,384]{1,0:T(8,128)S(1)} %join.1.refs_4_), channel_id=1, source_target_pairs={{8,16},{16,8},{9,17},{17,9},{10,18},{18,10},{11,19},{19,11},{12,20... | collective-permute-start | bytes 3538952 | tf_op jit(solution)/shard_map/ppermute | solution.py:194
  4.3 31.7 %collective-permute-start.6 = (f32[768,384]{1,0:T(8,128)S(1)}, f32[768,384]{1,0:T(8,128)S(1)}, u32[]{:S(2)}, u32[]{:S(2)}) collective-permute-start(f32[768,384]{1,0:T(8,128)S(1)} %join.1.refs_4_), channel_id=1, source_target_pairs={{0,8},{8,0},{16,24},{24,16},{1,9},{9,1},{17,25},{25,17},{2,10},{10... | collective-permute-start | bytes 3538952 | tf_op jit(solution)/shard_map/ppermute | solution.py:190
  10.1 19.0 %collective-permute-start = (f32[128,768]{1,0:T(8,128)S(1)}, f32[128,768]{1,0:T(8,128)S(1)}, u32[]{:S(2)}, u32[]{:S(2)}) collective-permute-start(f32[128,768]{1,0:T(8,128)S(1)} %get-tuple-element.60), channel_id=1, source_target_pairs={{0,4},{1,5},{2,6},{3,7},{4,0},{5,1},{6,2},{7,3},{8,12},{9,13},{10,... | collective-permute-start | bytes 1179656 | tf_op jit(solution)/shard_map/ppermute | solution.py:215
  11.6 17.5 %collective-permute-start.1 = (f32[128,768]{1,0:T(8,128)S(1)}, f32[128,768]{1,0:T(8,128)S(1)}, u32[]{:S(2)}, u32[]{:S(2)}) collective-permute-start(f32[128,768]{1,0:T(8,128)S(1)} %get-tuple-element.61), channel_id=1, source_target_pairs={{0,6},{1,7},{2,4},{3,5},{4,2},{5,3},{6,0},{7,1},{8,14},{9,15},{10,... | collective-permute-start | bytes 1179656 | tf_op jit(solution)/shard_map/ppermute | solution.py:215
  13.0 17.3 %collective-permute-start.3 = (f32[128,768]{1,0:T(8,128)S(1)}, f32[128,768]{1,0:T(8,128)S(1)}, u32[]{:S(2)}, u32[]{:S(2)}) collective-permute-start(f32[128,768]{1,0:T(8,128)S(1)} %get-tuple-element.63), channel_id=1, source_target_pairs={{0,2},{1,3},{2,0},{3,1},{4,6},{5,7},{6,4},{7,5},{8,10},{9,11},{10,... | collective-permute-start | bytes 1179656 | tf_op jit(solution)/shard_map/ppermute | solution.py:215
  29.1 1.7 %collective-permute-start.8 = (f32[128,768]{1,0:T(8,128)S(1)}, f32[128,768]{1,0:T(8,128)S(1)}, u32[]{:S(2)}, u32[]{:S(2)}) collective-permute-start(f32[128,768]{1,0:T(8,128)S(1)} %collective-permute-done.refs_1_), channel_id=1, source_target_pairs={{0,1},{1,0},{2,3},{3,2},{4,5},{5,4},{6,7},{7,6},{8,9},{9,8},{10,11... | collective-permute-start | bytes 1179656 | tf_op jit(solution)/shard_map/ppermute | solution.py:215
  29.1 2.3 %collective-permute-start.9 = (f32[128,768]{1,0:T(8,128)S(1)}, f32[128,768]{1,0:T(8,128)S(1)}, u32[]{:S(2)}, u32[]{:S(2)}) collective-permute-start(f32[128,768]{1,0:T(8,128)S(1)} %collective-permute-done.1.refs_1_), channel_id=1, source_target_pairs={{0,1},{1,0},{2,3},{3,2},{4,5},{5,4},{6,7},{7,6},{8,9},{9,8},{10,11... | collective-permute-start | bytes 1179656 | tf_op jit(solution)/shard_map/ppermute | solution.py:215
  32.8 3.3 %copy-start.12 = (f32[768,384]{1,0:T(8,128)}, f32[768,384]{1,0:T(8,128)S(1)}, u32[]{:S(2)}) copy-start(f32[768,384]{1,0:T(8,128)S(1)} %collective-permute-done.7) | copy-start | bytes 3538948
  36.1 16.9 %copy-start.4 = (f32[768,384]{1,0:T(8,128)}, f32[768,384]{1,0:T(8,128)S(1)}, u32[]{:S(2)}) copy-start(f32[768,384]{1,0:T(8,128)S(1)} %collective-permute-done.6.refs_4_) | copy-start | bytes 3538948
  36.1 46.9 %collective-permute-start.11 = (f32[768,384]{1,0:T(8,128)S(1)}, f32[768,384]{1,0:T(8,128)}, u32[]{:S(2)}, u32[]{:S(2)}) collective-permute-start(f32[768,384]{1,0:T(8,128)S(1)} %join.1.refs_4_), channel_id=1, source_target_pairs={{0,24},{24,0},{1,25},{25,1},{2,26},{26,2},{3,27},{27,3},{4,28},{28... | collective-permute-start | bytes 3538952 | tf_op jit(solution)/shard_map/ppermute | solution.py:200
  39.3 3.6 %collective-permute-start.2 = (f32[128,768]{1,0:T(8,128)S(1)}, f32[128,768]{1,0:T(8,128)S(1)}, u32[]{:S(2)}, u32[]{:S(2)}) collective-permute-start(f32[128,768]{1,0:T(8,128)S(1)} %get-tuple-element.62.refs_0_), channel_id=1, source_target_pairs={{0,1},{1,0},{2,3},{3,2},{4,5},{5,4},{6,7},{7,6},{8,9},{9,8},{10,11... | collective-permute-start | bytes 1179656 | tf_op jit(solution)/shard_map/ppermute | solution.py:215
  39.4 3.5 %collective-permute-start.4 = (f32[128,768]{1,0:T(8,128)S(1)}, f32[128,768]{1,0:T(8,128)S(1)}, u32[]{:S(2)}, u32[]{:S(2)}) collective-permute-start(f32[128,768]{1,0:T(8,128)S(1)} %collective-permute-done.3.refs_0_), channel_id=1, source_target_pairs={{0,1},{1,0},{2,3},{3,2},{4,5},{5,4},{6,7},{7,6},{8,9},{9,8},{10,11... | collective-permute-start | bytes 1179656 | tf_op jit(solution)/shard_map/ppermute | solution.py:215
  39.9 11.1 %collective-permute-start.12 = (f32[256,384]{1,0:T(8,128)S(1)}, f32[256,384]{1,0:T(8,128)S(1)}, u32[]{:S(2)}, u32[]{:S(2)}) collective-permute-start(f32[256,384]{1,0:T(8,128)S(1)} %get-tuple-element.66), channel_id=1, source_target_pairs={{0,2},{1,3},{2,0},{3,1},{4,6},{5,7},{6,4},{7,5},{8,10},{9,11},{10,... | collective-permute-start | bytes 1179656 | tf_op jit(solution)/shard_map/ppermute | solution.py:215
  41.4 10.8 %collective-permute-start.13 = (f32[256,384]{1,0:T(8,128)S(1)}, f32[256,384]{1,0:T(8,128)S(1)}, u32[]{:S(2)}, u32[]{:S(2)}) collective-permute-start(f32[256,384]{1,0:T(8,128)S(1)} %get-tuple-element.67), channel_id=1, source_target_pairs={{0,4},{1,5},{2,6},{3,7},{4,0},{5,1},{6,2},{7,3},{8,12},{9,13},{10,... | collective-permute-start | bytes 1179656 | tf_op jit(solution)/shard_map/ppermute | solution.py:215
  42.9 1.4 %copy-start = (f32[128,768]{1,0:T(8,128)}, f32[128,768]{1,0:T(8,128)S(1)}, u32[]{:S(2)}) copy-start(f32[128,768]{1,0:T(8,128)S(1)} %collective-permute-done.2.refs_2_) | copy-start | bytes 1179652
  42.9 1.4 %copy-start.2 = (f32[128,768]{1,0:T(8,128)}, f32[128,768]{1,0:T(8,128)S(1)}, u32[]{:S(2)}) copy-start(f32[128,768]{1,0:T(8,128)S(1)} %collective-permute-done.4.refs_3_) | copy-start | bytes 1179652
  51.0 0.7 copy-start.10
  51.7 3.4 %copy-start.6 = (f32[128,384]{1,0:T(8,128)}, f32[128,384]{1,0:T(8,128)S(1)}, u32[]{:S(2)}) copy-start(f32[128,384]{1,0:T(8,128)S(1)} %get-tuple-element.73.held_ref) | copy-start | bytes 589828
  52.2 0.7 copy-start.11
  52.9 2.2 %copy-start.8 = (f32[128,384]{1,0:T(8,128)}, f32[128,384]{1,0:T(8,128)S(1)}, u32[]{:S(2)}) copy-start(f32[128,384]{1,0:T(8,128)S(1)} %get-tuple-element.75.held_ref) | copy-start | bytes 589828
  55.1 17.0 %collective-permute-start.16 = (f32[256,384]{1,0:T(8,128)}, f32[256,384]{1,0:T(8,128)}, u32[]{:S(2)}, u32[]{:S(2)}) collective-permute-start(f32[256,384]{1,0:T(8,128)} %get-tuple-element.77), channel_id=1, source_target_pairs={{0,2},{1,3},{2,0},{3,1},{4,6},{5,7},{6,4},{7,5},{8,10},{9,11},{10,... | collective-permute-start | bytes 1179656 | tf_op jit(solution)/shard_map/ppermute | solution.py:215
  56.1 18.6 %collective-permute-start.18 = (f32[256,384]{1,0:T(8,128)}, f32[256,384]{1,0:T(8,128)}, u32[]{:S(2)}, u32[]{:S(2)}) collective-permute-start(f32[256,384]{1,0:T(8,128)} %get-tuple-element.78), channel_id=1, source_target_pairs={{0,4},{1,5},{2,6},{3,7},{4,0},{5,1},{6,2},{7,3},{8,12},{9,13},{10,... | collective-permute-start | bytes 1179656 | tf_op jit(solution)/shard_map/ppermute | solution.py:215
  57.7 11.9 %collective-permute-start.15 = (f32[128,384]{1,0:T(8,128)}, f32[128,384]{1,0:T(8,128)S(1)}, u32[]{:S(2)}, u32[]{:S(2)}) collective-permute-start(f32[128,384]{1,0:T(8,128)} %copy-done.11), channel_id=1, source_target_pairs={{0,2},{1,3},{2,0},{3,1},{4,6},{5,7},{6,4},{7,5},{8,10},{9,11},{10,... | collective-permute-start | bytes 589832 | tf_op jit(solution)/shard_map/ppermute | solution.py:215
  58.6 11.4 %copy-start.9 = (f32[128,384]{1,0:T(8,128)S(1)}, f32[128,384]{1,0:T(8,128)}, u32[]{:S(2)}) copy-start(f32[128,384]{1,0:T(8,128)} %copy-done.8) | copy-start | bytes 589828
  58.6 12.0 %copy-start.1 = (f32[128,768]{1,0:T(8,128)S(1)}, f32[128,768]{1,0:T(8,128)}, u32[]{:S(2)}) copy-start(f32[128,768]{1,0:T(8,128)} %copy-done) | copy-start | bytes 1179652
  58.6 12.0 %copy-start.3 = (f32[128,768]{1,0:T(8,128)S(1)}, f32[128,768]{1,0:T(8,128)}, u32[]{:S(2)}) copy-start(f32[128,768]{1,0:T(8,128)} %copy-done.2) | copy-start | bytes 1179652
  58.6 12.0 %collective-permute-start.14 = (f32[128,384]{1,0:T(8,128)}, f32[128,384]{1,0:T(8,128)S(1)}, u32[]{:S(2)}, u32[]{:S(2)}) collective-permute-start(f32[128,384]{1,0:T(8,128)} %copy-done.10), channel_id=1, source_target_pairs={{0,4},{1,5},{2,6},{3,7},{4,0},{5,1},{6,2},{7,3},{8,12},{9,13},{10,... | collective-permute-start | bytes 589832 | tf_op jit(solution)/shard_map/ppermute | solution.py:215
  59.2 11.5 %copy-start.5 = (f32[768,384]{1,0:T(8,128)S(1)}, f32[768,384]{1,0:T(8,128)}, u32[]{:S(2)}) copy-start(f32[768,384]{1,0:T(8,128)} %copy-done.4) | copy-start | bytes 3538948
  69.6 29.3 %collective-permute-start.10 = (f32[768,384]{1,0:T(8,128)S(1)}, f32[768,384]{1,0:T(8,128)S(1)}, u32[]{:S(2)}, u32[]{:S(2)}) collective-permute-start(f32[768,384]{1,0:T(8,128)S(1)} %broadcast_select_fusion.1), channel_id=1, source_target_pairs={{8,0},{16,24},{0,16},{24,8},{9,1},{17,25},{1,17},{25,9},{10,2},{18... | collective-permute-start | bytes 3538952 | tf_op jit(solution)/shard_map/ppermute | solution.py:203
  70.6 6.2 %collective-permute-start.20 = (f32[128,384]{1,0:T(8,128)S(1)}, f32[128,384]{1,0:T(8,128)S(1)}, u32[]{:S(2)}, u32[]{:S(2)}) collective-permute-start(f32[128,384]{1,0:T(8,128)S(1)} %fold.16), channel_id=1, source_target_pairs={{0,1},{1,0},{2,3},{3,2},{4,5},{5,4},{6,7},{7,6},{8,9},{9,8},{10,11... | collective-permute-start | bytes 589832 | tf_op jit(solution)/shard_map/ppermute | solution.py:215
  72.1 4.7 %copy-start.7 = (f32[128,384]{1,0:T(8,128)S(1)}, f32[128,384]{1,0:T(8,128)}, u32[]{:S(2)}) copy-start(f32[128,384]{1,0:T(8,128)} %copy-done.6) | copy-start | bytes 589828
  73.2 7.4 %collective-permute-start.17 = (f32[128,384]{1,0:T(8,128)S(1)}, f32[128,384]{1,0:T(8,128)S(1)}, u32[]{:S(2)}, u32[]{:S(2)}) collective-permute-start(f32[128,384]{1,0:T(8,128)S(1)} %get-tuple-element.83), channel_id=1, source_target_pairs={{0,4},{1,5},{2,6},{3,7},{4,0},{5,1},{6,2},{7,3},{8,12},{9,13},{10,... | collective-permute-start | bytes 589832 | tf_op jit(solution)/shard_map/ppermute | solution.py:215
  75.8 7.1 %copy-start.13 = (f32[768,384]{1,0:T(8,128)S(1)}, f32[768,384]{1,0:T(8,128)}, u32[]{:S(2)}) copy-start(f32[768,384]{1,0:T(8,128)} %copy-done.12) | copy-start | bytes 3538948
  75.8 7.1 %collective-permute-start.19 = (f32[128,384]{1,0:T(8,128)S(1)}, f32[128,384]{1,0:T(8,128)S(1)}, u32[]{:S(2)}, u32[]{:S(2)}) collective-permute-start(f32[128,384]{1,0:T(8,128)S(1)} %get-tuple-element.85), channel_id=1, source_target_pairs={{0,2},{1,3},{2,0},{3,1},{4,6},{5,7},{6,4},{7,5},{8,10},{9,11},{10,... | collective-permute-start | bytes 589832 | tf_op jit(solution)/shard_map/ppermute | solution.py:215
  85.7 10.5 %collective-permute-start.21 = (f32[256,384]{1,0:T(8,128)S(1)}, f32[256,384]{1,0:T(8,128)S(1)}, u32[]{:S(2)}, u32[]{:S(2)}) collective-permute-start(f32[256,384]{1,0:T(8,128)S(1)} %get-tuple-element.88), channel_id=1, source_target_pairs={{0,2},{1,3},{2,0},{3,1},{4,6},{5,7},{6,4},{7,5},{8,10},{9,11},{10,... | collective-permute-start | bytes 1179656 | tf_op jit(solution)/shard_map/ppermute | solution.py:215
  86.7 10.1 %collective-permute-start.23 = (f32[256,384]{1,0:T(8,128)S(1)}, f32[256,384]{1,0:T(8,128)S(1)}, u32[]{:S(2)}, u32[]{:S(2)}) collective-permute-start(f32[256,384]{1,0:T(8,128)S(1)} %get-tuple-element.89), channel_id=1, source_target_pairs={{0,4},{1,5},{2,6},{3,7},{4,0},{5,1},{6,2},{7,3},{8,12},{9,13},{10,... | collective-permute-start | bytes 1179656 | tf_op jit(solution)/shard_map/ppermute | solution.py:215
  87.2 10.9 %collective-permute-start.25 = (f32[128,384]{1,0:T(8,128)S(1)}, f32[128,384]{1,0:T(8,128)S(1)}, u32[]{:S(2)}, u32[]{:S(2)}) collective-permute-start(f32[128,384]{1,0:T(8,128)S(1)} %fold.19), channel_id=1, source_target_pairs={{0,1},{1,0},{2,3},{3,2},{4,5},{5,4},{6,7},{7,6},{8,9},{9,8},{10,11... | collective-permute-start | bytes 589832 | tf_op jit(solution)/shard_map/ppermute | solution.py:215
  96.3 5.7 %collective-permute-start.22 = (f32[128,384]{1,0:T(8,128)S(1)}, f32[128,384]{1,0:T(8,128)S(1)}, u32[]{:S(2)}, u32[]{:S(2)}) collective-permute-start(f32[128,384]{1,0:T(8,128)S(1)} %get-tuple-element.92), channel_id=1, source_target_pairs={{0,4},{1,5},{2,6},{3,7},{4,0},{5,1},{6,2},{7,3},{8,12},{9,13},{10,... | collective-permute-start | bytes 589832 | tf_op jit(solution)/shard_map/ppermute | solution.py:215
  96.9 5.7 %collective-permute-start.24 = (f32[128,384]{1,0:T(8,128)S(1)}, f32[128,384]{1,0:T(8,128)S(1)}, u32[]{:S(2)}, u32[]{:S(2)}) collective-permute-start(f32[128,384]{1,0:T(8,128)S(1)} %get-tuple-element.94), channel_id=1, source_target_pairs={{0,2},{1,3},{2,0},{3,1},{4,6},{5,7},{6,4},{7,5},{8,10},{9,11},{10,... | collective-permute-start | bytes 589832 | tf_op jit(solution)/shard_map/ppermute | solution.py:215
  104.0 8.2 %collective-permute-start.28 = (f32[256,384]{1,0:T(8,128)S(1)}, f32[256,384]{1,0:T(8,128)S(1)}, u32[]{:S(2)}, u32[]{:S(2)}) collective-permute-start(f32[256,384]{1,0:T(8,128)S(1)} %get-tuple-element.99), channel_id=1, source_target_pairs={{0,4},{1,5},{2,6},{3,7},{4,0},{5,1},{6,2},{7,3},{8,12},{9,13},{10,... | collective-permute-start | bytes 1179656 | tf_op jit(solution)/shard_map/ppermute | solution.py:215
  105.6 10.2 %collective-permute-start.26 = (f32[256,384]{1,0:T(8,128)S(1)}, f32[256,384]{1,0:T(8,128)S(1)}, u32[]{:S(2)}, u32[]{:S(2)}) collective-permute-start(f32[256,384]{1,0:T(8,128)S(1)} %get-tuple-element.98), channel_id=1, source_target_pairs={{0,2},{1,3},{2,0},{3,1},{4,6},{5,7},{6,4},{7,5},{8,10},{9,11},{10,... | collective-permute-start | bytes 1179656 | tf_op jit(solution)/shard_map/ppermute | solution.py:215
  112.3 5.7 %collective-permute-start.29 = (f32[128,384]{1,0:T(8,128)S(1)}, f32[128,384]{1,0:T(8,128)S(1)}, u32[]{:S(2)}, u32[]{:S(2)}) collective-permute-start(f32[128,384]{1,0:T(8,128)S(1)} %get-tuple-element.106), channel_id=1, source_target_pairs={{0,2},{1,3},{2,0},{3,1},{4,6},{5,7},{6,4},{7,5},{8,10},{9,11},{10,... | collective-permute-start | bytes 589832 | tf_op jit(solution)/shard_map/ppermute | solution.py:215
  113.7 4.4 %collective-permute-start.31 = (f32[128,384]{1,0:T(8,128)S(1)}, f32[128,384]{1,0:T(8,128)S(1)}, u32[]{:S(2)}, u32[]{:S(2)}) collective-permute-start(f32[128,384]{1,0:T(8,128)S(1)} %fold.23), channel_id=1, source_target_pairs={{0,1},{1,0},{2,3},{3,2},{4,5},{5,4},{6,7},{7,6},{8,9},{9,8},{10,11... | collective-permute-start | bytes 589832 | tf_op jit(solution)/shard_map/ppermute | solution.py:215
  115.9 5.7 %collective-permute-start.27 = (f32[128,384]{1,0:T(8,128)S(1)}, f32[128,384]{1,0:T(8,128)S(1)}, u32[]{:S(2)}, u32[]{:S(2)}) collective-permute-start(f32[128,384]{1,0:T(8,128)S(1)} %get-tuple-element.103), channel_id=1, source_target_pairs={{0,4},{1,5},{2,6},{3,7},{4,0},{5,1},{6,2},{7,3},{8,12},{9,13},{10,... | collective-permute-start | bytes 589832 | tf_op jit(solution)/shard_map/ppermute | solution.py:215
  118.1 3.5 %collective-permute-start.30 = (f32[128,384]{1,0:T(8,128)S(1)}, f32[128,384]{1,0:T(8,128)S(1)}, u32[]{:S(2)}, u32[]{:S(2)}) collective-permute-start(f32[128,384]{1,0:T(8,128)S(1)} %fold.22), channel_id=1, source_target_pairs={{0,1},{1,0},{2,3},{3,2},{4,5},{5,4},{6,7},{7,6},{8,9},{9,8},{10,11... | collective-permute-start | bytes 589832 | tf_op jit(solution)/shard_map/ppermute | solution.py:215

commit v12 on v10

--- a/solution.py
+++ b/solution.py
@@ -9,7 +9,7 @@
 
 TILE_O = 32
 TILE_V = 128
-VMEM_LIMIT = 12 * 1024 * 1024
+VMEM_LIMIT = 6 * 1024 * 1024
 
 
 def after(value, *earlier):
@@ -128,36 +128,38 @@
     return kernel_call(functools.partial(fold_kernel, rows, stays, goes), outs, [held, got], "fold")
 
 
-def write_kernel(d, half, offset, held_ref, got_ref, other_ref, *refs):
+def write_kernel(ds, half, mine_a, mine_b, other_a, other_b, *refs):
     out_ref, piece_ref, sems = refs[-3:]
     low = lax.axis_index("vir") % 2
-    place = lax.axis_index("occ") ^ d
-    width = held_ref.shape[1] // TILE_V
-    starts = [(2 * place + h) * (half // TILE_V) + offset // TILE_V for h in (low, 1 - low)]
-    piece_ref[...] = held_ref[...] + got_ref[...]
-    copies = [
-        pltpu.make_async_copy(source, out_ref.at[:, tiles(start, width)], sems.at[i])
-        for i, (source, start) in enumerate(zip((piece_ref, other_ref), starts))
-    ]
+    here = lax.axis_index("occ")
+    piece_ref[0] = mine_a[...] + mine_b[...]
+    piece_ref[1] = other_a[...] + other_b[...]
+    copies = []
+    for k, d in enumerate(ds):
+        for i, h in enumerate((low, 1 - low)):
+            start = (2 * (here ^ d) + h) * (half // TILE_V)
+            source = piece_ref.at[i, :, pl.ds(k * half, half)]
+            copies.append(pltpu.make_async_copy(source, out_ref.at[:, tiles(start, half // TILE_V)], sems.at[2 * k + i]))
     for copy in copies:
         copy.start()
     for copy in copies:
         copy.wait()
 
 
-def write(out, shape, d, half, offset, held, got, other):
+def write(out, shape, ds, half, pieces):
     given = [] if out is None else [out]
+    pieces = [pltpu.with_memory_space_constraint(x, pltpu.VMEM) for x in pieces]
     return pl.pallas_call(
-        functools.partial(write_kernel, d, half, offset),
+        functools.partial(write_kernel, ds, half),
         out_shape=jax.ShapeDtypeStruct(shape, jnp.float32),
-        in_specs=in_vmem(3) + in_hbm(len(given)),
+        in_specs=in_vmem(4) + in_hbm(len(given)),
         out_specs=pl.BlockSpec(memory_space=pltpu.HBM),
-        scratch_shapes=[pltpu.VMEM(held.shape, jnp.float32), pltpu.SemaphoreType.DMA((2,))],
-        input_output_aliases={3: 0} if given else {},
+        scratch_shapes=[pltpu.VMEM((2, *pieces[0].shape), jnp.float32), pltpu.SemaphoreType.DMA((2 * len(ds),))],
+        input_output_aliases={4: 0} if given else {},
         compiler_params=pltpu.CompilerParams(vmem_limit_bytes=VMEM_LIMIT),
         cost_estimate=pl.CostEstimate(flops=1, bytes_accessed=1, transcendentals=0),
         name="write",
-    )(held, got, other, *given)
+    )(*pieces, *given)
 
 
 def split(x):
@@ -165,40 +167,44 @@
     return high, (x - high.astype(jnp.float32)).astype(jnp.bfloat16)
 
 
-def dot_kernel(count, *refs):
-    left, block_ref, outs = refs[: 2 * count], refs[2 * count], refs[2 * count + 1 :]
-    rows = left[0].shape[0]
-    b_high, b_low = split(block_ref[...])
-    for h in range(2):
-        for i in range(count):
-            a_high, a_low = split(left[h * count + i][...])
-            total = None
-            for a, b in ((a_high, b_low), (a_low, b_high), (a_high, b_high)):
-                term = jnp.dot(a, b, preferred_element_type=jnp.float32)
-                total = term if total is None else total + term
-            outs[h][i * rows : (i + 1) * rows, :] = total
-
-
-def products(left, block):
+def dot_kernel(count, blocks, *refs):
+    left, right, outs = refs[: 2 * count], refs[2 * count : 2 * count + blocks], refs[2 * count + blocks :]
+    rows, width = left[0].shape[0], right[0].shape[1]
+    for k in range(blocks):
+        b_high, b_low = split(right[k][...])
+        for h in range(2):
+            for i in range(count):
+                a_high, a_low = split(left[h * count + i][...])
+                total = None
+                for a, b in ((a_high, b_low), (a_low, b_high), (a_high, b_high)):
+                    term = jnp.dot(a, b, preferred_element_type=jnp.float32)
+                    total = term if total is None else total + term
+                outs[h][i * rows : (i + 1) * rows, k * width : (k + 1) * width] = total
+
+
+def products(left, right):
     count = len(left[0])
-    shape = (count * left[0][0].shape[0], block.shape[1])
-    return kernel_call(functools.partial(dot_kernel, count), [shape] * 2, [*left[0], *left[1], block], "products")
-
-
-def line_blocks(own, nodes):
-    here = lax.axis_index("occ")
-
+    shape = (count * left[0][0].shape[0], len(right) * right[0].shape[1])
+    return kernel_call(functools.partial(dot_kernel, count, len(right)), [shape] * 2, [*left[0], *left[1], *right], "products")
+
+
+def line_stages(own, nodes):
     def direct(x, d):
         return lax.ppermute(x, "occ", [(i, i ^ d) for i in range(nodes)])
 
     if nodes != 4:
-        return [(d, own if d == 0 else direct(own, d), 0) for d in range(nodes)]
+        return [[(d, own if d == 0 else direct(own, d))] for d in range(nodes)]
     centre = lax.ppermute(own, "occ", [(1, 2), (2, 1)])
     near = direct(own, 1)
     far = lax.ppermute(after(own, centre, near), "occ", [(0, 3), (3, 0)])
+    here = lax.axis_index("occ")
     middle = (here == 1) | (here == 2)
-    last = lax.ppermute(jnp.where(middle, centre, own), "occ", [(1, 0), (2, 3), (0, 2), (3, 1)])
-    return [(0, own, 0), (1, near, 0), (3, (middle, centre, far), 0), (2, last, 0)]
+
+    def last(*earlier):
+        moving = jnp.where(middle, after(centre, *earlier), own)
+        return [(2, lax.ppermute(moving, "occ", [(1, 0), (2, 3), (0, 2), (3, 1)]))]
+
+    return [[(0, own), (1, near)], [(3, (middle, centre, far))], last]
 
 
 def per_device(sizes, amplitudes, amp_mask, integrals, int_mask):
@@ -215,7 +221,7 @@
     other = swap(theirs, 1)
     parts = cut(after(amp_mask, mine), amplitudes, groups, depth)
     (whole,) = kernel_call(join_kernel, [(depth, half)], [mine, after(other, *parts)], "join")
-    blocks = line_blocks(whole, n_occ)
+    stages = line_stages(whole, n_occ)
 
     rel = [[parts[0]] + [None] * (groups - 1), [None] * groups]
     for r in range(groups - 1, 0, -1):
@@ -231,18 +237,20 @@
     near = [[r for r in range(groups) if not r & o[0]] for o in orders]
 
     out = None
-    token = None
-    settled = []
-    for n, (d, block, offset) in enumerate(blocks):
-        if isinstance(block, tuple):
-            middle, centre, far = block
+    token = []
+    for n in range(len(stages)):
+        ds, right = [d for d, _ in stages[n]], [block for _, block in stages[n]]
+        if isinstance(right[0], tuple):
+            middle, centre, far = right[0]
             centre, far = lax.optimization_barrier((centre, far, *sent))[:2]
-            block = jnp.where(middle, centre, far)
-        if n > 0:
-            block = after(block, *token)
-        sent = products([[rel[h][r] for r in away[h]] for h in range(2)], block)
+            right = [jnp.where(middle, centre, far)]
+        right = list(lax.optimization_barrier((*right, *token))[: len(right)])
+        sent = products([[rel[h][r] for r in away[h]] for h in range(2)], right)
         moving = [swap(sent[h], 2 * orders[h][0]) for h in range(2)]
-        held = list(products([[rel[h][r] for r in near[h]] for h in range(2)], after(block, *sent, *settled)))
+        if callable(stages[-1]):
+            stages[-1] = stages[-1](*moving)
+        right[0] = after(right[0], *sent)
+        held = list(products([[rel[h][r] for r in near[h]] for h in range(2)], right))
         names = [near[0], near[1]]
         for level in range(1, len(bits)):
             for h in (1, 0):
@@ -250,12 +258,11 @@
                 stays = [i for i, r in enumerate(names[h]) if not r & bit]
                 goes = [i for i, r in enumerate(names[h]) if r & bit]
                 held[h], moved = fold(rows, stays, goes, held[h], moving[h])
-                moving[h] = swap(moved, 2 * bit)
+                moving[h] = swap(moved, 2 * bit + (h if level == len(bits) - 1 else 0))
                 names[h] = [names[h][i] for i in stays]
-        token = held if out is None else [*held, out]
-        settled = moving
-        (theirs,) = fold(rows, [0], [], held[1], moving[1])
-        out = write(out, (rows, n_occ * width), d, half, offset, held[0], moving[0], swap(theirs, 1))
+        pieces = [held[0], moving[0], swap(held[1], 1), moving[1]]
+        token = [*pieces[1:]] if out is None else [*pieces[1:], out]
+        out = write(out, (rows, n_occ * width), ds, half, pieces)
     return out
 
 

time: 119 us -> 122 us (1.025)
  waiting for transfers between devices: 60.5 us -> 67.5 us
  starting transfers between devices: 34.5 us -> 31.5 us
    ppermute x28 -> x23, starting transfers between devices: 24 us -> 18.2 us  [swap(): return lax.ppermute(x, 'vir', [(i, i ^ bits) for i in range(n_vir)])]
    ppermute x3, waiting for transfers between devices: 0.01 us -> 4.75 us  [the longest x1 4.75 us: line_stages(): far = lax.ppermute(after(own, centre, near), 'occ', [(0, 3), (3, 0)])]
    ppermute x3, starting transfers between devices: 7.44 us -> 10.3 us  [the longest x1 5.5 us: line_stages(): far = lax.ppermute(after(own, centre, near), 'occ', [(0, 3), (3, 0)])]
    ppermute x28 -> x23, waiting for transfers between devices: 54.8 us -> 57.1 us  [swap(): return lax.ppermute(x, 'vir', [(i, i ^ bits) for i in range(n_vir)])]
    pallas_call x4 -> x3, Pallas kernels: 3.13 us -> 2.58 us  [write(): pl.pallas_call(functools.partial(write_kernel, ds, half), out_shape=jax.S...]
    pallas_call x23 -> x15, Pallas kernels: 17.3 us -> 17.4 us  [kernel_call(): pl.pallas_call(body, out_shape=[pltpu.VMEM(shape, jnp.float32) for shape...]
  transfers between devices with their start and end apart: 32 -> 27, of which waited for: 12 -> 13; matrix products, arithmetic and copies ran while one was open for 1% -> 1% of each run, Pallas kernels for 14% -> 13%
where the time goes in v12:
time: 122 us
  waiting for transfers between devices  67.5 us (55%)
  starting transfers between devices  31.5 us (26%)
  Pallas kernels  20 us (16%)
  other arithmetic  1.52 us (1%)
    ppermute x23, waiting for transfers between devices, swap(): return lax.ppermute(x, 'vir', [(i, i ^ bits) for i in range(n_vir)])  57.1 us
    ppermute x23, starting transfers between devices, swap(): return lax.ppermute(x, 'vir', [(i, i ^ bits) for i in range(n_vir)])  18.2 us
    pallas_call x15, Pallas kernels, kernel_call(): pl.pallas_call(body, out_shape=[pltpu.VMEM(shape, jnp.float32) for shape...  17.4 us
    ppermute x1, waiting for transfers between devices, direct(): return lax.ppermute(x, 'occ', [(i, i ^ d) for i in range(nodes)])  5.65 us
    ppermute x1, starting transfers between devices, line_stages(): far = lax.ppermute(after(own, centre, near), 'occ', [(0, 3), (3, 0)])  5.5 us
    ppermute x1, waiting for transfers between devices, line_stages(): far = lax.ppermute(after(own, centre, near), 'occ', [(0, 3), (3, 0)])  4.75 us
    ppermute x1, starting transfers between devices, last(): return [(2, lax.ppermute(moving, 'occ', [(1, 0), (2, 3), (0, 2), (3, 1)]))]  4.09 us
    ppermute x1, starting transfers between devices, direct(): return lax.ppermute(x, 'occ', [(i, i ^ d) for i in range(nodes)])  3.01 us
  transfers between devices with their start and end apart: 27, of which 13 were waited for; matrix products, arithmetic and copies ran while one was open for 1% of the time, Pallas kernels for 13%

profile of v12, /device:TPU:0, one launch (start us, length us, event | category | flops | bytes accessed | tf_op | source)
XLA Modules:
  0.0 121.9 jit_solution(17836974982973762769)
XLA Ops:
  0.0 1.3 %halves.1 = (f32[384,384]{1,0:T(8,128)S(1)}, f32[384,384]{1,0:T(8,128)S(1)}) custom-call(s32[3,6]{1,0:T(4,128)} %mask_hbm.1, f32[384,768]{1,0:T(8,128)} %int_hbm.1), custom_call_target="tpu_custom_call" | custom-call | flops 1 | bytes 1 | tf_op jit(solution)/shard_map/halves/pallas_call | solution.py:30
  1.3 0.5 collective-permute-start.5
  1.8 1.4 %cut.1 = (f32[128,768]{1,0:T(8,128)S(1)}, f32[128,768]{1,0:T(8,128)S(1)}, f32[128,768]{1,0:T(8,128)S(1)}, f32[128,768]{1,0:T(8,128)S(1)}) custom-call(s32[4,24]{1,0:T(4,128)} %mask_hbm.2, f32[128,3072]{1,0:T(8,128)} %amp_hbm.1), custom_call_target="tpu_custom_call" | custom-call | flops 1 | bytes 1 | tf_op jit(solution)/shard_map/cut/pallas_call | solution.py:30
  3.3 0.2 collective-permute-done.5.other_ref
  3.5 0.1 join.1.refs_4_
  3.6 3.0 %collective-permute-start.9 = (f32[768,384]{1,0:T(8,128)S(1)}, f32[768,384]{1,0:T(8,128)S(1)}, u32[]{:S(2)}, u32[]{:S(2)}) collective-permute-start(f32[768,384]{1,0:T(8,128)S(1)} %join.1.refs_4_), channel_id=1, source_target_pairs={{0,8},{8,0},{16,24},{24,16},{1,9},{9,1},{17,25},{25,17},{2,10},{10... | collective-permute-start | bytes 3538952 | tf_op jit(solution)/shard_map/ppermute | solution.py:193
  6.6 0.7 collective-permute-start.6
  7.3 1.6 %collective-permute-start = (f32[128,768]{1,0:T(8,128)S(1)}, f32[128,768]{1,0:T(8,128)S(1)}, u32[]{:S(2)}, u32[]{:S(2)}) collective-permute-start(f32[128,768]{1,0:T(8,128)S(1)} %get-tuple-element.52), channel_id=1, source_target_pairs={{0,4},{1,5},{2,6},{3,7},{4,0},{5,1},{6,2},{7,3},{8,12},{9,13},{10,... | collective-permute-start | bytes 1179656 | tf_op jit(solution)/shard_map/ppermute | solution.py:218
  8.9 1.4 %collective-permute-start.1 = (f32[128,768]{1,0:T(8,128)S(1)}, f32[128,768]{1,0:T(8,128)S(1)}, u32[]{:S(2)}, u32[]{:S(2)}) collective-permute-start(f32[128,768]{1,0:T(8,128)S(1)} %get-tuple-element.53), channel_id=1, source_target_pairs={{0,6},{1,7},{2,4},{3,5},{4,2},{5,3},{6,0},{7,1},{8,14},{9,15},{10,... | collective-permute-start | bytes 1179656 | tf_op jit(solution)/shard_map/ppermute | solution.py:218
  10.3 0.5 collective-permute-start.3
  10.9 15.8 %collective-permute-done.refs_1_ = f32[128,768]{1,0:T(8,128)S(1)} collective-permute-done((f32[128,768]{1,0:T(8,128)S(1)}, f32[128,768]{1,0:T(8,128)S(1)}, u32[]{:S(2)}, u32[]{:S(2)}) %collective-permute-start) | collective-permute-done | bytes 393248 | tf_op jit(solution)/shard_map/ppermute | solution.py:218
  26.7 0.0 collective-permute-start.7
  26.7 0.0 collective-permute-done.1.refs_1_
  26.7 0.5 collective-permute-start.8
  27.2 5.7 %collective-permute-done.9.refs_5_ = f32[768,384]{1,0:T(8,128)S(1)} collective-permute-done((f32[768,384]{1,0:T(8,128)S(1)}, f32[768,384]{1,0:T(8,128)S(1)}, u32[]{:S(2)}, u32[]{:S(2)}) %collective-permute-start.9) | collective-permute-done | bytes 1179680 | tf_op jit(solution)/shard_map/ppermute | solution.py:193
  32.8 0.0 collective-permute-done.3.refs_0_
  32.9 0.0 collective-permute-done.7.refs_2_
  32.9 3.5 %products.6 = (f32[256,768]{1,0:T(8,128)}, f32[256,768]{1,0:T(8,128)}) custom-call(f32[128,768]{1,0:T(8,128)S(1)} %collective-permute-done.3.refs_0_, f32[128,768]{1,0:T(8,128)S(1)} %collective-permute-done.1.refs_1_, f32[128,768]{1,0:T(8,128)S(1)} %collective-permute-done.7.refs_2_, f32[128,768]{1,0:T(8,128)S(1)} %collective-permute-done.8.refs_3_, ...), custom_call_target="tpu_custom_call" | custom-call | flops 1 | bytes 1 | tf_op jit(solution)/shard_map/products/pallas_call | solution.py:30
  36.4 1.7 %collective-permute-start.10 = (f32[256,768]{1,0:T(8,128)}, f32[256,768]{1,0:T(8,128)}, u32[]{:S(2)}, u32[]{:S(2)}) collective-permute-start(f32[256,768]{1,0:T(8,128)} %get-tuple-element.60), channel_id=1, source_target_pairs={{0,2},{1,3},{2,0},{3,1},{4,6},{5,7},{6,4},{7,5},{8,10},{9,11},{10,... | collective-permute-start | bytes 2359304 | tf_op jit(solution)/shard_map/ppermute | solution.py:218
  38.2 1.5 %collective-permute-start.11 = (f32[256,768]{1,0:T(8,128)}, f32[256,768]{1,0:T(8,128)}, u32[]{:S(2)}, u32[]{:S(2)}) collective-permute-start(f32[256,768]{1,0:T(8,128)} %get-tuple-element.61), channel_id=1, source_target_pairs={{0,4},{1,5},{2,6},{3,7},{4,0},{5,1},{6,2},{7,3},{8,12},{9,13},{10,... | collective-permute-start | bytes 2359304 | tf_op jit(solution)/shard_map/ppermute | solution.py:218
  39.7 1.0 copy-done.6
  40.7 5.5 %collective-permute-start.13 = (f32[768,384]{1,0:T(8,128)S(1)}, f32[768,384]{1,0:T(8,128)}, u32[]{:S(2)}, u32[]{:S(2)}) collective-permute-start(f32[768,384]{1,0:T(8,128)S(1)} %join.1.refs_4_), channel_id=1, source_target_pairs={{0,24},{24,0},{1,25},{25,1},{2,26},{26,2},{3,27},{27,3},{4,28},{28... | collective-permute-start | bytes 3538952 | tf_op jit(solution)/shard_map/ppermute | solution.py:199
  46.2 0.1 collective-permute-start.2
  46.3 0.5 collective-permute-start.4
  46.8 9.1 %collective-permute-done.10.got_ref = f32[256,768]{1,0:T(8,128)} collective-permute-done((f32[256,768]{1,0:T(8,128)}, f32[256,768]{1,0:T(8,128)}, u32[]{:S(2)}, u32[]{:S(2)}) %collective-permute-start.10) | collective-permute-done | bytes 786464 | tf_op jit(solution)/shard_map/ppermute | solution.py:218
  55.9 1.1 collective-permute-done.11.got_ref
  57.0 0.1 broadcast_select_fusion.1
  57.1 4.1 %collective-permute-start.12 = (f32[768,384]{1,0:T(8,128)S(1)}, f32[768,384]{1,0:T(8,128)S(1)}, u32[]{:S(2)}, u32[]{:S(2)}) collective-permute-start(f32[768,384]{1,0:T(8,128)S(1)} %broadcast_select_fusion.1), channel_id=1, source_target_pairs={{8,0},{16,24},{0,16},{24,8},{9,1},{17,25},{1,17},{25,9},{10,2},{18... | collective-permute-start | bytes 3538952 | tf_op jit(solution)/shard_map/ppermute | solution.py:205
  61.2 2.7 %products.7 = (f32[256,768]{1,0:T(8,128)S(1)}, f32[256,768]{1,0:T(8,128)S(1)}) custom-call(f32[128,768]{1,0:T(8,128)S(1)} %get-tuple-element.54.refs_0_, f32[128,768]{1,0:T(8,128)S(1)} %collective-permute-done.refs_1_, f32[128,768]{1,0:T(8,128)S(1)} %collective-permute-done.2.refs_2_, f32[128,768]{1,0:T(8,128)S(1)} %collective-permute-done.4.refs_3_, ...), custom_call_target="tpu_custom_call" | custom-call | flops 1 | bytes 1 | tf_op jit(solution)/shard_map/products/pallas_call | solution.py:30
  63.9 1.2 %fold.6 = (f32[128,768]{1,0:T(8,128)S(1)}, f32[128,768]{1,0:T(8,128)S(1)}) custom-call(f32[256,768]{1,0:T(8,128)S(1)} %get-tuple-element.67.held_ref, f32[256,768]{1,0:T(8,128)} %collective-permute-done.10.got_ref), custom_call_target="tpu_custom_call" | custom-call | flops 1 | bytes 1 | tf_op jit(solution)/shard_map/fold/pallas_call | solution.py:30
  65.1 0.0 copy-start.7
  65.1 1.6 %collective-permute-start.14 = (f32[128,768]{1,0:T(8,128)S(1)}, f32[128,768]{1,0:T(8,128)S(1)}, u32[]{:S(2)}, u32[]{:S(2)}) collective-permute-start(f32[128,768]{1,0:T(8,128)S(1)} %get-tuple-element.68), channel_id=1, source_target_pairs={{0,4},{1,5},{2,6},{3,7},{4,0},{5,1},{6,2},{7,3},{8,12},{9,13},{10,... | collective-permute-start | bytes 1179656 | tf_op jit(solution)/shard_map/ppermute | solution.py:218
  66.7 1.2 %fold.7 = (f32[128,768]{1,0:T(8,128)S(1)}, f32[128,768]{1,0:T(8,128)S(1)}) custom-call(f32[256,768]{1,0:T(8,128)S(1)} %get-tuple-element.69.held_ref, f32[256,768]{1,0:T(8,128)} %collective-permute-done.11.got_ref), custom_call_target="tpu_custom_call" | custom-call | flops 1 | bytes 1 | tf_op jit(solution)/shard_map/fold/pallas_call | solution.py:30
  67.9 0.1 collective-permute-start.15
  68.1 0.6 collective-permute-start.16
  68.7 4.7 %collective-permute-done.13 = f32[768,384]{1,0:T(8,128)} collective-permute-done((f32[768,384]{1,0:T(8,128)S(1)}, f32[768,384]{1,0:T(8,128)}, u32[]{:S(2)}, u32[]{:S(2)}) %collective-permute-start.13) | collective-permute-done | bytes 1179680 | tf_op jit(solution)/shard_map/ppermute | solution.py:199
  73.4 1.4 %broadcast_select_fusion.refs_4_ = f32[768,384]{1,0:T(8,128)S(1)} fusion(f32[768,384]{1,0:T(8,128)S(1)} %copy-done.7, f32[768,384]{1,0:T(8,128)} %collective-permute-done.13, pred[]{:T(512)S(6)} %or.3), kind=kLoop, calls=%fused_computation | loop fusion | flops 294912 | bytes 3538945 | tf_op jit(solution)/shard_map/jit(_where)/select_n | solution.py:246
  74.8 0.0 collective-permute-done.14.mine_b
  74.8 0.0 collective-permute-done.15.other_a
  74.9 4.1 %collective-permute-done.16.other_b = f32[128,768]{1,0:T(8,128)S(1)} collective-permute-done((f32[128,768]{1,0:T(8,128)S(1)}, f32[128,768]{1,0:T(8,128)S(1)}, u32[]{:S(2)}, u32[]{:S(2)}) %collective-permute-start.16) | collective-permute-done | bytes 393248 | tf_op jit(solution)/shard_map/ppermute | solution.py:218
  79.0 1.4 %products.8 = (f32[256,384]{1,0:T(8,128)S(1)}, f32[256,384]{1,0:T(8,128)S(1)}) custom-call(f32[128,768]{1,0:T(8,128)S(1)} %copy-done.1, f32[128,768]{1,0:T(8,128)S(1)} %collective-permute-done.1.refs_1_, f32[128,768]{1,0:T(8,128)S(1)} %copy-done.3, f32[128,768]{1,0:T(8,128)S(1)} %copy-done.5, f32[768,384]{1,0:T(8,128)S(1)} %broadcast_select_fusion.refs_4_), custom_call_target="tpu_custom_call" | custom-call | flops 1 | bytes 1 | tf_op jit(solution)/shard_map/products/pallas_call | solution.py:30
  80.4 0.6 collective-permute-start.17
  81.0 0.5 collective-permute-start.19
  81.6 1.4 %products.9 = (f32[256,384]{1,0:T(8,128)S(1)}, f32[256,384]{1,0:T(8,128)S(1)}) custom-call(f32[128,768]{1,0:T(8,128)S(1)} %get-tuple-element.54.refs_0_, f32[128,768]{1,0:T(8,128)S(1)} %collective-permute-done.refs_1_, f32[128,768]{1,0:T(8,128)S(1)} %collective-permute-done.2.refs_2_, f32[128,768]{1,0:T(8,128)S(1)} %collective-permute-done.4.refs_3_, ...), custom_call_target="tpu_custom_call" | custom-call | flops 1 | bytes 1 | tf_op jit(solution)/shard_map/products/pallas_call | solution.py:30
  83.0 9.2 %collective-permute-done.17.got_ref = f32[256,384]{1,0:T(8,128)S(1)} collective-permute-done((f32[256,384]{1,0:T(8,128)S(1)}, f32[256,384]{1,0:T(8,128)S(1)}, u32[]{:S(2)}, u32[]{:S(2)}) %collective-permute-start.17) | collective-permute-done | bytes 393248 | tf_op jit(solution)/shard_map/ppermute | solution.py:218
  92.2 0.6 collective-permute-start.18
  92.8 0.0 collective-permute-done.19.got_ref
  92.8 0.1 collective-permute-start.20
  92.9 1.2 %collective-permute-start.21 = (f32[128,384]{1,0:T(8,128)S(1)}, f32[128,384]{1,0:T(8,128)S(1)}, u32[]{:S(2)}, u32[]{:S(2)}) collective-permute-start(f32[128,384]{1,0:T(8,128)S(1)} %get-tuple-element.80), channel_id=1, source_target_pairs={{0,3},{1,2},{2,1},{3,0},{4,7},{5,6},{6,5},{7,4},{8,11},{9,10},{10,... | collective-permute-start | bytes 589832 | tf_op jit(solution)/shard_map/ppermute | solution.py:218
  94.2 1.0 write.3.refs_0_
  95.2 3.8 %collective-permute-done.18.mine_b = f32[128,384]{1,0:T(8,128)S(1)} collective-permute-done((f32[128,384]{1,0:T(8,128)S(1)}, f32[128,384]{1,0:T(8,128)S(1)}, u32[]{:S(2)}, u32[]{:S(2)}) %collective-permute-start.18) | collective-permute-done | bytes 196640 | tf_op jit(solution)/shard_map/ppermute | solution.py:218
  98.9 0.7 collective-permute-done.21.other_b
  99.6 1.4 %products.10 = (f32[256,384]{1,0:T(8,128)S(1)}, f32[256,384]{1,0:T(8,128)S(1)}) custom-call(f32[128,768]{1,0:T(8,128)S(1)} %copy-done.1, f32[128,768]{1,0:T(8,128)S(1)} %collective-permute-done.1.refs_1_, f32[128,768]{1,0:T(8,128)S(1)} %copy-done.3, f32[128,768]{1,0:T(8,128)S(1)} %copy-done.5, f32[768,384]{1,0:T(8,128)S(1)} %collective-permute-done.12.refs_4_), custom_call_target="tpu_custom_call" | custom-call | flops 1 | bytes 1 | tf_op jit(solution)/shard_map/products/pallas_call | solution.py:30
  101.1 1.2 %collective-permute-start.22 = (f32[256,384]{1,0:T(8,128)S(1)}, f32[256,384]{1,0:T(8,128)S(1)}, u32[]{:S(2)}, u32[]{:S(2)}) collective-permute-start(f32[256,384]{1,0:T(8,128)S(1)} %get-tuple-element.83), channel_id=1, source_target_pairs={{0,2},{1,3},{2,0},{3,1},{4,6},{5,7},{6,4},{7,5},{8,10},{9,11},{10,... | collective-permute-start | bytes 1179656 | tf_op jit(solution)/shard_map/ppermute | solution.py:218
  102.3 0.9 collective-permute-start.24
  103.2 1.4 %products.11 = (f32[256,384]{1,0:T(8,128)S(1)}, f32[256,384]{1,0:T(8,128)S(1)}) custom-call(f32[128,768]{1,0:T(8,128)S(1)} %get-tuple-element.54.refs_0_, f32[128,768]{1,0:T(8,128)S(1)} %collective-permute-done.refs_1_, f32[128,768]{1,0:T(8,128)S(1)} %collective-permute-done.2.refs_2_, f32[128,768]{1,0:T(8,128)S(1)} %collective-permute-done.4.refs_3_, ...), custom_call_target="tpu_custom_call" | custom-call | flops 1 | bytes 1 | tf_op jit(solution)/shard_map/products/pallas_call | solution.py:30
  104.6 7.9 %collective-permute-done.22.got_ref = f32[256,384]{1,0:T(8,128)S(1)} collective-permute-done((f32[256,384]{1,0:T(8,128)S(1)}, f32[256,384]{1,0:T(8,128)S(1)}, u32[]{:S(2)}, u32[]{:S(2)}) %collective-permute-start.22) | collective-permute-done | bytes 393248 | tf_op jit(solution)/shard_map/ppermute | solution.py:218
  112.6 1.6 %collective-permute-start.23 = (f32[128,384]{1,0:T(8,128)S(1)}, f32[128,384]{1,0:T(8,128)S(1)}, u32[]{:S(2)}, u32[]{:S(2)}) collective-permute-start(f32[128,384]{1,0:T(8,128)S(1)} %get-tuple-element.88), channel_id=1, source_target_pairs={{0,4},{1,5},{2,6},{3,7},{4,0},{5,1},{6,2},{7,3},{8,12},{9,13},{10,... | collective-permute-start | bytes 589832 | tf_op jit(solution)/shard_map/ppermute | solution.py:218
  114.2 0.1 collective-permute-start.25
  114.3 0.7 collective-permute-start.26
  114.9 0.8 write.4.refs_0_
  115.7 3.3 %collective-permute-done.23.mine_b = f32[128,384]{1,0:T(8,128)S(1)} collective-permute-done((f32[128,384]{1,0:T(8,128)S(1)}, f32[128,384]{1,0:T(8,128)S(1)}, u32[]{:S(2)}, u32[]{:S(2)}) %collective-permute-start.23) | collective-permute-done | bytes 196640 | tf_op jit(solution)/shard_map/ppermute | solution.py:218
  119.0 2.0 %collective-permute-done.26.other_b = f32[128,384]{1,0:T(8,128)S(1)} collective-permute-done((f32[128,384]{1,0:T(8,128)S(1)}, f32[128,384]{1,0:T(8,128)S(1)}, u32[]{:S(2)}, u32[]{:S(2)}) %collective-permute-start.26) | collective-permute-done | bytes 196640 | tf_op jit(solution)/shard_map/ppermute | solution.py:218
  121.0 0.8 write.5
  (26 shorter events, 0.2 us)
Async XLA Ops:
  1.3 2.1 %collective-permute-start.5 = (f32[384,384]{1,0:T(8,128)S(1)}, f32[384,384]{1,0:T(8,128)S(1)}, u32[]{:S(2)}, u32[]{:S(2)}) collective-permute-start(f32[384,384]{1,0:T(8,128)S(1)} %get-tuple-element.56), channel_id=1, source_target_pairs={{0,1},{1,0},{2,3},{3,2},{4,5},{5,4},{6,7},{7,6},{8,9},{9,8},{10,11... | collective-permute-start | bytes 1769480 | tf_op jit(solution)/shard_map/ppermute | solution.py:218
  3.6 29.3 %collective-permute-start.9 = (f32[768,384]{1,0:T(8,128)S(1)}, f32[768,384]{1,0:T(8,128)S(1)}, u32[]{:S(2)}, u32[]{:S(2)}) collective-permute-start(f32[768,384]{1,0:T(8,128)S(1)} %join.1.refs_4_), channel_id=1, source_target_pairs={{0,8},{8,0},{16,24},{24,16},{1,9},{9,1},{17,25},{25,17},{2,10},{10... | collective-permute-start | bytes 3538952 | tf_op jit(solution)/shard_map/ppermute | solution.py:193
  6.6 33.1 %collective-permute-start.6 = (f32[768,384]{1,0:T(8,128)S(1)}, f32[768,384]{1,0:T(8,128)S(1)}, u32[]{:S(2)}, u32[]{:S(2)}) collective-permute-start(f32[768,384]{1,0:T(8,128)S(1)} %join.1.refs_4_), channel_id=1, source_target_pairs={{8,16},{16,8},{9,17},{17,9},{10,18},{18,10},{11,19},{19,11},{12,20... | collective-permute-start | bytes 3538952 | tf_op jit(solution)/shard_map/ppermute | solution.py:197
  7.3 19.4 %collective-permute-start = (f32[128,768]{1,0:T(8,128)S(1)}, f32[128,768]{1,0:T(8,128)S(1)}, u32[]{:S(2)}, u32[]{:S(2)}) collective-permute-start(f32[128,768]{1,0:T(8,128)S(1)} %get-tuple-element.52), channel_id=1, source_target_pairs={{0,4},{1,5},{2,6},{3,7},{4,0},{5,1},{6,2},{7,3},{8,12},{9,13},{10,... | collective-permute-start | bytes 1179656 | tf_op jit(solution)/shard_map/ppermute | solution.py:218
  8.9 17.8 %collective-permute-start.1 = (f32[128,768]{1,0:T(8,128)S(1)}, f32[128,768]{1,0:T(8,128)S(1)}, u32[]{:S(2)}, u32[]{:S(2)}) collective-permute-start(f32[128,768]{1,0:T(8,128)S(1)} %get-tuple-element.53), channel_id=1, source_target_pairs={{0,6},{1,7},{2,4},{3,5},{4,2},{5,3},{6,0},{7,1},{8,14},{9,15},{10,... | collective-permute-start | bytes 1179656 | tf_op jit(solution)/shard_map/ppermute | solution.py:218
  10.3 22.5 %collective-permute-start.3 = (f32[128,768]{1,0:T(8,128)S(1)}, f32[128,768]{1,0:T(8,128)S(1)}, u32[]{:S(2)}, u32[]{:S(2)}) collective-permute-start(f32[128,768]{1,0:T(8,128)S(1)} %get-tuple-element.55), channel_id=1, source_target_pairs={{0,2},{1,3},{2,0},{3,1},{4,6},{5,7},{6,4},{7,5},{8,10},{9,11},{10,... | collective-permute-start | bytes 1179656 | tf_op jit(solution)/shard_map/ppermute | solution.py:218
  26.7 6.2 %collective-permute-start.7 = (f32[128,768]{1,0:T(8,128)S(1)}, f32[128,768]{1,0:T(8,128)S(1)}, u32[]{:S(2)}, u32[]{:S(2)}) collective-permute-start(f32[128,768]{1,0:T(8,128)S(1)} %collective-permute-done.refs_1_), channel_id=1, source_target_pairs={{0,1},{1,0},{2,3},{3,2},{4,5},{5,4},{6,7},{7,6},{8,9},{9,8},{10,11... | collective-permute-start | bytes 1179656 | tf_op jit(solution)/shard_map/ppermute | solution.py:218
  26.7 6.2 %collective-permute-start.8 = (f32[128,768]{1,0:T(8,128)S(1)}, f32[128,768]{1,0:T(8,128)S(1)}, u32[]{:S(2)}, u32[]{:S(2)}) collective-permute-start(f32[128,768]{1,0:T(8,128)S(1)} %collective-permute-done.1.refs_1_), channel_id=1, source_target_pairs={{0,1},{1,0},{2,3},{3,2},{4,5},{5,4},{6,7},{7,6},{8,9},{9,8},{10,11... | collective-permute-start | bytes 1179656 | tf_op jit(solution)/shard_map/ppermute | solution.py:218
  32.8 3.6 %copy-start = (f32[128,768]{1,0:T(8,128)}, f32[128,768]{1,0:T(8,128)S(1)}, u32[]{:S(2)}) copy-start(f32[128,768]{1,0:T(8,128)S(1)} %collective-permute-done.3.refs_0_) | copy-start | bytes 1179652
  32.9 3.6 %copy-start.2 = (f32[128,768]{1,0:T(8,128)}, f32[128,768]{1,0:T(8,128)S(1)}, u32[]{:S(2)}) copy-start(f32[128,768]{1,0:T(8,128)S(1)} %collective-permute-done.7.refs_2_) | copy-start | bytes 1179652
  32.9 3.6 %copy-start.4 = (f32[128,768]{1,0:T(8,128)}, f32[128,768]{1,0:T(8,128)S(1)}, u32[]{:S(2)}) copy-start(f32[128,768]{1,0:T(8,128)S(1)} %collective-permute-done.8.refs_3_) | copy-start | bytes 1179652
  36.4 19.5 %collective-permute-start.10 = (f32[256,768]{1,0:T(8,128)}, f32[256,768]{1,0:T(8,128)}, u32[]{:S(2)}, u32[]{:S(2)}) collective-permute-start(f32[256,768]{1,0:T(8,128)} %get-tuple-element.60), channel_id=1, source_target_pairs={{0,2},{1,3},{2,0},{3,1},{4,6},{5,7},{6,4},{7,5},{8,10},{9,11},{10,... | collective-permute-start | bytes 2359304 | tf_op jit(solution)/shard_map/ppermute | solution.py:218
  38.2 18.8 %collective-permute-start.11 = (f32[256,768]{1,0:T(8,128)}, f32[256,768]{1,0:T(8,128)}, u32[]{:S(2)}, u32[]{:S(2)}) collective-permute-start(f32[256,768]{1,0:T(8,128)} %get-tuple-element.61), channel_id=1, source_target_pairs={{0,4},{1,5},{2,6},{3,7},{4,0},{5,1},{6,2},{7,3},{8,12},{9,13},{10,... | collective-permute-start | bytes 2359304 | tf_op jit(solution)/shard_map/ppermute | solution.py:218
  39.7 1.0 copy-start.6
  40.7 32.7 %collective-permute-start.13 = (f32[768,384]{1,0:T(8,128)S(1)}, f32[768,384]{1,0:T(8,128)}, u32[]{:S(2)}, u32[]{:S(2)}) collective-permute-start(f32[768,384]{1,0:T(8,128)S(1)} %join.1.refs_4_), channel_id=1, source_target_pairs={{0,24},{24,0},{1,25},{25,1},{2,26},{26,2},{3,27},{27,3},{4,28},{28... | collective-permute-start | bytes 3538952 | tf_op jit(solution)/shard_map/ppermute | solution.py:199
  46.2 15.0 %collective-permute-start.2 = (f32[128,768]{1,0:T(8,128)S(1)}, f32[128,768]{1,0:T(8,128)S(1)}, u32[]{:S(2)}, u32[]{:S(2)}) collective-permute-start(f32[128,768]{1,0:T(8,128)S(1)} %get-tuple-element.54.refs_0_), channel_id=1, source_target_pairs={{0,1},{1,0},{2,3},{3,2},{4,5},{5,4},{6,7},{7,6},{8,9},{9,8},{10,11... | collective-permute-start | bytes 1179656 | tf_op jit(solution)/shard_map/ppermute | solution.py:218
  46.3 14.9 %collective-permute-start.4 = (f32[128,768]{1,0:T(8,128)}, f32[128,768]{1,0:T(8,128)S(1)}, u32[]{:S(2)}, u32[]{:S(2)}) collective-permute-start(f32[128,768]{1,0:T(8,128)} %copy-done), channel_id=1, source_target_pairs={{0,1},{1,0},{2,3},{3,2},{4,5},{5,4},{6,7},{7,6},{8,9},{9,8},{10,11... | collective-permute-start | bytes 1179656 | tf_op jit(solution)/shard_map/ppermute | solution.py:218
  57.1 42.5 %collective-permute-start.12 = (f32[768,384]{1,0:T(8,128)S(1)}, f32[768,384]{1,0:T(8,128)S(1)}, u32[]{:S(2)}, u32[]{:S(2)}) collective-permute-start(f32[768,384]{1,0:T(8,128)S(1)} %broadcast_select_fusion.1), channel_id=1, source_target_pairs={{8,0},{16,24},{0,16},{24,8},{9,1},{17,25},{1,17},{25,9},{10,2},{18... | collective-permute-start | bytes 3538952 | tf_op jit(solution)/shard_map/ppermute | solution.py:205
  65.1 8.3 %copy-start.7 = (f32[768,384]{1,0:T(8,128)S(1)}, f32[768,384]{1,0:T(8,128)}, u32[]{:S(2)}) copy-start(f32[768,384]{1,0:T(8,128)} %copy-done.6) | copy-start | bytes 3538948
  65.1 9.7 %collective-permute-start.14 = (f32[128,768]{1,0:T(8,128)S(1)}, f32[128,768]{1,0:T(8,128)S(1)}, u32[]{:S(2)}, u32[]{:S(2)}) collective-permute-start(f32[128,768]{1,0:T(8,128)S(1)} %get-tuple-element.68), channel_id=1, source_target_pairs={{0,4},{1,5},{2,6},{3,7},{4,0},{5,1},{6,2},{7,3},{8,12},{9,13},{10,... | collective-permute-start | bytes 1179656 | tf_op jit(solution)/shard_map/ppermute | solution.py:218
  67.9 6.9 %collective-permute-start.15 = (f32[128,768]{1,0:T(8,128)S(1)}, f32[128,768]{1,0:T(8,128)S(1)}, u32[]{:S(2)}, u32[]{:S(2)}) collective-permute-start(f32[128,768]{1,0:T(8,128)S(1)} %get-tuple-element.70), channel_id=1, source_target_pairs={{0,1},{1,0},{2,3},{3,2},{4,5},{5,4},{6,7},{7,6},{8,9},{9,8},{10,11... | collective-permute-start | bytes 1179656 | tf_op jit(solution)/shard_map/ppermute | solution.py:218
  68.0 11.0 %copy-start.1 = (f32[128,768]{1,0:T(8,128)S(1)}, f32[128,768]{1,0:T(8,128)}, u32[]{:S(2)}) copy-start(f32[128,768]{1,0:T(8,128)} %copy-done) | copy-start | bytes 1179652
  68.0 11.0 %copy-start.3 = (f32[128,768]{1,0:T(8,128)S(1)}, f32[128,768]{1,0:T(8,128)}, u32[]{:S(2)}) copy-start(f32[128,768]{1,0:T(8,128)} %copy-done.2) | copy-start | bytes 1179652
  68.0 10.9 %copy-start.5 = (f32[128,768]{1,0:T(8,128)S(1)}, f32[128,768]{1,0:T(8,128)}, u32[]{:S(2)}) copy-start(f32[128,768]{1,0:T(8,128)} %copy-done.4) | copy-start | bytes 1179652
  68.1 10.9 %collective-permute-start.16 = (f32[128,768]{1,0:T(8,128)S(1)}, f32[128,768]{1,0:T(8,128)S(1)}, u32[]{:S(2)}, u32[]{:S(2)}) collective-permute-start(f32[128,768]{1,0:T(8,128)S(1)} %get-tuple-element.71), channel_id=1, source_target_pairs={{0,3},{1,2},{2,1},{3,0},{4,7},{5,6},{6,5},{7,4},{8,11},{9,10},{10,... | collective-permute-start | bytes 1179656 | tf_op jit(solution)/shard_map/ppermute | solution.py:218
  80.4 11.8 %collective-permute-start.17 = (f32[256,384]{1,0:T(8,128)S(1)}, f32[256,384]{1,0:T(8,128)S(1)}, u32[]{:S(2)}, u32[]{:S(2)}) collective-permute-start(f32[256,384]{1,0:T(8,128)S(1)} %get-tuple-element.73), channel_id=1, source_target_pairs={{0,2},{1,3},{2,0},{3,1},{4,6},{5,7},{6,4},{7,5},{8,10},{9,11},{10,... | collective-permute-start | bytes 1179656 | tf_op jit(solution)/shard_map/ppermute | solution.py:218
  81.0 11.8 %collective-permute-start.19 = (f32[256,384]{1,0:T(8,128)S(1)}, f32[256,384]{1,0:T(8,128)S(1)}, u32[]{:S(2)}, u32[]{:S(2)}) collective-permute-start(f32[256,384]{1,0:T(8,128)S(1)} %get-tuple-element.74), channel_id=1, source_target_pairs={{0,4},{1,5},{2,6},{3,7},{4,0},{5,1},{6,2},{7,3},{8,12},{9,13},{10,... | collective-permute-start | bytes 1179656 | tf_op jit(solution)/shard_map/ppermute | solution.py:218
  92.2 6.7 %collective-permute-start.18 = (f32[128,384]{1,0:T(8,128)S(1)}, f32[128,384]{1,0:T(8,128)S(1)}, u32[]{:S(2)}, u32[]{:S(2)}) collective-permute-start(f32[128,384]{1,0:T(8,128)S(1)} %get-tuple-element.77), channel_id=1, source_target_pairs={{0,4},{1,5},{2,6},{3,7},{4,0},{5,1},{6,2},{7,3},{8,12},{9,13},{10,... | collective-permute-start | bytes 589832 | tf_op jit(solution)/shard_map/ppermute | solution.py:218
  92.8 6.1 %collective-permute-start.20 = (f32[128,384]{1,0:T(8,128)S(1)}, f32[128,384]{1,0:T(8,128)S(1)}, u32[]{:S(2)}, u32[]{:S(2)}) collective-permute-start(f32[128,384]{1,0:T(8,128)S(1)} %get-tuple-element.79), channel_id=1, source_target_pairs={{0,1},{1,0},{2,3},{3,2},{4,5},{5,4},{6,7},{7,6},{8,9},{9,8},{10,11... | collective-permute-start | bytes 589832 | tf_op jit(solution)/shard_map/ppermute | solution.py:218
  92.9 6.7 %collective-permute-start.21 = (f32[128,384]{1,0:T(8,128)S(1)}, f32[128,384]{1,0:T(8,128)S(1)}, u32[]{:S(2)}, u32[]{:S(2)}) collective-permute-start(f32[128,384]{1,0:T(8,128)S(1)} %get-tuple-element.80), channel_id=1, source_target_pairs={{0,3},{1,2},{2,1},{3,0},{4,7},{5,6},{6,5},{7,4},{8,11},{9,10},{10,... | collective-permute-start | bytes 589832 | tf_op jit(solution)/shard_map/ppermute | solution.py:218
  101.1 11.5 %collective-permute-start.22 = (f32[256,384]{1,0:T(8,128)S(1)}, f32[256,384]{1,0:T(8,128)S(1)}, u32[]{:S(2)}, u32[]{:S(2)}) collective-permute-start(f32[256,384]{1,0:T(8,128)S(1)} %get-tuple-element.83), channel_id=1, source_target_pairs={{0,2},{1,3},{2,0},{3,1},{4,6},{5,7},{6,4},{7,5},{8,10},{9,11},{10,... | collective-permute-start | bytes 1179656 | tf_op jit(solution)/shard_map/ppermute | solution.py:218
  102.3 11.9 %collective-permute-start.24 = (f32[256,384]{1,0:T(8,128)S(1)}, f32[256,384]{1,0:T(8,128)S(1)}, u32[]{:S(2)}, u32[]{:S(2)}) collective-permute-start(f32[256,384]{1,0:T(8,128)S(1)} %get-tuple-element.84), channel_id=1, source_target_pairs={{0,4},{1,5},{2,6},{3,7},{4,0},{5,1},{6,2},{7,3},{8,12},{9,13},{10,... | collective-permute-start | bytes 1179656 | tf_op jit(solution)/shard_map/ppermute | solution.py:218
  112.6 6.4 %collective-permute-start.23 = (f32[128,384]{1,0:T(8,128)S(1)}, f32[128,384]{1,0:T(8,128)S(1)}, u32[]{:S(2)}, u32[]{:S(2)}) collective-permute-start(f32[128,384]{1,0:T(8,128)S(1)} %get-tuple-element.88), channel_id=1, source_target_pairs={{0,4},{1,5},{2,6},{3,7},{4,0},{5,1},{6,2},{7,3},{8,12},{9,13},{10,... | collective-permute-start | bytes 589832 | tf_op jit(solution)/shard_map/ppermute | solution.py:218
  114.2 4.8 %collective-permute-start.25 = (f32[128,384]{1,0:T(8,128)S(1)}, f32[128,384]{1,0:T(8,128)S(1)}, u32[]{:S(2)}, u32[]{:S(2)}) collective-permute-start(f32[128,384]{1,0:T(8,128)S(1)} %get-tuple-element.90), channel_id=1, source_target_pairs={{0,1},{1,0},{2,3},{3,2},{4,5},{5,4},{6,7},{7,6},{8,9},{9,8},{10,11... | collective-permute-start | bytes 589832 | tf_op jit(solution)/shard_map/ppermute | solution.py:218
  114.3 6.7 %collective-permute-start.26 = (f32[128,384]{1,0:T(8,128)S(1)}, f32[128,384]{1,0:T(8,128)S(1)}, u32[]{:S(2)}, u32[]{:S(2)}) collective-permute-start(f32[128,384]{1,0:T(8,128)S(1)} %get-tuple-element.91), channel_id=1, source_target_pairs={{0,3},{1,2},{2,1},{3,0},{4,7},{5,6},{6,5},{7,4},{8,11},{9,10},{10,... | collective-permute-start | bytes 589832 | tf_op jit(solution)/shard_map/ppermute | solution.py:218

commit v13 on v12

--- a/solution.py
+++ b/solution.py
@@ -204,7 +204,7 @@
         moving = jnp.where(middle, after(centre, *earlier), own)
         return [(2, lax.ppermute(moving, "occ", [(1, 0), (2, 3), (0, 2), (3, 1)]))]
 
-    return [[(0, own), (1, near)], [(3, (middle, centre, far))], last]
+    return [[(0, own)], [(1, near)], [(3, (middle, centre, far))], last]
 
 
 def per_device(sizes, amplitudes, amp_mask, integrals, int_mask):
@@ -247,10 +247,10 @@
         right = list(lax.optimization_barrier((*right, *token))[: len(right)])
         sent = products([[rel[h][r] for r in away[h]] for h in range(2)], right)
         moving = [swap(sent[h], 2 * orders[h][0]) for h in range(2)]
-        if callable(stages[-1]):
-            stages[-1] = stages[-1](*moving)
         right[0] = after(right[0], *sent)
         held = list(products([[rel[h][r] for r in near[h]] for h in range(2)], right))
+        if n == 1 and callable(stages[-1]):
+            stages[-1] = stages[-1](*held)
         names = [near[0], near[1]]
         for level in range(1, len(bits)):
             for h in (1, 0):
@@ -261,7 +261,9 @@
                 moving[h] = swap(moved, 2 * bit + (h if level == len(bits) - 1 else 0))
                 names[h] = [names[h][i] for i in stays]
         pieces = [held[0], moving[0], swap(held[1], 1), moving[1]]
-        token = [*pieces[1:]] if out is None else [*pieces[1:], out]
+        token = pieces if n + 2 == len(stages) else held
+        if out is not None:
+            token = [*token, out]
         out = write(out, (rows, n_occ * width), ds, half, pieces)
     return out
 

time: 122 us -> 122 us (level)
  waiting for transfers between devices: 67.5 us -> 57.4 us
  starting transfers between devices: 31.5 us -> 36.7 us
  Pallas kernels: 20 us -> 24.4 us
    ppermute x23 -> x28, starting transfers between devices: 18.2 us -> 26.3 us  [swap(): return lax.ppermute(x, 'vir', [(i, i ^ bits) for i in range(n_vir)])]
    ppermute x23 -> x28, waiting for transfers between devices: 57.1 us -> 51.8 us  [swap(): return lax.ppermute(x, 'vir', [(i, i ^ bits) for i in range(n_vir)])]
    ppermute x1, waiting for transfers between devices: 4.75 us -> 0.01 us  [line_stages(): far = lax.ppermute(after(own, centre, near), 'occ', [(0, 3), (3, 0)])]
    pallas_call x15 -> x19, Pallas kernels: 17.4 us -> 21.2 us  [kernel_call(): pl.pallas_call(body, out_shape=[pltpu.VMEM(shape, jnp.float32) for shape...]
    ppermute x1, starting transfers between devices: 4.09 us -> 1.05 us  [last(): return [(2, lax.ppermute(moving, 'occ', [(1, 0), (2, 3), (0, 2), (3, 1)]))]]
    pallas_call x3 -> x4, Pallas kernels: 2.58 us -> 3.21 us  [write(): pl.pallas_call(functools.partial(write_kernel, ds, half), out_shape=jax.S...]
  transfers between devices with their start and end apart: 27 -> 32, of which waited for: 13 -> 12; matrix products, arithmetic and copies ran while one was open for 1% -> 1% of each run, Pallas kernels for 13% -> 17%
where the time goes in v13:
time: 122 us
  waiting for transfers between devices  57.4 us (47%)
  starting transfers between devices  36.7 us (30%)
  Pallas kernels  24.4 us (20%)
  other arithmetic  1.53 us (1%)
    ppermute x28, waiting for transfers between devices, swap(): return lax.ppermute(x, 'vir', [(i, i ^ bits) for i in range(n_vir)])  51.8 us
    ppermute x28, starting transfers between devices, swap(): return lax.ppermute(x, 'vir', [(i, i ^ bits) for i in range(n_vir)])  26.3 us
    pallas_call x19, Pallas kernels, kernel_call(): pl.pallas_call(body, out_shape=[pltpu.VMEM(shape, jnp.float32) for shape...  21.2 us
    ppermute x1, starting transfers between devices, line_stages(): far = lax.ppermute(after(own, centre, near), 'occ', [(0, 3), (3, 0)])  5.66 us
    ppermute x1, waiting for transfers between devices, direct(): return lax.ppermute(x, 'occ', [(i, i ^ d) for i in range(nodes)])  5.65 us
    pallas_call x4, Pallas kernels, write(): pl.pallas_call(functools.partial(write_kernel, ds, half), out_shape=jax.S...  3.21 us
    ppermute x1, starting transfers between devices, direct(): return lax.ppermute(x, 'occ', [(i, i ^ d) for i in range(nodes)])  3.01 us
  transfers between devices with their start and end apart: 32, of which 12 were waited for; matrix products, arithmetic and copies ran while one was open for 1% of the time, Pallas kernels for 17%

profile of v13, /device:TPU:0, one launch (start us, length us, event | category | flops | bytes accessed | tf_op | source)
XLA Modules:
  0.0 121.6 jit_solution(924898778974236768)
XLA Ops:
  0.0 1.3 %halves.1 = (f32[384,384]{1,0:T(8,128)S(1)}, f32[384,384]{1,0:T(8,128)S(1)}) custom-call(s32[3,6]{1,0:T(4,128)} %mask_hbm.1, f32[384,768]{1,0:T(8,128)} %int_hbm.1), custom_call_target="tpu_custom_call" | custom-call | flops 1 | bytes 1 | tf_op jit(solution)/shard_map/halves/pallas_call | solution.py:30
  1.3 0.5 collective-permute-start.5
  1.8 1.4 %cut.1 = (f32[128,768]{1,0:T(8,128)S(1)}, f32[128,768]{1,0:T(8,128)S(1)}, f32[128,768]{1,0:T(8,128)S(1)}, f32[128,768]{1,0:T(8,128)S(1)}) custom-call(s32[4,24]{1,0:T(4,128)} %mask_hbm.2, f32[128,3072]{1,0:T(8,128)} %amp_hbm.1), custom_call_target="tpu_custom_call" | custom-call | flops 1 | bytes 1 | tf_op jit(solution)/shard_map/cut/pallas_call | solution.py:30
  3.3 0.2 collective-permute-done.5.other_ref
  3.5 0.1 join.1.refs_4_
  3.6 3.0 %collective-permute-start.7 = (f32[768,384]{1,0:T(8,128)S(1)}, f32[768,384]{1,0:T(8,128)S(1)}, u32[]{:S(2)}, u32[]{:S(2)}) collective-permute-start(f32[768,384]{1,0:T(8,128)S(1)} %join.1.refs_4_), channel_id=1, source_target_pairs={{0,8},{8,0},{16,24},{24,16},{1,9},{9,1},{17,25},{25,17},{2,10},{10... | collective-permute-start | bytes 3538952 | tf_op jit(solution)/shard_map/ppermute | solution.py:193
  6.6 0.7 collective-permute-start.6
  7.3 1.6 %collective-permute-start = (f32[128,768]{1,0:T(8,128)S(1)}, f32[128,768]{1,0:T(8,128)S(1)}, u32[]{:S(2)}, u32[]{:S(2)}) collective-permute-start(f32[128,768]{1,0:T(8,128)S(1)} %get-tuple-element.60), channel_id=1, source_target_pairs={{0,4},{1,5},{2,6},{3,7},{4,0},{5,1},{6,2},{7,3},{8,12},{9,13},{10,... | collective-permute-start | bytes 1179656 | tf_op jit(solution)/shard_map/ppermute | solution.py:218
  8.9 1.4 %collective-permute-start.1 = (f32[128,768]{1,0:T(8,128)S(1)}, f32[128,768]{1,0:T(8,128)S(1)}, u32[]{:S(2)}, u32[]{:S(2)}) collective-permute-start(f32[128,768]{1,0:T(8,128)S(1)} %get-tuple-element.61), channel_id=1, source_target_pairs={{0,6},{1,7},{2,4},{3,5},{4,2},{5,3},{6,0},{7,1},{8,14},{9,15},{10,... | collective-permute-start | bytes 1179656 | tf_op jit(solution)/shard_map/ppermute | solution.py:218
  10.3 0.5 collective-permute-start.3
  10.9 15.8 %collective-permute-done.refs_1_ = f32[128,768]{1,0:T(8,128)S(1)} collective-permute-done((f32[128,768]{1,0:T(8,128)S(1)}, f32[128,768]{1,0:T(8,128)S(1)}, u32[]{:S(2)}, u32[]{:S(2)}) %collective-permute-start) | collective-permute-done | bytes 393248 | tf_op jit(solution)/shard_map/ppermute | solution.py:218
  26.7 0.5 collective-permute-start.9
  27.2 5.7 %collective-permute-done.7.refs_4_ = f32[768,384]{1,0:T(8,128)S(1)} collective-permute-done((f32[768,384]{1,0:T(8,128)S(1)}, f32[768,384]{1,0:T(8,128)S(1)}, u32[]{:S(2)}, u32[]{:S(2)}) %collective-permute-start.7) | collective-permute-done | bytes 1179680 | tf_op jit(solution)/shard_map/ppermute | solution.py:193
  32.8 1.0 copy-done.2
  33.9 5.7 %collective-permute-start.13 = (f32[768,384]{1,0:T(8,128)S(1)}, f32[768,384]{1,0:T(8,128)}, u32[]{:S(2)}, u32[]{:S(2)}) collective-permute-start(f32[768,384]{1,0:T(8,128)S(1)} %join.1.refs_4_), channel_id=1, source_target_pairs={{0,24},{24,0},{1,25},{25,1},{2,26},{26,2},{3,27},{27,3},{4,28},{28... | collective-permute-start | bytes 3538952 | tf_op jit(solution)/shard_map/ppermute | solution.py:199
  39.6 0.1 collective-permute-start.2
  39.6 0.0 collective-permute-done.3.refs_0_
  39.7 0.5 collective-permute-start.4
  40.1 0.0 collective-permute-done.9.refs_3_
  40.2 2.1 %products.8 = (f32[256,384]{1,0:T(8,128)}, f32[256,384]{1,0:T(8,128)}) custom-call(f32[128,768]{1,0:T(8,128)S(1)} %collective-permute-done.3.refs_0_, f32[128,768]{1,0:T(8,128)S(1)} %collective-permute-done.1.refs_1_, f32[128,768]{1,0:T(8,128)S(1)} %collective-permute-done.8.refs_2_, f32[128,768]{1,0:T(8,128)S(1)} %collective-permute-done.9.refs_3_, ...), custom_call_target="tpu_custom_call" | custom-call | flops 1 | bytes 1 | tf_op jit(solution)/shard_map/products/pallas_call | solution.py:30
  42.3 1.5 %collective-permute-start.11 = (f32[256,384]{1,0:T(8,128)}, f32[256,384]{1,0:T(8,128)}, u32[]{:S(2)}, u32[]{:S(2)}) collective-permute-start(f32[256,384]{1,0:T(8,128)} %get-tuple-element.67), channel_id=1, source_target_pairs={{0,4},{1,5},{2,6},{3,7},{4,0},{5,1},{6,2},{7,3},{8,12},{9,13},{10,... | collective-permute-start | bytes 1179656 | tf_op jit(solution)/shard_map/ppermute | solution.py:218
  43.8 1.5 %collective-permute-start.10 = (f32[256,384]{1,0:T(8,128)}, f32[256,384]{1,0:T(8,128)}, u32[]{:S(2)}, u32[]{:S(2)}) collective-permute-start(f32[256,384]{1,0:T(8,128)} %get-tuple-element.66), channel_id=1, source_target_pairs={{0,2},{1,3},{2,0},{3,1},{4,6},{5,7},{6,4},{7,5},{8,10},{9,11},{10,... | collective-permute-start | bytes 1179656 | tf_op jit(solution)/shard_map/ppermute | solution.py:218
  45.3 2.4 %products.9 = (f32[256,384]{1,0:T(8,128)S(1)}, f32[256,384]{1,0:T(8,128)S(1)}) custom-call(f32[128,768]{1,0:T(8,128)S(1)} %get-tuple-element.62.refs_0_, f32[128,768]{1,0:T(8,128)S(1)} %collective-permute-done.refs_1_, f32[128,768]{1,0:T(8,128)S(1)} %collective-permute-done.2.refs_2_, f32[128,768]{1,0:T(8,128)} %collective-permute-done.4.refs_3_, ...), custom_call_target="tpu_custom_call" | custom-call | flops 1 | bytes 1 | tf_op jit(solution)/shard_map/products/pallas_call | solution.py:30
  47.7 6.0 %collective-permute-done.11.got_ref = f32[256,384]{1,0:T(8,128)} collective-permute-done((f32[256,384]{1,0:T(8,128)}, f32[256,384]{1,0:T(8,128)}, u32[]{:S(2)}, u32[]{:S(2)}) %collective-permute-start.11) | collective-permute-done | bytes 393248 | tf_op jit(solution)/shard_map/ppermute | solution.py:218
  53.7 1.0 fold.9
  54.8 0.4 collective-permute-start.18
  55.2 1.3 %collective-permute-start.17 = (f32[128,384]{1,0:T(8,128)S(1)}, f32[128,384]{1,0:T(8,128)S(1)}, u32[]{:S(2)}, u32[]{:S(2)}) collective-permute-start(f32[128,384]{1,0:T(8,128)S(1)} %get-tuple-element.72), channel_id=1, source_target_pairs={{0,1},{1,0},{2,3},{3,2},{4,5},{5,4},{6,7},{7,6},{8,9},{9,8},{10,11... | collective-permute-start | bytes 589832 | tf_op jit(solution)/shard_map/ppermute | solution.py:218
  56.5 1.0 fold.8
  57.5 1.4 %products.10 = (f32[256,384]{1,0:T(8,128)S(1)}, f32[256,384]{1,0:T(8,128)S(1)}) custom-call(f32[128,768]{1,0:T(8,128)S(1)} %collective-permute-done.3.refs_0_, f32[128,768]{1,0:T(8,128)S(1)} %collective-permute-done.1.refs_1_, f32[128,768]{1,0:T(8,128)S(1)} %collective-permute-done.8.refs_2_, f32[128,768]{1,0:T(8,128)S(1)} %copy-done.1, f32[768,384]{1,0:T(8,128)S(1)} %copy-done.3), custom_call_target="tpu_custom_call" | custom-call | flops 1 | bytes 1 | tf_op jit(solution)/shard_map/products/pallas_call | solution.py:30
  58.9 0.6 collective-permute-start.14
  59.5 1.5 %collective-permute-start.15 = (f32[256,384]{1,0:T(8,128)S(1)}, f32[256,384]{1,0:T(8,128)S(1)}, u32[]{:S(2)}, u32[]{:S(2)}) collective-permute-start(f32[256,384]{1,0:T(8,128)S(1)} %get-tuple-element.75), channel_id=1, source_target_pairs={{0,4},{1,5},{2,6},{3,7},{4,0},{5,1},{6,2},{7,3},{8,12},{9,13},{10,... | collective-permute-start | bytes 1179656 | tf_op jit(solution)/shard_map/ppermute | solution.py:218
  61.0 2.4 %products.11 = (f32[256,384]{1,0:T(8,128)S(1)}, f32[256,384]{1,0:T(8,128)S(1)}) custom-call(f32[128,768]{1,0:T(8,128)S(1)} %get-tuple-element.62.refs_0_, f32[128,768]{1,0:T(8,128)S(1)} %collective-permute-done.refs_1_, f32[128,768]{1,0:T(8,128)S(1)} %collective-permute-done.2.refs_2_, f32[128,768]{1,0:T(8,128)} %collective-permute-done.4.refs_3_, ...), custom_call_target="tpu_custom_call" | custom-call | flops 1 | bytes 1 | tf_op jit(solution)/shard_map/products/pallas_call | solution.py:30
  63.5 0.1 broadcast_select_fusion.1
  63.6 1.0 collective-permute-start.12
  64.6 0.5 collective-permute-start.16
  65.2 9.3 %collective-permute-done.16.mine_b = f32[128,384]{1,0:T(8,128)S(1)} collective-permute-done((f32[128,384]{1,0:T(8,128)S(1)}, f32[128,384]{1,0:T(8,128)S(1)}, u32[]{:S(2)}, u32[]{:S(2)}) %collective-permute-start.16) | collective-permute-done | bytes 196640 | tf_op jit(solution)/shard_map/ppermute | solution.py:218
  74.5 0.8 write.4.refs_0_
  75.4 1.4 %broadcast_select_fusion.refs_4_ = f32[768,384]{1,0:T(8,128)S(1)} fusion(f32[768,384]{1,0:T(8,128)S(1)} %copy-done.5, f32[768,384]{1,0:T(8,128)} %collective-permute-done.13, pred[]{:T(512)S(6)} %or.3), kind=kLoop, calls=%fused_computation | loop fusion | flops 294912 | bytes 3538945 | tf_op jit(solution)/shard_map/jit(_where)/select_n | solution.py:246
  76.8 1.4 %products.12 = (f32[256,384]{1,0:T(8,128)S(1)}, f32[256,384]{1,0:T(8,128)S(1)}) custom-call(f32[128,768]{1,0:T(8,128)S(1)} %collective-permute-done.3.refs_0_, f32[128,768]{1,0:T(8,128)S(1)} %collective-permute-done.1.refs_1_, f32[128,768]{1,0:T(8,128)S(1)} %collective-permute-done.8.refs_2_, f32[128,768]{1,0:T(8,128)S(1)} %copy-done.1, ...), custom_call_target="tpu_custom_call" | custom-call | flops 1 | bytes 1 | tf_op jit(solution)/shard_map/products/pallas_call | solution.py:30
  78.3 1.6 %collective-permute-start.19 = (f32[256,384]{1,0:T(8,128)S(1)}, f32[256,384]{1,0:T(8,128)S(1)}, u32[]{:S(2)}, u32[]{:S(2)}) collective-permute-start(f32[256,384]{1,0:T(8,128)S(1)} %get-tuple-element.88), channel_id=1, source_target_pairs={{0,2},{1,3},{2,0},{3,1},{4,6},{5,7},{6,4},{7,5},{8,10},{9,11},{10,... | collective-permute-start | bytes 1179656 | tf_op jit(solution)/shard_map/ppermute | solution.py:218
  79.8 1.5 %collective-permute-start.21 = (f32[256,384]{1,0:T(8,128)S(1)}, f32[256,384]{1,0:T(8,128)S(1)}, u32[]{:S(2)}, u32[]{:S(2)}) collective-permute-start(f32[256,384]{1,0:T(8,128)S(1)} %get-tuple-element.89), channel_id=1, source_target_pairs={{0,4},{1,5},{2,6},{3,7},{4,0},{5,1},{6,2},{7,3},{8,12},{9,13},{10,... | collective-permute-start | bytes 1179656 | tf_op jit(solution)/shard_map/ppermute | solution.py:218
  81.3 0.6 collective-permute-start.25
  82.0 2.4 %products.13 = (f32[256,384]{1,0:T(8,128)S(1)}, f32[256,384]{1,0:T(8,128)S(1)}) custom-call(f32[128,768]{1,0:T(8,128)S(1)} %get-tuple-element.62.refs_0_, f32[128,768]{1,0:T(8,128)S(1)} %collective-permute-done.refs_1_, f32[128,768]{1,0:T(8,128)S(1)} %collective-permute-done.2.refs_2_, f32[128,768]{1,0:T(8,128)} %collective-permute-done.4.refs_3_, ...), custom_call_target="tpu_custom_call" | custom-call | flops 1 | bytes 1 | tf_op jit(solution)/shard_map/products/pallas_call | solution.py:30
  84.4 5.9 %collective-permute-done.19.got_ref = f32[256,384]{1,0:T(8,128)S(1)} collective-permute-done((f32[256,384]{1,0:T(8,128)S(1)}, f32[256,384]{1,0:T(8,128)S(1)}, u32[]{:S(2)}, u32[]{:S(2)}) %collective-permute-start.19) | collective-permute-done | bytes 393248 | tf_op jit(solution)/shard_map/ppermute | solution.py:218
  90.3 1.5 %collective-permute-start.24 = (f32[128,384]{1,0:T(8,128)S(1)}, f32[128,384]{1,0:T(8,128)S(1)}, u32[]{:S(2)}, u32[]{:S(2)}) collective-permute-start(f32[128,384]{1,0:T(8,128)S(1)} %get-tuple-element.97), channel_id=1, source_target_pairs={{0,4},{1,5},{2,6},{3,7},{4,0},{5,1},{6,2},{7,3},{8,12},{9,13},{10,... | collective-permute-start | bytes 589832 | tf_op jit(solution)/shard_map/ppermute | solution.py:218
  91.9 0.6 collective-permute-start.20
  92.5 0.1 collective-permute-start.22
  92.6 1.6 %collective-permute-start.23 = (f32[128,384]{1,0:T(8,128)S(1)}, f32[128,384]{1,0:T(8,128)S(1)}, u32[]{:S(2)}, u32[]{:S(2)}) collective-permute-start(f32[128,384]{1,0:T(8,128)S(1)} %get-tuple-element.96), channel_id=1, source_target_pairs={{0,3},{1,2},{2,1},{3,0},{4,7},{5,6},{6,5},{7,4},{8,11},{9,10},{10,... | collective-permute-start | bytes 589832 | tf_op jit(solution)/shard_map/ppermute | solution.py:218
  94.2 1.8 %collective-permute-done.24.mine_b = f32[128,384]{1,0:T(8,128)S(1)} collective-permute-done((f32[128,384]{1,0:T(8,128)S(1)}, f32[128,384]{1,0:T(8,128)S(1)}, u32[]{:S(2)}, u32[]{:S(2)}) %collective-permute-start.24) | collective-permute-done | bytes 196640 | tf_op jit(solution)/shard_map/ppermute | solution.py:218
  96.0 0.8 write.5.refs_0_
  96.8 1.3 %collective-permute-done.20.mine_b = f32[128,384]{1,0:T(8,128)S(1)} collective-permute-done((f32[128,384]{1,0:T(8,128)S(1)}, f32[128,384]{1,0:T(8,128)S(1)}, u32[]{:S(2)}, u32[]{:S(2)}) %collective-permute-start.20) | collective-permute-done | bytes 196640 | tf_op jit(solution)/shard_map/ppermute | solution.py:218
  98.1 1.2 collective-permute-done.23.other_b
  99.3 1.4 %products.14 = (f32[256,384]{1,0:T(8,128)S(1)}, f32[256,384]{1,0:T(8,128)S(1)}) custom-call(f32[128,768]{1,0:T(8,128)S(1)} %collective-permute-done.3.refs_0_, f32[128,768]{1,0:T(8,128)S(1)} %collective-permute-done.1.refs_1_, f32[128,768]{1,0:T(8,128)S(1)} %collective-permute-done.8.refs_2_, f32[128,768]{1,0:T(8,128)S(1)} %copy-done.1, ...), custom_call_target="tpu_custom_call" | custom-call | flops 1 | bytes 1 | tf_op jit(solution)/shard_map/products/pallas_call | solution.py:30
  100.7 1.6 %collective-permute-start.27 = (f32[256,384]{1,0:T(8,128)S(1)}, f32[256,384]{1,0:T(8,128)S(1)}, u32[]{:S(2)}, u32[]{:S(2)}) collective-permute-start(f32[256,384]{1,0:T(8,128)S(1)} %get-tuple-element.100), channel_id=1, source_target_pairs={{0,2},{1,3},{2,0},{3,1},{4,6},{5,7},{6,4},{7,5},{8,10},{9,11},{10,... | collective-permute-start | bytes 1179656 | tf_op jit(solution)/shard_map/ppermute | solution.py:218
  102.3 1.5 %collective-permute-start.29 = (f32[256,384]{1,0:T(8,128)S(1)}, f32[256,384]{1,0:T(8,128)S(1)}, u32[]{:S(2)}, u32[]{:S(2)}) collective-permute-start(f32[256,384]{1,0:T(8,128)S(1)} %get-tuple-element.101), channel_id=1, source_target_pairs={{0,4},{1,5},{2,6},{3,7},{4,0},{5,1},{6,2},{7,3},{8,12},{9,13},{10,... | collective-permute-start | bytes 1179656 | tf_op jit(solution)/shard_map/ppermute | solution.py:218
  103.8 2.4 %products.15 = (f32[256,384]{1,0:T(8,128)S(1)}, f32[256,384]{1,0:T(8,128)S(1)}) custom-call(f32[128,768]{1,0:T(8,128)S(1)} %get-tuple-element.62.refs_0_, f32[128,768]{1,0:T(8,128)S(1)} %collective-permute-done.refs_1_, f32[128,768]{1,0:T(8,128)S(1)} %collective-permute-done.2.refs_2_, f32[128,768]{1,0:T(8,128)} %collective-permute-done.4.refs_3_, ...), custom_call_target="tpu_custom_call" | custom-call | flops 1 | bytes 1 | tf_op jit(solution)/shard_map/products/pallas_call | solution.py:30
  106.2 6.0 %collective-permute-done.27.got_ref = f32[256,384]{1,0:T(8,128)S(1)} collective-permute-done((f32[256,384]{1,0:T(8,128)S(1)}, f32[256,384]{1,0:T(8,128)S(1)}, u32[]{:S(2)}, u32[]{:S(2)}) %collective-permute-start.27) | collective-permute-done | bytes 393248 | tf_op jit(solution)/shard_map/ppermute | solution.py:218
  112.2 1.6 %collective-permute-start.28 = (f32[128,384]{1,0:T(8,128)S(1)}, f32[128,384]{1,0:T(8,128)S(1)}, u32[]{:S(2)}, u32[]{:S(2)}) collective-permute-start(f32[128,384]{1,0:T(8,128)S(1)} %get-tuple-element.105), channel_id=1, source_target_pairs={{0,4},{1,5},{2,6},{3,7},{4,0},{5,1},{6,2},{7,3},{8,12},{9,13},{10,... | collective-permute-start | bytes 589832 | tf_op jit(solution)/shard_map/ppermute | solution.py:218
  113.8 0.1 collective-permute-start.30
  113.9 1.6 %collective-permute-start.31 = (f32[128,384]{1,0:T(8,128)S(1)}, f32[128,384]{1,0:T(8,128)S(1)}, u32[]{:S(2)}, u32[]{:S(2)}) collective-permute-start(f32[128,384]{1,0:T(8,128)S(1)} %get-tuple-element.108), channel_id=1, source_target_pairs={{0,3},{1,2},{2,1},{3,0},{4,7},{5,6},{6,5},{7,4},{8,11},{9,10},{10,... | collective-permute-start | bytes 589832 | tf_op jit(solution)/shard_map/ppermute | solution.py:218
  115.5 0.8 write.6.refs_0_
  116.3 2.3 %collective-permute-done.28.mine_b = f32[128,384]{1,0:T(8,128)S(1)} collective-permute-done((f32[128,384]{1,0:T(8,128)S(1)}, f32[128,384]{1,0:T(8,128)S(1)}, u32[]{:S(2)}, u32[]{:S(2)}) %collective-permute-start.28) | collective-permute-done | bytes 196640 | tf_op jit(solution)/shard_map/ppermute | solution.py:218
  118.7 2.0 %collective-permute-done.31.other_b = f32[128,384]{1,0:T(8,128)S(1)} collective-permute-done((f32[128,384]{1,0:T(8,128)S(1)}, f32[128,384]{1,0:T(8,128)S(1)}, u32[]{:S(2)}, u32[]{:S(2)}) %collective-permute-start.31) | collective-permute-done | bytes 196640 | tf_op jit(solution)/shard_map/ppermute | solution.py:218
  120.6 0.8 write.7
  (37 shorter events, 0.3 us)
Async XLA Ops:
  1.3 2.1 %collective-permute-start.5 = (f32[384,384]{1,0:T(8,128)S(1)}, f32[384,384]{1,0:T(8,128)S(1)}, u32[]{:S(2)}, u32[]{:S(2)}) collective-permute-start(f32[384,384]{1,0:T(8,128)S(1)} %get-tuple-element.64), channel_id=1, source_target_pairs={{0,1},{1,0},{2,3},{3,2},{4,5},{5,4},{6,7},{7,6},{8,9},{9,8},{10,11... | collective-permute-start | bytes 1769480 | tf_op jit(solution)/shard_map/ppermute | solution.py:218
  3.6 29.3 %collective-permute-start.7 = (f32[768,384]{1,0:T(8,128)S(1)}, f32[768,384]{1,0:T(8,128)S(1)}, u32[]{:S(2)}, u32[]{:S(2)}) collective-permute-start(f32[768,384]{1,0:T(8,128)S(1)} %join.1.refs_4_), channel_id=1, source_target_pairs={{0,8},{8,0},{16,24},{24,16},{1,9},{9,1},{17,25},{25,17},{2,10},{10... | collective-permute-start | bytes 3538952 | tf_op jit(solution)/shard_map/ppermute | solution.py:193
  6.6 27.3 %collective-permute-start.6 = (f32[768,384]{1,0:T(8,128)S(1)}, f32[768,384]{1,0:T(8,128)S(1)}, u32[]{:S(2)}, u32[]{:S(2)}) collective-permute-start(f32[768,384]{1,0:T(8,128)S(1)} %join.1.refs_4_), channel_id=1, source_target_pairs={{8,16},{16,8},{9,17},{17,9},{10,18},{18,10},{11,19},{19,11},{12,20... | collective-permute-start | bytes 3538952 | tf_op jit(solution)/shard_map/ppermute | solution.py:197
  7.3 19.4 %collective-permute-start = (f32[128,768]{1,0:T(8,128)S(1)}, f32[128,768]{1,0:T(8,128)S(1)}, u32[]{:S(2)}, u32[]{:S(2)}) collective-permute-start(f32[128,768]{1,0:T(8,128)S(1)} %get-tuple-element.60), channel_id=1, source_target_pairs={{0,4},{1,5},{2,6},{3,7},{4,0},{5,1},{6,2},{7,3},{8,12},{9,13},{10,... | collective-permute-start | bytes 1179656 | tf_op jit(solution)/shard_map/ppermute | solution.py:218
  8.9 17.8 %collective-permute-start.1 = (f32[128,768]{1,0:T(8,128)S(1)}, f32[128,768]{1,0:T(8,128)S(1)}, u32[]{:S(2)}, u32[]{:S(2)}) collective-permute-start(f32[128,768]{1,0:T(8,128)S(1)} %get-tuple-element.61), channel_id=1, source_target_pairs={{0,6},{1,7},{2,4},{3,5},{4,2},{5,3},{6,0},{7,1},{8,14},{9,15},{10,... | collective-permute-start | bytes 1179656 | tf_op jit(solution)/shard_map/ppermute | solution.py:218
  10.3 29.3 %collective-permute-start.3 = (f32[128,768]{1,0:T(8,128)S(1)}, f32[128,768]{1,0:T(8,128)S(1)}, u32[]{:S(2)}, u32[]{:S(2)}) collective-permute-start(f32[128,768]{1,0:T(8,128)S(1)} %get-tuple-element.63), channel_id=1, source_target_pairs={{0,2},{1,3},{2,0},{3,1},{4,6},{5,7},{6,4},{7,5},{8,10},{9,11},{10,... | collective-permute-start | bytes 1179656 | tf_op jit(solution)/shard_map/ppermute | solution.py:218
  26.7 13.5 %collective-permute-start.8 = (f32[128,768]{1,0:T(8,128)S(1)}, f32[128,768]{1,0:T(8,128)S(1)}, u32[]{:S(2)}, u32[]{:S(2)}) collective-permute-start(f32[128,768]{1,0:T(8,128)S(1)} %collective-permute-done.refs_1_), channel_id=1, source_target_pairs={{0,1},{1,0},{2,3},{3,2},{4,5},{5,4},{6,7},{7,6},{8,9},{9,8},{10,11... | collective-permute-start | bytes 1179656 | tf_op jit(solution)/shard_map/ppermute | solution.py:218
  26.7 13.5 %collective-permute-start.9 = (f32[128,768]{1,0:T(8,128)S(1)}, f32[128,768]{1,0:T(8,128)S(1)}, u32[]{:S(2)}, u32[]{:S(2)}) collective-permute-start(f32[128,768]{1,0:T(8,128)S(1)} %collective-permute-done.1.refs_1_), channel_id=1, source_target_pairs={{0,1},{1,0},{2,3},{3,2},{4,5},{5,4},{6,7},{7,6},{8,9},{9,8},{10,11... | collective-permute-start | bytes 1179656 | tf_op jit(solution)/shard_map/ppermute | solution.py:218
  32.8 1.0 copy-start.2
  33.9 6.3 %copy-start.4 = (f32[768,384]{1,0:T(8,128)}, f32[768,384]{1,0:T(8,128)S(1)}, u32[]{:S(2)}) copy-start(f32[768,384]{1,0:T(8,128)S(1)} %collective-permute-done.6) | copy-start | bytes 3538948
  33.9 41.5 %collective-permute-start.13 = (f32[768,384]{1,0:T(8,128)S(1)}, f32[768,384]{1,0:T(8,128)}, u32[]{:S(2)}, u32[]{:S(2)}) collective-permute-start(f32[768,384]{1,0:T(8,128)S(1)} %join.1.refs_4_), channel_id=1, source_target_pairs={{0,24},{24,0},{1,25},{25,1},{2,26},{26,2},{3,27},{27,3},{4,28},{28... | collective-permute-start | bytes 3538952 | tf_op jit(solution)/shard_map/ppermute | solution.py:199
  39.6 5.8 %collective-permute-start.2 = (f32[128,768]{1,0:T(8,128)S(1)}, f32[128,768]{1,0:T(8,128)S(1)}, u32[]{:S(2)}, u32[]{:S(2)}) collective-permute-start(f32[128,768]{1,0:T(8,128)S(1)} %get-tuple-element.62.refs_0_), channel_id=1, source_target_pairs={{0,1},{1,0},{2,3},{3,2},{4,5},{5,4},{6,7},{7,6},{8,9},{9,8},{10,11... | collective-permute-start | bytes 1179656 | tf_op jit(solution)/shard_map/ppermute | solution.py:218
  39.7 5.7 %collective-permute-start.4 = (f32[128,768]{1,0:T(8,128)S(1)}, f32[128,768]{1,0:T(8,128)}, u32[]{:S(2)}, u32[]{:S(2)}) collective-permute-start(f32[128,768]{1,0:T(8,128)S(1)} %collective-permute-done.3.refs_0_), channel_id=1, source_target_pairs={{0,1},{1,0},{2,3},{3,2},{4,5},{5,4},{6,7},{7,6},{8,9},{9,8},{10,11... | collective-permute-start | bytes 1179656 | tf_op jit(solution)/shard_map/ppermute | solution.py:218
  40.2 2.2 %copy-start = (f32[128,768]{1,0:T(8,128)}, f32[128,768]{1,0:T(8,128)S(1)}, u32[]{:S(2)}) copy-start(f32[128,768]{1,0:T(8,128)S(1)} %collective-permute-done.9.refs_3_) | copy-start | bytes 1179652
  42.3 11.4 %collective-permute-start.11 = (f32[256,384]{1,0:T(8,128)}, f32[256,384]{1,0:T(8,128)}, u32[]{:S(2)}, u32[]{:S(2)}) collective-permute-start(f32[256,384]{1,0:T(8,128)} %get-tuple-element.67), channel_id=1, source_target_pairs={{0,4},{1,5},{2,6},{3,7},{4,0},{5,1},{6,2},{7,3},{8,12},{9,13},{10,... | collective-permute-start | bytes 1179656 | tf_op jit(solution)/shard_map/ppermute | solution.py:218
  43.8 12.6 %collective-permute-start.10 = (f32[256,384]{1,0:T(8,128)}, f32[256,384]{1,0:T(8,128)}, u32[]{:S(2)}, u32[]{:S(2)}) collective-permute-start(f32[256,384]{1,0:T(8,128)} %get-tuple-element.66), channel_id=1, source_target_pairs={{0,2},{1,3},{2,0},{3,1},{4,6},{5,7},{6,4},{7,5},{8,10},{9,11},{10,... | collective-permute-start | bytes 1179656 | tf_op jit(solution)/shard_map/ppermute | solution.py:218
  47.7 9.8 %copy-start.1 = (f32[128,768]{1,0:T(8,128)S(1)}, f32[128,768]{1,0:T(8,128)}, u32[]{:S(2)}) copy-start(f32[128,768]{1,0:T(8,128)} %copy-done) | copy-start | bytes 1179652
  47.7 9.8 %copy-start.3 = (f32[768,384]{1,0:T(8,128)S(1)}, f32[768,384]{1,0:T(8,128)}, u32[]{:S(2)}) copy-start(f32[768,384]{1,0:T(8,128)} %copy-done.2) | copy-start | bytes 3538948
  54.8 8.8 %collective-permute-start.18 = (f32[128,384]{1,0:T(8,128)S(1)}, f32[128,384]{1,0:T(8,128)S(1)}, u32[]{:S(2)}, u32[]{:S(2)}) collective-permute-start(f32[128,384]{1,0:T(8,128)S(1)} %get-tuple-element.86), channel_id=1, source_target_pairs={{0,3},{1,2},{2,1},{3,0},{4,7},{5,6},{6,5},{7,4},{8,11},{9,10},{10,... | collective-permute-start | bytes 589832 | tf_op jit(solution)/shard_map/ppermute | solution.py:218
  55.2 9.5 %collective-permute-start.17 = (f32[128,384]{1,0:T(8,128)S(1)}, f32[128,384]{1,0:T(8,128)S(1)}, u32[]{:S(2)}, u32[]{:S(2)}) collective-permute-start(f32[128,384]{1,0:T(8,128)S(1)} %get-tuple-element.72), channel_id=1, source_target_pairs={{0,1},{1,0},{2,3},{3,2},{4,5},{5,4},{6,7},{7,6},{8,9},{9,8},{10,11... | collective-permute-start | bytes 589832 | tf_op jit(solution)/shard_map/ppermute | solution.py:218
  58.9 16.4 %collective-permute-start.14 = (f32[256,384]{1,0:T(8,128)S(1)}, f32[256,384]{1,0:T(8,128)S(1)}, u32[]{:S(2)}, u32[]{:S(2)}) collective-permute-start(f32[256,384]{1,0:T(8,128)S(1)} %get-tuple-element.74), channel_id=1, source_target_pairs={{0,2},{1,3},{2,0},{3,1},{4,6},{5,7},{6,4},{7,5},{8,10},{9,11},{10,... | collective-permute-start | bytes 1179656 | tf_op jit(solution)/shard_map/ppermute | solution.py:218
  59.5 3.9 %copy-start.5 = (f32[768,384]{1,0:T(8,128)S(1)}, f32[768,384]{1,0:T(8,128)}, u32[]{:S(2)}) copy-start(f32[768,384]{1,0:T(8,128)} %copy-done.4) | copy-start | bytes 3538948
  59.5 15.8 %collective-permute-start.15 = (f32[256,384]{1,0:T(8,128)S(1)}, f32[256,384]{1,0:T(8,128)S(1)}, u32[]{:S(2)}, u32[]{:S(2)}) collective-permute-start(f32[256,384]{1,0:T(8,128)S(1)} %get-tuple-element.75), channel_id=1, source_target_pairs={{0,4},{1,5},{2,6},{3,7},{4,0},{5,1},{6,2},{7,3},{8,12},{9,13},{10,... | collective-permute-start | bytes 1179656 | tf_op jit(solution)/shard_map/ppermute | solution.py:218
  63.6 33.2 %collective-permute-start.12 = (f32[768,384]{1,0:T(8,128)S(1)}, f32[768,384]{1,0:T(8,128)S(1)}, u32[]{:S(2)}, u32[]{:S(2)}) collective-permute-start(f32[768,384]{1,0:T(8,128)S(1)} %broadcast_select_fusion.1), channel_id=1, source_target_pairs={{8,0},{16,24},{0,16},{24,8},{9,1},{17,25},{1,17},{25,9},{10,2},{18... | collective-permute-start | bytes 3538952 | tf_op jit(solution)/shard_map/ppermute | solution.py:205
  64.6 9.8 %collective-permute-start.16 = (f32[128,384]{1,0:T(8,128)S(1)}, f32[128,384]{1,0:T(8,128)S(1)}, u32[]{:S(2)}, u32[]{:S(2)}) collective-permute-start(f32[128,384]{1,0:T(8,128)S(1)} %get-tuple-element.85), channel_id=1, source_target_pairs={{0,4},{1,5},{2,6},{3,7},{4,0},{5,1},{6,2},{7,3},{8,12},{9,13},{10,... | collective-permute-start | bytes 589832 | tf_op jit(solution)/shard_map/ppermute | solution.py:218
  78.3 12.0 %collective-permute-start.19 = (f32[256,384]{1,0:T(8,128)S(1)}, f32[256,384]{1,0:T(8,128)S(1)}, u32[]{:S(2)}, u32[]{:S(2)}) collective-permute-start(f32[256,384]{1,0:T(8,128)S(1)} %get-tuple-element.88), channel_id=1, source_target_pairs={{0,2},{1,3},{2,0},{3,1},{4,6},{5,7},{6,4},{7,5},{8,10},{9,11},{10,... | collective-permute-start | bytes 1179656 | tf_op jit(solution)/shard_map/ppermute | solution.py:218
  79.8 12.0 %collective-permute-start.21 = (f32[256,384]{1,0:T(8,128)S(1)}, f32[256,384]{1,0:T(8,128)S(1)}, u32[]{:S(2)}, u32[]{:S(2)}) collective-permute-start(f32[256,384]{1,0:T(8,128)S(1)} %get-tuple-element.89), channel_id=1, source_target_pairs={{0,4},{1,5},{2,6},{3,7},{4,0},{5,1},{6,2},{7,3},{8,12},{9,13},{10,... | collective-permute-start | bytes 1179656 | tf_op jit(solution)/shard_map/ppermute | solution.py:218
  81.3 11.1 %collective-permute-start.26 = (f32[128,384]{1,0:T(8,128)S(1)}, f32[128,384]{1,0:T(8,128)S(1)}, u32[]{:S(2)}, u32[]{:S(2)}) collective-permute-start(f32[128,384]{1,0:T(8,128)S(1)} %get-tuple-element.98), channel_id=1, source_target_pairs={{0,3},{1,2},{2,1},{3,0},{4,7},{5,6},{6,5},{7,4},{8,11},{9,10},{10,... | collective-permute-start | bytes 589832 | tf_op jit(solution)/shard_map/ppermute | solution.py:218
  81.3 11.2 %collective-permute-start.25 = (f32[128,384]{1,0:T(8,128)S(1)}, f32[128,384]{1,0:T(8,128)S(1)}, u32[]{:S(2)}, u32[]{:S(2)}) collective-permute-start(f32[128,384]{1,0:T(8,128)S(1)} %get-tuple-element.84), channel_id=1, source_target_pairs={{0,1},{1,0},{2,3},{3,2},{4,5},{5,4},{6,7},{7,6},{8,9},{9,8},{10,11... | collective-permute-start | bytes 589832 | tf_op jit(solution)/shard_map/ppermute | solution.py:218
  90.3 5.7 %collective-permute-start.24 = (f32[128,384]{1,0:T(8,128)S(1)}, f32[128,384]{1,0:T(8,128)S(1)}, u32[]{:S(2)}, u32[]{:S(2)}) collective-permute-start(f32[128,384]{1,0:T(8,128)S(1)} %get-tuple-element.97), channel_id=1, source_target_pairs={{0,4},{1,5},{2,6},{3,7},{4,0},{5,1},{6,2},{7,3},{8,12},{9,13},{10,... | collective-permute-start | bytes 589832 | tf_op jit(solution)/shard_map/ppermute | solution.py:218
  91.9 6.2 %collective-permute-start.20 = (f32[128,384]{1,0:T(8,128)S(1)}, f32[128,384]{1,0:T(8,128)S(1)}, u32[]{:S(2)}, u32[]{:S(2)}) collective-permute-start(f32[128,384]{1,0:T(8,128)S(1)} %get-tuple-element.93), channel_id=1, source_target_pairs={{0,4},{1,5},{2,6},{3,7},{4,0},{5,1},{6,2},{7,3},{8,12},{9,13},{10,... | collective-permute-start | bytes 589832 | tf_op jit(solution)/shard_map/ppermute | solution.py:218
  92.5 5.6 %collective-permute-start.22 = (f32[128,384]{1,0:T(8,128)S(1)}, f32[128,384]{1,0:T(8,128)S(1)}, u32[]{:S(2)}, u32[]{:S(2)}) collective-permute-start(f32[128,384]{1,0:T(8,128)S(1)} %get-tuple-element.95), channel_id=1, source_target_pairs={{0,1},{1,0},{2,3},{3,2},{4,5},{5,4},{6,7},{7,6},{8,9},{9,8},{10,11... | collective-permute-start | bytes 589832 | tf_op jit(solution)/shard_map/ppermute | solution.py:218
  92.6 6.7 %collective-permute-start.23 = (f32[128,384]{1,0:T(8,128)S(1)}, f32[128,384]{1,0:T(8,128)S(1)}, u32[]{:S(2)}, u32[]{:S(2)}) collective-permute-start(f32[128,384]{1,0:T(8,128)S(1)} %get-tuple-element.96), channel_id=1, source_target_pairs={{0,3},{1,2},{2,1},{3,0},{4,7},{5,6},{6,5},{7,4},{8,11},{9,10},{10,... | collective-permute-start | bytes 589832 | tf_op jit(solution)/shard_map/ppermute | solution.py:218
  100.7 11.5 %collective-permute-start.27 = (f32[256,384]{1,0:T(8,128)S(1)}, f32[256,384]{1,0:T(8,128)S(1)}, u32[]{:S(2)}, u32[]{:S(2)}) collective-permute-start(f32[256,384]{1,0:T(8,128)S(1)} %get-tuple-element.100), channel_id=1, source_target_pairs={{0,2},{1,3},{2,0},{3,1},{4,6},{5,7},{6,4},{7,5},{8,10},{9,11},{10,... | collective-permute-start | bytes 1179656 | tf_op jit(solution)/shard_map/ppermute | solution.py:218
  102.3 11.5 %collective-permute-start.29 = (f32[256,384]{1,0:T(8,128)S(1)}, f32[256,384]{1,0:T(8,128)S(1)}, u32[]{:S(2)}, u32[]{:S(2)}) collective-permute-start(f32[256,384]{1,0:T(8,128)S(1)} %get-tuple-element.101), channel_id=1, source_target_pairs={{0,4},{1,5},{2,6},{3,7},{4,0},{5,1},{6,2},{7,3},{8,12},{9,13},{10,... | collective-permute-start | bytes 1179656 | tf_op jit(solution)/shard_map/ppermute | solution.py:218
  112.2 6.4 %collective-permute-start.28 = (f32[128,384]{1,0:T(8,128)S(1)}, f32[128,384]{1,0:T(8,128)S(1)}, u32[]{:S(2)}, u32[]{:S(2)}) collective-permute-start(f32[128,384]{1,0:T(8,128)S(1)} %get-tuple-element.105), channel_id=1, source_target_pairs={{0,4},{1,5},{2,6},{3,7},{4,0},{5,1},{6,2},{7,3},{8,12},{9,13},{10,... | collective-permute-start | bytes 589832 | tf_op jit(solution)/shard_map/ppermute | solution.py:218
  113.8 4.8 %collective-permute-start.30 = (f32[128,384]{1,0:T(8,128)S(1)}, f32[128,384]{1,0:T(8,128)S(1)}, u32[]{:S(2)}, u32[]{:S(2)}) collective-permute-start(f32[128,384]{1,0:T(8,128)S(1)} %get-tuple-element.107), channel_id=1, source_target_pairs={{0,1},{1,0},{2,3},{3,2},{4,5},{5,4},{6,7},{7,6},{8,9},{9,8},{10,11... | collective-permute-start | bytes 589832 | tf_op jit(solution)/shard_map/ppermute | solution.py:218
  113.9 6.7 %collective-permute-start.31 = (f32[128,384]{1,0:T(8,128)S(1)}, f32[128,384]{1,0:T(8,128)S(1)}, u32[]{:S(2)}, u32[]{:S(2)}) collective-permute-start(f32[128,384]{1,0:T(8,128)S(1)} %get-tuple-element.108), channel_id=1, source_target_pairs={{0,3},{1,2},{2,1},{3,0},{4,7},{5,6},{6,5},{7,4},{8,11},{9,10},{10,... | collective-permute-start | bytes 589832 | tf_op jit(solution)/shard_map/ppermute | solution.py:218

commit v14 on v11

--- a/solution.py
+++ b/solution.py
@@ -128,36 +128,45 @@
     return kernel_call(functools.partial(fold_kernel, rows, stays, goes), outs, [held, got], "fold")
 
 
-def write_kernel(d, half, offset, held_ref, got_ref, other_ref, *refs):
+def total_kernel(rows, *refs):
+    total = refs[0][rows:, :]
+    for ref in refs[1:-1]:
+        total = total + ref[rows:, :]
+    refs[-1][...] = total
+
+
+def write_kernel(d, mine, other, *refs):
     out_ref, piece_ref, sems = refs[-3:]
     low = lax.axis_index("vir") % 2
-    place = lax.axis_index("occ") ^ d
-    width = held_ref.shape[1] // TILE_V
-    starts = [(2 * place + h) * (half // TILE_V) + offset // TILE_V for h in (low, 1 - low)]
-    piece_ref[...] = held_ref[...] + got_ref[...]
-    copies = [
-        pltpu.make_async_copy(source, out_ref.at[:, tiles(start, width)], sems.at[i])
-        for i, (source, start) in enumerate(zip((piece_ref, other_ref), starts))
-    ]
-    for copy in copies:
-        copy.start()
+    here = lax.axis_index("occ")
+    rows, width = piece_ref.shape[1:]
+    copies = []
+    for i, (h, parts) in enumerate(((low, refs[:mine]), (1 - low, refs[mine : mine + other]))):
+        total = parts[0][:rows, :]
+        for ref in parts[1:]:
+            total = total + ref[:rows, :]
+        piece_ref[i] = total
+        start = (2 * (here ^ d) + h) * (width // TILE_V)
+        copies.append(pltpu.make_async_copy(piece_ref.at[i], out_ref.at[:, tiles(start, width // TILE_V)], sems.at[i]))
+        copies[i].start()
     for copy in copies:
         copy.wait()
 
 
-def write(out, shape, d, half, offset, held, got, other):
+def write(out, shape, d, mine, other):
     given = [] if out is None else [out]
+    parts = [pltpu.with_memory_space_constraint(x, pltpu.VMEM) for x in [*mine, *other]]
     return pl.pallas_call(
-        functools.partial(write_kernel, d, half, offset),
+        functools.partial(write_kernel, d, len(mine), len(other)),
         out_shape=jax.ShapeDtypeStruct(shape, jnp.float32),
-        in_specs=in_vmem(3) + in_hbm(len(given)),
+        in_specs=in_vmem(len(parts)) + in_hbm(len(given)),
         out_specs=pl.BlockSpec(memory_space=pltpu.HBM),
-        scratch_shapes=[pltpu.VMEM(held.shape, jnp.float32), pltpu.SemaphoreType.DMA((2,))],
-        input_output_aliases={3: 0} if given else {},
+        scratch_shapes=[pltpu.VMEM((2, shape[0], other[0].shape[1]), jnp.float32), pltpu.SemaphoreType.DMA((2,))],
+        input_output_aliases={len(parts): 0} if given else {},
         compiler_params=pltpu.CompilerParams(vmem_limit_bytes=VMEM_LIMIT),
         cost_estimate=pl.CostEstimate(flops=1, bytes_accessed=1, transcendentals=0),
         name="write",
-    )(held, got, other, *given)
+    )(*parts, *given)
 
 
 def split(x):
@@ -165,27 +174,28 @@
     return high, (x - high.astype(jnp.float32)).astype(jnp.bfloat16)
 
 
-def dot_kernel(count, *refs):
-    left, block_ref, outs = refs[: 2 * count], refs[2 * count], refs[2 * count + 1 :]
+def dot_kernel(count, outs, *refs):
+    left, block_ref, out_refs = refs[: count * outs], refs[count * outs], refs[count * outs + 1 :]
     rows = left[0].shape[0]
     b_high, b_low = split(block_ref[...])
-    for h in range(2):
+    for h in range(outs):
         for i in range(count):
             a_high, a_low = split(left[h * count + i][...])
             total = None
             for a, b in ((a_high, b_low), (a_low, b_high), (a_high, b_high)):
                 term = jnp.dot(a, b, preferred_element_type=jnp.float32)
                 total = term if total is None else total + term
-            outs[h][i * rows : (i + 1) * rows, :] = total
+            out_refs[h][i * rows : (i + 1) * rows, :] = total
 
 
 def products(left, block):
     count = len(left[0])
     shape = (count * left[0][0].shape[0], block.shape[1])
-    return kernel_call(functools.partial(dot_kernel, count), [shape] * 2, [*left[0], *left[1], block], "products")
-
-
-def line_blocks(own, nodes):
+    body = functools.partial(dot_kernel, count, len(left))
+    return list(kernel_call(body, [shape] * len(left), [x for rows in left for x in rows] + [block], "products"))
+
+
+def line_stages(own, nodes):
     def direct(x, d):
         return lax.ppermute(x, "occ", [(i, i ^ d) for i in range(nodes)])
 
@@ -193,15 +203,15 @@
         return [(d, own if d == 0 else direct(own, d)) for d in range(nodes)]
     centre = lax.ppermute(own, "occ", [(1, 2), (2, 1)])
     near = direct(own, 1)
-    return [(0, own), (1, near), (3, centre), (2, None)]
-
-
-def far_blocks(own, near, centre):
     far = lax.ppermute(after(own, centre, near), "occ", [(0, 3), (3, 0)])
     here = lax.axis_index("occ")
     middle = (here == 1) | (here == 2)
-    last = lax.ppermute(jnp.where(middle, centre, own), "occ", [(1, 0), (2, 3), (0, 2), (3, 1)])
-    return (middle, centre, far), last
+
+    def last(*earlier):
+        moving = jnp.where(middle, after(centre, *earlier), own)
+        return 2, lax.ppermute(moving, "occ", [(1, 0), (2, 3), (0, 2), (3, 1)])
+
+    return [(0, own), (1, near), (3, (middle, centre, far)), last]
 
 
 def per_device(sizes, amplitudes, amp_mask, integrals, int_mask):
@@ -218,7 +228,7 @@
     other = swap(theirs, 1)
     parts = cut(after(amp_mask, mine), amplitudes, groups, depth)
     (whole,) = kernel_call(join_kernel, [(depth, half)], [mine, after(other, *parts)], "join")
-    blocks = line_blocks(whole, n_occ)
+    stages = line_stages(whole, n_occ)
 
     rel = [[parts[0]] + [None] * (groups - 1), [None] * groups]
     for r in range(groups - 1, 0, -1):
@@ -233,23 +243,31 @@
     away = [[r for r in range(groups) if r & o[0]] for o in orders]
     near = [[r for r in range(groups) if not r & o[0]] for o in orders]
 
+    shape = (rows, n_occ * width)
     out = None
-    token = settled = []
-    for n in range(n_occ):
-        d, block = blocks[n]
+    token = []
+    for n in range(len(stages)):
+        d, block = stages[n]
         if isinstance(block, tuple):
             middle, centre, far = block
-            centre, far = lax.optimization_barrier((centre, far, *token))[:2]
+            centre, far = lax.optimization_barrier((centre, far, *held))[:2]
             block = jnp.where(middle, centre, far)
-        elif n > 0:
+        if token:
             block = after(block, *token)
+        if n + 1 < len(stages):
+            order = list(range(groups - 1, 0, -1))
+            sent = products([[rel[0][r], rel[1][r]] for r in order], block)
+            moving = [swap(sent[i], 2 * r) for i, r in enumerate(order)]
+            held = products([[rel[0][0], rel[1][0]]], after(block, *sent))
+            (theirs,) = kernel_call(functools.partial(total_kernel, rows), [(rows, width // 2)], [*held, *moving], "total")
+            token = held if out is None else [*held, out]
+            out = write(out, shape, d, [*held, *moving], [swap(theirs, 1)])
+            if n == 1 and callable(stages[-1]):
+                stages[-1] = stages[-1](*held)
+            continue
         sent = products([[rel[h][r] for r in away[h]] for h in range(2)], block)
         moving = [swap(sent[h], 2 * orders[h][0]) for h in range(2)]
-        if n == 0 and blocks[-1][1] is None:
-            first, second = lax.optimization_barrier((blocks[1][1], blocks[2][1], *sent))[:2]
-            passed = far_blocks(block, first, second)
-            blocks[1:] = [(1, first), (3, passed[0]), (2, passed[1])]
-        held = list(products([[rel[h][r] for r in near[h]] for h in range(2)], after(block, *sent, *settled)))
+        held = products([[rel[h][r] for r in near[h]] for h in range(2)], after(block, *sent))
         names = [near[0], near[1]]
         for level in range(1, len(bits)):
             for h in (1, 0):
@@ -257,12 +275,9 @@
                 stays = [i for i, r in enumerate(names[h]) if not r & bit]
                 goes = [i for i, r in enumerate(names[h]) if r & bit]
                 held[h], moved = fold(rows, stays, goes, held[h], moving[h])
-                moving[h] = swap(moved, 2 * bit)
+                moving[h] = swap(moved, 2 * bit + (h if level == len(bits) - 1 else 0))
                 names[h] = [names[h][i] for i in stays]
-        token = held if n == 0 else [*moving, out]
-        settled = moving if n == 0 else []
-        (theirs,) = fold(rows, [0], [], held[1], moving[1])
-        out = write(out, (rows, n_occ * width), d, half, 0, held[0], moving[0], swap(theirs, 1))
+        out = write(out, shape, d, [held[0], moving[0]], [swap(held[1], 1), moving[1]])
     return out
 
 

time: 123 us -> 137 us (1.11)
  waiting for transfers between devices: 66.3 us -> 79.6 us
  Pallas kernels: 20.4 us -> 23.1 us
    ppermute x3, waiting for transfers between devices: 0.01 us -> 11.9 us  [the longest x1 11.9 us: last(): return (2, lax.ppermute(moving, 'occ', [(1, 0), (2, 3), (0, 2), (3, 1)]))]
    ppermute x28 -> x25, waiting for transfers between devices: 63.1 us -> 67.7 us  [swap(): return lax.ppermute(x, 'vir', [(i, i ^ bits) for i in range(n_vir)])]
    ppermute x1, waiting for transfers between devices: 3.26 us -> 0.01 us  [direct(): return lax.ppermute(x, 'occ', [(i, i ^ d) for i in range(nodes)])]
    ppermute x1, starting transfers between devices: 5.76 us -> 3.01 us  [direct(): return lax.ppermute(x, 'occ', [(i, i ^ d) for i in range(nodes)])]
    pallas_call x23 -> x16, Pallas kernels: 17.3 us -> 19.9 us  [kernel_call(): pl.pallas_call(body, out_shape=[pltpu.VMEM(shape, jnp.float32) for shape...]
    ppermute x3, starting transfers between devices: 4.5 us -> 6.79 us  [the longest x1 4.37 us: line_stages(): far = lax.ppermute(after(own, centre, near), 'occ', [(0, 3), (3, 0)])]
    ppermute x28 -> x25, starting transfers between devices: 22.1 us -> 21.9 us  [swap(): return lax.ppermute(x, 'vir', [(i, i ^ bits) for i in range(n_vir)])]
  transfers between devices with their start and end apart: 32 -> 29, of which waited for: 19 -> 17; matrix products, arithmetic and copies ran while one was open for 1% -> 0% of each run, Pallas kernels for 14% -> 14%
where the time goes in v14:
time: 137 us
  waiting for transfers between devices  79.6 us (58%)
  starting transfers between devices  31.7 us (23%)
  Pallas kernels  23.1 us (17%)
  local copies, waits for them, and re-layouts  1.76 us (1%)
    ppermute x25, waiting for transfers between devices, swap(): return lax.ppermute(x, 'vir', [(i, i ^ bits) for i in range(n_vir)])  67.7 us
    ppermute x25, starting transfers between devices, swap(): return lax.ppermute(x, 'vir', [(i, i ^ bits) for i in range(n_vir)])  21.9 us
    pallas_call x16, Pallas kernels, kernel_call(): pl.pallas_call(body, out_shape=[pltpu.VMEM(shape, jnp.float32) for shape...  19.9 us
    ppermute x1, waiting for transfers between devices, last(): return (2, lax.ppermute(moving, 'occ', [(1, 0), (2, 3), (0, 2), (3, 1)]))  11.9 us
    ppermute x1, starting transfers between devices, line_stages(): far = lax.ppermute(after(own, centre, near), 'occ', [(0, 3), (3, 0)])  4.37 us
    pallas_call x4, Pallas kernels, write(): pl.pallas_call(functools.partial(write_kernel, d, len(mine), len(other)),...  3.17 us
    ppermute x1, starting transfers between devices, direct(): return lax.ppermute(x, 'occ', [(i, i ^ d) for i in range(nodes)])  3.01 us
  transfers between devices with their start and end apart: 29, of which 17 were waited for; matrix products, arithmetic and copies ran while one was open for 0% of the time, Pallas kernels for 14%

profile of v14, /device:TPU:0, one launch (start us, length us, event | category | flops | bytes accessed | tf_op | source)
XLA Modules:
  0.0 136.8 jit_solution(6186363815423366540)
XLA Ops:
  0.0 1.3 halves.1
  1.3 0.5 collective-permute-start.5
  1.8 1.4 %cut.1 = (f32[128,768]{1,0:T(8,128)S(1)}, f32[128,768]{1,0:T(8,128)S(1)}, f32[128,768]{1,0:T(8,128)S(1)}, f32[128,768]{1,0:T(8,128)S(1)}) custom-call(s32[4,24]{1,0:T(4,128)} %mask_hbm.2, f32[128,3072]{1,0:T(8,128)} %amp_hbm.1), custom_call_target="tpu_custom_call" | custom-call | flops 1 | bytes 1 | tf_op jit(solution)/shard_map/cut/pallas_call | solution.py:30
  3.3 0.2 collective-permute-done.5.other_ref
  3.5 0.1 join.1.refs_6_.refs_2_
  3.6 3.0 %collective-permute-start.7 = (f32[768,384]{1,0:T(8,128)S(1)}, f32[768,384]{1,0:T(8,128)}, u32[]{:S(2)}, u32[]{:S(2)}) collective-permute-start(f32[768,384]{1,0:T(8,128)S(1)} %join.1.refs_6_.refs_2_), channel_id=1, source_target_pairs={{0,8},{8,0},{16,24},{24,16},{1,9},{9,1},{17,25},{25,17},{2,10},{10... | collective-permute-start | bytes 3538952 | tf_op jit(solution)/shard_map/ppermute | solution.py:200
  6.6 1.7 %collective-permute-start.6 = (f32[768,384]{1,0:T(8,128)S(1)}, f32[768,384]{1,0:T(8,128)}, u32[]{:S(2)}, u32[]{:S(2)}) collective-permute-start(f32[768,384]{1,0:T(8,128)S(1)} %join.1.refs_6_.refs_2_), channel_id=1, source_target_pairs={{8,16},{16,8},{9,17},{17,9},{10,18},{18,10},{11,19},{19,11},{12,20... | collective-permute-start | bytes 3538952 | tf_op jit(solution)/shard_map/ppermute | solution.py:204
  8.3 1.5 %collective-permute-start = (f32[128,768]{1,0:T(8,128)S(1)}, f32[128,768]{1,0:T(8,128)S(1)}, u32[]{:S(2)}, u32[]{:S(2)}) collective-permute-start(f32[128,768]{1,0:T(8,128)S(1)} %get-tuple-element.45), channel_id=1, source_target_pairs={{0,4},{1,5},{2,6},{3,7},{4,0},{5,1},{6,2},{7,3},{8,12},{9,13},{10,... | collective-permute-start | bytes 1179656 | tf_op jit(solution)/shard_map/ppermute | solution.py:225
  9.8 1.4 %collective-permute-start.1 = (f32[128,768]{1,0:T(8,128)S(1)}, f32[128,768]{1,0:T(8,128)S(1)}, u32[]{:S(2)}, u32[]{:S(2)}) collective-permute-start(f32[128,768]{1,0:T(8,128)S(1)} %get-tuple-element.46), channel_id=1, source_target_pairs={{0,6},{1,7},{2,4},{3,5},{4,2},{5,3},{6,0},{7,1},{8,14},{9,15},{10,... | collective-permute-start | bytes 1179656 | tf_op jit(solution)/shard_map/ppermute | solution.py:225
  11.2 0.5 collective-permute-start.3
  11.8 15.8 %collective-permute-done.refs_2_.refs_1_ = f32[128,768]{1,0:T(8,128)S(1)} collective-permute-done((f32[128,768]{1,0:T(8,128)S(1)}, f32[128,768]{1,0:T(8,128)S(1)}, u32[]{:S(2)}, u32[]{:S(2)}) %collective-permute-start) | collective-permute-done | bytes 393248 | tf_op jit(solution)/shard_map/ppermute | solution.py:225
  27.6 0.5 collective-permute-start.8
  28.1 0.7 collective-permute-done.3.refs_4_.refs_0_
  28.8 1.0 collective-permute-done.9.refs_3_.refs_2_
  29.8 0.8 copy-done
  30.5 0.1 collective-permute-start.2
  30.7 1.0 copy-done.1
  31.7 3.0 %products.8 = (f32[256,384]{1,0:T(8,128)S(1)}, f32[256,384]{1,0:T(8,128)S(1)}, f32[256,384]{1,0:T(8,128)S(1)}) custom-call(f32[128,768]{1,0:T(8,128)S(1)} %collective-permute-done.1.refs_0_.refs_1_, f32[128,768]{1,0:T(8,128)} %collective-permute-done.8.refs_1_.refs_3_, f32[128,768]{1,0:T(8,128)S(1)} %collective-permute-done.refs_2_.refs_1_, ...), custom_call_target="tpu_custom_call" | custom-call | flops 1 | bytes 1 | tf_op jit(solution)/shard_map/products/pallas_call | solution.py:30
  34.7 2.5 %collective-permute-start.12 = (f32[256,384]{1,0:T(8,128)S(1)}, f32[256,384]{1,0:T(8,128)S(1)}, u32[]{:S(2)}, u32[]{:S(2)}) collective-permute-start(f32[256,384]{1,0:T(8,128)S(1)} %get-tuple-element.51), channel_id=1, source_target_pairs={{0,6},{1,7},{2,4},{3,5},{4,2},{5,3},{6,0},{7,1},{8,14},{9,15},{10,... | collective-permute-start | bytes 1179656 | tf_op jit(solution)/shard_map/ppermute | solution.py:225
  37.2 0.5 collective-permute-start.13
  37.7 0.5 collective-permute-start.14
  38.3 4.4 %collective-permute-start.11 = (f32[768,384]{1,0:T(8,128)S(1)}, f32[768,384]{1,0:T(8,128)S(1)}, u32[]{:S(2)}, u32[]{:S(2)}) collective-permute-start(f32[768,384]{1,0:T(8,128)S(1)} %join.1.refs_6_.refs_2_), channel_id=1, source_target_pairs={{0,24},{24,0},{1,25},{25,1},{2,26},{26,2},{3,27},{27,3},{4,28},{28... | collective-permute-start | bytes 3538952 | tf_op jit(solution)/shard_map/ppermute | solution.py:206
  42.7 0.8 products.9.refs_0_
  43.4 3.4 %products.10 = (f32[256,384]{1,0:T(8,128)S(1)}, f32[256,384]{1,0:T(8,128)S(1)}, f32[256,384]{1,0:T(8,128)S(1)}) custom-call(f32[128,768]{1,0:T(8,128)S(1)} %collective-permute-done.1.refs_0_.refs_1_, f32[128,768]{1,0:T(8,128)} %collective-permute-done.8.refs_1_.refs_3_, f32[128,768]{1,0:T(8,128)S(1)} %collective-permute-done.refs_2_.refs_1_, ...), custom_call_target="tpu_custom_call" | custom-call | flops 1 | bytes 1 | tf_op jit(solution)/shard_map/products/pallas_call | solution.py:30
  46.9 2.0 %products.11.refs_0_ = f32[256,384]{1,0:T(8,128)S(1)} custom-call(f32[128,768]{1,0:T(8,128)S(1)} %get-tuple-element.47.refs_0_, f32[128,768]{1,0:T(8,128)S(1)} %collective-permute-done.2.refs_1_.refs_2_, f32[768,384]{1,0:T(8,128)} %collective-permute-done.7.refs_6_.refs_2_), custom_call_target="tpu_custom_call" | custom-call | flops 1 | bytes 1 | tf_op jit(solution)/shard_map/products/pallas_call | solution.py:30
  48.9 0.1 broadcast_select_fusion.1
  49.1 0.7 collective-permute-start.10
  49.8 5.7 %collective-permute-done.13.refs_2_ = f32[256,384]{1,0:T(8,128)S(1)} collective-permute-done((f32[256,384]{1,0:T(8,128)S(1)}, f32[256,384]{1,0:T(8,128)S(1)}, u32[]{:S(2)}, u32[]{:S(2)}) %collective-permute-start.13) | collective-permute-done | bytes 393248 | tf_op jit(solution)/shard_map/ppermute | solution.py:225
  55.5 0.1 collective-permute-done.14.refs_3_
  55.6 0.1 collective-permute-start.15
  55.7 1.7 %collective-permute-start.16 = (f32[256,384]{1,0:T(8,128)S(1)}, f32[256,384]{1,0:T(8,128)S(1)}, u32[]{:S(2)}, u32[]{:S(2)}) collective-permute-start(f32[256,384]{1,0:T(8,128)S(1)} %get-tuple-element.56), channel_id=1, source_target_pairs={{0,6},{1,7},{2,4},{3,5},{4,2},{5,3},{6,0},{7,1},{8,14},{9,15},{10,... | collective-permute-start | bytes 1179656 | tf_op jit(solution)/shard_map/ppermute | solution.py:225
  57.4 1.3 collective-permute-start.17
  58.7 0.5 collective-permute-start.18
  59.3 0.8 write.4.refs_5_
  60.1 8.6 %collective-permute-done.16.refs_1_ = f32[256,384]{1,0:T(8,128)S(1)} collective-permute-done((f32[256,384]{1,0:T(8,128)S(1)}, f32[256,384]{1,0:T(8,128)S(1)}, u32[]{:S(2)}, u32[]{:S(2)}) %collective-permute-start.16) | collective-permute-done | bytes 393248 | tf_op jit(solution)/shard_map/ppermute | solution.py:225
  68.6 7.9 %collective-permute-done.17.refs_2_ = f32[256,384]{1,0:T(8,128)S(1)} collective-permute-done((f32[256,384]{1,0:T(8,128)S(1)}, f32[256,384]{1,0:T(8,128)S(1)}, u32[]{:S(2)}, u32[]{:S(2)}) %collective-permute-start.17) | collective-permute-done | bytes 393248 | tf_op jit(solution)/shard_map/ppermute | solution.py:225
  76.6 0.0 collective-permute-done.18.refs_3_
  76.6 0.1 collective-permute-start.19
  76.7 0.2 broadcast_select_fusion.refs_6_.refs_2_
  76.9 1.2 collective-permute-done.19.refs_4_
  78.1 0.8 write.5.refs_5_
  78.9 3.0 %products.12 = (f32[256,384]{1,0:T(8,128)S(1)}, f32[256,384]{1,0:T(8,128)S(1)}, f32[256,384]{1,0:T(8,128)S(1)}) custom-call(f32[128,768]{1,0:T(8,128)S(1)} %collective-permute-done.1.refs_0_.refs_1_, f32[128,768]{1,0:T(8,128)} %collective-permute-done.8.refs_1_.refs_3_, f32[128,768]{1,0:T(8,128)S(1)} %collective-permute-done.refs_2_.refs_1_, ...), custom_call_target="tpu_custom_call" | custom-call | flops 1 | bytes 1 | tf_op jit(solution)/shard_map/products/pallas_call | solution.py:30
  82.0 0.8 products.13.refs_0_
  82.8 11.9 %collective-permute-done.10.refs_4_ = f32[768,384]{1,0:T(8,128)S(1)} collective-permute-done((f32[768,384]{1,0:T(8,128)S(1)}, f32[768,384]{1,0:T(8,128)S(1)}, u32[]{:S(2)}, u32[]{:S(2)}) %collective-permute-start.10) | collective-permute-done | bytes 1179680 | tf_op jit(solution)/shard_map/ppermute | solution.py:212
  94.6 2.4 %products.14 = (f32[256,384]{1,0:T(8,128)S(1)}, f32[256,384]{1,0:T(8,128)S(1)}) custom-call(f32[128,768]{1,0:T(8,128)S(1)} %collective-permute-done.3.refs_4_.refs_0_, f32[128,768]{1,0:T(8,128)S(1)} %collective-permute-done.1.refs_0_.refs_1_, f32[128,768]{1,0:T(8,128)S(1)} %copy-done.2, f32[128,768]{1,0:T(8,128)} %collective-permute-done.8.refs_1_.refs_3_, ...), custom_call_target="tpu_custom_call" | custom-call | flops 1 | bytes 1 | tf_op jit(solution)/shard_map/products/pallas_call | solution.py:30
  97.0 1.6 %collective-permute-start.20 = (f32[256,384]{1,0:T(8,128)S(1)}, f32[256,384]{1,0:T(8,128)S(1)}, u32[]{:S(2)}, u32[]{:S(2)}) collective-permute-start(f32[256,384]{1,0:T(8,128)S(1)} %get-tuple-element.70), channel_id=1, source_target_pairs={{0,2},{1,3},{2,0},{3,1},{4,6},{5,7},{6,4},{7,5},{8,10},{9,11},{10,... | collective-permute-start | bytes 1179656 | tf_op jit(solution)/shard_map/ppermute | solution.py:225
  98.6 1.5 %collective-permute-start.25 = (f32[256,384]{1,0:T(8,128)S(1)}, f32[256,384]{1,0:T(8,128)S(1)}, u32[]{:S(2)}, u32[]{:S(2)}) collective-permute-start(f32[256,384]{1,0:T(8,128)S(1)} %get-tuple-element.65), channel_id=1, source_target_pairs={{0,6},{1,7},{2,4},{3,5},{4,2},{5,3},{6,0},{7,1},{8,14},{9,15},{10,... | collective-permute-start | bytes 1179656 | tf_op jit(solution)/shard_map/ppermute | solution.py:225
  100.1 0.5 collective-permute-start.26
  100.6 1.5 %collective-permute-start.27 = (f32[256,384]{1,0:T(8,128)S(1)}, f32[256,384]{1,0:T(8,128)S(1)}, u32[]{:S(2)}, u32[]{:S(2)}) collective-permute-start(f32[256,384]{1,0:T(8,128)S(1)} %get-tuple-element.67), channel_id=1, source_target_pairs={{0,2},{1,3},{2,0},{3,1},{4,6},{5,7},{6,4},{7,5},{8,10},{9,11},{10,... | collective-permute-start | bytes 1179656 | tf_op jit(solution)/shard_map/ppermute | solution.py:225
  102.1 1.5 %collective-permute-start.22 = (f32[256,384]{1,0:T(8,128)S(1)}, f32[256,384]{1,0:T(8,128)S(1)}, u32[]{:S(2)}, u32[]{:S(2)}) collective-permute-start(f32[256,384]{1,0:T(8,128)S(1)} %get-tuple-element.71), channel_id=1, source_target_pairs={{0,4},{1,5},{2,6},{3,7},{4,0},{5,1},{6,2},{7,3},{8,12},{9,13},{10,... | collective-permute-start | bytes 1179656 | tf_op jit(solution)/shard_map/ppermute | solution.py:225
  103.6 1.4 %products.15 = (f32[256,384]{1,0:T(8,128)S(1)}, f32[256,384]{1,0:T(8,128)S(1)}) custom-call(f32[128,768]{1,0:T(8,128)S(1)} %get-tuple-element.47.refs_0_, f32[128,768]{1,0:T(8,128)S(1)} %collective-permute-done.refs_2_.refs_1_, f32[128,768]{1,0:T(8,128)S(1)} %collective-permute-done.2.refs_1_.refs_2_, f32[128,768]{1,0:T(8,128)S(1)} %collective-permute-done.4.refs_5_.refs_3_, ...), custom_call_target="tpu_custom_call" | custom-call | flops 1 | bytes 1 | tf_op jit(solution)/shard_map/products/pallas_call | solution.py:30
  105.0 4.1 %collective-permute-done.20.got_ref = f32[256,384]{1,0:T(8,128)S(1)} collective-permute-done((f32[256,384]{1,0:T(8,128)S(1)}, f32[256,384]{1,0:T(8,128)S(1)}, u32[]{:S(2)}, u32[]{:S(2)}) %collective-permute-start.20) | collective-permute-done | bytes 393248 | tf_op jit(solution)/shard_map/ppermute | solution.py:225
  109.1 1.6 %collective-permute-start.21 = (f32[128,384]{1,0:T(8,128)S(1)}, f32[128,384]{1,0:T(8,128)S(1)}, u32[]{:S(2)}, u32[]{:S(2)}) collective-permute-start(f32[128,384]{1,0:T(8,128)S(1)} %get-tuple-element.75), channel_id=1, source_target_pairs={{0,4},{1,5},{2,6},{3,7},{4,0},{5,1},{6,2},{7,3},{8,12},{9,13},{10,... | collective-permute-start | bytes 589832 | tf_op jit(solution)/shard_map/ppermute | solution.py:225
  110.7 7.8 %collective-permute-done.25.refs_1_ = f32[256,384]{1,0:T(8,128)S(1)} collective-permute-done((f32[256,384]{1,0:T(8,128)S(1)}, f32[256,384]{1,0:T(8,128)S(1)}, u32[]{:S(2)}, u32[]{:S(2)}) %collective-permute-start.25) | collective-permute-done | bytes 393248 | tf_op jit(solution)/shard_map/ppermute | solution.py:225
  118.5 2.1 %collective-permute-done.26.refs_2_ = f32[256,384]{1,0:T(8,128)S(1)} collective-permute-done((f32[256,384]{1,0:T(8,128)S(1)}, f32[256,384]{1,0:T(8,128)S(1)}, u32[]{:S(2)}, u32[]{:S(2)}) %collective-permute-start.26) | collective-permute-done | bytes 393248 | tf_op jit(solution)/shard_map/ppermute | solution.py:225
  120.6 4.5 %collective-permute-done.27.refs_3_ = f32[256,384]{1,0:T(8,128)S(1)} collective-permute-done((f32[256,384]{1,0:T(8,128)S(1)}, f32[256,384]{1,0:T(8,128)S(1)}, u32[]{:S(2)}, u32[]{:S(2)}) %collective-permute-start.27) | collective-permute-done | bytes 393248 | tf_op jit(solution)/shard_map/ppermute | solution.py:225
  125.1 0.1 collective-permute-start.28
  125.2 3.8 %collective-permute-done.22.got_ref = f32[256,384]{1,0:T(8,128)S(1)} collective-permute-done((f32[256,384]{1,0:T(8,128)S(1)}, f32[256,384]{1,0:T(8,128)S(1)}, u32[]{:S(2)}, u32[]{:S(2)}) %collective-permute-start.22) | collective-permute-done | bytes 393248 | tf_op jit(solution)/shard_map/ppermute | solution.py:225
  129.0 0.1 collective-permute-start.23
  129.1 1.6 %collective-permute-start.24 = (f32[128,384]{1,0:T(8,128)S(1)}, f32[128,384]{1,0:T(8,128)S(1)}, u32[]{:S(2)}, u32[]{:S(2)}) collective-permute-start(f32[128,384]{1,0:T(8,128)S(1)} %get-tuple-element.78), channel_id=1, source_target_pairs={{0,3},{1,2},{2,1},{3,0},{4,7},{5,6},{6,5},{7,4},{8,11},{9,10},{10,... | collective-permute-start | bytes 589832 | tf_op jit(solution)/shard_map/ppermute | solution.py:225
  130.7 0.8 write.6.refs_4_
  131.5 0.1 collective-permute-done.21.refs_1_
  131.6 4.2 %collective-permute-done.24.refs_3_ = f32[128,384]{1,0:T(8,128)S(1)} collective-permute-done((f32[128,384]{1,0:T(8,128)S(1)}, f32[128,384]{1,0:T(8,128)S(1)}, u32[]{:S(2)}, u32[]{:S(2)}) %collective-permute-start.24) | collective-permute-done | bytes 196640 | tf_op jit(solution)/shard_map/ppermute | solution.py:225
  135.8 0.8 write.7
  (22 shorter events, 0.2 us)
Async XLA Ops:
  1.3 2.1 %collective-permute-start.5 = (f32[384,384]{1,0:T(8,128)S(1)}, f32[384,384]{1,0:T(8,128)S(1)}, u32[]{:S(2)}, u32[]{:S(2)}) collective-permute-start(f32[384,384]{1,0:T(8,128)S(1)} %get-tuple-element.49), channel_id=1, source_target_pairs={{0,1},{1,0},{2,3},{3,2},{4,5},{5,4},{6,7},{7,6},{8,9},{9,8},{10,11... | collective-permute-start | bytes 1769480 | tf_op jit(solution)/shard_map/ppermute | solution.py:225
  3.6 34.2 %collective-permute-start.7 = (f32[768,384]{1,0:T(8,128)S(1)}, f32[768,384]{1,0:T(8,128)}, u32[]{:S(2)}, u32[]{:S(2)}) collective-permute-start(f32[768,384]{1,0:T(8,128)S(1)} %join.1.refs_6_.refs_2_), channel_id=1, source_target_pairs={{0,8},{8,0},{16,24},{24,16},{1,9},{9,1},{17,25},{25,17},{2,10},{10... | collective-permute-start | bytes 3538952 | tf_op jit(solution)/shard_map/ppermute | solution.py:200
  6.6 31.7 %collective-permute-start.6 = (f32[768,384]{1,0:T(8,128)S(1)}, f32[768,384]{1,0:T(8,128)}, u32[]{:S(2)}, u32[]{:S(2)}) collective-permute-start(f32[768,384]{1,0:T(8,128)S(1)} %join.1.refs_6_.refs_2_), channel_id=1, source_target_pairs={{8,16},{16,8},{9,17},{17,9},{10,18},{18,10},{11,19},{19,11},{12,20... | collective-permute-start | bytes 3538952 | tf_op jit(solution)/shard_map/ppermute | solution.py:204
  8.3 19.3 %collective-permute-start = (f32[128,768]{1,0:T(8,128)S(1)}, f32[128,768]{1,0:T(8,128)S(1)}, u32[]{:S(2)}, u32[]{:S(2)}) collective-permute-start(f32[128,768]{1,0:T(8,128)S(1)} %get-tuple-element.45), channel_id=1, source_target_pairs={{0,4},{1,5},{2,6},{3,7},{4,0},{5,1},{6,2},{7,3},{8,12},{9,13},{10,... | collective-permute-start | bytes 1179656 | tf_op jit(solution)/shard_map/ppermute | solution.py:225
  9.8 17.8 %collective-permute-start.1 = (f32[128,768]{1,0:T(8,128)S(1)}, f32[128,768]{1,0:T(8,128)S(1)}, u32[]{:S(2)}, u32[]{:S(2)}) collective-permute-start(f32[128,768]{1,0:T(8,128)S(1)} %get-tuple-element.46), channel_id=1, source_target_pairs={{0,6},{1,7},{2,4},{3,5},{4,2},{5,3},{6,0},{7,1},{8,14},{9,15},{10,... | collective-permute-start | bytes 1179656 | tf_op jit(solution)/shard_map/ppermute | solution.py:225
  11.2 17.6 %collective-permute-start.3 = (f32[128,768]{1,0:T(8,128)S(1)}, f32[128,768]{1,0:T(8,128)S(1)}, u32[]{:S(2)}, u32[]{:S(2)}) collective-permute-start(f32[128,768]{1,0:T(8,128)S(1)} %get-tuple-element.48), channel_id=1, source_target_pairs={{0,2},{1,3},{2,0},{3,1},{4,6},{5,7},{6,4},{7,5},{8,10},{9,11},{10,... | collective-permute-start | bytes 1179656 | tf_op jit(solution)/shard_map/ppermute | solution.py:225
  27.6 2.2 %collective-permute-start.9 = (f32[128,768]{1,0:T(8,128)S(1)}, f32[128,768]{1,0:T(8,128)S(1)}, u32[]{:S(2)}, u32[]{:S(2)}) collective-permute-start(f32[128,768]{1,0:T(8,128)S(1)} %collective-permute-done.refs_2_.refs_1_), channel_id=1, source_target_pairs={{0,1},{1,0},{2,3},{3,2},{4,5},{5,4},{6,7},{7,6},{8,9},{9,8},{10,11... | collective-permute-start | bytes 1179656 | tf_op jit(solution)/shard_map/ppermute | solution.py:225
  27.6 3.1 %collective-permute-start.8 = (f32[128,768]{1,0:T(8,128)S(1)}, f32[128,768]{1,0:T(8,128)}, u32[]{:S(2)}, u32[]{:S(2)}) collective-permute-start(f32[128,768]{1,0:T(8,128)S(1)} %collective-permute-done.1.refs_0_.refs_1_), channel_id=1, source_target_pairs={{0,1},{1,0},{2,3},{3,2},{4,5},{5,4},{6,7},{7,6},{8,9},{9,8},{10,11... | collective-permute-start | bytes 1179656 | tf_op jit(solution)/shard_map/ppermute | solution.py:225
  28.8 1.9 %collective-permute-start.4 = (f32[128,768]{1,0:T(8,128)S(1)}, f32[128,768]{1,0:T(8,128)S(1)}, u32[]{:S(2)}, u32[]{:S(2)}) collective-permute-start(f32[128,768]{1,0:T(8,128)S(1)} %collective-permute-done.3.refs_4_.refs_0_), channel_id=1, source_target_pairs={{0,1},{1,0},{2,3},{3,2},{4,5},{5,4},{6,7},{7,6},{8,9},{9,8},{10,11... | collective-permute-start | bytes 1179656 | tf_op jit(solution)/shard_map/ppermute | solution.py:225
  29.8 0.8 copy-start
  30.5 12.1 %collective-permute-start.2 = (f32[128,768]{1,0:T(8,128)S(1)}, f32[128,768]{1,0:T(8,128)S(1)}, u32[]{:S(2)}, u32[]{:S(2)}) collective-permute-start(f32[128,768]{1,0:T(8,128)S(1)} %get-tuple-element.47.refs_0_), channel_id=1, source_target_pairs={{0,1},{1,0},{2,3},{3,2},{4,5},{5,4},{6,7},{7,6},{8,9},{9,8},{10,11... | collective-permute-start | bytes 1179656 | tf_op jit(solution)/shard_map/ppermute | solution.py:225
  30.7 1.0 copy-start.1
  34.7 15.1 %collective-permute-start.12 = (f32[256,384]{1,0:T(8,128)S(1)}, f32[256,384]{1,0:T(8,128)S(1)}, u32[]{:S(2)}, u32[]{:S(2)}) collective-permute-start(f32[256,384]{1,0:T(8,128)S(1)} %get-tuple-element.51), channel_id=1, source_target_pairs={{0,6},{1,7},{2,4},{3,5},{4,2},{5,3},{6,0},{7,1},{8,14},{9,15},{10,... | collective-permute-start | bytes 1179656 | tf_op jit(solution)/shard_map/ppermute | solution.py:225
  37.2 18.3 %collective-permute-start.13 = (f32[256,384]{1,0:T(8,128)S(1)}, f32[256,384]{1,0:T(8,128)S(1)}, u32[]{:S(2)}, u32[]{:S(2)}) collective-permute-start(f32[256,384]{1,0:T(8,128)S(1)} %get-tuple-element.52), channel_id=1, source_target_pairs={{0,4},{1,5},{2,6},{3,7},{4,0},{5,1},{6,2},{7,3},{8,12},{9,13},{10,... | collective-permute-start | bytes 1179656 | tf_op jit(solution)/shard_map/ppermute | solution.py:225
  37.7 17.8 %collective-permute-start.14 = (f32[256,384]{1,0:T(8,128)S(1)}, f32[256,384]{1,0:T(8,128)S(1)}, u32[]{:S(2)}, u32[]{:S(2)}) collective-permute-start(f32[256,384]{1,0:T(8,128)S(1)} %get-tuple-element.53), channel_id=1, source_target_pairs={{0,2},{1,3},{2,0},{3,1},{4,6},{5,7},{6,4},{7,5},{8,10},{9,11},{10,... | collective-permute-start | bytes 1179656 | tf_op jit(solution)/shard_map/ppermute | solution.py:225
  38.3 38.4 %collective-permute-start.11 = (f32[768,384]{1,0:T(8,128)S(1)}, f32[768,384]{1,0:T(8,128)S(1)}, u32[]{:S(2)}, u32[]{:S(2)}) collective-permute-start(f32[768,384]{1,0:T(8,128)S(1)} %join.1.refs_6_.refs_2_), channel_id=1, source_target_pairs={{0,24},{24,0},{1,25},{25,1},{2,26},{26,2},{3,27},{27,3},{4,28},{28... | collective-permute-start | bytes 3538952 | tf_op jit(solution)/shard_map/ppermute | solution.py:206
  49.1 45.6 %collective-permute-start.10 = (f32[768,384]{1,0:T(8,128)S(1)}, f32[768,384]{1,0:T(8,128)S(1)}, u32[]{:S(2)}, u32[]{:S(2)}) collective-permute-start(f32[768,384]{1,0:T(8,128)S(1)} %broadcast_select_fusion.1), channel_id=1, source_target_pairs={{8,0},{16,24},{0,16},{24,8},{9,1},{17,25},{1,17},{25,9},{10,2},{18... | collective-permute-start | bytes 3538952 | tf_op jit(solution)/shard_map/ppermute | solution.py:212
  55.6 3.1 %collective-permute-start.15 = (f32[128,384]{1,0:T(8,128)S(1)}, f32[128,384]{1,0:T(8,128)S(1)}, u32[]{:S(2)}, u32[]{:S(2)}) collective-permute-start(f32[128,384]{1,0:T(8,128)S(1)} %total.3), channel_id=1, source_target_pairs={{0,1},{1,0},{2,3},{3,2},{4,5},{5,4},{6,7},{7,6},{8,9},{9,8},{10,11... | collective-permute-start | bytes 589832 | tf_op jit(solution)/shard_map/ppermute | solution.py:225
  55.7 12.9 %collective-permute-start.16 = (f32[256,384]{1,0:T(8,128)S(1)}, f32[256,384]{1,0:T(8,128)S(1)}, u32[]{:S(2)}, u32[]{:S(2)}) collective-permute-start(f32[256,384]{1,0:T(8,128)S(1)} %get-tuple-element.56), channel_id=1, source_target_pairs={{0,6},{1,7},{2,4},{3,5},{4,2},{5,3},{6,0},{7,1},{8,14},{9,15},{10,... | collective-permute-start | bytes 1179656 | tf_op jit(solution)/shard_map/ppermute | solution.py:225
  57.4 19.1 %collective-permute-start.17 = (f32[256,384]{1,0:T(8,128)S(1)}, f32[256,384]{1,0:T(8,128)S(1)}, u32[]{:S(2)}, u32[]{:S(2)}) collective-permute-start(f32[256,384]{1,0:T(8,128)S(1)} %get-tuple-element.57), channel_id=1, source_target_pairs={{0,4},{1,5},{2,6},{3,7},{4,0},{5,1},{6,2},{7,3},{8,12},{9,13},{10,... | collective-permute-start | bytes 1179656 | tf_op jit(solution)/shard_map/ppermute | solution.py:225
  58.7 17.8 %collective-permute-start.18 = (f32[256,384]{1,0:T(8,128)S(1)}, f32[256,384]{1,0:T(8,128)S(1)}, u32[]{:S(2)}, u32[]{:S(2)}) collective-permute-start(f32[256,384]{1,0:T(8,128)S(1)} %get-tuple-element.58), channel_id=1, source_target_pairs={{0,2},{1,3},{2,0},{3,1},{4,6},{5,7},{6,4},{7,5},{8,10},{9,11},{10,... | collective-permute-start | bytes 1179656 | tf_op jit(solution)/shard_map/ppermute | solution.py:225
  76.6 1.5 %collective-permute-start.19 = (f32[128,384]{1,0:T(8,128)S(1)}, f32[128,384]{1,0:T(8,128)S(1)}, u32[]{:S(2)}, u32[]{:S(2)}) collective-permute-start(f32[128,384]{1,0:T(8,128)S(1)} %total.4), channel_id=1, source_target_pairs={{0,1},{1,0},{2,3},{3,2},{4,5},{5,4},{6,7},{7,6},{8,9},{9,8},{10,11... | collective-permute-start | bytes 589832 | tf_op jit(solution)/shard_map/ppermute | solution.py:225
  76.9 2.0 %copy-start.2 = (f32[128,768]{1,0:T(8,128)S(1)}, f32[128,768]{1,0:T(8,128)}, u32[]{:S(2)}) copy-start(f32[128,768]{1,0:T(8,128)} %copy-done) | copy-start | bytes 1179652
  97.0 12.0 %collective-permute-start.20 = (f32[256,384]{1,0:T(8,128)S(1)}, f32[256,384]{1,0:T(8,128)S(1)}, u32[]{:S(2)}, u32[]{:S(2)}) collective-permute-start(f32[256,384]{1,0:T(8,128)S(1)} %get-tuple-element.70), channel_id=1, source_target_pairs={{0,2},{1,3},{2,0},{3,1},{4,6},{5,7},{6,4},{7,5},{8,10},{9,11},{10,... | collective-permute-start | bytes 1179656 | tf_op jit(solution)/shard_map/ppermute | solution.py:225
  98.6 19.9 %collective-permute-start.25 = (f32[256,384]{1,0:T(8,128)S(1)}, f32[256,384]{1,0:T(8,128)S(1)}, u32[]{:S(2)}, u32[]{:S(2)}) collective-permute-start(f32[256,384]{1,0:T(8,128)S(1)} %get-tuple-element.65), channel_id=1, source_target_pairs={{0,6},{1,7},{2,4},{3,5},{4,2},{5,3},{6,0},{7,1},{8,14},{9,15},{10,... | collective-permute-start | bytes 1179656 | tf_op jit(solution)/shard_map/ppermute | solution.py:225
  100.1 20.5 %collective-permute-start.26 = (f32[256,384]{1,0:T(8,128)S(1)}, f32[256,384]{1,0:T(8,128)S(1)}, u32[]{:S(2)}, u32[]{:S(2)}) collective-permute-start(f32[256,384]{1,0:T(8,128)S(1)} %get-tuple-element.66), channel_id=1, source_target_pairs={{0,4},{1,5},{2,6},{3,7},{4,0},{5,1},{6,2},{7,3},{8,12},{9,13},{10,... | collective-permute-start | bytes 1179656 | tf_op jit(solution)/shard_map/ppermute | solution.py:225
  100.6 24.4 %collective-permute-start.27 = (f32[256,384]{1,0:T(8,128)S(1)}, f32[256,384]{1,0:T(8,128)S(1)}, u32[]{:S(2)}, u32[]{:S(2)}) collective-permute-start(f32[256,384]{1,0:T(8,128)S(1)} %get-tuple-element.67), channel_id=1, source_target_pairs={{0,2},{1,3},{2,0},{3,1},{4,6},{5,7},{6,4},{7,5},{8,10},{9,11},{10,... | collective-permute-start | bytes 1179656 | tf_op jit(solution)/shard_map/ppermute | solution.py:225
  102.1 26.9 %collective-permute-start.22 = (f32[256,384]{1,0:T(8,128)S(1)}, f32[256,384]{1,0:T(8,128)S(1)}, u32[]{:S(2)}, u32[]{:S(2)}) collective-permute-start(f32[256,384]{1,0:T(8,128)S(1)} %get-tuple-element.71), channel_id=1, source_target_pairs={{0,4},{1,5},{2,6},{3,7},{4,0},{5,1},{6,2},{7,3},{8,12},{9,13},{10,... | collective-permute-start | bytes 1179656 | tf_op jit(solution)/shard_map/ppermute | solution.py:225
  109.1 22.5 %collective-permute-start.21 = (f32[128,384]{1,0:T(8,128)S(1)}, f32[128,384]{1,0:T(8,128)S(1)}, u32[]{:S(2)}, u32[]{:S(2)}) collective-permute-start(f32[128,384]{1,0:T(8,128)S(1)} %get-tuple-element.75), channel_id=1, source_target_pairs={{0,4},{1,5},{2,6},{3,7},{4,0},{5,1},{6,2},{7,3},{8,12},{9,13},{10,... | collective-permute-start | bytes 589832 | tf_op jit(solution)/shard_map/ppermute | solution.py:225
  125.1 5.7 %collective-permute-start.28 = (f32[128,384]{1,0:T(8,128)S(1)}, f32[128,384]{1,0:T(8,128)S(1)}, u32[]{:S(2)}, u32[]{:S(2)}) collective-permute-start(f32[128,384]{1,0:T(8,128)S(1)} %total.5), channel_id=1, source_target_pairs={{0,1},{1,0},{2,3},{3,2},{4,5},{5,4},{6,7},{7,6},{8,9},{9,8},{10,11... | collective-permute-start | bytes 589832 | tf_op jit(solution)/shard_map/ppermute | solution.py:225
  129.0 2.6 %collective-permute-start.23 = (f32[128,384]{1,0:T(8,128)S(1)}, f32[128,384]{1,0:T(8,128)S(1)}, u32[]{:S(2)}, u32[]{:S(2)}) collective-permute-start(f32[128,384]{1,0:T(8,128)S(1)} %get-tuple-element.77), channel_id=1, source_target_pairs={{0,1},{1,0},{2,3},{3,2},{4,5},{5,4},{6,7},{7,6},{8,9},{9,8},{10,11... | collective-permute-start | bytes 589832 | tf_op jit(solution)/shard_map/ppermute | solution.py:225
  129.1 6.7 %collective-permute-start.24 = (f32[128,384]{1,0:T(8,128)S(1)}, f32[128,384]{1,0:T(8,128)S(1)}, u32[]{:S(2)}, u32[]{:S(2)}) collective-permute-start(f32[128,384]{1,0:T(8,128)S(1)} %get-tuple-element.78), channel_id=1, source_target_pairs={{0,3},{1,2},{2,1},{3,0},{4,7},{5,6},{6,5},{7,4},{8,11},{9,10},{10,... | collective-permute-start | bytes 589832 | tf_op jit(solution)/shard_map/ppermute | solution.py:225

commit v15 on v14

--- a/solution.py
+++ b/solution.py
@@ -244,8 +244,14 @@
     near = [[r for r in range(groups) if not r & o[0]] for o in orders]
 
     shape = (rows, n_occ * width)
+
+    def finish(out, d, held, moving):
+        (theirs,) = kernel_call(functools.partial(total_kernel, rows), [(rows, width // 2)], [*held, *moving], "total")
+        return write(out, shape, d, [*held, *moving], [swap(theirs, 1)])
+
     out = None
     token = []
+    waiting = None
     for n in range(len(stages)):
         d, block = stages[n]
         if isinstance(block, tuple):
@@ -254,18 +260,24 @@
             block = jnp.where(middle, centre, far)
         if token:
             block = after(block, *token)
-        if n + 1 < len(stages):
+        if n + 2 < len(stages):
             order = list(range(groups - 1, 0, -1))
             sent = products([[rel[0][r], rel[1][r]] for r in order], block)
             moving = [swap(sent[i], 2 * r) for i, r in enumerate(order)]
             held = products([[rel[0][0], rel[1][0]]], after(block, *sent))
-            (theirs,) = kernel_call(functools.partial(total_kernel, rows), [(rows, width // 2)], [*held, *moving], "total")
             token = held if out is None else [*held, out]
-            out = write(out, shape, d, [*held, *moving], [swap(theirs, 1)])
+            if n + 3 < len(stages):
+                out = finish(out, d, held, moving)
+            else:
+                waiting = d, held, moving
             if n == 1 and callable(stages[-1]):
                 stages[-1] = stages[-1](*held)
             continue
         sent = products([[rel[h][r] for r in away[h]] for h in range(2)], block)
+        if waiting is not None:
+            d_before, held, moving = waiting
+            out = finish(out, d_before, held, list(lax.optimization_barrier((*moving, *sent))[: len(moving)]))
+            waiting = None
         moving = [swap(sent[h], 2 * orders[h][0]) for h in range(2)]
         held = products([[rel[h][r] for r in near[h]] for h in range(2)], after(block, *sent))
         names = [near[0], near[1]]
@@ -277,7 +289,9 @@
                 held[h], moved = fold(rows, stays, goes, held[h], moving[h])
                 moving[h] = swap(moved, 2 * bit + (h if level == len(bits) - 1 else 0))
                 names[h] = [names[h][i] for i in stays]
-        out = write(out, shape, d, [held[0], moving[0]], [swap(held[1], 1), moving[1]])
+        other = [swap(held[1], 1), moving[1]]
+        token = [held[0], moving[0], *other]
+        out = write(out, shape, d, [held[0], moving[0]], other)
     return out
 
 

time: 137 us -> 127 us (0.927)
  waiting for transfers between devices: 79.6 us -> 69.4 us
    ppermute x25 -> x26, waiting for transfers between devices: 67.7 us -> 44.9 us  [swap(): return lax.ppermute(x, 'vir', [(i, i ^ bits) for i in range(n_vir)])]
    ppermute x1, waiting for transfers between devices: 0.01 us -> 22 us  [direct(): return lax.ppermute(x, 'occ', [(i, i ^ d) for i in range(nodes)])]
    ppermute x1, waiting for transfers between devices: 11.9 us -> 2.57 us  [last(): return (2, lax.ppermute(moving, 'occ', [(1, 0), (2, 3), (0, 2), (3, 1)]))]
    pallas_call x16 -> x17, Pallas kernels: 19.9 us -> 18.8 us  [kernel_call(): pl.pallas_call(body, out_shape=[pltpu.VMEM(shape, jnp.float32) for shape...]
    ppermute x25 -> x26, starting transfers between devices: 21.9 us -> 21.3 us  [swap(): return lax.ppermute(x, 'vir', [(i, i ^ bits) for i in range(n_vir)])]
  transfers between devices with their start and end apart: 29 -> 30, of which waited for: 17 -> 16; matrix products, arithmetic and copies ran while one was open for 0% -> 1% of each run, Pallas kernels for 14% -> 16%
where the time goes in v15:
time: 127 us
  waiting for transfers between devices  69.4 us (55%)
  starting transfers between devices  31.8 us (25%)
  Pallas kernels  22 us (17%)
  other arithmetic  1.53 us (1%)
  local copies, waits for them, and re-layouts  1.52 us (1%)
    ppermute x26, waiting for transfers between devices, swap(): return lax.ppermute(x, 'vir', [(i, i ^ bits) for i in range(n_vir)])  44.9 us
    ppermute x1, waiting for transfers between devices, direct(): return lax.ppermute(x, 'occ', [(i, i ^ d) for i in range(nodes)])  22 us
    ppermute x26, starting transfers between devices, swap(): return lax.ppermute(x, 'vir', [(i, i ^ bits) for i in range(n_vir)])  21.3 us
    pallas_call x17, Pallas kernels, kernel_call(): pl.pallas_call(body, out_shape=[pltpu.VMEM(shape, jnp.float32) for shape...  18.8 us
    ppermute x1, starting transfers between devices, line_stages(): far = lax.ppermute(after(own, centre, near), 'occ', [(0, 3), (3, 0)])  5.66 us
    pallas_call x4, Pallas kernels, write(): pl.pallas_call(functools.partial(write_kernel, d, len(mine), len(other)),...  3.18 us
    ppermute x1, starting transfers between devices, direct(): return lax.ppermute(x, 'occ', [(i, i ^ d) for i in range(nodes)])  3.01 us
    ppermute x1, waiting for transfers between devices, last(): return (2, lax.ppermute(moving, 'occ', [(1, 0), (2, 3), (0, 2), (3, 1)]))  2.57 us
  transfers between devices with their start and end apart: 30, of which 16 were waited for; matrix products, arithmetic and copies ran while one was open for 1% of the time, Pallas kernels for 16%

profile of v15, /device:TPU:0, one launch (start us, length us, event | category | flops | bytes accessed | tf_op | source)
XLA Modules:
  0.0 126.7 jit_solution(14179321057828846995)
XLA Ops:
  0.0 1.3 %halves.1 = (f32[384,384]{1,0:T(8,128)S(1)}, f32[384,384]{1,0:T(8,128)S(1)}) custom-call(s32[3,6]{1,0:T(4,128)} %mask_hbm.1, f32[384,768]{1,0:T(8,128)} %int_hbm.1), custom_call_target="tpu_custom_call" | custom-call | flops 1 | bytes 1 | tf_op jit(solution)/shard_map/halves/pallas_call | solution.py:30
  1.3 0.5 collective-permute-start.5
  1.8 1.4 %cut.1 = (f32[128,768]{1,0:T(8,128)S(1)}, f32[128,768]{1,0:T(8,128)S(1)}, f32[128,768]{1,0:T(8,128)S(1)}, f32[128,768]{1,0:T(8,128)S(1)}) custom-call(s32[4,24]{1,0:T(4,128)} %mask_hbm.2, f32[128,3072]{1,0:T(8,128)} %amp_hbm.1), custom_call_target="tpu_custom_call" | custom-call | flops 1 | bytes 1 | tf_op jit(solution)/shard_map/cut/pallas_call | solution.py:30
  3.3 0.2 collective-permute-done.5.other_ref
  3.5 0.1 join.1.refs_6_.refs_2_
  3.6 3.0 %collective-permute-start.7 = (f32[768,384]{1,0:T(8,128)S(1)}, f32[768,384]{1,0:T(8,128)S(1)}, u32[]{:S(2)}, u32[]{:S(2)}) collective-permute-start(f32[768,384]{1,0:T(8,128)S(1)} %join.1.refs_6_.refs_2_), channel_id=1, source_target_pairs={{0,8},{8,0},{16,24},{24,16},{1,9},{9,1},{17,25},{25,17},{2,10},{10... | collective-permute-start | bytes 3538952 | tf_op jit(solution)/shard_map/ppermute | solution.py:200
  6.6 0.7 collective-permute-start.6
  7.3 1.6 %collective-permute-start = (f32[128,768]{1,0:T(8,128)S(1)}, f32[128,768]{1,0:T(8,128)S(1)}, u32[]{:S(2)}, u32[]{:S(2)}) collective-permute-start(f32[128,768]{1,0:T(8,128)S(1)} %get-tuple-element.53), channel_id=1, source_target_pairs={{0,4},{1,5},{2,6},{3,7},{4,0},{5,1},{6,2},{7,3},{8,12},{9,13},{10,... | collective-permute-start | bytes 1179656 | tf_op jit(solution)/shard_map/ppermute | solution.py:225
  8.9 1.4 %collective-permute-start.1 = (f32[128,768]{1,0:T(8,128)S(1)}, f32[128,768]{1,0:T(8,128)S(1)}, u32[]{:S(2)}, u32[]{:S(2)}) collective-permute-start(f32[128,768]{1,0:T(8,128)S(1)} %get-tuple-element.54), channel_id=1, source_target_pairs={{0,6},{1,7},{2,4},{3,5},{4,2},{5,3},{6,0},{7,1},{8,14},{9,15},{10,... | collective-permute-start | bytes 1179656 | tf_op jit(solution)/shard_map/ppermute | solution.py:225
  10.3 0.5 collective-permute-start.3
  10.9 22.0 %collective-permute-done.7.refs_6_.refs_2_ = f32[768,384]{1,0:T(8,128)S(1)} collective-permute-done((f32[768,384]{1,0:T(8,128)S(1)}, f32[768,384]{1,0:T(8,128)S(1)}, u32[]{:S(2)}, u32[]{:S(2)}) %collective-permute-start.7) | collective-permute-done | bytes 1179680 | tf_op jit(solution)/shard_map/ppermute | solution.py:200
  32.8 1.0 copy-done
  33.9 5.7 %collective-permute-start.11 = (f32[768,384]{1,0:T(8,128)S(1)}, f32[768,384]{1,0:T(8,128)}, u32[]{:S(2)}, u32[]{:S(2)}) collective-permute-start(f32[768,384]{1,0:T(8,128)S(1)} %join.1.refs_6_.refs_2_), channel_id=1, source_target_pairs={{0,24},{24,0},{1,25},{25,1},{2,26},{26,2},{3,27},{27,3},{4,28},{28... | collective-permute-start | bytes 3538952 | tf_op jit(solution)/shard_map/ppermute | solution.py:206
  39.6 0.1 collective-permute-start.9
  39.7 0.5 collective-permute-start.8
  40.2 0.1 collective-permute-start.4
  40.2 0.4 collective-permute-start.2
  40.7 0.8 collective-permute-done.9.refs_3_.refs_2_
  41.5 1.1 collective-permute-done.8.refs_1_.refs_3_
  42.6 3.1 %products.8 = (f32[256,384]{1,0:T(8,128)S(1)}, f32[256,384]{1,0:T(8,128)S(1)}, f32[256,384]{1,0:T(8,128)S(1)}) custom-call(f32[128,768]{1,0:T(8,128)S(1)} %collective-permute-done.1.refs_0_.refs_1_, f32[128,768]{1,0:T(8,128)} %collective-permute-done.8.refs_1_.refs_3_, f32[128,768]{1,0:T(8,128)S(1)} %collective-permute-done.refs_2_.refs_1_, ...), custom_call_target="tpu_custom_call" | custom-call | flops 1 | bytes 1 | tf_op jit(solution)/shard_map/products/pallas_call | solution.py:30
  45.7 2.5 %collective-permute-start.12 = (f32[256,384]{1,0:T(8,128)S(1)}, f32[256,384]{1,0:T(8,128)S(1)}, u32[]{:S(2)}, u32[]{:S(2)}) collective-permute-start(f32[256,384]{1,0:T(8,128)S(1)} %get-tuple-element.59), channel_id=1, source_target_pairs={{0,6},{1,7},{2,4},{3,5},{4,2},{5,3},{6,0},{7,1},{8,14},{9,15},{10,... | collective-permute-start | bytes 1179656 | tf_op jit(solution)/shard_map/ppermute | solution.py:225
  48.3 0.5 collective-permute-start.13
  48.8 0.5 collective-permute-start.14
  49.3 0.8 products.9.refs_0_
  50.1 3.1 %products.10 = (f32[256,384]{1,0:T(8,128)S(1)}, f32[256,384]{1,0:T(8,128)S(1)}, f32[256,384]{1,0:T(8,128)S(1)}) custom-call(f32[128,768]{1,0:T(8,128)S(1)} %collective-permute-done.1.refs_0_.refs_1_, f32[128,768]{1,0:T(8,128)} %collective-permute-done.8.refs_1_.refs_3_, f32[128,768]{1,0:T(8,128)S(1)} %collective-permute-done.refs_2_.refs_1_, ...), custom_call_target="tpu_custom_call" | custom-call | flops 1 | bytes 1 | tf_op jit(solution)/shard_map/products/pallas_call | solution.py:30
  53.2 0.8 products.11.refs_0_
  54.0 0.5 copy-done.3
  54.5 0.1 broadcast_select_fusion.1
  54.6 1.1 collective-permute-start.10
  55.7 3.0 %collective-permute-done.12.refs_1_ = f32[256,384]{1,0:T(8,128)S(1)} collective-permute-done((f32[256,384]{1,0:T(8,128)S(1)}, f32[256,384]{1,0:T(8,128)S(1)}, u32[]{:S(2)}, u32[]{:S(2)}) %collective-permute-start.12) | collective-permute-done | bytes 393248 | tf_op jit(solution)/shard_map/ppermute | solution.py:225
  58.7 7.6 %collective-permute-done.13.refs_2_ = f32[256,384]{1,0:T(8,128)S(1)} collective-permute-done((f32[256,384]{1,0:T(8,128)S(1)}, f32[256,384]{1,0:T(8,128)S(1)}, u32[]{:S(2)}, u32[]{:S(2)}) %collective-permute-start.13) | collective-permute-done | bytes 393248 | tf_op jit(solution)/shard_map/ppermute | solution.py:225
  66.3 0.1 collective-permute-done.14.refs_3_
  66.4 0.1 collective-permute-start.15
  66.5 1.4 %collective-permute-done.15.refs_4_ = f32[128,384]{1,0:T(8,128)S(1)} collective-permute-done((f32[128,384]{1,0:T(8,128)S(1)}, f32[128,384]{1,0:T(8,128)S(1)}, u32[]{:S(2)}, u32[]{:S(2)}) %collective-permute-start.15) | collective-permute-done | bytes 196640 | tf_op jit(solution)/shard_map/ppermute | solution.py:225
  67.9 0.8 write.4.refs_5_
  68.8 1.4 %broadcast_select_fusion.refs_4_ = f32[768,384]{1,0:T(8,128)S(1)} fusion(f32[768,384]{1,0:T(8,128)S(1)} %copy-done.3, f32[768,384]{1,0:T(8,128)} %collective-permute-done.11, pred[]{:T(512)S(6)} %or.3), kind=kLoop, calls=%fused_computation | loop fusion | flops 294912 | bytes 3538945 | tf_op jit(solution)/shard_map/jit(_where)/select_n | solution.py:260
  70.2 2.5 %products.12 = (f32[256,384]{1,0:T(8,128)S(1)}, f32[256,384]{1,0:T(8,128)S(1)}) custom-call(f32[128,768]{1,0:T(8,128)S(1)} %collective-permute-done.3.refs_4_.refs_0_, f32[128,768]{1,0:T(8,128)S(1)} %collective-permute-done.1.refs_0_.refs_1_, f32[128,768]{1,0:T(8,128)} %collective-permute-done.9.refs_3_.refs_2_, ...), custom_call_target="tpu_custom_call" | custom-call | flops 1 | bytes 1 | tf_op jit(solution)/shard_map/products/pallas_call | solution.py:30
  72.7 1.6 %collective-permute-start.16 = (f32[256,384]{1,0:T(8,128)S(1)}, f32[256,384]{1,0:T(8,128)S(1)}, u32[]{:S(2)}, u32[]{:S(2)}) collective-permute-start(f32[256,384]{1,0:T(8,128)S(1)} %get-tuple-element.73), channel_id=1, source_target_pairs={{0,2},{1,3},{2,0},{3,1},{4,6},{5,7},{6,4},{7,5},{8,10},{9,11},{10,... | collective-permute-start | bytes 1179656 | tf_op jit(solution)/shard_map/ppermute | solution.py:225
  74.3 0.7 collective-permute-start.18
  75.0 1.4 %products.13 = (f32[256,384]{1,0:T(8,128)S(1)}, f32[256,384]{1,0:T(8,128)S(1)}) custom-call(f32[128,768]{1,0:T(8,128)S(1)} %get-tuple-element.55.refs_0_, f32[128,768]{1,0:T(8,128)S(1)} %collective-permute-done.refs_2_.refs_1_, f32[128,768]{1,0:T(8,128)S(1)} %collective-permute-done.2.refs_1_.refs_2_, f32[128,768]{1,0:T(8,128)S(1)} %collective-permute-done.4.refs_5_.refs_3_, ...), custom_call_target="tpu_custom_call" | custom-call | flops 1 | bytes 1 | tf_op jit(solution)/shard_map/products/pallas_call | solution.py:30
  76.4 7.5 %collective-permute-done.16.got_ref = f32[256,384]{1,0:T(8,128)S(1)} collective-permute-done((f32[256,384]{1,0:T(8,128)S(1)}, f32[256,384]{1,0:T(8,128)S(1)}, u32[]{:S(2)}, u32[]{:S(2)}) %collective-permute-start.16) | collective-permute-done | bytes 393248 | tf_op jit(solution)/shard_map/ppermute | solution.py:225
  84.0 1.5 %collective-permute-start.17 = (f32[128,384]{1,0:T(8,128)S(1)}, f32[128,384]{1,0:T(8,128)S(1)}, u32[]{:S(2)}, u32[]{:S(2)}) collective-permute-start(f32[128,384]{1,0:T(8,128)S(1)} %get-tuple-element.78), channel_id=1, source_target_pairs={{0,4},{1,5},{2,6},{3,7},{4,0},{5,1},{6,2},{7,3},{8,12},{9,13},{10,... | collective-permute-start | bytes 589832 | tf_op jit(solution)/shard_map/ppermute | solution.py:225
  85.5 0.1 collective-permute-start.19
  85.6 0.9 collective-permute-start.20
  86.5 1.3 %collective-permute-start.26 = (f32[256,384]{1,0:T(8,128)S(1)}, f32[256,384]{1,0:T(8,128)S(1)}, u32[]{:S(2)}, u32[]{:S(2)}) collective-permute-start(f32[256,384]{1,0:T(8,128)S(1)} %get-tuple-element.64), channel_id=1, source_target_pairs={{0,6},{1,7},{2,4},{3,5},{4,2},{5,3},{6,0},{7,1},{8,14},{9,15},{10,... | collective-permute-start | bytes 1179656 | tf_op jit(solution)/shard_map/ppermute | solution.py:225
  87.8 2.6 %collective-permute-done.10.refs_4_ = f32[768,384]{1,0:T(8,128)S(1)} collective-permute-done((f32[768,384]{1,0:T(8,128)S(1)}, f32[768,384]{1,0:T(8,128)S(1)}, u32[]{:S(2)}, u32[]{:S(2)}) %collective-permute-start.10) | collective-permute-done | bytes 1179680 | tf_op jit(solution)/shard_map/ppermute | solution.py:212
  90.3 1.4 %collective-permute-start.27 = (f32[256,384]{1,0:T(8,128)S(1)}, f32[256,384]{1,0:T(8,128)S(1)}, u32[]{:S(2)}, u32[]{:S(2)}) collective-permute-start(f32[256,384]{1,0:T(8,128)S(1)} %get-tuple-element.65), channel_id=1, source_target_pairs={{0,4},{1,5},{2,6},{3,7},{4,0},{5,1},{6,2},{7,3},{8,12},{9,13},{10,... | collective-permute-start | bytes 1179656 | tf_op jit(solution)/shard_map/ppermute | solution.py:225
  91.8 1.5 %collective-permute-start.28 = (f32[256,384]{1,0:T(8,128)S(1)}, f32[256,384]{1,0:T(8,128)S(1)}, u32[]{:S(2)}, u32[]{:S(2)}) collective-permute-start(f32[256,384]{1,0:T(8,128)S(1)} %get-tuple-element.66), channel_id=1, source_target_pairs={{0,2},{1,3},{2,0},{3,1},{4,6},{5,7},{6,4},{7,5},{8,10},{9,11},{10,... | collective-permute-start | bytes 1179656 | tf_op jit(solution)/shard_map/ppermute | solution.py:225
  93.3 2.5 %products.14 = (f32[256,384]{1,0:T(8,128)S(1)}, f32[256,384]{1,0:T(8,128)S(1)}) custom-call(f32[128,768]{1,0:T(8,128)S(1)} %collective-permute-done.3.refs_4_.refs_0_, f32[128,768]{1,0:T(8,128)S(1)} %collective-permute-done.1.refs_0_.refs_1_, f32[128,768]{1,0:T(8,128)} %collective-permute-done.9.refs_3_.refs_2_, ...), custom_call_target="tpu_custom_call" | custom-call | flops 1 | bytes 1 | tf_op jit(solution)/shard_map/products/pallas_call | solution.py:30
  95.8 0.6 collective-permute-start.21
  96.4 0.6 collective-permute-start.23
  97.0 4.9 %collective-permute-done.26.refs_1_ = f32[256,384]{1,0:T(8,128)S(1)} collective-permute-done((f32[256,384]{1,0:T(8,128)S(1)}, f32[256,384]{1,0:T(8,128)S(1)}, u32[]{:S(2)}, u32[]{:S(2)}) %collective-permute-start.26) | collective-permute-done | bytes 393248 | tf_op jit(solution)/shard_map/ppermute | solution.py:225
  101.9 7.9 %collective-permute-done.27.refs_2_ = f32[256,384]{1,0:T(8,128)S(1)} collective-permute-done((f32[256,384]{1,0:T(8,128)S(1)}, f32[256,384]{1,0:T(8,128)S(1)}, u32[]{:S(2)}, u32[]{:S(2)}) %collective-permute-start.27) | collective-permute-done | bytes 393248 | tf_op jit(solution)/shard_map/ppermute | solution.py:225
  109.8 0.5 collective-permute-done.28.refs_3_
  110.5 1.4 %products.15 = (f32[256,384]{1,0:T(8,128)S(1)}, f32[256,384]{1,0:T(8,128)S(1)}) custom-call(f32[128,768]{1,0:T(8,128)S(1)} %get-tuple-element.55.refs_0_, f32[128,768]{1,0:T(8,128)S(1)} %collective-permute-done.refs_2_.refs_1_, f32[128,768]{1,0:T(8,128)S(1)} %collective-permute-done.2.refs_1_.refs_2_, f32[128,768]{1,0:T(8,128)S(1)} %collective-permute-done.4.refs_5_.refs_3_, ...), custom_call_target="tpu_custom_call" | custom-call | flops 1 | bytes 1 | tf_op jit(solution)/shard_map/products/pallas_call | solution.py:30
  111.9 6.3 %collective-permute-done.21.got_ref = f32[256,384]{1,0:T(8,128)S(1)} collective-permute-done((f32[256,384]{1,0:T(8,128)S(1)}, f32[256,384]{1,0:T(8,128)S(1)}, u32[]{:S(2)}, u32[]{:S(2)}) %collective-permute-start.21) | collective-permute-done | bytes 393248 | tf_op jit(solution)/shard_map/ppermute | solution.py:225
  118.2 0.7 collective-permute-start.22
  118.9 0.1 collective-permute-start.24
  119.0 1.6 %collective-permute-start.25 = (f32[128,384]{1,0:T(8,128)S(1)}, f32[128,384]{1,0:T(8,128)S(1)}, u32[]{:S(2)}, u32[]{:S(2)}) collective-permute-start(f32[128,384]{1,0:T(8,128)S(1)} %get-tuple-element.91), channel_id=1, source_target_pairs={{0,3},{1,2},{2,1},{3,0},{4,7},{5,6},{6,5},{7,4},{8,11},{9,10},{10,... | collective-permute-start | bytes 589832 | tf_op jit(solution)/shard_map/ppermute | solution.py:225
  120.6 0.8 write.5.refs_4_
  121.5 0.8 write.6.refs_4_
  122.3 2.4 %collective-permute-done.22.refs_1_ = f32[128,384]{1,0:T(8,128)S(1)} collective-permute-done((f32[128,384]{1,0:T(8,128)S(1)}, f32[128,384]{1,0:T(8,128)S(1)}, u32[]{:S(2)}, u32[]{:S(2)}) %collective-permute-start.22) | collective-permute-done | bytes 196640 | tf_op jit(solution)/shard_map/ppermute | solution.py:225
  124.7 1.1 collective-permute-done.25.refs_3_
  125.7 0.8 write.7
  (27 shorter events, 0.4 us)
Async XLA Ops:
  1.3 2.1 %collective-permute-start.5 = (f32[384,384]{1,0:T(8,128)S(1)}, f32[384,384]{1,0:T(8,128)S(1)}, u32[]{:S(2)}, u32[]{:S(2)}) collective-permute-start(f32[384,384]{1,0:T(8,128)S(1)} %get-tuple-element.57), channel_id=1, source_target_pairs={{0,1},{1,0},{2,3},{3,2},{4,5},{5,4},{6,7},{7,6},{8,9},{9,8},{10,11... | collective-permute-start | bytes 1769480 | tf_op jit(solution)/shard_map/ppermute | solution.py:225
  3.6 29.3 %collective-permute-start.7 = (f32[768,384]{1,0:T(8,128)S(1)}, f32[768,384]{1,0:T(8,128)S(1)}, u32[]{:S(2)}, u32[]{:S(2)}) collective-permute-start(f32[768,384]{1,0:T(8,128)S(1)} %join.1.refs_6_.refs_2_), channel_id=1, source_target_pairs={{0,8},{8,0},{16,24},{24,16},{1,9},{9,1},{17,25},{25,17},{2,10},{10... | collective-permute-start | bytes 3538952 | tf_op jit(solution)/shard_map/ppermute | solution.py:200
  6.6 27.3 %collective-permute-start.6 = (f32[768,384]{1,0:T(8,128)S(1)}, f32[768,384]{1,0:T(8,128)S(1)}, u32[]{:S(2)}, u32[]{:S(2)}) collective-permute-start(f32[768,384]{1,0:T(8,128)S(1)} %join.1.refs_6_.refs_2_), channel_id=1, source_target_pairs={{8,16},{16,8},{9,17},{17,9},{10,18},{18,10},{11,19},{19,11},{12,20... | collective-permute-start | bytes 3538952 | tf_op jit(solution)/shard_map/ppermute | solution.py:204
  7.3 32.3 %collective-permute-start = (f32[128,768]{1,0:T(8,128)S(1)}, f32[128,768]{1,0:T(8,128)S(1)}, u32[]{:S(2)}, u32[]{:S(2)}) collective-permute-start(f32[128,768]{1,0:T(8,128)S(1)} %get-tuple-element.53), channel_id=1, source_target_pairs={{0,4},{1,5},{2,6},{3,7},{4,0},{5,1},{6,2},{7,3},{8,12},{9,13},{10,... | collective-permute-start | bytes 1179656 | tf_op jit(solution)/shard_map/ppermute | solution.py:225
  8.9 30.8 %collective-permute-start.1 = (f32[128,768]{1,0:T(8,128)S(1)}, f32[128,768]{1,0:T(8,128)S(1)}, u32[]{:S(2)}, u32[]{:S(2)}) collective-permute-start(f32[128,768]{1,0:T(8,128)S(1)} %get-tuple-element.54), channel_id=1, source_target_pairs={{0,6},{1,7},{2,4},{3,5},{4,2},{5,3},{6,0},{7,1},{8,14},{9,15},{10,... | collective-permute-start | bytes 1179656 | tf_op jit(solution)/shard_map/ppermute | solution.py:225
  10.3 29.8 %collective-permute-start.3 = (f32[128,768]{1,0:T(8,128)S(1)}, f32[128,768]{1,0:T(8,128)S(1)}, u32[]{:S(2)}, u32[]{:S(2)}) collective-permute-start(f32[128,768]{1,0:T(8,128)S(1)} %get-tuple-element.56), channel_id=1, source_target_pairs={{0,2},{1,3},{2,0},{3,1},{4,6},{5,7},{6,4},{7,5},{8,10},{9,11},{10,... | collective-permute-start | bytes 1179656 | tf_op jit(solution)/shard_map/ppermute | solution.py:225
  32.8 1.0 copy-start
  33.9 6.3 %copy-start.2 = (f32[768,384]{1,0:T(8,128)}, f32[768,384]{1,0:T(8,128)S(1)}, u32[]{:S(2)}) copy-start(f32[768,384]{1,0:T(8,128)S(1)} %collective-permute-done.6) | copy-start | bytes 3538948
  33.9 34.9 %collective-permute-start.11 = (f32[768,384]{1,0:T(8,128)S(1)}, f32[768,384]{1,0:T(8,128)}, u32[]{:S(2)}, u32[]{:S(2)}) collective-permute-start(f32[768,384]{1,0:T(8,128)S(1)} %join.1.refs_6_.refs_2_), channel_id=1, source_target_pairs={{0,24},{24,0},{1,25},{25,1},{2,26},{26,2},{3,27},{27,3},{4,28},{28... | collective-permute-start | bytes 3538952 | tf_op jit(solution)/shard_map/ppermute | solution.py:206
  39.6 1.9 %collective-permute-start.9 = (f32[128,768]{1,0:T(8,128)S(1)}, f32[128,768]{1,0:T(8,128)}, u32[]{:S(2)}, u32[]{:S(2)}) collective-permute-start(f32[128,768]{1,0:T(8,128)S(1)} %collective-permute-done.refs_2_.refs_1_), channel_id=1, source_target_pairs={{0,1},{1,0},{2,3},{3,2},{4,5},{5,4},{6,7},{7,6},{8,9},{9,8},{10,11... | collective-permute-start | bytes 1179656 | tf_op jit(solution)/shard_map/ppermute | solution.py:225
  39.7 3.0 %collective-permute-start.8 = (f32[128,768]{1,0:T(8,128)S(1)}, f32[128,768]{1,0:T(8,128)}, u32[]{:S(2)}, u32[]{:S(2)}) collective-permute-start(f32[128,768]{1,0:T(8,128)S(1)} %collective-permute-done.1.refs_0_.refs_1_), channel_id=1, source_target_pairs={{0,1},{1,0},{2,3},{3,2},{4,5},{5,4},{6,7},{7,6},{8,9},{9,8},{10,11... | collective-permute-start | bytes 1179656 | tf_op jit(solution)/shard_map/ppermute | solution.py:225
  40.2 2.5 %collective-permute-start.4 = (f32[128,768]{1,0:T(8,128)S(1)}, f32[128,768]{1,0:T(8,128)S(1)}, u32[]{:S(2)}, u32[]{:S(2)}) collective-permute-start(f32[128,768]{1,0:T(8,128)S(1)} %collective-permute-done.3.refs_4_.refs_0_), channel_id=1, source_target_pairs={{0,1},{1,0},{2,3},{3,2},{4,5},{5,4},{6,7},{7,6},{8,9},{9,8},{10,11... | collective-permute-start | bytes 1179656 | tf_op jit(solution)/shard_map/ppermute | solution.py:225
  40.2 9.1 %collective-permute-start.2 = (f32[128,768]{1,0:T(8,128)S(1)}, f32[128,768]{1,0:T(8,128)S(1)}, u32[]{:S(2)}, u32[]{:S(2)}) collective-permute-start(f32[128,768]{1,0:T(8,128)S(1)} %get-tuple-element.55.refs_0_), channel_id=1, source_target_pairs={{0,1},{1,0},{2,3},{3,2},{4,5},{5,4},{6,7},{7,6},{8,9},{9,8},{10,11... | collective-permute-start | bytes 1179656 | tf_op jit(solution)/shard_map/ppermute | solution.py:225
  45.7 13.0 %collective-permute-start.12 = (f32[256,384]{1,0:T(8,128)S(1)}, f32[256,384]{1,0:T(8,128)S(1)}, u32[]{:S(2)}, u32[]{:S(2)}) collective-permute-start(f32[256,384]{1,0:T(8,128)S(1)} %get-tuple-element.59), channel_id=1, source_target_pairs={{0,6},{1,7},{2,4},{3,5},{4,2},{5,3},{6,0},{7,1},{8,14},{9,15},{10,... | collective-permute-start | bytes 1179656 | tf_op jit(solution)/shard_map/ppermute | solution.py:225
  48.3 18.0 %collective-permute-start.13 = (f32[256,384]{1,0:T(8,128)S(1)}, f32[256,384]{1,0:T(8,128)S(1)}, u32[]{:S(2)}, u32[]{:S(2)}) collective-permute-start(f32[256,384]{1,0:T(8,128)S(1)} %get-tuple-element.60), channel_id=1, source_target_pairs={{0,4},{1,5},{2,6},{3,7},{4,0},{5,1},{6,2},{7,3},{8,12},{9,13},{10,... | collective-permute-start | bytes 1179656 | tf_op jit(solution)/shard_map/ppermute | solution.py:225
  48.8 1.3 %copy-start.1 = (f32[768,384]{1,0:T(8,128)S(1)}, f32[768,384]{1,0:T(8,128)}, u32[]{:S(2)}) copy-start(f32[768,384]{1,0:T(8,128)} %copy-done) | copy-start | bytes 3538948
  48.8 17.6 %collective-permute-start.14 = (f32[256,384]{1,0:T(8,128)S(1)}, f32[256,384]{1,0:T(8,128)S(1)}, u32[]{:S(2)}, u32[]{:S(2)}) collective-permute-start(f32[256,384]{1,0:T(8,128)S(1)} %get-tuple-element.61), channel_id=1, source_target_pairs={{0,2},{1,3},{2,0},{3,1},{4,6},{5,7},{6,4},{7,5},{8,10},{9,11},{10,... | collective-permute-start | bytes 1179656 | tf_op jit(solution)/shard_map/ppermute | solution.py:225
  53.2 1.3 %copy-start.3 = (f32[768,384]{1,0:T(8,128)S(1)}, f32[768,384]{1,0:T(8,128)}, u32[]{:S(2)}) copy-start(f32[768,384]{1,0:T(8,128)} %copy-done.2) | copy-start | bytes 3538948
  54.6 35.7 %collective-permute-start.10 = (f32[768,384]{1,0:T(8,128)S(1)}, f32[768,384]{1,0:T(8,128)S(1)}, u32[]{:S(2)}, u32[]{:S(2)}) collective-permute-start(f32[768,384]{1,0:T(8,128)S(1)} %broadcast_select_fusion.1), channel_id=1, source_target_pairs={{8,0},{16,24},{0,16},{24,8},{9,1},{17,25},{1,17},{25,9},{10,2},{18... | collective-permute-start | bytes 3538952 | tf_op jit(solution)/shard_map/ppermute | solution.py:212
  66.4 1.5 %collective-permute-start.15 = (f32[128,384]{1,0:T(8,128)S(1)}, f32[128,384]{1,0:T(8,128)S(1)}, u32[]{:S(2)}, u32[]{:S(2)}) collective-permute-start(f32[128,384]{1,0:T(8,128)S(1)} %total.2), channel_id=1, source_target_pairs={{0,1},{1,0},{2,3},{3,2},{4,5},{5,4},{6,7},{7,6},{8,9},{9,8},{10,11... | collective-permute-start | bytes 589832 | tf_op jit(solution)/shard_map/ppermute | solution.py:225
  72.7 11.2 %collective-permute-start.16 = (f32[256,384]{1,0:T(8,128)S(1)}, f32[256,384]{1,0:T(8,128)S(1)}, u32[]{:S(2)}, u32[]{:S(2)}) collective-permute-start(f32[256,384]{1,0:T(8,128)S(1)} %get-tuple-element.73), channel_id=1, source_target_pairs={{0,2},{1,3},{2,0},{3,1},{4,6},{5,7},{6,4},{7,5},{8,10},{9,11},{10,... | collective-permute-start | bytes 1179656 | tf_op jit(solution)/shard_map/ppermute | solution.py:225
  74.3 11.2 %collective-permute-start.18 = (f32[256,384]{1,0:T(8,128)S(1)}, f32[256,384]{1,0:T(8,128)S(1)}, u32[]{:S(2)}, u32[]{:S(2)}) collective-permute-start(f32[256,384]{1,0:T(8,128)S(1)} %get-tuple-element.74), channel_id=1, source_target_pairs={{0,4},{1,5},{2,6},{3,7},{4,0},{5,1},{6,2},{7,3},{8,12},{9,13},{10,... | collective-permute-start | bytes 1179656 | tf_op jit(solution)/shard_map/ppermute | solution.py:225
  84.0 7.8 %collective-permute-start.17 = (f32[128,384]{1,0:T(8,128)S(1)}, f32[128,384]{1,0:T(8,128)S(1)}, u32[]{:S(2)}, u32[]{:S(2)}) collective-permute-start(f32[128,384]{1,0:T(8,128)S(1)} %get-tuple-element.78), channel_id=1, source_target_pairs={{0,4},{1,5},{2,6},{3,7},{4,0},{5,1},{6,2},{7,3},{8,12},{9,13},{10,... | collective-permute-start | bytes 589832 | tf_op jit(solution)/shard_map/ppermute | solution.py:225
  85.5 7.8 %collective-permute-start.19 = (f32[128,384]{1,0:T(8,128)S(1)}, f32[128,384]{1,0:T(8,128)S(1)}, u32[]{:S(2)}, u32[]{:S(2)}) collective-permute-start(f32[128,384]{1,0:T(8,128)S(1)} %get-tuple-element.80), channel_id=1, source_target_pairs={{0,1},{1,0},{2,3},{3,2},{4,5},{5,4},{6,7},{7,6},{8,9},{9,8},{10,11... | collective-permute-start | bytes 589832 | tf_op jit(solution)/shard_map/ppermute | solution.py:225
  85.6 7.7 %collective-permute-start.20 = (f32[128,384]{1,0:T(8,128)S(1)}, f32[128,384]{1,0:T(8,128)S(1)}, u32[]{:S(2)}, u32[]{:S(2)}) collective-permute-start(f32[128,384]{1,0:T(8,128)S(1)} %get-tuple-element.81), channel_id=1, source_target_pairs={{0,3},{1,2},{2,1},{3,0},{4,7},{5,6},{6,5},{7,4},{8,11},{9,10},{10,... | collective-permute-start | bytes 589832 | tf_op jit(solution)/shard_map/ppermute | solution.py:225
  86.5 15.4 %collective-permute-start.26 = (f32[256,384]{1,0:T(8,128)S(1)}, f32[256,384]{1,0:T(8,128)S(1)}, u32[]{:S(2)}, u32[]{:S(2)}) collective-permute-start(f32[256,384]{1,0:T(8,128)S(1)} %get-tuple-element.64), channel_id=1, source_target_pairs={{0,6},{1,7},{2,4},{3,5},{4,2},{5,3},{6,0},{7,1},{8,14},{9,15},{10,... | collective-permute-start | bytes 1179656 | tf_op jit(solution)/shard_map/ppermute | solution.py:225
  90.3 19.5 %collective-permute-start.27 = (f32[256,384]{1,0:T(8,128)S(1)}, f32[256,384]{1,0:T(8,128)S(1)}, u32[]{:S(2)}, u32[]{:S(2)}) collective-permute-start(f32[256,384]{1,0:T(8,128)S(1)} %get-tuple-element.65), channel_id=1, source_target_pairs={{0,4},{1,5},{2,6},{3,7},{4,0},{5,1},{6,2},{7,3},{8,12},{9,13},{10,... | collective-permute-start | bytes 1179656 | tf_op jit(solution)/shard_map/ppermute | solution.py:225
  91.8 18.5 %collective-permute-start.28 = (f32[256,384]{1,0:T(8,128)S(1)}, f32[256,384]{1,0:T(8,128)S(1)}, u32[]{:S(2)}, u32[]{:S(2)}) collective-permute-start(f32[256,384]{1,0:T(8,128)S(1)} %get-tuple-element.66), channel_id=1, source_target_pairs={{0,2},{1,3},{2,0},{3,1},{4,6},{5,7},{6,4},{7,5},{8,10},{9,11},{10,... | collective-permute-start | bytes 1179656 | tf_op jit(solution)/shard_map/ppermute | solution.py:225
  95.8 22.4 %collective-permute-start.21 = (f32[256,384]{1,0:T(8,128)S(1)}, f32[256,384]{1,0:T(8,128)S(1)}, u32[]{:S(2)}, u32[]{:S(2)}) collective-permute-start(f32[256,384]{1,0:T(8,128)S(1)} %get-tuple-element.83), channel_id=1, source_target_pairs={{0,2},{1,3},{2,0},{3,1},{4,6},{5,7},{6,4},{7,5},{8,10},{9,11},{10,... | collective-permute-start | bytes 1179656 | tf_op jit(solution)/shard_map/ppermute | solution.py:225
  96.4 22.5 %collective-permute-start.23 = (f32[256,384]{1,0:T(8,128)S(1)}, f32[256,384]{1,0:T(8,128)S(1)}, u32[]{:S(2)}, u32[]{:S(2)}) collective-permute-start(f32[256,384]{1,0:T(8,128)S(1)} %get-tuple-element.84), channel_id=1, source_target_pairs={{0,4},{1,5},{2,6},{3,7},{4,0},{5,1},{6,2},{7,3},{8,12},{9,13},{10,... | collective-permute-start | bytes 1179656 | tf_op jit(solution)/shard_map/ppermute | solution.py:225
  110.4 10.3 %collective-permute-start.29 = (f32[128,384]{1,0:T(8,128)S(1)}, f32[128,384]{1,0:T(8,128)S(1)}, u32[]{:S(2)}, u32[]{:S(2)}) collective-permute-start(f32[128,384]{1,0:T(8,128)S(1)} %total.3), channel_id=1, source_target_pairs={{0,1},{1,0},{2,3},{3,2},{4,5},{5,4},{6,7},{7,6},{8,9},{9,8},{10,11... | collective-permute-start | bytes 589832 | tf_op jit(solution)/shard_map/ppermute | solution.py:225
  118.2 6.4 %collective-permute-start.22 = (f32[128,384]{1,0:T(8,128)S(1)}, f32[128,384]{1,0:T(8,128)S(1)}, u32[]{:S(2)}, u32[]{:S(2)}) collective-permute-start(f32[128,384]{1,0:T(8,128)S(1)} %get-tuple-element.88), channel_id=1, source_target_pairs={{0,4},{1,5},{2,6},{3,7},{4,0},{5,1},{6,2},{7,3},{8,12},{9,13},{10,... | collective-permute-start | bytes 589832 | tf_op jit(solution)/shard_map/ppermute | solution.py:225
  118.9 5.7 %collective-permute-start.24 = (f32[128,384]{1,0:T(8,128)S(1)}, f32[128,384]{1,0:T(8,128)S(1)}, u32[]{:S(2)}, u32[]{:S(2)}) collective-permute-start(f32[128,384]{1,0:T(8,128)S(1)} %get-tuple-element.90), channel_id=1, source_target_pairs={{0,1},{1,0},{2,3},{3,2},{4,5},{5,4},{6,7},{7,6},{8,9},{9,8},{10,11... | collective-permute-start | bytes 589832 | tf_op jit(solution)/shard_map/ppermute | solution.py:225
  119.0 6.7 %collective-permute-start.25 = (f32[128,384]{1,0:T(8,128)S(1)}, f32[128,384]{1,0:T(8,128)S(1)}, u32[]{:S(2)}, u32[]{:S(2)}) collective-permute-start(f32[128,384]{1,0:T(8,128)S(1)} %get-tuple-element.91), channel_id=1, source_target_pairs={{0,3},{1,2},{2,1},{3,0},{4,7},{5,6},{6,5},{7,4},{8,11},{9,10},{10,... | collective-permute-start | bytes 589832 | tf_op jit(solution)/shard_map/ppermute | solution.py:225

commit v16 on v12

--- a/solution.py
+++ b/solution.py
@@ -200,11 +200,8 @@
     here = lax.axis_index("occ")
     middle = (here == 1) | (here == 2)
 
-    def last(*earlier):
-        moving = jnp.where(middle, after(centre, *earlier), own)
-        return [(2, lax.ppermute(moving, "occ", [(1, 0), (2, 3), (0, 2), (3, 1)]))]
-
-    return [[(0, own), (1, near)], [(3, (middle, centre, far))], last]
+    last = lax.ppermute(jnp.where(middle, centre, own), "occ", [(1, 0), (2, 3), (0, 2), (3, 1)])
+    return [[(0, own)], [(1, near)], [(3, (middle, centre, far))], [(2, last)]]
 
 
 def per_device(sizes, amplitudes, amp_mask, integrals, int_mask):
@@ -237,7 +234,7 @@
     near = [[r for r in range(groups) if not r & o[0]] for o in orders]
 
     out = None
-    token = []
+    token = settled = []
     for n in range(len(stages)):
         ds, right = [d for d, _ in stages[n]], [block for _, block in stages[n]]
         if isinstance(right[0], tuple):
@@ -247,9 +244,7 @@
         right = list(lax.optimization_barrier((*right, *token))[: len(right)])
         sent = products([[rel[h][r] for r in away[h]] for h in range(2)], right)
         moving = [swap(sent[h], 2 * orders[h][0]) for h in range(2)]
-        if callable(stages[-1]):
-            stages[-1] = stages[-1](*moving)
-        right[0] = after(right[0], *sent)
+        right[0] = after(right[0], *sent, *settled)
         held = list(products([[rel[h][r] for r in near[h]] for h in range(2)], right))
         names = [near[0], near[1]]
         for level in range(1, len(bits)):
@@ -261,7 +256,8 @@
                 moving[h] = swap(moved, 2 * bit + (h if level == len(bits) - 1 else 0))
                 names[h] = [names[h][i] for i in stays]
         pieces = [held[0], moving[0], swap(held[1], 1), moving[1]]
-        token = [*pieces[1:]] if out is None else [*pieces[1:], out]
+        token = [*held] if out is None else [*held, out]
+        settled = moving if n + 2 < len(stages) else []
         out = write(out, (rows, n_occ * width), ds, half, pieces)
     return out
 

time: 122 us -> 127 us (1.041)
  waiting for transfers between devices: 67.5 us -> 69.8 us
  starting transfers between devices: 31.5 us -> 33 us
    ppermute x23 -> x28, waiting for transfers between devices: 57.1 us -> 64.2 us  [swap(): return lax.ppermute(x, 'vir', [(i, i ^ bits) for i in range(n_vir)])]
    ppermute x1, waiting for transfers between devices: 4.75 us -> 0.01 us  [line_stages(): far = lax.ppermute(after(own, centre, near), 'occ', [(0, 3), (3, 0)])]
    ppermute x23 -> x28, starting transfers between devices: 18.2 us -> 22.6 us  [swap(): return lax.ppermute(x, 'vir', [(i, i ^ bits) for i in range(n_vir)])]
    ppermute x1, starting transfers between devices: 4.09 us -> 0.98 us  [line_stages(): lax.ppermute(jnp.where(middle, centre, own), 'occ', [(1, 0), (2, 3), (0,...]
    pallas_call x3 -> x4, Pallas kernels: 2.58 us -> 3.21 us  [write(): pl.pallas_call(functools.partial(write_kernel, ds, half), out_shape=jax.S...]
    pallas_call x15 -> x19, Pallas kernels: 17.4 us -> 17.2 us  [kernel_call(): pl.pallas_call(body, out_shape=[pltpu.VMEM(shape, jnp.float32) for shape...]
  transfers between devices with their start and end apart: 27 -> 32, of which waited for: 13 -> 12; matrix products, arithmetic and copies ran while one was open for 1% -> 1% of each run, Pallas kernels for 13% -> 13%
where the time goes in v16:
time: 127 us; the launch traced here: 126 us
  waiting for transfers between devices  69.8 us (55%)
  starting transfers between devices  33 us (26%)
  Pallas kernels  20.4 us (16%)
  other arithmetic  1.53 us (1%)
    ppermute x28, waiting for transfers between devices, swap(): return lax.ppermute(x, 'vir', [(i, i ^ bits) for i in range(n_vir)])  64.2 us
    ppermute x28, starting transfers between devices, swap(): return lax.ppermute(x, 'vir', [(i, i ^ bits) for i in range(n_vir)])  22.6 us
    pallas_call x19, Pallas kernels, kernel_call(): pl.pallas_call(body, out_shape=[pltpu.VMEM(shape, jnp.float32) for shape...  17.2 us
    ppermute x1, starting transfers between devices, line_stages(): far = lax.ppermute(after(own, centre, near), 'occ', [(0, 3), (3, 0)])  5.66 us
    ppermute x1, waiting for transfers between devices, direct(): return lax.ppermute(x, 'occ', [(i, i ^ d) for i in range(nodes)])  5.65 us
    pallas_call x4, Pallas kernels, write(): pl.pallas_call(functools.partial(write_kernel, ds, half), out_shape=jax.S...  3.21 us
    ppermute x1, starting transfers between devices, direct(): return lax.ppermute(x, 'occ', [(i, i ^ d) for i in range(nodes)])  3.01 us
  transfers between devices with their start and end apart: 32, of which 12 were waited for; matrix products, arithmetic and copies ran while one was open for 1% of the time, Pallas kernels for 13%

profile of v16, /device:TPU:0, one launch (start us, length us, event | category | flops | bytes accessed | tf_op | source)
XLA Modules:
  0.0 126.3 jit_solution(11710894884280005881)
XLA Ops:
  0.0 1.3 %halves.1 = (f32[384,384]{1,0:T(8,128)S(1)}, f32[384,384]{1,0:T(8,128)S(1)}) custom-call(s32[3,6]{1,0:T(4,128)} %mask_hbm.1, f32[384,768]{1,0:T(8,128)} %int_hbm.1), custom_call_target="tpu_custom_call" | custom-call | flops 1 | bytes 1 | tf_op jit(solution)/shard_map/halves/pallas_call | solution.py:30
  1.3 0.5 collective-permute-start.5
  1.8 1.4 %cut.1 = (f32[128,768]{1,0:T(8,128)S(1)}, f32[128,768]{1,0:T(8,128)S(1)}, f32[128,768]{1,0:T(8,128)S(1)}, f32[128,768]{1,0:T(8,128)S(1)}) custom-call(s32[4,24]{1,0:T(4,128)} %mask_hbm.2, f32[128,3072]{1,0:T(8,128)} %amp_hbm.1), custom_call_target="tpu_custom_call" | custom-call | flops 1 | bytes 1 | tf_op jit(solution)/shard_map/cut/pallas_call | solution.py:30
  3.3 0.2 collective-permute-done.5.other_ref
  3.5 0.1 join.1.refs_4_
  3.6 3.0 %collective-permute-start.8 = (f32[768,384]{1,0:T(8,128)S(1)}, f32[768,384]{1,0:T(8,128)S(1)}, u32[]{:S(2)}, u32[]{:S(2)}) collective-permute-start(f32[768,384]{1,0:T(8,128)S(1)} %join.1.refs_4_), channel_id=1, source_target_pairs={{0,8},{8,0},{16,24},{24,16},{1,9},{9,1},{17,25},{25,17},{2,10},{10... | collective-permute-start | bytes 3538952 | tf_op jit(solution)/shard_map/ppermute | solution.py:193
  6.6 0.7 collective-permute-start.6
  7.3 1.6 %collective-permute-start = (f32[128,768]{1,0:T(8,128)S(1)}, f32[128,768]{1,0:T(8,128)S(1)}, u32[]{:S(2)}, u32[]{:S(2)}) collective-permute-start(f32[128,768]{1,0:T(8,128)S(1)} %get-tuple-element.59), channel_id=1, source_target_pairs={{0,4},{1,5},{2,6},{3,7},{4,0},{5,1},{6,2},{7,3},{8,12},{9,13},{10,... | collective-permute-start | bytes 1179656 | tf_op jit(solution)/shard_map/ppermute | solution.py:215
  8.9 1.4 %collective-permute-start.1 = (f32[128,768]{1,0:T(8,128)S(1)}, f32[128,768]{1,0:T(8,128)S(1)}, u32[]{:S(2)}, u32[]{:S(2)}) collective-permute-start(f32[128,768]{1,0:T(8,128)S(1)} %get-tuple-element.60), channel_id=1, source_target_pairs={{0,6},{1,7},{2,4},{3,5},{4,2},{5,3},{6,0},{7,1},{8,14},{9,15},{10,... | collective-permute-start | bytes 1179656 | tf_op jit(solution)/shard_map/ppermute | solution.py:215
  10.3 0.5 collective-permute-start.3
  10.9 15.8 %collective-permute-done.refs_1_ = f32[128,768]{1,0:T(8,128)S(1)} collective-permute-done((f32[128,768]{1,0:T(8,128)S(1)}, f32[128,768]{1,0:T(8,128)S(1)}, u32[]{:S(2)}, u32[]{:S(2)}) %collective-permute-start) | collective-permute-done | bytes 393248 | tf_op jit(solution)/shard_map/ppermute | solution.py:215
  26.7 0.5 collective-permute-start.11
  27.2 5.7 %collective-permute-done.8.refs_4_ = f32[768,384]{1,0:T(8,128)S(1)} collective-permute-done((f32[768,384]{1,0:T(8,128)S(1)}, f32[768,384]{1,0:T(8,128)S(1)}, u32[]{:S(2)}, u32[]{:S(2)}) %collective-permute-start.8) | collective-permute-done | bytes 1179680 | tf_op jit(solution)/shard_map/ppermute | solution.py:193
  32.8 1.0 copy-done.4
  33.9 5.7 %collective-permute-start.9 = (f32[768,384]{1,0:T(8,128)S(1)}, f32[768,384]{1,0:T(8,128)}, u32[]{:S(2)}, u32[]{:S(2)}) collective-permute-start(f32[768,384]{1,0:T(8,128)S(1)} %join.1.refs_4_), channel_id=1, source_target_pairs={{0,24},{24,0},{1,25},{25,1},{2,26},{26,2},{3,27},{27,3},{4,28},{28... | collective-permute-start | bytes 3538952 | tf_op jit(solution)/shard_map/ppermute | solution.py:199
  39.5 0.1 collective-permute-start.2
  39.6 0.0 collective-permute-done.3.refs_0_
  39.6 0.5 collective-permute-start.4
  40.1 2.2 %products.8 = (f32[256,384]{1,0:T(8,128)}, f32[256,384]{1,0:T(8,128)}) custom-call(f32[128,768]{1,0:T(8,128)S(1)} %collective-permute-done.3.refs_0_, f32[128,768]{1,0:T(8,128)S(1)} %collective-permute-done.1.refs_1_, f32[128,768]{1,0:T(8,128)S(1)} %collective-permute-done.10.refs_2_, f32[128,768]{1,0:T(8,128)S(1)} %collective-permute-done.11.refs_3_, ...), custom_call_target="tpu_custom_call" | custom-call | flops 1 | bytes 1 | tf_op jit(solution)/shard_map/products/pallas_call | solution.py:30
  42.3 1.6 %collective-permute-start.13 = (f32[256,384]{1,0:T(8,128)}, f32[256,384]{1,0:T(8,128)}, u32[]{:S(2)}, u32[]{:S(2)}) collective-permute-start(f32[256,384]{1,0:T(8,128)} %get-tuple-element.67), channel_id=1, source_target_pairs={{0,4},{1,5},{2,6},{3,7},{4,0},{5,1},{6,2},{7,3},{8,12},{9,13},{10,... | collective-permute-start | bytes 1179656 | tf_op jit(solution)/shard_map/ppermute | solution.py:215
  43.9 1.5 %collective-permute-start.12 = (f32[256,384]{1,0:T(8,128)}, f32[256,384]{1,0:T(8,128)}, u32[]{:S(2)}, u32[]{:S(2)}) collective-permute-start(f32[256,384]{1,0:T(8,128)} %get-tuple-element.66), channel_id=1, source_target_pairs={{0,2},{1,3},{2,0},{3,1},{4,6},{5,7},{6,4},{7,5},{8,10},{9,11},{10,... | collective-permute-start | bytes 1179656 | tf_op jit(solution)/shard_map/ppermute | solution.py:215
  45.4 1.4 %products.9 = (f32[256,384]{1,0:T(8,128)S(1)}, f32[256,384]{1,0:T(8,128)S(1)}) custom-call(f32[128,768]{1,0:T(8,128)S(1)} %get-tuple-element.61.refs_0_, f32[128,768]{1,0:T(8,128)S(1)} %collective-permute-done.refs_1_, f32[128,768]{1,0:T(8,128)S(1)} %collective-permute-done.2.refs_2_, f32[128,768]{1,0:T(8,128)S(1)} %collective-permute-done.4.refs_3_, ...), custom_call_target="tpu_custom_call" | custom-call | flops 1 | bytes 1 | tf_op jit(solution)/shard_map/products/pallas_call | solution.py:30
  46.8 7.0 %collective-permute-done.13.got_ref = f32[256,384]{1,0:T(8,128)} collective-permute-done((f32[256,384]{1,0:T(8,128)}, f32[256,384]{1,0:T(8,128)}, u32[]{:S(2)}, u32[]{:S(2)}) %collective-permute-start.13) | collective-permute-done | bytes 393248 | tf_op jit(solution)/shard_map/ppermute | solution.py:215
  53.8 1.0 fold.9
  54.9 0.4 collective-permute-start.15
  55.3 0.1 broadcast_select_fusion.1
  55.4 1.0 collective-permute-start.7
  56.4 1.1 collective-permute-start.18
  57.4 0.0 collective-permute-done.12.got_ref
  57.4 1.1 fold.8
  58.5 1.4 %products.10 = (f32[256,384]{1,0:T(8,128)S(1)}, f32[256,384]{1,0:T(8,128)S(1)}) custom-call(f32[128,768]{1,0:T(8,128)S(1)} %collective-permute-done.3.refs_0_, f32[128,768]{1,0:T(8,128)S(1)} %collective-permute-done.1.refs_1_, f32[128,768]{1,0:T(8,128)S(1)} %copy-done.1, f32[128,768]{1,0:T(8,128)S(1)} %copy-done.3, f32[768,384]{1,0:T(8,128)S(1)} %copy-done.5), custom_call_target="tpu_custom_call" | custom-call | flops 1 | bytes 1 | tf_op jit(solution)/shard_map/products/pallas_call | solution.py:30
  60.0 1.6 %collective-permute-start.17 = (f32[256,384]{1,0:T(8,128)S(1)}, f32[256,384]{1,0:T(8,128)S(1)}, u32[]{:S(2)}, u32[]{:S(2)}) collective-permute-start(f32[256,384]{1,0:T(8,128)S(1)} %get-tuple-element.75), channel_id=1, source_target_pairs={{0,4},{1,5},{2,6},{3,7},{4,0},{5,1},{6,2},{7,3},{8,12},{9,13},{10,... | collective-permute-start | bytes 1179656 | tf_op jit(solution)/shard_map/ppermute | solution.py:215
  61.6 0.5 collective-permute-done.15.other_b
  62.1 1.0 collective-permute-start.16
  63.0 0.0 collective-permute-done.18.other_a
  63.0 1.5 %collective-permute-start.14 = (f32[128,384]{1,0:T(8,128)S(1)}, f32[128,384]{1,0:T(8,128)S(1)}, u32[]{:S(2)}, u32[]{:S(2)}) collective-permute-start(f32[128,384]{1,0:T(8,128)S(1)} %get-tuple-element.78), channel_id=1, source_target_pairs={{0,4},{1,5},{2,6},{3,7},{4,0},{5,1},{6,2},{7,3},{8,12},{9,13},{10,... | collective-permute-start | bytes 589832 | tf_op jit(solution)/shard_map/ppermute | solution.py:215
  64.6 10.7 %collective-permute-done.14.mine_b = f32[128,384]{1,0:T(8,128)S(1)} collective-permute-done((f32[128,384]{1,0:T(8,128)S(1)}, f32[128,384]{1,0:T(8,128)S(1)}, u32[]{:S(2)}, u32[]{:S(2)}) %collective-permute-start.14) | collective-permute-done | bytes 196640 | tf_op jit(solution)/shard_map/ppermute | solution.py:215
  75.3 0.8 write.4.refs_0_
  76.1 1.4 %products.11 = (f32[256,384]{1,0:T(8,128)S(1)}, f32[256,384]{1,0:T(8,128)S(1)}) custom-call(f32[128,768]{1,0:T(8,128)S(1)} %get-tuple-element.61.refs_0_, f32[128,768]{1,0:T(8,128)S(1)} %collective-permute-done.refs_1_, f32[128,768]{1,0:T(8,128)S(1)} %collective-permute-done.2.refs_2_, f32[128,768]{1,0:T(8,128)S(1)} %collective-permute-done.4.refs_3_, ...), custom_call_target="tpu_custom_call" | custom-call | flops 1 | bytes 1 | tf_op jit(solution)/shard_map/products/pallas_call | solution.py:30
  77.6 0.1 collective-permute-start.20
  77.7 0.0 collective-permute-done.9
  77.7 1.4 %broadcast_select_fusion.refs_4_ = f32[768,384]{1,0:T(8,128)S(1)} fusion(f32[768,384]{1,0:T(8,128)S(1)} %copy-done.7, f32[768,384]{1,0:T(8,128)} %collective-permute-done.9, pred[]{:T(512)S(6)} %or.3), kind=kLoop, calls=%fused_computation | loop fusion | flops 294912 | bytes 3538945 | tf_op jit(solution)/shard_map/jit(_where)/select_n | solution.py:243
  79.1 1.4 %products.12 = (f32[256,384]{1,0:T(8,128)S(1)}, f32[256,384]{1,0:T(8,128)S(1)}) custom-call(f32[128,768]{1,0:T(8,128)S(1)} %collective-permute-done.3.refs_0_, f32[128,768]{1,0:T(8,128)S(1)} %collective-permute-done.1.refs_1_, f32[128,768]{1,0:T(8,128)S(1)} %copy-done.1, f32[128,768]{1,0:T(8,128)S(1)} %copy-done.3, f32[768,384]{1,0:T(8,128)S(1)} %broadcast_select_fusion.refs_4_), custom_call_target="tpu_custom_call" | custom-call | flops 1 | bytes 1 | tf_op jit(solution)/shard_map/products/pallas_call | solution.py:30
  80.5 0.8 collective-permute-start.21
  81.4 1.5 %collective-permute-start.22 = (f32[256,384]{1,0:T(8,128)S(1)}, f32[256,384]{1,0:T(8,128)S(1)}, u32[]{:S(2)}, u32[]{:S(2)}) collective-permute-start(f32[256,384]{1,0:T(8,128)S(1)} %get-tuple-element.87), channel_id=1, source_target_pairs={{0,4},{1,5},{2,6},{3,7},{4,0},{5,1},{6,2},{7,3},{8,12},{9,13},{10,... | collective-permute-start | bytes 1179656 | tf_op jit(solution)/shard_map/ppermute | solution.py:215
  82.9 0.5 collective-permute-start.19
  83.4 0.8 collective-permute-done.20.other_b
  84.2 13.3 %collective-permute-done.19.mine_b = f32[128,384]{1,0:T(8,128)S(1)} collective-permute-done((f32[128,384]{1,0:T(8,128)S(1)}, f32[128,384]{1,0:T(8,128)S(1)}, u32[]{:S(2)}, u32[]{:S(2)}) %collective-permute-start.19) | collective-permute-done | bytes 196640 | tf_op jit(solution)/shard_map/ppermute | solution.py:215
  97.4 1.4 %products.13 = (f32[256,384]{1,0:T(8,128)S(1)}, f32[256,384]{1,0:T(8,128)S(1)}) custom-call(f32[128,768]{1,0:T(8,128)S(1)} %get-tuple-element.61.refs_0_, f32[128,768]{1,0:T(8,128)S(1)} %collective-permute-done.refs_1_, f32[128,768]{1,0:T(8,128)S(1)} %collective-permute-done.2.refs_2_, f32[128,768]{1,0:T(8,128)S(1)} %collective-permute-done.4.refs_3_, ...), custom_call_target="tpu_custom_call" | custom-call | flops 1 | bytes 1 | tf_op jit(solution)/shard_map/products/pallas_call | solution.py:30
  98.9 0.8 write.5.refs_0_
  99.8 1.4 %products.14 = (f32[256,384]{1,0:T(8,128)S(1)}, f32[256,384]{1,0:T(8,128)S(1)}) custom-call(f32[128,768]{1,0:T(8,128)S(1)} %collective-permute-done.3.refs_0_, f32[128,768]{1,0:T(8,128)S(1)} %collective-permute-done.1.refs_1_, f32[128,768]{1,0:T(8,128)S(1)} %copy-done.1, f32[128,768]{1,0:T(8,128)S(1)} %copy-done.3, f32[768,384]{1,0:T(8,128)S(1)} %collective-permute-done.7.refs_4_), custom_call_target="tpu_custom_call" | custom-call | flops 1 | bytes 1 | tf_op jit(solution)/shard_map/products/pallas_call | solution.py:30
  101.3 1.0 collective-permute-start.24
  102.3 1.5 %collective-permute-start.26 = (f32[256,384]{1,0:T(8,128)S(1)}, f32[256,384]{1,0:T(8,128)S(1)}, u32[]{:S(2)}, u32[]{:S(2)}) collective-permute-start(f32[256,384]{1,0:T(8,128)S(1)} %get-tuple-element.97), channel_id=1, source_target_pairs={{0,4},{1,5},{2,6},{3,7},{4,0},{5,1},{6,2},{7,3},{8,12},{9,13},{10,... | collective-permute-start | bytes 1179656 | tf_op jit(solution)/shard_map/ppermute | solution.py:215
  103.8 0.5 collective-permute-start.29
  104.3 1.2 collective-permute-start.31
  105.5 1.4 %products.15 = (f32[256,384]{1,0:T(8,128)S(1)}, f32[256,384]{1,0:T(8,128)S(1)}) custom-call(f32[128,768]{1,0:T(8,128)S(1)} %get-tuple-element.61.refs_0_, f32[128,768]{1,0:T(8,128)S(1)} %collective-permute-done.refs_1_, f32[128,768]{1,0:T(8,128)S(1)} %collective-permute-done.2.refs_2_, f32[128,768]{1,0:T(8,128)S(1)} %collective-permute-done.4.refs_3_, ...), custom_call_target="tpu_custom_call" | custom-call | flops 1 | bytes 1 | tf_op jit(solution)/shard_map/products/pallas_call | solution.py:30
  106.9 6.4 %collective-permute-done.24.got_ref = f32[256,384]{1,0:T(8,128)S(1)} collective-permute-done((f32[256,384]{1,0:T(8,128)S(1)}, f32[256,384]{1,0:T(8,128)S(1)}, u32[]{:S(2)}, u32[]{:S(2)}) %collective-permute-start.24) | collective-permute-done | bytes 393248 | tf_op jit(solution)/shard_map/ppermute | solution.py:215
  113.3 1.6 %collective-permute-start.25 = (f32[128,384]{1,0:T(8,128)S(1)}, f32[128,384]{1,0:T(8,128)S(1)}, u32[]{:S(2)}, u32[]{:S(2)}) collective-permute-start(f32[128,384]{1,0:T(8,128)S(1)} %get-tuple-element.101), channel_id=1, source_target_pairs={{0,4},{1,5},{2,6},{3,7},{4,0},{5,1},{6,2},{7,3},{8,12},{9,13},{10,... | collective-permute-start | bytes 589832 | tf_op jit(solution)/shard_map/ppermute | solution.py:215
  115.0 0.1 collective-permute-start.27
  115.0 3.5 %collective-permute-done.29.mine_b = f32[128,384]{1,0:T(8,128)S(1)} collective-permute-done((f32[128,384]{1,0:T(8,128)S(1)}, f32[128,384]{1,0:T(8,128)S(1)}, u32[]{:S(2)}, u32[]{:S(2)}) %collective-permute-start.29) | collective-permute-done | bytes 196640 | tf_op jit(solution)/shard_map/ppermute | solution.py:215
  118.5 0.8 write.6.refs_0_
  119.3 1.8 %collective-permute-done.25.mine_b = f32[128,384]{1,0:T(8,128)S(1)} collective-permute-done((f32[128,384]{1,0:T(8,128)S(1)}, f32[128,384]{1,0:T(8,128)S(1)}, u32[]{:S(2)}, u32[]{:S(2)}) %collective-permute-start.25) | collective-permute-done | bytes 196640 | tf_op jit(solution)/shard_map/ppermute | solution.py:215
  121.2 4.2 %collective-permute-done.28.other_b = f32[128,384]{1,0:T(8,128)S(1)} collective-permute-done((f32[128,384]{1,0:T(8,128)S(1)}, f32[128,384]{1,0:T(8,128)S(1)}, u32[]{:S(2)}, u32[]{:S(2)}) %collective-permute-start.28) | collective-permute-done | bytes 196640 | tf_op jit(solution)/shard_map/ppermute | solution.py:215
  125.3 0.8 write.7
  (41 shorter events, 0.3 us)
Async XLA Ops:
  1.3 2.1 %collective-permute-start.5 = (f32[384,384]{1,0:T(8,128)S(1)}, f32[384,384]{1,0:T(8,128)S(1)}, u32[]{:S(2)}, u32[]{:S(2)}) collective-permute-start(f32[384,384]{1,0:T(8,128)S(1)} %get-tuple-element.63), channel_id=1, source_target_pairs={{0,1},{1,0},{2,3},{3,2},{4,5},{5,4},{6,7},{7,6},{8,9},{9,8},{10,11... | collective-permute-start | bytes 1769480 | tf_op jit(solution)/shard_map/ppermute | solution.py:215
  3.6 29.3 %collective-permute-start.8 = (f32[768,384]{1,0:T(8,128)S(1)}, f32[768,384]{1,0:T(8,128)S(1)}, u32[]{:S(2)}, u32[]{:S(2)}) collective-permute-start(f32[768,384]{1,0:T(8,128)S(1)} %join.1.refs_4_), channel_id=1, source_target_pairs={{0,8},{8,0},{16,24},{24,16},{1,9},{9,1},{17,25},{25,17},{2,10},{10... | collective-permute-start | bytes 3538952 | tf_op jit(solution)/shard_map/ppermute | solution.py:193
  6.6 27.3 %collective-permute-start.6 = (f32[768,384]{1,0:T(8,128)S(1)}, f32[768,384]{1,0:T(8,128)S(1)}, u32[]{:S(2)}, u32[]{:S(2)}) collective-permute-start(f32[768,384]{1,0:T(8,128)S(1)} %join.1.refs_4_), channel_id=1, source_target_pairs={{8,16},{16,8},{9,17},{17,9},{10,18},{18,10},{11,19},{19,11},{12,20... | collective-permute-start | bytes 3538952 | tf_op jit(solution)/shard_map/ppermute | solution.py:197
  7.3 19.4 %collective-permute-start = (f32[128,768]{1,0:T(8,128)S(1)}, f32[128,768]{1,0:T(8,128)S(1)}, u32[]{:S(2)}, u32[]{:S(2)}) collective-permute-start(f32[128,768]{1,0:T(8,128)S(1)} %get-tuple-element.59), channel_id=1, source_target_pairs={{0,4},{1,5},{2,6},{3,7},{4,0},{5,1},{6,2},{7,3},{8,12},{9,13},{10,... | collective-permute-start | bytes 1179656 | tf_op jit(solution)/shard_map/ppermute | solution.py:215
  8.9 17.8 %collective-permute-start.1 = (f32[128,768]{1,0:T(8,128)S(1)}, f32[128,768]{1,0:T(8,128)S(1)}, u32[]{:S(2)}, u32[]{:S(2)}) collective-permute-start(f32[128,768]{1,0:T(8,128)S(1)} %get-tuple-element.60), channel_id=1, source_target_pairs={{0,6},{1,7},{2,4},{3,5},{4,2},{5,3},{6,0},{7,1},{8,14},{9,15},{10,... | collective-permute-start | bytes 1179656 | tf_op jit(solution)/shard_map/ppermute | solution.py:215
  10.3 29.3 %collective-permute-start.3 = (f32[128,768]{1,0:T(8,128)S(1)}, f32[128,768]{1,0:T(8,128)S(1)}, u32[]{:S(2)}, u32[]{:S(2)}) collective-permute-start(f32[128,768]{1,0:T(8,128)S(1)} %get-tuple-element.62), channel_id=1, source_target_pairs={{0,2},{1,3},{2,0},{3,1},{4,6},{5,7},{6,4},{7,5},{8,10},{9,11},{10,... | collective-permute-start | bytes 1179656 | tf_op jit(solution)/shard_map/ppermute | solution.py:215
  26.7 13.5 %collective-permute-start.10 = (f32[128,768]{1,0:T(8,128)S(1)}, f32[128,768]{1,0:T(8,128)S(1)}, u32[]{:S(2)}, u32[]{:S(2)}) collective-permute-start(f32[128,768]{1,0:T(8,128)S(1)} %collective-permute-done.refs_1_), channel_id=1, source_target_pairs={{0,1},{1,0},{2,3},{3,2},{4,5},{5,4},{6,7},{7,6},{8,9},{9,8},{10,11... | collective-permute-start | bytes 1179656 | tf_op jit(solution)/shard_map/ppermute | solution.py:215
  26.7 13.5 %collective-permute-start.11 = (f32[128,768]{1,0:T(8,128)S(1)}, f32[128,768]{1,0:T(8,128)S(1)}, u32[]{:S(2)}, u32[]{:S(2)}) collective-permute-start(f32[128,768]{1,0:T(8,128)S(1)} %collective-permute-done.1.refs_1_), channel_id=1, source_target_pairs={{0,1},{1,0},{2,3},{3,2},{4,5},{5,4},{6,7},{7,6},{8,9},{9,8},{10,11... | collective-permute-start | bytes 1179656 | tf_op jit(solution)/shard_map/ppermute | solution.py:215
  32.8 1.0 copy-start.4
  33.9 8.4 %copy-start.6 = (f32[768,384]{1,0:T(8,128)}, f32[768,384]{1,0:T(8,128)S(1)}, u32[]{:S(2)}) copy-start(f32[768,384]{1,0:T(8,128)S(1)} %collective-permute-done.6) | copy-start | bytes 3538948
  33.9 43.8 %collective-permute-start.9 = (f32[768,384]{1,0:T(8,128)S(1)}, f32[768,384]{1,0:T(8,128)}, u32[]{:S(2)}, u32[]{:S(2)}) collective-permute-start(f32[768,384]{1,0:T(8,128)S(1)} %join.1.refs_4_), channel_id=1, source_target_pairs={{0,24},{24,0},{1,25},{25,1},{2,26},{26,2},{3,27},{27,3},{4,28},{28... | collective-permute-start | bytes 3538952 | tf_op jit(solution)/shard_map/ppermute | solution.py:199
  39.5 5.9 %collective-permute-start.2 = (f32[128,768]{1,0:T(8,128)S(1)}, f32[128,768]{1,0:T(8,128)S(1)}, u32[]{:S(2)}, u32[]{:S(2)}) collective-permute-start(f32[128,768]{1,0:T(8,128)S(1)} %get-tuple-element.61.refs_0_), channel_id=1, source_target_pairs={{0,1},{1,0},{2,3},{3,2},{4,5},{5,4},{6,7},{7,6},{8,9},{9,8},{10,11... | collective-permute-start | bytes 1179656 | tf_op jit(solution)/shard_map/ppermute | solution.py:215
  39.6 5.8 %collective-permute-start.4 = (f32[128,768]{1,0:T(8,128)S(1)}, f32[128,768]{1,0:T(8,128)S(1)}, u32[]{:S(2)}, u32[]{:S(2)}) collective-permute-start(f32[128,768]{1,0:T(8,128)S(1)} %collective-permute-done.3.refs_0_), channel_id=1, source_target_pairs={{0,1},{1,0},{2,3},{3,2},{4,5},{5,4},{6,7},{7,6},{8,9},{9,8},{10,11... | collective-permute-start | bytes 1179656 | tf_op jit(solution)/shard_map/ppermute | solution.py:215
  40.1 2.2 %copy-start = (f32[128,768]{1,0:T(8,128)}, f32[128,768]{1,0:T(8,128)S(1)}, u32[]{:S(2)}) copy-start(f32[128,768]{1,0:T(8,128)S(1)} %collective-permute-done.10.refs_2_) | copy-start | bytes 1179652
  40.1 2.2 %copy-start.2 = (f32[128,768]{1,0:T(8,128)}, f32[128,768]{1,0:T(8,128)S(1)}, u32[]{:S(2)}) copy-start(f32[128,768]{1,0:T(8,128)S(1)} %collective-permute-done.11.refs_3_) | copy-start | bytes 1179652
  42.3 11.5 %collective-permute-start.13 = (f32[256,384]{1,0:T(8,128)}, f32[256,384]{1,0:T(8,128)}, u32[]{:S(2)}, u32[]{:S(2)}) collective-permute-start(f32[256,384]{1,0:T(8,128)} %get-tuple-element.67), channel_id=1, source_target_pairs={{0,4},{1,5},{2,6},{3,7},{4,0},{5,1},{6,2},{7,3},{8,12},{9,13},{10,... | collective-permute-start | bytes 1179656 | tf_op jit(solution)/shard_map/ppermute | solution.py:215
  43.9 13.5 %collective-permute-start.12 = (f32[256,384]{1,0:T(8,128)}, f32[256,384]{1,0:T(8,128)}, u32[]{:S(2)}, u32[]{:S(2)}) collective-permute-start(f32[256,384]{1,0:T(8,128)} %get-tuple-element.66), channel_id=1, source_target_pairs={{0,2},{1,3},{2,0},{3,1},{4,6},{5,7},{6,4},{7,5},{8,10},{9,11},{10,... | collective-permute-start | bytes 1179656 | tf_op jit(solution)/shard_map/ppermute | solution.py:215
  45.4 9.9 %copy-start.7 = (f32[768,384]{1,0:T(8,128)S(1)}, f32[768,384]{1,0:T(8,128)}, u32[]{:S(2)}) copy-start(f32[768,384]{1,0:T(8,128)} %copy-done.6) | copy-start | bytes 3538948
  54.8 3.7 %copy-start.1 = (f32[128,768]{1,0:T(8,128)S(1)}, f32[128,768]{1,0:T(8,128)}, u32[]{:S(2)}) copy-start(f32[128,768]{1,0:T(8,128)} %copy-done) | copy-start | bytes 1179652
  54.9 3.7 %copy-start.3 = (f32[128,768]{1,0:T(8,128)S(1)}, f32[128,768]{1,0:T(8,128)}, u32[]{:S(2)}) copy-start(f32[128,768]{1,0:T(8,128)} %copy-done.2) | copy-start | bytes 1179652
  54.9 7.2 %collective-permute-start.15 = (f32[128,384]{1,0:T(8,128)S(1)}, f32[128,384]{1,0:T(8,128)S(1)}, u32[]{:S(2)}, u32[]{:S(2)}) collective-permute-start(f32[128,384]{1,0:T(8,128)S(1)} %get-tuple-element.79), channel_id=1, source_target_pairs={{0,3},{1,2},{2,1},{3,0},{4,7},{5,6},{6,5},{7,4},{8,11},{9,10},{10,... | collective-permute-start | bytes 589832 | tf_op jit(solution)/shard_map/ppermute | solution.py:215
  55.3 3.3 %copy-start.5 = (f32[768,384]{1,0:T(8,128)S(1)}, f32[768,384]{1,0:T(8,128)}, u32[]{:S(2)}) copy-start(f32[768,384]{1,0:T(8,128)} %copy-done.4) | copy-start | bytes 3538948
  55.4 44.4 %collective-permute-start.7 = (f32[768,384]{1,0:T(8,128)S(1)}, f32[768,384]{1,0:T(8,128)S(1)}, u32[]{:S(2)}, u32[]{:S(2)}) collective-permute-start(f32[768,384]{1,0:T(8,128)S(1)} %broadcast_select_fusion.1), channel_id=1, source_target_pairs={{8,0},{16,24},{0,16},{24,8},{9,1},{17,25},{1,17},{25,9},{10,2},{18... | collective-permute-start | bytes 3538952 | tf_op jit(solution)/shard_map/ppermute | solution.py:203
  56.4 6.7 %collective-permute-start.18 = (f32[128,384]{1,0:T(8,128)S(1)}, f32[128,384]{1,0:T(8,128)S(1)}, u32[]{:S(2)}, u32[]{:S(2)}) collective-permute-start(f32[128,384]{1,0:T(8,128)S(1)} %get-tuple-element.72), channel_id=1, source_target_pairs={{0,1},{1,0},{2,3},{3,2},{4,5},{5,4},{6,7},{7,6},{8,9},{9,8},{10,11... | collective-permute-start | bytes 589832 | tf_op jit(solution)/shard_map/ppermute | solution.py:215
  60.0 17.5 %collective-permute-start.17 = (f32[256,384]{1,0:T(8,128)S(1)}, f32[256,384]{1,0:T(8,128)S(1)}, u32[]{:S(2)}, u32[]{:S(2)}) collective-permute-start(f32[256,384]{1,0:T(8,128)S(1)} %get-tuple-element.75), channel_id=1, source_target_pairs={{0,4},{1,5},{2,6},{3,7},{4,0},{5,1},{6,2},{7,3},{8,12},{9,13},{10,... | collective-permute-start | bytes 1179656 | tf_op jit(solution)/shard_map/ppermute | solution.py:215
  62.1 15.5 %collective-permute-start.16 = (f32[256,384]{1,0:T(8,128)S(1)}, f32[256,384]{1,0:T(8,128)S(1)}, u32[]{:S(2)}, u32[]{:S(2)}) collective-permute-start(f32[256,384]{1,0:T(8,128)S(1)} %get-tuple-element.74), channel_id=1, source_target_pairs={{0,2},{1,3},{2,0},{3,1},{4,6},{5,7},{6,4},{7,5},{8,10},{9,11},{10,... | collective-permute-start | bytes 1179656 | tf_op jit(solution)/shard_map/ppermute | solution.py:215
  63.0 12.2 %collective-permute-start.14 = (f32[128,384]{1,0:T(8,128)S(1)}, f32[128,384]{1,0:T(8,128)S(1)}, u32[]{:S(2)}, u32[]{:S(2)}) collective-permute-start(f32[128,384]{1,0:T(8,128)S(1)} %get-tuple-element.78), channel_id=1, source_target_pairs={{0,4},{1,5},{2,6},{3,7},{4,0},{5,1},{6,2},{7,3},{8,12},{9,13},{10,... | collective-permute-start | bytes 589832 | tf_op jit(solution)/shard_map/ppermute | solution.py:215
  77.6 6.6 %collective-permute-start.20 = (f32[128,384]{1,0:T(8,128)S(1)}, f32[128,384]{1,0:T(8,128)S(1)}, u32[]{:S(2)}, u32[]{:S(2)}) collective-permute-start(f32[128,384]{1,0:T(8,128)S(1)} %get-tuple-element.89), channel_id=1, source_target_pairs={{0,3},{1,2},{2,1},{3,0},{4,7},{5,6},{6,5},{7,4},{8,11},{9,10},{10,... | collective-permute-start | bytes 589832 | tf_op jit(solution)/shard_map/ppermute | solution.py:215
  80.5 19.2 %collective-permute-start.21 = (f32[256,384]{1,0:T(8,128)S(1)}, f32[256,384]{1,0:T(8,128)S(1)}, u32[]{:S(2)}, u32[]{:S(2)}) collective-permute-start(f32[256,384]{1,0:T(8,128)S(1)} %get-tuple-element.86), channel_id=1, source_target_pairs={{0,2},{1,3},{2,0},{3,1},{4,6},{5,7},{6,4},{7,5},{8,10},{9,11},{10,... | collective-permute-start | bytes 1179656 | tf_op jit(solution)/shard_map/ppermute | solution.py:215
  81.4 18.4 %collective-permute-start.22 = (f32[256,384]{1,0:T(8,128)S(1)}, f32[256,384]{1,0:T(8,128)S(1)}, u32[]{:S(2)}, u32[]{:S(2)}) collective-permute-start(f32[256,384]{1,0:T(8,128)S(1)} %get-tuple-element.87), channel_id=1, source_target_pairs={{0,4},{1,5},{2,6},{3,7},{4,0},{5,1},{6,2},{7,3},{8,12},{9,13},{10,... | collective-permute-start | bytes 1179656 | tf_op jit(solution)/shard_map/ppermute | solution.py:215
  82.9 14.6 %collective-permute-start.19 = (f32[128,384]{1,0:T(8,128)S(1)}, f32[128,384]{1,0:T(8,128)S(1)}, u32[]{:S(2)}, u32[]{:S(2)}) collective-permute-start(f32[128,384]{1,0:T(8,128)S(1)} %get-tuple-element.88), channel_id=1, source_target_pairs={{0,4},{1,5},{2,6},{3,7},{4,0},{5,1},{6,2},{7,3},{8,12},{9,13},{10,... | collective-permute-start | bytes 589832 | tf_op jit(solution)/shard_map/ppermute | solution.py:215
  84.1 14.7 %collective-permute-start.23 = (f32[128,384]{1,0:T(8,128)S(1)}, f32[128,384]{1,0:T(8,128)S(1)}, u32[]{:S(2)}, u32[]{:S(2)}) collective-permute-start(f32[128,384]{1,0:T(8,128)S(1)} %get-tuple-element.84), channel_id=1, source_target_pairs={{0,1},{1,0},{2,3},{3,2},{4,5},{5,4},{6,7},{7,6},{8,9},{9,8},{10,11... | collective-permute-start | bytes 589832 | tf_op jit(solution)/shard_map/ppermute | solution.py:215
  101.3 12.0 %collective-permute-start.24 = (f32[256,384]{1,0:T(8,128)S(1)}, f32[256,384]{1,0:T(8,128)S(1)}, u32[]{:S(2)}, u32[]{:S(2)}) collective-permute-start(f32[256,384]{1,0:T(8,128)S(1)} %get-tuple-element.96), channel_id=1, source_target_pairs={{0,2},{1,3},{2,0},{3,1},{4,6},{5,7},{6,4},{7,5},{8,10},{9,11},{10,... | collective-permute-start | bytes 1179656 | tf_op jit(solution)/shard_map/ppermute | solution.py:215
  102.3 12.7 %collective-permute-start.26 = (f32[256,384]{1,0:T(8,128)S(1)}, f32[256,384]{1,0:T(8,128)S(1)}, u32[]{:S(2)}, u32[]{:S(2)}) collective-permute-start(f32[256,384]{1,0:T(8,128)S(1)} %get-tuple-element.97), channel_id=1, source_target_pairs={{0,4},{1,5},{2,6},{3,7},{4,0},{5,1},{6,2},{7,3},{8,12},{9,13},{10,... | collective-permute-start | bytes 1179656 | tf_op jit(solution)/shard_map/ppermute | solution.py:215
  103.8 14.7 %collective-permute-start.29 = (f32[128,384]{1,0:T(8,128)S(1)}, f32[128,384]{1,0:T(8,128)S(1)}, u32[]{:S(2)}, u32[]{:S(2)}) collective-permute-start(f32[128,384]{1,0:T(8,128)S(1)} %get-tuple-element.105), channel_id=1, source_target_pairs={{0,4},{1,5},{2,6},{3,7},{4,0},{5,1},{6,2},{7,3},{8,12},{9,13},{10,... | collective-permute-start | bytes 589832 | tf_op jit(solution)/shard_map/ppermute | solution.py:215
  104.3 14.2 %collective-permute-start.30 = (f32[128,384]{1,0:T(8,128)S(1)}, f32[128,384]{1,0:T(8,128)S(1)}, u32[]{:S(2)}, u32[]{:S(2)}) collective-permute-start(f32[128,384]{1,0:T(8,128)S(1)} %get-tuple-element.94), channel_id=1, source_target_pairs={{0,1},{1,0},{2,3},{3,2},{4,5},{5,4},{6,7},{7,6},{8,9},{9,8},{10,11... | collective-permute-start | bytes 589832 | tf_op jit(solution)/shard_map/ppermute | solution.py:215
  104.3 14.2 %collective-permute-start.31 = (f32[128,384]{1,0:T(8,128)S(1)}, f32[128,384]{1,0:T(8,128)S(1)}, u32[]{:S(2)}, u32[]{:S(2)}) collective-permute-start(f32[128,384]{1,0:T(8,128)S(1)} %get-tuple-element.106), channel_id=1, source_target_pairs={{0,3},{1,2},{2,1},{3,0},{4,7},{5,6},{6,5},{7,4},{8,11},{9,10},{10,... | collective-permute-start | bytes 589832 | tf_op jit(solution)/shard_map/ppermute | solution.py:215
  113.3 7.8 %collective-permute-start.25 = (f32[128,384]{1,0:T(8,128)S(1)}, f32[128,384]{1,0:T(8,128)S(1)}, u32[]{:S(2)}, u32[]{:S(2)}) collective-permute-start(f32[128,384]{1,0:T(8,128)S(1)} %get-tuple-element.101), channel_id=1, source_target_pairs={{0,4},{1,5},{2,6},{3,7},{4,0},{5,1},{6,2},{7,3},{8,12},{9,13},{10,... | collective-permute-start | bytes 589832 | tf_op jit(solution)/shard_map/ppermute | solution.py:215
  115.0 6.2 %collective-permute-start.27 = (f32[128,384]{1,0:T(8,128)S(1)}, f32[128,384]{1,0:T(8,128)S(1)}, u32[]{:S(2)}, u32[]{:S(2)}) collective-permute-start(f32[128,384]{1,0:T(8,128)S(1)} %get-tuple-element.103), channel_id=1, source_target_pairs={{0,1},{1,0},{2,3},{3,2},{4,5},{5,4},{6,7},{7,6},{8,9},{9,8},{10,11... | collective-permute-start | bytes 589832 | tf_op jit(solution)/shard_map/ppermute | solution.py:215
  118.5 6.8 %collective-permute-start.28 = (f32[128,384]{1,0:T(8,128)S(1)}, f32[128,384]{1,0:T(8,128)S(1)}, u32[]{:S(2)}, u32[]{:S(2)}) collective-permute-start(f32[128,384]{1,0:T(8,128)S(1)} %get-tuple-element.104), channel_id=1, source_target_pairs={{0,3},{1,2},{2,1},{3,0},{4,7},{5,6},{6,5},{7,4},{8,11},{9,10},{10,... | collective-permute-start | bytes 589832 | tf_op jit(solution)/shard_map/ppermute | solution.py:215

commit v17 on v16

--- a/solution.py
+++ b/solution.py
@@ -234,7 +234,7 @@
     near = [[r for r in range(groups) if not r & o[0]] for o in orders]
 
     out = None
-    token = settled = []
+    token = []
     for n in range(len(stages)):
         ds, right = [d for d, _ in stages[n]], [block for _, block in stages[n]]
         if isinstance(right[0], tuple):
@@ -244,7 +244,7 @@
         right = list(lax.optimization_barrier((*right, *token))[: len(right)])
         sent = products([[rel[h][r] for r in away[h]] for h in range(2)], right)
         moving = [swap(sent[h], 2 * orders[h][0]) for h in range(2)]
-        right[0] = after(right[0], *sent, *settled)
+        right[0] = after(right[0], *sent)
         held = list(products([[rel[h][r] for r in near[h]] for h in range(2)], right))
         names = [near[0], near[1]]
         for level in range(1, len(bits)):
@@ -257,7 +257,6 @@
                 names[h] = [names[h][i] for i in stays]
         pieces = [held[0], moving[0], swap(held[1], 1), moving[1]]
         token = [*held] if out is None else [*held, out]
-        settled = moving if n + 2 < len(stages) else []
         out = write(out, (rows, n_occ * width), ds, half, pieces)
     return out
 

time: 127 us -> 121 us (0.953)
  waiting for transfers between devices: 69.8 us -> 65.4 us
    ppermute x28, waiting for transfers between devices: 64.2 us -> 60.1 us  [swap(): return lax.ppermute(x, 'vir', [(i, i ^ bits) for i in range(n_vir)])]
  transfers between devices with their start and end apart: 32 -> 32, of which waited for: 12 -> 14; matrix products, arithmetic and copies ran while one was open for 1% -> 1% of each run, Pallas kernels for 13% -> 14%
where the time goes in v17:
time: 121 us
  waiting for transfers between devices  65.4 us (54%)
  starting transfers between devices  33.3 us (28%)
  Pallas kernels  20.5 us (17%)
  other arithmetic  1.53 us (1%)
    ppermute x28, waiting for transfers between devices, swap(): return lax.ppermute(x, 'vir', [(i, i ^ bits) for i in range(n_vir)])  60.1 us
    ppermute x28, starting transfers between devices, swap(): return lax.ppermute(x, 'vir', [(i, i ^ bits) for i in range(n_vir)])  21.8 us
    pallas_call x19, Pallas kernels, kernel_call(): pl.pallas_call(body, out_shape=[pltpu.VMEM(shape, jnp.float32) for shape...  17.2 us
    ppermute x1, starting transfers between devices, line_stages(): far = lax.ppermute(after(own, centre, near), 'occ', [(0, 3), (3, 0)])  5.67 us
    ppermute x1, waiting for transfers between devices, direct(): return lax.ppermute(x, 'occ', [(i, i ^ d) for i in range(nodes)])  5.25 us
    pallas_call x4, Pallas kernels, write(): pl.pallas_call(functools.partial(write_kernel, ds, half), out_shape=jax.S...  3.22 us
    ppermute x1, starting transfers between devices, direct(): return lax.ppermute(x, 'occ', [(i, i ^ d) for i in range(nodes)])  3.01 us
  transfers between devices with their start and end apart: 32, of which 14 were waited for; matrix products, arithmetic and copies ran while one was open for 1% of the time, Pallas kernels for 14%

profile of v17, /device:TPU:0, one launch (start us, length us, event | category | flops | bytes accessed | tf_op | source)
XLA Modules:
  0.0 121.2 jit_solution(13502517859217251665)
XLA Ops:
  0.0 1.3 %halves.1 = (f32[384,384]{1,0:T(8,128)S(1)}, f32[384,384]{1,0:T(8,128)S(1)}) custom-call(s32[3,6]{1,0:T(4,128)} %mask_hbm.1, f32[384,768]{1,0:T(8,128)} %int_hbm.1), custom_call_target="tpu_custom_call" | custom-call | flops 1 | bytes 1 | tf_op jit(solution)/shard_map/halves/pallas_call | solution.py:30
  1.3 0.5 collective-permute-start.5
  1.8 1.4 %cut.1 = (f32[128,768]{1,0:T(8,128)S(1)}, f32[128,768]{1,0:T(8,128)S(1)}, f32[128,768]{1,0:T(8,128)S(1)}, f32[128,768]{1,0:T(8,128)S(1)}) custom-call(s32[4,24]{1,0:T(4,128)} %mask_hbm.2, f32[128,3072]{1,0:T(8,128)} %amp_hbm.1), custom_call_target="tpu_custom_call" | custom-call | flops 1 | bytes 1 | tf_op jit(solution)/shard_map/cut/pallas_call | solution.py:30
  3.3 0.2 collective-permute-done.5.other_ref
  3.5 0.1 join.1.refs_4_
  3.6 3.0 %collective-permute-start.8 = (f32[768,384]{1,0:T(8,128)S(1)}, f32[768,384]{1,0:T(8,128)S(1)}, u32[]{:S(2)}, u32[]{:S(2)}) collective-permute-start(f32[768,384]{1,0:T(8,128)S(1)} %join.1.refs_4_), channel_id=1, source_target_pairs={{0,8},{8,0},{16,24},{24,16},{1,9},{9,1},{17,25},{25,17},{2,10},{10... | collective-permute-start | bytes 3538952 | tf_op jit(solution)/shard_map/ppermute | solution.py:193
  6.6 0.7 collective-permute-start.6
  7.3 2.5 %collective-permute-start.1 = (f32[128,768]{1,0:T(8,128)S(1)}, f32[128,768]{1,0:T(8,128)S(1)}, u32[]{:S(2)}, u32[]{:S(2)}) collective-permute-start(f32[128,768]{1,0:T(8,128)S(1)} %get-tuple-element.60), channel_id=1, source_target_pairs={{0,6},{1,7},{2,4},{3,5},{4,2},{5,3},{6,0},{7,1},{8,14},{9,15},{10,... | collective-permute-start | bytes 1179656 | tf_op jit(solution)/shard_map/ppermute | solution.py:215
  9.8 0.5 collective-permute-start
  10.3 0.5 collective-permute-start.3
  10.9 9.5 %collective-permute-done.1.refs_1_ = f32[128,768]{1,0:T(8,128)S(1)} collective-permute-done((f32[128,768]{1,0:T(8,128)S(1)}, f32[128,768]{1,0:T(8,128)S(1)}, u32[]{:S(2)}, u32[]{:S(2)}) %collective-permute-start.1) | collective-permute-done | bytes 393248 | tf_op jit(solution)/shard_map/ppermute | solution.py:215
  20.3 7.3 %collective-permute-done.refs_1_ = f32[128,768]{1,0:T(8,128)S(1)} collective-permute-done((f32[128,768]{1,0:T(8,128)S(1)}, f32[128,768]{1,0:T(8,128)S(1)}, u32[]{:S(2)}, u32[]{:S(2)}) %collective-permute-start) | collective-permute-done | bytes 393248 | tf_op jit(solution)/shard_map/ppermute | solution.py:215
  27.6 0.0 collective-permute-start.10
  27.6 5.3 %collective-permute-done.8.refs_4_ = f32[768,384]{1,0:T(8,128)S(1)} collective-permute-done((f32[768,384]{1,0:T(8,128)S(1)}, f32[768,384]{1,0:T(8,128)S(1)}, u32[]{:S(2)}, u32[]{:S(2)}) %collective-permute-start.8) | collective-permute-done | bytes 1179680 | tf_op jit(solution)/shard_map/ppermute | solution.py:193
  32.9 5.7 %collective-permute-start.9 = (f32[768,384]{1,0:T(8,128)S(1)}, f32[768,384]{1,0:T(8,128)}, u32[]{:S(2)}, u32[]{:S(2)}) collective-permute-start(f32[768,384]{1,0:T(8,128)S(1)} %join.1.refs_4_), channel_id=1, source_target_pairs={{0,24},{24,0},{1,25},{25,1},{2,26},{26,2},{3,27},{27,3},{4,28},{28... | collective-permute-start | bytes 3538952 | tf_op jit(solution)/shard_map/ppermute | solution.py:199
  38.5 0.1 collective-permute-start.2
  38.6 0.5 collective-permute-start.4
  39.1 0.0 collective-permute-done.10.refs_2_
  39.1 2.2 %products.8 = (f32[256,384]{1,0:T(8,128)}, f32[256,384]{1,0:T(8,128)}) custom-call(f32[128,768]{1,0:T(8,128)S(1)} %collective-permute-done.3.refs_0_, f32[128,768]{1,0:T(8,128)S(1)} %collective-permute-done.1.refs_1_, f32[128,768]{1,0:T(8,128)S(1)} %collective-permute-done.10.refs_2_, f32[128,768]{1,0:T(8,128)S(1)} %collective-permute-done.11.refs_3_, ...), custom_call_target="tpu_custom_call" | custom-call | flops 1 | bytes 1 | tf_op jit(solution)/shard_map/products/pallas_call | solution.py:30
  41.3 1.6 %collective-permute-start.13 = (f32[256,384]{1,0:T(8,128)}, f32[256,384]{1,0:T(8,128)}, u32[]{:S(2)}, u32[]{:S(2)}) collective-permute-start(f32[256,384]{1,0:T(8,128)} %get-tuple-element.67), channel_id=1, source_target_pairs={{0,4},{1,5},{2,6},{3,7},{4,0},{5,1},{6,2},{7,3},{8,12},{9,13},{10,... | collective-permute-start | bytes 1179656 | tf_op jit(solution)/shard_map/ppermute | solution.py:215
  42.9 1.5 %collective-permute-start.12 = (f32[256,384]{1,0:T(8,128)}, f32[256,384]{1,0:T(8,128)}, u32[]{:S(2)}, u32[]{:S(2)}) collective-permute-start(f32[256,384]{1,0:T(8,128)} %get-tuple-element.66), channel_id=1, source_target_pairs={{0,2},{1,3},{2,0},{3,1},{4,6},{5,7},{6,4},{7,5},{8,10},{9,11},{10,... | collective-permute-start | bytes 1179656 | tf_op jit(solution)/shard_map/ppermute | solution.py:215
  44.4 0.0 collective-permute-done.2.refs_2_
  44.4 1.4 %products.9 = (f32[256,384]{1,0:T(8,128)S(1)}, f32[256,384]{1,0:T(8,128)S(1)}) custom-call(f32[128,768]{1,0:T(8,128)S(1)} %get-tuple-element.61.refs_0_, f32[128,768]{1,0:T(8,128)S(1)} %collective-permute-done.refs_1_, f32[128,768]{1,0:T(8,128)S(1)} %collective-permute-done.2.refs_2_, f32[128,768]{1,0:T(8,128)S(1)} %collective-permute-done.4.refs_3_, ...), custom_call_target="tpu_custom_call" | custom-call | flops 1 | bytes 1 | tf_op jit(solution)/shard_map/products/pallas_call | solution.py:30
  45.8 7.0 %collective-permute-done.13.got_ref = f32[256,384]{1,0:T(8,128)} collective-permute-done((f32[256,384]{1,0:T(8,128)}, f32[256,384]{1,0:T(8,128)}, u32[]{:S(2)}, u32[]{:S(2)}) %collective-permute-start.13) | collective-permute-done | bytes 393248 | tf_op jit(solution)/shard_map/ppermute | solution.py:215
  52.8 1.0 fold.9
  53.9 0.1 collective-permute-start.17
  54.0 0.1 broadcast_select_fusion.1
  54.1 2.1 %collective-permute-start.7 = (f32[768,384]{1,0:T(8,128)S(1)}, f32[768,384]{1,0:T(8,128)S(1)}, u32[]{:S(2)}, u32[]{:S(2)}) collective-permute-start(f32[768,384]{1,0:T(8,128)S(1)} %broadcast_select_fusion.1), channel_id=1, source_target_pairs={{8,0},{16,24},{0,16},{24,8},{9,1},{17,25},{1,17},{25,9},{10,2},{18... | collective-permute-start | bytes 3538952 | tf_op jit(solution)/shard_map/ppermute | solution.py:203
  56.2 1.3 %collective-permute-start.18 = (f32[128,384]{1,0:T(8,128)S(1)}, f32[128,384]{1,0:T(8,128)S(1)}, u32[]{:S(2)}, u32[]{:S(2)}) collective-permute-start(f32[128,384]{1,0:T(8,128)S(1)} %get-tuple-element.84), channel_id=1, source_target_pairs={{0,3},{1,2},{2,1},{3,0},{4,7},{5,6},{6,5},{7,4},{8,11},{9,10},{10,... | collective-permute-start | bytes 589832 | tf_op jit(solution)/shard_map/ppermute | solution.py:215
  57.5 1.1 fold.8
  58.5 1.4 %products.10 = (f32[256,384]{1,0:T(8,128)S(1)}, f32[256,384]{1,0:T(8,128)S(1)}) custom-call(f32[128,768]{1,0:T(8,128)S(1)} %collective-permute-done.3.refs_0_, f32[128,768]{1,0:T(8,128)S(1)} %collective-permute-done.1.refs_1_, f32[128,768]{1,0:T(8,128)S(1)} %copy-done.3, f32[128,768]{1,0:T(8,128)S(1)} %copy-done.1, f32[768,384]{1,0:T(8,128)S(1)} %copy-done.5), custom_call_target="tpu_custom_call" | custom-call | flops 1 | bytes 1 | tf_op jit(solution)/shard_map/products/pallas_call | solution.py:30
  60.0 1.6 %collective-permute-start.15 = (f32[256,384]{1,0:T(8,128)S(1)}, f32[256,384]{1,0:T(8,128)S(1)}, u32[]{:S(2)}, u32[]{:S(2)}) collective-permute-start(f32[256,384]{1,0:T(8,128)S(1)} %get-tuple-element.75), channel_id=1, source_target_pairs={{0,4},{1,5},{2,6},{3,7},{4,0},{5,1},{6,2},{7,3},{8,12},{9,13},{10,... | collective-permute-start | bytes 1179656 | tf_op jit(solution)/shard_map/ppermute | solution.py:215
  61.6 0.5 collective-permute-start.14
  62.1 1.0 collective-permute-done.18.other_b
  63.1 1.5 %collective-permute-start.16 = (f32[128,384]{1,0:T(8,128)S(1)}, f32[128,384]{1,0:T(8,128)S(1)}, u32[]{:S(2)}, u32[]{:S(2)}) collective-permute-start(f32[128,384]{1,0:T(8,128)S(1)} %get-tuple-element.83), channel_id=1, source_target_pairs={{0,4},{1,5},{2,6},{3,7},{4,0},{5,1},{6,2},{7,3},{8,12},{9,13},{10,... | collective-permute-start | bytes 589832 | tf_op jit(solution)/shard_map/ppermute | solution.py:215
  64.6 11.0 %collective-permute-done.16.mine_b = f32[128,384]{1,0:T(8,128)S(1)} collective-permute-done((f32[128,384]{1,0:T(8,128)S(1)}, f32[128,384]{1,0:T(8,128)S(1)}, u32[]{:S(2)}, u32[]{:S(2)}) %collective-permute-start.16) | collective-permute-done | bytes 196640 | tf_op jit(solution)/shard_map/ppermute | solution.py:215
  75.6 0.8 write.4.refs_0_
  76.4 1.4 %products.11 = (f32[256,384]{1,0:T(8,128)S(1)}, f32[256,384]{1,0:T(8,128)S(1)}) custom-call(f32[128,768]{1,0:T(8,128)S(1)} %get-tuple-element.61.refs_0_, f32[128,768]{1,0:T(8,128)S(1)} %collective-permute-done.refs_1_, f32[128,768]{1,0:T(8,128)S(1)} %collective-permute-done.2.refs_2_, f32[128,768]{1,0:T(8,128)S(1)} %collective-permute-done.4.refs_3_, ...), custom_call_target="tpu_custom_call" | custom-call | flops 1 | bytes 1 | tf_op jit(solution)/shard_map/products/pallas_call | solution.py:30
  77.9 0.1 collective-permute-start.22
  78.0 1.4 %broadcast_select_fusion.refs_4_ = f32[768,384]{1,0:T(8,128)S(1)} fusion(f32[768,384]{1,0:T(8,128)S(1)} %copy-done.7, f32[768,384]{1,0:T(8,128)} %collective-permute-done.9, pred[]{:T(512)S(6)} %or.3), kind=kLoop, calls=%fused_computation | loop fusion | flops 294912 | bytes 3538945 | tf_op jit(solution)/shard_map/jit(_where)/select_n | solution.py:243
  79.4 1.4 %products.12 = (f32[256,384]{1,0:T(8,128)S(1)}, f32[256,384]{1,0:T(8,128)S(1)}) custom-call(f32[128,768]{1,0:T(8,128)S(1)} %collective-permute-done.3.refs_0_, f32[128,768]{1,0:T(8,128)S(1)} %collective-permute-done.1.refs_1_, f32[128,768]{1,0:T(8,128)S(1)} %copy-done.3, f32[128,768]{1,0:T(8,128)S(1)} %copy-done.1, f32[768,384]{1,0:T(8,128)S(1)} %broadcast_select_fusion.refs_4_), custom_call_target="tpu_custom_call" | custom-call | flops 1 | bytes 1 | tf_op jit(solution)/shard_map/products/pallas_call | solution.py:30
  80.9 1.6 %collective-permute-start.20 = (f32[256,384]{1,0:T(8,128)S(1)}, f32[256,384]{1,0:T(8,128)S(1)}, u32[]{:S(2)}, u32[]{:S(2)}) collective-permute-start(f32[256,384]{1,0:T(8,128)S(1)} %get-tuple-element.87), channel_id=1, source_target_pairs={{0,4},{1,5},{2,6},{3,7},{4,0},{5,1},{6,2},{7,3},{8,12},{9,13},{10,... | collective-permute-start | bytes 1179656 | tf_op jit(solution)/shard_map/ppermute | solution.py:215
  82.5 0.5 collective-permute-start.19
  83.0 1.0 collective-permute-start.23
  84.0 0.5 collective-permute-start.21
  84.5 1.4 %products.13 = (f32[256,384]{1,0:T(8,128)S(1)}, f32[256,384]{1,0:T(8,128)S(1)}) custom-call(f32[128,768]{1,0:T(8,128)S(1)} %get-tuple-element.61.refs_0_, f32[128,768]{1,0:T(8,128)S(1)} %collective-permute-done.refs_1_, f32[128,768]{1,0:T(8,128)S(1)} %collective-permute-done.2.refs_2_, f32[128,768]{1,0:T(8,128)S(1)} %collective-permute-done.4.refs_3_, ...), custom_call_target="tpu_custom_call" | custom-call | flops 1 | bytes 1 | tf_op jit(solution)/shard_map/products/pallas_call | solution.py:30
  85.9 11.2 %collective-permute-done.23.other_b = f32[128,384]{1,0:T(8,128)S(1)} collective-permute-done((f32[128,384]{1,0:T(8,128)S(1)}, f32[128,384]{1,0:T(8,128)S(1)}, u32[]{:S(2)}, u32[]{:S(2)}) %collective-permute-start.23) | collective-permute-done | bytes 196640 | tf_op jit(solution)/shard_map/ppermute | solution.py:215
  97.2 0.8 write.5.refs_0_
  98.1 1.4 %products.14 = (f32[256,384]{1,0:T(8,128)S(1)}, f32[256,384]{1,0:T(8,128)S(1)}) custom-call(f32[128,768]{1,0:T(8,128)S(1)} %collective-permute-done.3.refs_0_, f32[128,768]{1,0:T(8,128)S(1)} %collective-permute-done.1.refs_1_, f32[128,768]{1,0:T(8,128)S(1)} %copy-done.3, f32[128,768]{1,0:T(8,128)S(1)} %copy-done.1, f32[768,384]{1,0:T(8,128)S(1)} %collective-permute-done.7.refs_4_), custom_call_target="tpu_custom_call" | custom-call | flops 1 | bytes 1 | tf_op jit(solution)/shard_map/products/pallas_call | solution.py:30
  99.5 1.1 collective-permute-start.26
  100.6 0.5 collective-permute-start.24
  101.2 1.6 %collective-permute-start.31 = (f32[128,384]{1,0:T(8,128)S(1)}, f32[128,384]{1,0:T(8,128)S(1)}, u32[]{:S(2)}, u32[]{:S(2)}) collective-permute-start(f32[128,384]{1,0:T(8,128)S(1)} %get-tuple-element.106), channel_id=1, source_target_pairs={{0,3},{1,2},{2,1},{3,0},{4,7},{5,6},{6,5},{7,4},{8,11},{9,10},{10,... | collective-permute-start | bytes 589832 | tf_op jit(solution)/shard_map/ppermute | solution.py:215
  102.8 1.0 collective-permute-start.29
  103.8 1.4 %products.15 = (f32[256,384]{1,0:T(8,128)S(1)}, f32[256,384]{1,0:T(8,128)S(1)}) custom-call(f32[128,768]{1,0:T(8,128)S(1)} %get-tuple-element.61.refs_0_, f32[128,768]{1,0:T(8,128)S(1)} %collective-permute-done.refs_1_, f32[128,768]{1,0:T(8,128)S(1)} %collective-permute-done.2.refs_2_, f32[128,768]{1,0:T(8,128)S(1)} %collective-permute-done.4.refs_3_, ...), custom_call_target="tpu_custom_call" | custom-call | flops 1 | bytes 1 | tf_op jit(solution)/shard_map/products/pallas_call | solution.py:30
  105.2 6.3 %collective-permute-done.26.got_ref = f32[256,384]{1,0:T(8,128)S(1)} collective-permute-done((f32[256,384]{1,0:T(8,128)S(1)}, f32[256,384]{1,0:T(8,128)S(1)}, u32[]{:S(2)}, u32[]{:S(2)}) %collective-permute-start.26) | collective-permute-done | bytes 393248 | tf_op jit(solution)/shard_map/ppermute | solution.py:215
  111.6 0.1 collective-permute-start.27
  111.6 1.0 collective-permute-done.24.got_ref
  112.7 1.0 collective-permute-start.25
  113.7 0.8 collective-permute-done.31.other_b
  114.5 0.9 collective-permute-done.29.mine_b
  115.4 0.8 write.6.refs_0_
  116.2 3.7 %collective-permute-done.28.other_b = f32[128,384]{1,0:T(8,128)S(1)} collective-permute-done((f32[128,384]{1,0:T(8,128)S(1)}, f32[128,384]{1,0:T(8,128)S(1)}, u32[]{:S(2)}, u32[]{:S(2)}) %collective-permute-start.28) | collective-permute-done | bytes 196640 | tf_op jit(solution)/shard_map/ppermute | solution.py:215
  119.9 0.3 collective-permute-done.25.mine_b
  120.2 0.8 write.7
  (41 shorter events, 0.3 us)
Async XLA Ops:
  1.3 2.1 %collective-permute-start.5 = (f32[384,384]{1,0:T(8,128)S(1)}, f32[384,384]{1,0:T(8,128)S(1)}, u32[]{:S(2)}, u32[]{:S(2)}) collective-permute-start(f32[384,384]{1,0:T(8,128)S(1)} %get-tuple-element.63), channel_id=1, source_target_pairs={{0,1},{1,0},{2,3},{3,2},{4,5},{5,4},{6,7},{7,6},{8,9},{9,8},{10,11... | collective-permute-start | bytes 1769480 | tf_op jit(solution)/shard_map/ppermute | solution.py:215
  3.6 29.3 %collective-permute-start.8 = (f32[768,384]{1,0:T(8,128)S(1)}, f32[768,384]{1,0:T(8,128)S(1)}, u32[]{:S(2)}, u32[]{:S(2)}) collective-permute-start(f32[768,384]{1,0:T(8,128)S(1)} %join.1.refs_4_), channel_id=1, source_target_pairs={{0,8},{8,0},{16,24},{24,16},{1,9},{9,1},{17,25},{25,17},{2,10},{10... | collective-permute-start | bytes 3538952 | tf_op jit(solution)/shard_map/ppermute | solution.py:193
  6.6 26.3 %collective-permute-start.6 = (f32[768,384]{1,0:T(8,128)S(1)}, f32[768,384]{1,0:T(8,128)S(1)}, u32[]{:S(2)}, u32[]{:S(2)}) collective-permute-start(f32[768,384]{1,0:T(8,128)S(1)} %join.1.refs_4_), channel_id=1, source_target_pairs={{8,16},{16,8},{9,17},{17,9},{10,18},{18,10},{11,19},{19,11},{12,20... | collective-permute-start | bytes 3538952 | tf_op jit(solution)/shard_map/ppermute | solution.py:197
  7.3 13.0 %collective-permute-start.1 = (f32[128,768]{1,0:T(8,128)S(1)}, f32[128,768]{1,0:T(8,128)S(1)}, u32[]{:S(2)}, u32[]{:S(2)}) collective-permute-start(f32[128,768]{1,0:T(8,128)S(1)} %get-tuple-element.60), channel_id=1, source_target_pairs={{0,6},{1,7},{2,4},{3,5},{4,2},{5,3},{6,0},{7,1},{8,14},{9,15},{10,... | collective-permute-start | bytes 1179656 | tf_op jit(solution)/shard_map/ppermute | solution.py:215
  9.8 17.8 %collective-permute-start = (f32[128,768]{1,0:T(8,128)S(1)}, f32[128,768]{1,0:T(8,128)S(1)}, u32[]{:S(2)}, u32[]{:S(2)}) collective-permute-start(f32[128,768]{1,0:T(8,128)S(1)} %get-tuple-element.59), channel_id=1, source_target_pairs={{0,4},{1,5},{2,6},{3,7},{4,0},{5,1},{6,2},{7,3},{8,12},{9,13},{10,... | collective-permute-start | bytes 1179656 | tf_op jit(solution)/shard_map/ppermute | solution.py:215
  10.3 28.3 %collective-permute-start.3 = (f32[128,768]{1,0:T(8,128)S(1)}, f32[128,768]{1,0:T(8,128)S(1)}, u32[]{:S(2)}, u32[]{:S(2)}) collective-permute-start(f32[128,768]{1,0:T(8,128)S(1)} %get-tuple-element.62), channel_id=1, source_target_pairs={{0,2},{1,3},{2,0},{3,1},{4,6},{5,7},{6,4},{7,5},{8,10},{9,11},{10,... | collective-permute-start | bytes 1179656 | tf_op jit(solution)/shard_map/ppermute | solution.py:215
  20.3 18.8 %collective-permute-start.11 = (f32[128,768]{1,0:T(8,128)S(1)}, f32[128,768]{1,0:T(8,128)S(1)}, u32[]{:S(2)}, u32[]{:S(2)}) collective-permute-start(f32[128,768]{1,0:T(8,128)S(1)} %collective-permute-done.1.refs_1_), channel_id=1, source_target_pairs={{0,1},{1,0},{2,3},{3,2},{4,5},{5,4},{6,7},{7,6},{8,9},{9,8},{10,11... | collective-permute-start | bytes 1179656 | tf_op jit(solution)/shard_map/ppermute | solution.py:215
  27.6 11.5 %collective-permute-start.10 = (f32[128,768]{1,0:T(8,128)S(1)}, f32[128,768]{1,0:T(8,128)S(1)}, u32[]{:S(2)}, u32[]{:S(2)}) collective-permute-start(f32[128,768]{1,0:T(8,128)S(1)} %collective-permute-done.refs_1_), channel_id=1, source_target_pairs={{0,1},{1,0},{2,3},{3,2},{4,5},{5,4},{6,7},{7,6},{8,9},{9,8},{10,11... | collective-permute-start | bytes 1179656 | tf_op jit(solution)/shard_map/ppermute | solution.py:215
  32.8 8.4 %copy-start.4 = (f32[768,384]{1,0:T(8,128)}, f32[768,384]{1,0:T(8,128)S(1)}, u32[]{:S(2)}) copy-start(f32[768,384]{1,0:T(8,128)S(1)} %collective-permute-done.8.refs_4_) | copy-start | bytes 3538948
  32.9 6.3 %copy-start.6 = (f32[768,384]{1,0:T(8,128)}, f32[768,384]{1,0:T(8,128)S(1)}, u32[]{:S(2)}) copy-start(f32[768,384]{1,0:T(8,128)S(1)} %collective-permute-done.6) | copy-start | bytes 3538948
  32.9 45.2 %collective-permute-start.9 = (f32[768,384]{1,0:T(8,128)S(1)}, f32[768,384]{1,0:T(8,128)}, u32[]{:S(2)}, u32[]{:S(2)}) collective-permute-start(f32[768,384]{1,0:T(8,128)S(1)} %join.1.refs_4_), channel_id=1, source_target_pairs={{0,24},{24,0},{1,25},{25,1},{2,26},{26,2},{3,27},{27,3},{4,28},{28... | collective-permute-start | bytes 3538952 | tf_op jit(solution)/shard_map/ppermute | solution.py:199
  38.5 5.9 %collective-permute-start.2 = (f32[128,768]{1,0:T(8,128)S(1)}, f32[128,768]{1,0:T(8,128)S(1)}, u32[]{:S(2)}, u32[]{:S(2)}) collective-permute-start(f32[128,768]{1,0:T(8,128)S(1)} %get-tuple-element.61.refs_0_), channel_id=1, source_target_pairs={{0,1},{1,0},{2,3},{3,2},{4,5},{5,4},{6,7},{7,6},{8,9},{9,8},{10,11... | collective-permute-start | bytes 1179656 | tf_op jit(solution)/shard_map/ppermute | solution.py:215
  38.6 5.8 %collective-permute-start.4 = (f32[128,768]{1,0:T(8,128)S(1)}, f32[128,768]{1,0:T(8,128)S(1)}, u32[]{:S(2)}, u32[]{:S(2)}) collective-permute-start(f32[128,768]{1,0:T(8,128)S(1)} %collective-permute-done.3.refs_0_), channel_id=1, source_target_pairs={{0,1},{1,0},{2,3},{3,2},{4,5},{5,4},{6,7},{7,6},{8,9},{9,8},{10,11... | collective-permute-start | bytes 1179656 | tf_op jit(solution)/shard_map/ppermute | solution.py:215
  39.1 2.2 %copy-start = (f32[128,768]{1,0:T(8,128)}, f32[128,768]{1,0:T(8,128)S(1)}, u32[]{:S(2)}) copy-start(f32[128,768]{1,0:T(8,128)S(1)} %collective-permute-done.11.refs_3_) | copy-start | bytes 1179652
  39.1 2.2 %copy-start.2 = (f32[128,768]{1,0:T(8,128)}, f32[128,768]{1,0:T(8,128)S(1)}, u32[]{:S(2)}) copy-start(f32[128,768]{1,0:T(8,128)S(1)} %collective-permute-done.10.refs_2_) | copy-start | bytes 1179652
  41.3 11.5 %collective-permute-start.13 = (f32[256,384]{1,0:T(8,128)}, f32[256,384]{1,0:T(8,128)}, u32[]{:S(2)}, u32[]{:S(2)}) collective-permute-start(f32[256,384]{1,0:T(8,128)} %get-tuple-element.67), channel_id=1, source_target_pairs={{0,4},{1,5},{2,6},{3,7},{4,0},{5,1},{6,2},{7,3},{8,12},{9,13},{10,... | collective-permute-start | bytes 1179656 | tf_op jit(solution)/shard_map/ppermute | solution.py:215
  42.9 14.6 %collective-permute-start.12 = (f32[256,384]{1,0:T(8,128)}, f32[256,384]{1,0:T(8,128)}, u32[]{:S(2)}, u32[]{:S(2)}) collective-permute-start(f32[256,384]{1,0:T(8,128)} %get-tuple-element.66), channel_id=1, source_target_pairs={{0,2},{1,3},{2,0},{3,1},{4,6},{5,7},{6,4},{7,5},{8,10},{9,11},{10,... | collective-permute-start | bytes 1179656 | tf_op jit(solution)/shard_map/ppermute | solution.py:215
  44.4 9.5 %copy-start.7 = (f32[768,384]{1,0:T(8,128)S(1)}, f32[768,384]{1,0:T(8,128)}, u32[]{:S(2)}) copy-start(f32[768,384]{1,0:T(8,128)} %copy-done.6) | copy-start | bytes 3538948
  53.8 4.7 %copy-start.1 = (f32[128,768]{1,0:T(8,128)S(1)}, f32[128,768]{1,0:T(8,128)}, u32[]{:S(2)}) copy-start(f32[128,768]{1,0:T(8,128)} %copy-done) | copy-start | bytes 1179652
  53.8 4.7 %copy-start.3 = (f32[128,768]{1,0:T(8,128)S(1)}, f32[128,768]{1,0:T(8,128)}, u32[]{:S(2)}) copy-start(f32[128,768]{1,0:T(8,128)} %copy-done.2) | copy-start | bytes 1179652
  53.9 7.7 %collective-permute-start.17 = (f32[128,384]{1,0:T(8,128)S(1)}, f32[128,384]{1,0:T(8,128)S(1)}, u32[]{:S(2)}, u32[]{:S(2)}) collective-permute-start(f32[128,384]{1,0:T(8,128)S(1)} %get-tuple-element.72), channel_id=1, source_target_pairs={{0,1},{1,0},{2,3},{3,2},{4,5},{5,4},{6,7},{7,6},{8,9},{9,8},{10,11... | collective-permute-start | bytes 589832 | tf_op jit(solution)/shard_map/ppermute | solution.py:215
  53.9 4.6 %copy-start.5 = (f32[768,384]{1,0:T(8,128)S(1)}, f32[768,384]{1,0:T(8,128)}, u32[]{:S(2)}) copy-start(f32[768,384]{1,0:T(8,128)} %copy-done.4) | copy-start | bytes 3538948
  54.1 44.0 %collective-permute-start.7 = (f32[768,384]{1,0:T(8,128)S(1)}, f32[768,384]{1,0:T(8,128)S(1)}, u32[]{:S(2)}, u32[]{:S(2)}) collective-permute-start(f32[768,384]{1,0:T(8,128)S(1)} %broadcast_select_fusion.1), channel_id=1, source_target_pairs={{8,0},{16,24},{0,16},{24,8},{9,1},{17,25},{1,17},{25,9},{10,2},{18... | collective-permute-start | bytes 3538952 | tf_op jit(solution)/shard_map/ppermute | solution.py:203
  56.2 6.9 %collective-permute-start.18 = (f32[128,384]{1,0:T(8,128)S(1)}, f32[128,384]{1,0:T(8,128)S(1)}, u32[]{:S(2)}, u32[]{:S(2)}) collective-permute-start(f32[128,384]{1,0:T(8,128)S(1)} %get-tuple-element.84), channel_id=1, source_target_pairs={{0,3},{1,2},{2,1},{3,0},{4,7},{5,6},{6,5},{7,4},{8,11},{9,10},{10,... | collective-permute-start | bytes 589832 | tf_op jit(solution)/shard_map/ppermute | solution.py:215
  60.0 17.8 %collective-permute-start.15 = (f32[256,384]{1,0:T(8,128)S(1)}, f32[256,384]{1,0:T(8,128)S(1)}, u32[]{:S(2)}, u32[]{:S(2)}) collective-permute-start(f32[256,384]{1,0:T(8,128)S(1)} %get-tuple-element.75), channel_id=1, source_target_pairs={{0,4},{1,5},{2,6},{3,7},{4,0},{5,1},{6,2},{7,3},{8,12},{9,13},{10,... | collective-permute-start | bytes 1179656 | tf_op jit(solution)/shard_map/ppermute | solution.py:215
  61.6 16.4 %collective-permute-start.14 = (f32[256,384]{1,0:T(8,128)S(1)}, f32[256,384]{1,0:T(8,128)S(1)}, u32[]{:S(2)}, u32[]{:S(2)}) collective-permute-start(f32[256,384]{1,0:T(8,128)S(1)} %get-tuple-element.74), channel_id=1, source_target_pairs={{0,2},{1,3},{2,0},{3,1},{4,6},{5,7},{6,4},{7,5},{8,10},{9,11},{10,... | collective-permute-start | bytes 1179656 | tf_op jit(solution)/shard_map/ppermute | solution.py:215
  63.1 12.5 %collective-permute-start.16 = (f32[128,384]{1,0:T(8,128)S(1)}, f32[128,384]{1,0:T(8,128)S(1)}, u32[]{:S(2)}, u32[]{:S(2)}) collective-permute-start(f32[128,384]{1,0:T(8,128)S(1)} %get-tuple-element.83), channel_id=1, source_target_pairs={{0,4},{1,5},{2,6},{3,7},{4,0},{5,1},{6,2},{7,3},{8,12},{9,13},{10,... | collective-permute-start | bytes 589832 | tf_op jit(solution)/shard_map/ppermute | solution.py:215
  77.9 6.1 %collective-permute-start.22 = (f32[128,384]{1,0:T(8,128)S(1)}, f32[128,384]{1,0:T(8,128)S(1)}, u32[]{:S(2)}, u32[]{:S(2)}) collective-permute-start(f32[128,384]{1,0:T(8,128)S(1)} %get-tuple-element.82), channel_id=1, source_target_pairs={{0,1},{1,0},{2,3},{3,2},{4,5},{5,4},{6,7},{7,6},{8,9},{9,8},{10,11... | collective-permute-start | bytes 589832 | tf_op jit(solution)/shard_map/ppermute | solution.py:215
  80.9 17.1 %collective-permute-start.20 = (f32[256,384]{1,0:T(8,128)S(1)}, f32[256,384]{1,0:T(8,128)S(1)}, u32[]{:S(2)}, u32[]{:S(2)}) collective-permute-start(f32[256,384]{1,0:T(8,128)S(1)} %get-tuple-element.87), channel_id=1, source_target_pairs={{0,4},{1,5},{2,6},{3,7},{4,0},{5,1},{6,2},{7,3},{8,12},{9,13},{10,... | collective-permute-start | bytes 1179656 | tf_op jit(solution)/shard_map/ppermute | solution.py:215
  82.5 15.6 %collective-permute-start.19 = (f32[256,384]{1,0:T(8,128)S(1)}, f32[256,384]{1,0:T(8,128)S(1)}, u32[]{:S(2)}, u32[]{:S(2)}) collective-permute-start(f32[256,384]{1,0:T(8,128)S(1)} %get-tuple-element.86), channel_id=1, source_target_pairs={{0,2},{1,3},{2,0},{3,1},{4,6},{5,7},{6,4},{7,5},{8,10},{9,11},{10,... | collective-permute-start | bytes 1179656 | tf_op jit(solution)/shard_map/ppermute | solution.py:215
  83.0 14.2 %collective-permute-start.23 = (f32[128,384]{1,0:T(8,128)S(1)}, f32[128,384]{1,0:T(8,128)S(1)}, u32[]{:S(2)}, u32[]{:S(2)}) collective-permute-start(f32[128,384]{1,0:T(8,128)S(1)} %get-tuple-element.94), channel_id=1, source_target_pairs={{0,3},{1,2},{2,1},{3,0},{4,7},{5,6},{6,5},{7,4},{8,11},{9,10},{10,... | collective-permute-start | bytes 589832 | tf_op jit(solution)/shard_map/ppermute | solution.py:215
  84.0 13.1 %collective-permute-start.21 = (f32[128,384]{1,0:T(8,128)S(1)}, f32[128,384]{1,0:T(8,128)S(1)}, u32[]{:S(2)}, u32[]{:S(2)}) collective-permute-start(f32[128,384]{1,0:T(8,128)S(1)} %get-tuple-element.93), channel_id=1, source_target_pairs={{0,4},{1,5},{2,6},{3,7},{4,0},{5,1},{6,2},{7,3},{8,12},{9,13},{10,... | collective-permute-start | bytes 589832 | tf_op jit(solution)/shard_map/ppermute | solution.py:215
  99.5 12.0 %collective-permute-start.26 = (f32[256,384]{1,0:T(8,128)S(1)}, f32[256,384]{1,0:T(8,128)S(1)}, u32[]{:S(2)}, u32[]{:S(2)}) collective-permute-start(f32[256,384]{1,0:T(8,128)S(1)} %get-tuple-element.97), channel_id=1, source_target_pairs={{0,4},{1,5},{2,6},{3,7},{4,0},{5,1},{6,2},{7,3},{8,12},{9,13},{10,... | collective-permute-start | bytes 1179656 | tf_op jit(solution)/shard_map/ppermute | solution.py:215
  100.6 12.0 %collective-permute-start.24 = (f32[256,384]{1,0:T(8,128)S(1)}, f32[256,384]{1,0:T(8,128)S(1)}, u32[]{:S(2)}, u32[]{:S(2)}) collective-permute-start(f32[256,384]{1,0:T(8,128)S(1)} %get-tuple-element.96), channel_id=1, source_target_pairs={{0,2},{1,3},{2,0},{3,1},{4,6},{5,7},{6,4},{7,5},{8,10},{9,11},{10,... | collective-permute-start | bytes 1179656 | tf_op jit(solution)/shard_map/ppermute | solution.py:215
  101.2 11.5 %collective-permute-start.30 = (f32[128,384]{1,0:T(8,128)S(1)}, f32[128,384]{1,0:T(8,128)S(1)}, u32[]{:S(2)}, u32[]{:S(2)}) collective-permute-start(f32[128,384]{1,0:T(8,128)S(1)} %get-tuple-element.92), channel_id=1, source_target_pairs={{0,1},{1,0},{2,3},{3,2},{4,5},{5,4},{6,7},{7,6},{8,9},{9,8},{10,11... | collective-permute-start | bytes 589832 | tf_op jit(solution)/shard_map/ppermute | solution.py:215
  101.2 13.4 %collective-permute-start.31 = (f32[128,384]{1,0:T(8,128)S(1)}, f32[128,384]{1,0:T(8,128)S(1)}, u32[]{:S(2)}, u32[]{:S(2)}) collective-permute-start(f32[128,384]{1,0:T(8,128)S(1)} %get-tuple-element.106), channel_id=1, source_target_pairs={{0,3},{1,2},{2,1},{3,0},{4,7},{5,6},{6,5},{7,4},{8,11},{9,10},{10,... | collective-permute-start | bytes 589832 | tf_op jit(solution)/shard_map/ppermute | solution.py:215
  102.8 12.6 %collective-permute-start.29 = (f32[128,384]{1,0:T(8,128)S(1)}, f32[128,384]{1,0:T(8,128)S(1)}, u32[]{:S(2)}, u32[]{:S(2)}) collective-permute-start(f32[128,384]{1,0:T(8,128)S(1)} %get-tuple-element.105), channel_id=1, source_target_pairs={{0,4},{1,5},{2,6},{3,7},{4,0},{5,1},{6,2},{7,3},{8,12},{9,13},{10,... | collective-permute-start | bytes 589832 | tf_op jit(solution)/shard_map/ppermute | solution.py:215
  111.6 4.6 %collective-permute-start.27 = (f32[128,384]{1,0:T(8,128)S(1)}, f32[128,384]{1,0:T(8,128)S(1)}, u32[]{:S(2)}, u32[]{:S(2)}) collective-permute-start(f32[128,384]{1,0:T(8,128)S(1)} %get-tuple-element.103), channel_id=1, source_target_pairs={{0,1},{1,0},{2,3},{3,2},{4,5},{5,4},{6,7},{7,6},{8,9},{9,8},{10,11... | collective-permute-start | bytes 589832 | tf_op jit(solution)/shard_map/ppermute | solution.py:215
  112.6 7.3 %collective-permute-start.28 = (f32[128,384]{1,0:T(8,128)S(1)}, f32[128,384]{1,0:T(8,128)S(1)}, u32[]{:S(2)}, u32[]{:S(2)}) collective-permute-start(f32[128,384]{1,0:T(8,128)S(1)} %get-tuple-element.104), channel_id=1, source_target_pairs={{0,3},{1,2},{2,1},{3,0},{4,7},{5,6},{6,5},{7,4},{8,11},{9,10},{10,... | collective-permute-start | bytes 589832 | tf_op jit(solution)/shard_map/ppermute | solution.py:215
  112.7 7.5 %collective-permute-start.25 = (f32[128,384]{1,0:T(8,128)S(1)}, f32[128,384]{1,0:T(8,128)S(1)}, u32[]{:S(2)}, u32[]{:S(2)}) collective-permute-start(f32[128,384]{1,0:T(8,128)S(1)} %get-tuple-element.101), channel_id=1, source_target_pairs={{0,4},{1,5},{2,6},{3,7},{4,0},{5,1},{6,2},{7,3},{8,12},{9,13},{10,... | collective-permute-start | bytes 589832 | tf_op jit(solution)/shard_map/ppermute | solution.py:215

commit v18 on v10

--- a/solution.py
+++ b/solution.py
@@ -253,7 +253,7 @@
                 moving[h] = swap(moved, 2 * bit)
                 names[h] = [names[h][i] for i in stays]
         token = held if out is None else [*held, out]
-        settled = moving
+        settled = moving if n == 0 else []
         (theirs,) = fold(rows, [0], [], held[1], moving[1])
         out = write(out, (rows, n_occ * width), d, half, offset, held[0], moving[0], swap(theirs, 1))
     return out

time: 119 us -> 119 us (level)
  Pallas kernels: 20.5 us -> 24.5 us
  waiting for transfers between devices: 60.5 us -> 56.5 us
    pallas_call x23, Pallas kernels: 17.3 us -> 21.4 us  [kernel_call(): pl.pallas_call(body, out_shape=[pltpu.VMEM(shape, jnp.float32) for shape...]
    ppermute x28, waiting for transfers between devices: 54.8 us -> 50.8 us  [swap(): return lax.ppermute(x, 'vir', [(i, i ^ bits) for i in range(n_vir)])]
  transfers between devices with their start and end apart: 32 -> 32, of which waited for: 12 -> 13; matrix products, arithmetic and copies ran while one was open for 1% -> 1% of each run, Pallas kernels for 14% -> 18%
where the time goes in v18:
time: 119 us
  waiting for transfers between devices  56.5 us (47%)
  starting transfers between devices  34.7 us (29%)
  Pallas kernels  24.5 us (21%)
  other arithmetic  1.53 us (1%)
    ppermute x28, waiting for transfers between devices, swap(): return lax.ppermute(x, 'vir', [(i, i ^ bits) for i in range(n_vir)])  50.8 us
    ppermute x28, starting transfers between devices, swap(): return lax.ppermute(x, 'vir', [(i, i ^ bits) for i in range(n_vir)])  24.3 us
    pallas_call x23, Pallas kernels, kernel_call(): pl.pallas_call(body, out_shape=[pltpu.VMEM(shape, jnp.float32) for shape...  21.4 us
    ppermute x1, starting transfers between devices, line_blocks(): far = lax.ppermute(after(own, centre, near), 'occ', [(0, 3), (3, 0)])  5.66 us
    ppermute x1, waiting for transfers between devices, direct(): return lax.ppermute(x, 'occ', [(i, i ^ d) for i in range(nodes)])  5.65 us
    pallas_call x4, Pallas kernels, write(): pl.pallas_call(functools.partial(write_kernel, d, half, offset), out_shap...  3.13 us
    ppermute x1, starting transfers between devices, direct(): return lax.ppermute(x, 'occ', [(i, i ^ d) for i in range(nodes)])  3.01 us
  transfers between devices with their start and end apart: 32, of which 13 were waited for; matrix products, arithmetic and copies ran while one was open for 1% of the time, Pallas kernels for 18%

profile of v18, /device:TPU:0, one launch (start us, length us, event | category | flops | bytes accessed | tf_op | source)
XLA Modules:
  0.0 118.8 jit_solution(14099005257188498004)
XLA Ops:
  0.0 1.3 %halves.1 = (f32[384,384]{1,0:T(8,128)S(1)}, f32[384,384]{1,0:T(8,128)S(1)}) custom-call(s32[3,6]{1,0:T(4,128)} %mask_hbm.1, f32[384,768]{1,0:T(8,128)} %int_hbm.1), custom_call_target="tpu_custom_call" | custom-call | flops 1 | bytes 1 | tf_op jit(solution)/shard_map/halves/pallas_call | solution.py:30
  1.3 0.5 collective-permute-start.5
  1.8 1.4 %cut.1 = (f32[128,768]{1,0:T(8,128)S(1)}, f32[128,768]{1,0:T(8,128)S(1)}, f32[128,768]{1,0:T(8,128)S(1)}, f32[128,768]{1,0:T(8,128)S(1)}) custom-call(s32[4,24]{1,0:T(4,128)} %mask_hbm.2, f32[128,3072]{1,0:T(8,128)} %amp_hbm.1), custom_call_target="tpu_custom_call" | custom-call | flops 1 | bytes 1 | tf_op jit(solution)/shard_map/cut/pallas_call | solution.py:30
  3.3 0.2 collective-permute-done.5.other_ref
  3.5 0.1 join.1.refs_4_
  3.6 3.0 %collective-permute-start.8 = (f32[768,384]{1,0:T(8,128)S(1)}, f32[768,384]{1,0:T(8,128)S(1)}, u32[]{:S(2)}, u32[]{:S(2)}) collective-permute-start(f32[768,384]{1,0:T(8,128)S(1)} %join.1.refs_4_), channel_id=1, source_target_pairs={{0,8},{8,0},{16,24},{24,16},{1,9},{9,1},{17,25},{25,17},{2,10},{10... | collective-permute-start | bytes 3538952 | tf_op jit(solution)/shard_map/ppermute | solution.py:192
  6.6 0.7 collective-permute-start.6
  7.3 1.6 %collective-permute-start = (f32[128,768]{1,0:T(8,128)S(1)}, f32[128,768]{1,0:T(8,128)S(1)}, u32[]{:S(2)}, u32[]{:S(2)}) collective-permute-start(f32[128,768]{1,0:T(8,128)S(1)} %get-tuple-element.59), channel_id=1, source_target_pairs={{0,4},{1,5},{2,6},{3,7},{4,0},{5,1},{6,2},{7,3},{8,12},{9,13},{10,... | collective-permute-start | bytes 1179656 | tf_op jit(solution)/shard_map/ppermute | solution.py:212
  8.9 1.4 %collective-permute-start.1 = (f32[128,768]{1,0:T(8,128)S(1)}, f32[128,768]{1,0:T(8,128)S(1)}, u32[]{:S(2)}, u32[]{:S(2)}) collective-permute-start(f32[128,768]{1,0:T(8,128)S(1)} %get-tuple-element.60), channel_id=1, source_target_pairs={{0,6},{1,7},{2,4},{3,5},{4,2},{5,3},{6,0},{7,1},{8,14},{9,15},{10,... | collective-permute-start | bytes 1179656 | tf_op jit(solution)/shard_map/ppermute | solution.py:212
  10.3 0.5 collective-permute-start.3
  10.9 15.8 %collective-permute-done.refs_1_ = f32[128,768]{1,0:T(8,128)S(1)} collective-permute-done((f32[128,768]{1,0:T(8,128)S(1)}, f32[128,768]{1,0:T(8,128)S(1)}, u32[]{:S(2)}, u32[]{:S(2)}) %collective-permute-start) | collective-permute-done | bytes 393248 | tf_op jit(solution)/shard_map/ppermute | solution.py:212
  26.7 0.0 collective-permute-start.10
  26.7 0.5 collective-permute-start.11
  27.2 5.7 %collective-permute-done.8.refs_4_ = f32[768,384]{1,0:T(8,128)S(1)} collective-permute-done((f32[768,384]{1,0:T(8,128)S(1)}, f32[768,384]{1,0:T(8,128)S(1)}, u32[]{:S(2)}, u32[]{:S(2)}) %collective-permute-start.8) | collective-permute-done | bytes 1179680 | tf_op jit(solution)/shard_map/ppermute | solution.py:192
  32.8 1.0 copy-done.2
  33.9 5.7 %collective-permute-start.9 = (f32[768,384]{1,0:T(8,128)S(1)}, f32[768,384]{1,0:T(8,128)}, u32[]{:S(2)}, u32[]{:S(2)}) collective-permute-start(f32[768,384]{1,0:T(8,128)S(1)} %join.1.refs_4_), channel_id=1, source_target_pairs={{0,24},{24,0},{1,25},{25,1},{2,26},{26,2},{3,27},{27,3},{4,28},{28... | collective-permute-start | bytes 3538952 | tf_op jit(solution)/shard_map/ppermute | solution.py:198
  39.6 0.1 collective-permute-start.2
  39.7 0.5 collective-permute-start.4
  40.2 2.1 %products.8 = (f32[256,384]{1,0:T(8,128)}, f32[256,384]{1,0:T(8,128)}) custom-call(f32[128,768]{1,0:T(8,128)S(1)} %collective-permute-done.3.refs_0_, f32[128,768]{1,0:T(8,128)S(1)} %collective-permute-done.1.refs_1_, f32[128,768]{1,0:T(8,128)S(1)} %collective-permute-done.10.refs_2_, f32[128,768]{1,0:T(8,128)S(1)} %collective-permute-done.11.refs_3_, ...), custom_call_target="tpu_custom_call" | custom-call | flops 1 | bytes 1 | tf_op jit(solution)/shard_map/products/pallas_call | solution.py:30
  42.3 1.5 %collective-permute-start.13 = (f32[256,384]{1,0:T(8,128)}, f32[256,384]{1,0:T(8,128)}, u32[]{:S(2)}, u32[]{:S(2)}) collective-permute-start(f32[256,384]{1,0:T(8,128)} %get-tuple-element.67), channel_id=1, source_target_pairs={{0,4},{1,5},{2,6},{3,7},{4,0},{5,1},{6,2},{7,3},{8,12},{9,13},{10,... | collective-permute-start | bytes 1179656 | tf_op jit(solution)/shard_map/ppermute | solution.py:212
  43.8 1.5 %collective-permute-start.12 = (f32[256,384]{1,0:T(8,128)}, f32[256,384]{1,0:T(8,128)}, u32[]{:S(2)}, u32[]{:S(2)}) collective-permute-start(f32[256,384]{1,0:T(8,128)} %get-tuple-element.66), channel_id=1, source_target_pairs={{0,2},{1,3},{2,0},{3,1},{4,6},{5,7},{6,4},{7,5},{8,10},{9,11},{10,... | collective-permute-start | bytes 1179656 | tf_op jit(solution)/shard_map/ppermute | solution.py:212
  45.3 2.5 %products.9 = (f32[256,384]{1,0:T(8,128)S(1)}, f32[256,384]{1,0:T(8,128)S(1)}) custom-call(f32[128,768]{1,0:T(8,128)S(1)} %get-tuple-element.61.refs_0_, f32[128,768]{1,0:T(8,128)S(1)} %collective-permute-done.refs_1_, f32[128,768]{1,0:T(8,128)S(1)} %collective-permute-done.2.refs_2_, f32[128,768]{1,0:T(8,128)} %collective-permute-done.4.refs_3_, ...), custom_call_target="tpu_custom_call" | custom-call | flops 1 | bytes 1 | tf_op jit(solution)/shard_map/products/pallas_call | solution.py:30
  47.8 5.9 %collective-permute-done.13.got_ref = f32[256,384]{1,0:T(8,128)} collective-permute-done((f32[256,384]{1,0:T(8,128)}, f32[256,384]{1,0:T(8,128)}, u32[]{:S(2)}, u32[]{:S(2)}) %collective-permute-start.13) | collective-permute-done | bytes 393248 | tf_op jit(solution)/shard_map/ppermute | solution.py:212
  53.7 1.0 fold.13
  54.8 1.6 %collective-permute-start.15 = (f32[128,384]{1,0:T(8,128)S(1)}, f32[128,384]{1,0:T(8,128)S(1)}, u32[]{:S(2)}, u32[]{:S(2)}) collective-permute-start(f32[128,384]{1,0:T(8,128)S(1)} %get-tuple-element.79), channel_id=1, source_target_pairs={{0,2},{1,3},{2,0},{3,1},{4,6},{5,7},{6,4},{7,5},{8,10},{9,11},{10,... | collective-permute-start | bytes 589832 | tf_op jit(solution)/shard_map/ppermute | solution.py:212
  56.3 0.1 broadcast_select_fusion.1
  56.5 1.1 collective-permute-start.7
  57.5 1.1 fold.12
  58.6 1.6 %collective-permute-start.14 = (f32[128,384]{1,0:T(8,128)S(1)}, f32[128,384]{1,0:T(8,128)S(1)}, u32[]{:S(2)}, u32[]{:S(2)}) collective-permute-start(f32[128,384]{1,0:T(8,128)S(1)} %get-tuple-element.78), channel_id=1, source_target_pairs={{0,4},{1,5},{2,6},{3,7},{4,0},{5,1},{6,2},{7,3},{8,12},{9,13},{10,... | collective-permute-start | bytes 589832 | tf_op jit(solution)/shard_map/ppermute | solution.py:212
  60.2 1.4 %products.10 = (f32[256,384]{1,0:T(8,128)S(1)}, f32[256,384]{1,0:T(8,128)S(1)}) custom-call(f32[128,768]{1,0:T(8,128)S(1)} %collective-permute-done.3.refs_0_, f32[128,768]{1,0:T(8,128)S(1)} %collective-permute-done.1.refs_1_, f32[128,768]{1,0:T(8,128)S(1)} %collective-permute-done.10.refs_2_, f32[128,768]{1,0:T(8,128)S(1)} %copy-done.1, ...), custom_call_target="tpu_custom_call" | custom-call | flops 1 | bytes 1 | tf_op jit(solution)/shard_map/products/pallas_call | solution.py:30
  61.6 0.6 collective-permute-start.17
  62.2 0.5 collective-permute-start.16
  62.7 3.4 %collective-permute-done.14.got_ref = f32[128,384]{1,0:T(8,128)S(1)} collective-permute-done((f32[128,384]{1,0:T(8,128)S(1)}, f32[128,384]{1,0:T(8,128)S(1)}, u32[]{:S(2)}, u32[]{:S(2)}) %collective-permute-start.14) | collective-permute-done | bytes 196640 | tf_op jit(solution)/shard_map/ppermute | solution.py:212
  66.1 1.4 %collective-permute-done.18.other_ref = f32[128,384]{1,0:T(8,128)S(1)} collective-permute-done((f32[128,384]{1,0:T(8,128)S(1)}, f32[128,384]{1,0:T(8,128)S(1)}, u32[]{:S(2)}, u32[]{:S(2)}) %collective-permute-start.18) | collective-permute-done | bytes 196640 | tf_op jit(solution)/shard_map/ppermute | solution.py:212
  67.6 0.8 write.4.refs_0_
  68.4 2.4 %products.11 = (f32[256,384]{1,0:T(8,128)S(1)}, f32[256,384]{1,0:T(8,128)S(1)}) custom-call(f32[128,768]{1,0:T(8,128)S(1)} %get-tuple-element.61.refs_0_, f32[128,768]{1,0:T(8,128)S(1)} %collective-permute-done.refs_1_, f32[128,768]{1,0:T(8,128)S(1)} %collective-permute-done.2.refs_2_, f32[128,768]{1,0:T(8,128)} %collective-permute-done.4.refs_3_, ...), custom_call_target="tpu_custom_call" | custom-call | flops 1 | bytes 1 | tf_op jit(solution)/shard_map/products/pallas_call | solution.py:30
  70.8 2.0 %collective-permute-done.17.got_ref = f32[256,384]{1,0:T(8,128)S(1)} collective-permute-done((f32[256,384]{1,0:T(8,128)S(1)}, f32[256,384]{1,0:T(8,128)S(1)}, u32[]{:S(2)}, u32[]{:S(2)}) %collective-permute-start.17) | collective-permute-done | bytes 393248 | tf_op jit(solution)/shard_map/ppermute | solution.py:212
  72.8 0.6 collective-permute-start.22
  73.5 1.4 %broadcast_select_fusion.refs_4_ = f32[768,384]{1,0:T(8,128)S(1)} fusion(f32[768,384]{1,0:T(8,128)S(1)} %copy-done.5, f32[768,384]{1,0:T(8,128)} %collective-permute-done.9, pred[]{:T(512)S(6)} %or.3), kind=kLoop, calls=%fused_computation | loop fusion | flops 294912 | bytes 3538945 | tf_op jit(solution)/shard_map/jit(_where)/select_n | solution.py:240
  74.9 1.4 %products.12 = (f32[256,384]{1,0:T(8,128)S(1)}, f32[256,384]{1,0:T(8,128)S(1)}) custom-call(f32[128,768]{1,0:T(8,128)S(1)} %collective-permute-done.3.refs_0_, f32[128,768]{1,0:T(8,128)S(1)} %collective-permute-done.1.refs_1_, f32[128,768]{1,0:T(8,128)S(1)} %collective-permute-done.10.refs_2_, f32[128,768]{1,0:T(8,128)S(1)} %copy-done.1, ...), custom_call_target="tpu_custom_call" | custom-call | flops 1 | bytes 1 | tf_op jit(solution)/shard_map/products/pallas_call | solution.py:30
  76.3 1.6 %collective-permute-start.19 = (f32[256,384]{1,0:T(8,128)S(1)}, f32[256,384]{1,0:T(8,128)S(1)}, u32[]{:S(2)}, u32[]{:S(2)}) collective-permute-start(f32[256,384]{1,0:T(8,128)S(1)} %get-tuple-element.86), channel_id=1, source_target_pairs={{0,2},{1,3},{2,0},{3,1},{4,6},{5,7},{6,4},{7,5},{8,10},{9,11},{10,... | collective-permute-start | bytes 1179656 | tf_op jit(solution)/shard_map/ppermute | solution.py:212
  77.8 1.3 %collective-permute-start.20 = (f32[256,384]{1,0:T(8,128)S(1)}, f32[256,384]{1,0:T(8,128)S(1)}, u32[]{:S(2)}, u32[]{:S(2)}) collective-permute-start(f32[256,384]{1,0:T(8,128)S(1)} %get-tuple-element.87), channel_id=1, source_target_pairs={{0,4},{1,5},{2,6},{3,7},{4,0},{5,1},{6,2},{7,3},{8,12},{9,13},{10,... | collective-permute-start | bytes 1179656 | tf_op jit(solution)/shard_map/ppermute | solution.py:212
  79.1 0.7 collective-permute-start.21
  79.9 0.3 collective-permute-done.22.got_ref
  80.2 0.1 collective-permute-start.23
  80.3 2.4 %products.13 = (f32[256,384]{1,0:T(8,128)S(1)}, f32[256,384]{1,0:T(8,128)S(1)}) custom-call(f32[128,768]{1,0:T(8,128)S(1)} %get-tuple-element.61.refs_0_, f32[128,768]{1,0:T(8,128)S(1)} %collective-permute-done.refs_1_, f32[128,768]{1,0:T(8,128)S(1)} %collective-permute-done.2.refs_2_, f32[128,768]{1,0:T(8,128)} %collective-permute-done.4.refs_3_, ...), custom_call_target="tpu_custom_call" | custom-call | flops 1 | bytes 1 | tf_op jit(solution)/shard_map/products/pallas_call | solution.py:30
  82.7 8.1 %collective-permute-done.21.got_ref = f32[128,384]{1,0:T(8,128)S(1)} collective-permute-done((f32[128,384]{1,0:T(8,128)S(1)}, f32[128,384]{1,0:T(8,128)S(1)}, u32[]{:S(2)}, u32[]{:S(2)}) %collective-permute-start.21) | collective-permute-done | bytes 196640 | tf_op jit(solution)/shard_map/ppermute | solution.py:212
  90.8 0.8 write.5.refs_0_
  91.8 1.4 %products.14 = (f32[256,384]{1,0:T(8,128)S(1)}, f32[256,384]{1,0:T(8,128)S(1)}) custom-call(f32[128,768]{1,0:T(8,128)S(1)} %collective-permute-done.3.refs_0_, f32[128,768]{1,0:T(8,128)S(1)} %collective-permute-done.1.refs_1_, f32[128,768]{1,0:T(8,128)S(1)} %collective-permute-done.10.refs_2_, f32[128,768]{1,0:T(8,128)S(1)} %copy-done.1, ...), custom_call_target="tpu_custom_call" | custom-call | flops 1 | bytes 1 | tf_op jit(solution)/shard_map/products/pallas_call | solution.py:30
  93.2 1.8 %collective-permute-start.26 = (f32[256,384]{1,0:T(8,128)S(1)}, f32[256,384]{1,0:T(8,128)S(1)}, u32[]{:S(2)}, u32[]{:S(2)}) collective-permute-start(f32[256,384]{1,0:T(8,128)S(1)} %get-tuple-element.97), channel_id=1, source_target_pairs={{0,4},{1,5},{2,6},{3,7},{4,0},{5,1},{6,2},{7,3},{8,12},{9,13},{10,... | collective-permute-start | bytes 1179656 | tf_op jit(solution)/shard_map/ppermute | solution.py:212
  95.0 0.5 collective-permute-start.24
  95.5 1.5 %collective-permute-start.30 = (f32[128,384]{1,0:T(8,128)S(1)}, f32[128,384]{1,0:T(8,128)S(1)}, u32[]{:S(2)}, u32[]{:S(2)}) collective-permute-start(f32[128,384]{1,0:T(8,128)S(1)} %get-tuple-element.106), channel_id=1, source_target_pairs={{0,2},{1,3},{2,0},{3,1},{4,6},{5,7},{6,4},{7,5},{8,10},{9,11},{10,... | collective-permute-start | bytes 589832 | tf_op jit(solution)/shard_map/ppermute | solution.py:212
  97.0 2.4 %products.15 = (f32[256,384]{1,0:T(8,128)S(1)}, f32[256,384]{1,0:T(8,128)S(1)}) custom-call(f32[128,768]{1,0:T(8,128)S(1)} %get-tuple-element.61.refs_0_, f32[128,768]{1,0:T(8,128)S(1)} %collective-permute-done.refs_1_, f32[128,768]{1,0:T(8,128)S(1)} %collective-permute-done.2.refs_2_, f32[128,768]{1,0:T(8,128)} %collective-permute-done.4.refs_3_, ...), custom_call_target="tpu_custom_call" | custom-call | flops 1 | bytes 1 | tf_op jit(solution)/shard_map/products/pallas_call | solution.py:30
  99.5 3.4 %collective-permute-done.26.got_ref = f32[256,384]{1,0:T(8,128)S(1)} collective-permute-done((f32[256,384]{1,0:T(8,128)S(1)}, f32[256,384]{1,0:T(8,128)S(1)}, u32[]{:S(2)}, u32[]{:S(2)}) %collective-permute-start.26) | collective-permute-done | bytes 393248 | tf_op jit(solution)/shard_map/ppermute | solution.py:212
  102.9 1.5 %collective-permute-start.27 = (f32[128,384]{1,0:T(8,128)S(1)}, f32[128,384]{1,0:T(8,128)S(1)}, u32[]{:S(2)}, u32[]{:S(2)}) collective-permute-start(f32[128,384]{1,0:T(8,128)S(1)} %get-tuple-element.104), channel_id=1, source_target_pairs={{0,2},{1,3},{2,0},{3,1},{4,6},{5,7},{6,4},{7,5},{8,10},{9,11},{10,... | collective-permute-start | bytes 589832 | tf_op jit(solution)/shard_map/ppermute | solution.py:212
  104.4 1.5 %collective-permute-start.29 = (f32[128,384]{1,0:T(8,128)S(1)}, f32[128,384]{1,0:T(8,128)S(1)}, u32[]{:S(2)}, u32[]{:S(2)}) collective-permute-start(f32[128,384]{1,0:T(8,128)S(1)} %get-tuple-element.105), channel_id=1, source_target_pairs={{0,4},{1,5},{2,6},{3,7},{4,0},{5,1},{6,2},{7,3},{8,12},{9,13},{10,... | collective-permute-start | bytes 589832 | tf_op jit(solution)/shard_map/ppermute | solution.py:212
  105.9 4.4 %collective-permute-done.30.got_ref = f32[128,384]{1,0:T(8,128)S(1)} collective-permute-done((f32[128,384]{1,0:T(8,128)S(1)}, f32[128,384]{1,0:T(8,128)S(1)}, u32[]{:S(2)}, u32[]{:S(2)}) %collective-permute-start.30) | collective-permute-done | bytes 196640 | tf_op jit(solution)/shard_map/ppermute | solution.py:212
  110.4 0.1 collective-permute-start.31
  110.5 0.7 collective-permute-start.25
  111.2 1.3 %collective-permute-done.27.got_ref = f32[128,384]{1,0:T(8,128)S(1)} collective-permute-done((f32[128,384]{1,0:T(8,128)S(1)}, f32[128,384]{1,0:T(8,128)S(1)}, u32[]{:S(2)}, u32[]{:S(2)}) %collective-permute-start.27) | collective-permute-done | bytes 196640 | tf_op jit(solution)/shard_map/ppermute | solution.py:212
  112.5 0.1 collective-permute-start.28
  112.6 0.8 write.6.refs_0_
  113.4 4.5 %collective-permute-done.25.got_ref = f32[128,384]{1,0:T(8,128)S(1)} collective-permute-done((f32[128,384]{1,0:T(8,128)S(1)}, f32[128,384]{1,0:T(8,128)S(1)}, u32[]{:S(2)}, u32[]{:S(2)}) %collective-permute-start.25) | collective-permute-done | bytes 196640 | tf_op jit(solution)/shard_map/ppermute | solution.py:212
  117.9 0.8 write.7
  (41 shorter events, 0.4 us)
Async XLA Ops:
  1.3 2.1 %collective-permute-start.5 = (f32[384,384]{1,0:T(8,128)S(1)}, f32[384,384]{1,0:T(8,128)S(1)}, u32[]{:S(2)}, u32[]{:S(2)}) collective-permute-start(f32[384,384]{1,0:T(8,128)S(1)} %get-tuple-element.63), channel_id=1, source_target_pairs={{0,1},{1,0},{2,3},{3,2},{4,5},{5,4},{6,7},{7,6},{8,9},{9,8},{10,11... | collective-permute-start | bytes 1769480 | tf_op jit(solution)/shard_map/ppermute | solution.py:212
  3.6 29.3 %collective-permute-start.8 = (f32[768,384]{1,0:T(8,128)S(1)}, f32[768,384]{1,0:T(8,128)S(1)}, u32[]{:S(2)}, u32[]{:S(2)}) collective-permute-start(f32[768,384]{1,0:T(8,128)S(1)} %join.1.refs_4_), channel_id=1, source_target_pairs={{0,8},{8,0},{16,24},{24,16},{1,9},{9,1},{17,25},{25,17},{2,10},{10... | collective-permute-start | bytes 3538952 | tf_op jit(solution)/shard_map/ppermute | solution.py:192
  6.6 27.3 %collective-permute-start.6 = (f32[768,384]{1,0:T(8,128)S(1)}, f32[768,384]{1,0:T(8,128)S(1)}, u32[]{:S(2)}, u32[]{:S(2)}) collective-permute-start(f32[768,384]{1,0:T(8,128)S(1)} %join.1.refs_4_), channel_id=1, source_target_pairs={{8,16},{16,8},{9,17},{17,9},{10,18},{18,10},{11,19},{19,11},{12,20... | collective-permute-start | bytes 3538952 | tf_op jit(solution)/shard_map/ppermute | solution.py:196
  7.3 19.4 %collective-permute-start = (f32[128,768]{1,0:T(8,128)S(1)}, f32[128,768]{1,0:T(8,128)S(1)}, u32[]{:S(2)}, u32[]{:S(2)}) collective-permute-start(f32[128,768]{1,0:T(8,128)S(1)} %get-tuple-element.59), channel_id=1, source_target_pairs={{0,4},{1,5},{2,6},{3,7},{4,0},{5,1},{6,2},{7,3},{8,12},{9,13},{10,... | collective-permute-start | bytes 1179656 | tf_op jit(solution)/shard_map/ppermute | solution.py:212
  8.9 17.8 %collective-permute-start.1 = (f32[128,768]{1,0:T(8,128)S(1)}, f32[128,768]{1,0:T(8,128)S(1)}, u32[]{:S(2)}, u32[]{:S(2)}) collective-permute-start(f32[128,768]{1,0:T(8,128)S(1)} %get-tuple-element.60), channel_id=1, source_target_pairs={{0,6},{1,7},{2,4},{3,5},{4,2},{5,3},{6,0},{7,1},{8,14},{9,15},{10,... | collective-permute-start | bytes 1179656 | tf_op jit(solution)/shard_map/ppermute | solution.py:212
  10.3 29.3 %collective-permute-start.3 = (f32[128,768]{1,0:T(8,128)S(1)}, f32[128,768]{1,0:T(8,128)S(1)}, u32[]{:S(2)}, u32[]{:S(2)}) collective-permute-start(f32[128,768]{1,0:T(8,128)S(1)} %get-tuple-element.62), channel_id=1, source_target_pairs={{0,2},{1,3},{2,0},{3,1},{4,6},{5,7},{6,4},{7,5},{8,10},{9,11},{10,... | collective-permute-start | bytes 1179656 | tf_op jit(solution)/shard_map/ppermute | solution.py:212
  26.7 13.5 %collective-permute-start.10 = (f32[128,768]{1,0:T(8,128)S(1)}, f32[128,768]{1,0:T(8,128)S(1)}, u32[]{:S(2)}, u32[]{:S(2)}) collective-permute-start(f32[128,768]{1,0:T(8,128)S(1)} %collective-permute-done.refs_1_), channel_id=1, source_target_pairs={{0,1},{1,0},{2,3},{3,2},{4,5},{5,4},{6,7},{7,6},{8,9},{9,8},{10,11... | collective-permute-start | bytes 1179656 | tf_op jit(solution)/shard_map/ppermute | solution.py:212
  26.7 13.5 %collective-permute-start.11 = (f32[128,768]{1,0:T(8,128)S(1)}, f32[128,768]{1,0:T(8,128)S(1)}, u32[]{:S(2)}, u32[]{:S(2)}) collective-permute-start(f32[128,768]{1,0:T(8,128)S(1)} %collective-permute-done.1.refs_1_), channel_id=1, source_target_pairs={{0,1},{1,0},{2,3},{3,2},{4,5},{5,4},{6,7},{7,6},{8,9},{9,8},{10,11... | collective-permute-start | bytes 1179656 | tf_op jit(solution)/shard_map/ppermute | solution.py:212
  32.8 1.0 copy-start.2
  33.9 6.3 %copy-start.4 = (f32[768,384]{1,0:T(8,128)}, f32[768,384]{1,0:T(8,128)S(1)}, u32[]{:S(2)}) copy-start(f32[768,384]{1,0:T(8,128)S(1)} %collective-permute-done.6) | copy-start | bytes 3538948
  33.9 39.6 %collective-permute-start.9 = (f32[768,384]{1,0:T(8,128)S(1)}, f32[768,384]{1,0:T(8,128)}, u32[]{:S(2)}, u32[]{:S(2)}) collective-permute-start(f32[768,384]{1,0:T(8,128)S(1)} %join.1.refs_4_), channel_id=1, source_target_pairs={{0,24},{24,0},{1,25},{25,1},{2,26},{26,2},{3,27},{27,3},{4,28},{28... | collective-permute-start | bytes 3538952 | tf_op jit(solution)/shard_map/ppermute | solution.py:198
  39.6 5.8 %collective-permute-start.2 = (f32[128,768]{1,0:T(8,128)S(1)}, f32[128,768]{1,0:T(8,128)S(1)}, u32[]{:S(2)}, u32[]{:S(2)}) collective-permute-start(f32[128,768]{1,0:T(8,128)S(1)} %get-tuple-element.61.refs_0_), channel_id=1, source_target_pairs={{0,1},{1,0},{2,3},{3,2},{4,5},{5,4},{6,7},{7,6},{8,9},{9,8},{10,11... | collective-permute-start | bytes 1179656 | tf_op jit(solution)/shard_map/ppermute | solution.py:212
  39.7 5.7 %collective-permute-start.4 = (f32[128,768]{1,0:T(8,128)S(1)}, f32[128,768]{1,0:T(8,128)}, u32[]{:S(2)}, u32[]{:S(2)}) collective-permute-start(f32[128,768]{1,0:T(8,128)S(1)} %collective-permute-done.3.refs_0_), channel_id=1, source_target_pairs={{0,1},{1,0},{2,3},{3,2},{4,5},{5,4},{6,7},{7,6},{8,9},{9,8},{10,11... | collective-permute-start | bytes 1179656 | tf_op jit(solution)/shard_map/ppermute | solution.py:212
  40.2 2.2 %copy-start = (f32[128,768]{1,0:T(8,128)}, f32[128,768]{1,0:T(8,128)S(1)}, u32[]{:S(2)}) copy-start(f32[128,768]{1,0:T(8,128)S(1)} %collective-permute-done.11.refs_3_) | copy-start | bytes 1179652
  42.3 11.4 %collective-permute-start.13 = (f32[256,384]{1,0:T(8,128)}, f32[256,384]{1,0:T(8,128)}, u32[]{:S(2)}, u32[]{:S(2)}) collective-permute-start(f32[256,384]{1,0:T(8,128)} %get-tuple-element.67), channel_id=1, source_target_pairs={{0,4},{1,5},{2,6},{3,7},{4,0},{5,1},{6,2},{7,3},{8,12},{9,13},{10,... | collective-permute-start | bytes 1179656 | tf_op jit(solution)/shard_map/ppermute | solution.py:212
  43.8 13.7 %collective-permute-start.12 = (f32[256,384]{1,0:T(8,128)}, f32[256,384]{1,0:T(8,128)}, u32[]{:S(2)}, u32[]{:S(2)}) collective-permute-start(f32[256,384]{1,0:T(8,128)} %get-tuple-element.66), channel_id=1, source_target_pairs={{0,2},{1,3},{2,0},{3,1},{4,6},{5,7},{6,4},{7,5},{8,10},{9,11},{10,... | collective-permute-start | bytes 1179656 | tf_op jit(solution)/shard_map/ppermute | solution.py:212
  45.3 11.0 %copy-start.5 = (f32[768,384]{1,0:T(8,128)S(1)}, f32[768,384]{1,0:T(8,128)}, u32[]{:S(2)}) copy-start(f32[768,384]{1,0:T(8,128)} %copy-done.4) | copy-start | bytes 3538948
  54.8 5.4 %copy-start.1 = (f32[128,768]{1,0:T(8,128)S(1)}, f32[128,768]{1,0:T(8,128)}, u32[]{:S(2)}) copy-start(f32[128,768]{1,0:T(8,128)} %copy-done) | copy-start | bytes 1179652
  54.8 7.4 %collective-permute-start.15 = (f32[128,384]{1,0:T(8,128)S(1)}, f32[128,384]{1,0:T(8,128)S(1)}, u32[]{:S(2)}, u32[]{:S(2)}) collective-permute-start(f32[128,384]{1,0:T(8,128)S(1)} %get-tuple-element.79), channel_id=1, source_target_pairs={{0,2},{1,3},{2,0},{3,1},{4,6},{5,7},{6,4},{7,5},{8,10},{9,11},{10,... | collective-permute-start | bytes 589832 | tf_op jit(solution)/shard_map/ppermute | solution.py:212
  56.3 3.8 %copy-start.3 = (f32[768,384]{1,0:T(8,128)S(1)}, f32[768,384]{1,0:T(8,128)}, u32[]{:S(2)}) copy-start(f32[768,384]{1,0:T(8,128)} %copy-done.2) | copy-start | bytes 3538948
  56.5 35.3 %collective-permute-start.7 = (f32[768,384]{1,0:T(8,128)S(1)}, f32[768,384]{1,0:T(8,128)S(1)}, u32[]{:S(2)}, u32[]{:S(2)}) collective-permute-start(f32[768,384]{1,0:T(8,128)S(1)} %broadcast_select_fusion.1), channel_id=1, source_target_pairs={{8,0},{16,24},{0,16},{24,8},{9,1},{17,25},{1,17},{25,9},{10,2},{18... | collective-permute-start | bytes 3538952 | tf_op jit(solution)/shard_map/ppermute | solution.py:200
  58.6 7.5 %collective-permute-start.14 = (f32[128,384]{1,0:T(8,128)S(1)}, f32[128,384]{1,0:T(8,128)S(1)}, u32[]{:S(2)}, u32[]{:S(2)}) collective-permute-start(f32[128,384]{1,0:T(8,128)S(1)} %get-tuple-element.78), channel_id=1, source_target_pairs={{0,4},{1,5},{2,6},{3,7},{4,0},{5,1},{6,2},{7,3},{8,12},{9,13},{10,... | collective-permute-start | bytes 589832 | tf_op jit(solution)/shard_map/ppermute | solution.py:212
  61.6 11.1 %collective-permute-start.17 = (f32[256,384]{1,0:T(8,128)S(1)}, f32[256,384]{1,0:T(8,128)S(1)}, u32[]{:S(2)}, u32[]{:S(2)}) collective-permute-start(f32[256,384]{1,0:T(8,128)S(1)} %get-tuple-element.75), channel_id=1, source_target_pairs={{0,4},{1,5},{2,6},{3,7},{4,0},{5,1},{6,2},{7,3},{8,12},{9,13},{10,... | collective-permute-start | bytes 1179656 | tf_op jit(solution)/shard_map/ppermute | solution.py:212
  62.2 11.2 %collective-permute-start.16 = (f32[256,384]{1,0:T(8,128)S(1)}, f32[256,384]{1,0:T(8,128)S(1)}, u32[]{:S(2)}, u32[]{:S(2)}) collective-permute-start(f32[256,384]{1,0:T(8,128)S(1)} %get-tuple-element.74), channel_id=1, source_target_pairs={{0,2},{1,3},{2,0},{3,1},{4,6},{5,7},{6,4},{7,5},{8,10},{9,11},{10,... | collective-permute-start | bytes 1179656 | tf_op jit(solution)/shard_map/ppermute | solution.py:212
  66.1 1.4 %collective-permute-start.18 = (f32[128,384]{1,0:T(8,128)S(1)}, f32[128,384]{1,0:T(8,128)S(1)}, u32[]{:S(2)}, u32[]{:S(2)}) collective-permute-start(f32[128,384]{1,0:T(8,128)S(1)} %fold.16), channel_id=1, source_target_pairs={{0,1},{1,0},{2,3},{3,2},{4,5},{5,4},{6,7},{7,6},{8,9},{9,8},{10,11... | collective-permute-start | bytes 589832 | tf_op jit(solution)/shard_map/ppermute | solution.py:212
  72.8 7.4 %collective-permute-start.22 = (f32[128,384]{1,0:T(8,128)S(1)}, f32[128,384]{1,0:T(8,128)S(1)}, u32[]{:S(2)}, u32[]{:S(2)}) collective-permute-start(f32[128,384]{1,0:T(8,128)S(1)} %get-tuple-element.94), channel_id=1, source_target_pairs={{0,2},{1,3},{2,0},{3,1},{4,6},{5,7},{6,4},{7,5},{8,10},{9,11},{10,... | collective-permute-start | bytes 589832 | tf_op jit(solution)/shard_map/ppermute | solution.py:212
  76.3 15.4 %collective-permute-start.19 = (f32[256,384]{1,0:T(8,128)S(1)}, f32[256,384]{1,0:T(8,128)S(1)}, u32[]{:S(2)}, u32[]{:S(2)}) collective-permute-start(f32[256,384]{1,0:T(8,128)S(1)} %get-tuple-element.86), channel_id=1, source_target_pairs={{0,2},{1,3},{2,0},{3,1},{4,6},{5,7},{6,4},{7,5},{8,10},{9,11},{10,... | collective-permute-start | bytes 1179656 | tf_op jit(solution)/shard_map/ppermute | solution.py:212
  77.8 13.9 %collective-permute-start.20 = (f32[256,384]{1,0:T(8,128)S(1)}, f32[256,384]{1,0:T(8,128)S(1)}, u32[]{:S(2)}, u32[]{:S(2)}) collective-permute-start(f32[256,384]{1,0:T(8,128)S(1)} %get-tuple-element.87), channel_id=1, source_target_pairs={{0,4},{1,5},{2,6},{3,7},{4,0},{5,1},{6,2},{7,3},{8,12},{9,13},{10,... | collective-permute-start | bytes 1179656 | tf_op jit(solution)/shard_map/ppermute | solution.py:212
  79.1 11.7 %collective-permute-start.21 = (f32[128,384]{1,0:T(8,128)S(1)}, f32[128,384]{1,0:T(8,128)S(1)}, u32[]{:S(2)}, u32[]{:S(2)}) collective-permute-start(f32[128,384]{1,0:T(8,128)S(1)} %get-tuple-element.93), channel_id=1, source_target_pairs={{0,4},{1,5},{2,6},{3,7},{4,0},{5,1},{6,2},{7,3},{8,12},{9,13},{10,... | collective-permute-start | bytes 589832 | tf_op jit(solution)/shard_map/ppermute | solution.py:212
  80.2 10.7 %collective-permute-start.23 = (f32[128,384]{1,0:T(8,128)S(1)}, f32[128,384]{1,0:T(8,128)S(1)}, u32[]{:S(2)}, u32[]{:S(2)}) collective-permute-start(f32[128,384]{1,0:T(8,128)S(1)} %fold.19), channel_id=1, source_target_pairs={{0,1},{1,0},{2,3},{3,2},{4,5},{5,4},{6,7},{7,6},{8,9},{9,8},{10,11... | collective-permute-start | bytes 589832 | tf_op jit(solution)/shard_map/ppermute | solution.py:212
  93.2 9.7 %collective-permute-start.26 = (f32[256,384]{1,0:T(8,128)S(1)}, f32[256,384]{1,0:T(8,128)S(1)}, u32[]{:S(2)}, u32[]{:S(2)}) collective-permute-start(f32[256,384]{1,0:T(8,128)S(1)} %get-tuple-element.97), channel_id=1, source_target_pairs={{0,4},{1,5},{2,6},{3,7},{4,0},{5,1},{6,2},{7,3},{8,12},{9,13},{10,... | collective-permute-start | bytes 1179656 | tf_op jit(solution)/shard_map/ppermute | solution.py:212
  95.0 15.4 %collective-permute-start.24 = (f32[256,384]{1,0:T(8,128)S(1)}, f32[256,384]{1,0:T(8,128)S(1)}, u32[]{:S(2)}, u32[]{:S(2)}) collective-permute-start(f32[256,384]{1,0:T(8,128)S(1)} %get-tuple-element.96), channel_id=1, source_target_pairs={{0,2},{1,3},{2,0},{3,1},{4,6},{5,7},{6,4},{7,5},{8,10},{9,11},{10,... | collective-permute-start | bytes 1179656 | tf_op jit(solution)/shard_map/ppermute | solution.py:212
  95.5 14.8 %collective-permute-start.30 = (f32[128,384]{1,0:T(8,128)S(1)}, f32[128,384]{1,0:T(8,128)S(1)}, u32[]{:S(2)}, u32[]{:S(2)}) collective-permute-start(f32[128,384]{1,0:T(8,128)S(1)} %get-tuple-element.106), channel_id=1, source_target_pairs={{0,2},{1,3},{2,0},{3,1},{4,6},{5,7},{6,4},{7,5},{8,10},{9,11},{10,... | collective-permute-start | bytes 589832 | tf_op jit(solution)/shard_map/ppermute | solution.py:212
  102.9 9.5 %collective-permute-start.27 = (f32[128,384]{1,0:T(8,128)S(1)}, f32[128,384]{1,0:T(8,128)S(1)}, u32[]{:S(2)}, u32[]{:S(2)}) collective-permute-start(f32[128,384]{1,0:T(8,128)S(1)} %get-tuple-element.104), channel_id=1, source_target_pairs={{0,2},{1,3},{2,0},{3,1},{4,6},{5,7},{6,4},{7,5},{8,10},{9,11},{10,... | collective-permute-start | bytes 589832 | tf_op jit(solution)/shard_map/ppermute | solution.py:212
  104.4 8.2 %collective-permute-start.29 = (f32[128,384]{1,0:T(8,128)S(1)}, f32[128,384]{1,0:T(8,128)S(1)}, u32[]{:S(2)}, u32[]{:S(2)}) collective-permute-start(f32[128,384]{1,0:T(8,128)S(1)} %get-tuple-element.105), channel_id=1, source_target_pairs={{0,4},{1,5},{2,6},{3,7},{4,0},{5,1},{6,2},{7,3},{8,12},{9,13},{10,... | collective-permute-start | bytes 589832 | tf_op jit(solution)/shard_map/ppermute | solution.py:212
  110.4 2.2 %collective-permute-start.31 = (f32[128,384]{1,0:T(8,128)S(1)}, f32[128,384]{1,0:T(8,128)S(1)}, u32[]{:S(2)}, u32[]{:S(2)}) collective-permute-start(f32[128,384]{1,0:T(8,128)S(1)} %fold.23), channel_id=1, source_target_pairs={{0,1},{1,0},{2,3},{3,2},{4,5},{5,4},{6,7},{7,6},{8,9},{9,8},{10,11... | collective-permute-start | bytes 589832 | tf_op jit(solution)/shard_map/ppermute | solution.py:212
  110.5 7.4 %collective-permute-start.25 = (f32[128,384]{1,0:T(8,128)S(1)}, f32[128,384]{1,0:T(8,128)S(1)}, u32[]{:S(2)}, u32[]{:S(2)}) collective-permute-start(f32[128,384]{1,0:T(8,128)S(1)} %get-tuple-element.101), channel_id=1, source_target_pairs={{0,4},{1,5},{2,6},{3,7},{4,0},{5,1},{6,2},{7,3},{8,12},{9,13},{10,... | collective-permute-start | bytes 589832 | tf_op jit(solution)/shard_map/ppermute | solution.py:212
  112.5 5.4 %collective-permute-start.28 = (f32[128,384]{1,0:T(8,128)S(1)}, f32[128,384]{1,0:T(8,128)S(1)}, u32[]{:S(2)}, u32[]{:S(2)}) collective-permute-start(f32[128,384]{1,0:T(8,128)S(1)} %fold.22), channel_id=1, source_target_pairs={{0,1},{1,0},{2,3},{3,2},{4,5},{5,4},{6,7},{7,6},{8,9},{9,8},{10,11... | collective-permute-start | bytes 589832 | tf_op jit(solution)/shard_map/ppermute | solution.py:212

commit v19 on v18

--- a/solution.py
+++ b/solution.py
@@ -250,12 +250,17 @@
                 stays = [i for i, r in enumerate(names[h]) if not r & bit]
                 goes = [i for i, r in enumerate(names[h]) if r & bit]
                 held[h], moved = fold(rows, stays, goes, held[h], moving[h])
-                moving[h] = swap(moved, 2 * bit)
+                across = n + 1 == n_occ and level + 1 == len(bits)
+                moving[h] = swap(moved, 2 * bit + (h if across else 0))
                 names[h] = [names[h][i] for i in stays]
         token = held if out is None else [*held, out]
         settled = moving if n == 0 else []
-        (theirs,) = fold(rows, [0], [], held[1], moving[1])
-        out = write(out, (rows, n_occ * width), d, half, offset, held[0], moving[0], swap(theirs, 1))
+        if n + 1 == n_occ:
+            (other,) = fold(rows, [0], [], swap(held[1], 1), moving[1])
+        else:
+            (theirs,) = fold(rows, [0], [], held[1], moving[1])
+            other = swap(theirs, 1)
+        out = write(out, (rows, n_occ * width), d, half, offset, held[0], moving[0], other)
     return out
 
 

time: 119 us -> 119 us (level)
  transfers between devices with their start and end apart: 32 -> 32, of which waited for: 13 -> 12; matrix products, arithmetic and copies ran while one was open for 1% -> 1% of each run, Pallas kernels for 18% -> 18%
where the time goes in v19:
time: 119 us; the launch traced here: 118 us
  waiting for transfers between devices  57.3 us (48%)
  starting transfers between devices  33.6 us (28%)
  Pallas kernels  24.5 us (21%)
  other arithmetic  1.53 us (1%)
    ppermute x28, waiting for transfers between devices, swap(): return lax.ppermute(x, 'vir', [(i, i ^ bits) for i in range(n_vir)])  51.6 us
    ppermute x28, starting transfers between devices, swap(): return lax.ppermute(x, 'vir', [(i, i ^ bits) for i in range(n_vir)])  23.1 us
    pallas_call x23, Pallas kernels, kernel_call(): pl.pallas_call(body, out_shape=[pltpu.VMEM(shape, jnp.float32) for shape...  21.4 us
    ppermute x1, starting transfers between devices, line_blocks(): far = lax.ppermute(after(own, centre, near), 'occ', [(0, 3), (3, 0)])  5.66 us
    ppermute x1, waiting for transfers between devices, direct(): return lax.ppermute(x, 'occ', [(i, i ^ d) for i in range(nodes)])  5.65 us
    pallas_call x4, Pallas kernels, write(): pl.pallas_call(functools.partial(write_kernel, d, half, offset), out_shap...  3.12 us
    ppermute x1, starting transfers between devices, direct(): return lax.ppermute(x, 'occ', [(i, i ^ d) for i in range(nodes)])  3.01 us
  transfers between devices with their start and end apart: 32, of which 12 were waited for; matrix products, arithmetic and copies ran while one was open for 1% of the time, Pallas kernels for 18%

profile of v19, /device:TPU:0, one launch (start us, length us, event | category | flops | bytes accessed | tf_op | source)
XLA Modules:
  0.0 118.4 jit_solution(9132976062441364321)
XLA Ops:
  0.0 1.3 %halves.1 = (f32[384,384]{1,0:T(8,128)S(1)}, f32[384,384]{1,0:T(8,128)S(1)}) custom-call(s32[3,6]{1,0:T(4,128)} %mask_hbm.1, f32[384,768]{1,0:T(8,128)} %int_hbm.1), custom_call_target="tpu_custom_call" | custom-call | flops 1 | bytes 1 | tf_op jit(solution)/shard_map/halves/pallas_call | solution.py:30
  1.3 0.5 collective-permute-start.5
  1.8 1.4 %cut.1 = (f32[128,768]{1,0:T(8,128)S(1)}, f32[128,768]{1,0:T(8,128)S(1)}, f32[128,768]{1,0:T(8,128)S(1)}, f32[128,768]{1,0:T(8,128)S(1)}) custom-call(s32[4,24]{1,0:T(4,128)} %mask_hbm.2, f32[128,3072]{1,0:T(8,128)} %amp_hbm.1), custom_call_target="tpu_custom_call" | custom-call | flops 1 | bytes 1 | tf_op jit(solution)/shard_map/cut/pallas_call | solution.py:30
  3.3 0.2 collective-permute-done.5.other_ref
  3.5 0.1 join.1.refs_4_
  3.6 3.0 %collective-permute-start.8 = (f32[768,384]{1,0:T(8,128)S(1)}, f32[768,384]{1,0:T(8,128)S(1)}, u32[]{:S(2)}, u32[]{:S(2)}) collective-permute-start(f32[768,384]{1,0:T(8,128)S(1)} %join.1.refs_4_), channel_id=1, source_target_pairs={{0,8},{8,0},{16,24},{24,16},{1,9},{9,1},{17,25},{25,17},{2,10},{10... | collective-permute-start | bytes 3538952 | tf_op jit(solution)/shard_map/ppermute | solution.py:192
  6.6 0.7 collective-permute-start.6
  7.3 1.6 %collective-permute-start = (f32[128,768]{1,0:T(8,128)S(1)}, f32[128,768]{1,0:T(8,128)S(1)}, u32[]{:S(2)}, u32[]{:S(2)}) collective-permute-start(f32[128,768]{1,0:T(8,128)S(1)} %get-tuple-element.59), channel_id=1, source_target_pairs={{0,4},{1,5},{2,6},{3,7},{4,0},{5,1},{6,2},{7,3},{8,12},{9,13},{10,... | collective-permute-start | bytes 1179656 | tf_op jit(solution)/shard_map/ppermute | solution.py:212
  8.9 1.4 %collective-permute-start.1 = (f32[128,768]{1,0:T(8,128)S(1)}, f32[128,768]{1,0:T(8,128)S(1)}, u32[]{:S(2)}, u32[]{:S(2)}) collective-permute-start(f32[128,768]{1,0:T(8,128)S(1)} %get-tuple-element.60), channel_id=1, source_target_pairs={{0,6},{1,7},{2,4},{3,5},{4,2},{5,3},{6,0},{7,1},{8,14},{9,15},{10,... | collective-permute-start | bytes 1179656 | tf_op jit(solution)/shard_map/ppermute | solution.py:212
  10.3 0.5 collective-permute-start.3
  10.9 15.8 %collective-permute-done.refs_1_ = f32[128,768]{1,0:T(8,128)S(1)} collective-permute-done((f32[128,768]{1,0:T(8,128)S(1)}, f32[128,768]{1,0:T(8,128)S(1)}, u32[]{:S(2)}, u32[]{:S(2)}) %collective-permute-start) | collective-permute-done | bytes 393248 | tf_op jit(solution)/shard_map/ppermute | solution.py:212
  26.7 0.5 collective-permute-start.11
  27.2 5.7 %collective-permute-done.8.refs_4_ = f32[768,384]{1,0:T(8,128)S(1)} collective-permute-done((f32[768,384]{1,0:T(8,128)S(1)}, f32[768,384]{1,0:T(8,128)S(1)}, u32[]{:S(2)}, u32[]{:S(2)}) %collective-permute-start.8) | collective-permute-done | bytes 1179680 | tf_op jit(solution)/shard_map/ppermute | solution.py:192
  32.8 1.0 copy-done.2
  33.9 0.0 collective-permute-done.6
  33.9 5.7 %collective-permute-start.9 = (f32[768,384]{1,0:T(8,128)S(1)}, f32[768,384]{1,0:T(8,128)}, u32[]{:S(2)}, u32[]{:S(2)}) collective-permute-start(f32[768,384]{1,0:T(8,128)S(1)} %join.1.refs_4_), channel_id=1, source_target_pairs={{0,24},{24,0},{1,25},{25,1},{2,26},{26,2},{3,27},{27,3},{4,28},{28... | collective-permute-start | bytes 3538952 | tf_op jit(solution)/shard_map/ppermute | solution.py:198
  39.6 0.1 collective-permute-start.2
  39.6 0.0 collective-permute-done.3.refs_0_
  39.7 0.5 collective-permute-start.4
  40.2 2.1 %products.8 = (f32[256,384]{1,0:T(8,128)}, f32[256,384]{1,0:T(8,128)}) custom-call(f32[128,768]{1,0:T(8,128)S(1)} %collective-permute-done.3.refs_0_, f32[128,768]{1,0:T(8,128)S(1)} %collective-permute-done.1.refs_1_, f32[128,768]{1,0:T(8,128)S(1)} %collective-permute-done.10.refs_2_, f32[128,768]{1,0:T(8,128)S(1)} %collective-permute-done.11.refs_3_, ...), custom_call_target="tpu_custom_call" | custom-call | flops 1 | bytes 1 | tf_op jit(solution)/shard_map/products/pallas_call | solution.py:30
  42.3 1.5 %collective-permute-start.13 = (f32[256,384]{1,0:T(8,128)}, f32[256,384]{1,0:T(8,128)}, u32[]{:S(2)}, u32[]{:S(2)}) collective-permute-start(f32[256,384]{1,0:T(8,128)} %get-tuple-element.67), channel_id=1, source_target_pairs={{0,4},{1,5},{2,6},{3,7},{4,0},{5,1},{6,2},{7,3},{8,12},{9,13},{10,... | collective-permute-start | bytes 1179656 | tf_op jit(solution)/shard_map/ppermute | solution.py:212
  43.8 1.5 %collective-permute-start.12 = (f32[256,384]{1,0:T(8,128)}, f32[256,384]{1,0:T(8,128)}, u32[]{:S(2)}, u32[]{:S(2)}) collective-permute-start(f32[256,384]{1,0:T(8,128)} %get-tuple-element.66), channel_id=1, source_target_pairs={{0,2},{1,3},{2,0},{3,1},{4,6},{5,7},{6,4},{7,5},{8,10},{9,11},{10,... | collective-permute-start | bytes 1179656 | tf_op jit(solution)/shard_map/ppermute | solution.py:212
  45.3 2.5 %products.9 = (f32[256,384]{1,0:T(8,128)S(1)}, f32[256,384]{1,0:T(8,128)S(1)}) custom-call(f32[128,768]{1,0:T(8,128)S(1)} %get-tuple-element.61.refs_0_, f32[128,768]{1,0:T(8,128)S(1)} %collective-permute-done.refs_1_, f32[128,768]{1,0:T(8,128)S(1)} %collective-permute-done.2.refs_2_, f32[128,768]{1,0:T(8,128)} %collective-permute-done.4.refs_3_, ...), custom_call_target="tpu_custom_call" | custom-call | flops 1 | bytes 1 | tf_op jit(solution)/shard_map/products/pallas_call | solution.py:30
  47.8 5.9 %collective-permute-done.13.got_ref = f32[256,384]{1,0:T(8,128)} collective-permute-done((f32[256,384]{1,0:T(8,128)}, f32[256,384]{1,0:T(8,128)}, u32[]{:S(2)}, u32[]{:S(2)}) %collective-permute-start.13) | collective-permute-done | bytes 393248 | tf_op jit(solution)/shard_map/ppermute | solution.py:212
  53.7 1.0 fold.13
  54.8 1.6 %collective-permute-start.15 = (f32[128,384]{1,0:T(8,128)S(1)}, f32[128,384]{1,0:T(8,128)S(1)}, u32[]{:S(2)}, u32[]{:S(2)}) collective-permute-start(f32[128,384]{1,0:T(8,128)S(1)} %get-tuple-element.79), channel_id=1, source_target_pairs={{0,2},{1,3},{2,0},{3,1},{4,6},{5,7},{6,4},{7,5},{8,10},{9,11},{10,... | collective-permute-start | bytes 589832 | tf_op jit(solution)/shard_map/ppermute | solution.py:212
  56.3 0.1 broadcast_select_fusion.1
  56.5 1.1 collective-permute-start.7
  57.5 1.1 fold.12
  58.6 1.6 %collective-permute-start.14 = (f32[128,384]{1,0:T(8,128)S(1)}, f32[128,384]{1,0:T(8,128)S(1)}, u32[]{:S(2)}, u32[]{:S(2)}) collective-permute-start(f32[128,384]{1,0:T(8,128)S(1)} %get-tuple-element.78), channel_id=1, source_target_pairs={{0,4},{1,5},{2,6},{3,7},{4,0},{5,1},{6,2},{7,3},{8,12},{9,13},{10,... | collective-permute-start | bytes 589832 | tf_op jit(solution)/shard_map/ppermute | solution.py:212
  60.2 1.4 %products.10 = (f32[256,384]{1,0:T(8,128)S(1)}, f32[256,384]{1,0:T(8,128)S(1)}) custom-call(f32[128,768]{1,0:T(8,128)S(1)} %collective-permute-done.3.refs_0_, f32[128,768]{1,0:T(8,128)S(1)} %collective-permute-done.1.refs_1_, f32[128,768]{1,0:T(8,128)S(1)} %collective-permute-done.10.refs_2_, f32[128,768]{1,0:T(8,128)S(1)} %copy-done.1, ...), custom_call_target="tpu_custom_call" | custom-call | flops 1 | bytes 1 | tf_op jit(solution)/shard_map/products/pallas_call | solution.py:30
  61.6 0.6 collective-permute-start.17
  62.2 0.5 collective-permute-start.16
  62.7 3.4 %collective-permute-done.14.got_ref = f32[128,384]{1,0:T(8,128)S(1)} collective-permute-done((f32[128,384]{1,0:T(8,128)S(1)}, f32[128,384]{1,0:T(8,128)S(1)}, u32[]{:S(2)}, u32[]{:S(2)}) %collective-permute-start.14) | collective-permute-done | bytes 196640 | tf_op jit(solution)/shard_map/ppermute | solution.py:212
  66.1 1.4 %collective-permute-done.18.other_ref = f32[128,384]{1,0:T(8,128)S(1)} collective-permute-done((f32[128,384]{1,0:T(8,128)S(1)}, f32[128,384]{1,0:T(8,128)S(1)}, u32[]{:S(2)}, u32[]{:S(2)}) %collective-permute-start.18) | collective-permute-done | bytes 196640 | tf_op jit(solution)/shard_map/ppermute | solution.py:212
  67.6 0.8 write.4.refs_0_
  68.4 2.4 %products.11 = (f32[256,384]{1,0:T(8,128)S(1)}, f32[256,384]{1,0:T(8,128)S(1)}) custom-call(f32[128,768]{1,0:T(8,128)S(1)} %get-tuple-element.61.refs_0_, f32[128,768]{1,0:T(8,128)S(1)} %collective-permute-done.refs_1_, f32[128,768]{1,0:T(8,128)S(1)} %collective-permute-done.2.refs_2_, f32[128,768]{1,0:T(8,128)} %collective-permute-done.4.refs_3_, ...), custom_call_target="tpu_custom_call" | custom-call | flops 1 | bytes 1 | tf_op jit(solution)/shard_map/products/pallas_call | solution.py:30
  70.8 2.0 %collective-permute-done.17.got_ref = f32[256,384]{1,0:T(8,128)S(1)} collective-permute-done((f32[256,384]{1,0:T(8,128)S(1)}, f32[256,384]{1,0:T(8,128)S(1)}, u32[]{:S(2)}, u32[]{:S(2)}) %collective-permute-start.17) | collective-permute-done | bytes 393248 | tf_op jit(solution)/shard_map/ppermute | solution.py:212
  72.8 0.6 collective-permute-start.22
  73.5 1.4 %broadcast_select_fusion.refs_4_ = f32[768,384]{1,0:T(8,128)S(1)} fusion(f32[768,384]{1,0:T(8,128)S(1)} %copy-done.5, f32[768,384]{1,0:T(8,128)} %collective-permute-done.9, pred[]{:T(512)S(6)} %or.3), kind=kLoop, calls=%fused_computation | loop fusion | flops 294912 | bytes 3538945 | tf_op jit(solution)/shard_map/jit(_where)/select_n | solution.py:240
  74.9 1.4 %products.12 = (f32[256,384]{1,0:T(8,128)S(1)}, f32[256,384]{1,0:T(8,128)S(1)}) custom-call(f32[128,768]{1,0:T(8,128)S(1)} %collective-permute-done.3.refs_0_, f32[128,768]{1,0:T(8,128)S(1)} %collective-permute-done.1.refs_1_, f32[128,768]{1,0:T(8,128)S(1)} %collective-permute-done.10.refs_2_, f32[128,768]{1,0:T(8,128)S(1)} %copy-done.1, ...), custom_call_target="tpu_custom_call" | custom-call | flops 1 | bytes 1 | tf_op jit(solution)/shard_map/products/pallas_call | solution.py:30
  76.3 1.6 %collective-permute-start.19 = (f32[256,384]{1,0:T(8,128)S(1)}, f32[256,384]{1,0:T(8,128)S(1)}, u32[]{:S(2)}, u32[]{:S(2)}) collective-permute-start(f32[256,384]{1,0:T(8,128)S(1)} %get-tuple-element.86), channel_id=1, source_target_pairs={{0,2},{1,3},{2,0},{3,1},{4,6},{5,7},{6,4},{7,5},{8,10},{9,11},{10,... | collective-permute-start | bytes 1179656 | tf_op jit(solution)/shard_map/ppermute | solution.py:212
  77.8 1.3 %collective-permute-start.20 = (f32[256,384]{1,0:T(8,128)S(1)}, f32[256,384]{1,0:T(8,128)S(1)}, u32[]{:S(2)}, u32[]{:S(2)}) collective-permute-start(f32[256,384]{1,0:T(8,128)S(1)} %get-tuple-element.87), channel_id=1, source_target_pairs={{0,4},{1,5},{2,6},{3,7},{4,0},{5,1},{6,2},{7,3},{8,12},{9,13},{10,... | collective-permute-start | bytes 1179656 | tf_op jit(solution)/shard_map/ppermute | solution.py:212
  79.1 0.7 collective-permute-start.21
  79.9 0.3 collective-permute-done.22.got_ref
  80.2 0.1 collective-permute-start.23
  80.3 2.4 %products.13 = (f32[256,384]{1,0:T(8,128)S(1)}, f32[256,384]{1,0:T(8,128)S(1)}) custom-call(f32[128,768]{1,0:T(8,128)S(1)} %get-tuple-element.61.refs_0_, f32[128,768]{1,0:T(8,128)S(1)} %collective-permute-done.refs_1_, f32[128,768]{1,0:T(8,128)S(1)} %collective-permute-done.2.refs_2_, f32[128,768]{1,0:T(8,128)} %collective-permute-done.4.refs_3_, ...), custom_call_target="tpu_custom_call" | custom-call | flops 1 | bytes 1 | tf_op jit(solution)/shard_map/products/pallas_call | solution.py:30
  82.7 8.1 %collective-permute-done.21.got_ref = f32[128,384]{1,0:T(8,128)S(1)} collective-permute-done((f32[128,384]{1,0:T(8,128)S(1)}, f32[128,384]{1,0:T(8,128)S(1)}, u32[]{:S(2)}, u32[]{:S(2)}) %collective-permute-start.21) | collective-permute-done | bytes 196640 | tf_op jit(solution)/shard_map/ppermute | solution.py:212
  90.8 0.8 write.5.refs_0_
  91.8 1.4 %products.14 = (f32[256,384]{1,0:T(8,128)S(1)}, f32[256,384]{1,0:T(8,128)S(1)}) custom-call(f32[128,768]{1,0:T(8,128)S(1)} %collective-permute-done.3.refs_0_, f32[128,768]{1,0:T(8,128)S(1)} %collective-permute-done.1.refs_1_, f32[128,768]{1,0:T(8,128)S(1)} %collective-permute-done.10.refs_2_, f32[128,768]{1,0:T(8,128)S(1)} %copy-done.1, ...), custom_call_target="tpu_custom_call" | custom-call | flops 1 | bytes 1 | tf_op jit(solution)/shard_map/products/pallas_call | solution.py:30
  93.2 1.8 %collective-permute-start.26 = (f32[256,384]{1,0:T(8,128)S(1)}, f32[256,384]{1,0:T(8,128)S(1)}, u32[]{:S(2)}, u32[]{:S(2)}) collective-permute-start(f32[256,384]{1,0:T(8,128)S(1)} %get-tuple-element.97), channel_id=1, source_target_pairs={{0,4},{1,5},{2,6},{3,7},{4,0},{5,1},{6,2},{7,3},{8,12},{9,13},{10,... | collective-permute-start | bytes 1179656 | tf_op jit(solution)/shard_map/ppermute | solution.py:212
  95.0 0.5 collective-permute-start.24
  95.5 1.5 %collective-permute-start.30 = (f32[128,384]{1,0:T(8,128)S(1)}, f32[128,384]{1,0:T(8,128)S(1)}, u32[]{:S(2)}, u32[]{:S(2)}) collective-permute-start(f32[128,384]{1,0:T(8,128)S(1)} %get-tuple-element.106), channel_id=1, source_target_pairs={{0,2},{1,3},{2,0},{3,1},{4,6},{5,7},{6,4},{7,5},{8,10},{9,11},{10,... | collective-permute-start | bytes 589832 | tf_op jit(solution)/shard_map/ppermute | solution.py:212
  97.0 0.3 collective-permute-start.29
  97.3 2.4 %products.15 = (f32[256,384]{1,0:T(8,128)S(1)}, f32[256,384]{1,0:T(8,128)S(1)}) custom-call(f32[128,768]{1,0:T(8,128)S(1)} %get-tuple-element.61.refs_0_, f32[128,768]{1,0:T(8,128)S(1)} %collective-permute-done.refs_1_, f32[128,768]{1,0:T(8,128)S(1)} %collective-permute-done.2.refs_2_, f32[128,768]{1,0:T(8,128)} %collective-permute-done.4.refs_3_, ...), custom_call_target="tpu_custom_call" | custom-call | flops 1 | bytes 1 | tf_op jit(solution)/shard_map/products/pallas_call | solution.py:30
  99.7 8.5 %collective-permute-done.30.got_ref = f32[128,384]{1,0:T(8,128)S(1)} collective-permute-done((f32[128,384]{1,0:T(8,128)S(1)}, f32[128,384]{1,0:T(8,128)S(1)}, u32[]{:S(2)}, u32[]{:S(2)}) %collective-permute-start.30) | collective-permute-done | bytes 196640 | tf_op jit(solution)/shard_map/ppermute | solution.py:212
  108.3 0.1 collective-permute-start.31
  108.4 0.5 collective-permute-start.27
  109.0 1.2 collective-permute-start.28
  110.2 0.6 collective-permute-start.25
  110.8 0.8 write.6.refs_0_
  111.6 4.3 %collective-permute-done.28.got_ref = f32[128,384]{1,0:T(8,128)S(1)} collective-permute-done((f32[128,384]{1,0:T(8,128)S(1)}, f32[128,384]{1,0:T(8,128)S(1)}, u32[]{:S(2)}, u32[]{:S(2)}) %collective-permute-start.28) | collective-permute-done | bytes 196640 | tf_op jit(solution)/shard_map/ppermute | solution.py:212
  115.9 1.6 %collective-permute-done.25.got_ref = f32[128,384]{1,0:T(8,128)S(1)} collective-permute-done((f32[128,384]{1,0:T(8,128)S(1)}, f32[128,384]{1,0:T(8,128)S(1)}, u32[]{:S(2)}, u32[]{:S(2)}) %collective-permute-start.25) | collective-permute-done | bytes 196640 | tf_op jit(solution)/shard_map/ppermute | solution.py:212
  117.5 0.8 write.7
  (41 shorter events, 0.4 us)
Async XLA Ops:
  1.3 2.1 %collective-permute-start.5 = (f32[384,384]{1,0:T(8,128)S(1)}, f32[384,384]{1,0:T(8,128)S(1)}, u32[]{:S(2)}, u32[]{:S(2)}) collective-permute-start(f32[384,384]{1,0:T(8,128)S(1)} %get-tuple-element.63), channel_id=1, source_target_pairs={{0,1},{1,0},{2,3},{3,2},{4,5},{5,4},{6,7},{7,6},{8,9},{9,8},{10,11... | collective-permute-start | bytes 1769480 | tf_op jit(solution)/shard_map/ppermute | solution.py:212
  3.6 29.3 %collective-permute-start.8 = (f32[768,384]{1,0:T(8,128)S(1)}, f32[768,384]{1,0:T(8,128)S(1)}, u32[]{:S(2)}, u32[]{:S(2)}) collective-permute-start(f32[768,384]{1,0:T(8,128)S(1)} %join.1.refs_4_), channel_id=1, source_target_pairs={{0,8},{8,0},{16,24},{24,16},{1,9},{9,1},{17,25},{25,17},{2,10},{10... | collective-permute-start | bytes 3538952 | tf_op jit(solution)/shard_map/ppermute | solution.py:192
  6.6 27.3 %collective-permute-start.6 = (f32[768,384]{1,0:T(8,128)S(1)}, f32[768,384]{1,0:T(8,128)S(1)}, u32[]{:S(2)}, u32[]{:S(2)}) collective-permute-start(f32[768,384]{1,0:T(8,128)S(1)} %join.1.refs_4_), channel_id=1, source_target_pairs={{8,16},{16,8},{9,17},{17,9},{10,18},{18,10},{11,19},{19,11},{12,20... | collective-permute-start | bytes 3538952 | tf_op jit(solution)/shard_map/ppermute | solution.py:196
  7.3 19.4 %collective-permute-start = (f32[128,768]{1,0:T(8,128)S(1)}, f32[128,768]{1,0:T(8,128)S(1)}, u32[]{:S(2)}, u32[]{:S(2)}) collective-permute-start(f32[128,768]{1,0:T(8,128)S(1)} %get-tuple-element.59), channel_id=1, source_target_pairs={{0,4},{1,5},{2,6},{3,7},{4,0},{5,1},{6,2},{7,3},{8,12},{9,13},{10,... | collective-permute-start | bytes 1179656 | tf_op jit(solution)/shard_map/ppermute | solution.py:212
  8.9 17.8 %collective-permute-start.1 = (f32[128,768]{1,0:T(8,128)S(1)}, f32[128,768]{1,0:T(8,128)S(1)}, u32[]{:S(2)}, u32[]{:S(2)}) collective-permute-start(f32[128,768]{1,0:T(8,128)S(1)} %get-tuple-element.60), channel_id=1, source_target_pairs={{0,6},{1,7},{2,4},{3,5},{4,2},{5,3},{6,0},{7,1},{8,14},{9,15},{10,... | collective-permute-start | bytes 1179656 | tf_op jit(solution)/shard_map/ppermute | solution.py:212
  10.3 29.3 %collective-permute-start.3 = (f32[128,768]{1,0:T(8,128)S(1)}, f32[128,768]{1,0:T(8,128)S(1)}, u32[]{:S(2)}, u32[]{:S(2)}) collective-permute-start(f32[128,768]{1,0:T(8,128)S(1)} %get-tuple-element.62), channel_id=1, source_target_pairs={{0,2},{1,3},{2,0},{3,1},{4,6},{5,7},{6,4},{7,5},{8,10},{9,11},{10,... | collective-permute-start | bytes 1179656 | tf_op jit(solution)/shard_map/ppermute | solution.py:212
  26.7 13.5 %collective-permute-start.10 = (f32[128,768]{1,0:T(8,128)S(1)}, f32[128,768]{1,0:T(8,128)S(1)}, u32[]{:S(2)}, u32[]{:S(2)}) collective-permute-start(f32[128,768]{1,0:T(8,128)S(1)} %collective-permute-done.refs_1_), channel_id=1, source_target_pairs={{0,1},{1,0},{2,3},{3,2},{4,5},{5,4},{6,7},{7,6},{8,9},{9,8},{10,11... | collective-permute-start | bytes 1179656 | tf_op jit(solution)/shard_map/ppermute | solution.py:212
  26.7 13.5 %collective-permute-start.11 = (f32[128,768]{1,0:T(8,128)S(1)}, f32[128,768]{1,0:T(8,128)S(1)}, u32[]{:S(2)}, u32[]{:S(2)}) collective-permute-start(f32[128,768]{1,0:T(8,128)S(1)} %collective-permute-done.1.refs_1_), channel_id=1, source_target_pairs={{0,1},{1,0},{2,3},{3,2},{4,5},{5,4},{6,7},{7,6},{8,9},{9,8},{10,11... | collective-permute-start | bytes 1179656 | tf_op jit(solution)/shard_map/ppermute | solution.py:212
  32.8 1.0 copy-start.2
  33.9 6.3 %copy-start.4 = (f32[768,384]{1,0:T(8,128)}, f32[768,384]{1,0:T(8,128)S(1)}, u32[]{:S(2)}) copy-start(f32[768,384]{1,0:T(8,128)S(1)} %collective-permute-done.6) | copy-start | bytes 3538948
  33.9 39.6 %collective-permute-start.9 = (f32[768,384]{1,0:T(8,128)S(1)}, f32[768,384]{1,0:T(8,128)}, u32[]{:S(2)}, u32[]{:S(2)}) collective-permute-start(f32[768,384]{1,0:T(8,128)S(1)} %join.1.refs_4_), channel_id=1, source_target_pairs={{0,24},{24,0},{1,25},{25,1},{2,26},{26,2},{3,27},{27,3},{4,28},{28... | collective-permute-start | bytes 3538952 | tf_op jit(solution)/shard_map/ppermute | solution.py:198
  39.6 5.8 %collective-permute-start.2 = (f32[128,768]{1,0:T(8,128)S(1)}, f32[128,768]{1,0:T(8,128)S(1)}, u32[]{:S(2)}, u32[]{:S(2)}) collective-permute-start(f32[128,768]{1,0:T(8,128)S(1)} %get-tuple-element.61.refs_0_), channel_id=1, source_target_pairs={{0,1},{1,0},{2,3},{3,2},{4,5},{5,4},{6,7},{7,6},{8,9},{9,8},{10,11... | collective-permute-start | bytes 1179656 | tf_op jit(solution)/shard_map/ppermute | solution.py:212
  39.7 5.7 %collective-permute-start.4 = (f32[128,768]{1,0:T(8,128)S(1)}, f32[128,768]{1,0:T(8,128)}, u32[]{:S(2)}, u32[]{:S(2)}) collective-permute-start(f32[128,768]{1,0:T(8,128)S(1)} %collective-permute-done.3.refs_0_), channel_id=1, source_target_pairs={{0,1},{1,0},{2,3},{3,2},{4,5},{5,4},{6,7},{7,6},{8,9},{9,8},{10,11... | collective-permute-start | bytes 1179656 | tf_op jit(solution)/shard_map/ppermute | solution.py:212
  40.2 2.2 %copy-start = (f32[128,768]{1,0:T(8,128)}, f32[128,768]{1,0:T(8,128)S(1)}, u32[]{:S(2)}) copy-start(f32[128,768]{1,0:T(8,128)S(1)} %collective-permute-done.11.refs_3_) | copy-start | bytes 1179652
  42.3 11.4 %collective-permute-start.13 = (f32[256,384]{1,0:T(8,128)}, f32[256,384]{1,0:T(8,128)}, u32[]{:S(2)}, u32[]{:S(2)}) collective-permute-start(f32[256,384]{1,0:T(8,128)} %get-tuple-element.67), channel_id=1, source_target_pairs={{0,4},{1,5},{2,6},{3,7},{4,0},{5,1},{6,2},{7,3},{8,12},{9,13},{10,... | collective-permute-start | bytes 1179656 | tf_op jit(solution)/shard_map/ppermute | solution.py:212
  43.8 13.7 %collective-permute-start.12 = (f32[256,384]{1,0:T(8,128)}, f32[256,384]{1,0:T(8,128)}, u32[]{:S(2)}, u32[]{:S(2)}) collective-permute-start(f32[256,384]{1,0:T(8,128)} %get-tuple-element.66), channel_id=1, source_target_pairs={{0,2},{1,3},{2,0},{3,1},{4,6},{5,7},{6,4},{7,5},{8,10},{9,11},{10,... | collective-permute-start | bytes 1179656 | tf_op jit(solution)/shard_map/ppermute | solution.py:212
  45.3 11.0 %copy-start.5 = (f32[768,384]{1,0:T(8,128)S(1)}, f32[768,384]{1,0:T(8,128)}, u32[]{:S(2)}) copy-start(f32[768,384]{1,0:T(8,128)} %copy-done.4) | copy-start | bytes 3538948
  54.8 5.4 %copy-start.1 = (f32[128,768]{1,0:T(8,128)S(1)}, f32[128,768]{1,0:T(8,128)}, u32[]{:S(2)}) copy-start(f32[128,768]{1,0:T(8,128)} %copy-done) | copy-start | bytes 1179652
  54.8 7.4 %collective-permute-start.15 = (f32[128,384]{1,0:T(8,128)S(1)}, f32[128,384]{1,0:T(8,128)S(1)}, u32[]{:S(2)}, u32[]{:S(2)}) collective-permute-start(f32[128,384]{1,0:T(8,128)S(1)} %get-tuple-element.79), channel_id=1, source_target_pairs={{0,2},{1,3},{2,0},{3,1},{4,6},{5,7},{6,4},{7,5},{8,10},{9,11},{10,... | collective-permute-start | bytes 589832 | tf_op jit(solution)/shard_map/ppermute | solution.py:212
  56.3 3.8 %copy-start.3 = (f32[768,384]{1,0:T(8,128)S(1)}, f32[768,384]{1,0:T(8,128)}, u32[]{:S(2)}) copy-start(f32[768,384]{1,0:T(8,128)} %copy-done.2) | copy-start | bytes 3538948
  56.5 35.3 %collective-permute-start.7 = (f32[768,384]{1,0:T(8,128)S(1)}, f32[768,384]{1,0:T(8,128)S(1)}, u32[]{:S(2)}, u32[]{:S(2)}) collective-permute-start(f32[768,384]{1,0:T(8,128)S(1)} %broadcast_select_fusion.1), channel_id=1, source_target_pairs={{8,0},{16,24},{0,16},{24,8},{9,1},{17,25},{1,17},{25,9},{10,2},{18... | collective-permute-start | bytes 3538952 | tf_op jit(solution)/shard_map/ppermute | solution.py:200
  58.6 7.5 %collective-permute-start.14 = (f32[128,384]{1,0:T(8,128)S(1)}, f32[128,384]{1,0:T(8,128)S(1)}, u32[]{:S(2)}, u32[]{:S(2)}) collective-permute-start(f32[128,384]{1,0:T(8,128)S(1)} %get-tuple-element.78), channel_id=1, source_target_pairs={{0,4},{1,5},{2,6},{3,7},{4,0},{5,1},{6,2},{7,3},{8,12},{9,13},{10,... | collective-permute-start | bytes 589832 | tf_op jit(solution)/shard_map/ppermute | solution.py:212
  61.6 11.1 %collective-permute-start.17 = (f32[256,384]{1,0:T(8,128)S(1)}, f32[256,384]{1,0:T(8,128)S(1)}, u32[]{:S(2)}, u32[]{:S(2)}) collective-permute-start(f32[256,384]{1,0:T(8,128)S(1)} %get-tuple-element.75), channel_id=1, source_target_pairs={{0,4},{1,5},{2,6},{3,7},{4,0},{5,1},{6,2},{7,3},{8,12},{9,13},{10,... | collective-permute-start | bytes 1179656 | tf_op jit(solution)/shard_map/ppermute | solution.py:212
  62.2 11.2 %collective-permute-start.16 = (f32[256,384]{1,0:T(8,128)S(1)}, f32[256,384]{1,0:T(8,128)S(1)}, u32[]{:S(2)}, u32[]{:S(2)}) collective-permute-start(f32[256,384]{1,0:T(8,128)S(1)} %get-tuple-element.74), channel_id=1, source_target_pairs={{0,2},{1,3},{2,0},{3,1},{4,6},{5,7},{6,4},{7,5},{8,10},{9,11},{10,... | collective-permute-start | bytes 1179656 | tf_op jit(solution)/shard_map/ppermute | solution.py:212
  66.1 1.4 %collective-permute-start.18 = (f32[128,384]{1,0:T(8,128)S(1)}, f32[128,384]{1,0:T(8,128)S(1)}, u32[]{:S(2)}, u32[]{:S(2)}) collective-permute-start(f32[128,384]{1,0:T(8,128)S(1)} %fold.16), channel_id=1, source_target_pairs={{0,1},{1,0},{2,3},{3,2},{4,5},{5,4},{6,7},{7,6},{8,9},{9,8},{10,11... | collective-permute-start | bytes 589832 | tf_op jit(solution)/shard_map/ppermute | solution.py:212
  72.8 7.4 %collective-permute-start.22 = (f32[128,384]{1,0:T(8,128)S(1)}, f32[128,384]{1,0:T(8,128)S(1)}, u32[]{:S(2)}, u32[]{:S(2)}) collective-permute-start(f32[128,384]{1,0:T(8,128)S(1)} %get-tuple-element.94), channel_id=1, source_target_pairs={{0,2},{1,3},{2,0},{3,1},{4,6},{5,7},{6,4},{7,5},{8,10},{9,11},{10,... | collective-permute-start | bytes 589832 | tf_op jit(solution)/shard_map/ppermute | solution.py:212
  76.3 15.4 %collective-permute-start.19 = (f32[256,384]{1,0:T(8,128)S(1)}, f32[256,384]{1,0:T(8,128)S(1)}, u32[]{:S(2)}, u32[]{:S(2)}) collective-permute-start(f32[256,384]{1,0:T(8,128)S(1)} %get-tuple-element.86), channel_id=1, source_target_pairs={{0,2},{1,3},{2,0},{3,1},{4,6},{5,7},{6,4},{7,5},{8,10},{9,11},{10,... | collective-permute-start | bytes 1179656 | tf_op jit(solution)/shard_map/ppermute | solution.py:212
  77.8 13.9 %collective-permute-start.20 = (f32[256,384]{1,0:T(8,128)S(1)}, f32[256,384]{1,0:T(8,128)S(1)}, u32[]{:S(2)}, u32[]{:S(2)}) collective-permute-start(f32[256,384]{1,0:T(8,128)S(1)} %get-tuple-element.87), channel_id=1, source_target_pairs={{0,4},{1,5},{2,6},{3,7},{4,0},{5,1},{6,2},{7,3},{8,12},{9,13},{10,... | collective-permute-start | bytes 1179656 | tf_op jit(solution)/shard_map/ppermute | solution.py:212
  79.1 11.7 %collective-permute-start.21 = (f32[128,384]{1,0:T(8,128)S(1)}, f32[128,384]{1,0:T(8,128)S(1)}, u32[]{:S(2)}, u32[]{:S(2)}) collective-permute-start(f32[128,384]{1,0:T(8,128)S(1)} %get-tuple-element.93), channel_id=1, source_target_pairs={{0,4},{1,5},{2,6},{3,7},{4,0},{5,1},{6,2},{7,3},{8,12},{9,13},{10,... | collective-permute-start | bytes 589832 | tf_op jit(solution)/shard_map/ppermute | solution.py:212
  80.2 10.7 %collective-permute-start.23 = (f32[128,384]{1,0:T(8,128)S(1)}, f32[128,384]{1,0:T(8,128)S(1)}, u32[]{:S(2)}, u32[]{:S(2)}) collective-permute-start(f32[128,384]{1,0:T(8,128)S(1)} %fold.19), channel_id=1, source_target_pairs={{0,1},{1,0},{2,3},{3,2},{4,5},{5,4},{6,7},{7,6},{8,9},{9,8},{10,11... | collective-permute-start | bytes 589832 | tf_op jit(solution)/shard_map/ppermute | solution.py:212
  93.2 15.2 %collective-permute-start.26 = (f32[256,384]{1,0:T(8,128)S(1)}, f32[256,384]{1,0:T(8,128)S(1)}, u32[]{:S(2)}, u32[]{:S(2)}) collective-permute-start(f32[256,384]{1,0:T(8,128)S(1)} %get-tuple-element.97), channel_id=1, source_target_pairs={{0,4},{1,5},{2,6},{3,7},{4,0},{5,1},{6,2},{7,3},{8,12},{9,13},{10,... | collective-permute-start | bytes 1179656 | tf_op jit(solution)/shard_map/ppermute | solution.py:212
  95.0 15.1 %collective-permute-start.24 = (f32[256,384]{1,0:T(8,128)S(1)}, f32[256,384]{1,0:T(8,128)S(1)}, u32[]{:S(2)}, u32[]{:S(2)}) collective-permute-start(f32[256,384]{1,0:T(8,128)S(1)} %get-tuple-element.96), channel_id=1, source_target_pairs={{0,2},{1,3},{2,0},{3,1},{4,6},{5,7},{6,4},{7,5},{8,10},{9,11},{10,... | collective-permute-start | bytes 1179656 | tf_op jit(solution)/shard_map/ppermute | solution.py:212
  95.5 12.7 %collective-permute-start.30 = (f32[128,384]{1,0:T(8,128)S(1)}, f32[128,384]{1,0:T(8,128)S(1)}, u32[]{:S(2)}, u32[]{:S(2)}) collective-permute-start(f32[128,384]{1,0:T(8,128)S(1)} %get-tuple-element.106), channel_id=1, source_target_pairs={{0,2},{1,3},{2,0},{3,1},{4,6},{5,7},{6,4},{7,5},{8,10},{9,11},{10,... | collective-permute-start | bytes 589832 | tf_op jit(solution)/shard_map/ppermute | solution.py:212
  97.0 13.7 %collective-permute-start.29 = (f32[128,384]{1,0:T(8,128)S(1)}, f32[128,384]{1,0:T(8,128)S(1)}, u32[]{:S(2)}, u32[]{:S(2)}) collective-permute-start(f32[128,384]{1,0:T(8,128)S(1)} %get-tuple-element.105), channel_id=1, source_target_pairs={{0,4},{1,5},{2,6},{3,7},{4,0},{5,1},{6,2},{7,3},{8,12},{9,13},{10,... | collective-permute-start | bytes 589832 | tf_op jit(solution)/shard_map/ppermute | solution.py:212
  108.3 2.5 %collective-permute-start.31 = (f32[128,384]{1,0:T(8,128)S(1)}, f32[128,384]{1,0:T(8,128)S(1)}, u32[]{:S(2)}, u32[]{:S(2)}) collective-permute-start(f32[128,384]{1,0:T(8,128)S(1)} %fold.23), channel_id=1, source_target_pairs={{0,1},{1,0},{2,3},{3,2},{4,5},{5,4},{6,7},{7,6},{8,9},{9,8},{10,11... | collective-permute-start | bytes 589832 | tf_op jit(solution)/shard_map/ppermute | solution.py:212
  108.4 3.1 %collective-permute-start.27 = (f32[128,384]{1,0:T(8,128)S(1)}, f32[128,384]{1,0:T(8,128)S(1)}, u32[]{:S(2)}, u32[]{:S(2)}) collective-permute-start(f32[128,384]{1,0:T(8,128)S(1)} %get-tuple-element.103), channel_id=1, source_target_pairs={{0,1},{1,0},{2,3},{3,2},{4,5},{5,4},{6,7},{7,6},{8,9},{9,8},{10,11... | collective-permute-start | bytes 589832 | tf_op jit(solution)/shard_map/ppermute | solution.py:212
  109.0 6.9 %collective-permute-start.28 = (f32[128,384]{1,0:T(8,128)S(1)}, f32[128,384]{1,0:T(8,128)S(1)}, u32[]{:S(2)}, u32[]{:S(2)}) collective-permute-start(f32[128,384]{1,0:T(8,128)S(1)} %get-tuple-element.104), channel_id=1, source_target_pairs={{0,3},{1,2},{2,1},{3,0},{4,7},{5,6},{6,5},{7,4},{8,11},{9,10},{10,... | collective-permute-start | bytes 589832 | tf_op jit(solution)/shard_map/ppermute | solution.py:212
  110.2 7.3 %collective-permute-start.25 = (f32[128,384]{1,0:T(8,128)S(1)}, f32[128,384]{1,0:T(8,128)S(1)}, u32[]{:S(2)}, u32[]{:S(2)}) collective-permute-start(f32[128,384]{1,0:T(8,128)S(1)} %get-tuple-element.101), channel_id=1, source_target_pairs={{0,4},{1,5},{2,6},{3,7},{4,0},{5,1},{6,2},{7,3},{8,12},{9,13},{10,... | collective-permute-start | bytes 589832 | tf_op jit(solution)/shard_map/ppermute | solution.py:212

commit v20 on v18

--- a/solution.py
+++ b/solution.py
@@ -233,6 +233,7 @@
     out = None
     token = None
     settled = []
+    late = []
     for n, (d, block, offset) in enumerate(blocks):
         if isinstance(block, tuple):
             middle, centre, far = block
@@ -250,12 +251,20 @@
                 stays = [i for i, r in enumerate(names[h]) if not r & bit]
                 goes = [i for i, r in enumerate(names[h]) if r & bit]
                 held[h], moved = fold(rows, stays, goes, held[h], moving[h])
-                moving[h] = swap(moved, 2 * bit)
+                across = n + 2 >= n_occ and level + 1 == len(bits)
+                moving[h] = swap(moved, 2 * bit + (h if across else 0))
                 names[h] = [names[h][i] for i in stays]
         token = held if out is None else [*held, out]
         settled = moving if n == 0 else []
+        if n + 2 >= n_occ:
+            late.append((d, held[0], moving, swap(held[1], 1), token))
+            continue
         (theirs,) = fold(rows, [0], [], held[1], moving[1])
         out = write(out, (rows, n_occ * width), d, half, offset, held[0], moving[0], swap(theirs, 1))
+    for i, (d, held_mine, moving, theirs, _) in enumerate(late):
+        got = lax.optimization_barrier((*moving, theirs, *(late[1][4] if i == 0 else [])))[:3]
+        (other,) = fold(rows, [0], [], got[2], got[1])
+        out = write(out, (rows, n_occ * width), d, half, 0, held_mine, got[0], other)
     return out
 
 

time: 119 us -> 115 us (0.966)
  Pallas kernels: 24.5 us -> 20.5 us
  starting transfers between devices: 34.7 us -> 32.7 us
  waiting for transfers between devices: 56.5 us -> 58.1 us
    pallas_call x23, Pallas kernels: 21.4 us -> 17.3 us  [kernel_call(): pl.pallas_call(body, out_shape=[pltpu.VMEM(shape, jnp.float32) for shape...]
    ppermute x28, starting transfers between devices: 24.3 us -> 22.3 us  [swap(): return lax.ppermute(x, 'vir', [(i, i ^ bits) for i in range(n_vir)])]
    ppermute x28, waiting for transfers between devices: 50.8 us -> 52.4 us  [swap(): return lax.ppermute(x, 'vir', [(i, i ^ bits) for i in range(n_vir)])]
  transfers between devices with their start and end apart: 32 -> 32, of which waited for: 13 -> 13; matrix products, arithmetic and copies ran while one was open for 1% -> 1% of each run, Pallas kernels for 18% -> 15%
where the time goes in v20:
time: 115 us; the launch traced here: 114 us
  waiting for transfers between devices  58.1 us (51%)
  starting transfers between devices  32.7 us (28%)
  Pallas kernels  20.5 us (18%)
  other arithmetic  1.53 us (1%)
    ppermute x28, waiting for transfers between devices, swap(): return lax.ppermute(x, 'vir', [(i, i ^ bits) for i in range(n_vir)])  52.4 us
    ppermute x28, starting transfers between devices, swap(): return lax.ppermute(x, 'vir', [(i, i ^ bits) for i in range(n_vir)])  22.3 us
    pallas_call x23, Pallas kernels, kernel_call(): pl.pallas_call(body, out_shape=[pltpu.VMEM(shape, jnp.float32) for shape...  17.3 us
    ppermute x1, starting transfers between devices, line_blocks(): far = lax.ppermute(after(own, centre, near), 'occ', [(0, 3), (3, 0)])  5.66 us
    ppermute x1, waiting for transfers between devices, direct(): return lax.ppermute(x, 'occ', [(i, i ^ d) for i in range(nodes)])  5.65 us
    pallas_call x4, Pallas kernels, write(): pl.pallas_call(functools.partial(write_kernel, d, half, offset), out_shap...  3.13 us
    ppermute x1, starting transfers between devices, direct(): return lax.ppermute(x, 'occ', [(i, i ^ d) for i in range(nodes)])  3.01 us
  transfers between devices with their start and end apart: 32, of which 13 were waited for; matrix products, arithmetic and copies ran while one was open for 1% of the time, Pallas kernels for 15%

profile of v20, /device:TPU:0, one launch (start us, length us, event | category | flops | bytes accessed | tf_op | source)
XLA Modules:
  0.0 114.3 jit_solution(12557071061088600931)
XLA Ops:
  0.0 1.3 %halves.1 = (f32[384,384]{1,0:T(8,128)S(1)}, f32[384,384]{1,0:T(8,128)S(1)}) custom-call(s32[3,6]{1,0:T(4,128)} %mask_hbm.1, f32[384,768]{1,0:T(8,128)} %int_hbm.1), custom_call_target="tpu_custom_call" | custom-call | flops 1 | bytes 1 | tf_op jit(solution)/shard_map/halves/pallas_call | solution.py:30
  1.3 0.5 collective-permute-start.5
  1.8 1.4 %cut.1 = (f32[128,768]{1,0:T(8,128)S(1)}, f32[128,768]{1,0:T(8,128)S(1)}, f32[128,768]{1,0:T(8,128)S(1)}, f32[128,768]{1,0:T(8,128)S(1)}) custom-call(s32[4,24]{1,0:T(4,128)} %mask_hbm.2, f32[128,3072]{1,0:T(8,128)} %amp_hbm.1), custom_call_target="tpu_custom_call" | custom-call | flops 1 | bytes 1 | tf_op jit(solution)/shard_map/cut/pallas_call | solution.py:30
  3.3 0.2 collective-permute-done.5.other_ref
  3.5 0.1 join.1.refs_4_
  3.6 3.0 %collective-permute-start.8 = (f32[768,384]{1,0:T(8,128)S(1)}, f32[768,384]{1,0:T(8,128)S(1)}, u32[]{:S(2)}, u32[]{:S(2)}) collective-permute-start(f32[768,384]{1,0:T(8,128)S(1)} %join.1.refs_4_), channel_id=1, source_target_pairs={{0,8},{8,0},{16,24},{24,16},{1,9},{9,1},{17,25},{25,17},{2,10},{10... | collective-permute-start | bytes 3538952 | tf_op jit(solution)/shard_map/ppermute | solution.py:192
  6.6 0.7 collective-permute-start.6
  7.3 1.6 %collective-permute-start = (f32[128,768]{1,0:T(8,128)S(1)}, f32[128,768]{1,0:T(8,128)S(1)}, u32[]{:S(2)}, u32[]{:S(2)}) collective-permute-start(f32[128,768]{1,0:T(8,128)S(1)} %get-tuple-element.65), channel_id=1, source_target_pairs={{0,4},{1,5},{2,6},{3,7},{4,0},{5,1},{6,2},{7,3},{8,12},{9,13},{10,... | collective-permute-start | bytes 1179656 | tf_op jit(solution)/shard_map/ppermute | solution.py:212
  8.9 1.4 %collective-permute-start.1 = (f32[128,768]{1,0:T(8,128)S(1)}, f32[128,768]{1,0:T(8,128)S(1)}, u32[]{:S(2)}, u32[]{:S(2)}) collective-permute-start(f32[128,768]{1,0:T(8,128)S(1)} %get-tuple-element.66), channel_id=1, source_target_pairs={{0,6},{1,7},{2,4},{3,5},{4,2},{5,3},{6,0},{7,1},{8,14},{9,15},{10,... | collective-permute-start | bytes 1179656 | tf_op jit(solution)/shard_map/ppermute | solution.py:212
  10.3 0.5 collective-permute-start.3
  10.9 15.8 %collective-permute-done.refs_1_ = f32[128,768]{1,0:T(8,128)S(1)} collective-permute-done((f32[128,768]{1,0:T(8,128)S(1)}, f32[128,768]{1,0:T(8,128)S(1)}, u32[]{:S(2)}, u32[]{:S(2)}) %collective-permute-start) | collective-permute-done | bytes 393248 | tf_op jit(solution)/shard_map/ppermute | solution.py:212
  26.7 0.0 collective-permute-start.10
  26.7 0.0 collective-permute-done.1.refs_1_
  26.7 0.5 collective-permute-start.11
  27.2 5.7 %collective-permute-done.8.refs_4_ = f32[768,384]{1,0:T(8,128)S(1)} collective-permute-done((f32[768,384]{1,0:T(8,128)S(1)}, f32[768,384]{1,0:T(8,128)S(1)}, u32[]{:S(2)}, u32[]{:S(2)}) %collective-permute-start.8) | collective-permute-done | bytes 1179680 | tf_op jit(solution)/shard_map/ppermute | solution.py:192
  32.8 1.0 copy-done.4
  33.9 0.0 collective-permute-done.6
  33.9 5.7 %collective-permute-start.9 = (f32[768,384]{1,0:T(8,128)S(1)}, f32[768,384]{1,0:T(8,128)}, u32[]{:S(2)}, u32[]{:S(2)}) collective-permute-start(f32[768,384]{1,0:T(8,128)S(1)} %join.1.refs_4_), channel_id=1, source_target_pairs={{0,24},{24,0},{1,25},{25,1},{2,26},{26,2},{3,27},{27,3},{4,28},{28... | collective-permute-start | bytes 3538952 | tf_op jit(solution)/shard_map/ppermute | solution.py:198
  39.5 0.1 collective-permute-start.2
  39.6 0.5 collective-permute-start.4
  40.1 2.2 %products.8 = (f32[256,384]{1,0:T(8,128)}, f32[256,384]{1,0:T(8,128)}) custom-call(f32[128,768]{1,0:T(8,128)S(1)} %collective-permute-done.3.refs_0_, f32[128,768]{1,0:T(8,128)S(1)} %collective-permute-done.1.refs_1_, f32[128,768]{1,0:T(8,128)S(1)} %collective-permute-done.10.refs_2_, f32[128,768]{1,0:T(8,128)S(1)} %collective-permute-done.11.refs_3_, ...), custom_call_target="tpu_custom_call" | custom-call | flops 1 | bytes 1 | tf_op jit(solution)/shard_map/products/pallas_call | solution.py:30
  42.3 1.6 %collective-permute-start.13 = (f32[256,384]{1,0:T(8,128)}, f32[256,384]{1,0:T(8,128)}, u32[]{:S(2)}, u32[]{:S(2)}) collective-permute-start(f32[256,384]{1,0:T(8,128)} %get-tuple-element.73), channel_id=1, source_target_pairs={{0,4},{1,5},{2,6},{3,7},{4,0},{5,1},{6,2},{7,3},{8,12},{9,13},{10,... | collective-permute-start | bytes 1179656 | tf_op jit(solution)/shard_map/ppermute | solution.py:212
  43.9 1.5 %collective-permute-start.12 = (f32[256,384]{1,0:T(8,128)}, f32[256,384]{1,0:T(8,128)}, u32[]{:S(2)}, u32[]{:S(2)}) collective-permute-start(f32[256,384]{1,0:T(8,128)} %get-tuple-element.72), channel_id=1, source_target_pairs={{0,2},{1,3},{2,0},{3,1},{4,6},{5,7},{6,4},{7,5},{8,10},{9,11},{10,... | collective-permute-start | bytes 1179656 | tf_op jit(solution)/shard_map/ppermute | solution.py:212
  45.4 1.4 %products.9 = (f32[256,384]{1,0:T(8,128)S(1)}, f32[256,384]{1,0:T(8,128)S(1)}) custom-call(f32[128,768]{1,0:T(8,128)S(1)} %get-tuple-element.67.refs_0_, f32[128,768]{1,0:T(8,128)S(1)} %collective-permute-done.refs_1_, f32[128,768]{1,0:T(8,128)S(1)} %collective-permute-done.2.refs_2_, f32[128,768]{1,0:T(8,128)S(1)} %collective-permute-done.4.refs_3_, ...), custom_call_target="tpu_custom_call" | custom-call | flops 1 | bytes 1 | tf_op jit(solution)/shard_map/products/pallas_call | solution.py:30
  46.8 7.0 %collective-permute-done.13.got_ref = f32[256,384]{1,0:T(8,128)} collective-permute-done((f32[256,384]{1,0:T(8,128)}, f32[256,384]{1,0:T(8,128)}, u32[]{:S(2)}, u32[]{:S(2)}) %collective-permute-start.13) | collective-permute-done | bytes 393248 | tf_op jit(solution)/shard_map/ppermute | solution.py:212
  53.8 1.0 fold.13
  54.9 1.6 %collective-permute-start.15 = (f32[128,384]{1,0:T(8,128)S(1)}, f32[128,384]{1,0:T(8,128)S(1)}, u32[]{:S(2)}, u32[]{:S(2)}) collective-permute-start(f32[128,384]{1,0:T(8,128)S(1)} %get-tuple-element.85), channel_id=1, source_target_pairs={{0,2},{1,3},{2,0},{3,1},{4,6},{5,7},{6,4},{7,5},{8,10},{9,11},{10,... | collective-permute-start | bytes 589832 | tf_op jit(solution)/shard_map/ppermute | solution.py:212
  56.4 0.1 broadcast_select_fusion.1
  56.6 1.1 collective-permute-start.7
  57.6 1.1 fold.12
  58.7 1.6 %collective-permute-start.14 = (f32[128,384]{1,0:T(8,128)S(1)}, f32[128,384]{1,0:T(8,128)S(1)}, u32[]{:S(2)}, u32[]{:S(2)}) collective-permute-start(f32[128,384]{1,0:T(8,128)S(1)} %get-tuple-element.84), channel_id=1, source_target_pairs={{0,4},{1,5},{2,6},{3,7},{4,0},{5,1},{6,2},{7,3},{8,12},{9,13},{10,... | collective-permute-start | bytes 589832 | tf_op jit(solution)/shard_map/ppermute | solution.py:212
  60.3 1.4 %products.10 = (f32[256,384]{1,0:T(8,128)S(1)}, f32[256,384]{1,0:T(8,128)S(1)}) custom-call(f32[128,768]{1,0:T(8,128)S(1)} %collective-permute-done.3.refs_0_, f32[128,768]{1,0:T(8,128)S(1)} %collective-permute-done.1.refs_1_, f32[128,768]{1,0:T(8,128)S(1)} %copy-done.1, f32[128,768]{1,0:T(8,128)S(1)} %copy-done.3, f32[768,384]{1,0:T(8,128)S(1)} %copy-done.5), custom_call_target="tpu_custom_call" | custom-call | flops 1 | bytes 1 | tf_op jit(solution)/shard_map/products/pallas_call | solution.py:30
  61.7 0.6 collective-permute-start.17
  62.3 0.5 collective-permute-start.16
  62.8 3.4 %collective-permute-done.14.got_ref = f32[128,384]{1,0:T(8,128)S(1)} collective-permute-done((f32[128,384]{1,0:T(8,128)S(1)}, f32[128,384]{1,0:T(8,128)S(1)}, u32[]{:S(2)}, u32[]{:S(2)}) %collective-permute-start.14) | collective-permute-done | bytes 196640 | tf_op jit(solution)/shard_map/ppermute | solution.py:212
  66.2 1.4 %collective-permute-done.18.other_ref = f32[128,384]{1,0:T(8,128)S(1)} collective-permute-done((f32[128,384]{1,0:T(8,128)S(1)}, f32[128,384]{1,0:T(8,128)S(1)}, u32[]{:S(2)}, u32[]{:S(2)}) %collective-permute-start.18) | collective-permute-done | bytes 196640 | tf_op jit(solution)/shard_map/ppermute | solution.py:212
  67.7 0.8 write.4.refs_0_
  68.4 1.4 %products.11 = (f32[256,384]{1,0:T(8,128)S(1)}, f32[256,384]{1,0:T(8,128)S(1)}) custom-call(f32[128,768]{1,0:T(8,128)S(1)} %get-tuple-element.67.refs_0_, f32[128,768]{1,0:T(8,128)S(1)} %collective-permute-done.refs_1_, f32[128,768]{1,0:T(8,128)S(1)} %collective-permute-done.2.refs_2_, f32[128,768]{1,0:T(8,128)S(1)} %collective-permute-done.4.refs_3_, ...), custom_call_target="tpu_custom_call" | custom-call | flops 1 | bytes 1 | tf_op jit(solution)/shard_map/products/pallas_call | solution.py:30
  69.9 3.0 %collective-permute-done.17.got_ref = f32[256,384]{1,0:T(8,128)S(1)} collective-permute-done((f32[256,384]{1,0:T(8,128)S(1)}, f32[256,384]{1,0:T(8,128)S(1)}, u32[]{:S(2)}, u32[]{:S(2)}) %collective-permute-start.17) | collective-permute-done | bytes 393248 | tf_op jit(solution)/shard_map/ppermute | solution.py:212
  72.9 0.6 collective-permute-start.22
  73.5 1.4 %broadcast_select_fusion.refs_4_ = f32[768,384]{1,0:T(8,128)S(1)} fusion(f32[768,384]{1,0:T(8,128)S(1)} %copy-done.7, f32[768,384]{1,0:T(8,128)} %collective-permute-done.9, pred[]{:T(512)S(6)} %or.3), kind=kLoop, calls=%fused_computation | loop fusion | flops 294912 | bytes 3538945 | tf_op jit(solution)/shard_map/jit(_where)/select_n | solution.py:241
  74.9 1.4 %products.12 = (f32[256,384]{1,0:T(8,128)S(1)}, f32[256,384]{1,0:T(8,128)S(1)}) custom-call(f32[128,768]{1,0:T(8,128)S(1)} %collective-permute-done.3.refs_0_, f32[128,768]{1,0:T(8,128)S(1)} %collective-permute-done.1.refs_1_, f32[128,768]{1,0:T(8,128)S(1)} %copy-done.1, f32[128,768]{1,0:T(8,128)S(1)} %copy-done.3, f32[768,384]{1,0:T(8,128)S(1)} %broadcast_select_fusion.refs_4_), custom_call_target="tpu_custom_call" | custom-call | flops 1 | bytes 1 | tf_op jit(solution)/shard_map/products/pallas_call | solution.py:30
  76.4 1.6 %collective-permute-start.19 = (f32[256,384]{1,0:T(8,128)S(1)}, f32[256,384]{1,0:T(8,128)S(1)}, u32[]{:S(2)}, u32[]{:S(2)}) collective-permute-start(f32[256,384]{1,0:T(8,128)S(1)} %get-tuple-element.92), channel_id=1, source_target_pairs={{0,2},{1,3},{2,0},{3,1},{4,6},{5,7},{6,4},{7,5},{8,10},{9,11},{10,... | collective-permute-start | bytes 1179656 | tf_op jit(solution)/shard_map/ppermute | solution.py:212
  77.9 1.3 %collective-permute-start.20 = (f32[256,384]{1,0:T(8,128)S(1)}, f32[256,384]{1,0:T(8,128)S(1)}, u32[]{:S(2)}, u32[]{:S(2)}) collective-permute-start(f32[256,384]{1,0:T(8,128)S(1)} %get-tuple-element.93), channel_id=1, source_target_pairs={{0,4},{1,5},{2,6},{3,7},{4,0},{5,1},{6,2},{7,3},{8,12},{9,13},{10,... | collective-permute-start | bytes 1179656 | tf_op jit(solution)/shard_map/ppermute | solution.py:212
  79.2 0.8 collective-permute-start.21
  80.0 0.3 collective-permute-done.22.got_ref
  80.3 0.1 collective-permute-start.23
  80.3 1.4 %products.13 = (f32[256,384]{1,0:T(8,128)S(1)}, f32[256,384]{1,0:T(8,128)S(1)}) custom-call(f32[128,768]{1,0:T(8,128)S(1)} %get-tuple-element.67.refs_0_, f32[128,768]{1,0:T(8,128)S(1)} %collective-permute-done.refs_1_, f32[128,768]{1,0:T(8,128)S(1)} %collective-permute-done.2.refs_2_, f32[128,768]{1,0:T(8,128)S(1)} %collective-permute-done.4.refs_3_, ...), custom_call_target="tpu_custom_call" | custom-call | flops 1 | bytes 1 | tf_op jit(solution)/shard_map/products/pallas_call | solution.py:30
  81.8 9.2 %collective-permute-done.21.got_ref = f32[128,384]{1,0:T(8,128)S(1)} collective-permute-done((f32[128,384]{1,0:T(8,128)S(1)}, f32[128,384]{1,0:T(8,128)S(1)}, u32[]{:S(2)}, u32[]{:S(2)}) %collective-permute-start.21) | collective-permute-done | bytes 196640 | tf_op jit(solution)/shard_map/ppermute | solution.py:212
  90.9 0.8 write.5.refs_0_
  91.8 1.4 %products.14 = (f32[256,384]{1,0:T(8,128)S(1)}, f32[256,384]{1,0:T(8,128)S(1)}) custom-call(f32[128,768]{1,0:T(8,128)S(1)} %collective-permute-done.3.refs_0_, f32[128,768]{1,0:T(8,128)S(1)} %collective-permute-done.1.refs_1_, f32[128,768]{1,0:T(8,128)S(1)} %copy-done.1, f32[128,768]{1,0:T(8,128)S(1)} %copy-done.3, f32[768,384]{1,0:T(8,128)S(1)} %collective-permute-done.7.refs_4_), custom_call_target="tpu_custom_call" | custom-call | flops 1 | bytes 1 | tf_op jit(solution)/shard_map/products/pallas_call | solution.py:30
  93.3 0.6 collective-permute-start.24
  93.9 0.9 collective-permute-start.26
  94.8 1.1 collective-permute-start.29
  95.9 1.6 %collective-permute-start.30 = (f32[128,384]{1,0:T(8,128)S(1)}, f32[128,384]{1,0:T(8,128)S(1)}, u32[]{:S(2)}, u32[]{:S(2)}) collective-permute-start(f32[128,384]{1,0:T(8,128)S(1)} %get-tuple-element.115), channel_id=1, source_target_pairs={{0,3},{1,2},{2,1},{3,0},{4,7},{5,6},{6,5},{7,4},{8,11},{9,10},{10,... | collective-permute-start | bytes 589832 | tf_op jit(solution)/shard_map/ppermute | solution.py:212
  97.5 1.4 %products.15 = (f32[256,384]{1,0:T(8,128)S(1)}, f32[256,384]{1,0:T(8,128)S(1)}) custom-call(f32[128,768]{1,0:T(8,128)S(1)} %get-tuple-element.67.refs_0_, f32[128,768]{1,0:T(8,128)S(1)} %collective-permute-done.refs_1_, f32[128,768]{1,0:T(8,128)S(1)} %collective-permute-done.2.refs_2_, f32[128,768]{1,0:T(8,128)S(1)} %collective-permute-done.4.refs_3_, ...), custom_call_target="tpu_custom_call" | custom-call | flops 1 | bytes 1 | tf_op jit(solution)/shard_map/products/pallas_call | solution.py:30
  98.9 6.1 %collective-permute-done.24.got_ref = f32[256,384]{1,0:T(8,128)S(1)} collective-permute-done((f32[256,384]{1,0:T(8,128)S(1)}, f32[256,384]{1,0:T(8,128)S(1)}, u32[]{:S(2)}, u32[]{:S(2)}) %collective-permute-start.24) | collective-permute-done | bytes 393248 | tf_op jit(solution)/shard_map/ppermute | solution.py:212
  105.0 1.2 %collective-permute-start.25 = (f32[128,384]{1,0:T(8,128)S(1)}, f32[128,384]{1,0:T(8,128)S(1)}, u32[]{:S(2)}, u32[]{:S(2)}) collective-permute-start(f32[128,384]{1,0:T(8,128)S(1)} %get-tuple-element.107), channel_id=1, source_target_pairs={{0,4},{1,5},{2,6},{3,7},{4,0},{5,1},{6,2},{7,3},{8,12},{9,13},{10,... | collective-permute-start | bytes 589832 | tf_op jit(solution)/shard_map/ppermute | solution.py:212
  106.3 0.1 collective-permute-start.27
  106.4 3.8 %collective-permute-done.29.got_ref = f32[128,384]{1,0:T(8,128)S(1)} collective-permute-done((f32[128,384]{1,0:T(8,128)S(1)}, f32[128,384]{1,0:T(8,128)S(1)}, u32[]{:S(2)}, u32[]{:S(2)}) %collective-permute-start.29) | collective-permute-done | bytes 196640 | tf_op jit(solution)/shard_map/ppermute | solution.py:212
  110.2 0.8 write.6.refs_0_
  111.0 1.4 %collective-permute-done.25.got_ref = f32[128,384]{1,0:T(8,128)S(1)} collective-permute-done((f32[128,384]{1,0:T(8,128)S(1)}, f32[128,384]{1,0:T(8,128)S(1)}, u32[]{:S(2)}, u32[]{:S(2)}) %collective-permute-start.25) | collective-permute-done | bytes 196640 | tf_op jit(solution)/shard_map/ppermute | solution.py:212
  112.4 0.9 collective-permute-done.27.got_ref
  113.3 0.8 write.7
  (45 shorter events, 0.4 us)
Async XLA Ops:
  1.3 2.1 %collective-permute-start.5 = (f32[384,384]{1,0:T(8,128)S(1)}, f32[384,384]{1,0:T(8,128)S(1)}, u32[]{:S(2)}, u32[]{:S(2)}) collective-permute-start(f32[384,384]{1,0:T(8,128)S(1)} %get-tuple-element.69), channel_id=1, source_target_pairs={{0,1},{1,0},{2,3},{3,2},{4,5},{5,4},{6,7},{7,6},{8,9},{9,8},{10,11... | collective-permute-start | bytes 1769480 | tf_op jit(solution)/shard_map/ppermute | solution.py:212
  3.6 29.3 %collective-permute-start.8 = (f32[768,384]{1,0:T(8,128)S(1)}, f32[768,384]{1,0:T(8,128)S(1)}, u32[]{:S(2)}, u32[]{:S(2)}) collective-permute-start(f32[768,384]{1,0:T(8,128)S(1)} %join.1.refs_4_), channel_id=1, source_target_pairs={{0,8},{8,0},{16,24},{24,16},{1,9},{9,1},{17,25},{25,17},{2,10},{10... | collective-permute-start | bytes 3538952 | tf_op jit(solution)/shard_map/ppermute | solution.py:192
  6.6 27.3 %collective-permute-start.6 = (f32[768,384]{1,0:T(8,128)S(1)}, f32[768,384]{1,0:T(8,128)S(1)}, u32[]{:S(2)}, u32[]{:S(2)}) collective-permute-start(f32[768,384]{1,0:T(8,128)S(1)} %join.1.refs_4_), channel_id=1, source_target_pairs={{8,16},{16,8},{9,17},{17,9},{10,18},{18,10},{11,19},{19,11},{12,20... | collective-permute-start | bytes 3538952 | tf_op jit(solution)/shard_map/ppermute | solution.py:196
  7.3 19.4 %collective-permute-start = (f32[128,768]{1,0:T(8,128)S(1)}, f32[128,768]{1,0:T(8,128)S(1)}, u32[]{:S(2)}, u32[]{:S(2)}) collective-permute-start(f32[128,768]{1,0:T(8,128)S(1)} %get-tuple-element.65), channel_id=1, source_target_pairs={{0,4},{1,5},{2,6},{3,7},{4,0},{5,1},{6,2},{7,3},{8,12},{9,13},{10,... | collective-permute-start | bytes 1179656 | tf_op jit(solution)/shard_map/ppermute | solution.py:212
  8.9 17.8 %collective-permute-start.1 = (f32[128,768]{1,0:T(8,128)S(1)}, f32[128,768]{1,0:T(8,128)S(1)}, u32[]{:S(2)}, u32[]{:S(2)}) collective-permute-start(f32[128,768]{1,0:T(8,128)S(1)} %get-tuple-element.66), channel_id=1, source_target_pairs={{0,6},{1,7},{2,4},{3,5},{4,2},{5,3},{6,0},{7,1},{8,14},{9,15},{10,... | collective-permute-start | bytes 1179656 | tf_op jit(solution)/shard_map/ppermute | solution.py:212
  10.3 29.3 %collective-permute-start.3 = (f32[128,768]{1,0:T(8,128)S(1)}, f32[128,768]{1,0:T(8,128)S(1)}, u32[]{:S(2)}, u32[]{:S(2)}) collective-permute-start(f32[128,768]{1,0:T(8,128)S(1)} %get-tuple-element.68), channel_id=1, source_target_pairs={{0,2},{1,3},{2,0},{3,1},{4,6},{5,7},{6,4},{7,5},{8,10},{9,11},{10,... | collective-permute-start | bytes 1179656 | tf_op jit(solution)/shard_map/ppermute | solution.py:212
  26.7 13.5 %collective-permute-start.10 = (f32[128,768]{1,0:T(8,128)S(1)}, f32[128,768]{1,0:T(8,128)S(1)}, u32[]{:S(2)}, u32[]{:S(2)}) collective-permute-start(f32[128,768]{1,0:T(8,128)S(1)} %collective-permute-done.refs_1_), channel_id=1, source_target_pairs={{0,1},{1,0},{2,3},{3,2},{4,5},{5,4},{6,7},{7,6},{8,9},{9,8},{10,11... | collective-permute-start | bytes 1179656 | tf_op jit(solution)/shard_map/ppermute | solution.py:212
  26.7 13.5 %collective-permute-start.11 = (f32[128,768]{1,0:T(8,128)S(1)}, f32[128,768]{1,0:T(8,128)S(1)}, u32[]{:S(2)}, u32[]{:S(2)}) collective-permute-start(f32[128,768]{1,0:T(8,128)S(1)} %collective-permute-done.1.refs_1_), channel_id=1, source_target_pairs={{0,1},{1,0},{2,3},{3,2},{4,5},{5,4},{6,7},{7,6},{8,9},{9,8},{10,11... | collective-permute-start | bytes 1179656 | tf_op jit(solution)/shard_map/ppermute | solution.py:212
  32.8 1.0 copy-start.4
  33.9 8.4 %copy-start.6 = (f32[768,384]{1,0:T(8,128)}, f32[768,384]{1,0:T(8,128)S(1)}, u32[]{:S(2)}) copy-start(f32[768,384]{1,0:T(8,128)S(1)} %collective-permute-done.6) | copy-start | bytes 3538948
  33.9 39.7 %collective-permute-start.9 = (f32[768,384]{1,0:T(8,128)S(1)}, f32[768,384]{1,0:T(8,128)}, u32[]{:S(2)}, u32[]{:S(2)}) collective-permute-start(f32[768,384]{1,0:T(8,128)S(1)} %join.1.refs_4_), channel_id=1, source_target_pairs={{0,24},{24,0},{1,25},{25,1},{2,26},{26,2},{3,27},{27,3},{4,28},{28... | collective-permute-start | bytes 3538952 | tf_op jit(solution)/shard_map/ppermute | solution.py:198
  39.5 5.9 %collective-permute-start.2 = (f32[128,768]{1,0:T(8,128)S(1)}, f32[128,768]{1,0:T(8,128)S(1)}, u32[]{:S(2)}, u32[]{:S(2)}) collective-permute-start(f32[128,768]{1,0:T(8,128)S(1)} %get-tuple-element.67.refs_0_), channel_id=1, source_target_pairs={{0,1},{1,0},{2,3},{3,2},{4,5},{5,4},{6,7},{7,6},{8,9},{9,8},{10,11... | collective-permute-start | bytes 1179656 | tf_op jit(solution)/shard_map/ppermute | solution.py:212
  39.6 5.8 %collective-permute-start.4 = (f32[128,768]{1,0:T(8,128)S(1)}, f32[128,768]{1,0:T(8,128)S(1)}, u32[]{:S(2)}, u32[]{:S(2)}) collective-permute-start(f32[128,768]{1,0:T(8,128)S(1)} %collective-permute-done.3.refs_0_), channel_id=1, source_target_pairs={{0,1},{1,0},{2,3},{3,2},{4,5},{5,4},{6,7},{7,6},{8,9},{9,8},{10,11... | collective-permute-start | bytes 1179656 | tf_op jit(solution)/shard_map/ppermute | solution.py:212
  40.1 2.2 %copy-start = (f32[128,768]{1,0:T(8,128)}, f32[128,768]{1,0:T(8,128)S(1)}, u32[]{:S(2)}) copy-start(f32[128,768]{1,0:T(8,128)S(1)} %collective-permute-done.10.refs_2_) | copy-start | bytes 1179652
  40.1 2.2 %copy-start.2 = (f32[128,768]{1,0:T(8,128)}, f32[128,768]{1,0:T(8,128)S(1)}, u32[]{:S(2)}) copy-start(f32[128,768]{1,0:T(8,128)S(1)} %collective-permute-done.11.refs_3_) | copy-start | bytes 1179652
  42.3 11.5 %collective-permute-start.13 = (f32[256,384]{1,0:T(8,128)}, f32[256,384]{1,0:T(8,128)}, u32[]{:S(2)}, u32[]{:S(2)}) collective-permute-start(f32[256,384]{1,0:T(8,128)} %get-tuple-element.73), channel_id=1, source_target_pairs={{0,4},{1,5},{2,6},{3,7},{4,0},{5,1},{6,2},{7,3},{8,12},{9,13},{10,... | collective-permute-start | bytes 1179656 | tf_op jit(solution)/shard_map/ppermute | solution.py:212
  43.9 13.7 %collective-permute-start.12 = (f32[256,384]{1,0:T(8,128)}, f32[256,384]{1,0:T(8,128)}, u32[]{:S(2)}, u32[]{:S(2)}) collective-permute-start(f32[256,384]{1,0:T(8,128)} %get-tuple-element.72), channel_id=1, source_target_pairs={{0,2},{1,3},{2,0},{3,1},{4,6},{5,7},{6,4},{7,5},{8,10},{9,11},{10,... | collective-permute-start | bytes 1179656 | tf_op jit(solution)/shard_map/ppermute | solution.py:212
  45.4 11.0 %copy-start.7 = (f32[768,384]{1,0:T(8,128)S(1)}, f32[768,384]{1,0:T(8,128)}, u32[]{:S(2)}) copy-start(f32[768,384]{1,0:T(8,128)} %copy-done.6) | copy-start | bytes 3538948
  54.8 5.4 %copy-start.1 = (f32[128,768]{1,0:T(8,128)S(1)}, f32[128,768]{1,0:T(8,128)}, u32[]{:S(2)}) copy-start(f32[128,768]{1,0:T(8,128)} %copy-done) | copy-start | bytes 1179652
  54.9 5.4 %copy-start.3 = (f32[128,768]{1,0:T(8,128)S(1)}, f32[128,768]{1,0:T(8,128)}, u32[]{:S(2)}) copy-start(f32[128,768]{1,0:T(8,128)} %copy-done.2) | copy-start | bytes 1179652
  54.9 7.4 %collective-permute-start.15 = (f32[128,384]{1,0:T(8,128)S(1)}, f32[128,384]{1,0:T(8,128)S(1)}, u32[]{:S(2)}, u32[]{:S(2)}) collective-permute-start(f32[128,384]{1,0:T(8,128)S(1)} %get-tuple-element.85), channel_id=1, source_target_pairs={{0,2},{1,3},{2,0},{3,1},{4,6},{5,7},{6,4},{7,5},{8,10},{9,11},{10,... | collective-permute-start | bytes 589832 | tf_op jit(solution)/shard_map/ppermute | solution.py:212
  56.4 3.8 %copy-start.5 = (f32[768,384]{1,0:T(8,128)S(1)}, f32[768,384]{1,0:T(8,128)}, u32[]{:S(2)}) copy-start(f32[768,384]{1,0:T(8,128)} %copy-done.4) | copy-start | bytes 3538948
  56.6 35.3 %collective-permute-start.7 = (f32[768,384]{1,0:T(8,128)S(1)}, f32[768,384]{1,0:T(8,128)S(1)}, u32[]{:S(2)}, u32[]{:S(2)}) collective-permute-start(f32[768,384]{1,0:T(8,128)S(1)} %broadcast_select_fusion.1), channel_id=1, source_target_pairs={{8,0},{16,24},{0,16},{24,8},{9,1},{17,25},{1,17},{25,9},{10,2},{18... | collective-permute-start | bytes 3538952 | tf_op jit(solution)/shard_map/ppermute | solution.py:200
  58.7 7.5 %collective-permute-start.14 = (f32[128,384]{1,0:T(8,128)S(1)}, f32[128,384]{1,0:T(8,128)S(1)}, u32[]{:S(2)}, u32[]{:S(2)}) collective-permute-start(f32[128,384]{1,0:T(8,128)S(1)} %get-tuple-element.84), channel_id=1, source_target_pairs={{0,4},{1,5},{2,6},{3,7},{4,0},{5,1},{6,2},{7,3},{8,12},{9,13},{10,... | collective-permute-start | bytes 589832 | tf_op jit(solution)/shard_map/ppermute | solution.py:212
  61.7 11.1 %collective-permute-start.17 = (f32[256,384]{1,0:T(8,128)S(1)}, f32[256,384]{1,0:T(8,128)S(1)}, u32[]{:S(2)}, u32[]{:S(2)}) collective-permute-start(f32[256,384]{1,0:T(8,128)S(1)} %get-tuple-element.81), channel_id=1, source_target_pairs={{0,4},{1,5},{2,6},{3,7},{4,0},{5,1},{6,2},{7,3},{8,12},{9,13},{10,... | collective-permute-start | bytes 1179656 | tf_op jit(solution)/shard_map/ppermute | solution.py:212
  62.3 11.2 %collective-permute-start.16 = (f32[256,384]{1,0:T(8,128)S(1)}, f32[256,384]{1,0:T(8,128)S(1)}, u32[]{:S(2)}, u32[]{:S(2)}) collective-permute-start(f32[256,384]{1,0:T(8,128)S(1)} %get-tuple-element.80), channel_id=1, source_target_pairs={{0,2},{1,3},{2,0},{3,1},{4,6},{5,7},{6,4},{7,5},{8,10},{9,11},{10,... | collective-permute-start | bytes 1179656 | tf_op jit(solution)/shard_map/ppermute | solution.py:212
  66.2 1.4 %collective-permute-start.18 = (f32[128,384]{1,0:T(8,128)S(1)}, f32[128,384]{1,0:T(8,128)S(1)}, u32[]{:S(2)}, u32[]{:S(2)}) collective-permute-start(f32[128,384]{1,0:T(8,128)S(1)} %fold.16), channel_id=1, source_target_pairs={{0,1},{1,0},{2,3},{3,2},{4,5},{5,4},{6,7},{7,6},{8,9},{9,8},{10,11... | collective-permute-start | bytes 589832 | tf_op jit(solution)/shard_map/ppermute | solution.py:212
  72.9 7.4 %collective-permute-start.22 = (f32[128,384]{1,0:T(8,128)S(1)}, f32[128,384]{1,0:T(8,128)S(1)}, u32[]{:S(2)}, u32[]{:S(2)}) collective-permute-start(f32[128,384]{1,0:T(8,128)S(1)} %get-tuple-element.100), channel_id=1, source_target_pairs={{0,2},{1,3},{2,0},{3,1},{4,6},{5,7},{6,4},{7,5},{8,10},{9,11},{10,... | collective-permute-start | bytes 589832 | tf_op jit(solution)/shard_map/ppermute | solution.py:212
  76.4 15.3 %collective-permute-start.19 = (f32[256,384]{1,0:T(8,128)S(1)}, f32[256,384]{1,0:T(8,128)S(1)}, u32[]{:S(2)}, u32[]{:S(2)}) collective-permute-start(f32[256,384]{1,0:T(8,128)S(1)} %get-tuple-element.92), channel_id=1, source_target_pairs={{0,2},{1,3},{2,0},{3,1},{4,6},{5,7},{6,4},{7,5},{8,10},{9,11},{10,... | collective-permute-start | bytes 1179656 | tf_op jit(solution)/shard_map/ppermute | solution.py:212
  77.9 13.8 %collective-permute-start.20 = (f32[256,384]{1,0:T(8,128)S(1)}, f32[256,384]{1,0:T(8,128)S(1)}, u32[]{:S(2)}, u32[]{:S(2)}) collective-permute-start(f32[256,384]{1,0:T(8,128)S(1)} %get-tuple-element.93), channel_id=1, source_target_pairs={{0,4},{1,5},{2,6},{3,7},{4,0},{5,1},{6,2},{7,3},{8,12},{9,13},{10,... | collective-permute-start | bytes 1179656 | tf_op jit(solution)/shard_map/ppermute | solution.py:212
  79.2 11.7 %collective-permute-start.21 = (f32[128,384]{1,0:T(8,128)S(1)}, f32[128,384]{1,0:T(8,128)S(1)}, u32[]{:S(2)}, u32[]{:S(2)}) collective-permute-start(f32[128,384]{1,0:T(8,128)S(1)} %get-tuple-element.99), channel_id=1, source_target_pairs={{0,4},{1,5},{2,6},{3,7},{4,0},{5,1},{6,2},{7,3},{8,12},{9,13},{10,... | collective-permute-start | bytes 589832 | tf_op jit(solution)/shard_map/ppermute | solution.py:212
  80.3 10.7 %collective-permute-start.23 = (f32[128,384]{1,0:T(8,128)S(1)}, f32[128,384]{1,0:T(8,128)S(1)}, u32[]{:S(2)}, u32[]{:S(2)}) collective-permute-start(f32[128,384]{1,0:T(8,128)S(1)} %fold.19), channel_id=1, source_target_pairs={{0,1},{1,0},{2,3},{3,2},{4,5},{5,4},{6,7},{7,6},{8,9},{9,8},{10,11... | collective-permute-start | bytes 589832 | tf_op jit(solution)/shard_map/ppermute | solution.py:212
  93.3 11.7 %collective-permute-start.24 = (f32[256,384]{1,0:T(8,128)S(1)}, f32[256,384]{1,0:T(8,128)S(1)}, u32[]{:S(2)}, u32[]{:S(2)}) collective-permute-start(f32[256,384]{1,0:T(8,128)S(1)} %get-tuple-element.102), channel_id=1, source_target_pairs={{0,2},{1,3},{2,0},{3,1},{4,6},{5,7},{6,4},{7,5},{8,10},{9,11},{10,... | collective-permute-start | bytes 1179656 | tf_op jit(solution)/shard_map/ppermute | solution.py:212
  93.9 12.4 %collective-permute-start.26 = (f32[256,384]{1,0:T(8,128)S(1)}, f32[256,384]{1,0:T(8,128)S(1)}, u32[]{:S(2)}, u32[]{:S(2)}) collective-permute-start(f32[256,384]{1,0:T(8,128)S(1)} %get-tuple-element.103), channel_id=1, source_target_pairs={{0,4},{1,5},{2,6},{3,7},{4,0},{5,1},{6,2},{7,3},{8,12},{9,13},{10,... | collective-permute-start | bytes 1179656 | tf_op jit(solution)/shard_map/ppermute | solution.py:212
  94.8 15.4 %collective-permute-start.29 = (f32[128,384]{1,0:T(8,128)S(1)}, f32[128,384]{1,0:T(8,128)S(1)}, u32[]{:S(2)}, u32[]{:S(2)}) collective-permute-start(f32[128,384]{1,0:T(8,128)S(1)} %get-tuple-element.114), channel_id=1, source_target_pairs={{0,4},{1,5},{2,6},{3,7},{4,0},{5,1},{6,2},{7,3},{8,12},{9,13},{10,... | collective-permute-start | bytes 589832 | tf_op jit(solution)/shard_map/ppermute | solution.py:212
  95.9 14.2 %collective-permute-start.31 = (f32[128,384]{1,0:T(8,128)S(1)}, f32[128,384]{1,0:T(8,128)S(1)}, u32[]{:S(2)}, u32[]{:S(2)}) collective-permute-start(f32[128,384]{1,0:T(8,128)S(1)} %get-tuple-element.98), channel_id=1, source_target_pairs={{0,1},{1,0},{2,3},{3,2},{4,5},{5,4},{6,7},{7,6},{8,9},{9,8},{10,11... | collective-permute-start | bytes 589832 | tf_op jit(solution)/shard_map/ppermute | solution.py:212
  95.9 14.2 %collective-permute-start.30 = (f32[128,384]{1,0:T(8,128)S(1)}, f32[128,384]{1,0:T(8,128)S(1)}, u32[]{:S(2)}, u32[]{:S(2)}) collective-permute-start(f32[128,384]{1,0:T(8,128)S(1)} %get-tuple-element.115), channel_id=1, source_target_pairs={{0,3},{1,2},{2,1},{3,0},{4,7},{5,6},{6,5},{7,4},{8,11},{9,10},{10,... | collective-permute-start | bytes 589832 | tf_op jit(solution)/shard_map/ppermute | solution.py:212
  105.0 7.4 %collective-permute-start.25 = (f32[128,384]{1,0:T(8,128)S(1)}, f32[128,384]{1,0:T(8,128)S(1)}, u32[]{:S(2)}, u32[]{:S(2)}) collective-permute-start(f32[128,384]{1,0:T(8,128)S(1)} %get-tuple-element.107), channel_id=1, source_target_pairs={{0,4},{1,5},{2,6},{3,7},{4,0},{5,1},{6,2},{7,3},{8,12},{9,13},{10,... | collective-permute-start | bytes 589832 | tf_op jit(solution)/shard_map/ppermute | solution.py:212
  106.3 7.0 %collective-permute-start.27 = (f32[128,384]{1,0:T(8,128)S(1)}, f32[128,384]{1,0:T(8,128)S(1)}, u32[]{:S(2)}, u32[]{:S(2)}) collective-permute-start(f32[128,384]{1,0:T(8,128)S(1)} %get-tuple-element.109), channel_id=1, source_target_pairs={{0,3},{1,2},{2,1},{3,0},{4,7},{5,6},{6,5},{7,4},{8,11},{9,10},{10,... | collective-permute-start | bytes 589832 | tf_op jit(solution)/shard_map/ppermute | solution.py:212
  110.1 3.1 %collective-permute-start.28 = (f32[128,384]{1,0:T(8,128)S(1)}, f32[128,384]{1,0:T(8,128)S(1)}, u32[]{:S(2)}, u32[]{:S(2)}) collective-permute-start(f32[128,384]{1,0:T(8,128)S(1)} %get-tuple-element.110), channel_id=1, source_target_pairs={{0,1},{1,0},{2,3},{3,2},{4,5},{5,4},{6,7},{7,6},{8,9},{9,8},{10,11... | collective-permute-start | bytes 589832 | tf_op jit(solution)/shard_map/ppermute | solution.py:212

commit v21 on v20

--- a/solution.py
+++ b/solution.py
@@ -254,7 +254,7 @@
                 across = n + 2 >= n_occ and level + 1 == len(bits)
                 moving[h] = swap(moved, 2 * bit + (h if across else 0))
                 names[h] = [names[h][i] for i in stays]
-        token = held if out is None else [*held, out]
+        token = [*held, out] if n == 1 else [*held]
         settled = moving if n == 0 else []
         if n + 2 >= n_occ:
             late.append((d, held[0], moving, swap(held[1], 1), token))

time: 115 us -> 123 us (1.070)
  waiting for transfers between devices: 58.1 us -> 65.7 us
    ppermute x1, waiting for transfers between devices: 0.01 us -> 4.85 us  [line_blocks(): lax.ppermute(jnp.where(middle, centre, own), 'occ', [(1, 0), (2, 3), (0,...]
    ppermute x28, waiting for transfers between devices: 52.4 us -> 55.2 us  [swap(): return lax.ppermute(x, 'vir', [(i, i ^ bits) for i in range(n_vir)])]
  transfers between devices with their start and end apart: 32 -> 32, of which waited for: 13 -> 15; matrix products, arithmetic and copies ran while one was open for 1% -> 1% of each run, Pallas kernels for 15% -> 14%
where the time goes in v21:
time: 123 us; the launch traced here: 122 us
  waiting for transfers between devices  65.7 us (53%)
  starting transfers between devices  33.1 us (27%)
  Pallas kernels  20.4 us (17%)
  other arithmetic  1.53 us (1%)
    ppermute x28, waiting for transfers between devices, swap(): return lax.ppermute(x, 'vir', [(i, i ^ bits) for i in range(n_vir)])  55.2 us
    ppermute x28, starting transfers between devices, swap(): return lax.ppermute(x, 'vir', [(i, i ^ bits) for i in range(n_vir)])  22.6 us
    pallas_call x23, Pallas kernels, kernel_call(): pl.pallas_call(body, out_shape=[pltpu.VMEM(shape, jnp.float32) for shape...  17.3 us
    ppermute x1, starting transfers between devices, line_blocks(): far = lax.ppermute(after(own, centre, near), 'occ', [(0, 3), (3, 0)])  5.66 us
    ppermute x1, waiting for transfers between devices, direct(): return lax.ppermute(x, 'occ', [(i, i ^ d) for i in range(nodes)])  5.65 us
    ppermute x1, waiting for transfers between devices, line_blocks(): lax.ppermute(jnp.where(middle, centre, own), 'occ', [(1, 0), (2, 3), (0,...  4.85 us
    pallas_call x4, Pallas kernels, write(): pl.pallas_call(functools.partial(write_kernel, d, half, offset), out_shap...  3.13 us
    ppermute x1, starting transfers between devices, direct(): return lax.ppermute(x, 'occ', [(i, i ^ d) for i in range(nodes)])  3.01 us
  transfers between devices with their start and end apart: 32, of which 15 were waited for; matrix products, arithmetic and copies ran while one was open for 1% of the time, Pallas kernels for 14%

profile of v21, /device:TPU:0, one launch (start us, length us, event | category | flops | bytes accessed | tf_op | source)
XLA Modules:
  0.0 122.2 jit_solution(18378346454790678222)
XLA Ops:
  0.0 1.3 %halves.1 = (f32[384,384]{1,0:T(8,128)S(1)}, f32[384,384]{1,0:T(8,128)S(1)}) custom-call(s32[3,6]{1,0:T(4,128)} %mask_hbm.1, f32[384,768]{1,0:T(8,128)} %int_hbm.1), custom_call_target="tpu_custom_call" | custom-call | flops 1 | bytes 1 | tf_op jit(solution)/shard_map/halves/pallas_call | solution.py:30
  1.3 0.5 collective-permute-start.5
  1.8 1.4 %cut.1 = (f32[128,768]{1,0:T(8,128)S(1)}, f32[128,768]{1,0:T(8,128)S(1)}, f32[128,768]{1,0:T(8,128)S(1)}, f32[128,768]{1,0:T(8,128)S(1)}) custom-call(s32[4,24]{1,0:T(4,128)} %mask_hbm.2, f32[128,3072]{1,0:T(8,128)} %amp_hbm.1), custom_call_target="tpu_custom_call" | custom-call | flops 1 | bytes 1 | tf_op jit(solution)/shard_map/cut/pallas_call | solution.py:30
  3.3 0.2 collective-permute-done.5.other_ref
  3.5 0.1 join.1.refs_4_
  3.6 3.0 %collective-permute-start.8 = (f32[768,384]{1,0:T(8,128)S(1)}, f32[768,384]{1,0:T(8,128)S(1)}, u32[]{:S(2)}, u32[]{:S(2)}) collective-permute-start(f32[768,384]{1,0:T(8,128)S(1)} %join.1.refs_4_), channel_id=1, source_target_pairs={{0,8},{8,0},{16,24},{24,16},{1,9},{9,1},{17,25},{25,17},{2,10},{10... | collective-permute-start | bytes 3538952 | tf_op jit(solution)/shard_map/ppermute | solution.py:192
  6.6 0.7 collective-permute-start.6
  7.3 1.6 %collective-permute-start = (f32[128,768]{1,0:T(8,128)S(1)}, f32[128,768]{1,0:T(8,128)S(1)}, u32[]{:S(2)}, u32[]{:S(2)}) collective-permute-start(f32[128,768]{1,0:T(8,128)S(1)} %get-tuple-element.65), channel_id=1, source_target_pairs={{0,4},{1,5},{2,6},{3,7},{4,0},{5,1},{6,2},{7,3},{8,12},{9,13},{10,... | collective-permute-start | bytes 1179656 | tf_op jit(solution)/shard_map/ppermute | solution.py:212
  8.9 1.4 %collective-permute-start.1 = (f32[128,768]{1,0:T(8,128)S(1)}, f32[128,768]{1,0:T(8,128)S(1)}, u32[]{:S(2)}, u32[]{:S(2)}) collective-permute-start(f32[128,768]{1,0:T(8,128)S(1)} %get-tuple-element.66), channel_id=1, source_target_pairs={{0,6},{1,7},{2,4},{3,5},{4,2},{5,3},{6,0},{7,1},{8,14},{9,15},{10,... | collective-permute-start | bytes 1179656 | tf_op jit(solution)/shard_map/ppermute | solution.py:212
  10.3 0.5 collective-permute-start.3
  10.9 15.8 %collective-permute-done.refs_1_ = f32[128,768]{1,0:T(8,128)S(1)} collective-permute-done((f32[128,768]{1,0:T(8,128)S(1)}, f32[128,768]{1,0:T(8,128)S(1)}, u32[]{:S(2)}, u32[]{:S(2)}) %collective-permute-start) | collective-permute-done | bytes 393248 | tf_op jit(solution)/shard_map/ppermute | solution.py:212
  26.7 0.5 collective-permute-start.11
  27.2 5.7 %collective-permute-done.8.refs_4_ = f32[768,384]{1,0:T(8,128)S(1)} collective-permute-done((f32[768,384]{1,0:T(8,128)S(1)}, f32[768,384]{1,0:T(8,128)S(1)}, u32[]{:S(2)}, u32[]{:S(2)}) %collective-permute-start.8) | collective-permute-done | bytes 1179680 | tf_op jit(solution)/shard_map/ppermute | solution.py:192
  32.8 1.0 copy-done.4
  33.9 5.7 %collective-permute-start.9 = (f32[768,384]{1,0:T(8,128)S(1)}, f32[768,384]{1,0:T(8,128)}, u32[]{:S(2)}, u32[]{:S(2)}) collective-permute-start(f32[768,384]{1,0:T(8,128)S(1)} %join.1.refs_4_), channel_id=1, source_target_pairs={{0,24},{24,0},{1,25},{25,1},{2,26},{26,2},{3,27},{27,3},{4,28},{28... | collective-permute-start | bytes 3538952 | tf_op jit(solution)/shard_map/ppermute | solution.py:198
  39.5 0.1 collective-permute-start.2
  39.6 0.5 collective-permute-start.4
  40.2 2.2 %products.8 = (f32[256,384]{1,0:T(8,128)}, f32[256,384]{1,0:T(8,128)}) custom-call(f32[128,768]{1,0:T(8,128)S(1)} %collective-permute-done.3.refs_0_, f32[128,768]{1,0:T(8,128)S(1)} %collective-permute-done.1.refs_1_, f32[128,768]{1,0:T(8,128)S(1)} %collective-permute-done.10.refs_2_, f32[128,768]{1,0:T(8,128)S(1)} %collective-permute-done.11.refs_3_, ...), custom_call_target="tpu_custom_call" | custom-call | flops 1 | bytes 1 | tf_op jit(solution)/shard_map/products/pallas_call | solution.py:30
  42.3 1.5 %collective-permute-start.13 = (f32[256,384]{1,0:T(8,128)}, f32[256,384]{1,0:T(8,128)}, u32[]{:S(2)}, u32[]{:S(2)}) collective-permute-start(f32[256,384]{1,0:T(8,128)} %get-tuple-element.73), channel_id=1, source_target_pairs={{0,4},{1,5},{2,6},{3,7},{4,0},{5,1},{6,2},{7,3},{8,12},{9,13},{10,... | collective-permute-start | bytes 1179656 | tf_op jit(solution)/shard_map/ppermute | solution.py:212
  43.8 1.5 %collective-permute-start.12 = (f32[256,384]{1,0:T(8,128)}, f32[256,384]{1,0:T(8,128)}, u32[]{:S(2)}, u32[]{:S(2)}) collective-permute-start(f32[256,384]{1,0:T(8,128)} %get-tuple-element.72), channel_id=1, source_target_pairs={{0,2},{1,3},{2,0},{3,1},{4,6},{5,7},{6,4},{7,5},{8,10},{9,11},{10,... | collective-permute-start | bytes 1179656 | tf_op jit(solution)/shard_map/ppermute | solution.py:212
  45.3 1.4 %products.9 = (f32[256,384]{1,0:T(8,128)S(1)}, f32[256,384]{1,0:T(8,128)S(1)}) custom-call(f32[128,768]{1,0:T(8,128)S(1)} %get-tuple-element.67.refs_0_, f32[128,768]{1,0:T(8,128)S(1)} %collective-permute-done.refs_1_, f32[128,768]{1,0:T(8,128)S(1)} %collective-permute-done.2.refs_2_, f32[128,768]{1,0:T(8,128)S(1)} %collective-permute-done.4.refs_3_, ...), custom_call_target="tpu_custom_call" | custom-call | flops 1 | bytes 1 | tf_op jit(solution)/shard_map/products/pallas_call | solution.py:30
  46.7 7.0 %collective-permute-done.13.got_ref = f32[256,384]{1,0:T(8,128)} collective-permute-done((f32[256,384]{1,0:T(8,128)}, f32[256,384]{1,0:T(8,128)}, u32[]{:S(2)}, u32[]{:S(2)}) %collective-permute-start.13) | collective-permute-done | bytes 393248 | tf_op jit(solution)/shard_map/ppermute | solution.py:212
  53.7 1.0 fold.13
  54.8 1.6 %collective-permute-start.15 = (f32[128,384]{1,0:T(8,128)S(1)}, f32[128,384]{1,0:T(8,128)S(1)}, u32[]{:S(2)}, u32[]{:S(2)}) collective-permute-start(f32[128,384]{1,0:T(8,128)S(1)} %get-tuple-element.85), channel_id=1, source_target_pairs={{0,2},{1,3},{2,0},{3,1},{4,6},{5,7},{6,4},{7,5},{8,10},{9,11},{10,... | collective-permute-start | bytes 589832 | tf_op jit(solution)/shard_map/ppermute | solution.py:212
  56.4 0.1 broadcast_select_fusion.1
  56.5 1.1 collective-permute-start.7
  57.6 1.1 fold.12
  58.6 1.6 %collective-permute-start.14 = (f32[128,384]{1,0:T(8,128)S(1)}, f32[128,384]{1,0:T(8,128)S(1)}, u32[]{:S(2)}, u32[]{:S(2)}) collective-permute-start(f32[128,384]{1,0:T(8,128)S(1)} %get-tuple-element.84), channel_id=1, source_target_pairs={{0,4},{1,5},{2,6},{3,7},{4,0},{5,1},{6,2},{7,3},{8,12},{9,13},{10,... | collective-permute-start | bytes 589832 | tf_op jit(solution)/shard_map/ppermute | solution.py:212
  60.2 1.4 %products.10 = (f32[256,384]{1,0:T(8,128)S(1)}, f32[256,384]{1,0:T(8,128)S(1)}) custom-call(f32[128,768]{1,0:T(8,128)S(1)} %collective-permute-done.3.refs_0_, f32[128,768]{1,0:T(8,128)S(1)} %collective-permute-done.1.refs_1_, f32[128,768]{1,0:T(8,128)S(1)} %copy-done.1, f32[128,768]{1,0:T(8,128)S(1)} %copy-done.3, f32[768,384]{1,0:T(8,128)S(1)} %copy-done.5), custom_call_target="tpu_custom_call" | custom-call | flops 1 | bytes 1 | tf_op jit(solution)/shard_map/products/pallas_call | solution.py:30
  61.6 0.6 collective-permute-start.16
  62.2 0.5 collective-permute-start.17
  62.8 3.1 %collective-permute-done.14.got_ref = f32[128,384]{1,0:T(8,128)S(1)} collective-permute-done((f32[128,384]{1,0:T(8,128)S(1)}, f32[128,384]{1,0:T(8,128)S(1)}, u32[]{:S(2)}, u32[]{:S(2)}) %collective-permute-start.14) | collective-permute-done | bytes 196640 | tf_op jit(solution)/shard_map/ppermute | solution.py:212
  65.8 1.4 %collective-permute-done.18.other_ref = f32[128,384]{1,0:T(8,128)S(1)} collective-permute-done((f32[128,384]{1,0:T(8,128)S(1)}, f32[128,384]{1,0:T(8,128)S(1)}, u32[]{:S(2)}, u32[]{:S(2)}) %collective-permute-start.18) | collective-permute-done | bytes 196640 | tf_op jit(solution)/shard_map/ppermute | solution.py:212
  67.3 0.8 write.4.refs_0_
  68.1 1.4 %products.11 = (f32[256,384]{1,0:T(8,128)S(1)}, f32[256,384]{1,0:T(8,128)S(1)}) custom-call(f32[128,768]{1,0:T(8,128)S(1)} %get-tuple-element.67.refs_0_, f32[128,768]{1,0:T(8,128)S(1)} %collective-permute-done.refs_1_, f32[128,768]{1,0:T(8,128)S(1)} %collective-permute-done.2.refs_2_, f32[128,768]{1,0:T(8,128)S(1)} %collective-permute-done.4.refs_3_, ...), custom_call_target="tpu_custom_call" | custom-call | flops 1 | bytes 1 | tf_op jit(solution)/shard_map/products/pallas_call | solution.py:30
  69.5 1.6 %collective-permute-done.16.got_ref = f32[256,384]{1,0:T(8,128)S(1)} collective-permute-done((f32[256,384]{1,0:T(8,128)S(1)}, f32[256,384]{1,0:T(8,128)S(1)}, u32[]{:S(2)}, u32[]{:S(2)}) %collective-permute-start.16) | collective-permute-done | bytes 393248 | tf_op jit(solution)/shard_map/ppermute | solution.py:212
  71.1 1.7 %collective-permute-done.17.got_ref = f32[256,384]{1,0:T(8,128)S(1)} collective-permute-done((f32[256,384]{1,0:T(8,128)S(1)}, f32[256,384]{1,0:T(8,128)S(1)}, u32[]{:S(2)}, u32[]{:S(2)}) %collective-permute-start.17) | collective-permute-done | bytes 393248 | tf_op jit(solution)/shard_map/ppermute | solution.py:212
  72.8 1.4 %broadcast_select_fusion.refs_4_ = f32[768,384]{1,0:T(8,128)S(1)} fusion(f32[768,384]{1,0:T(8,128)S(1)} %copy-done.7, f32[768,384]{1,0:T(8,128)} %collective-permute-done.9, pred[]{:T(512)S(6)} %or.3), kind=kLoop, calls=%fused_computation | loop fusion | flops 294912 | bytes 3538945 | tf_op jit(solution)/shard_map/jit(_where)/select_n | solution.py:241
  74.2 1.4 %products.12 = (f32[256,384]{1,0:T(8,128)S(1)}, f32[256,384]{1,0:T(8,128)S(1)}) custom-call(f32[128,768]{1,0:T(8,128)S(1)} %collective-permute-done.3.refs_0_, f32[128,768]{1,0:T(8,128)S(1)} %collective-permute-done.1.refs_1_, f32[128,768]{1,0:T(8,128)S(1)} %copy-done.1, f32[128,768]{1,0:T(8,128)S(1)} %copy-done.3, f32[768,384]{1,0:T(8,128)S(1)} %broadcast_select_fusion.refs_4_), custom_call_target="tpu_custom_call" | custom-call | flops 1 | bytes 1 | tf_op jit(solution)/shard_map/products/pallas_call | solution.py:30
  75.7 0.6 collective-permute-start.19
  76.3 1.5 %collective-permute-start.20 = (f32[256,384]{1,0:T(8,128)S(1)}, f32[256,384]{1,0:T(8,128)S(1)}, u32[]{:S(2)}, u32[]{:S(2)}) collective-permute-start(f32[256,384]{1,0:T(8,128)S(1)} %get-tuple-element.93), channel_id=1, source_target_pairs={{0,4},{1,5},{2,6},{3,7},{4,0},{5,1},{6,2},{7,3},{8,12},{9,13},{10,... | collective-permute-start | bytes 1179656 | tf_op jit(solution)/shard_map/ppermute | solution.py:212
  77.8 1.4 %products.13 = (f32[256,384]{1,0:T(8,128)S(1)}, f32[256,384]{1,0:T(8,128)S(1)}) custom-call(f32[128,768]{1,0:T(8,128)S(1)} %get-tuple-element.67.refs_0_, f32[128,768]{1,0:T(8,128)S(1)} %collective-permute-done.refs_1_, f32[128,768]{1,0:T(8,128)S(1)} %collective-permute-done.2.refs_2_, f32[128,768]{1,0:T(8,128)S(1)} %collective-permute-done.4.refs_3_, ...), custom_call_target="tpu_custom_call" | custom-call | flops 1 | bytes 1 | tf_op jit(solution)/shard_map/products/pallas_call | solution.py:30
  79.2 6.2 %collective-permute-done.19.got_ref = f32[256,384]{1,0:T(8,128)S(1)} collective-permute-done((f32[256,384]{1,0:T(8,128)S(1)}, f32[256,384]{1,0:T(8,128)S(1)}, u32[]{:S(2)}, u32[]{:S(2)}) %collective-permute-start.19) | collective-permute-done | bytes 393248 | tf_op jit(solution)/shard_map/ppermute | solution.py:212
  85.5 4.9 %collective-permute-done.7.refs_4_ = f32[768,384]{1,0:T(8,128)S(1)} collective-permute-done((f32[768,384]{1,0:T(8,128)S(1)}, f32[768,384]{1,0:T(8,128)S(1)}, u32[]{:S(2)}, u32[]{:S(2)}) %collective-permute-start.7) | collective-permute-done | bytes 1179680 | tf_op jit(solution)/shard_map/ppermute | solution.py:200
  90.3 1.4 %products.14 = (f32[256,384]{1,0:T(8,128)S(1)}, f32[256,384]{1,0:T(8,128)S(1)}) custom-call(f32[128,768]{1,0:T(8,128)S(1)} %collective-permute-done.3.refs_0_, f32[128,768]{1,0:T(8,128)S(1)} %collective-permute-done.1.refs_1_, f32[128,768]{1,0:T(8,128)S(1)} %copy-done.1, f32[128,768]{1,0:T(8,128)S(1)} %copy-done.3, f32[768,384]{1,0:T(8,128)S(1)} %collective-permute-done.7.refs_4_), custom_call_target="tpu_custom_call" | custom-call | flops 1 | bytes 1 | tf_op jit(solution)/shard_map/products/pallas_call | solution.py:30
  91.8 1.5 %collective-permute-start.21 = (f32[256,384]{1,0:T(8,128)S(1)}, f32[256,384]{1,0:T(8,128)S(1)}, u32[]{:S(2)}, u32[]{:S(2)}) collective-permute-start(f32[256,384]{1,0:T(8,128)S(1)} %get-tuple-element.100), channel_id=1, source_target_pairs={{0,2},{1,3},{2,0},{3,1},{4,6},{5,7},{6,4},{7,5},{8,10},{9,11},{10,... | collective-permute-start | bytes 1179656 | tf_op jit(solution)/shard_map/ppermute | solution.py:212
  93.2 1.5 %collective-permute-start.23 = (f32[256,384]{1,0:T(8,128)S(1)}, f32[256,384]{1,0:T(8,128)S(1)}, u32[]{:S(2)}, u32[]{:S(2)}) collective-permute-start(f32[256,384]{1,0:T(8,128)S(1)} %get-tuple-element.101), channel_id=1, source_target_pairs={{0,4},{1,5},{2,6},{3,7},{4,0},{5,1},{6,2},{7,3},{8,12},{9,13},{10,... | collective-permute-start | bytes 1179656 | tf_op jit(solution)/shard_map/ppermute | solution.py:212
  94.8 0.5 collective-permute-start.30
  95.3 0.6 collective-permute-start.29
  95.9 11.2 %collective-permute-done.30.got_ref = f32[128,384]{1,0:T(8,128)S(1)} collective-permute-done((f32[128,384]{1,0:T(8,128)S(1)}, f32[128,384]{1,0:T(8,128)S(1)}, u32[]{:S(2)}, u32[]{:S(2)}) %collective-permute-start.30) | collective-permute-done | bytes 196640 | tf_op jit(solution)/shard_map/ppermute | solution.py:212
  107.1 0.1 collective-permute-start.31
  107.2 1.5 %collective-permute-start.26 = (f32[128,384]{1,0:T(8,128)S(1)}, f32[128,384]{1,0:T(8,128)S(1)}, u32[]{:S(2)}, u32[]{:S(2)}) collective-permute-start(f32[128,384]{1,0:T(8,128)S(1)} %get-tuple-element.112), channel_id=1, source_target_pairs={{0,4},{1,5},{2,6},{3,7},{4,0},{5,1},{6,2},{7,3},{8,12},{9,13},{10,... | collective-permute-start | bytes 589832 | tf_op jit(solution)/shard_map/ppermute | solution.py:212
  108.7 1.4 %products.15 = (f32[256,384]{1,0:T(8,128)S(1)}, f32[256,384]{1,0:T(8,128)S(1)}) custom-call(f32[128,768]{1,0:T(8,128)S(1)} %get-tuple-element.67.refs_0_, f32[128,768]{1,0:T(8,128)S(1)} %collective-permute-done.refs_1_, f32[128,768]{1,0:T(8,128)S(1)} %collective-permute-done.2.refs_2_, f32[128,768]{1,0:T(8,128)S(1)} %collective-permute-done.4.refs_3_, ...), custom_call_target="tpu_custom_call" | custom-call | flops 1 | bytes 1 | tf_op jit(solution)/shard_map/products/pallas_call | solution.py:30
  110.1 1.3 %collective-permute-start.27 = (f32[128,384]{1,0:T(8,128)S(1)}, f32[128,384]{1,0:T(8,128)S(1)}, u32[]{:S(2)}, u32[]{:S(2)}) collective-permute-start(f32[128,384]{1,0:T(8,128)S(1)} %get-tuple-element.113), channel_id=1, source_target_pairs={{0,3},{1,2},{2,1},{3,0},{4,7},{5,6},{6,5},{7,4},{8,11},{9,10},{10,... | collective-permute-start | bytes 589832 | tf_op jit(solution)/shard_map/ppermute | solution.py:212
  111.5 0.4 collective-permute-start.28
  112.0 0.6 collective-permute-start.22
  112.5 0.1 collective-permute-start.24
  112.6 1.9 %collective-permute-done.26.got_ref = f32[128,384]{1,0:T(8,128)S(1)} collective-permute-done((f32[128,384]{1,0:T(8,128)S(1)}, f32[128,384]{1,0:T(8,128)S(1)}, u32[]{:S(2)}, u32[]{:S(2)}) %collective-permute-start.26) | collective-permute-done | bytes 196640 | tf_op jit(solution)/shard_map/ppermute | solution.py:212
  114.5 0.8 write.5.refs_0_
  115.3 1.7 %collective-permute-done.27.got_ref = f32[128,384]{1,0:T(8,128)S(1)} collective-permute-done((f32[128,384]{1,0:T(8,128)S(1)}, f32[128,384]{1,0:T(8,128)S(1)}, u32[]{:S(2)}, u32[]{:S(2)}) %collective-permute-start.27) | collective-permute-done | bytes 196640 | tf_op jit(solution)/shard_map/ppermute | solution.py:212
  117.1 0.8 write.6.refs_0_
  117.9 1.1 collective-permute-done.22.got_ref
  119.0 2.3 %collective-permute-done.24.got_ref = f32[128,384]{1,0:T(8,128)S(1)} collective-permute-done((f32[128,384]{1,0:T(8,128)S(1)}, f32[128,384]{1,0:T(8,128)S(1)}, u32[]{:S(2)}, u32[]{:S(2)}) %collective-permute-start.24) | collective-permute-done | bytes 196640 | tf_op jit(solution)/shard_map/ppermute | solution.py:212
  121.3 0.8 write.7
  (45 shorter events, 0.5 us)
Async XLA Ops:
  1.3 2.1 %collective-permute-start.5 = (f32[384,384]{1,0:T(8,128)S(1)}, f32[384,384]{1,0:T(8,128)S(1)}, u32[]{:S(2)}, u32[]{:S(2)}) collective-permute-start(f32[384,384]{1,0:T(8,128)S(1)} %get-tuple-element.69), channel_id=1, source_target_pairs={{0,1},{1,0},{2,3},{3,2},{4,5},{5,4},{6,7},{7,6},{8,9},{9,8},{10,11... | collective-permute-start | bytes 1769480 | tf_op jit(solution)/shard_map/ppermute | solution.py:212
  3.6 29.3 %collective-permute-start.8 = (f32[768,384]{1,0:T(8,128)S(1)}, f32[768,384]{1,0:T(8,128)S(1)}, u32[]{:S(2)}, u32[]{:S(2)}) collective-permute-start(f32[768,384]{1,0:T(8,128)S(1)} %join.1.refs_4_), channel_id=1, source_target_pairs={{0,8},{8,0},{16,24},{24,16},{1,9},{9,1},{17,25},{25,17},{2,10},{10... | collective-permute-start | bytes 3538952 | tf_op jit(solution)/shard_map/ppermute | solution.py:192
  6.6 27.3 %collective-permute-start.6 = (f32[768,384]{1,0:T(8,128)S(1)}, f32[768,384]{1,0:T(8,128)S(1)}, u32[]{:S(2)}, u32[]{:S(2)}) collective-permute-start(f32[768,384]{1,0:T(8,128)S(1)} %join.1.refs_4_), channel_id=1, source_target_pairs={{8,16},{16,8},{9,17},{17,9},{10,18},{18,10},{11,19},{19,11},{12,20... | collective-permute-start | bytes 3538952 | tf_op jit(solution)/shard_map/ppermute | solution.py:196
  7.3 19.4 %collective-permute-start = (f32[128,768]{1,0:T(8,128)S(1)}, f32[128,768]{1,0:T(8,128)S(1)}, u32[]{:S(2)}, u32[]{:S(2)}) collective-permute-start(f32[128,768]{1,0:T(8,128)S(1)} %get-tuple-element.65), channel_id=1, source_target_pairs={{0,4},{1,5},{2,6},{3,7},{4,0},{5,1},{6,2},{7,3},{8,12},{9,13},{10,... | collective-permute-start | bytes 1179656 | tf_op jit(solution)/shard_map/ppermute | solution.py:212
  8.9 17.8 %collective-permute-start.1 = (f32[128,768]{1,0:T(8,128)S(1)}, f32[128,768]{1,0:T(8,128)S(1)}, u32[]{:S(2)}, u32[]{:S(2)}) collective-permute-start(f32[128,768]{1,0:T(8,128)S(1)} %get-tuple-element.66), channel_id=1, source_target_pairs={{0,6},{1,7},{2,4},{3,5},{4,2},{5,3},{6,0},{7,1},{8,14},{9,15},{10,... | collective-permute-start | bytes 1179656 | tf_op jit(solution)/shard_map/ppermute | solution.py:212
  10.3 29.3 %collective-permute-start.3 = (f32[128,768]{1,0:T(8,128)S(1)}, f32[128,768]{1,0:T(8,128)S(1)}, u32[]{:S(2)}, u32[]{:S(2)}) collective-permute-start(f32[128,768]{1,0:T(8,128)S(1)} %get-tuple-element.68), channel_id=1, source_target_pairs={{0,2},{1,3},{2,0},{3,1},{4,6},{5,7},{6,4},{7,5},{8,10},{9,11},{10,... | collective-permute-start | bytes 1179656 | tf_op jit(solution)/shard_map/ppermute | solution.py:212
  26.7 13.5 %collective-permute-start.10 = (f32[128,768]{1,0:T(8,128)S(1)}, f32[128,768]{1,0:T(8,128)S(1)}, u32[]{:S(2)}, u32[]{:S(2)}) collective-permute-start(f32[128,768]{1,0:T(8,128)S(1)} %collective-permute-done.refs_1_), channel_id=1, source_target_pairs={{0,1},{1,0},{2,3},{3,2},{4,5},{5,4},{6,7},{7,6},{8,9},{9,8},{10,11... | collective-permute-start | bytes 1179656 | tf_op jit(solution)/shard_map/ppermute | solution.py:212
  26.7 13.5 %collective-permute-start.11 = (f32[128,768]{1,0:T(8,128)S(1)}, f32[128,768]{1,0:T(8,128)S(1)}, u32[]{:S(2)}, u32[]{:S(2)}) collective-permute-start(f32[128,768]{1,0:T(8,128)S(1)} %collective-permute-done.1.refs_1_), channel_id=1, source_target_pairs={{0,1},{1,0},{2,3},{3,2},{4,5},{5,4},{6,7},{7,6},{8,9},{9,8},{10,11... | collective-permute-start | bytes 1179656 | tf_op jit(solution)/shard_map/ppermute | solution.py:212
  32.8 1.0 copy-start.4
  33.9 6.3 %copy-start.6 = (f32[768,384]{1,0:T(8,128)}, f32[768,384]{1,0:T(8,128)S(1)}, u32[]{:S(2)}) copy-start(f32[768,384]{1,0:T(8,128)S(1)} %collective-permute-done.6) | copy-start | bytes 3538948
  33.9 38.9 %collective-permute-start.9 = (f32[768,384]{1,0:T(8,128)S(1)}, f32[768,384]{1,0:T(8,128)}, u32[]{:S(2)}, u32[]{:S(2)}) collective-permute-start(f32[768,384]{1,0:T(8,128)S(1)} %join.1.refs_4_), channel_id=1, source_target_pairs={{0,24},{24,0},{1,25},{25,1},{2,26},{26,2},{3,27},{27,3},{4,28},{28... | collective-permute-start | bytes 3538952 | tf_op jit(solution)/shard_map/ppermute | solution.py:198
  39.5 5.8 %collective-permute-start.2 = (f32[128,768]{1,0:T(8,128)S(1)}, f32[128,768]{1,0:T(8,128)S(1)}, u32[]{:S(2)}, u32[]{:S(2)}) collective-permute-start(f32[128,768]{1,0:T(8,128)S(1)} %get-tuple-element.67.refs_0_), channel_id=1, source_target_pairs={{0,1},{1,0},{2,3},{3,2},{4,5},{5,4},{6,7},{7,6},{8,9},{9,8},{10,11... | collective-permute-start | bytes 1179656 | tf_op jit(solution)/shard_map/ppermute | solution.py:212
  39.6 5.7 %collective-permute-start.4 = (f32[128,768]{1,0:T(8,128)S(1)}, f32[128,768]{1,0:T(8,128)S(1)}, u32[]{:S(2)}, u32[]{:S(2)}) collective-permute-start(f32[128,768]{1,0:T(8,128)S(1)} %collective-permute-done.3.refs_0_), channel_id=1, source_target_pairs={{0,1},{1,0},{2,3},{3,2},{4,5},{5,4},{6,7},{7,6},{8,9},{9,8},{10,11... | collective-permute-start | bytes 1179656 | tf_op jit(solution)/shard_map/ppermute | solution.py:212
  40.1 2.2 %copy-start = (f32[128,768]{1,0:T(8,128)}, f32[128,768]{1,0:T(8,128)S(1)}, u32[]{:S(2)}) copy-start(f32[128,768]{1,0:T(8,128)S(1)} %collective-permute-done.10.refs_2_) | copy-start | bytes 1179652
  40.1 2.2 %copy-start.2 = (f32[128,768]{1,0:T(8,128)}, f32[128,768]{1,0:T(8,128)S(1)}, u32[]{:S(2)}) copy-start(f32[128,768]{1,0:T(8,128)S(1)} %collective-permute-done.11.refs_3_) | copy-start | bytes 1179652
  42.3 11.4 %collective-permute-start.13 = (f32[256,384]{1,0:T(8,128)}, f32[256,384]{1,0:T(8,128)}, u32[]{:S(2)}, u32[]{:S(2)}) collective-permute-start(f32[256,384]{1,0:T(8,128)} %get-tuple-element.73), channel_id=1, source_target_pairs={{0,4},{1,5},{2,6},{3,7},{4,0},{5,1},{6,2},{7,3},{8,12},{9,13},{10,... | collective-permute-start | bytes 1179656 | tf_op jit(solution)/shard_map/ppermute | solution.py:212
  43.8 13.7 %collective-permute-start.12 = (f32[256,384]{1,0:T(8,128)}, f32[256,384]{1,0:T(8,128)}, u32[]{:S(2)}, u32[]{:S(2)}) collective-permute-start(f32[256,384]{1,0:T(8,128)} %get-tuple-element.72), channel_id=1, source_target_pairs={{0,2},{1,3},{2,0},{3,1},{4,6},{5,7},{6,4},{7,5},{8,10},{9,11},{10,... | collective-permute-start | bytes 1179656 | tf_op jit(solution)/shard_map/ppermute | solution.py:212
  45.3 11.0 %copy-start.7 = (f32[768,384]{1,0:T(8,128)S(1)}, f32[768,384]{1,0:T(8,128)}, u32[]{:S(2)}) copy-start(f32[768,384]{1,0:T(8,128)} %copy-done.6) | copy-start | bytes 3538948
  54.8 5.4 %copy-start.1 = (f32[128,768]{1,0:T(8,128)S(1)}, f32[128,768]{1,0:T(8,128)}, u32[]{:S(2)}) copy-start(f32[128,768]{1,0:T(8,128)} %copy-done) | copy-start | bytes 1179652
  54.8 5.4 %copy-start.3 = (f32[128,768]{1,0:T(8,128)S(1)}, f32[128,768]{1,0:T(8,128)}, u32[]{:S(2)}) copy-start(f32[128,768]{1,0:T(8,128)} %copy-done.2) | copy-start | bytes 1179652
  54.8 7.4 %collective-permute-start.15 = (f32[128,384]{1,0:T(8,128)S(1)}, f32[128,384]{1,0:T(8,128)S(1)}, u32[]{:S(2)}, u32[]{:S(2)}) collective-permute-start(f32[128,384]{1,0:T(8,128)S(1)} %get-tuple-element.85), channel_id=1, source_target_pairs={{0,2},{1,3},{2,0},{3,1},{4,6},{5,7},{6,4},{7,5},{8,10},{9,11},{10,... | collective-permute-start | bytes 589832 | tf_op jit(solution)/shard_map/ppermute | solution.py:212
  56.4 3.8 %copy-start.5 = (f32[768,384]{1,0:T(8,128)S(1)}, f32[768,384]{1,0:T(8,128)}, u32[]{:S(2)}) copy-start(f32[768,384]{1,0:T(8,128)} %copy-done.4) | copy-start | bytes 3538948
  56.5 33.9 %collective-permute-start.7 = (f32[768,384]{1,0:T(8,128)S(1)}, f32[768,384]{1,0:T(8,128)S(1)}, u32[]{:S(2)}, u32[]{:S(2)}) collective-permute-start(f32[768,384]{1,0:T(8,128)S(1)} %broadcast_select_fusion.1), channel_id=1, source_target_pairs={{8,0},{16,24},{0,16},{24,8},{9,1},{17,25},{1,17},{25,9},{10,2},{18... | collective-permute-start | bytes 3538952 | tf_op jit(solution)/shard_map/ppermute | solution.py:200
  58.6 7.2 %collective-permute-start.14 = (f32[128,384]{1,0:T(8,128)S(1)}, f32[128,384]{1,0:T(8,128)S(1)}, u32[]{:S(2)}, u32[]{:S(2)}) collective-permute-start(f32[128,384]{1,0:T(8,128)S(1)} %get-tuple-element.84), channel_id=1, source_target_pairs={{0,4},{1,5},{2,6},{3,7},{4,0},{5,1},{6,2},{7,3},{8,12},{9,13},{10,... | collective-permute-start | bytes 589832 | tf_op jit(solution)/shard_map/ppermute | solution.py:212
  61.6 9.4 %collective-permute-start.16 = (f32[256,384]{1,0:T(8,128)S(1)}, f32[256,384]{1,0:T(8,128)S(1)}, u32[]{:S(2)}, u32[]{:S(2)}) collective-permute-start(f32[256,384]{1,0:T(8,128)S(1)} %get-tuple-element.80), channel_id=1, source_target_pairs={{0,2},{1,3},{2,0},{3,1},{4,6},{5,7},{6,4},{7,5},{8,10},{9,11},{10,... | collective-permute-start | bytes 1179656 | tf_op jit(solution)/shard_map/ppermute | solution.py:212
  62.2 10.5 %collective-permute-start.17 = (f32[256,384]{1,0:T(8,128)S(1)}, f32[256,384]{1,0:T(8,128)S(1)}, u32[]{:S(2)}, u32[]{:S(2)}) collective-permute-start(f32[256,384]{1,0:T(8,128)S(1)} %get-tuple-element.81), channel_id=1, source_target_pairs={{0,4},{1,5},{2,6},{3,7},{4,0},{5,1},{6,2},{7,3},{8,12},{9,13},{10,... | collective-permute-start | bytes 1179656 | tf_op jit(solution)/shard_map/ppermute | solution.py:212
  65.8 1.4 %collective-permute-start.18 = (f32[128,384]{1,0:T(8,128)S(1)}, f32[128,384]{1,0:T(8,128)S(1)}, u32[]{:S(2)}, u32[]{:S(2)}) collective-permute-start(f32[128,384]{1,0:T(8,128)S(1)} %fold.16), channel_id=1, source_target_pairs={{0,1},{1,0},{2,3},{3,2},{4,5},{5,4},{6,7},{7,6},{8,9},{9,8},{10,11... | collective-permute-start | bytes 589832 | tf_op jit(solution)/shard_map/ppermute | solution.py:212
  75.7 9.7 %collective-permute-start.19 = (f32[256,384]{1,0:T(8,128)S(1)}, f32[256,384]{1,0:T(8,128)S(1)}, u32[]{:S(2)}, u32[]{:S(2)}) collective-permute-start(f32[256,384]{1,0:T(8,128)S(1)} %get-tuple-element.92), channel_id=1, source_target_pairs={{0,2},{1,3},{2,0},{3,1},{4,6},{5,7},{6,4},{7,5},{8,10},{9,11},{10,... | collective-permute-start | bytes 1179656 | tf_op jit(solution)/shard_map/ppermute | solution.py:212
  76.3 9.2 %collective-permute-start.20 = (f32[256,384]{1,0:T(8,128)S(1)}, f32[256,384]{1,0:T(8,128)S(1)}, u32[]{:S(2)}, u32[]{:S(2)}) collective-permute-start(f32[256,384]{1,0:T(8,128)S(1)} %get-tuple-element.93), channel_id=1, source_target_pairs={{0,4},{1,5},{2,6},{3,7},{4,0},{5,1},{6,2},{7,3},{8,12},{9,13},{10,... | collective-permute-start | bytes 1179656 | tf_op jit(solution)/shard_map/ppermute | solution.py:212
  91.8 18.3 %collective-permute-start.21 = (f32[256,384]{1,0:T(8,128)S(1)}, f32[256,384]{1,0:T(8,128)S(1)}, u32[]{:S(2)}, u32[]{:S(2)}) collective-permute-start(f32[256,384]{1,0:T(8,128)S(1)} %get-tuple-element.100), channel_id=1, source_target_pairs={{0,2},{1,3},{2,0},{3,1},{4,6},{5,7},{6,4},{7,5},{8,10},{9,11},{10,... | collective-permute-start | bytes 1179656 | tf_op jit(solution)/shard_map/ppermute | solution.py:212
  93.2 18.2 %collective-permute-start.23 = (f32[256,384]{1,0:T(8,128)S(1)}, f32[256,384]{1,0:T(8,128)S(1)}, u32[]{:S(2)}, u32[]{:S(2)}) collective-permute-start(f32[256,384]{1,0:T(8,128)S(1)} %get-tuple-element.101), channel_id=1, source_target_pairs={{0,4},{1,5},{2,6},{3,7},{4,0},{5,1},{6,2},{7,3},{8,12},{9,13},{10,... | collective-permute-start | bytes 1179656 | tf_op jit(solution)/shard_map/ppermute | solution.py:212
  94.8 12.3 %collective-permute-start.30 = (f32[128,384]{1,0:T(8,128)S(1)}, f32[128,384]{1,0:T(8,128)S(1)}, u32[]{:S(2)}, u32[]{:S(2)}) collective-permute-start(f32[128,384]{1,0:T(8,128)S(1)} %get-tuple-element.118), channel_id=1, source_target_pairs={{0,2},{1,3},{2,0},{3,1},{4,6},{5,7},{6,4},{7,5},{8,10},{9,11},{10,... | collective-permute-start | bytes 589832 | tf_op jit(solution)/shard_map/ppermute | solution.py:212
  95.3 16.7 %collective-permute-start.29 = (f32[128,384]{1,0:T(8,128)S(1)}, f32[128,384]{1,0:T(8,128)S(1)}, u32[]{:S(2)}, u32[]{:S(2)}) collective-permute-start(f32[128,384]{1,0:T(8,128)S(1)} %get-tuple-element.117), channel_id=1, source_target_pairs={{0,4},{1,5},{2,6},{3,7},{4,0},{5,1},{6,2},{7,3},{8,12},{9,13},{10,... | collective-permute-start | bytes 589832 | tf_op jit(solution)/shard_map/ppermute | solution.py:212
  107.1 5.4 %collective-permute-start.31 = (f32[128,384]{1,0:T(8,128)S(1)}, f32[128,384]{1,0:T(8,128)S(1)}, u32[]{:S(2)}, u32[]{:S(2)}) collective-permute-start(f32[128,384]{1,0:T(8,128)S(1)} %fold.23), channel_id=1, source_target_pairs={{0,1},{1,0},{2,3},{3,2},{4,5},{5,4},{6,7},{7,6},{8,9},{9,8},{10,11... | collective-permute-start | bytes 589832 | tf_op jit(solution)/shard_map/ppermute | solution.py:212
  107.2 7.3 %collective-permute-start.26 = (f32[128,384]{1,0:T(8,128)S(1)}, f32[128,384]{1,0:T(8,128)S(1)}, u32[]{:S(2)}, u32[]{:S(2)}) collective-permute-start(f32[128,384]{1,0:T(8,128)S(1)} %get-tuple-element.112), channel_id=1, source_target_pairs={{0,4},{1,5},{2,6},{3,7},{4,0},{5,1},{6,2},{7,3},{8,12},{9,13},{10,... | collective-permute-start | bytes 589832 | tf_op jit(solution)/shard_map/ppermute | solution.py:212
  110.1 6.9 %collective-permute-start.27 = (f32[128,384]{1,0:T(8,128)S(1)}, f32[128,384]{1,0:T(8,128)S(1)}, u32[]{:S(2)}, u32[]{:S(2)}) collective-permute-start(f32[128,384]{1,0:T(8,128)S(1)} %get-tuple-element.113), channel_id=1, source_target_pairs={{0,3},{1,2},{2,1},{3,0},{4,7},{5,6},{6,5},{7,4},{8,11},{9,10},{10,... | collective-permute-start | bytes 589832 | tf_op jit(solution)/shard_map/ppermute | solution.py:212
  111.5 5.5 %collective-permute-start.28 = (f32[128,384]{1,0:T(8,128)S(1)}, f32[128,384]{1,0:T(8,128)S(1)}, u32[]{:S(2)}, u32[]{:S(2)}) collective-permute-start(f32[128,384]{1,0:T(8,128)S(1)} %get-tuple-element.98), channel_id=1, source_target_pairs={{0,1},{1,0},{2,3},{3,2},{4,5},{5,4},{6,7},{7,6},{8,9},{9,8},{10,11... | collective-permute-start | bytes 589832 | tf_op jit(solution)/shard_map/ppermute | solution.py:212
  112.0 7.0 %collective-permute-start.22 = (f32[128,384]{1,0:T(8,128)S(1)}, f32[128,384]{1,0:T(8,128)S(1)}, u32[]{:S(2)}, u32[]{:S(2)}) collective-permute-start(f32[128,384]{1,0:T(8,128)S(1)} %get-tuple-element.105), channel_id=1, source_target_pairs={{0,4},{1,5},{2,6},{3,7},{4,0},{5,1},{6,2},{7,3},{8,12},{9,13},{10,... | collective-permute-start | bytes 589832 | tf_op jit(solution)/shard_map/ppermute | solution.py:212
  112.5 8.7 %collective-permute-start.24 = (f32[128,384]{1,0:T(8,128)S(1)}, f32[128,384]{1,0:T(8,128)S(1)}, u32[]{:S(2)}, u32[]{:S(2)}) collective-permute-start(f32[128,384]{1,0:T(8,128)S(1)} %get-tuple-element.107), channel_id=1, source_target_pairs={{0,3},{1,2},{2,1},{3,0},{4,7},{5,6},{6,5},{7,4},{8,11},{9,10},{10,... | collective-permute-start | bytes 589832 | tf_op jit(solution)/shard_map/ppermute | solution.py:212
  114.5 6.7 %collective-permute-start.25 = (f32[128,384]{1,0:T(8,128)S(1)}, f32[128,384]{1,0:T(8,128)S(1)}, u32[]{:S(2)}, u32[]{:S(2)}) collective-permute-start(f32[128,384]{1,0:T(8,128)S(1)} %get-tuple-element.108), channel_id=1, source_target_pairs={{0,1},{1,0},{2,3},{3,2},{4,5},{5,4},{6,7},{7,6},{8,9},{9,8},{10,11... | collective-permute-start | bytes 589832 | tf_op jit(solution)/shard_map/ppermute | solution.py:212
